TPU v7x, 32 devices: a whole 2x2x4 slice. The times are simulated.
32 devices in a mesh: dp: 4 (over x, core), tm: 4 (over z), space: 2 (over y).
Axes of the slice: x: 2, y: 2, z: 4, core: 2. Of those that a mesh axis runs over, the one named last changes fastest.
Arguments:
- query_heads: bfloat16 [4, 4, 256, 3072], P('dp', 'tm', None, 'space')
- key_heads: bfloat16 [4, 4, 256, 3072], P('dp', 'tm', None, 'space')
- value_heads: bfloat16 [4, 4, 256, 3072], P('dp', 'tm', None, 'space')
- cotangent: bfloat16 [4, 4, 256, 3072], P('dp', 'tm', 'space'), may hold values from -6 to 6
- task_ids: int32 [4], P('dp'), may hold values from 0 to 15
- lengths: int32 [4], P('dp'), may hold values from 1 to 4, as said below
- gains: float32 [2, 16, 3072], P(None, None, 'space'), may hold values from 0.5 to 2
Outputs:
- grad_queries: bfloat16 [4, 4, 256, 3072], P('dp', 'tm', None, 'space')
- grad_keys: bfloat16 [4, 4, 256, 3072], P('dp', 'tm', None, 'space')
- grad_gains: float32 [2, 16, 3072], P(None, None, 'space')
Inputs may be any that keep to these rules, and one draw needn't show every extreme that they name: `lengths`: at least one clip has all 4 frames valid.
All inputs are finite; a program needn't handle non-finite values.
Results may differ from a plain program's by a relative error of at most 0.003.
The roundings to bfloat16 on the way count: a program that leaves them out, or rounds other values in their place, can miss the bound.
Values may be sent and summed in bfloat16 or wider, within the bound.
No kernel may reach another device: no remote copies, remote signals or barrier semaphores. Data moves between devices by JAX's collectives and lax.ppermute only.
A program may use at most 128 MiB of HBM per device.

v0:
```python
import functools

import jax
import jax.numpy as jnp
from jax import lax
from jax.experimental import pallas as pl
from jax.experimental.pallas import tpu as pltpu
from jax.sharding import PartitionSpec as P

HEAD_DIM = 128
GROUP = 16
VMEM_BYTES = 48 * 1024 * 1024


def params():
    return pltpu.CompilerParams(vmem_limit_bytes=VMEM_BYTES)


def columns_dot(left, right):
    return lax.dot_general(
        left, right, (((1,), (1,)), ((), ())), preferred_element_type=jnp.float32
    )


def dot(left, right):
    return jnp.dot(left, right, preferred_element_type=jnp.float32)


def forward_kernel(query_ref, key_ref, value_ref, weights_ref, attended_ref):
    score_scale = HEAD_DIM ** (-0.5)
    for head in range(weights_ref.shape[0]):
        cols = pl.ds(head * HEAD_DIM, HEAD_DIM)
        scores = columns_dot(key_ref[:, cols], query_ref[:, cols])
        largest = jnp.max(scores, axis=0, keepdims=True)
        raised = jnp.exp((scores - largest) * score_scale)
        weights = raised * (1.0 / jnp.sum(raised, axis=0, keepdims=True))
        weights_ref[head] = weights
        attended = dot(value_ref[:, cols].T, weights.astype(jnp.bfloat16))
        attended_ref[head] = attended.astype(jnp.bfloat16)


def forward(queries, key_rows, values, per_step):
    patches, feat = queries.shape
    heads = feat // HEAD_DIM
    field = pl.BlockSpec((patches, per_step * HEAD_DIM), lambda i: (0, i))
    return pl.pallas_call(
        forward_kernel,
        grid=(heads // per_step,),
        in_specs=[field] * 3,
        out_specs=[
            pl.BlockSpec((per_step, patches, patches), lambda i: (i, 0, 0)),
            pl.BlockSpec((per_step, HEAD_DIM, patches), lambda i: (i, 0, 0)),
        ],
        out_shape=[
            jax.ShapeDtypeStruct((heads, patches, patches), jnp.float32),
            jax.ShapeDtypeStruct((heads, HEAD_DIM, patches), jnp.bfloat16),
        ],
        compiler_params=params(),
        cost_estimate=pl.CostEstimate(
            flops=4 * heads * patches * patches * HEAD_DIM,
            bytes_accessed=heads * patches * (patches * 4 + 8 * HEAD_DIM),
            transcendentals=heads * patches * patches,
        ),
        name="spatial_forward",
    )(queries, key_rows, values)


def backward_kernel(query_ref, key_ref, value_ref, weights_ref, grad_ref, gq_ref, gk_ref):
    score_scale = HEAD_DIM ** (-0.5)
    for head in range(weights_ref.shape[0]):
        cols = pl.ds(head * HEAD_DIM, HEAD_DIM)
        weights = weights_ref[head]
        spatial_grad = dot(value_ref[:, cols], grad_ref[head])
        row_sum = jnp.sum(spatial_grad * weights, axis=0, keepdims=True)
        scores = (weights * (spatial_grad - row_sum) * score_scale).astype(jnp.bfloat16)
        gk_ref[:, cols] = dot(scores, query_ref[:, cols]).astype(jnp.bfloat16)
        grad_query = dot(key_ref[:, cols].T, scores).astype(jnp.bfloat16)
        gq_ref[:, cols] = grad_query.T


def backward(queries, key_rows, values, weights, grads, per_step):
    patches, feat = queries.shape
    heads = feat // HEAD_DIM
    field = pl.BlockSpec((patches, per_step * HEAD_DIM), lambda i: (0, i))
    return pl.pallas_call(
        backward_kernel,
        grid=(heads // per_step,),
        in_specs=[
            field,
            field,
            field,
            pl.BlockSpec((per_step, patches, patches), lambda i: (i, 0, 0)),
            pl.BlockSpec((per_step, HEAD_DIM, patches), lambda i: (i, 0, 0)),
        ],
        out_specs=[field, field],
        out_shape=[jax.ShapeDtypeStruct((patches, feat), jnp.bfloat16)] * 2,
        compiler_params=params(),
        cost_estimate=pl.CostEstimate(
            flops=6 * heads * patches * patches * HEAD_DIM,
            bytes_accessed=heads * patches * (patches * 4 + 12 * HEAD_DIM),
            transcendentals=0,
        ),
        name="spatial_backward",
    )(queries, key_rows, values, weights, grads)


def turn_kernel(field_ref, turned_ref):
    for head in range(turned_ref.shape[2]):
        cols = pl.ds(head * HEAD_DIM, HEAD_DIM)
        turned_ref[0, 0, head] = field_ref[:, cols].T


def turn(field, frames, spaces):
    patches, feat = field.shape
    heads = feat // (frames * spaces * HEAD_DIM)
    return pl.pallas_call(
        turn_kernel,
        grid=(frames, spaces),
        in_specs=[pl.BlockSpec((patches, heads * HEAD_DIM), lambda f, s: (0, s * frames + f))],
        out_specs=pl.BlockSpec((1, 1, heads, HEAD_DIM, patches), lambda f, s: (f, s, 0, 0, 0)),
        out_shape=jax.ShapeDtypeStruct((frames, spaces, heads, HEAD_DIM, patches), jnp.bfloat16),
        compiler_params=params(),
        cost_estimate=pl.CostEstimate(
            flops=0, bytes_accessed=4 * patches * feat, transcendentals=0
        ),
        name="turn_cotangent",
    )(field)


def temporal_kernel(length_ref, attended_ref, upstream_ref, gain_ref, grad_ref, mixed_ref, mixed_sum):
    frames, _, feat, lanes = attended_ref.shape
    half = GROUP // 2
    score_scale = feat ** (-0.5)
    length = length_ref[0]
    pairs = [(t, u) for t in range(frames) for u in range(t + 1)]
    every = range(frames)
    valid = [jnp.where(t < length, 1.0, 0.0).astype(jnp.float32) for t in every]
    bias = [jnp.where(u < length, 0.0, -1e30).astype(jnp.float32) for u in every]

    def load(ref, t, group):
        index = (t, 0) if len(ref.shape) == 4 else (t, 0, 0)
        block = ref[index + (pl.ds(group * GROUP, GROUP), slice(None))].astype(jnp.float32)
        return block[:half], block[half:]

    def total(piece):
        return jnp.broadcast_to(jnp.sum(piece, axis=0, keepdims=True), (half, lanes))

    squares = [jnp.zeros((half, lanes), jnp.float32) for _ in every]
    for group in range(feat // GROUP):
        for t in every:
            low, high = load(attended_ref, t, group)
            squares[t] = squares[t] + (low * low + high * high)
    inverse = [lax.rsqrt(total(squares[t]) * (1.0 / feat) + 1e-06) for t in every]

    raw = {pair: jnp.zeros((half, lanes), jnp.float32) for pair in pairs}
    grad = {pair: jnp.zeros((half, lanes), jnp.float32) for pair in pairs}
    for group in range(feat // GROUP):
        fields = [load(attended_ref, t, group) for t in every]
        ups = [load(upstream_ref, t, group) for t in every]
        for side in range(2):
            rows = pl.ds(group * GROUP + side * half, half)
            gain = gain_ref[0, rows, :]
            normed = [fields[t][side] * inverse[t] for t in every]
            gained = [normed[t] * gain for t in every]
            for t, u in pairs:
                raw[t, u] = raw[t, u] + gained[t] * normed[u]
                grad[t, u] = grad[t, u] + ups[t][side] * fields[u][side]

    value_part, score_part = {}, {}
    for t in every:
        seen = range(t + 1)
        for u in seen:
            raw[t, u] = total(raw[t, u])
            grad[t, u] = total(grad[t, u]) * valid[t]
        scores = [raw[t, u] * score_scale + bias[u] for u in seen]
        largest = functools.reduce(jnp.maximum, scores)
        raised = [jnp.exp(score - largest) for score in scores]
        over = 1.0 / functools.reduce(jnp.add, raised)
        weights = [piece * over for piece in raised]
        mean_grad = functools.reduce(jnp.add, [weights[u] * grad[t, u] for u in seen])
        for u in seen:
            rounded = weights[u].astype(jnp.bfloat16).astype(jnp.float32)
            value_part[t, u] = (rounded + (1.0 if u == t else 0.0)) * valid[t]
            score_part[t, u] = weights[u] * (grad[t, u] - mean_grad) * score_scale

    both = {(t, u): score_part[t, u] * (2.0 if t == u else 1.0) for t, u in pairs}
    both.update({(u, t): both[t, u] for t, u in pairs})
    raw.update({(u, t): raw[t, u] for t, u in pairs})
    mean_part = [
        functools.reduce(jnp.add, [both[u, v] * raw[u, v] for v in every]) * (1.0 / feat)
        for u in every
    ]

    @pl.when(pl.program_id(1) == 0)
    def _():
        mixed_sum[...] = jnp.zeros_like(mixed_sum)

    for group in range(feat // GROUP):
        fields = [load(attended_ref, t, group) for t in every]
        ups = [load(upstream_ref, t, group) for t in every]
        outs = [[] for _ in every]
        for side in range(2):
            rows = pl.ds(group * GROUP + side * half, half)
            gain = gain_ref[0, rows, :]
            normed = [fields[t][side] * inverse[t] for t in every]
            mixed = jnp.zeros((half, lanes), jnp.float32)
            for u in every:
                crossed = functools.reduce(jnp.add, [both[u, v] * normed[v] for v in every])
                mixed = mixed + crossed * normed[u]
                from_norm = inverse[u] * (gain * crossed - normed[u] * mean_part[u])
                direct = functools.reduce(
                    jnp.add, [value_part[t, u] * ups[t][side] for t in range(u, frames)]
                )
                outs[u].append(direct + from_norm)
            mixed_sum[rows, :] += mixed
        for u in every:
            grad_ref[u, 0, pl.ds(group * GROUP, GROUP), :] = jnp.concatenate(
                outs[u], axis=0
            ).astype(jnp.bfloat16)

    @pl.when(pl.program_id(1) == pl.num_programs(1) - 1)
    def _():
        summed = jnp.sum(mixed_sum[...].T, axis=0, keepdims=True) * 0.5
        mixed_ref[0] = jnp.broadcast_to(summed, mixed_ref.shape[1:])


def temporal(attended, upstream, gain, length):
    frames, heads, feat, patches = attended.shape
    spaces = upstream.shape[1]
    lanes = patches // spaces
    return pl.pallas_call(
        temporal_kernel,
        grid=(heads, spaces),
        in_specs=[
            pl.BlockSpec(memory_space=pltpu.SMEM),
            pl.BlockSpec((frames, 1, feat, lanes), lambda h, s: (0, h, 0, s)),
            pl.BlockSpec((frames, 1, 1, feat, lanes), lambda h, s: (0, s, h, 0, 0)),
            pl.BlockSpec((1, feat, lanes), lambda h, s: (h, 0, 0)),
        ],
        out_specs=[
            pl.BlockSpec((frames, 1, feat, lanes), lambda h, s: (0, h, 0, s)),
            pl.BlockSpec((1, 8, feat), lambda h, s: (h, 0, 0)),
        ],
        out_shape=[
            jax.ShapeDtypeStruct(attended.shape, jnp.bfloat16),
            jax.ShapeDtypeStruct((heads, 8, feat), jnp.float32),
        ],
        scratch_shapes=[pltpu.VMEM((feat, lanes), jnp.float32)],
        compiler_params=params(),
        cost_estimate=pl.CostEstimate(
            flops=heads * patches * feat * 200,
            bytes_accessed=6 * frames * heads * patches * feat,
            transcendentals=heads * patches * 16,
        ),
        name="temporal",
    )(length, attended, upstream, gain)


def split_by_heads(query_heads, key_heads, value_heads, cotangent, task_ids, lengths, gains, frames, spaces):
    patches, feat = query_heads.shape[2:]
    heads = feat // HEAD_DIM
    own = heads // frames
    tasks = gains.shape[1]
    queries, key_rows, values = (
        field.reshape(patches, feat) for field in (query_heads, key_heads, value_heads)
    )
    turned = turn(cotangent.reshape(cotangent.shape[2:]), frames, spaces)
    upstream = lax.all_to_all(
        turned.reshape((frames * spaces,) + turned.shape[2:]),
        ("tm", "space"),
        split_axis=0,
        concat_axis=0,
        tiled=True,
    ).reshape(turned.shape)
    weights, attended = forward(queries, key_rows, values, own)
    all_attended = lax.all_to_all(
        attended.reshape(frames, own, HEAD_DIM, patches), "tm", split_axis=0, concat_axis=0, tiled=True
    )
    rows = lax.dynamic_index_in_dim(gains, task_ids[0], 1, keepdims=False)
    product = lax.dynamic_slice_in_dim(
        rows[0] * rows[1], lax.axis_index("tm") * (own * HEAD_DIM), own * HEAD_DIM, 0
    )
    gain = jnp.broadcast_to(
        product.reshape(own, HEAD_DIM, 1), (own, HEAD_DIM, patches // spaces)
    )
    grads, mixed = temporal(all_attended, upstream, gain, lengths)
    returned = lax.all_to_all(grads, "tm", split_axis=0, concat_axis=0, tiled=True)
    marked = jnp.concatenate(
        [mixed[:, 0], jnp.full((1, HEAD_DIM), task_ids[0].astype(jnp.float32))], axis=0
    )
    gathered = lax.all_gather(marked, ("dp", "tm")).reshape(-1, frames, own + 1, HEAD_DIM)
    clip_tasks = gathered[:, 0, own, 0]
    clip_mixed = gathered[:, :, :own].reshape(-1, 1, feat)
    chosen = clip_tasks[:, None] == jnp.arange(tasks, dtype=jnp.float32)
    task_mixed = jnp.sum(jnp.where(chosen[:, :, None], clip_mixed, 0.0), axis=0)
    grad_gains = jnp.stack([gains[1] * task_mixed, gains[0] * task_mixed])
    grad_queries, grad_keys = backward(
        queries, key_rows, values, weights, returned.reshape(heads, HEAD_DIM, patches), own
    )
    return (
        grad_queries.reshape(query_heads.shape),
        grad_keys.reshape(query_heads.shape),
        grad_gains,
    )


def temporal_grads(attended, upstream, gain_query, gain_keys, length):
    highest = lax.Precision.HIGHEST
    frames = attended.shape[0]
    score_scale = attended.shape[-1] ** (-0.5)
    floats = attended.astype(jnp.float32)
    inverse_rms = lax.rsqrt(jnp.mean(floats * floats, axis=-1, keepdims=True) + 1e-06)
    normed = floats * inverse_rms
    t_query = normed * gain_query
    t_keys = normed * gain_keys
    scores = jnp.einsum("txhd,uxhd->xhtu", t_query, t_keys, precision=highest) * score_scale
    frame_ids = jnp.arange(frames, dtype=jnp.int32)
    allowed = (frame_ids[None, :] <= frame_ids[:, None]) & (frame_ids[None, :] < length)
    scores = jnp.where(allowed, scores, -1e30)
    weights = jax.nn.softmax(scores, axis=-1)
    weights_low = lax.optimization_barrier(weights.astype(jnp.bfloat16)).astype(jnp.float32)
    valid_rows = (frame_ids < length).astype(jnp.float32)
    masked = upstream.astype(jnp.float32) * valid_rows[:, None, None, None]
    grad_weights = jnp.einsum("txhd,uxhd->xhtu", masked, floats, precision=highest)
    from_values = jnp.einsum("xhtu,txhd->uxhd", weights_low, masked, precision=highest)
    grad_scores = (
        weights
        * (grad_weights - jnp.sum(grad_weights * weights, axis=-1, keepdims=True))
        * score_scale
    )
    grad_tquery = jnp.einsum("xhtu,uxhd->txhd", grad_scores, t_keys, precision=highest)
    grad_tkeys = jnp.einsum("xhtu,txhd->uxhd", grad_scores, t_query, precision=highest)
    grad_normed = grad_tquery * gain_query + grad_tkeys * gain_keys
    grad_gain_query = jnp.sum(grad_tquery * normed, axis=(0, 1))
    grad_gain_keys = jnp.sum(grad_tkeys * normed, axis=(0, 1))
    from_norm = inverse_rms * (
        grad_normed - normed * jnp.mean(grad_normed * normed, axis=-1, keepdims=True)
    )
    grad_total = (masked + from_values + from_norm).astype(jnp.bfloat16)
    return (grad_total, grad_gain_query, grad_gain_keys)


def split_by_patches(query_heads, key_heads, value_heads, cotangent, task_ids, lengths, gains):
    patches, feat = query_heads.shape[2:]
    heads = feat // HEAD_DIM
    queries, key_rows, values = (
        field.reshape(patches, feat) for field in (query_heads, key_heads, value_heads)
    )
    weights, attended = forward(queries, key_rows, values, 1)
    attended_field = jnp.transpose(attended, (2, 0, 1)).reshape(1, 1, patches, feat)
    upstream = lax.all_to_all(
        lax.all_to_all(cotangent, "space", split_axis=3, concat_axis=2, tiled=True),
        "tm",
        split_axis=2,
        concat_axis=1,
        tiled=True,
    )
    frames_attended = lax.all_to_all(attended_field, "tm", split_axis=2, concat_axis=1, tiled=True)
    frames, local_patches = frames_attended.shape[1:3]
    selector = (task_ids[0] == jnp.arange(gains.shape[1], dtype=jnp.int32)).astype(jnp.float32)
    gain_query = jnp.sum(selector[:, None] * gains[0], axis=0).reshape(heads, HEAD_DIM)
    gain_keys = jnp.sum(selector[:, None] * gains[1], axis=0).reshape(heads, HEAD_DIM)
    grad_total, grad_gq, grad_gk = temporal_grads(
        frames_attended.reshape(frames, local_patches, heads, HEAD_DIM),
        upstream.reshape(frames, local_patches, heads, HEAD_DIM),
        gain_query,
        gain_keys,
        lengths[0],
    )
    gain_terms = jnp.stack(
        [
            selector[:, None] * grad_gq.reshape(1, feat),
            selector[:, None] * grad_gk.reshape(1, feat),
        ]
    )
    grad_gains = lax.psum(gain_terms, ("dp", "tm"))
    returned = lax.all_to_all(
        grad_total.reshape(1, frames, local_patches, feat),
        "tm",
        split_axis=1,
        concat_axis=2,
        tiled=True,
    )
    head_grads = jnp.transpose(returned.reshape(patches, heads, HEAD_DIM), (1, 2, 0))
    grad_queries, grad_keys = backward(queries, key_rows, values, weights, head_grads, 1)
    return (
        grad_queries.reshape(query_heads.shape),
        grad_keys.reshape(query_heads.shape),
        grad_gains,
    )


def solution(mesh):
    frames, spaces = mesh.shape["tm"], mesh.shape["space"]

    def local(query_heads, *others):
        heads = query_heads.shape[3] // HEAD_DIM
        if frames <= 4 and heads % frames == 0:
            return split_by_heads(query_heads, *others, frames, spaces)
        return split_by_patches(query_heads, *others)

    return jax.shard_map(
        local,
        mesh=mesh,
        in_specs=(
            P("dp", "tm", None, "space"),
            P("dp", "tm", None, "space"),
            P("dp", "tm", None, "space"),
            P("dp", "tm", "space", None),
            P("dp"),
            P("dp"),
            P(None, None, "space"),
        ),
        out_specs=(
            P("dp", "tm", None, "space"),
            P("dp", "tm", None, "space"),
            P(None, None, "space"),
        ),
        check_vma=False,
    )
```

profile of v0, /device:TPU:0, one launch (start us, length us, event | category | flops | bytes accessed | tf_op | source)
XLA Modules:
  0.0 119.0 jit_solution(15573092917503363539)
XLA Ops:
  0.6 0.0 copy-start
  0.6 1.1 copy-done
  1.8 1.1 copy-done.2
  2.9 1.1 copy-done.4
  4.0 5.7 %spatial_forward.1 = (f32[12,256,256]{2,1,0:T(8,128)}, bf16[12,128,256]{2,1,0:T(8,128)(2,1)}) custom-call(bf16[256,1536]{1,0:T(8,128)(2,1)S(1)} %bitcast.27, bf16[256,1536]{1,0:T(8,128)(2,1)S(1)} %bitcast.29, bf16[256,1536]{1,0:T(8,128)(2,1)S(1)} %bitcast.31), custom_call_target="tpu_custom_call" | custom-call | flops 402653184 | bytes 6291456 | tf_op jit(solution)/shard_map/spatial_forward/pallas_call | solution.py:46
  9.8 6.3 %all-to-all-start = ((bf16[4,3,128,256]{3,2,1,0:T(8,128)(2,1)}), bf16[4,3,128,256]{3,2,1,0:T(8,128)(2,1)S(1)}, u32[]{:S(2)}, u32[]{:S(2)}) async-start(bf16[4,3,128,256]{3,2,1,0:T(8,128)(2,1)} %bitcast.3), calls=%async_computation | async-start | bytes 1572864 | tf_op jit(solution)/shard_map/all_to_all | solution.py:276
  16.1 0.0 copy-done.6
  16.1 3.1 %turn_cotangent.1 = bf16[4,2,3,128,128]{4,3,2,1,0:T(8,128)(2,1)} custom-call(bf16[128,3072]{1,0:T(8,128)(2,1)S(1)} %bitcast.33), custom_call_target="tpu_custom_call" | custom-call | bytes 1572864 | tf_op jit(solution)/shard_map/turn_cotangent/pallas_call | solution.py:116
  19.2 17.0 %all-to-all-done.attended_ref = bf16[4,3,128,256]{3,2,1,0:T(8,128)(2,1)S(1)} async-done(((bf16[4,3,128,256]{3,2,1,0:T(8,128)(2,1)}), bf16[4,3,128,256]{3,2,1,0:T(8,128)(2,1)S(1)}, u32[]{:S(2)}, u32[]{:S(2)}) %all-to-all-start) | async-done | bytes 786464 | tf_op jit(solution)/shard_map/all_to_all | solution.py:276
  36.2 4.3 %all-to-all-start.1 = ((bf16[8,3,128,128]{3,2,1,0:T(8,128)(2,1)}), bf16[8,3,128,128]{3,2,1,0:T(8,128)(2,1)}, u32[]{:S(2)}, u32[]{:S(2)}) async-start(bf16[8,3,128,128]{3,2,1,0:T(8,128)(2,1)} %bitcast.5), calls=%async_computation.1 | async-start | bytes 1572864 | tf_op jit(solution)/shard_map/all_to_all | solution.py:268
  41.9 0.1 fusion
  42.0 18.3 %all-to-all-done.1 = bf16[8,3,128,128]{3,2,1,0:T(8,128)(2,1)} async-done(((bf16[8,3,128,128]{3,2,1,0:T(8,128)(2,1)}), bf16[8,3,128,128]{3,2,1,0:T(8,128)(2,1)}, u32[]{:S(2)}, u32[]{:S(2)}) %all-to-all-start.1) | async-done | bytes 786464 | tf_op jit(solution)/shard_map/all_to_all | solution.py:268
  60.3 0.1 broadcast_in_dim.33.gain_ref
  60.4 5.0 %temporal.1 = (bf16[4,3,128,256]{3,2,1,0:T(8,128)(2,1)S(1)}, f32[3,8,128]{2,1,0:T(8,128)S(1)}) custom-call(s32[1]{0:T(128)S(6)} %copy.15.length_ref, bf16[4,3,128,256]{3,2,1,0:T(8,128)(2,1)S(1)} %all-to-all-done.attended_ref, bf16[4,2,3,128,128]{4,3,2,1,0:T(8,128)(2,1)} %bitcast.6.upstream_ref, f32[3,128,128]{2,1,0:T(8,128)S(1)} %broadcast_in_dim.33.gain_ref), custom_call_target="tpu_custom_call" | custom-call | flops 19660800 | bytes 2359296 | tf_op jit(solution)/shard_map/temporal/pallas_call | solution.py:231
  65.4 0.0 copy-start.7
  65.4 0.9 copy-done.7
  66.3 3.5 %all-to-all-start.2 = ((bf16[4,3,128,256]{3,2,1,0:T(8,128)(2,1)}), bf16[4,3,128,256]{3,2,1,0:T(8,128)(2,1)S(1)}, u32[]{:S(2)}, u32[]{:S(2)}) async-start(bf16[4,3,128,256]{3,2,1,0:T(8,128)(2,1)} %copy-done.7), calls=%async_computation.2 | async-start | bytes 1572864 | tf_op jit(solution)/shard_map/all_to_all | solution.py:287
  69.8 41.8 %all-gather.1 = f32[16,4,128]{2,1,0:T(4,128)S(1)} all-gather(f32[1,4,128]{2,1,0:T(4,128)S(1)} %pad_bitcast_fusion), channel_id=2, replica_groups=mesh['dp'=4,'tm'=4,'space'=2] {'dp','tm'}, dimensions={0}, use_global_device_ids=true | all-gather | bytes 34816 | tf_op jit(solution)/shard_map/all_gather | solution.py:291
  111.6 0.1 slice_reduce_fusion
  111.7 0.1 iota_compare_fusion
  111.8 0.1 select_reduce_fusion
  111.9 0.7 pad_maximum_fusion
  112.6 0.0 all-to-all-done.2
  112.6 6.4 %spatial_backward.1 = (bf16[256,1536]{1,0:T(8,128)(2,1)}, bf16[256,1536]{1,0:T(8,128)(2,1)}) custom-call(bf16[256,1536]{1,0:T(8,128)(2,1)S(1)} %bitcast.28, bf16[256,1536]{1,0:T(8,128)(2,1)S(1)} %bitcast.30, bf16[256,1536]{1,0:T(8,128)(2,1)S(1)} %bitcast.32, f32[12,256,256]{2,1,0:T(8,128)} %get-tuple-element.9.weights_ref, bf16[12,128,256]{2,1,0:T(8,128)(2,1)S(1)} %bitcast.26), custom_call_target="tpu_custom_call" | custom-call | flops 603979776 | bytes 7864320 | tf_op jit(solution)/shard_map/spatial_backward/pallas_call | solution.py:85
  (16 shorter events, 0.1 us)
Async XLA Ops:
  0.6 1.1 copy-start
  1.8 1.1 copy-start.2
  2.9 1.1 copy-start.4
  4.0 12.0 %copy-start.6 = (bf16[1,1,128,3072]{3,2,1,0:T(8,128)(2,1)S(1)}, bf16[1,1,128,3072]{3,2,1,0:T(8,128)(2,1)}, u32[]{:S(2)}) copy-start(bf16[1,1,128,3072]{3,2,1,0:T(8,128)(2,1)} %param.10) | copy-start | bytes 2359300
  4.0 37.8 %copy-start.8 = (f32[2,16,1536]{2,1,0:T(8,128)S(1)}, f32[2,16,1536]{2,1,0:T(8,128)}, u32[]{:S(2)}) copy-start(f32[2,16,1536]{2,1,0:T(8,128)} %param.13) | copy-start | bytes 589828
  9.8 26.4 %all-to-all-start = ((bf16[4,3,128,256]{3,2,1,0:T(8,128)(2,1)}), bf16[4,3,128,256]{3,2,1,0:T(8,128)(2,1)S(1)}, u32[]{:S(2)}, u32[]{:S(2)}) async-start(bf16[4,3,128,256]{3,2,1,0:T(8,128)(2,1)} %bitcast.3), calls=%async_computation | async-start | bytes 1572864 | tf_op jit(solution)/shard_map/all_to_all | solution.py:276
  36.2 76.4 %copy-start.1 = (bf16[1,1,256,1536]{3,2,1,0:T(8,128)(2,1)S(1)}, bf16[1,1,256,1536]{3,2,1,0:T(8,128)(2,1)}, u32[]{:S(2)}) copy-start(bf16[1,1,256,1536]{3,2,1,0:T(8,128)(2,1)} %param.7) | copy-start | bytes 2359300
  36.2 76.4 %copy-start.3 = (bf16[1,1,256,1536]{3,2,1,0:T(8,128)(2,1)S(1)}, bf16[1,1,256,1536]{3,2,1,0:T(8,128)(2,1)}, u32[]{:S(2)}) copy-start(bf16[1,1,256,1536]{3,2,1,0:T(8,128)(2,1)} %param.8) | copy-start | bytes 2359300
  36.2 76.4 %copy-start.5 = (bf16[1,1,256,1536]{3,2,1,0:T(8,128)(2,1)S(1)}, bf16[1,1,256,1536]{3,2,1,0:T(8,128)(2,1)}, u32[]{:S(2)}) copy-start(bf16[1,1,256,1536]{3,2,1,0:T(8,128)(2,1)} %param.9) | copy-start | bytes 2359300
  36.2 24.1 %all-to-all-start.1 = ((bf16[8,3,128,128]{3,2,1,0:T(8,128)(2,1)}), bf16[8,3,128,128]{3,2,1,0:T(8,128)(2,1)}, u32[]{:S(2)}, u32[]{:S(2)}) async-start(bf16[8,3,128,128]{3,2,1,0:T(8,128)(2,1)} %bitcast.5), calls=%async_computation.1 | async-start | bytes 1572864 | tf_op jit(solution)/shard_map/all_to_all | solution.py:268
  65.4 0.9 copy-start.7
  66.3 46.3 %all-to-all-start.2 = ((bf16[4,3,128,256]{3,2,1,0:T(8,128)(2,1)}), bf16[4,3,128,256]{3,2,1,0:T(8,128)(2,1)S(1)}, u32[]{:S(2)}, u32[]{:S(2)}) async-start(bf16[4,3,128,256]{3,2,1,0:T(8,128)(2,1)} %copy-done.7), calls=%async_computation.2 | async-start | bytes 1572864 | tf_op jit(solution)/shard_map/all_to_all | solution.py:287
where the time goes:
time: 120 us; the launch traced here: 119 us
  blocking collectives  41.8 us (35%)
  waiting for transfers between devices  35.4 us (30%)
  Pallas kernels  20.1 us (17%)
  starting transfers between devices  14.2 us (12%)
  local copies, waits for them, and re-layouts  4.55 us (4%)
  between operations  2.03 us (2%)
    all_gather x1, blocking collectives, split_by_heads(): lax.all_gather(marked, ('dp', 'tm')).reshape(-1, frames, own + 1, HEAD_DIM)  41.8 us
    all_to_all x1, waiting for transfers between devices, split_by_heads(): lax.all_to_all(turned.reshape((frames * spaces,) + turned.shape[2:]), ('t...  18.3 us
    all_to_all x1, waiting for transfers between devices, split_by_heads(): lax.all_to_all(attended.reshape(frames, own, HEAD_DIM, patches), 'tm', sp...  17 us
    pallas_call x1, Pallas kernels, backward(): pl.pallas_call(backward_kernel, grid=(heads // per_step,), in_specs=[fiel...  6.36 us
    all_to_all x1, starting transfers between devices, split_by_heads(): lax.all_to_all(attended.reshape(frames, own, HEAD_DIM, patches), 'tm', sp...  6.32 us
    pallas_call x1, Pallas kernels, forward(): pl.pallas_call(forward_kernel, grid=(heads // per_step,), in_specs=[field...  5.71 us
    pallas_call x1, Pallas kernels, temporal(): pl.pallas_call(temporal_kernel, grid=(heads, spaces), in_specs=[pl.BlockS...  4.98 us
    all_to_all x1, starting transfers between devices, split_by_heads(): lax.all_to_all(turned.reshape((frames * spaces,) + turned.shape[2:]), ('t...  4.35 us
  transfers between devices with their start and end apart: 3, of which 2 were waited for; matrix products, arithmetic and copies ran while one was open for 1% of the time, Pallas kernels for 3%

commit v1 on v0

v1 whole, which is shorter than its diff:
```python
import functools

import jax
import jax.numpy as jnp
from jax import lax
from jax.experimental import pallas as pl
from jax.experimental.pallas import tpu as pltpu
from jax.sharding import PartitionSpec as P

HEAD_DIM = 128
GROUP = 16
VMEM_BYTES = 48 * 1024 * 1024


def params():
    return pltpu.CompilerParams(vmem_limit_bytes=VMEM_BYTES)


def columns_dot(left, right):
    return lax.dot_general(
        left, right, (((1,), (1,)), ((), ())), preferred_element_type=jnp.float32
    )


def dot(left, right):
    return jnp.dot(left, right, preferred_element_type=jnp.float32)


def partner(scalars, distance):
    return jnp.bitwise_xor(scalars[0], distance)


def forward_kernel(scalars, query_ref, key_ref, value_ref, weights_ref, *attended_refs):
    score_scale = HEAD_DIM ** (-0.5)
    pieces = []
    for head in range(weights_ref.shape[0]):
        cols = pl.ds(head * HEAD_DIM, HEAD_DIM)
        scores = columns_dot(key_ref[:, cols], query_ref[:, cols])
        largest = jnp.max(scores, axis=0, keepdims=True)
        raised = jnp.exp((scores - largest) * score_scale)
        weights = raised * (1.0 / jnp.sum(raised, axis=0, keepdims=True))
        weights_ref[head] = weights
        attended = dot(value_ref[:, cols].T, weights.astype(jnp.bfloat16))
        pieces.append(attended.astype(jnp.bfloat16))
    for step, attended_ref in enumerate(attended_refs):

        @pl.when(pl.program_id(0) == step)
        def _():
            for head, piece in enumerate(pieces):
                attended_ref[head] = piece


def forward(scalars, queries, key_rows, values, groups):
    patches, feat = queries.shape
    heads = feat // HEAD_DIM
    own = heads // groups
    field = pl.BlockSpec((patches, own * HEAD_DIM), lambda d, sc: (0, partner(sc, d)))
    whole = pl.BlockSpec((own, HEAD_DIM, patches), lambda d, sc: (0, 0, 0))
    weights, *attended = pl.pallas_call(
        forward_kernel,
        grid_spec=pltpu.PrefetchScalarGridSpec(
            num_scalar_prefetch=1,
            grid=(groups,),
            in_specs=[field] * 3,
            out_specs=[pl.BlockSpec((own, patches, patches), lambda d, sc: (d, 0, 0))]
            + [whole] * groups,
        ),
        out_shape=[jax.ShapeDtypeStruct((heads, patches, patches), jnp.float32)]
        + [jax.ShapeDtypeStruct((own, HEAD_DIM, patches), jnp.bfloat16)] * groups,
        compiler_params=params(),
        cost_estimate=pl.CostEstimate(
            flops=4 * heads * patches * patches * HEAD_DIM,
            bytes_accessed=heads * patches * (patches * 4 + 8 * HEAD_DIM),
            transcendentals=heads * patches * patches,
        ),
        name="spatial_forward",
    )(scalars, queries, key_rows, values)
    return weights, attended


def backward_kernel(scalars, query_ref, key_ref, value_ref, weights_ref, grad_ref, *refs):
    gq_ref, gk_ref = refs[-2:]
    score_scale = HEAD_DIM ** (-0.5)
    for head in range(weights_ref.shape[0]):
        cols = pl.ds(head * HEAD_DIM, HEAD_DIM)
        weights = weights_ref[head]
        spatial_grad = dot(value_ref[:, cols], grad_ref[head])
        row_sum = jnp.sum(spatial_grad * weights, axis=0, keepdims=True)
        scores = (weights * (spatial_grad - row_sum) * score_scale).astype(jnp.bfloat16)
        gk_ref[:, cols] = dot(scores, query_ref[:, cols]).astype(jnp.bfloat16)
        grad_query = dot(key_ref[:, cols].T, scores).astype(jnp.bfloat16)
        gq_ref[:, cols] = grad_query.T


def backward(scalars, queries, key_rows, values, weights, grads, distance, earlier):
    patches, feat = queries.shape
    own = grads.shape[0]
    field = pl.BlockSpec(
        (patches, HEAD_DIM), lambda i, sc: (0, partner(sc, distance) * own + i)
    )
    return pl.pallas_call(
        backward_kernel,
        grid_spec=pltpu.PrefetchScalarGridSpec(
            num_scalar_prefetch=1,
            grid=(own,),
            in_specs=[
                field,
                field,
                field,
                pl.BlockSpec((1, patches, patches), lambda i, sc: (distance * own + i, 0, 0)),
                pl.BlockSpec((1, HEAD_DIM, patches), lambda i, sc: (i, 0, 0)),
            ]
            + [pl.BlockSpec(memory_space=pl.ANY)] * len(earlier),
            out_specs=[field, field],
        ),
        out_shape=[jax.ShapeDtypeStruct((patches, feat), jnp.bfloat16)] * 2,
        input_output_aliases={6 + index: index for index in range(len(earlier))},
        compiler_params=params(),
        cost_estimate=pl.CostEstimate(
            flops=6 * own * patches * patches * HEAD_DIM,
            bytes_accessed=own * patches * (patches * 4 + 12 * HEAD_DIM),
            transcendentals=0,
        ),
        name="spatial_backward",
    )(scalars, queries, key_rows, values, weights, grads, *earlier)


def turn_kernel(spaces, scalars, *refs):
    turned_ref = refs[-1]
    for index, ref in enumerate(refs[:-1]):
        frame = partner(scalars, index // spaces)
        part = jnp.bitwise_xor(scalars[1], index % spaces)
        turned_ref[frame, part, 0] = ref[...].T


def turn(scalars, pieces, frames, spaces):
    patches, feat = pieces[0].shape
    heads = feat // HEAD_DIM
    return pl.pallas_call(
        functools.partial(turn_kernel, spaces),
        grid_spec=pltpu.PrefetchScalarGridSpec(
            num_scalar_prefetch=1,
            grid=(heads,),
            in_specs=[pl.BlockSpec((patches, HEAD_DIM), lambda i, sc: (0, i))] * len(pieces),
            out_specs=pl.BlockSpec(
                (frames, spaces, 1, HEAD_DIM, patches), lambda i, sc: (0, 0, i, 0, 0)
            ),
        ),
        out_shape=jax.ShapeDtypeStruct((frames, spaces, heads, HEAD_DIM, patches), jnp.bfloat16),
        compiler_params=params(),
        cost_estimate=pl.CostEstimate(
            flops=0, bytes_accessed=4 * len(pieces) * patches * feat, transcendentals=0
        ),
        name="turn_cotangent",
    )(scalars, *pieces)


def temporal_part(length, attended_ref, upstream_ref, gain_ref, grad_ref, mixed_sum, part):
    frames, feat, _ = attended_ref.shape
    lanes = upstream_ref.shape[-1]
    here = pl.ds(part * lanes, lanes)
    half = GROUP // 2
    score_scale = feat ** (-0.5)
    pairs = [(t, u) for t in range(frames) for u in range(t + 1)]
    every = range(frames)
    valid = [jnp.where(t < length, 1.0, 0.0).astype(jnp.float32) for t in every]
    bias = [jnp.where(u < length, 0.0, -1e30).astype(jnp.float32) for u in every]

    def split(block):
        block = block.astype(jnp.float32)
        return block[:half], block[half:]

    def load_fields(group):
        return [split(attended_ref[t, pl.ds(group * GROUP, GROUP), here]) for t in every]

    def load_ups(group):
        return [split(upstream_ref[t, part, 0, pl.ds(group * GROUP, GROUP), :]) for t in every]

    def total(piece):
        return jnp.broadcast_to(jnp.sum(piece, axis=0, keepdims=True), (half, lanes))

    squares = [jnp.zeros((half, lanes), jnp.float32) for _ in every]
    for group in range(feat // GROUP):
        for t, (low, high) in enumerate(load_fields(group)):
            squares[t] = squares[t] + (low * low + high * high)
    inverse = [lax.rsqrt(total(squares[t]) * (1.0 / feat) + 1e-06) for t in every]

    raw = {pair: jnp.zeros((half, lanes), jnp.float32) for pair in pairs}
    grad = {pair: jnp.zeros((half, lanes), jnp.float32) for pair in pairs}
    for group in range(feat // GROUP):
        fields, ups = load_fields(group), load_ups(group)
        for side in range(2):
            gain = gain_ref[0, pl.ds(group * GROUP + side * half, half), :]
            normed = [fields[t][side] * inverse[t] for t in every]
            gained = [normed[t] * gain for t in every]
            for t, u in pairs:
                raw[t, u] = raw[t, u] + gained[t] * normed[u]
                grad[t, u] = grad[t, u] + ups[t][side] * fields[u][side]

    value_part, score_part = {}, {}
    for t in every:
        seen = range(t + 1)
        for u in seen:
            raw[t, u] = total(raw[t, u])
            grad[t, u] = total(grad[t, u]) * valid[t]
        scores = [raw[t, u] * score_scale + bias[u] for u in seen]
        largest = functools.reduce(jnp.maximum, scores)
        raised = [jnp.exp(score - largest) for score in scores]
        over = 1.0 / functools.reduce(jnp.add, raised)
        weights = [piece * over for piece in raised]
        mean_grad = functools.reduce(jnp.add, [weights[u] * grad[t, u] for u in seen])
        for u in seen:
            rounded = weights[u].astype(jnp.bfloat16).astype(jnp.float32)
            value_part[t, u] = (rounded + (1.0 if u == t else 0.0)) * valid[t]
            score_part[t, u] = weights[u] * (grad[t, u] - mean_grad) * score_scale

    both = {(t, u): score_part[t, u] * (2.0 if t == u else 1.0) for t, u in pairs}
    both.update({(u, t): both[t, u] for t, u in pairs})
    raw.update({(u, t): raw[t, u] for t, u in pairs})
    mean_part = [
        functools.reduce(jnp.add, [both[u, v] * raw[u, v] for v in every]) * (1.0 / feat)
        for u in every
    ]

    for group in range(feat // GROUP):
        fields, ups = load_fields(group), load_ups(group)
        outs = [[] for _ in every]
        for side in range(2):
            rows = pl.ds(group * GROUP + side * half, half)
            gain = gain_ref[0, rows, :]
            normed = [fields[t][side] * inverse[t] for t in every]
            mixed = jnp.zeros((half, lanes), jnp.float32)
            for u in every:
                crossed = functools.reduce(jnp.add, [both[u, v] * normed[v] for v in every])
                mixed = mixed + crossed * normed[u]
                from_norm = inverse[u] * (gain * crossed - normed[u] * mean_part[u])
                direct = functools.reduce(
                    jnp.add, [value_part[t, u] * ups[t][side] for t in range(u, frames)]
                )
                outs[u].append(direct + from_norm)
            mixed_sum[rows, :] = mixed if part == 0 else mixed_sum[rows, :] + mixed
        for u in every:
            grad_ref[u, pl.ds(group * GROUP, GROUP), here] = jnp.concatenate(
                outs[u], axis=0
            ).astype(jnp.bfloat16)


def temporal_kernel(frames, scalars, *refs):
    attended_refs, (upstream_ref, gain_ref) = refs[:frames], refs[frames : frames + 2]
    grad_refs, mixed_ref = refs[frames + 2 : 2 * frames + 2], refs[2 * frames + 2]
    attended, grads, mixed_sum = refs[2 * frames + 3 :]
    head = pl.program_id(0)
    for distance, ref in enumerate(attended_refs):
        attended[partner(scalars, distance)] = ref[0]
    for part in range(upstream_ref.shape[1]):
        temporal_part(scalars[2], attended, upstream_ref, gain_ref, grads, mixed_sum, part)
    for distance, ref in enumerate(grad_refs):
        ref[0] = grads[partner(scalars, distance)]

    @pl.when(head == 0)
    def _():
        mixed_ref[...] = jnp.full(mixed_ref.shape, scalars[3].astype(jnp.float32))

    mixed_ref[pl.ds(head, 1), :] = jnp.sum(mixed_sum[...].T, axis=0, keepdims=True) * 0.5


def temporal(scalars, attended, upstream, gain):
    frames, spaces, heads, feat, lanes = upstream.shape
    patches = spaces * lanes
    rows = -(-(heads + 1) // 8) * 8
    plane = pl.BlockSpec((1, feat, patches), lambda i, sc: (i, 0, 0))
    *grads, mixed = pl.pallas_call(
        functools.partial(temporal_kernel, frames),
        grid_spec=pltpu.PrefetchScalarGridSpec(
            num_scalar_prefetch=1,
            grid=(heads,),
            in_specs=[plane] * frames
            + [
                pl.BlockSpec((frames, spaces, 1, feat, lanes), lambda i, sc: (0, 0, i, 0, 0)),
                pl.BlockSpec((1, feat, lanes), lambda i, sc: (i, 0, 0)),
            ],
            out_specs=[plane] * frames + [pl.BlockSpec((rows, feat), lambda i, sc: (0, 0))],
            scratch_shapes=[
                pltpu.VMEM((frames, feat, patches), jnp.bfloat16),
                pltpu.VMEM((frames, feat, patches), jnp.bfloat16),
                pltpu.VMEM((feat, lanes), jnp.float32),
            ],
        ),
        out_shape=[jax.ShapeDtypeStruct((heads, feat, patches), jnp.bfloat16)] * frames
        + [jax.ShapeDtypeStruct((rows, feat), jnp.float32)],
        compiler_params=params(),
        cost_estimate=pl.CostEstimate(
            flops=heads * patches * feat * 200,
            bytes_accessed=6 * frames * heads * patches * feat,
            transcendentals=heads * patches * 16,
        ),
        name="temporal",
    )(scalars, *attended, upstream, gain)
    return grads, mixed


def gains_kernel(heads, frames, scalars, *refs):
    mixed_refs, gains_ref, grad_ref = refs[:-2], refs[-2], refs[-1]
    tasks = gains_ref.shape[1]
    rows = mixed_refs[0].shape[0] // frames
    task_ids = lax.broadcasted_iota(jnp.int32, (tasks, HEAD_DIM), 0).astype(jnp.float32)
    for distance in range(frames):
        for head in range(heads):
            mixed = jnp.zeros((tasks, HEAD_DIM), jnp.float32)
            for ref in mixed_refs:
                task = ref[pl.ds(distance * rows + heads, 1), :]
                row = ref[pl.ds(distance * rows + head, 1), :]
                mixed = mixed + jnp.where(task_ids == task, row, 0.0)
            start = (partner(scalars, distance) * heads + head) * HEAD_DIM
            cols = pl.ds(pl.multiple_of(start, HEAD_DIM), HEAD_DIM)
            grad_ref[0, :, cols] = gains_ref[1, :, cols] * mixed
            grad_ref[1, :, cols] = gains_ref[0, :, cols] * mixed


def gain_gradients(scalars, mixed, gains, heads, frames):
    return pl.pallas_call(
        functools.partial(gains_kernel, heads, frames),
        in_specs=[pl.BlockSpec(memory_space=pltpu.SMEM)]
        + [pl.BlockSpec(memory_space=pltpu.VMEM)] * (len(mixed) + 1),
        out_specs=pl.BlockSpec(memory_space=pltpu.VMEM),
        out_shape=jax.ShapeDtypeStruct(gains.shape, jnp.float32),
        compiler_params=params(),
        name="gain_gradients",
    )(scalars, *mixed, gains)


def swap(field, axis, size, distance):
    return lax.ppermute(field, axis, [(i, i ^ distance) for i in range(size)])


def split_by_heads(
    query_heads, key_heads, value_heads, cotangent, task_ids, lengths, gains, clips, frames, spaces
):
    patches, feat = query_heads.shape[2:]
    heads = feat // HEAD_DIM
    own = heads // frames
    width = own * HEAD_DIM
    queries, key_rows, values = (
        field.reshape(patches, feat) for field in (query_heads, key_heads, value_heads)
    )
    frame, space = lax.axis_index("tm"), lax.axis_index("space")
    scalars = jnp.stack([frame, space, lengths[0], task_ids[0]]).astype(jnp.int32)

    incoming = cotangent.reshape(cotangent.shape[2:])
    pieces = []
    for distance in range(frames * spaces):
        block = (space ^ (distance % spaces)) * frames + (frame ^ (distance // spaces))
        piece = lax.dynamic_slice_in_dim(incoming, block * width, width, 1)
        if distance:
            piece = swap(piece, ("tm", "space"), frames * spaces, distance)
        pieces.append(piece)
    weights, attended = forward(scalars, queries, key_rows, values, frames)
    attended = [attended[0]] + [
        swap(attended[distance], "tm", frames, distance) for distance in range(1, frames)
    ]
    upstream = turn(scalars, pieces, frames, spaces)
    rows = lax.dynamic_index_in_dim(gains, task_ids[0], 1, keepdims=False)
    product = lax.dynamic_slice_in_dim(rows[0] * rows[1], frame * width, width, 0)
    gain = jnp.broadcast_to(
        product.reshape(own, HEAD_DIM, 1), (own, HEAD_DIM, patches // spaces)
    )
    grads, mixed = temporal(scalars, attended, upstream, gain)
    grads = [grads[0]] + [
        swap(grads[distance], "tm", frames, distance) for distance in range(1, frames)
    ]
    mixed = jnp.concatenate(
        [mixed] + [swap(mixed, "tm", frames, distance) for distance in range(1, frames)], axis=0
    )
    mixed = [mixed] + [swap(mixed, "dp", clips, distance) for distance in range(1, clips)]
    grad_gains = gain_gradients(scalars, mixed, gains, own, frames)
    results = ()
    for distance in range(frames):
        results = backward(
            scalars, queries, key_rows, values, weights, grads[distance], distance, results
        )
    grad_queries, grad_keys = results
    return (
        grad_queries.reshape(query_heads.shape),
        grad_keys.reshape(query_heads.shape),
        grad_gains,
    )


def temporal_grads(attended, upstream, gain_query, gain_keys, length):
    highest = lax.Precision.HIGHEST
    frames = attended.shape[0]
    score_scale = attended.shape[-1] ** (-0.5)
    floats = attended.astype(jnp.float32)
    inverse_rms = lax.rsqrt(jnp.mean(floats * floats, axis=-1, keepdims=True) + 1e-06)
    normed = floats * inverse_rms
    t_query = normed * gain_query
    t_keys = normed * gain_keys
    scores = jnp.einsum("txhd,uxhd->xhtu", t_query, t_keys, precision=highest) * score_scale
    frame_ids = jnp.arange(frames, dtype=jnp.int32)
    allowed = (frame_ids[None, :] <= frame_ids[:, None]) & (frame_ids[None, :] < length)
    scores = jnp.where(allowed, scores, -1e30)
    weights = jax.nn.softmax(scores, axis=-1)
    weights_low = lax.optimization_barrier(weights.astype(jnp.bfloat16)).astype(jnp.float32)
    valid_rows = (frame_ids < length).astype(jnp.float32)
    masked = upstream.astype(jnp.float32) * valid_rows[:, None, None, None]
    grad_weights = jnp.einsum("txhd,uxhd->xhtu", masked, floats, precision=highest)
    from_values = jnp.einsum("xhtu,txhd->uxhd", weights_low, masked, precision=highest)
    grad_scores = (
        weights
        * (grad_weights - jnp.sum(grad_weights * weights, axis=-1, keepdims=True))
        * score_scale
    )
    grad_tquery = jnp.einsum("xhtu,uxhd->txhd", grad_scores, t_keys, precision=highest)
    grad_tkeys = jnp.einsum("xhtu,txhd->uxhd", grad_scores, t_query, precision=highest)
    grad_normed = grad_tquery * gain_query + grad_tkeys * gain_keys
    grad_gain_query = jnp.sum(grad_tquery * normed, axis=(0, 1))
    grad_gain_keys = jnp.sum(grad_tkeys * normed, axis=(0, 1))
    from_norm = inverse_rms * (
        grad_normed - normed * jnp.mean(grad_normed * normed, axis=-1, keepdims=True)
    )
    grad_total = (masked + from_values + from_norm).astype(jnp.bfloat16)
    return (grad_total, grad_gain_query, grad_gain_keys)


def split_by_patches(query_heads, key_heads, value_heads, cotangent, task_ids, lengths, gains):
    patches, feat = query_heads.shape[2:]
    heads = feat // HEAD_DIM
    queries, key_rows, values = (
        field.reshape(patches, feat) for field in (query_heads, key_heads, value_heads)
    )
    scalars = jnp.zeros((1,), jnp.int32)
    weights, attended = forward(scalars, queries, key_rows, values, heads)
    attended_field = jnp.transpose(jnp.concatenate(attended), (2, 0, 1)).reshape(1, 1, patches, feat)
    upstream = lax.all_to_all(
        lax.all_to_all(cotangent, "space", split_axis=3, concat_axis=2, tiled=True),
        "tm",
        split_axis=2,
        concat_axis=1,
        tiled=True,
    )
    frames_attended = lax.all_to_all(attended_field, "tm", split_axis=2, concat_axis=1, tiled=True)
    frames, local_patches = frames_attended.shape[1:3]
    selector = (task_ids[0] == jnp.arange(gains.shape[1], dtype=jnp.int32)).astype(jnp.float32)
    gain_query = jnp.sum(selector[:, None] * gains[0], axis=0).reshape(heads, HEAD_DIM)
    gain_keys = jnp.sum(selector[:, None] * gains[1], axis=0).reshape(heads, HEAD_DIM)
    grad_total, grad_gq, grad_gk = temporal_grads(
        frames_attended.reshape(frames, local_patches, heads, HEAD_DIM),
        upstream.reshape(frames, local_patches, heads, HEAD_DIM),
        gain_query,
        gain_keys,
        lengths[0],
    )
    gain_terms = jnp.stack(
        [
            selector[:, None] * grad_gq.reshape(1, feat),
            selector[:, None] * grad_gk.reshape(1, feat),
        ]
    )
    grad_gains = lax.psum(gain_terms, ("dp", "tm"))
    returned = lax.all_to_all(
        grad_total.reshape(1, frames, local_patches, feat),
        "tm",
        split_axis=1,
        concat_axis=2,
        tiled=True,
    )
    head_grads = jnp.transpose(returned.reshape(patches, heads, HEAD_DIM), (1, 2, 0))
    grad_queries, grad_keys = backward(
        scalars, queries, key_rows, values, weights, head_grads, 0, ()
    )
    return (
        grad_queries.reshape(query_heads.shape),
        grad_keys.reshape(query_heads.shape),
        grad_gains,
    )


def solution(mesh):
    clips, frames, spaces = (mesh.shape[axis] for axis in ("dp", "tm", "space"))

    def local(query_heads, *others):
        heads = query_heads.shape[3] // HEAD_DIM
        powers = all(size & (size - 1) == 0 for size in (clips, frames, spaces))
        if powers and frames <= 4 and heads % frames == 0:
            return split_by_heads(query_heads, *others, clips, frames, spaces)
        return split_by_patches(query_heads, *others)

    return jax.shard_map(
        local,
        mesh=mesh,
        in_specs=(
            P("dp", "tm", None, "space"),
            P("dp", "tm", None, "space"),
            P("dp", "tm", None, "space"),
            P("dp", "tm", "space", None),
            P("dp"),
            P("dp"),
            P(None, None, "space"),
        ),
        out_specs=(
            P("dp", "tm", None, "space"),
            P("dp", "tm", None, "space"),
            P(None, None, "space"),
        ),
        check_vma=False,
    )
```

time: 120 us -> 94.5 us (0.79)
  blocking collectives: 41.8 us -> 0 us
  waiting for transfers between devices: 35.4 us -> 12.2 us
  starting transfers between devices: 14.2 us -> 36.1 us
  local copies, waits for them, and re-layouts: 4.55 us -> 16.7 us
  Pallas kernels: 20.1 us -> 26.5 us
    all_gather x1 -> x0, blocking collectives: 41.8 us -> none  [split_by_heads(): lax.all_gather(marked, ('dp', 'tm')).reshape(-1, frames, own + 1, HEAD_DIM)]
    ppermute x0 -> x19, starting transfers between devices: none -> 36.1 us  [swap(): return lax.ppermute(field, axis, [(i, i ^ distance) for i in range(size)])]
    all_to_all x3 -> x0, waiting for transfers between devices: 35.4 us -> none  [the longest x1 18.3 us: split_by_heads(): lax.all_to_all(turned.reshape((frames * spaces,) + turned.shape[2:]), ('t...]
    all_to_all x3 -> x0, starting transfers between devices: 14.2 us -> none  [the longest x1 6.32 us: split_by_heads(): lax.all_to_all(attended.reshape(frames, own, HEAD_DIM, patches), 'tm', sp...]
    ppermute x0 -> x19, waiting for transfers between devices: none -> 12.2 us  [swap(): return lax.ppermute(field, axis, [(i, i ^ distance) for i in range(size)])]
    unnamed x20 -> x41, local copies, waits for them, and re-layouts: 4.3 us -> 14.5 us
    pallas_call x4 -> x8, Pallas kernels: 20.1 us -> 26.5 us  [the longest x4 11.6 us: backward(): pl.pallas_call(backward_kernel, grid_spec=pltpu.PrefetchScalarGridSpec(nu...]
    dynamic_slice x0 -> x1, local copies, waits for them, and re-layouts: none -> 2.03 us  [split_by_heads(): piece = lax.dynamic_slice_in_dim(incoming, block * width, width, 1)]
  transfers between devices with their start and end apart: 3 -> 19, of which waited for: 2 -> 3; matrix products, arithmetic and copies ran while one was open for 1% -> 0% of each run, Pallas kernels for 3% -> 21%
where the time goes in v1:
time: 94.5 us; the launch traced here: 93.7 us
  starting transfers between devices  36.1 us (38%)
  Pallas kernels  26.5 us (28%)
  local copies, waits for them, and re-layouts  16.7 us (18%)
  waiting for transfers between devices  12.2 us (13%)
  between operations  2.11 us (2%)
    ppermute x19, starting transfers between devices, swap(): return lax.ppermute(field, axis, [(i, i ^ distance) for i in range(size)])  36.1 us
    unnamed x41, local copies, waits for them, and re-layouts  14.5 us
    ppermute x19, waiting for transfers between devices, swap(): return lax.ppermute(field, axis, [(i, i ^ distance) for i in range(size)])  12.2 us
    pallas_call x4, Pallas kernels, backward(): pl.pallas_call(backward_kernel, grid_spec=pltpu.PrefetchScalarGridSpec(nu...  11.6 us
    pallas_call x1, Pallas kernels, forward(): pl.pallas_call(forward_kernel, grid_spec=pltpu.PrefetchScalarGridSpec(num...  6.75 us
    pallas_call x1, Pallas kernels, temporal(): pl.pallas_call(functools.partial(temporal_kernel, frames), grid_spec=pltp...  4.35 us
    pallas_call x1, Pallas kernels, turn(): pl.pallas_call(functools.partial(turn_kernel, spaces), grid_spec=pltpu.Pr...  2.54 us
    dynamic_slice x1, local copies, waits for them, and re-layouts, split_by_heads(): piece = lax.dynamic_slice_in_dim(incoming, block * width, width, 1)  2.03 us
  transfers between devices with their start and end apart: 19, of which 3 were waited for; matrix products, arithmetic and copies ran while one was open for 0% of the time, Pallas kernels for 21%

profile of v1, /device:TPU:0, one launch (start us, length us, event | category | flops | bytes accessed | tf_op | source)
XLA Modules:
  0.0 93.7 jit_solution(2426086963226873374)
XLA Ops:
  0.7 2.0 %dynamic-slice_bitcast_fusion = (bf16[128,384]{1,0:T(8,128)(2,1)}, bf16[128,384]{1,0:T(8,128)(2,1)S(1)}, bf16[128,384]{1,0:T(8,128)(2,1)S(1)}, bf16[128,384]{1,0...) fusion(bf16[1,1,128,3072]{3,2,1,0:T(8,128)(2,1)} %param.10, ...), kind=kLoop, calls=%fused_computation | loop fusion | bytes 1572896 | tf_op jit(solution)/shard_map/dynamic_slice | solution.py:353
  2.7 3.0 %collective-permute-start.3 = (bf16[128,384]{1,0:T(8,128)(2,1)S(1)}, bf16[128,384]{1,0:T(8,128)(2,1)S(1)}, u32[]{:S(2)}, u32[]{:S(2)}) collective-permute-start(bf16[128,384]{1,0:T(8,128)(2,1)S(1)} %get-tuple-element.44), channel_id=1, source_target_pairs={{0,1},{1,0},{2,3},{3,2},{4,5},{5,4},{6,7},{7,6},{8,9},{9,8},{10,11... | collective-permute-start | bytes 294920 | tf_op jit(solution)/shard_map/ppermute | solution.py:333
  5.7 1.6 %collective-permute-start.4 = (bf16[128,384]{1,0:T(8,128)(2,1)S(1)}, bf16[128,384]{1,0:T(8,128)(2,1)S(1)}, u32[]{:S(2)}, u32[]{:S(2)}) collective-permute-start(bf16[128,384]{1,0:T(8,128)(2,1)S(1)} %get-tuple-element.43), channel_id=1, source_target_pairs={{0,2},{1,3},{2,0},{3,1},{4,6},{5,7},{6,4},{7,5},{8,10},{9,11},{10,... | collective-permute-start | bytes 294920 | tf_op jit(solution)/shard_map/ppermute | solution.py:333
  7.3 3.0 %collective-permute-start.6 = (bf16[128,384]{1,0:T(8,128)(2,1)S(1)}, bf16[128,384]{1,0:T(8,128)(2,1)S(1)}, u32[]{:S(2)}, u32[]{:S(2)}) collective-permute-start(bf16[128,384]{1,0:T(8,128)(2,1)S(1)} %get-tuple-element.41), channel_id=1, source_target_pairs={{0,4},{1,5},{2,6},{3,7},{4,0},{5,1},{6,2},{7,3},{8,12},{9,13},{10,... | collective-permute-start | bytes 294920 | tf_op jit(solution)/shard_map/ppermute | solution.py:333
  10.3 1.3 %collective-permute-start.7 = (bf16[128,384]{1,0:T(8,128)(2,1)S(1)}, bf16[128,384]{1,0:T(8,128)(2,1)S(1)}, u32[]{:S(2)}, u32[]{:S(2)}) collective-permute-start(bf16[128,384]{1,0:T(8,128)(2,1)S(1)} %get-tuple-element.40), channel_id=1, source_target_pairs={{0,5},{1,4},{2,7},{3,6},{4,1},{5,0},{6,3},{7,2},{8,13},{9,12},{10,... | collective-permute-start | bytes 294920 | tf_op jit(solution)/shard_map/ppermute | solution.py:333
  12.9 1.1 %copy-done.1 = bf16[1,1,256,1536]{3,2,1,0:T(8,128)(2,1)S(1)} copy-done((bf16[1,1,256,1536]{3,2,1,0:T(8,128)(2,1)S(1)}, bf16[1,1,256,1536]{3,2,1,0:T(8,128)(2,1)}, u32[]{:S(2)}) %copy-start.1) | copy-done | bytes 786456
  16.3 6.7 %spatial_forward.1 = (f32[12,256,256]{2,1,0:T(8,128)}, bf16[3,128,256]{2,1,0:T(8,128)(2,1)S(1)}, bf16[3,128,256]{2,1,0:T(8,128)(2,1)}, bf16[3,128,256]{2,1,0:T(8,128)(2,1)}, bf16[3,128,256]{2,1,0:T(8,128)(2,1)}) custom-call(s32[4]{0:T(128)S(1)} %pad_add_fusion.scalars, bf16[256,1536]{1,0:T(8,128)(2,1)S(1)} %bitcast.28, bf16[256,1536]{1,0:T(8,128)(2,1)S(1)} %bitcast.33, ...), custom_call_target="tpu_custom_call" | custom-call | flops 402653184 | bytes 6291456 | tf_op jit(solution)/shard_map/spatial_forward/pallas_call | solution.py:59
  23.8 1.6 %collective-permute-start = (bf16[3,128,256]{2,1,0:T(8,128)(2,1)}, bf16[3,128,256]{2,1,0:T(8,128)(2,1)}, u32[]{:S(2)}, u32[]{:S(2)}) collective-permute-start(bf16[3,128,256]{2,1,0:T(8,128)(2,1)} %get-tuple-element.23), channel_id=1, source_target_pairs={{0,2},{2,0},{4,6},{6,4},{1,3},{3,1},{5,7},{7,5},{8,10},{10,8},{12,... | collective-permute-start | bytes 589832 | tf_op jit(solution)/shard_map/ppermute | solution.py:333
  26.0 2.6 %collective-permute-start.1 = (bf16[3,128,256]{2,1,0:T(8,128)(2,1)}, bf16[3,128,256]{2,1,0:T(8,128)(2,1)}, u32[]{:S(2)}, u32[]{:S(2)}) collective-permute-start(bf16[3,128,256]{2,1,0:T(8,128)(2,1)} %get-tuple-element.24), channel_id=1, source_target_pairs={{0,4},{2,6},{4,0},{6,2},{1,5},{3,7},{5,1},{7,3},{8,12},{10,14},{12... | collective-permute-start | bytes 589832 | tf_op jit(solution)/shard_map/ppermute | solution.py:333
  30.1 3.6 %collective-permute-start.8 = (bf16[128,384]{1,0:T(8,128)(2,1)}, bf16[128,384]{1,0:T(8,128)(2,1)}, u32[]{:S(2)}, u32[]{:S(2)}) collective-permute-start(bf16[128,384]{1,0:T(8,128)(2,1)} %get-tuple-element.46), channel_id=1, source_target_pairs={{0,6},{1,7},{2,4},{3,5},{4,2},{5,3},{6,0},{7,1},{8,14},{9,15},{10,... | collective-permute-start | bytes 294920 | tf_op jit(solution)/shard_map/ppermute | solution.py:333
  34.4 8.5 %collective-permute-done.8.refs_6_ = bf16[128,384]{1,0:T(8,128)(2,1)} collective-permute-done((bf16[128,384]{1,0:T(8,128)(2,1)}, bf16[128,384]{1,0:T(8,128)(2,1)}, u32[]{:S(2)}, u32[]{:S(2)}) %collective-permute-start.8) | collective-permute-done | bytes 98336 | tf_op jit(solution)/shard_map/ppermute | solution.py:333
  47.5 2.5 %turn_cotangent.1.refs_4_ = bf16[4,2,3,128,128]{4,3,2,1,0:T(8,128)(2,1)S(1)} custom-call(s32[4]{0:T(128)S(1)} %pad_add_fusion.scalars, bf16[128,384]{1,0:T(8,128)(2,1)S(1)} %get-tuple-element.45.refs_0_, bf16[128,384]{1,0:T(8,128)(2,1)S(1)} %collective-permute-done.3.refs_1_, bf16[128,384]{1,0:T(8,128)(2,1)S(1)} %copy-done.12, ...), custom_call_target="tpu_custom_call" | custom-call | bytes 1572864 | tf_op jit(solution)/shard_map/turn_cotangent/pallas_call | solution.py:139
  51.1 4.3 %temporal.1 = (bf16[3,128,256]{2,1,0:T(8,128)(2,1)S(1)}, bf16[3,128,256]{2,1,0:T(8,128)(2,1)S(1)}, bf16[3,128,256]{2,1,0:T(8,128)(2,1)S(1)}, bf16[3,128,256]{2,1,0:T(8,128)(2,1)S(1)}, f32[8,128]{1,0:T(8,128)S(1)}) custom-call(s32[4]{0:T(128)S(1)} %pad_add_fusion.scalars, bf16[3,128,256]{2,1,0:T(8,128)(2,1)S(1)} %copy-done.10, ...), custom_call_target="tpu_custom_call" | custom-call | flops 19660800 | bytes 2359296 | tf_op jit(solution)/shard_map/temporal/pallas_call | solution.py:272
  55.5 9.9 %collective-permute-start.13 = (f32[8,128]{1,0:T(8,128)S(1)}, f32[8,128]{1,0:T(8,128)S(1)}, u32[]{:S(2)}, u32[]{:S(2)}) collective-permute-start(f32[8,128]{1,0:T(8,128)S(1)} %get-tuple-element.38), channel_id=1, source_target_pairs={{0,2},{2,0},{4,6},{6,4},{1,3},{3,1},{5,7},{7,5},{8,10},{10,8},{12,... | collective-permute-start | bytes 12296 | tf_op jit(solution)/shard_map/ppermute | solution.py:333
  66.5 1.4 %collective-permute-start.15 = (f32[8,128]{1,0:T(8,128)S(1)}, f32[8,128]{1,0:T(8,128)S(1)}, u32[]{:S(2)}, u32[]{:S(2)}) collective-permute-start(f32[8,128]{1,0:T(8,128)S(1)} %get-tuple-element.38), channel_id=1, source_target_pairs={{0,6},{2,4},{4,2},{6,0},{1,7},{3,5},{5,3},{7,1},{8,14},{10,12},{12... | collective-permute-start | bytes 12296 | tf_op jit(solution)/shard_map/ppermute | solution.py:333
  67.9 2.4 %collective-permute-start.10 = (bf16[3,128,256]{2,1,0:T(8,128)(2,1)S(1)}, bf16[3,128,256]{2,1,0:T(8,128)(2,1)S(1)}, u32[]{:S(2)}, u32[]{:S(2)}) collective-permute-start(bf16[3,128,256]{2,1,0:T(8,128)(2,1)S(1)} %get-tuple-element.26), channel_id=1, source_target_pairs={{0,6},{2,4},{4,2},{6,0},{1,7},{3,5},{5,3},{7,1},{8,14},{10,12},{12... | collective-permute-start | bytes 589832 | tf_op jit(solution)/shard_map/ppermute | solution.py:333
  70.3 1.9 %collective-permute-start.12 = (bf16[3,128,256]{2,1,0:T(8,128)(2,1)S(1)}, bf16[3,128,256]{2,1,0:T(8,128)(2,1)S(1)}, u32[]{:S(2)}, u32[]{:S(2)}) collective-permute-start(bf16[3,128,256]{2,1,0:T(8,128)(2,1)S(1)} %get-tuple-element.28), channel_id=1, source_target_pairs={{0,2},{2,0},{4,6},{6,4},{1,3},{3,1},{5,7},{7,5},{8,10},{10,8},{12,... | collective-permute-start | bytes 589832 | tf_op jit(solution)/shard_map/ppermute | solution.py:333
  72.3 2.7 %collective-permute-done.14 = f32[8,128]{1,0:T(8,128)S(1)} collective-permute-done((f32[8,128]{1,0:T(8,128)S(1)}, f32[8,128]{1,0:T(8,128)S(1)}, u32[]{:S(2)}, u32[]{:S(2)}) %collective-permute-start.14) | collective-permute-done | bytes 4128 | tf_op jit(solution)/shard_map/ppermute | solution.py:333
  75.0 1.5 %collective-permute-start.17 = (f32[32,128]{1,0:T(8,128)S(1)}, f32[32,128]{1,0:T(8,128)S(1)}, u32[]{:S(2)}, u32[]{:S(2)}) collective-permute-start(f32[32,128]{1,0:T(8,128)S(1)} %constant_dynamic-update-slice_fusion.refs_0_), channel_id=1, source_target_pairs={{0,16},{8,24},{16,0},{24,8},{1,17},{9,25},{17,1},{25,9},{2,18},{10... | collective-permute-start | bytes 49160 | tf_op jit(solution)/shard_map/ppermute | solution.py:333
  80.8 2.9 %spatial_backward.4 = (bf16[256,1536]{1,0:T(8,128)(2,1)}, bf16[256,1536]{1,0:T(8,128)(2,1)}) custom-call(s32[4]{0:T(128)S(1)} %pad_add_fusion.scalars, bf16[256,1536]{1,0:T(8,128)(2,1)S(1)} %bitcast.29, bf16[256,1536]{1,0:T(8,128)(2,1)S(1)} %bitcast.34, bf16[256,1536]{1,0:T(8,128)(2,1)S(1)} %bitcast.39, f32[12,256,256]{2,1,0:T(8,128)S(1)} %copy-done, ...), custom_call_target="tpu_custom_call" | custom-call | flops 150994944 | bytes 1966080 | tf_op jit(solution)/shard_map/spatial_backward/pallas_call | solution.py:101
  83.7 1.3 %gain_gradients.1 = f32[2,16,1536]{2,1,0:T(8,128)} custom-call(s32[4]{0:T(128)S(1)} %pad_add_fusion.scalars, f32[32,128]{1,0:T(8,128)S(1)} %constant_dynamic-update-slice_fusion.refs_0_, f32[32,128]{1,0:T(8,128)S(1)} %collective-permute-done.16.refs_1_, f32[32,128]{1,0:T(8,128)S(1)} %collective-permute-done.17.refs_2_, ...), custom_call_target="tpu_custom_call" | custom-call | tf_op jit(solution)/shard_map/gain_gradients/pallas_call | solution.py:321
  85.0 2.9 %spatial_backward.5 = (bf16[256,1536]{1,0:T(8,128)(2,1)}, bf16[256,1536]{1,0:T(8,128)(2,1)}) custom-call(s32[4]{0:T(128)S(1)} %pad_add_fusion.scalars, bf16[256,1536]{1,0:T(8,128)(2,1)S(1)} %bitcast.30, bf16[256,1536]{1,0:T(8,128)(2,1)S(1)} %bitcast.35, bf16[256,1536]{1,0:T(8,128)(2,1)S(1)} %bitcast.40, ...), custom_call_target="tpu_custom_call", output_to_operand_aliasing={{0}: (6, {}), {1}: (7, {})} | custom-call | flops 150994944 | bytes 1966080 | tf_op jit(solution)/shard_map/spatial_backward/pallas_call | solution.py:101
  87.9 2.9 %spatial_backward.6 = (bf16[256,1536]{1,0:T(8,128)(2,1)}, bf16[256,1536]{1,0:T(8,128)(2,1)}) custom-call(s32[4]{0:T(128)S(1)} %pad_add_fusion.scalars, bf16[256,1536]{1,0:T(8,128)(2,1)S(1)} %bitcast.31, bf16[256,1536]{1,0:T(8,128)(2,1)S(1)} %bitcast.36, bf16[256,1536]{1,0:T(8,128)(2,1)S(1)} %bitcast.41, ...), custom_call_target="tpu_custom_call", output_to_operand_aliasing={{0}: (6, {}), {1}: (7, {})} | custom-call | flops 150994944 | bytes 1966080 | tf_op jit(solution)/shard_map/spatial_backward/pallas_call | solution.py:101
  90.8 2.9 %spatial_backward.7 = (bf16[256,1536]{1,0:T(8,128)(2,1)}, bf16[256,1536]{1,0:T(8,128)(2,1)}) custom-call(s32[4]{0:T(128)S(1)} %pad_add_fusion.scalars, bf16[256,1536]{1,0:T(8,128)(2,1)S(1)} %bitcast.32, bf16[256,1536]{1,0:T(8,128)(2,1)S(1)} %bitcast.37, bf16[256,1536]{1,0:T(8,128)(2,1)S(1)} %bitcast.42, ...), custom_call_target="tpu_custom_call", output_to_operand_aliasing={{0}: (6, {}), {1}: (7, {})} | custom-call | flops 150994944 | bytes 1966080 | tf_op jit(solution)/shard_map/spatial_backward/pallas_call | solution.py:101
  (68 shorter events, 17.0 us)
Async XLA Ops:
  0.6 33.7 %copy-start.8 = (f32[2,16,1536]{2,1,0:T(8,128)S(1)}, f32[2,16,1536]{2,1,0:T(8,128)}, u32[]{:S(2)}) copy-start(f32[2,16,1536]{2,1,0:T(8,128)} %refs_4_.1) | copy-start | bytes 589828
  2.7 21.0 %collective-permute-start.3 = (bf16[128,384]{1,0:T(8,128)(2,1)S(1)}, bf16[128,384]{1,0:T(8,128)(2,1)S(1)}, u32[]{:S(2)}, u32[]{:S(2)}) collective-permute-start(bf16[128,384]{1,0:T(8,128)(2,1)S(1)} %get-tuple-element.44), channel_id=1, source_target_pairs={{0,1},{1,0},{2,3},{3,2},{4,5},{5,4},{6,7},{7,6},{8,9},{9,8},{10,11... | collective-permute-start | bytes 294920 | tf_op jit(solution)/shard_map/ppermute | solution.py:333
  5.7 19.6 %collective-permute-start.4 = (bf16[128,384]{1,0:T(8,128)(2,1)S(1)}, bf16[128,384]{1,0:T(8,128)(2,1)S(1)}, u32[]{:S(2)}, u32[]{:S(2)}) collective-permute-start(bf16[128,384]{1,0:T(8,128)(2,1)S(1)} %get-tuple-element.43), channel_id=1, source_target_pairs={{0,2},{1,3},{2,0},{3,1},{4,6},{5,7},{6,4},{7,5},{8,10},{9,11},{10,... | collective-permute-start | bytes 294920 | tf_op jit(solution)/shard_map/ppermute | solution.py:333
  7.3 21.3 %collective-permute-start.5 = (bf16[128,384]{1,0:T(8,128)(2,1)S(1)}, bf16[128,384]{1,0:T(8,128)(2,1)S(1)}, u32[]{:S(2)}, u32[]{:S(2)}) collective-permute-start(bf16[128,384]{1,0:T(8,128)(2,1)S(1)} %get-tuple-element.42), channel_id=1, source_target_pairs={{0,3},{1,2},{2,1},{3,0},{4,7},{5,6},{6,5},{7,4},{8,11},{9,10},{10,... | collective-permute-start | bytes 294920 | tf_op jit(solution)/shard_map/ppermute | solution.py:333
  7.3 22.1 %collective-permute-start.6 = (bf16[128,384]{1,0:T(8,128)(2,1)S(1)}, bf16[128,384]{1,0:T(8,128)(2,1)S(1)}, u32[]{:S(2)}, u32[]{:S(2)}) collective-permute-start(bf16[128,384]{1,0:T(8,128)(2,1)S(1)} %get-tuple-element.41), channel_id=1, source_target_pairs={{0,4},{1,5},{2,6},{3,7},{4,0},{5,1},{6,2},{7,3},{8,12},{9,13},{10,... | collective-permute-start | bytes 294920 | tf_op jit(solution)/shard_map/ppermute | solution.py:333
  10.3 23.4 %collective-permute-start.7 = (bf16[128,384]{1,0:T(8,128)(2,1)S(1)}, bf16[128,384]{1,0:T(8,128)(2,1)S(1)}, u32[]{:S(2)}, u32[]{:S(2)}) collective-permute-start(bf16[128,384]{1,0:T(8,128)(2,1)S(1)} %get-tuple-element.40), channel_id=1, source_target_pairs={{0,5},{1,4},{2,7},{3,6},{4,1},{5,0},{6,3},{7,2},{8,13},{9,12},{10,... | collective-permute-start | bytes 294920 | tf_op jit(solution)/shard_map/ppermute | solution.py:333
  12.9 1.1 %copy-start.1 = (bf16[1,1,256,1536]{3,2,1,0:T(8,128)(2,1)S(1)}, bf16[1,1,256,1536]{3,2,1,0:T(8,128)(2,1)}, u32[]{:S(2)}) copy-start(bf16[1,1,256,1536]{3,2,1,0:T(8,128)(2,1)} %param.7) | copy-start | bytes 2359300
  23.7 53.7 %copy-start = (f32[12,256,256]{2,1,0:T(8,128)S(1)}, f32[12,256,256]{2,1,0:T(8,128)}, u32[]{:S(2)}) copy-start(f32[12,256,256]{2,1,0:T(8,128)} %get-tuple-element.21.weights_ref) | copy-start | bytes 9437188
  23.8 26.3 %collective-permute-start = (bf16[3,128,256]{2,1,0:T(8,128)(2,1)}, bf16[3,128,256]{2,1,0:T(8,128)(2,1)}, u32[]{:S(2)}, u32[]{:S(2)}) collective-permute-start(bf16[3,128,256]{2,1,0:T(8,128)(2,1)} %get-tuple-element.23), channel_id=1, source_target_pairs={{0,2},{2,0},{4,6},{6,4},{1,3},{3,1},{5,7},{7,5},{8,10},{10,8},{12,... | collective-permute-start | bytes 589832 | tf_op jit(solution)/shard_map/ppermute | solution.py:333
  26.0 24.1 %collective-permute-start.1 = (bf16[3,128,256]{2,1,0:T(8,128)(2,1)}, bf16[3,128,256]{2,1,0:T(8,128)(2,1)}, u32[]{:S(2)}, u32[]{:S(2)}) collective-permute-start(bf16[3,128,256]{2,1,0:T(8,128)(2,1)} %get-tuple-element.24), channel_id=1, source_target_pairs={{0,4},{2,6},{4,0},{6,2},{1,5},{3,7},{5,1},{7,3},{8,12},{10,14},{12... | collective-permute-start | bytes 589832 | tf_op jit(solution)/shard_map/ppermute | solution.py:333
  29.2 20.9 %collective-permute-start.2 = (bf16[3,128,256]{2,1,0:T(8,128)(2,1)}, bf16[3,128,256]{2,1,0:T(8,128)(2,1)}, u32[]{:S(2)}, u32[]{:S(2)}) collective-permute-start(bf16[3,128,256]{2,1,0:T(8,128)(2,1)} %get-tuple-element.25), channel_id=1, source_target_pairs={{0,6},{2,4},{4,2},{6,0},{1,7},{3,5},{5,3},{7,1},{8,14},{10,12},{12... | collective-permute-start | bytes 589832 | tf_op jit(solution)/shard_map/ppermute | solution.py:333
  30.1 12.9 %collective-permute-start.8 = (bf16[128,384]{1,0:T(8,128)(2,1)}, bf16[128,384]{1,0:T(8,128)(2,1)}, u32[]{:S(2)}, u32[]{:S(2)}) collective-permute-start(bf16[128,384]{1,0:T(8,128)(2,1)} %get-tuple-element.46), channel_id=1, source_target_pairs={{0,6},{1,7},{2,4},{3,5},{4,2},{5,3},{6,0},{7,1},{8,14},{9,15},{10,... | collective-permute-start | bytes 294920 | tf_op jit(solution)/shard_map/ppermute | solution.py:333
  34.3 9.6 %collective-permute-start.9 = (bf16[128,384]{1,0:T(8,128)(2,1)}, bf16[128,384]{1,0:T(8,128)(2,1)}, u32[]{:S(2)}, u32[]{:S(2)}) collective-permute-start(bf16[128,384]{1,0:T(8,128)(2,1)} %get-tuple-element.39), channel_id=1, source_target_pairs={{0,7},{1,6},{2,5},{3,4},{4,3},{5,2},{6,1},{7,0},{8,15},{9,14},{10,... | collective-permute-start | bytes 294920 | tf_op jit(solution)/shard_map/ppermute | solution.py:333
  55.5 14.9 %collective-permute-start.13 = (f32[8,128]{1,0:T(8,128)S(1)}, f32[8,128]{1,0:T(8,128)S(1)}, u32[]{:S(2)}, u32[]{:S(2)}) collective-permute-start(f32[8,128]{1,0:T(8,128)S(1)} %get-tuple-element.38), channel_id=1, source_target_pairs={{0,2},{2,0},{4,6},{6,4},{1,3},{3,1},{5,7},{7,5},{8,10},{10,8},{12,... | collective-permute-start | bytes 12296 | tf_op jit(solution)/shard_map/ppermute | solution.py:333
  65.4 9.5 %collective-permute-start.14 = (f32[8,128]{1,0:T(8,128)S(1)}, f32[8,128]{1,0:T(8,128)S(1)}, u32[]{:S(2)}, u32[]{:S(2)}) collective-permute-start(f32[8,128]{1,0:T(8,128)S(1)} %get-tuple-element.38), channel_id=1, source_target_pairs={{0,4},{2,6},{4,0},{6,2},{1,5},{3,7},{5,1},{7,3},{8,12},{10,14},{12... | collective-permute-start | bytes 12296 | tf_op jit(solution)/shard_map/ppermute | solution.py:333
  66.5 8.4 %collective-permute-start.15 = (f32[8,128]{1,0:T(8,128)S(1)}, f32[8,128]{1,0:T(8,128)S(1)}, u32[]{:S(2)}, u32[]{:S(2)}) collective-permute-start(f32[8,128]{1,0:T(8,128)S(1)} %get-tuple-element.38), channel_id=1, source_target_pairs={{0,6},{2,4},{4,2},{6,0},{1,7},{3,5},{5,3},{7,1},{8,14},{10,12},{12... | collective-permute-start | bytes 12296 | tf_op jit(solution)/shard_map/ppermute | solution.py:333
  67.9 23.0 %collective-permute-start.10 = (bf16[3,128,256]{2,1,0:T(8,128)(2,1)S(1)}, bf16[3,128,256]{2,1,0:T(8,128)(2,1)S(1)}, u32[]{:S(2)}, u32[]{:S(2)}) collective-permute-start(bf16[3,128,256]{2,1,0:T(8,128)(2,1)S(1)} %get-tuple-element.26), channel_id=1, source_target_pairs={{0,6},{2,4},{4,2},{6,0},{1,7},{3,5},{5,3},{7,1},{8,14},{10,12},{12... | collective-permute-start | bytes 589832 | tf_op jit(solution)/shard_map/ppermute | solution.py:333
  70.3 17.6 %collective-permute-start.11 = (bf16[3,128,256]{2,1,0:T(8,128)(2,1)S(1)}, bf16[3,128,256]{2,1,0:T(8,128)(2,1)S(1)}, u32[]{:S(2)}, u32[]{:S(2)}) collective-permute-start(bf16[3,128,256]{2,1,0:T(8,128)(2,1)S(1)} %get-tuple-element.27), channel_id=1, source_target_pairs={{0,4},{2,6},{4,0},{6,2},{1,5},{3,7},{5,1},{7,3},{8,12},{10,14},{12... | collective-permute-start | bytes 589832 | tf_op jit(solution)/shard_map/ppermute | solution.py:333
  70.3 14.7 %collective-permute-start.12 = (bf16[3,128,256]{2,1,0:T(8,128)(2,1)S(1)}, bf16[3,128,256]{2,1,0:T(8,128)(2,1)S(1)}, u32[]{:S(2)}, u32[]{:S(2)}) collective-permute-start(bf16[3,128,256]{2,1,0:T(8,128)(2,1)S(1)} %get-tuple-element.28), channel_id=1, source_target_pairs={{0,2},{2,0},{4,6},{6,4},{1,3},{3,1},{5,7},{7,5},{8,10},{10,8},{12,... | collective-permute-start | bytes 589832 | tf_op jit(solution)/shard_map/ppermute | solution.py:333
  74.9 1.6 %collective-permute-start.16 = (f32[32,128]{1,0:T(8,128)S(1)}, f32[32,128]{1,0:T(8,128)S(1)}, u32[]{:S(2)}, u32[]{:S(2)}) collective-permute-start(f32[32,128]{1,0:T(8,128)S(1)} %constant_dynamic-update-slice_fusion.refs_0_), channel_id=1, source_target_pairs={{0,8},{8,0},{16,24},{24,16},{1,9},{9,1},{17,25},{25,17},{2,10},{10... | collective-permute-start | bytes 49160 | tf_op jit(solution)/shard_map/ppermute | solution.py:333
  75.0 8.7 %collective-permute-start.17 = (f32[32,128]{1,0:T(8,128)S(1)}, f32[32,128]{1,0:T(8,128)S(1)}, u32[]{:S(2)}, u32[]{:S(2)}) collective-permute-start(f32[32,128]{1,0:T(8,128)S(1)} %constant_dynamic-update-slice_fusion.refs_0_), channel_id=1, source_target_pairs={{0,16},{8,24},{16,0},{24,8},{1,17},{9,25},{17,1},{25,9},{2,18},{10... | collective-permute-start | bytes 49160 | tf_op jit(solution)/shard_map/ppermute | solution.py:333
  76.6 7.2 %collective-permute-start.18 = (f32[32,128]{1,0:T(8,128)S(1)}, f32[32,128]{1,0:T(8,128)S(1)}, u32[]{:S(2)}, u32[]{:S(2)}) collective-permute-start(f32[32,128]{1,0:T(8,128)S(1)} %constant_dynamic-update-slice_fusion.refs_0_), channel_id=1, source_target_pairs={{0,24},{8,16},{16,8},{24,0},{1,25},{9,17},{17,9},{25,1},{2,26},{10... | collective-permute-start | bytes 49160 | tf_op jit(solution)/shard_map/ppermute | solution.py:333
  77.4 1.1 %copy-start.2 = (bf16[1,1,256,1536]{3,2,1,0:T(8,128)(2,1)S(1)}, bf16[1,1,256,1536]{3,2,1,0:T(8,128)(2,1)}, u32[]{:S(2)}) copy-start(bf16[1,1,256,1536]{3,2,1,0:T(8,128)(2,1)} %param.7) | copy-start | bytes 2359300
  80.8 4.2 %copy-start.3 = (bf16[1,1,256,1536]{3,2,1,0:T(8,128)(2,1)S(1)}, bf16[1,1,256,1536]{3,2,1,0:T(8,128)(2,1)}, u32[]{:S(2)}) copy-start(bf16[1,1,256,1536]{3,2,1,0:T(8,128)(2,1)} %param.7) | copy-start | bytes 2359300
  (14 other events, 12.2 us)

commit v2 on v1

--- a/solution.py
+++ b/solution.py
@@ -9,11 +9,11 @@
 
 HEAD_DIM = 128
 GROUP = 16
-VMEM_BYTES = 48 * 1024 * 1024
-
-
-def params():
-    return pltpu.CompilerParams(vmem_limit_bytes=VMEM_BYTES)
+MIB = 1024 * 1024
+
+
+def params(patches):
+    return pltpu.CompilerParams(vmem_limit_bytes=(16 if patches <= 512 else 60) * MIB)
 
 
 def columns_dot(left, right):
@@ -30,44 +30,49 @@
     return jnp.bitwise_xor(scalars[0], distance)
 
 
-def forward_kernel(scalars, query_ref, key_ref, value_ref, weights_ref, *attended_refs):
+def forward_kernel(scalars, query_ref, key_ref, value_ref, weights_ref, *refs):
+    (queries, key_rows, values, arrived), attended_refs = refs[-4:], refs[:-4]
     score_scale = HEAD_DIM ** (-0.5)
-    pieces = []
-    for head in range(weights_ref.shape[0]):
-        cols = pl.ds(head * HEAD_DIM, HEAD_DIM)
-        scores = columns_dot(key_ref[:, cols], query_ref[:, cols])
-        largest = jnp.max(scores, axis=0, keepdims=True)
-        raised = jnp.exp((scores - largest) * score_scale)
-        weights = raised * (1.0 / jnp.sum(raised, axis=0, keepdims=True))
-        weights_ref[head] = weights
-        attended = dot(value_ref[:, cols].T, weights.astype(jnp.bfloat16))
-        pieces.append(attended.astype(jnp.bfloat16))
-    for step, attended_ref in enumerate(attended_refs):
-
-        @pl.when(pl.program_id(0) == step)
-        def _():
-            for head, piece in enumerate(pieces):
-                attended_ref[head] = piece
+    groups, _, width = queries.shape
+    copies = []
+    for group in range(groups):
+        cols = pl.ds(pl.multiple_of(partner(scalars, group) * width, HEAD_DIM), width)
+        for field, (source, target) in enumerate(
+            ((query_ref, queries), (key_ref, key_rows), (value_ref, values))
+        ):
+            copy = pltpu.make_async_copy(
+                source.at[:, cols], target.at[group], arrived.at[group, field]
+            )
+            copy.start()
+            copies.append(copy)
+    for group in range(groups):
+        for copy in copies[3 * group : 3 * group + 3]:
+            copy.wait()
+        for head in range(width // HEAD_DIM):
+            cols = pl.ds(head * HEAD_DIM, HEAD_DIM)
+            scores = columns_dot(key_rows[group, :, cols], queries[group, :, cols])
+            largest = jnp.max(scores, axis=0, keepdims=True)
+            raised = jnp.exp((scores - largest) * score_scale)
+            weights = raised * (1.0 / jnp.sum(raised, axis=0, keepdims=True))
+            weights_ref[group * (width // HEAD_DIM) + head] = weights
+            attended = dot(values[group, :, cols].T, weights.astype(jnp.bfloat16))
+            attended_refs[group][head] = attended.astype(jnp.bfloat16)
 
 
 def forward(scalars, queries, key_rows, values, groups):
     patches, feat = queries.shape
     heads = feat // HEAD_DIM
     own = heads // groups
-    field = pl.BlockSpec((patches, own * HEAD_DIM), lambda d, sc: (0, partner(sc, d)))
-    whole = pl.BlockSpec((own, HEAD_DIM, patches), lambda d, sc: (0, 0, 0))
     weights, *attended = pl.pallas_call(
         forward_kernel,
-        grid_spec=pltpu.PrefetchScalarGridSpec(
-            num_scalar_prefetch=1,
-            grid=(groups,),
-            in_specs=[field] * 3,
-            out_specs=[pl.BlockSpec((own, patches, patches), lambda d, sc: (d, 0, 0))]
-            + [whole] * groups,
-        ),
+        in_specs=[pl.BlockSpec(memory_space=pltpu.SMEM)]
+        + [pl.BlockSpec(memory_space=pltpu.HBM)] * 3,
+        out_specs=[pl.BlockSpec(memory_space=pltpu.VMEM)] * (1 + groups),
+        scratch_shapes=[pltpu.VMEM((groups, patches, feat // groups), jnp.bfloat16)] * 3
+        + [pltpu.SemaphoreType.DMA((groups, 3))],
         out_shape=[jax.ShapeDtypeStruct((heads, patches, patches), jnp.float32)]
         + [jax.ShapeDtypeStruct((own, HEAD_DIM, patches), jnp.bfloat16)] * groups,
-        compiler_params=params(),
+        compiler_params=params(patches),
         cost_estimate=pl.CostEstimate(
             flops=4 * heads * patches * patches * HEAD_DIM,
             bytes_accessed=heads * patches * (patches * 4 + 8 * HEAD_DIM),
@@ -96,26 +101,26 @@
     patches, feat = queries.shape
     own = grads.shape[0]
     field = pl.BlockSpec(
-        (patches, HEAD_DIM), lambda i, sc: (0, partner(sc, distance) * own + i)
+        (patches, own * HEAD_DIM), lambda i, sc: (0, partner(sc, distance))
     )
     return pl.pallas_call(
         backward_kernel,
         grid_spec=pltpu.PrefetchScalarGridSpec(
             num_scalar_prefetch=1,
-            grid=(own,),
+            grid=(1,),
             in_specs=[
                 field,
                 field,
                 field,
-                pl.BlockSpec((1, patches, patches), lambda i, sc: (distance * own + i, 0, 0)),
-                pl.BlockSpec((1, HEAD_DIM, patches), lambda i, sc: (i, 0, 0)),
+                pl.BlockSpec((own, patches, patches), lambda i, sc: (distance, 0, 0)),
+                pl.BlockSpec((own, HEAD_DIM, patches), lambda i, sc: (0, 0, 0)),
             ]
             + [pl.BlockSpec(memory_space=pl.ANY)] * len(earlier),
             out_specs=[field, field],
         ),
         out_shape=[jax.ShapeDtypeStruct((patches, feat), jnp.bfloat16)] * 2,
         input_output_aliases={6 + index: index for index in range(len(earlier))},
-        compiler_params=params(),
+        compiler_params=params(patches),
         cost_estimate=pl.CostEstimate(
             flops=6 * own * patches * patches * HEAD_DIM,
             bytes_accessed=own * patches * (patches * 4 + 12 * HEAD_DIM),
@@ -125,34 +130,59 @@
     )(scalars, queries, key_rows, values, weights, grads, *earlier)
 
 
-def turn_kernel(spaces, scalars, *refs):
-    turned_ref = refs[-1]
-    for index, ref in enumerate(refs[:-1]):
-        frame = partner(scalars, index // spaces)
-        part = jnp.bitwise_xor(scalars[1], index % spaces)
-        turned_ref[frame, part, 0] = ref[...].T
-
-
-def turn(scalars, pieces, frames, spaces):
-    patches, feat = pieces[0].shape
+def pack_kernel(frames, spaces, field_ref, packed_ref, sent):
+    width = packed_ref.shape[2]
+    copies = []
+    for frame in range(frames):
+        for space in range(spaces):
+            index = frame * spaces + space
+            cols = pl.ds((space * frames + frame) * width, width)
+            copy = pltpu.make_async_copy(field_ref.at[:, cols], packed_ref.at[index], sent.at[index])
+            copy.start()
+            copies.append(copy)
+    for copy in copies:
+        copy.wait()
+
+
+def pack(field, frames, spaces):
+    patches, feat = field.shape
+    devices = frames * spaces
+    return pl.pallas_call(
+        functools.partial(pack_kernel, frames, spaces),
+        in_specs=[pl.BlockSpec(memory_space=pl.ANY)],
+        out_specs=pl.BlockSpec(memory_space=pl.ANY),
+        out_shape=jax.ShapeDtypeStruct((devices, patches, feat // devices), field.dtype),
+        scratch_shapes=[pltpu.SemaphoreType.DMA((devices,))],
+        compiler_params=params(0),
+        cost_estimate=pl.CostEstimate(
+            flops=0, bytes_accessed=4 * patches * feat, transcendentals=0
+        ),
+        name="pack_cotangent",
+    )(field)
+
+
+def turn_kernel(field_ref, turned_ref):
+    spaces, frames = turned_ref.shape[:2]
+    for space in range(spaces):
+        for frame in range(frames):
+            turned_ref[space, frame, 0] = field_ref[frame * spaces + space].T
+
+
+def turn(field, frames, spaces):
+    devices, patches, feat = field.shape
     heads = feat // HEAD_DIM
     return pl.pallas_call(
-        functools.partial(turn_kernel, spaces),
-        grid_spec=pltpu.PrefetchScalarGridSpec(
-            num_scalar_prefetch=1,
-            grid=(heads,),
-            in_specs=[pl.BlockSpec((patches, HEAD_DIM), lambda i, sc: (0, i))] * len(pieces),
-            out_specs=pl.BlockSpec(
-                (frames, spaces, 1, HEAD_DIM, patches), lambda i, sc: (0, 0, i, 0, 0)
-            ),
-        ),
-        out_shape=jax.ShapeDtypeStruct((frames, spaces, heads, HEAD_DIM, patches), jnp.bfloat16),
-        compiler_params=params(),
+        turn_kernel,
+        grid=(heads,),
+        in_specs=[pl.BlockSpec((devices, patches, HEAD_DIM), lambda i: (0, 0, i))],
+        out_specs=pl.BlockSpec((spaces, frames, 1, HEAD_DIM, patches), lambda i: (0, 0, i, 0, 0)),
+        out_shape=jax.ShapeDtypeStruct((spaces, frames, heads, HEAD_DIM, patches), field.dtype),
+        compiler_params=params(patches),
         cost_estimate=pl.CostEstimate(
-            flops=0, bytes_accessed=4 * len(pieces) * patches * feat, transcendentals=0
+            flops=0, bytes_accessed=4 * devices * patches * feat, transcendentals=0
         ),
         name="turn_cotangent",
-    )(scalars, *pieces)
+    )(field)
 
 
 def temporal_part(length, attended_ref, upstream_ref, gain_ref, grad_ref, mixed_sum, part):
@@ -174,7 +204,7 @@
         return [split(attended_ref[t, pl.ds(group * GROUP, GROUP), here]) for t in every]
 
     def load_ups(group):
-        return [split(upstream_ref[t, part, 0, pl.ds(group * GROUP, GROUP), :]) for t in every]
+        return [split(upstream_ref[part, t, 0, pl.ds(group * GROUP, GROUP), :]) for t in every]
 
     def total(piece):
         return jnp.broadcast_to(jnp.sum(piece, axis=0, keepdims=True), (half, lanes))
@@ -252,20 +282,20 @@
     head = pl.program_id(0)
     for distance, ref in enumerate(attended_refs):
         attended[partner(scalars, distance)] = ref[0]
-    for part in range(upstream_ref.shape[1]):
-        temporal_part(scalars[2], attended, upstream_ref, gain_ref, grads, mixed_sum, part)
+    for part in range(upstream_ref.shape[0]):
+        temporal_part(scalars[1], attended, upstream_ref, gain_ref, grads, mixed_sum, part)
     for distance, ref in enumerate(grad_refs):
         ref[0] = grads[partner(scalars, distance)]
 
     @pl.when(head == 0)
     def _():
-        mixed_ref[...] = jnp.full(mixed_ref.shape, scalars[3].astype(jnp.float32))
+        mixed_ref[...] = jnp.full(mixed_ref.shape, scalars[2].astype(jnp.float32))
 
     mixed_ref[pl.ds(head, 1), :] = jnp.sum(mixed_sum[...].T, axis=0, keepdims=True) * 0.5
 
 
 def temporal(scalars, attended, upstream, gain):
-    frames, spaces, heads, feat, lanes = upstream.shape
+    spaces, frames, heads, feat, lanes = upstream.shape
     patches = spaces * lanes
     rows = -(-(heads + 1) // 8) * 8
     plane = pl.BlockSpec((1, feat, patches), lambda i, sc: (i, 0, 0))
@@ -276,7 +306,7 @@
             grid=(heads,),
             in_specs=[plane] * frames
             + [
-                pl.BlockSpec((frames, spaces, 1, feat, lanes), lambda i, sc: (0, 0, i, 0, 0)),
+                pl.BlockSpec((spaces, frames, 1, feat, lanes), lambda i, sc: (0, 0, i, 0, 0)),
                 pl.BlockSpec((1, feat, lanes), lambda i, sc: (i, 0, 0)),
             ],
             out_specs=[plane] * frames + [pl.BlockSpec((rows, feat), lambda i, sc: (0, 0))],
@@ -288,7 +318,7 @@
         ),
         out_shape=[jax.ShapeDtypeStruct((heads, feat, patches), jnp.bfloat16)] * frames
         + [jax.ShapeDtypeStruct((rows, feat), jnp.float32)],
-        compiler_params=params(),
+        compiler_params=params(patches),
         cost_estimate=pl.CostEstimate(
             flops=heads * patches * feat * 200,
             bytes_accessed=6 * frames * heads * patches * feat,
@@ -299,17 +329,20 @@
     return grads, mixed
 
 
-def gains_kernel(heads, frames, scalars, *refs):
+def gains_kernel(heads, frames, clips, scalars, *refs):
     mixed_refs, gains_ref, grad_ref = refs[:-2], refs[-2], refs[-1]
     tasks = gains_ref.shape[1]
-    rows = mixed_refs[0].shape[0] // frames
+    rows = sum(ref.shape[0] for ref in mixed_refs) // (frames * clips)
+    each = mixed_refs[0].shape[0] // rows
     task_ids = lax.broadcasted_iota(jnp.int32, (tasks, HEAD_DIM), 0).astype(jnp.float32)
     for distance in range(frames):
         for head in range(heads):
             mixed = jnp.zeros((tasks, HEAD_DIM), jnp.float32)
-            for ref in mixed_refs:
-                task = ref[pl.ds(distance * rows + heads, 1), :]
-                row = ref[pl.ds(distance * rows + head, 1), :]
+            for clip in range(clips):
+                block = distance * clips + clip
+                ref, start = mixed_refs[block // each], block % each * rows
+                task = ref[pl.ds(start + heads, 1), :]
+                row = ref[pl.ds(start + head, 1), :]
                 mixed = mixed + jnp.where(task_ids == task, row, 0.0)
             start = (partner(scalars, distance) * heads + head) * HEAD_DIM
             cols = pl.ds(pl.multiple_of(start, HEAD_DIM), HEAD_DIM)
@@ -317,14 +350,14 @@
             grad_ref[1, :, cols] = gains_ref[0, :, cols] * mixed
 
 
-def gain_gradients(scalars, mixed, gains, heads, frames):
+def gain_gradients(scalars, mixed, gains, heads, frames, clips):
     return pl.pallas_call(
-        functools.partial(gains_kernel, heads, frames),
+        functools.partial(gains_kernel, heads, frames, clips),
         in_specs=[pl.BlockSpec(memory_space=pltpu.SMEM)]
         + [pl.BlockSpec(memory_space=pltpu.VMEM)] * (len(mixed) + 1),
         out_specs=pl.BlockSpec(memory_space=pltpu.VMEM),
         out_shape=jax.ShapeDtypeStruct(gains.shape, jnp.float32),
-        compiler_params=params(),
+        compiler_params=params(0),
         name="gain_gradients",
     )(scalars, *mixed, gains)
 
@@ -343,22 +376,18 @@
     queries, key_rows, values = (
         field.reshape(patches, feat) for field in (query_heads, key_heads, value_heads)
     )
-    frame, space = lax.axis_index("tm"), lax.axis_index("space")
-    scalars = jnp.stack([frame, space, lengths[0], task_ids[0]]).astype(jnp.int32)
-
-    incoming = cotangent.reshape(cotangent.shape[2:])
-    pieces = []
-    for distance in range(frames * spaces):
-        block = (space ^ (distance % spaces)) * frames + (frame ^ (distance // spaces))
-        piece = lax.dynamic_slice_in_dim(incoming, block * width, width, 1)
-        if distance:
-            piece = swap(piece, ("tm", "space"), frames * spaces, distance)
-        pieces.append(piece)
+    frame = lax.axis_index("tm")
+    scalars = jnp.stack([frame, lengths[0], task_ids[0]]).astype(jnp.int32)
+
+    packed = pack(cotangent.reshape(cotangent.shape[2:]), frames, spaces)
+    incoming = lax.all_to_all(packed, ("tm", "space"), split_axis=0, concat_axis=0, tiled=True)
+    queries, _ = lax.optimization_barrier((queries, packed))
     weights, attended = forward(scalars, queries, key_rows, values, frames)
     attended = [attended[0]] + [
         swap(attended[distance], "tm", frames, distance) for distance in range(1, frames)
     ]
-    upstream = turn(scalars, pieces, frames, spaces)
+    incoming, _ = lax.optimization_barrier((incoming, weights))
+    upstream = turn(incoming, frames, spaces)
     rows = lax.dynamic_index_in_dim(gains, task_ids[0], 1, keepdims=False)
     product = lax.dynamic_slice_in_dim(rows[0] * rows[1], frame * width, width, 0)
     gain = jnp.broadcast_to(
@@ -368,11 +397,13 @@
     grads = [grads[0]] + [
         swap(grads[distance], "tm", frames, distance) for distance in range(1, frames)
     ]
-    mixed = jnp.concatenate(
-        [mixed] + [swap(mixed, "tm", frames, distance) for distance in range(1, frames)], axis=0
-    )
-    mixed = [mixed] + [swap(mixed, "dp", clips, distance) for distance in range(1, clips)]
-    grad_gains = gain_gradients(scalars, mixed, gains, own, frames)
+    rounds = [("dp", clips, 1 << bit) for bit in range(clips.bit_length() - 1)]
+    rounds += [("tm", frames, 1 << bit) for bit in range(frames.bit_length() - 1)]
+    mixed = [mixed]
+    for axis, size, distance in rounds:
+        joined = jnp.concatenate(mixed, axis=0)
+        mixed = [joined, swap(joined, axis, size, distance)]
+    grad_gains = gain_gradients(scalars, mixed, gains, own, frames, clips)
     results = ()
     for distance in range(frames):
         results = backward(
@@ -480,7 +511,7 @@
 
     def local(query_heads, *others):
         heads = query_heads.shape[3] // HEAD_DIM
-        powers = all(size & (size - 1) == 0 for size in (clips, frames, spaces))
+        powers = all(size & (size - 1) == 0 for size in (clips, frames))
         if powers and frames <= 4 and heads % frames == 0:
             return split_by_heads(query_heads, *others, clips, frames, spaces)
         return split_by_patches(query_heads, *others)

time: 94.5 us -> 80.8 us (0.86)
  local copies, waits for them, and re-layouts: 16.7 us -> 4.65 us
  waiting for transfers between devices: 12.2 us -> 24.2 us
  starting transfers between devices: 36.1 us -> 24.9 us
  Pallas kernels: 26.5 us -> 24.3 us
    ppermute x19 -> x10, starting transfers between devices: 36.1 us -> 17.6 us  [swap(): return lax.ppermute(field, axis, [(i, i ^ distance) for i in range(size)])]
    all_to_all x0 -> x1, waiting for transfers between devices: none -> 14.5 us  [split_by_heads(): lax.all_to_all(packed, ('tm', 'space'), split_axis=0, concat_axis=0, tile...]
    unnamed x41 -> x19, local copies, waits for them, and re-layouts: 14.5 us -> 4.55 us
    all_to_all x0 -> x1, starting transfers between devices: none -> 7.29 us  [split_by_heads(): lax.all_to_all(packed, ('tm', 'space'), split_axis=0, concat_axis=0, tile...]
    ppermute x19 -> x10, waiting for transfers between devices: 12.2 us -> 9.72 us  [swap(): return lax.ppermute(field, axis, [(i, i ^ distance) for i in range(size)])]
    pallas_call x4, Pallas kernels: 11.6 us -> 9.23 us  [backward(): pl.pallas_call(backward_kernel, grid_spec=pltpu.PrefetchScalarGridSpec(nu...]
    dynamic_slice x1 -> x0, local copies, waits for them, and re-layouts: 2.03 us -> none  [split_by_heads(): piece = lax.dynamic_slice_in_dim(incoming, block * width, width, 1)]
    pallas_call x3 -> x4, Pallas kernels: 10.5 us -> 10.8 us  [the longest x1 6.22 us: forward(): pl.pallas_call(forward_kernel, in_specs=[pl.BlockSpec(memory_space=pltpu....]
  transfers between devices with their start and end apart: 19 -> 11, of which waited for: 3 -> 5; matrix products, arithmetic and copies ran while one was open for 0% -> 0% of each run, Pallas kernels for 21% -> 21%
where the time goes in v2:
time: 80.8 us; the launch traced here: 80.3 us
  starting transfers between devices  24.9 us (31%)
  Pallas kernels  24.3 us (30%)
  waiting for transfers between devices  24.2 us (30%)
  local copies, waits for them, and re-layouts  4.65 us (6%)
  between operations  2.03 us (3%)
    ppermute x10, starting transfers between devices, swap(): return lax.ppermute(field, axis, [(i, i ^ distance) for i in range(size)])  17.6 us
    all_to_all x1, waiting for transfers between devices, split_by_heads(): lax.all_to_all(packed, ('tm', 'space'), split_axis=0, concat_axis=0, tile...  14.5 us
    ppermute x10, waiting for transfers between devices, swap(): return lax.ppermute(field, axis, [(i, i ^ distance) for i in range(size)])  9.72 us
    pallas_call x4, Pallas kernels, backward(): pl.pallas_call(backward_kernel, grid_spec=pltpu.PrefetchScalarGridSpec(nu...  9.23 us
    all_to_all x1, starting transfers between devices, split_by_heads(): lax.all_to_all(packed, ('tm', 'space'), split_axis=0, concat_axis=0, tile...  7.29 us
    pallas_call x1, Pallas kernels, forward(): pl.pallas_call(forward_kernel, in_specs=[pl.BlockSpec(memory_space=pltpu....  6.22 us
    unnamed x19, local copies, waits for them, and re-layouts  4.55 us
    pallas_call x1, Pallas kernels, temporal(): pl.pallas_call(functools.partial(temporal_kernel, frames), grid_spec=pltp...  4.36 us
  transfers between devices with their start and end apart: 11, of which 5 were waited for; matrix products, arithmetic and copies ran while one was open for 0% of the time, Pallas kernels for 21%

profile of v2, /device:TPU:0, one launch (start us, length us, event | category | flops | bytes accessed | tf_op | source)
XLA Modules:
  0.0 80.3 jit_solution(12458024785836013777)
XLA Ops:
  0.6 1.1 %copy-done.6 = bf16[1,1,128,3072]{3,2,1,0:T(8,128)(2,1)S(1)} copy-done((bf16[1,1,128,3072]{3,2,1,0:T(8,128)(2,1)S(1)}, bf16[1,1,128,3072]{3,2,1,0:T(8,128)(2,1)}, u32[]{:S(2)}) %copy-start.6) | copy-done | bytes 786456
  2.7 7.3 %all-to-all-start = ((bf16[8,128,384]{2,1,0:T(8,128)(2,1)}), bf16[8,128,384]{2,1,0:T(8,128)(2,1)}, u32[]{:S(2)}, u32[]{:S(2)}) async-start(bf16[8,128,384]{2,1,0:T(8,128)(2,1)} %pack_cotangent.1), calls=%async_computation | async-start | bytes 1572864 | tf_op jit(solution)/shard_map/all_to_all | solution.py:383
  11.4 1.1 %copy-done = bf16[1,1,256,1536]{3,2,1,0:T(8,128)(2,1)S(1)} copy-done((bf16[1,1,256,1536]{3,2,1,0:T(8,128)(2,1)S(1)}, bf16[1,1,256,1536]{3,2,1,0:T(8,128)(2,1)}, u32[]{:S(2)}) %copy-start) | copy-done | bytes 786456
  12.5 1.1 %copy-done.2 = bf16[1,1,256,1536]{3,2,1,0:T(8,128)(2,1)S(1)} copy-done((bf16[1,1,256,1536]{3,2,1,0:T(8,128)(2,1)S(1)}, bf16[1,1,256,1536]{3,2,1,0:T(8,128)(2,1)}, u32[]{:S(2)}) %copy-start.2) | copy-done | bytes 786456
  13.7 1.1 %copy-done.4 = bf16[1,1,256,1536]{3,2,1,0:T(8,128)(2,1)S(1)} copy-done((bf16[1,1,256,1536]{3,2,1,0:T(8,128)(2,1)S(1)}, bf16[1,1,256,1536]{3,2,1,0:T(8,128)(2,1)}, u32[]{:S(2)}) %copy-start.4) | copy-done | bytes 786456
  14.8 6.2 %spatial_forward.1 = (f32[12,256,256]{2,1,0:T(8,128)S(1)}, bf16[3,128,256]{2,1,0:T(8,128)(2,1)S(1)}, bf16[3,128,256]{2,1,0:T(8,128)(2,1)}, bf16[3,128,256]{2,1,0:T(8,128)(2,1)}, bf16[3,128,256]{2,1,0:T(8,128)(2,1)}) custom-call(s32[3]{0:T(128)S(1)} %pad_add_fusion.scalars, bf16[256,1536]{1,0:T(8,128)(2,1)S(1)} %bitcast.12, bf16[256,1536]{1,0:T(8,128)(2,1)S(1)} %bitcast.17, ...), custom_call_target="tpu_custom_call" | custom-call | flops 402653184 | bytes 6291456 | tf_op jit(solution)/shard_map/spatial_forward/pallas_call | solution.py:66
  21.0 2.1 %collective-permute-start = (bf16[3,128,256]{2,1,0:T(8,128)(2,1)}, bf16[3,128,256]{2,1,0:T(8,128)(2,1)}, u32[]{:S(2)}, u32[]{:S(2)}) collective-permute-start(bf16[3,128,256]{2,1,0:T(8,128)(2,1)} %get-tuple-element.26), channel_id=1, source_target_pairs={{0,2},{2,0},{4,6},{6,4},{1,3},{3,1},{5,7},{7,5},{8,10},{10,8},{12,... | collective-permute-start | bytes 589832 | tf_op jit(solution)/shard_map/ppermute | solution.py:366
  23.1 2.4 %collective-permute-start.1 = (bf16[3,128,256]{2,1,0:T(8,128)(2,1)}, bf16[3,128,256]{2,1,0:T(8,128)(2,1)}, u32[]{:S(2)}, u32[]{:S(2)}) collective-permute-start(bf16[3,128,256]{2,1,0:T(8,128)(2,1)} %get-tuple-element.27), channel_id=1, source_target_pairs={{0,4},{2,6},{4,0},{6,2},{1,5},{3,7},{5,1},{7,3},{8,12},{10,14},{12... | collective-permute-start | bytes 589832 | tf_op jit(solution)/shard_map/ppermute | solution.py:366
  25.6 14.5 %all-to-all-done.field_ref = bf16[8,128,384]{2,1,0:T(8,128)(2,1)} async-done(((bf16[8,128,384]{2,1,0:T(8,128)(2,1)}), bf16[8,128,384]{2,1,0:T(8,128)(2,1)}, u32[]{:S(2)}, u32[]{:S(2)}) %all-to-all-start) | async-done | bytes 786464 | tf_op jit(solution)/shard_map/all_to_all | solution.py:383
  40.2 2.3 %turn_cotangent.1.refs_4_ = bf16[2,4,3,128,128]{4,3,2,1,0:T(8,128)(2,1)S(1)} custom-call(bf16[8,128,384]{2,1,0:T(8,128)(2,1)} %all-to-all-done.field_ref), custom_call_target="tpu_custom_call" | custom-call | bytes 1572864 | tf_op jit(solution)/shard_map/turn_cotangent/pallas_call | solution.py:174
  42.5 1.8 %collective-permute-done.1.refs_2_ = bf16[3,128,256]{2,1,0:T(8,128)(2,1)} collective-permute-done((bf16[3,128,256]{2,1,0:T(8,128)(2,1)}, bf16[3,128,256]{2,1,0:T(8,128)(2,1)}, u32[]{:S(2)}, u32[]{:S(2)}) %collective-permute-start.1) | collective-permute-done | bytes 196640 | tf_op jit(solution)/shard_map/ppermute | solution.py:366
  44.5 4.4 %temporal.1 = (bf16[3,128,256]{2,1,0:T(8,128)(2,1)S(1)}, bf16[3,128,256]{2,1,0:T(8,128)(2,1)S(1)}, bf16[3,128,256]{2,1,0:T(8,128)(2,1)S(1)}, bf16[3,128,256]{2,1,0:T(8,128)(2,1)S(1)}, f32[8,128]{1,0:T(8,128)S(1)}) custom-call(s32[3]{0:T(128)S(1)} %pad_add_fusion.scalars, bf16[3,128,256]{2,1,0:T(8,128)(2,1)S(1)} %get-tuple-element.25.refs_0_, ...), custom_call_target="tpu_custom_call" | custom-call | flops 19660800 | bytes 2359296 | tf_op jit(solution)/shard_map/temporal/pallas_call | solution.py:302
  49.1 4.7 %collective-permute-start.4 = (bf16[3,128,256]{2,1,0:T(8,128)(2,1)S(1)}, bf16[3,128,256]{2,1,0:T(8,128)(2,1)S(1)}, u32[]{:S(2)}, u32[]{:S(2)}) collective-permute-start(bf16[3,128,256]{2,1,0:T(8,128)(2,1)S(1)} %get-tuple-element.31), channel_id=1, source_target_pairs={{0,4},{2,6},{4,0},{6,2},{1,5},{3,7},{5,1},{7,3},{8,12},{10,14},{12... | collective-permute-start | bytes 589832 | tf_op jit(solution)/shard_map/ppermute | solution.py:366
  53.9 1.6 %collective-permute-start.7 = (f32[16,128]{1,0:T(8,128)S(1)}, f32[16,128]{1,0:T(8,128)S(1)}, u32[]{:S(2)}, u32[]{:S(2)}) collective-permute-start(f32[16,128]{1,0:T(8,128)S(1)} %pad_maximum_fusion.1), channel_id=1, source_target_pairs={{0,16},{8,24},{16,0},{24,8},{1,17},{9,25},{17,1},{25,9},{2,18},{10... | collective-permute-start | bytes 24584 | tf_op jit(solution)/shard_map/ppermute | solution.py:366
  55.4 2.2 %collective-permute-done.7 = f32[16,128]{1,0:T(8,128)S(1)} collective-permute-done((f32[16,128]{1,0:T(8,128)S(1)}, f32[16,128]{1,0:T(8,128)S(1)}, u32[]{:S(2)}, u32[]{:S(2)}) %collective-permute-start.7) | collective-permute-done | bytes 8224 | tf_op jit(solution)/shard_map/ppermute | solution.py:366
  57.6 2.0 %collective-permute-start.8 = (f32[32,128]{1,0:T(8,128)S(1)}, f32[32,128]{1,0:T(8,128)S(1)}, u32[]{:S(2)}, u32[]{:S(2)}) collective-permute-start(f32[32,128]{1,0:T(8,128)S(1)} %pad_maximum_fusion), channel_id=1, source_target_pairs={{0,2},{2,0},{4,6},{6,4},{1,3},{3,1},{5,7},{7,5},{8,10},{10,8},{12,... | collective-permute-start | bytes 49160 | tf_op jit(solution)/shard_map/ppermute | solution.py:366
  59.5 3.4 %collective-permute-done.8 = f32[32,128]{1,0:T(8,128)S(1)} collective-permute-done((f32[32,128]{1,0:T(8,128)S(1)}, f32[32,128]{1,0:T(8,128)S(1)}, u32[]{:S(2)}, u32[]{:S(2)}) %collective-permute-start.8) | collective-permute-done | bytes 16416 | tf_op jit(solution)/shard_map/ppermute | solution.py:366
  62.9 4.5 %collective-permute-start.9 = (f32[64,128]{1,0:T(8,128)S(1)}, f32[64,128]{1,0:T(8,128)S(1)}, u32[]{:S(2)}, u32[]{:S(2)}) collective-permute-start(f32[64,128]{1,0:T(8,128)S(1)} %constant_dynamic-update-slice_fusion.refs_0_), channel_id=1, source_target_pairs={{0,4},{2,6},{4,0},{6,2},{1,5},{3,7},{5,1},{7,3},{8,12},{10,14},{12... | collective-permute-start | bytes 98312 | tf_op jit(solution)/shard_map/ppermute | solution.py:366
  67.4 2.3 %spatial_backward.4 = (bf16[256,1536]{1,0:T(8,128)(2,1)}, bf16[256,1536]{1,0:T(8,128)(2,1)}) custom-call(s32[3]{0:T(128)S(1)} %pad_add_fusion.scalars, bf16[256,1536]{1,0:T(8,128)(2,1)S(1)} %bitcast.13, bf16[256,1536]{1,0:T(8,128)(2,1)S(1)} %bitcast.18, bf16[256,1536]{1,0:T(8,128)(2,1)S(1)} %bitcast.23, f32[12,256,256]{2,1,0:T(8,128)S(1)} %get-tuple-element.24.weights_ref, ...), custom_call_target="tpu_custom_call" | custom-call | flops 150994944 | bytes 1966080 | tf_op jit(solution)/shard_map/spatial_backward/pallas_call | solution.py:106
  69.8 2.3 %collective-permute-done.9.refs_1_ = f32[64,128]{1,0:T(8,128)S(1)} collective-permute-done((f32[64,128]{1,0:T(8,128)S(1)}, f32[64,128]{1,0:T(8,128)S(1)}, u32[]{:S(2)}, u32[]{:S(2)}) %collective-permute-start.9) | collective-permute-done | bytes 32800 | tf_op jit(solution)/shard_map/ppermute | solution.py:366
  72.1 1.3 %gain_gradients.1 = f32[2,16,1536]{2,1,0:T(8,128)} custom-call(s32[3]{0:T(128)S(1)} %pad_add_fusion.scalars, f32[64,128]{1,0:T(8,128)S(1)} %constant_dynamic-update-slice_fusion.refs_0_, f32[64,128]{1,0:T(8,128)S(1)} %collective-permute-done.9.refs_1_, f32[2,16,1536]{2,1,0:T(8,128)S(1)} %copy-done.7), custom_call_target="tpu_custom_call" | custom-call | tf_op jit(solution)/shard_map/gain_gradients/pallas_call | solution.py:354
  73.4 2.3 %spatial_backward.5 = (bf16[256,1536]{1,0:T(8,128)(2,1)}, bf16[256,1536]{1,0:T(8,128)(2,1)}) custom-call(s32[3]{0:T(128)S(1)} %pad_add_fusion.scalars, bf16[256,1536]{1,0:T(8,128)(2,1)S(1)} %bitcast.14, bf16[256,1536]{1,0:T(8,128)(2,1)S(1)} %bitcast.19, bf16[256,1536]{1,0:T(8,128)(2,1)S(1)} %bitcast.24, ...), custom_call_target="tpu_custom_call", output_to_operand_aliasing={{0}: (6, {}), {1}: (7, {})} | custom-call | flops 150994944 | bytes 1966080 | tf_op jit(solution)/shard_map/spatial_backward/pallas_call | solution.py:106
  75.7 2.3 %spatial_backward.6 = (bf16[256,1536]{1,0:T(8,128)(2,1)}, bf16[256,1536]{1,0:T(8,128)(2,1)}) custom-call(s32[3]{0:T(128)S(1)} %pad_add_fusion.scalars, bf16[256,1536]{1,0:T(8,128)(2,1)S(1)} %bitcast.15, bf16[256,1536]{1,0:T(8,128)(2,1)S(1)} %bitcast.20, bf16[256,1536]{1,0:T(8,128)(2,1)S(1)} %bitcast.25, ...), custom_call_target="tpu_custom_call", output_to_operand_aliasing={{0}: (6, {}), {1}: (7, {})} | custom-call | flops 150994944 | bytes 1966080 | tf_op jit(solution)/shard_map/spatial_backward/pallas_call | solution.py:106
  78.0 2.3 %spatial_backward.7 = (bf16[256,1536]{1,0:T(8,128)(2,1)}, bf16[256,1536]{1,0:T(8,128)(2,1)}) custom-call(s32[3]{0:T(128)S(1)} %pad_add_fusion.scalars, bf16[256,1536]{1,0:T(8,128)(2,1)S(1)} %bitcast.16, bf16[256,1536]{1,0:T(8,128)(2,1)S(1)} %bitcast.21, bf16[256,1536]{1,0:T(8,128)(2,1)S(1)} %bitcast.26, ...), custom_call_target="tpu_custom_call", output_to_operand_aliasing={{0}: (6, {}), {1}: (7, {})} | custom-call | flops 150994944 | bytes 1966080 | tf_op jit(solution)/shard_map/spatial_backward/pallas_call | solution.py:106
  (32 shorter events, 1.6 us)
Async XLA Ops:
  0.6 1.1 %copy-start.6 = (bf16[1,1,128,3072]{3,2,1,0:T(8,128)(2,1)S(1)}, bf16[1,1,128,3072]{3,2,1,0:T(8,128)(2,1)}, u32[]{:S(2)}) copy-start(bf16[1,1,128,3072]{3,2,1,0:T(8,128)(2,1)} %param.10) | copy-start | bytes 2359300
  1.8 23.8 %copy-start.7 = (f32[2,16,1536]{2,1,0:T(8,128)S(1)}, f32[2,16,1536]{2,1,0:T(8,128)}, u32[]{:S(2)}) copy-start(f32[2,16,1536]{2,1,0:T(8,128)} %refs_2_.1) | copy-start | bytes 589828
  2.7 37.4 %all-to-all-start = ((bf16[8,128,384]{2,1,0:T(8,128)(2,1)}), bf16[8,128,384]{2,1,0:T(8,128)(2,1)}, u32[]{:S(2)}, u32[]{:S(2)}) async-start(bf16[8,128,384]{2,1,0:T(8,128)(2,1)} %pack_cotangent.1), calls=%async_computation | async-start | bytes 1572864 | tf_op jit(solution)/shard_map/all_to_all | solution.py:383
  11.4 1.1 %copy-start = (bf16[1,1,256,1536]{3,2,1,0:T(8,128)(2,1)S(1)}, bf16[1,1,256,1536]{3,2,1,0:T(8,128)(2,1)}, u32[]{:S(2)}) copy-start(bf16[1,1,256,1536]{3,2,1,0:T(8,128)(2,1)} %param.7) | copy-start | bytes 2359300
  12.5 1.1 %copy-start.2 = (bf16[1,1,256,1536]{3,2,1,0:T(8,128)(2,1)S(1)}, bf16[1,1,256,1536]{3,2,1,0:T(8,128)(2,1)}, u32[]{:S(2)}) copy-start(bf16[1,1,256,1536]{3,2,1,0:T(8,128)(2,1)} %param.8) | copy-start | bytes 2359300
  13.7 1.1 %copy-start.4 = (bf16[1,1,256,1536]{3,2,1,0:T(8,128)(2,1)S(1)}, bf16[1,1,256,1536]{3,2,1,0:T(8,128)(2,1)}, u32[]{:S(2)}) copy-start(bf16[1,1,256,1536]{3,2,1,0:T(8,128)(2,1)} %param.9) | copy-start | bytes 2359300
  21.0 21.5 %collective-permute-start = (bf16[3,128,256]{2,1,0:T(8,128)(2,1)}, bf16[3,128,256]{2,1,0:T(8,128)(2,1)}, u32[]{:S(2)}, u32[]{:S(2)}) collective-permute-start(bf16[3,128,256]{2,1,0:T(8,128)(2,1)} %get-tuple-element.26), channel_id=1, source_target_pairs={{0,2},{2,0},{4,6},{6,4},{1,3},{3,1},{5,7},{7,5},{8,10},{10,8},{12,... | collective-permute-start | bytes 589832 | tf_op jit(solution)/shard_map/ppermute | solution.py:366
  23.1 21.3 %collective-permute-start.1 = (bf16[3,128,256]{2,1,0:T(8,128)(2,1)}, bf16[3,128,256]{2,1,0:T(8,128)(2,1)}, u32[]{:S(2)}, u32[]{:S(2)}) collective-permute-start(bf16[3,128,256]{2,1,0:T(8,128)(2,1)} %get-tuple-element.27), channel_id=1, source_target_pairs={{0,4},{2,6},{4,0},{6,2},{1,5},{3,7},{5,1},{7,3},{8,12},{10,14},{12... | collective-permute-start | bytes 589832 | tf_op jit(solution)/shard_map/ppermute | solution.py:366
  25.5 18.9 %collective-permute-start.2 = (bf16[3,128,256]{2,1,0:T(8,128)(2,1)}, bf16[3,128,256]{2,1,0:T(8,128)(2,1)}, u32[]{:S(2)}, u32[]{:S(2)}) collective-permute-start(bf16[3,128,256]{2,1,0:T(8,128)(2,1)} %get-tuple-element.28), channel_id=1, source_target_pairs={{0,6},{2,4},{4,2},{6,0},{1,7},{3,5},{5,3},{7,1},{8,14},{10,12},{12... | collective-permute-start | bytes 589832 | tf_op jit(solution)/shard_map/ppermute | solution.py:366
  40.2 27.3 %copy-start.1 = (bf16[1,1,256,1536]{3,2,1,0:T(8,128)(2,1)S(1)}, bf16[1,1,256,1536]{3,2,1,0:T(8,128)(2,1)}, u32[]{:S(2)}) copy-start(bf16[1,1,256,1536]{3,2,1,0:T(8,128)(2,1)} %param.7) | copy-start | bytes 2359300
  40.2 27.3 %copy-start.3 = (bf16[1,1,256,1536]{3,2,1,0:T(8,128)(2,1)S(1)}, bf16[1,1,256,1536]{3,2,1,0:T(8,128)(2,1)}, u32[]{:S(2)}) copy-start(bf16[1,1,256,1536]{3,2,1,0:T(8,128)(2,1)} %param.8) | copy-start | bytes 2359300
  40.2 27.3 %copy-start.5 = (bf16[1,1,256,1536]{3,2,1,0:T(8,128)(2,1)S(1)}, bf16[1,1,256,1536]{3,2,1,0:T(8,128)(2,1)}, u32[]{:S(2)}) copy-start(bf16[1,1,256,1536]{3,2,1,0:T(8,128)(2,1)} %param.9) | copy-start | bytes 2359300
  48.8 5.0 %collective-permute-start.6 = (f32[8,128]{1,0:T(8,128)S(1)}, f32[8,128]{1,0:T(8,128)S(1)}, u32[]{:S(2)}, u32[]{:S(2)}) collective-permute-start(f32[8,128]{1,0:T(8,128)S(1)} %get-tuple-element.42), channel_id=1, source_target_pairs={{0,8},{8,0},{16,24},{24,16},{1,9},{9,1},{17,25},{25,17},{2,10},{10... | collective-permute-start | bytes 12296 | tf_op jit(solution)/shard_map/ppermute | solution.py:366
  48.9 29.0 %collective-permute-start.3 = (bf16[3,128,256]{2,1,0:T(8,128)(2,1)S(1)}, bf16[3,128,256]{2,1,0:T(8,128)(2,1)S(1)}, u32[]{:S(2)}, u32[]{:S(2)}) collective-permute-start(bf16[3,128,256]{2,1,0:T(8,128)(2,1)S(1)} %get-tuple-element.30), channel_id=1, source_target_pairs={{0,6},{2,4},{4,2},{6,0},{1,7},{3,5},{5,3},{7,1},{8,14},{10,12},{12... | collective-permute-start | bytes 589832 | tf_op jit(solution)/shard_map/ppermute | solution.py:366
  49.1 26.5 %collective-permute-start.4 = (bf16[3,128,256]{2,1,0:T(8,128)(2,1)S(1)}, bf16[3,128,256]{2,1,0:T(8,128)(2,1)S(1)}, u32[]{:S(2)}, u32[]{:S(2)}) collective-permute-start(bf16[3,128,256]{2,1,0:T(8,128)(2,1)S(1)} %get-tuple-element.31), channel_id=1, source_target_pairs={{0,4},{2,6},{4,0},{6,2},{1,5},{3,7},{5,1},{7,3},{8,12},{10,14},{12... | collective-permute-start | bytes 589832 | tf_op jit(solution)/shard_map/ppermute | solution.py:366
  53.9 19.5 %collective-permute-start.5 = (bf16[3,128,256]{2,1,0:T(8,128)(2,1)S(1)}, bf16[3,128,256]{2,1,0:T(8,128)(2,1)S(1)}, u32[]{:S(2)}, u32[]{:S(2)}) collective-permute-start(bf16[3,128,256]{2,1,0:T(8,128)(2,1)S(1)} %get-tuple-element.32), channel_id=1, source_target_pairs={{0,2},{2,0},{4,6},{6,4},{1,3},{3,1},{5,7},{7,5},{8,10},{10,8},{12,... | collective-permute-start | bytes 589832 | tf_op jit(solution)/shard_map/ppermute | solution.py:366
  53.9 3.7 %collective-permute-start.7 = (f32[16,128]{1,0:T(8,128)S(1)}, f32[16,128]{1,0:T(8,128)S(1)}, u32[]{:S(2)}, u32[]{:S(2)}) collective-permute-start(f32[16,128]{1,0:T(8,128)S(1)} %pad_maximum_fusion.1), channel_id=1, source_target_pairs={{0,16},{8,24},{16,0},{24,8},{1,17},{9,25},{17,1},{25,9},{2,18},{10... | collective-permute-start | bytes 24584 | tf_op jit(solution)/shard_map/ppermute | solution.py:366
  57.6 5.3 %collective-permute-start.8 = (f32[32,128]{1,0:T(8,128)S(1)}, f32[32,128]{1,0:T(8,128)S(1)}, u32[]{:S(2)}, u32[]{:S(2)}) collective-permute-start(f32[32,128]{1,0:T(8,128)S(1)} %pad_maximum_fusion), channel_id=1, source_target_pairs={{0,2},{2,0},{4,6},{6,4},{1,3},{3,1},{5,7},{7,5},{8,10},{10,8},{12,... | collective-permute-start | bytes 49160 | tf_op jit(solution)/shard_map/ppermute | solution.py:366
  62.9 9.2 %collective-permute-start.9 = (f32[64,128]{1,0:T(8,128)S(1)}, f32[64,128]{1,0:T(8,128)S(1)}, u32[]{:S(2)}, u32[]{:S(2)}) collective-permute-start(f32[64,128]{1,0:T(8,128)S(1)} %constant_dynamic-update-slice_fusion.refs_0_), channel_id=1, source_target_pairs={{0,4},{2,6},{4,0},{6,2},{1,5},{3,7},{5,1},{7,3},{8,12},{10,14},{12... | collective-permute-start | bytes 98312 | tf_op jit(solution)/shard_map/ppermute | solution.py:366

commit v3 on v2

--- a/solution.py
+++ b/solution.py
@@ -16,6 +16,10 @@
     return pltpu.CompilerParams(vmem_limit_bytes=(16 if patches <= 512 else 60) * MIB)
 
 
+def cost(microseconds):
+    return pl.CostEstimate(flops=int(microseconds * 1e8), bytes_accessed=0, transcendentals=0)
+
+
 def columns_dot(left, right):
     return lax.dot_general(
         left, right, (((1,), (1,)), ((), ())), preferred_element_type=jnp.float32
@@ -30,10 +34,12 @@
     return jnp.bitwise_xor(scalars[0], distance)
 
 
-def forward_kernel(scalars, query_ref, key_ref, value_ref, weights_ref, *refs):
-    (queries, key_rows, values, arrived), attended_refs = refs[-4:], refs[:-4]
+def forward_kernel(scalars, query_ref, key_ref, value_ref, *refs):
+    (queries, turned_keys, values, weights_ref), refs = refs[:4], refs[4:]
+    (key_rows, arrived), attended_refs = refs[-2:], refs[:-2]
     score_scale = HEAD_DIM ** (-0.5)
     groups, _, width = queries.shape
+    own = width // HEAD_DIM
     copies = []
     for group in range(groups):
         cols = pl.ds(pl.multiple_of(partner(scalars, group) * width, HEAD_DIM), width)
@@ -48,86 +54,92 @@
     for group in range(groups):
         for copy in copies[3 * group : 3 * group + 3]:
             copy.wait()
-        for head in range(width // HEAD_DIM):
+        for head in range(own):
             cols = pl.ds(head * HEAD_DIM, HEAD_DIM)
-            scores = columns_dot(key_rows[group, :, cols], queries[group, :, cols])
+            keys_here = key_rows[group, :, cols]
+            scores = columns_dot(keys_here, queries[group, :, cols])
             largest = jnp.max(scores, axis=0, keepdims=True)
             raised = jnp.exp((scores - largest) * score_scale)
             weights = raised * (1.0 / jnp.sum(raised, axis=0, keepdims=True))
-            weights_ref[group * (width // HEAD_DIM) + head] = weights
+            weights_ref[group * own + head] = weights
             attended = dot(values[group, :, cols].T, weights.astype(jnp.bfloat16))
             attended_refs[group][head] = attended.astype(jnp.bfloat16)
+            turned_keys[group * own + head] = keys_here.T
 
 
 def forward(scalars, queries, key_rows, values, groups):
     patches, feat = queries.shape
     heads = feat // HEAD_DIM
     own = heads // groups
-    weights, *attended = pl.pallas_call(
+    by_group = (groups, patches, feat // groups)
+    *kept, weights, attended = [
+        jax.ShapeDtypeStruct(by_group, jnp.bfloat16),
+        jax.ShapeDtypeStruct((heads, HEAD_DIM, patches), jnp.bfloat16),
+        jax.ShapeDtypeStruct(by_group, jnp.bfloat16),
+        jax.ShapeDtypeStruct((heads, patches, patches), jnp.float32),
+        jax.ShapeDtypeStruct((own, HEAD_DIM, patches), jnp.bfloat16),
+    ]
+    shapes = [*kept, weights] + [attended] * groups
+    fields = [
+        pltpu.with_memory_space_constraint(field, pltpu.HBM) for field in (queries, key_rows, values)
+    ]
+    results = pl.pallas_call(
         forward_kernel,
         in_specs=[pl.BlockSpec(memory_space=pltpu.SMEM)]
         + [pl.BlockSpec(memory_space=pltpu.HBM)] * 3,
-        out_specs=[pl.BlockSpec(memory_space=pltpu.VMEM)] * (1 + groups),
-        scratch_shapes=[pltpu.VMEM((groups, patches, feat // groups), jnp.bfloat16)] * 3
-        + [pltpu.SemaphoreType.DMA((groups, 3))],
-        out_shape=[jax.ShapeDtypeStruct((heads, patches, patches), jnp.float32)]
-        + [jax.ShapeDtypeStruct((own, HEAD_DIM, patches), jnp.bfloat16)] * groups,
+        out_specs=[pl.BlockSpec(memory_space=pltpu.VMEM)] * len(shapes),
+        scratch_shapes=[pltpu.VMEM(by_group, jnp.bfloat16), pltpu.SemaphoreType.DMA((groups, 3))],
+        out_shape=shapes,
         compiler_params=params(patches),
-        cost_estimate=pl.CostEstimate(
-            flops=4 * heads * patches * patches * HEAD_DIM,
-            bytes_accessed=heads * patches * (patches * 4 + 8 * HEAD_DIM),
-            transcendentals=heads * patches * patches,
-        ),
+        cost_estimate=cost(6),
         name="spatial_forward",
-    )(scalars, queries, key_rows, values)
-    return weights, attended
-
-
-def backward_kernel(scalars, query_ref, key_ref, value_ref, weights_ref, grad_ref, *refs):
-    gq_ref, gk_ref = refs[-2:]
+    )(scalars, *fields)
+    return results[:4], results[4:]
+
+
+def backward_kernel(distance, scalars, *refs):
+    queries, turned_keys, values, weights_ref, grad_ref = refs[:5]
+    gq_ref, gk_ref, gq, gk, sent = refs[-5:]
     score_scale = HEAD_DIM ** (-0.5)
-    for head in range(weights_ref.shape[0]):
+    own = grad_ref.shape[0]
+    copies = []
+    for head in range(own):
         cols = pl.ds(head * HEAD_DIM, HEAD_DIM)
-        weights = weights_ref[head]
-        spatial_grad = dot(value_ref[:, cols], grad_ref[head])
+        weights = weights_ref[distance * own + head]
+        spatial_grad = dot(values[distance, :, cols], grad_ref[head])
         row_sum = jnp.sum(spatial_grad * weights, axis=0, keepdims=True)
         scores = (weights * (spatial_grad - row_sum) * score_scale).astype(jnp.bfloat16)
-        gk_ref[:, cols] = dot(scores, query_ref[:, cols]).astype(jnp.bfloat16)
-        grad_query = dot(key_ref[:, cols].T, scores).astype(jnp.bfloat16)
-        gq_ref[:, cols] = grad_query.T
-
-
-def backward(scalars, queries, key_rows, values, weights, grads, distance, earlier):
-    patches, feat = queries.shape
+        gk[head] = dot(scores, queries[distance, :, cols]).astype(jnp.bfloat16)
+        gq[head] = dot(turned_keys[distance * own + head], scores).astype(jnp.bfloat16).T
+        start = (partner(scalars, distance) * own + head) * HEAD_DIM
+        there = pl.ds(pl.multiple_of(start, HEAD_DIM), HEAD_DIM)
+        for side, (source, target) in enumerate(((gq, gq_ref), (gk, gk_ref))):
+            copy = pltpu.make_async_copy(
+                source.at[head], target.at[:, there], sent.at[head, side]
+            )
+            copy.start()
+            copies.append(copy)
+    for copy in copies:
+        copy.wait()
+
+
+def backward(scalars, kept, grads, distance, earlier):
+    groups, patches, width = kept[0].shape
     own = grads.shape[0]
-    field = pl.BlockSpec(
-        (patches, own * HEAD_DIM), lambda i, sc: (0, partner(sc, distance))
-    )
     return pl.pallas_call(
-        backward_kernel,
-        grid_spec=pltpu.PrefetchScalarGridSpec(
-            num_scalar_prefetch=1,
-            grid=(1,),
-            in_specs=[
-                field,
-                field,
-                field,
-                pl.BlockSpec((own, patches, patches), lambda i, sc: (distance, 0, 0)),
-                pl.BlockSpec((own, HEAD_DIM, patches), lambda i, sc: (0, 0, 0)),
-            ]
-            + [pl.BlockSpec(memory_space=pl.ANY)] * len(earlier),
-            out_specs=[field, field],
-        ),
-        out_shape=[jax.ShapeDtypeStruct((patches, feat), jnp.bfloat16)] * 2,
+        functools.partial(backward_kernel, distance),
+        in_specs=[pl.BlockSpec(memory_space=pltpu.SMEM)]
+        + [pl.BlockSpec(memory_space=pltpu.VMEM)] * 5
+        + [pl.BlockSpec(memory_space=pl.ANY)] * len(earlier),
+        out_specs=[pl.BlockSpec(memory_space=pl.ANY)] * 2,
+        scratch_shapes=[pltpu.VMEM((own, patches, HEAD_DIM), jnp.bfloat16)] * 2
+        + [pltpu.SemaphoreType.DMA((own, 2))],
+        out_shape=[jax.ShapeDtypeStruct((patches, groups * width), jnp.bfloat16)] * 2,
         input_output_aliases={6 + index: index for index in range(len(earlier))},
         compiler_params=params(patches),
-        cost_estimate=pl.CostEstimate(
-            flops=6 * own * patches * patches * HEAD_DIM,
-            bytes_accessed=own * patches * (patches * 4 + 12 * HEAD_DIM),
-            transcendentals=0,
-        ),
+        cost_estimate=cost(2),
         name="spatial_backward",
-    )(scalars, queries, key_rows, values, weights, grads, *earlier)
+    )(scalars, *kept, grads, *earlier)
 
 
 def pack_kernel(frames, spaces, field_ref, packed_ref, sent):
@@ -154,11 +166,9 @@
         out_shape=jax.ShapeDtypeStruct((devices, patches, feat // devices), field.dtype),
         scratch_shapes=[pltpu.SemaphoreType.DMA((devices,))],
         compiler_params=params(0),
-        cost_estimate=pl.CostEstimate(
-            flops=0, bytes_accessed=4 * patches * feat, transcendentals=0
-        ),
+        cost_estimate=cost(1),
         name="pack_cotangent",
-    )(field)
+    )(pltpu.with_memory_space_constraint(field, pltpu.HBM))
 
 
 def turn_kernel(field_ref, turned_ref):
@@ -178,9 +188,7 @@
         out_specs=pl.BlockSpec((spaces, frames, 1, HEAD_DIM, patches), lambda i: (0, 0, i, 0, 0)),
         out_shape=jax.ShapeDtypeStruct((spaces, frames, heads, HEAD_DIM, patches), field.dtype),
         compiler_params=params(patches),
-        cost_estimate=pl.CostEstimate(
-            flops=0, bytes_accessed=4 * devices * patches * feat, transcendentals=0
-        ),
+        cost_estimate=cost(2),
         name="turn_cotangent",
     )(field)
 
@@ -319,11 +327,7 @@
         out_shape=[jax.ShapeDtypeStruct((heads, feat, patches), jnp.bfloat16)] * frames
         + [jax.ShapeDtypeStruct((rows, feat), jnp.float32)],
         compiler_params=params(patches),
-        cost_estimate=pl.CostEstimate(
-            flops=heads * patches * feat * 200,
-            bytes_accessed=6 * frames * heads * patches * feat,
-            transcendentals=heads * patches * 16,
-        ),
+        cost_estimate=cost(4),
         name="temporal",
     )(scalars, *attended, upstream, gain)
     return grads, mixed
@@ -358,6 +362,7 @@
         out_specs=pl.BlockSpec(memory_space=pltpu.VMEM),
         out_shape=jax.ShapeDtypeStruct(gains.shape, jnp.float32),
         compiler_params=params(0),
+        cost_estimate=cost(1),
         name="gain_gradients",
     )(scalars, *mixed, gains)
 
@@ -382,11 +387,11 @@
     packed = pack(cotangent.reshape(cotangent.shape[2:]), frames, spaces)
     incoming = lax.all_to_all(packed, ("tm", "space"), split_axis=0, concat_axis=0, tiled=True)
     queries, _ = lax.optimization_barrier((queries, packed))
-    weights, attended = forward(scalars, queries, key_rows, values, frames)
+    kept, attended = forward(scalars, queries, key_rows, values, frames)
     attended = [attended[0]] + [
         swap(attended[distance], "tm", frames, distance) for distance in range(1, frames)
     ]
-    incoming, _ = lax.optimization_barrier((incoming, weights))
+    incoming, _ = lax.optimization_barrier((incoming, kept[3]))
     upstream = turn(incoming, frames, spaces)
     rows = lax.dynamic_index_in_dim(gains, task_ids[0], 1, keepdims=False)
     product = lax.dynamic_slice_in_dim(rows[0] * rows[1], frame * width, width, 0)
@@ -399,16 +404,21 @@
     ]
     rounds = [("dp", clips, 1 << bit) for bit in range(clips.bit_length() - 1)]
     rounds += [("tm", frames, 1 << bit) for bit in range(frames.bit_length() - 1)]
-    mixed = [mixed]
-    for axis, size, distance in rounds:
+    mixed, results, distance = [mixed], (), 0
+    for number, (axis, size, step) in enumerate(rounds):
         joined = jnp.concatenate(mixed, axis=0)
-        mixed = [joined, swap(joined, axis, size, distance)]
+        if results and number >= 2:
+            joined, results = lax.optimization_barrier((joined, results))
+        mixed = [joined, swap(joined, axis, size, step)]
+        if number < 2 and distance < frames:
+            here, mixed[1] = lax.optimization_barrier((grads[distance], mixed[1]))
+            results = backward(scalars, kept, here, distance, results)
+            distance += 1
     grad_gains = gain_gradients(scalars, mixed, gains, own, frames, clips)
-    results = ()
-    for distance in range(frames):
-        results = backward(
-            scalars, queries, key_rows, values, weights, grads[distance], distance, results
-        )
+    if results:
+        grad_gains, results = lax.optimization_barrier((grad_gains, results))
+    for distance in range(distance, frames):
+        results = backward(scalars, kept, grads[distance], distance, results)
     grad_queries, grad_keys = results
     return (
         grad_queries.reshape(query_heads.shape),
@@ -460,8 +470,8 @@
         field.reshape(patches, feat) for field in (query_heads, key_heads, value_heads)
     )
     scalars = jnp.zeros((1,), jnp.int32)
-    weights, attended = forward(scalars, queries, key_rows, values, heads)
-    attended_field = jnp.transpose(jnp.concatenate(attended), (2, 0, 1)).reshape(1, 1, patches, feat)
+    kept, attended = forward(scalars, queries, key_rows, values, 1)
+    attended_field = jnp.transpose(attended[0], (2, 0, 1)).reshape(1, 1, patches, feat)
     upstream = lax.all_to_all(
         lax.all_to_all(cotangent, "space", split_axis=3, concat_axis=2, tiled=True),
         "tm",
@@ -496,9 +506,7 @@
         tiled=True,
     )
     head_grads = jnp.transpose(returned.reshape(patches, heads, HEAD_DIM), (1, 2, 0))
-    grad_queries, grad_keys = backward(
-        scalars, queries, key_rows, values, weights, head_grads, 0, ()
-    )
+    grad_queries, grad_keys = backward(scalars, kept, head_grads, 0, ())
     return (
         grad_queries.reshape(query_heads.shape),
         grad_keys.reshape(query_heads.shape),

time: 80.8 us -> 102 us (1.26)
  Pallas kernels: 24.3 us -> 49.2 us
  local copies, waits for them, and re-layouts: 4.65 us -> 2.76 us
  starting transfers between devices: 24.9 us -> 23.7 us
    pallas_call x1, Pallas kernels: 0.93 us -> 25 us  [pack(): pl.pallas_call(functools.partial(pack_kernel, frames, spaces), in_specs=[...]
    unnamed x19 -> x14, local copies, waits for them, and re-layouts: 4.55 us -> 2.66 us
    ppermute x10, starting transfers between devices: 17.6 us -> 16.4 us  [swap(): return lax.ppermute(field, axis, [(i, i ^ distance) for i in range(size)])]
  transfers between devices with their start and end apart: 11 -> 11, of which waited for: 5 -> 4; matrix products, arithmetic and copies ran while one was open for 0% -> 0% of each run, Pallas kernels for 21% -> 17%
where the time goes in v3:
time: 102 us
  Pallas kernels  49.2 us (48%)
  waiting for transfers between devices  24 us (24%)
  starting transfers between devices  23.7 us (23%)
  local copies, waits for them, and re-layouts  2.76 us (3%)
  between operations  2.07 us (2%)
    pallas_call x1, Pallas kernels, pack(): pl.pallas_call(functools.partial(pack_kernel, frames, spaces), in_specs=[...  25 us
    ppermute x10, starting transfers between devices, swap(): return lax.ppermute(field, axis, [(i, i ^ distance) for i in range(size)])  16.4 us
    all_to_all x1, waiting for transfers between devices, split_by_heads(): lax.all_to_all(packed, ('tm', 'space'), split_axis=0, concat_axis=0, tile...  14.5 us
    ppermute x10, waiting for transfers between devices, swap(): return lax.ppermute(field, axis, [(i, i ^ distance) for i in range(size)])  9.51 us
    pallas_call x4, Pallas kernels, backward(): pl.pallas_call(functools.partial(backward_kernel, distance), in_specs=[pl...  9.17 us
    all_to_all x1, starting transfers between devices, split_by_heads(): lax.all_to_all(packed, ('tm', 'space'), split_axis=0, concat_axis=0, tile...  7.29 us
    pallas_call x1, Pallas kernels, forward(): pl.pallas_call(forward_kernel, in_specs=[pl.BlockSpec(memory_space=pltpu....  7.1 us
    pallas_call x1, Pallas kernels, temporal(): pl.pallas_call(functools.partial(temporal_kernel, frames), grid_spec=pltp...  4.36 us
  transfers between devices with their start and end apart: 11, of which 4 were waited for; matrix products, arithmetic and copies ran while one was open for 0% of the time, Pallas kernels for 17%

profile of v3, /device:TPU:0, one launch (start us, length us, event | category | flops | bytes accessed | tf_op | source)
XLA Modules:
  0.0 102.0 jit_solution(3263012636107339666)
XLA Ops:
  0.6 25.0 %pack_cotangent.1 = bf16[8,128,384]{2,1,0:T(8,128)(2,1)} custom-call(bf16[128,3072]{1,0:T(8,128)(2,1)} %bitcast.17), custom_call_target="tpu_custom_call" | custom-call | flops 100000000 | tf_op jit(solution)/shard_map/pack_cotangent/pallas_call | solution.py:162
  25.6 7.3 %all-to-all-start = ((bf16[8,128,384]{2,1,0:T(8,128)(2,1)}), bf16[8,128,384]{2,1,0:T(8,128)(2,1)}, u32[]{:S(2)}, u32[]{:S(2)}) async-start(bf16[8,128,384]{2,1,0:T(8,128)(2,1)} %pack_cotangent.1), calls=%async_computation | async-start | bytes 1572864 | tf_op jit(solution)/shard_map/all_to_all | solution.py:388
  34.3 7.1 %spatial_forward.1 = (bf16[4,256,384]{2,1,0:T(8,128)(2,1)S(1)}, bf16[12,128,256]{2,1,0:T(8,128)(2,1)S(1)}, bf16[4,256,384]{2,1,0:T(8,128)(2,1)S(1)}, f32[12,256,...) custom-call(s32[3]{0:T(128)S(1)} %pad_add_fusion.scalars, ...), custom_call_target="tpu_custom_call" | custom-call | flops 600000000 | tf_op jit(solution)/shard_map/spatial_forward/pallas_call | solution.py:86
  41.4 0.9 copy-done
  42.3 0.9 copy-done.2
  43.2 0.9 copy-done.4
  44.1 2.0 %collective-permute-start = (bf16[3,128,256]{2,1,0:T(8,128)(2,1)}, bf16[3,128,256]{2,1,0:T(8,128)(2,1)}, u32[]{:S(2)}, u32[]{:S(2)}) collective-permute-start(bf16[3,128,256]{2,1,0:T(8,128)(2,1)} %get-tuple-element.45), channel_id=1, source_target_pairs={{0,2},{2,0},{4,6},{6,4},{1,3},{3,1},{5,7},{7,5},{8,10},{10,8},{12,... | collective-permute-start | bytes 589832 | tf_op jit(solution)/shard_map/ppermute | solution.py:371
  46.1 2.4 %collective-permute-start.1 = (bf16[3,128,256]{2,1,0:T(8,128)(2,1)}, bf16[3,128,256]{2,1,0:T(8,128)(2,1)}, u32[]{:S(2)}, u32[]{:S(2)}) collective-permute-start(bf16[3,128,256]{2,1,0:T(8,128)(2,1)} %get-tuple-element.46), channel_id=1, source_target_pairs={{0,4},{2,6},{4,0},{6,2},{1,5},{3,7},{5,1},{7,3},{8,12},{10,14},{12... | collective-permute-start | bytes 589832 | tf_op jit(solution)/shard_map/ppermute | solution.py:371
  48.6 14.5 %all-to-all-done.field_ref = bf16[8,128,384]{2,1,0:T(8,128)(2,1)} async-done(((bf16[8,128,384]{2,1,0:T(8,128)(2,1)}), bf16[8,128,384]{2,1,0:T(8,128)(2,1)}, u32[]{:S(2)}, u32[]{:S(2)}) %all-to-all-start) | async-done | bytes 786464 | tf_op jit(solution)/shard_map/all_to_all | solution.py:388
  63.1 2.3 %turn_cotangent.1.refs_4_ = bf16[2,4,3,128,128]{4,3,2,1,0:T(8,128)(2,1)S(1)} custom-call(bf16[8,128,384]{2,1,0:T(8,128)(2,1)} %all-to-all-done.field_ref), custom_call_target="tpu_custom_call" | custom-call | flops 200000000 | tf_op jit(solution)/shard_map/turn_cotangent/pallas_call | solution.py:184
  65.5 1.8 %collective-permute-done.1.refs_2_ = bf16[3,128,256]{2,1,0:T(8,128)(2,1)} collective-permute-done((bf16[3,128,256]{2,1,0:T(8,128)(2,1)}, bf16[3,128,256]{2,1,0:T(8,128)(2,1)}, u32[]{:S(2)}, u32[]{:S(2)}) %collective-permute-start.1) | collective-permute-done | bytes 196640 | tf_op jit(solution)/shard_map/ppermute | solution.py:371
  67.4 4.4 %temporal.1 = (bf16[3,128,256]{2,1,0:T(8,128)(2,1)S(1)}, bf16[3,128,256]{2,1,0:T(8,128)(2,1)S(1)}, bf16[3,128,256]{2,1,0:T(8,128)(2,1)S(1)}, bf16[3,128,256]{2,1,0:T(8,128)(2,1)S(1)}, f32[8,128]{1,0:T(8,128)S(1)}) custom-call(s32[3]{0:T(128)S(1)} %pad_add_fusion.scalars, bf16[3,128,256]{2,1,0:T(8,128)(2,1)S(1)} %get-tuple-element.44.refs_0_, ...), custom_call_target="tpu_custom_call" | custom-call | flops 400000000 | tf_op jit(solution)/shard_map/temporal/pallas_call | solution.py:310
  71.8 3.5 %collective-permute-start.6 = (bf16[3,128,256]{2,1,0:T(8,128)(2,1)S(1)}, bf16[3,128,256]{2,1,0:T(8,128)(2,1)S(1)}, u32[]{:S(2)}, u32[]{:S(2)}) collective-permute-start(bf16[3,128,256]{2,1,0:T(8,128)(2,1)S(1)} %get-tuple-element.54), channel_id=1, source_target_pairs={{0,2},{2,0},{4,6},{6,4},{1,3},{3,1},{5,7},{7,5},{8,10},{10,8},{12,... | collective-permute-start | bytes 589832 | tf_op jit(solution)/shard_map/ppermute | solution.py:371
  75.2 1.1 %collective-permute-start.3 = (bf16[3,128,256]{2,1,0:T(8,128)(2,1)S(1)}, bf16[3,128,256]{2,1,0:T(8,128)(2,1)S(1)}, u32[]{:S(2)}, u32[]{:S(2)}) collective-permute-start(bf16[3,128,256]{2,1,0:T(8,128)(2,1)S(1)} %get-tuple-element.49), channel_id=1, source_target_pairs={{0,6},{2,4},{4,2},{6,0},{1,7},{3,5},{5,3},{7,1},{8,14},{10,12},{12... | collective-permute-start | bytes 589832 | tf_op jit(solution)/shard_map/ppermute | solution.py:371
  76.9 1.5 %collective-permute-start.7 = (f32[16,128]{1,0:T(8,128)S(1)}, f32[16,128]{1,0:T(8,128)S(1)}, u32[]{:S(2)}, u32[]{:S(2)}) collective-permute-start(f32[16,128]{1,0:T(8,128)S(1)} %pad_maximum_fusion.2), channel_id=1, source_target_pairs={{0,16},{8,24},{16,0},{24,8},{1,17},{9,25},{17,1},{25,9},{2,18},{10... | collective-permute-start | bytes 24584 | tf_op jit(solution)/shard_map/ppermute | solution.py:371
  78.4 2.3 %spatial_backward.4 = (bf16[256,1536]{1,0:T(8,128)(2,1)}, bf16[256,1536]{1,0:T(8,128)(2,1)}) custom-call(s32[3]{0:T(128)S(1)} %pad_add_fusion.scalars, bf16[4,256,384]{2,1,0:T(8,128)(2,1)S(1)} %copy-done.1, bf16[12,128,256]{2,1,0:T(8,128)(2,1)S(1)} %copy-done.3, bf16[4,256,384]{2,1,0:T(8,128)(2,1)S(1)} %copy-done.5, ...), custom_call_target="tpu_custom_call" | custom-call | flops 200000000 | tf_op jit(solution)/shard_map/spatial_backward/pallas_call | solution.py:129
  80.7 2.3 %spatial_backward.5 = (bf16[256,1536]{1,0:T(8,128)(2,1)}, bf16[256,1536]{1,0:T(8,128)(2,1)}) custom-call(s32[3]{0:T(128)S(1)} %pad_add_fusion.scalars, bf16[4,256,384]{2,1,0:T(8,128)(2,1)S(1)} %copy-done.1, bf16[12,128,256]{2,1,0:T(8,128)(2,1)S(1)} %copy-done.3, bf16[4,256,384]{2,1,0:T(8,128)(2,1)S(1)} %copy-done.5, ...), custom_call_target="tpu_custom_call", output_to_operand_aliasing={{0}: (6, {}), {1}: (7, {})} | custom-call | flops 200000000 | tf_op jit(solution)/shard_map/spatial_backward/pallas_call | solution.py:129
  83.0 2.8 %collective-permute-start.8 = (f32[32,128]{1,0:T(8,128)S(1)}, f32[32,128]{1,0:T(8,128)S(1)}, u32[]{:S(2)}, u32[]{:S(2)}) collective-permute-start(f32[32,128]{1,0:T(8,128)S(1)} %pad_maximum_fusion.1), channel_id=1, source_target_pairs={{0,2},{2,0},{4,6},{6,4},{1,3},{3,1},{5,7},{7,5},{8,10},{10,8},{12,... | collective-permute-start | bytes 49160 | tf_op jit(solution)/shard_map/ppermute | solution.py:371
  85.8 1.7 %collective-permute-done.8 = f32[32,128]{1,0:T(8,128)S(1)} collective-permute-done((f32[32,128]{1,0:T(8,128)S(1)}, f32[32,128]{1,0:T(8,128)S(1)}, u32[]{:S(2)}, u32[]{:S(2)}) %collective-permute-start.8) | collective-permute-done | bytes 16416 | tf_op jit(solution)/shard_map/ppermute | solution.py:371
  87.6 2.6 %collective-permute-start.9 = (f32[64,128]{1,0:T(8,128)S(1)}, f32[64,128]{1,0:T(8,128)S(1)}, u32[]{:S(2)}, u32[]{:S(2)}) collective-permute-start(f32[64,128]{1,0:T(8,128)S(1)} %pad_maximum_fusion.refs_0_), channel_id=1, source_target_pairs={{0,4},{2,6},{4,0},{6,2},{1,5},{3,7},{5,1},{7,3},{8,12},{10,14},{12... | collective-permute-start | bytes 98312 | tf_op jit(solution)/shard_map/ppermute | solution.py:371
  90.2 5.9 %collective-permute-done.9.refs_1_ = f32[64,128]{1,0:T(8,128)S(1)} collective-permute-done((f32[64,128]{1,0:T(8,128)S(1)}, f32[64,128]{1,0:T(8,128)S(1)}, u32[]{:S(2)}, u32[]{:S(2)}) %collective-permute-start.9) | collective-permute-done | bytes 32800 | tf_op jit(solution)/shard_map/ppermute | solution.py:371
  96.1 1.3 %gain_gradients.1 = f32[2,16,1536]{2,1,0:T(8,128)} custom-call(s32[3]{0:T(128)S(1)} %pad_add_fusion.scalars, f32[64,128]{1,0:T(8,128)S(1)} %pad_maximum_fusion.refs_0_, f32[64,128]{1,0:T(8,128)S(1)} %collective-permute-done.9.refs_1_, f32[2,16,1536]{2,1,0:T(8,128)S(1)} %copy-done.6), custom_call_target="tpu_custom_call" | custom-call | flops 100000000 | tf_op jit(solution)/shard_map/gain_gradients/pallas_call | solution.py:358
  97.4 2.3 %spatial_backward.6 = (bf16[256,1536]{1,0:T(8,128)(2,1)}, bf16[256,1536]{1,0:T(8,128)(2,1)}) custom-call(s32[3]{0:T(128)S(1)} %pad_add_fusion.scalars, bf16[4,256,384]{2,1,0:T(8,128)(2,1)S(1)} %copy-done.1, bf16[12,128,256]{2,1,0:T(8,128)(2,1)S(1)} %copy-done.3, bf16[4,256,384]{2,1,0:T(8,128)(2,1)S(1)} %copy-done.5, ...), custom_call_target="tpu_custom_call", output_to_operand_aliasing={{0}: (6, {}), {1}: (7, {})} | custom-call | flops 200000000 | tf_op jit(solution)/shard_map/spatial_backward/pallas_call | solution.py:129
  99.7 2.3 %spatial_backward.7 = (bf16[256,1536]{1,0:T(8,128)(2,1)}, bf16[256,1536]{1,0:T(8,128)(2,1)}) custom-call(s32[3]{0:T(128)S(1)} %pad_add_fusion.scalars, bf16[4,256,384]{2,1,0:T(8,128)(2,1)S(1)} %copy-done.1, bf16[12,128,256]{2,1,0:T(8,128)(2,1)S(1)} %copy-done.3, bf16[4,256,384]{2,1,0:T(8,128)(2,1)S(1)} %copy-done.5, ...), custom_call_target="tpu_custom_call", output_to_operand_aliasing={{0}: (6, {}), {1}: (7, {})} | custom-call | flops 200000000 | tf_op jit(solution)/shard_map/spatial_backward/pallas_call | solution.py:129
  (27 shorter events, 0.9 us)
Async XLA Ops:
  0.6 47.8 %copy-start.6 = (f32[2,16,1536]{2,1,0:T(8,128)S(1)}, f32[2,16,1536]{2,1,0:T(8,128)}, u32[]{:S(2)}) copy-start(f32[2,16,1536]{2,1,0:T(8,128)} %refs_2_.1) | copy-start | bytes 589828
  25.6 37.4 %all-to-all-start = ((bf16[8,128,384]{2,1,0:T(8,128)(2,1)}), bf16[8,128,384]{2,1,0:T(8,128)(2,1)}, u32[]{:S(2)}, u32[]{:S(2)}) async-start(bf16[8,128,384]{2,1,0:T(8,128)(2,1)} %pack_cotangent.1), calls=%async_computation | async-start | bytes 1572864 | tf_op jit(solution)/shard_map/all_to_all | solution.py:388
  41.4 0.9 copy-start
  42.3 0.9 copy-start.2
  43.2 0.9 copy-start.4
  44.1 21.4 %collective-permute-start = (bf16[3,128,256]{2,1,0:T(8,128)(2,1)}, bf16[3,128,256]{2,1,0:T(8,128)(2,1)}, u32[]{:S(2)}, u32[]{:S(2)}) collective-permute-start(bf16[3,128,256]{2,1,0:T(8,128)(2,1)} %get-tuple-element.45), channel_id=1, source_target_pairs={{0,2},{2,0},{4,6},{6,4},{1,3},{3,1},{5,7},{7,5},{8,10},{10,8},{12,... | collective-permute-start | bytes 589832 | tf_op jit(solution)/shard_map/ppermute | solution.py:371
  46.1 21.2 %collective-permute-start.1 = (bf16[3,128,256]{2,1,0:T(8,128)(2,1)}, bf16[3,128,256]{2,1,0:T(8,128)(2,1)}, u32[]{:S(2)}, u32[]{:S(2)}) collective-permute-start(bf16[3,128,256]{2,1,0:T(8,128)(2,1)} %get-tuple-element.46), channel_id=1, source_target_pairs={{0,4},{2,6},{4,0},{6,2},{1,5},{3,7},{5,1},{7,3},{8,12},{10,14},{12... | collective-permute-start | bytes 589832 | tf_op jit(solution)/shard_map/ppermute | solution.py:371
  48.5 18.8 %collective-permute-start.2 = (bf16[3,128,256]{2,1,0:T(8,128)(2,1)}, bf16[3,128,256]{2,1,0:T(8,128)(2,1)}, u32[]{:S(2)}, u32[]{:S(2)}) collective-permute-start(bf16[3,128,256]{2,1,0:T(8,128)(2,1)} %get-tuple-element.47), channel_id=1, source_target_pairs={{0,6},{2,4},{4,2},{6,0},{1,7},{3,5},{5,3},{7,1},{8,14},{10,12},{12... | collective-permute-start | bytes 589832 | tf_op jit(solution)/shard_map/ppermute | solution.py:371
  63.1 15.3 %copy-start.1 = (bf16[4,256,384]{2,1,0:T(8,128)(2,1)S(1)}, bf16[4,256,384]{2,1,0:T(8,128)(2,1)}, u32[]{:S(2)}) copy-start(bf16[4,256,384]{2,1,0:T(8,128)(2,1)} %copy-done) | copy-start | bytes 2359300
  63.1 15.3 %copy-start.3 = (bf16[12,128,256]{2,1,0:T(8,128)(2,1)S(1)}, bf16[12,128,256]{2,1,0:T(8,128)(2,1)}, u32[]{:S(2)}) copy-start(bf16[12,128,256]{2,1,0:T(8,128)(2,1)} %copy-done.2) | copy-start | bytes 2359300
  63.1 15.3 %copy-start.5 = (bf16[4,256,384]{2,1,0:T(8,128)(2,1)S(1)}, bf16[4,256,384]{2,1,0:T(8,128)(2,1)}, u32[]{:S(2)}) copy-start(bf16[4,256,384]{2,1,0:T(8,128)(2,1)} %copy-done.4) | copy-start | bytes 2359300
  71.8 8.9 %collective-permute-start.6 = (bf16[3,128,256]{2,1,0:T(8,128)(2,1)S(1)}, bf16[3,128,256]{2,1,0:T(8,128)(2,1)S(1)}, u32[]{:S(2)}, u32[]{:S(2)}) collective-permute-start(bf16[3,128,256]{2,1,0:T(8,128)(2,1)S(1)} %get-tuple-element.54), channel_id=1, source_target_pairs={{0,2},{2,0},{4,6},{6,4},{1,3},{3,1},{5,7},{7,5},{8,10},{10,8},{12,... | collective-permute-start | bytes 589832 | tf_op jit(solution)/shard_map/ppermute | solution.py:371
  75.2 1.6 %collective-permute-start.5 = (f32[8,128]{1,0:T(8,128)S(1)}, f32[8,128]{1,0:T(8,128)S(1)}, u32[]{:S(2)}, u32[]{:S(2)}) collective-permute-start(f32[8,128]{1,0:T(8,128)S(1)} %get-tuple-element.51), channel_id=1, source_target_pairs={{0,8},{8,0},{16,24},{24,16},{1,9},{9,1},{17,25},{25,17},{2,10},{10... | collective-permute-start | bytes 12296 | tf_op jit(solution)/shard_map/ppermute | solution.py:371
  75.2 24.5 %collective-permute-start.3 = (bf16[3,128,256]{2,1,0:T(8,128)(2,1)S(1)}, bf16[3,128,256]{2,1,0:T(8,128)(2,1)S(1)}, u32[]{:S(2)}, u32[]{:S(2)}) collective-permute-start(bf16[3,128,256]{2,1,0:T(8,128)(2,1)S(1)} %get-tuple-element.49), channel_id=1, source_target_pairs={{0,6},{2,4},{4,2},{6,0},{1,7},{3,5},{5,3},{7,1},{8,14},{10,12},{12... | collective-permute-start | bytes 589832 | tf_op jit(solution)/shard_map/ppermute | solution.py:371
  76.3 21.0 %collective-permute-start.4 = (bf16[3,128,256]{2,1,0:T(8,128)(2,1)S(1)}, bf16[3,128,256]{2,1,0:T(8,128)(2,1)S(1)}, u32[]{:S(2)}, u32[]{:S(2)}) collective-permute-start(bf16[3,128,256]{2,1,0:T(8,128)(2,1)S(1)} %get-tuple-element.50), channel_id=1, source_target_pairs={{0,4},{2,6},{4,0},{6,2},{1,5},{3,7},{5,1},{7,3},{8,12},{10,14},{12... | collective-permute-start | bytes 589832 | tf_op jit(solution)/shard_map/ppermute | solution.py:371
  76.9 3.8 %collective-permute-start.7 = (f32[16,128]{1,0:T(8,128)S(1)}, f32[16,128]{1,0:T(8,128)S(1)}, u32[]{:S(2)}, u32[]{:S(2)}) collective-permute-start(f32[16,128]{1,0:T(8,128)S(1)} %pad_maximum_fusion.2), channel_id=1, source_target_pairs={{0,16},{8,24},{16,0},{24,8},{1,17},{9,25},{17,1},{25,9},{2,18},{10... | collective-permute-start | bytes 24584 | tf_op jit(solution)/shard_map/ppermute | solution.py:371
  83.0 4.6 %collective-permute-start.8 = (f32[32,128]{1,0:T(8,128)S(1)}, f32[32,128]{1,0:T(8,128)S(1)}, u32[]{:S(2)}, u32[]{:S(2)}) collective-permute-start(f32[32,128]{1,0:T(8,128)S(1)} %pad_maximum_fusion.1), channel_id=1, source_target_pairs={{0,2},{2,0},{4,6},{6,4},{1,3},{3,1},{5,7},{7,5},{8,10},{10,8},{12,... | collective-permute-start | bytes 49160 | tf_op jit(solution)/shard_map/ppermute | solution.py:371
  87.6 8.6 %collective-permute-start.9 = (f32[64,128]{1,0:T(8,128)S(1)}, f32[64,128]{1,0:T(8,128)S(1)}, u32[]{:S(2)}, u32[]{:S(2)}) collective-permute-start(f32[64,128]{1,0:T(8,128)S(1)} %pad_maximum_fusion.refs_0_), channel_id=1, source_target_pairs={{0,4},{2,6},{4,0},{6,2},{1,5},{3,7},{5,1},{7,3},{8,12},{10,14},{12... | collective-permute-start | bytes 98312 | tf_op jit(solution)/shard_map/ppermute | solution.py:371

commit v4 on v3

--- a/solution.py
+++ b/solution.py
@@ -34,9 +34,8 @@
     return jnp.bitwise_xor(scalars[0], distance)
 
 
-def forward_kernel(scalars, query_ref, key_ref, value_ref, *refs):
-    (queries, turned_keys, values, weights_ref), refs = refs[:4], refs[4:]
-    (key_rows, arrived), attended_refs = refs[-2:], refs[:-2]
+def forward_kernel(scalars, query_ref, key_ref, value_ref, weights_ref, *refs):
+    (queries, key_rows, values, arrived), attended_refs = refs[-4:], refs[:-4]
     score_scale = HEAD_DIM ** (-0.5)
     groups, _, width = queries.shape
     own = width // HEAD_DIM
@@ -56,75 +55,70 @@
             copy.wait()
         for head in range(own):
             cols = pl.ds(head * HEAD_DIM, HEAD_DIM)
-            keys_here = key_rows[group, :, cols]
-            scores = columns_dot(keys_here, queries[group, :, cols])
+            scores = columns_dot(key_rows[group, :, cols], queries[group, :, cols])
             largest = jnp.max(scores, axis=0, keepdims=True)
             raised = jnp.exp((scores - largest) * score_scale)
             weights = raised * (1.0 / jnp.sum(raised, axis=0, keepdims=True))
             weights_ref[group * own + head] = weights
             attended = dot(values[group, :, cols].T, weights.astype(jnp.bfloat16))
             attended_refs[group][head] = attended.astype(jnp.bfloat16)
-            turned_keys[group * own + head] = keys_here.T
 
 
 def forward(scalars, queries, key_rows, values, groups):
     patches, feat = queries.shape
     heads = feat // HEAD_DIM
     own = heads // groups
-    by_group = (groups, patches, feat // groups)
-    *kept, weights, attended = [
-        jax.ShapeDtypeStruct(by_group, jnp.bfloat16),
-        jax.ShapeDtypeStruct((heads, HEAD_DIM, patches), jnp.bfloat16),
-        jax.ShapeDtypeStruct(by_group, jnp.bfloat16),
-        jax.ShapeDtypeStruct((heads, patches, patches), jnp.float32),
-        jax.ShapeDtypeStruct((own, HEAD_DIM, patches), jnp.bfloat16),
-    ]
-    shapes = [*kept, weights] + [attended] * groups
     fields = [
         pltpu.with_memory_space_constraint(field, pltpu.HBM) for field in (queries, key_rows, values)
     ]
-    results = pl.pallas_call(
+    weights, *attended = pl.pallas_call(
         forward_kernel,
         in_specs=[pl.BlockSpec(memory_space=pltpu.SMEM)]
         + [pl.BlockSpec(memory_space=pltpu.HBM)] * 3,
-        out_specs=[pl.BlockSpec(memory_space=pltpu.VMEM)] * len(shapes),
-        scratch_shapes=[pltpu.VMEM(by_group, jnp.bfloat16), pltpu.SemaphoreType.DMA((groups, 3))],
-        out_shape=shapes,
+        out_specs=[pl.BlockSpec(memory_space=pltpu.VMEM)] * (1 + groups),
+        scratch_shapes=[pltpu.VMEM((groups, patches, feat // groups), jnp.bfloat16)] * 3
+        + [pltpu.SemaphoreType.DMA((groups, 3))],
+        out_shape=[jax.ShapeDtypeStruct((heads, patches, patches), jnp.float32)]
+        + [jax.ShapeDtypeStruct((own, HEAD_DIM, patches), jnp.bfloat16)] * groups,
         compiler_params=params(patches),
         cost_estimate=cost(6),
         name="spatial_forward",
     )(scalars, *fields)
-    return results[:4], results[4:]
-
-
-def backward_kernel(distance, scalars, *refs):
-    queries, turned_keys, values, weights_ref, grad_ref = refs[:5]
+    return weights, attended
+
+
+def backward_kernel(distance, scalars, query_ref, key_ref, value_ref, weights_ref, grad_ref, *refs):
     gq_ref, gk_ref, gq, gk, sent = refs[-5:]
     score_scale = HEAD_DIM ** (-0.5)
     own = grad_ref.shape[0]
-    copies = []
-    for head in range(own):
+    start = partner(scalars, distance) * (own * HEAD_DIM)
+    columns = [
+        pl.ds(pl.multiple_of(start + head * HEAD_DIM, HEAD_DIM), HEAD_DIM) for head in range(own)
+    ]
+    spatial_grads = [dot(value_ref[:, columns[head]], grad_ref[head]) for head in range(own)]
+    all_scores = []
+    for head, spatial_grad in enumerate(spatial_grads):
+        weights = weights_ref[distance * own + head]
+        row_sum = jnp.sum(spatial_grad * weights, axis=0, keepdims=True)
+        scores = weights * (spatial_grad - row_sum) * score_scale
+        all_scores.append(scores.astype(jnp.bfloat16))
+    for head, scores in enumerate(all_scores):
         cols = pl.ds(head * HEAD_DIM, HEAD_DIM)
-        weights = weights_ref[distance * own + head]
-        spatial_grad = dot(values[distance, :, cols], grad_ref[head])
-        row_sum = jnp.sum(spatial_grad * weights, axis=0, keepdims=True)
-        scores = (weights * (spatial_grad - row_sum) * score_scale).astype(jnp.bfloat16)
-        gk[head] = dot(scores, queries[distance, :, cols]).astype(jnp.bfloat16)
-        gq[head] = dot(turned_keys[distance * own + head], scores).astype(jnp.bfloat16).T
-        start = (partner(scalars, distance) * own + head) * HEAD_DIM
-        there = pl.ds(pl.multiple_of(start, HEAD_DIM), HEAD_DIM)
-        for side, (source, target) in enumerate(((gq, gq_ref), (gk, gk_ref))):
-            copy = pltpu.make_async_copy(
-                source.at[head], target.at[:, there], sent.at[head, side]
-            )
-            copy.start()
-            copies.append(copy)
+        gk[:, cols] = dot(scores, query_ref[:, columns[head]]).astype(jnp.bfloat16)
+        gq[:, cols] = dot(key_ref[:, columns[head]].T, scores).astype(jnp.bfloat16).T
+    there = pl.ds(pl.multiple_of(start, HEAD_DIM), own * HEAD_DIM)
+    copies = [
+        pltpu.make_async_copy(gq, gq_ref.at[:, there], sent.at[0]),
+        pltpu.make_async_copy(gk, gk_ref.at[:, there], sent.at[1]),
+    ]
+    for copy in copies:
+        copy.start()
     for copy in copies:
         copy.wait()
 
 
-def backward(scalars, kept, grads, distance, earlier):
-    groups, patches, width = kept[0].shape
+def backward(scalars, fields, weights, grads, distance, earlier):
+    patches, feat = fields[0].shape
     own = grads.shape[0]
     return pl.pallas_call(
         functools.partial(backward_kernel, distance),
@@ -132,14 +126,14 @@
         + [pl.BlockSpec(memory_space=pltpu.VMEM)] * 5
         + [pl.BlockSpec(memory_space=pl.ANY)] * len(earlier),
         out_specs=[pl.BlockSpec(memory_space=pl.ANY)] * 2,
-        scratch_shapes=[pltpu.VMEM((own, patches, HEAD_DIM), jnp.bfloat16)] * 2
-        + [pltpu.SemaphoreType.DMA((own, 2))],
-        out_shape=[jax.ShapeDtypeStruct((patches, groups * width), jnp.bfloat16)] * 2,
+        scratch_shapes=[pltpu.VMEM((patches, own * HEAD_DIM), jnp.bfloat16)] * 2
+        + [pltpu.SemaphoreType.DMA((2,))],
+        out_shape=[jax.ShapeDtypeStruct((patches, feat), jnp.bfloat16)] * 2,
         input_output_aliases={6 + index: index for index in range(len(earlier))},
         compiler_params=params(patches),
         cost_estimate=cost(2),
         name="spatial_backward",
-    )(scalars, *kept, grads, *earlier)
+    )(scalars, *fields, weights, grads, *earlier)
 
 
 def pack_kernel(frames, spaces, field_ref, packed_ref, sent):
@@ -168,7 +162,7 @@
         compiler_params=params(0),
         cost_estimate=cost(1),
         name="pack_cotangent",
-    )(pltpu.with_memory_space_constraint(field, pltpu.HBM))
+    )(field)
 
 
 def turn_kernel(field_ref, turned_ref):
@@ -387,11 +381,12 @@
     packed = pack(cotangent.reshape(cotangent.shape[2:]), frames, spaces)
     incoming = lax.all_to_all(packed, ("tm", "space"), split_axis=0, concat_axis=0, tiled=True)
     queries, _ = lax.optimization_barrier((queries, packed))
-    kept, attended = forward(scalars, queries, key_rows, values, frames)
+    fields = (queries, key_rows, values)
+    weights, attended = forward(scalars, *fields, frames)
     attended = [attended[0]] + [
         swap(attended[distance], "tm", frames, distance) for distance in range(1, frames)
     ]
-    incoming, _ = lax.optimization_barrier((incoming, kept[3]))
+    incoming, _ = lax.optimization_barrier((incoming, weights))
     upstream = turn(incoming, frames, spaces)
     rows = lax.dynamic_index_in_dim(gains, task_ids[0], 1, keepdims=False)
     product = lax.dynamic_slice_in_dim(rows[0] * rows[1], frame * width, width, 0)
@@ -410,15 +405,17 @@
         if results and number >= 2:
             joined, results = lax.optimization_barrier((joined, results))
         mixed = [joined, swap(joined, axis, size, step)]
-        if number < 2 and distance < frames:
-            here, mixed[1] = lax.optimization_barrier((grads[distance], mixed[1]))
-            results = backward(scalars, kept, here, distance, results)
+        here = grads[distance]
+        if number == 0:
+            here, mixed[1] = lax.optimization_barrier((here, mixed[1]))
+        if number in (0, 2) and distance < frames - 1:
+            results = backward(scalars, fields, weights, here, distance, results)
             distance += 1
     grad_gains = gain_gradients(scalars, mixed, gains, own, frames, clips)
     if results:
         grad_gains, results = lax.optimization_barrier((grad_gains, results))
     for distance in range(distance, frames):
-        results = backward(scalars, kept, grads[distance], distance, results)
+        results = backward(scalars, fields, weights, grads[distance], distance, results)
     grad_queries, grad_keys = results
     return (
         grad_queries.reshape(query_heads.shape),
@@ -470,7 +467,8 @@
         field.reshape(patches, feat) for field in (query_heads, key_heads, value_heads)
     )
     scalars = jnp.zeros((1,), jnp.int32)
-    kept, attended = forward(scalars, queries, key_rows, values, 1)
+    fields = (queries, key_rows, values)
+    weights, attended = forward(scalars, *fields, 1)
     attended_field = jnp.transpose(attended[0], (2, 0, 1)).reshape(1, 1, patches, feat)
     upstream = lax.all_to_all(
         lax.all_to_all(cotangent, "space", split_axis=3, concat_axis=2, tiled=True),
@@ -506,7 +504,7 @@
         tiled=True,
     )
     head_grads = jnp.transpose(returned.reshape(patches, heads, HEAD_DIM), (1, 2, 0))
-    grad_queries, grad_keys = backward(scalars, kept, head_grads, 0, ())
+    grad_queries, grad_keys = backward(scalars, fields, weights, head_grads, 0, ())
     return (
         grad_queries.reshape(query_heads.shape),
         grad_keys.reshape(query_heads.shape),

time: 102 us -> 77.1 us (0.76)
  Pallas kernels: 49.2 us -> 23.7 us
  local copies, waits for them, and re-layouts: 2.76 us -> 1.25 us
  starting transfers between devices: 23.7 us -> 24.8 us
    pallas_call x1, Pallas kernels: 25 us -> 0.93 us  [pack(): pl.pallas_call(functools.partial(pack_kernel, frames, spaces), in_specs=[...]
    all_to_all x1, waiting for transfers between devices: 14.5 us -> 17 us  [split_by_heads(): lax.all_to_all(packed, ('tm', 'space'), split_axis=0, concat_axis=0, tile...]
    ppermute x10, waiting for transfers between devices: 9.51 us -> 7.81 us  [swap(): return lax.ppermute(field, axis, [(i, i ^ distance) for i in range(size)])]
    unnamed x14 -> x10, local copies, waits for them, and re-layouts: 2.66 us -> 1.14 us
    pallas_call x4, Pallas kernels: 9.17 us -> 7.73 us  [backward(): pl.pallas_call(functools.partial(backward_kernel, distance), in_specs=[pl...]
    ppermute x10, starting transfers between devices: 16.4 us -> 17.5 us  [swap(): return lax.ppermute(field, axis, [(i, i ^ distance) for i in range(size)])]
  transfers between devices with their start and end apart: 11 -> 11, of which waited for: 4 -> 5; matrix products, arithmetic and copies ran while one was open for 0% -> 0% of each run, Pallas kernels for 17% -> 21%
where the time goes in v4:
time: 77.1 us; the launch traced here: 76.8 us
  starting transfers between devices  24.8 us (32%)
  waiting for transfers between devices  24.8 us (32%)
  Pallas kernels  23.7 us (31%)
  between operations  2.04 us (3%)
  local copies, waits for them, and re-layouts  1.25 us (2%)
    ppermute x10, starting transfers between devices, swap(): return lax.ppermute(field, axis, [(i, i ^ distance) for i in range(size)])  17.5 us
    all_to_all x1, waiting for transfers between devices, split_by_heads(): lax.all_to_all(packed, ('tm', 'space'), split_axis=0, concat_axis=0, tile...  17 us
    ppermute x10, waiting for transfers between devices, swap(): return lax.ppermute(field, axis, [(i, i ^ distance) for i in range(size)])  7.81 us
    pallas_call x4, Pallas kernels, backward(): pl.pallas_call(functools.partial(backward_kernel, distance), in_specs=[pl...  7.73 us
    all_to_all x1, starting transfers between devices, split_by_heads(): lax.all_to_all(packed, ('tm', 'space'), split_axis=0, concat_axis=0, tile...  7.29 us
    pallas_call x1, Pallas kernels, forward(): pl.pallas_call(forward_kernel, in_specs=[pl.BlockSpec(memory_space=pltpu....  7.06 us
    pallas_call x1, Pallas kernels, temporal(): pl.pallas_call(functools.partial(temporal_kernel, frames), grid_spec=pltp...  4.36 us
    pallas_call x1, Pallas kernels, turn(): pl.pallas_call(turn_kernel, grid=(heads,), in_specs=[pl.BlockSpec((device...  2.34 us
  transfers between devices with their start and end apart: 11, of which 5 were waited for; matrix products, arithmetic and copies ran while one was open for 0% of the time, Pallas kernels for 21%

profile of v4, /device:TPU:0, one launch (start us, length us, event | category | flops | bytes accessed | tf_op | source)
XLA Modules:
  0.0 76.8 jit_solution(7701338338490245141)
XLA Ops:
  0.6 1.1 %copy-done.3 = bf16[1,1,128,3072]{3,2,1,0:T(8,128)(2,1)S(1)} copy-done((bf16[1,1,128,3072]{3,2,1,0:T(8,128)(2,1)S(1)}, bf16[1,1,128,3072]{3,2,1,0:T(8,128)(2,1)}, u32[]{:S(2)}) %copy-start.3) | copy-done | bytes 786456
  1.8 0.9 %pack_cotangent.1 = bf16[8,128,384]{2,1,0:T(8,128)(2,1)} custom-call(bf16[128,3072]{1,0:T(8,128)(2,1)S(1)} %bitcast.27), custom_call_target="tpu_custom_call" | custom-call | flops 100000000 | tf_op jit(solution)/shard_map/pack_cotangent/pallas_call | solution.py:156
  2.7 7.3 %all-to-all-start = ((bf16[8,128,384]{2,1,0:T(8,128)(2,1)}), bf16[8,128,384]{2,1,0:T(8,128)(2,1)}, u32[]{:S(2)}, u32[]{:S(2)}) async-start(bf16[8,128,384]{2,1,0:T(8,128)(2,1)} %pack_cotangent.1), calls=%async_computation | async-start | bytes 1572864 | tf_op jit(solution)/shard_map/all_to_all | solution.py:382
  11.4 7.1 %spatial_forward.1 = (f32[12,256,256]{2,1,0:T(8,128)S(1)}, bf16[3,128,256]{2,1,0:T(8,128)(2,1)S(1)}, bf16[3,128,256]{2,1,0:T(8,128)(2,1)}, bf16[3,128,256]{2,1,0:T(8,128)(2,1)}, bf16[3,128,256]{2,1,0:T(8,128)(2,1)}) custom-call(s32[3]{0:T(128)S(1)} %pad_add_fusion.scalars, bf16[256,1536]{1,0:T(8,128)(2,1)} %bitcast.12, bf16[256,1536]{1,0:T(8,128)(2,1)} %bitcast.17, ...), custom_call_target="tpu_custom_call" | custom-call | flops 600000000 | tf_op jit(solution)/shard_map/spatial_forward/pallas_call | solution.py:74
  18.5 2.1 %collective-permute-start = (bf16[3,128,256]{2,1,0:T(8,128)(2,1)}, bf16[3,128,256]{2,1,0:T(8,128)(2,1)}, u32[]{:S(2)}, u32[]{:S(2)}) collective-permute-start(bf16[3,128,256]{2,1,0:T(8,128)(2,1)} %get-tuple-element.37), channel_id=1, source_target_pairs={{0,2},{2,0},{4,6},{6,4},{1,3},{3,1},{5,7},{7,5},{8,10},{10,8},{12,... | collective-permute-start | bytes 589832 | tf_op jit(solution)/shard_map/ppermute | solution.py:365
  20.5 2.4 %collective-permute-start.1 = (bf16[3,128,256]{2,1,0:T(8,128)(2,1)}, bf16[3,128,256]{2,1,0:T(8,128)(2,1)}, u32[]{:S(2)}, u32[]{:S(2)}) collective-permute-start(bf16[3,128,256]{2,1,0:T(8,128)(2,1)} %get-tuple-element.38), channel_id=1, source_target_pairs={{0,4},{2,6},{4,0},{6,2},{1,5},{3,7},{5,1},{7,3},{8,12},{10,14},{12... | collective-permute-start | bytes 589832 | tf_op jit(solution)/shard_map/ppermute | solution.py:365
  23.1 17.0 %all-to-all-done.field_ref = bf16[8,128,384]{2,1,0:T(8,128)(2,1)} async-done(((bf16[8,128,384]{2,1,0:T(8,128)(2,1)}), bf16[8,128,384]{2,1,0:T(8,128)(2,1)}, u32[]{:S(2)}, u32[]{:S(2)}) %all-to-all-start) | async-done | bytes 786464 | tf_op jit(solution)/shard_map/all_to_all | solution.py:382
  40.1 2.3 %turn_cotangent.1.refs_4_ = bf16[2,4,3,128,128]{4,3,2,1,0:T(8,128)(2,1)S(1)} custom-call(bf16[8,128,384]{2,1,0:T(8,128)(2,1)} %all-to-all-done.field_ref), custom_call_target="tpu_custom_call" | custom-call | flops 200000000 | tf_op jit(solution)/shard_map/turn_cotangent/pallas_call | solution.py:178
  42.5 1.8 %collective-permute-done.1.refs_2_ = bf16[3,128,256]{2,1,0:T(8,128)(2,1)} collective-permute-done((bf16[3,128,256]{2,1,0:T(8,128)(2,1)}, bf16[3,128,256]{2,1,0:T(8,128)(2,1)}, u32[]{:S(2)}, u32[]{:S(2)}) %collective-permute-start.1) | collective-permute-done | bytes 196640 | tf_op jit(solution)/shard_map/ppermute | solution.py:365
  44.4 4.4 %temporal.1 = (bf16[3,128,256]{2,1,0:T(8,128)(2,1)S(1)}, bf16[3,128,256]{2,1,0:T(8,128)(2,1)S(1)}, bf16[3,128,256]{2,1,0:T(8,128)(2,1)S(1)}, bf16[3,128,256]{2,1,0:T(8,128)(2,1)S(1)}, f32[8,128]{1,0:T(8,128)S(1)}) custom-call(s32[3]{0:T(128)S(1)} %pad_add_fusion.scalars, bf16[3,128,256]{2,1,0:T(8,128)(2,1)S(1)} %get-tuple-element.36.refs_0_, ...), custom_call_target="tpu_custom_call" | custom-call | flops 400000000 | tf_op jit(solution)/shard_map/temporal/pallas_call | solution.py:304
  48.9 3.1 %collective-permute-start.4 = (bf16[3,128,256]{2,1,0:T(8,128)(2,1)S(1)}, bf16[3,128,256]{2,1,0:T(8,128)(2,1)S(1)}, u32[]{:S(2)}, u32[]{:S(2)}) collective-permute-start(bf16[3,128,256]{2,1,0:T(8,128)(2,1)S(1)} %get-tuple-element.42), channel_id=1, source_target_pairs={{0,4},{2,6},{4,0},{6,2},{1,5},{3,7},{5,1},{7,3},{8,12},{10,14},{12... | collective-permute-start | bytes 589832 | tf_op jit(solution)/shard_map/ppermute | solution.py:365
  52.0 0.4 collective-permute-start.8
  52.4 1.5 %collective-permute-start.6 = (f32[16,128]{1,0:T(8,128)S(1)}, f32[16,128]{1,0:T(8,128)S(1)}, u32[]{:S(2)}, u32[]{:S(2)}) collective-permute-start(f32[16,128]{1,0:T(8,128)S(1)} %pad_maximum_fusion.2), channel_id=1, source_target_pairs={{0,16},{8,24},{16,0},{24,8},{1,17},{9,25},{17,1},{25,9},{2,18},{10... | collective-permute-start | bytes 24584 | tf_op jit(solution)/shard_map/ppermute | solution.py:365
  53.9 1.9 %spatial_backward.4 = (bf16[256,1536]{1,0:T(8,128)(2,1)}, bf16[256,1536]{1,0:T(8,128)(2,1)}) custom-call(s32[3]{0:T(128)S(1)} %pad_add_fusion.scalars, bf16[256,1536]{1,0:T(8,128)(2,1)S(1)} %bitcast.13, bf16[256,1536]{1,0:T(8,128)(2,1)S(1)} %bitcast.18, bf16[256,1536]{1,0:T(8,128)(2,1)S(1)} %bitcast.23, f32[12,256,256]{2,1,0:T(8,128)S(1)} %get-tuple-element.35.weights_ref, ...), custom_call_target="tpu_custom_call" | custom-call | flops 200000000 | tf_op jit(solution)/shard_map/spatial_backward/pallas_call | solution.py:123
  55.9 0.2 collective-permute-done.6
  56.1 1.6 %collective-permute-start.7 = (f32[32,128]{1,0:T(8,128)S(1)}, f32[32,128]{1,0:T(8,128)S(1)}, u32[]{:S(2)}, u32[]{:S(2)}) collective-permute-start(f32[32,128]{1,0:T(8,128)S(1)} %pad_maximum_fusion.1), channel_id=1, source_target_pairs={{0,2},{2,0},{4,6},{6,4},{1,3},{3,1},{5,7},{7,5},{8,10},{10,8},{12,... | collective-permute-start | bytes 49160 | tf_op jit(solution)/shard_map/ppermute | solution.py:365
  57.7 2.7 %collective-permute-start.3 = (bf16[3,128,256]{2,1,0:T(8,128)(2,1)S(1)}, bf16[3,128,256]{2,1,0:T(8,128)(2,1)S(1)}, u32[]{:S(2)}, u32[]{:S(2)}) collective-permute-start(bf16[3,128,256]{2,1,0:T(8,128)(2,1)S(1)} %get-tuple-element.41), channel_id=1, source_target_pairs={{0,6},{2,4},{4,2},{6,0},{1,7},{3,5},{5,3},{7,1},{8,14},{10,12},{12... | collective-permute-start | bytes 589832 | tf_op jit(solution)/shard_map/ppermute | solution.py:365
  60.4 1.7 %collective-permute-done.7 = f32[32,128]{1,0:T(8,128)S(1)} collective-permute-done((f32[32,128]{1,0:T(8,128)S(1)}, f32[32,128]{1,0:T(8,128)S(1)}, u32[]{:S(2)}, u32[]{:S(2)}) %collective-permute-start.7) | collective-permute-done | bytes 16416 | tf_op jit(solution)/shard_map/ppermute | solution.py:365
  62.1 1.9 %spatial_backward.5 = (bf16[256,1536]{1,0:T(8,128)(2,1)}, bf16[256,1536]{1,0:T(8,128)(2,1)}) custom-call(s32[3]{0:T(128)S(1)} %pad_add_fusion.scalars, bf16[256,1536]{1,0:T(8,128)(2,1)S(1)} %bitcast.14, bf16[256,1536]{1,0:T(8,128)(2,1)S(1)} %bitcast.19, bf16[256,1536]{1,0:T(8,128)(2,1)S(1)} %bitcast.24, ...), custom_call_target="tpu_custom_call", output_to_operand_aliasing={{0}: (6, {}), {1}: (7, {})} | custom-call | flops 200000000 | tf_op jit(solution)/shard_map/spatial_backward/pallas_call | solution.py:123
  64.0 3.5 %collective-permute-start.9 = (f32[64,128]{1,0:T(8,128)S(1)}, f32[64,128]{1,0:T(8,128)S(1)}, u32[]{:S(2)}, u32[]{:S(2)}) collective-permute-start(f32[64,128]{1,0:T(8,128)S(1)} %pad_maximum_fusion.refs_0_), channel_id=1, source_target_pairs={{0,4},{2,6},{4,0},{6,2},{1,5},{3,7},{5,1},{7,3},{8,12},{10,14},{12... | collective-permute-start | bytes 98312 | tf_op jit(solution)/shard_map/ppermute | solution.py:365
  67.6 4.0 %collective-permute-done.9.refs_1_ = f32[64,128]{1,0:T(8,128)S(1)} collective-permute-done((f32[64,128]{1,0:T(8,128)S(1)}, f32[64,128]{1,0:T(8,128)S(1)}, u32[]{:S(2)}, u32[]{:S(2)}) %collective-permute-start.9) | collective-permute-done | bytes 32800 | tf_op jit(solution)/shard_map/ppermute | solution.py:365
  71.6 1.3 %gain_gradients.1 = f32[2,16,1536]{2,1,0:T(8,128)} custom-call(s32[3]{0:T(128)S(1)} %pad_add_fusion.scalars, f32[64,128]{1,0:T(8,128)S(1)} %pad_maximum_fusion.refs_0_, f32[64,128]{1,0:T(8,128)S(1)} %collective-permute-done.9.refs_1_, f32[2,16,1536]{2,1,0:T(8,128)S(1)} %copy-done.4), custom_call_target="tpu_custom_call" | custom-call | flops 100000000 | tf_op jit(solution)/shard_map/gain_gradients/pallas_call | solution.py:352
  72.9 1.9 %spatial_backward.6 = (bf16[256,1536]{1,0:T(8,128)(2,1)}, bf16[256,1536]{1,0:T(8,128)(2,1)}) custom-call(s32[3]{0:T(128)S(1)} %pad_add_fusion.scalars, bf16[256,1536]{1,0:T(8,128)(2,1)S(1)} %bitcast.15, bf16[256,1536]{1,0:T(8,128)(2,1)S(1)} %bitcast.20, bf16[256,1536]{1,0:T(8,128)(2,1)S(1)} %bitcast.25, ...), custom_call_target="tpu_custom_call", output_to_operand_aliasing={{0}: (6, {}), {1}: (7, {})} | custom-call | flops 200000000 | tf_op jit(solution)/shard_map/spatial_backward/pallas_call | solution.py:123
  74.8 1.9 %spatial_backward.7 = (bf16[256,1536]{1,0:T(8,128)(2,1)}, bf16[256,1536]{1,0:T(8,128)(2,1)}) custom-call(s32[3]{0:T(128)S(1)} %pad_add_fusion.scalars, bf16[256,1536]{1,0:T(8,128)(2,1)S(1)} %bitcast.16, bf16[256,1536]{1,0:T(8,128)(2,1)S(1)} %bitcast.21, bf16[256,1536]{1,0:T(8,128)(2,1)S(1)} %bitcast.26, ...), custom_call_target="tpu_custom_call", output_to_operand_aliasing={{0}: (6, {}), {1}: (7, {})} | custom-call | flops 200000000 | tf_op jit(solution)/shard_map/spatial_backward/pallas_call | solution.py:123
  (23 shorter events, 0.5 us)
Async XLA Ops:
  0.6 1.1 %copy-start.3 = (bf16[1,1,128,3072]{3,2,1,0:T(8,128)(2,1)S(1)}, bf16[1,1,128,3072]{3,2,1,0:T(8,128)(2,1)}, u32[]{:S(2)}) copy-start(bf16[1,1,128,3072]{3,2,1,0:T(8,128)(2,1)} %param.10) | copy-start | bytes 2359300
  1.8 21.2 %copy-start.4 = (f32[2,16,1536]{2,1,0:T(8,128)S(1)}, f32[2,16,1536]{2,1,0:T(8,128)}, u32[]{:S(2)}) copy-start(f32[2,16,1536]{2,1,0:T(8,128)} %refs_2_.1) | copy-start | bytes 589828
  2.7 37.4 %all-to-all-start = ((bf16[8,128,384]{2,1,0:T(8,128)(2,1)}), bf16[8,128,384]{2,1,0:T(8,128)(2,1)}, u32[]{:S(2)}, u32[]{:S(2)}) async-start(bf16[8,128,384]{2,1,0:T(8,128)(2,1)} %pack_cotangent.1), calls=%async_computation | async-start | bytes 1572864 | tf_op jit(solution)/shard_map/all_to_all | solution.py:382
  18.5 24.0 %collective-permute-start = (bf16[3,128,256]{2,1,0:T(8,128)(2,1)}, bf16[3,128,256]{2,1,0:T(8,128)(2,1)}, u32[]{:S(2)}, u32[]{:S(2)}) collective-permute-start(bf16[3,128,256]{2,1,0:T(8,128)(2,1)} %get-tuple-element.37), channel_id=1, source_target_pairs={{0,2},{2,0},{4,6},{6,4},{1,3},{3,1},{5,7},{7,5},{8,10},{10,8},{12,... | collective-permute-start | bytes 589832 | tf_op jit(solution)/shard_map/ppermute | solution.py:365
  20.5 23.8 %collective-permute-start.1 = (bf16[3,128,256]{2,1,0:T(8,128)(2,1)}, bf16[3,128,256]{2,1,0:T(8,128)(2,1)}, u32[]{:S(2)}, u32[]{:S(2)}) collective-permute-start(bf16[3,128,256]{2,1,0:T(8,128)(2,1)} %get-tuple-element.38), channel_id=1, source_target_pairs={{0,4},{2,6},{4,0},{6,2},{1,5},{3,7},{5,1},{7,3},{8,12},{10,14},{12... | collective-permute-start | bytes 589832 | tf_op jit(solution)/shard_map/ppermute | solution.py:365
  22.9 21.4 %collective-permute-start.2 = (bf16[3,128,256]{2,1,0:T(8,128)(2,1)}, bf16[3,128,256]{2,1,0:T(8,128)(2,1)}, u32[]{:S(2)}, u32[]{:S(2)}) collective-permute-start(bf16[3,128,256]{2,1,0:T(8,128)(2,1)} %get-tuple-element.39), channel_id=1, source_target_pairs={{0,6},{2,4},{4,2},{6,0},{1,7},{3,5},{5,3},{7,1},{8,14},{10,12},{12... | collective-permute-start | bytes 589832 | tf_op jit(solution)/shard_map/ppermute | solution.py:365
  40.1 13.8 %copy-start = (bf16[1,1,256,1536]{3,2,1,0:T(8,128)(2,1)S(1)}, bf16[1,1,256,1536]{3,2,1,0:T(8,128)(2,1)}, u32[]{:S(2)}) copy-start(bf16[1,1,256,1536]{3,2,1,0:T(8,128)(2,1)} %param.7) | copy-start | bytes 2359300
  40.1 13.8 %copy-start.1 = (bf16[1,1,256,1536]{3,2,1,0:T(8,128)(2,1)S(1)}, bf16[1,1,256,1536]{3,2,1,0:T(8,128)(2,1)}, u32[]{:S(2)}) copy-start(bf16[1,1,256,1536]{3,2,1,0:T(8,128)(2,1)} %param.8) | copy-start | bytes 2359300
  40.1 13.8 %copy-start.2 = (bf16[1,1,256,1536]{3,2,1,0:T(8,128)(2,1)S(1)}, bf16[1,1,256,1536]{3,2,1,0:T(8,128)(2,1)}, u32[]{:S(2)}) copy-start(bf16[1,1,256,1536]{3,2,1,0:T(8,128)(2,1)} %param.9) | copy-start | bytes 2359300
  48.8 3.6 %collective-permute-start.5 = (f32[8,128]{1,0:T(8,128)S(1)}, f32[8,128]{1,0:T(8,128)S(1)}, u32[]{:S(2)}, u32[]{:S(2)}) collective-permute-start(f32[8,128]{1,0:T(8,128)S(1)} %get-tuple-element.43), channel_id=1, source_target_pairs={{0,8},{8,0},{16,24},{24,16},{1,9},{9,1},{17,25},{25,17},{2,10},{10... | collective-permute-start | bytes 12296 | tf_op jit(solution)/shard_map/ppermute | solution.py:365
  48.9 24.0 %collective-permute-start.4 = (bf16[3,128,256]{2,1,0:T(8,128)(2,1)S(1)}, bf16[3,128,256]{2,1,0:T(8,128)(2,1)S(1)}, u32[]{:S(2)}, u32[]{:S(2)}) collective-permute-start(bf16[3,128,256]{2,1,0:T(8,128)(2,1)S(1)} %get-tuple-element.42), channel_id=1, source_target_pairs={{0,4},{2,6},{4,0},{6,2},{1,5},{3,7},{5,1},{7,3},{8,12},{10,14},{12... | collective-permute-start | bytes 589832 | tf_op jit(solution)/shard_map/ppermute | solution.py:365
  52.0 10.1 %collective-permute-start.8 = (bf16[3,128,256]{2,1,0:T(8,128)(2,1)S(1)}, bf16[3,128,256]{2,1,0:T(8,128)(2,1)S(1)}, u32[]{:S(2)}, u32[]{:S(2)}) collective-permute-start(bf16[3,128,256]{2,1,0:T(8,128)(2,1)S(1)} %get-tuple-element.50), channel_id=1, source_target_pairs={{0,2},{2,0},{4,6},{6,4},{1,3},{3,1},{5,7},{7,5},{8,10},{10,8},{12,... | collective-permute-start | bytes 589832 | tf_op jit(solution)/shard_map/ppermute | solution.py:365
  52.4 3.7 %collective-permute-start.6 = (f32[16,128]{1,0:T(8,128)S(1)}, f32[16,128]{1,0:T(8,128)S(1)}, u32[]{:S(2)}, u32[]{:S(2)}) collective-permute-start(f32[16,128]{1,0:T(8,128)S(1)} %pad_maximum_fusion.2), channel_id=1, source_target_pairs={{0,16},{8,24},{16,0},{24,8},{1,17},{9,25},{17,1},{25,9},{2,18},{10... | collective-permute-start | bytes 24584 | tf_op jit(solution)/shard_map/ppermute | solution.py:365
  56.1 6.0 %collective-permute-start.7 = (f32[32,128]{1,0:T(8,128)S(1)}, f32[32,128]{1,0:T(8,128)S(1)}, u32[]{:S(2)}, u32[]{:S(2)}) collective-permute-start(f32[32,128]{1,0:T(8,128)S(1)} %pad_maximum_fusion.1), channel_id=1, source_target_pairs={{0,2},{2,0},{4,6},{6,4},{1,3},{3,1},{5,7},{7,5},{8,10},{10,8},{12,... | collective-permute-start | bytes 49160 | tf_op jit(solution)/shard_map/ppermute | solution.py:365
  57.7 17.1 %collective-permute-start.3 = (bf16[3,128,256]{2,1,0:T(8,128)(2,1)S(1)}, bf16[3,128,256]{2,1,0:T(8,128)(2,1)S(1)}, u32[]{:S(2)}, u32[]{:S(2)}) collective-permute-start(bf16[3,128,256]{2,1,0:T(8,128)(2,1)S(1)} %get-tuple-element.41), channel_id=1, source_target_pairs={{0,6},{2,4},{4,2},{6,0},{1,7},{3,5},{5,3},{7,1},{8,14},{10,12},{12... | collective-permute-start | bytes 589832 | tf_op jit(solution)/shard_map/ppermute | solution.py:365
  64.0 7.6 %collective-permute-start.9 = (f32[64,128]{1,0:T(8,128)S(1)}, f32[64,128]{1,0:T(8,128)S(1)}, u32[]{:S(2)}, u32[]{:S(2)}) collective-permute-start(f32[64,128]{1,0:T(8,128)S(1)} %pad_maximum_fusion.refs_0_), channel_id=1, source_target_pairs={{0,4},{2,6},{4,0},{6,2},{1,5},{3,7},{5,1},{7,3},{8,12},{10,14},{12... | collective-permute-start | bytes 98312 | tf_op jit(solution)/shard_map/ppermute | solution.py:365

commit v5 on v4

--- a/solution.py
+++ b/solution.py
@@ -102,17 +102,19 @@
         row_sum = jnp.sum(spatial_grad * weights, axis=0, keepdims=True)
         scores = weights * (spatial_grad - row_sum) * score_scale
         all_scores.append(scores.astype(jnp.bfloat16))
+    there = pl.ds(pl.multiple_of(start, HEAD_DIM), own * HEAD_DIM)
+    copies = [
+        pltpu.make_async_copy(gk, gk_ref.at[:, there], sent.at[0]),
+        pltpu.make_async_copy(gq, gq_ref.at[:, there], sent.at[1]),
+    ]
     for head, scores in enumerate(all_scores):
         cols = pl.ds(head * HEAD_DIM, HEAD_DIM)
         gk[:, cols] = dot(scores, query_ref[:, columns[head]]).astype(jnp.bfloat16)
+    copies[0].start()
+    for head, scores in enumerate(all_scores):
+        cols = pl.ds(head * HEAD_DIM, HEAD_DIM)
         gq[:, cols] = dot(key_ref[:, columns[head]].T, scores).astype(jnp.bfloat16).T
-    there = pl.ds(pl.multiple_of(start, HEAD_DIM), own * HEAD_DIM)
-    copies = [
-        pltpu.make_async_copy(gq, gq_ref.at[:, there], sent.at[0]),
-        pltpu.make_async_copy(gk, gk_ref.at[:, there], sent.at[1]),
-    ]
-    for copy in copies:
-        copy.start()
+    copies[1].start()
     for copy in copies:
         copy.wait()
 
@@ -397,23 +399,22 @@
     grads = [grads[0]] + [
         swap(grads[distance], "tm", frames, distance) for distance in range(1, frames)
     ]
-    rounds = [("dp", clips, 1 << bit) for bit in range(clips.bit_length() - 1)]
-    rounds += [("tm", frames, 1 << bit) for bit in range(frames.bit_length() - 1)]
-    mixed, results, distance = [mixed], (), 0
-    for number, (axis, size, step) in enumerate(rounds):
-        joined = jnp.concatenate(mixed, axis=0)
-        if results and number >= 2:
-            joined, results = lax.optimization_barrier((joined, results))
-        mixed = [joined, swap(joined, axis, size, step)]
-        here = grads[distance]
-        if number == 0:
-            here, mixed[1] = lax.optimization_barrier((here, mixed[1]))
-        if number in (0, 2) and distance < frames - 1:
-            results = backward(scalars, fields, weights, here, distance, results)
-            distance += 1
+    here = grads[0]
+    for bit in range(clips.bit_length() - 1):
+        other = swap(mixed, "dp", clips, 1 << bit)
+        if bit == 0:
+            here, other = lax.optimization_barrier((here, other))
+        mixed = jnp.concatenate([mixed, other], axis=0)
+    results = backward(scalars, fields, weights, here, 0, ())
+    mixed, results = lax.optimization_barrier((mixed, results))
+    mixed = [mixed] + [swap(mixed, "tm", frames, distance) for distance in range(1, frames)]
+    distance = 1
+    if frames > 2:
+        results = backward(scalars, fields, weights, grads[1], 1, results)
+        mixed, results = lax.optimization_barrier((mixed, results))
+        distance = 2
     grad_gains = gain_gradients(scalars, mixed, gains, own, frames, clips)
-    if results:
-        grad_gains, results = lax.optimization_barrier((grad_gains, results))
+    grad_gains, results = lax.optimization_barrier((grad_gains, results))
     for distance in range(distance, frames):
         results = backward(scalars, fields, weights, grads[distance], distance, results)
     grad_queries, grad_keys = results

time: 77.1 us -> 77.5 us (level)
  waiting for transfers between devices: 24.8 us -> 25.8 us
    ppermute x10 -> x11, waiting for transfers between devices: 7.81 us -> 8.77 us  [swap(): return lax.ppermute(field, axis, [(i, i ^ distance) for i in range(size)])]
    ppermute x10 -> x11, starting transfers between devices: 17.5 us -> 17 us  [swap(): return lax.ppermute(field, axis, [(i, i ^ distance) for i in range(size)])]
  transfers between devices with their start and end apart: 11 -> 12, of which waited for: 5 -> 5; matrix products, arithmetic and copies ran while one was open for 0% -> 0% of each run, Pallas kernels for 21% -> 21%
where the time goes in v5:
time: 77.5 us; the launch traced here: 77.2 us
  waiting for transfers between devices  25.8 us (33%)
  starting transfers between devices  24.3 us (31%)
  Pallas kernels  23.6 us (30%)
  between operations  2.05 us (3%)
  local copies, waits for them, and re-layouts  1.25 us (2%)
    all_to_all x1, waiting for transfers between devices, split_by_heads(): lax.all_to_all(packed, ('tm', 'space'), split_axis=0, concat_axis=0, tile...  17 us
    ppermute x11, starting transfers between devices, swap(): return lax.ppermute(field, axis, [(i, i ^ distance) for i in range(size)])  17 us
    ppermute x11, waiting for transfers between devices, swap(): return lax.ppermute(field, axis, [(i, i ^ distance) for i in range(size)])  8.77 us
    pallas_call x4, Pallas kernels, backward(): pl.pallas_call(functools.partial(backward_kernel, distance), in_specs=[pl...  7.69 us
    all_to_all x1, starting transfers between devices, split_by_heads(): lax.all_to_all(packed, ('tm', 'space'), split_axis=0, concat_axis=0, tile...  7.29 us
    pallas_call x1, Pallas kernels, forward(): pl.pallas_call(forward_kernel, in_specs=[pl.BlockSpec(memory_space=pltpu....  7.06 us
    pallas_call x1, Pallas kernels, temporal(): pl.pallas_call(functools.partial(temporal_kernel, frames), grid_spec=pltp...  4.36 us
    pallas_call x1, Pallas kernels, turn(): pl.pallas_call(turn_kernel, grid=(heads,), in_specs=[pl.BlockSpec((device...  2.34 us
  transfers between devices with their start and end apart: 12, of which 5 were waited for; matrix products, arithmetic and copies ran while one was open for 0% of the time, Pallas kernels for 21%

profile of v5, /device:TPU:0, one launch (start us, length us, event | category | flops | bytes accessed | tf_op | source)
XLA Modules:
  0.0 77.2 jit_solution(2083537674116290934)
XLA Ops:
  0.6 1.1 %copy-done.3 = bf16[1,1,128,3072]{3,2,1,0:T(8,128)(2,1)S(1)} copy-done((bf16[1,1,128,3072]{3,2,1,0:T(8,128)(2,1)S(1)}, bf16[1,1,128,3072]{3,2,1,0:T(8,128)(2,1)}, u32[]{:S(2)}) %copy-start.3) | copy-done | bytes 786456
  1.8 0.9 %pack_cotangent.1 = bf16[8,128,384]{2,1,0:T(8,128)(2,1)} custom-call(bf16[128,3072]{1,0:T(8,128)(2,1)S(1)} %bitcast.27), custom_call_target="tpu_custom_call" | custom-call | flops 100000000 | tf_op jit(solution)/shard_map/pack_cotangent/pallas_call | solution.py:158
  2.7 7.3 %all-to-all-start = ((bf16[8,128,384]{2,1,0:T(8,128)(2,1)}), bf16[8,128,384]{2,1,0:T(8,128)(2,1)}, u32[]{:S(2)}, u32[]{:S(2)}) async-start(bf16[8,128,384]{2,1,0:T(8,128)(2,1)} %pack_cotangent.1), calls=%async_computation | async-start | bytes 1572864 | tf_op jit(solution)/shard_map/all_to_all | solution.py:384
  11.4 7.1 %spatial_forward.1 = (f32[12,256,256]{2,1,0:T(8,128)S(1)}, bf16[3,128,256]{2,1,0:T(8,128)(2,1)S(1)}, bf16[3,128,256]{2,1,0:T(8,128)(2,1)}, bf16[3,128,256]{2,1,0:T(8,128)(2,1)}, bf16[3,128,256]{2,1,0:T(8,128)(2,1)}) custom-call(s32[3]{0:T(128)S(1)} %pad_add_fusion.scalars, bf16[256,1536]{1,0:T(8,128)(2,1)} %bitcast.12, bf16[256,1536]{1,0:T(8,128)(2,1)} %bitcast.17, ...), custom_call_target="tpu_custom_call" | custom-call | flops 600000000 | tf_op jit(solution)/shard_map/spatial_forward/pallas_call | solution.py:74
  18.5 2.1 %collective-permute-start = (bf16[3,128,256]{2,1,0:T(8,128)(2,1)}, bf16[3,128,256]{2,1,0:T(8,128)(2,1)}, u32[]{:S(2)}, u32[]{:S(2)}) collective-permute-start(bf16[3,128,256]{2,1,0:T(8,128)(2,1)} %get-tuple-element.40), channel_id=1, source_target_pairs={{0,2},{2,0},{4,6},{6,4},{1,3},{3,1},{5,7},{7,5},{8,10},{10,8},{12,... | collective-permute-start | bytes 589832 | tf_op jit(solution)/shard_map/ppermute | solution.py:367
  20.5 2.4 %collective-permute-start.1 = (bf16[3,128,256]{2,1,0:T(8,128)(2,1)}, bf16[3,128,256]{2,1,0:T(8,128)(2,1)}, u32[]{:S(2)}, u32[]{:S(2)}) collective-permute-start(bf16[3,128,256]{2,1,0:T(8,128)(2,1)} %get-tuple-element.41), channel_id=1, source_target_pairs={{0,4},{2,6},{4,0},{6,2},{1,5},{3,7},{5,1},{7,3},{8,12},{10,14},{12... | collective-permute-start | bytes 589832 | tf_op jit(solution)/shard_map/ppermute | solution.py:367
  23.1 17.0 %all-to-all-done.field_ref = bf16[8,128,384]{2,1,0:T(8,128)(2,1)} async-done(((bf16[8,128,384]{2,1,0:T(8,128)(2,1)}), bf16[8,128,384]{2,1,0:T(8,128)(2,1)}, u32[]{:S(2)}, u32[]{:S(2)}) %all-to-all-start) | async-done | bytes 786464 | tf_op jit(solution)/shard_map/all_to_all | solution.py:384
  40.1 2.3 %turn_cotangent.1.refs_4_ = bf16[2,4,3,128,128]{4,3,2,1,0:T(8,128)(2,1)S(1)} custom-call(bf16[8,128,384]{2,1,0:T(8,128)(2,1)} %all-to-all-done.field_ref), custom_call_target="tpu_custom_call" | custom-call | flops 200000000 | tf_op jit(solution)/shard_map/turn_cotangent/pallas_call | solution.py:180
  42.5 1.8 %collective-permute-done.1.refs_2_ = bf16[3,128,256]{2,1,0:T(8,128)(2,1)} collective-permute-done((bf16[3,128,256]{2,1,0:T(8,128)(2,1)}, bf16[3,128,256]{2,1,0:T(8,128)(2,1)}, u32[]{:S(2)}, u32[]{:S(2)}) %collective-permute-start.1) | collective-permute-done | bytes 196640 | tf_op jit(solution)/shard_map/ppermute | solution.py:367
  44.4 4.4 %temporal.1 = (bf16[3,128,256]{2,1,0:T(8,128)(2,1)S(1)}, bf16[3,128,256]{2,1,0:T(8,128)(2,1)S(1)}, bf16[3,128,256]{2,1,0:T(8,128)(2,1)S(1)}, bf16[3,128,256]{2,1,0:T(8,128)(2,1)S(1)}, f32[8,128]{1,0:T(8,128)S(1)}) custom-call(s32[3]{0:T(128)S(1)} %pad_add_fusion.scalars, bf16[3,128,256]{2,1,0:T(8,128)(2,1)S(1)} %get-tuple-element.39.refs_0_, ...), custom_call_target="tpu_custom_call" | custom-call | flops 400000000 | tf_op jit(solution)/shard_map/temporal/pallas_call | solution.py:306
  48.9 0.2 collective-permute-start.3
  49.1 4.7 %collective-permute-start.4 = (bf16[3,128,256]{2,1,0:T(8,128)(2,1)S(1)}, bf16[3,128,256]{2,1,0:T(8,128)(2,1)S(1)}, u32[]{:S(2)}, u32[]{:S(2)}) collective-permute-start(bf16[3,128,256]{2,1,0:T(8,128)(2,1)S(1)} %get-tuple-element.45), channel_id=1, source_target_pairs={{0,4},{2,6},{4,0},{6,2},{1,5},{3,7},{5,1},{7,3},{8,12},{10,14},{12... | collective-permute-start | bytes 589832 | tf_op jit(solution)/shard_map/ppermute | solution.py:367
  53.8 1.6 %collective-permute-start.6 = (f32[16,128]{1,0:T(8,128)S(1)}, f32[16,128]{1,0:T(8,128)S(1)}, u32[]{:S(2)}, u32[]{:S(2)}) collective-permute-start(f32[16,128]{1,0:T(8,128)S(1)} %pad_maximum_fusion.1), channel_id=1, source_target_pairs={{0,16},{8,24},{16,0},{24,8},{1,17},{9,25},{17,1},{25,9},{2,18},{10... | collective-permute-start | bytes 24584 | tf_op jit(solution)/shard_map/ppermute | solution.py:367
  55.4 1.9 %spatial_backward.4 = (bf16[256,1536]{1,0:T(8,128)(2,1)}, bf16[256,1536]{1,0:T(8,128)(2,1)}) custom-call(s32[3]{0:T(128)S(1)} %pad_add_fusion.scalars, bf16[256,1536]{1,0:T(8,128)(2,1)S(1)} %bitcast.13, bf16[256,1536]{1,0:T(8,128)(2,1)S(1)} %bitcast.18, bf16[256,1536]{1,0:T(8,128)(2,1)S(1)} %bitcast.23, f32[12,256,256]{2,1,0:T(8,128)S(1)} %get-tuple-element.38.weights_ref, ...), custom_call_target="tpu_custom_call" | custom-call | flops 200000000 | tf_op jit(solution)/shard_map/spatial_backward/pallas_call | solution.py:125
  57.3 0.2 collective-permute-done.6
  57.5 1.4 %collective-permute-start.9 = (f32[32,128]{1,0:T(8,128)S(1)}, f32[32,128]{1,0:T(8,128)S(1)}, u32[]{:S(2)}, u32[]{:S(2)}) collective-permute-start(f32[32,128]{1,0:T(8,128)S(1)} %pad_maximum_fusion.refs_0_), channel_id=1, source_target_pairs={{0,6},{2,4},{4,2},{6,0},{1,7},{3,5},{5,3},{7,1},{8,14},{10,12},{12... | collective-permute-start | bytes 49160 | tf_op jit(solution)/shard_map/ppermute | solution.py:367
  58.9 2.0 %collective-permute-start.8 = (f32[32,128]{1,0:T(8,128)S(1)}, f32[32,128]{1,0:T(8,128)S(1)}, u32[]{:S(2)}, u32[]{:S(2)}) collective-permute-start(f32[32,128]{1,0:T(8,128)S(1)} %pad_maximum_fusion.refs_0_), channel_id=1, source_target_pairs={{0,4},{2,6},{4,0},{6,2},{1,5},{3,7},{5,1},{7,3},{8,12},{10,14},{12... | collective-permute-start | bytes 49160 | tf_op jit(solution)/shard_map/ppermute | solution.py:367
  60.9 1.9 %collective-permute-done.10.grad_ref = bf16[3,128,256]{2,1,0:T(8,128)(2,1)S(1)} collective-permute-done((bf16[3,128,256]{2,1,0:T(8,128)(2,1)S(1)}, bf16[3,128,256]{2,1,0:T(8,128)(2,1)S(1)}, u32[]{:S(2)}, u32[]{:S(2)}) %collective-permute-start.10) | collective-permute-done | bytes 196640 | tf_op jit(solution)/shard_map/ppermute | solution.py:367
  62.8 2.5 %collective-permute-start.7 = (f32[32,128]{1,0:T(8,128)S(1)}, f32[32,128]{1,0:T(8,128)S(1)}, u32[]{:S(2)}, u32[]{:S(2)}) collective-permute-start(f32[32,128]{1,0:T(8,128)S(1)} %pad_maximum_fusion.refs_0_), channel_id=1, source_target_pairs={{0,2},{2,0},{4,6},{6,4},{1,3},{3,1},{5,7},{7,5},{8,10},{10,8},{12,... | collective-permute-start | bytes 49160 | tf_op jit(solution)/shard_map/ppermute | solution.py:367
  65.3 1.9 %spatial_backward.5 = (bf16[256,1536]{1,0:T(8,128)(2,1)}, bf16[256,1536]{1,0:T(8,128)(2,1)}) custom-call(s32[3]{0:T(128)S(1)} %pad_add_fusion.scalars, bf16[256,1536]{1,0:T(8,128)(2,1)S(1)} %bitcast.14, bf16[256,1536]{1,0:T(8,128)(2,1)S(1)} %bitcast.19, bf16[256,1536]{1,0:T(8,128)(2,1)S(1)} %bitcast.24, ...), custom_call_target="tpu_custom_call", output_to_operand_aliasing={{0}: (6, {}), {1}: (7, {})} | custom-call | flops 200000000 | tf_op jit(solution)/shard_map/spatial_backward/pallas_call | solution.py:125
  67.3 4.8 %collective-permute-done.8.refs_2_ = f32[32,128]{1,0:T(8,128)S(1)} collective-permute-done((f32[32,128]{1,0:T(8,128)S(1)}, f32[32,128]{1,0:T(8,128)S(1)}, u32[]{:S(2)}, u32[]{:S(2)}) %collective-permute-start.8) | collective-permute-done | bytes 16416 | tf_op jit(solution)/shard_map/ppermute | solution.py:367
  72.0 1.3 %gain_gradients.1 = f32[2,16,1536]{2,1,0:T(8,128)} custom-call(s32[3]{0:T(128)S(1)} %pad_add_fusion.scalars, f32[32,128]{1,0:T(8,128)S(1)} %pad_maximum_fusion.refs_0_, f32[32,128]{1,0:T(8,128)S(1)} %collective-permute-done.7.refs_1_, f32[32,128]{1,0:T(8,128)S(1)} %collective-permute-done.8.refs_2_, f32[32,128]{1,0:T(8,128)S(1)} %collective-permute-done.9.refs_3_, ...), custom_call_target="tpu_custom_call" | custom-call | flops 100000000 | tf_op jit(solution)/shard_map/gain_gradients/pallas_call | solution.py:354
  73.3 1.9 %spatial_backward.6 = (bf16[256,1536]{1,0:T(8,128)(2,1)}, bf16[256,1536]{1,0:T(8,128)(2,1)}) custom-call(s32[3]{0:T(128)S(1)} %pad_add_fusion.scalars, bf16[256,1536]{1,0:T(8,128)(2,1)S(1)} %bitcast.15, bf16[256,1536]{1,0:T(8,128)(2,1)S(1)} %bitcast.20, bf16[256,1536]{1,0:T(8,128)(2,1)S(1)} %bitcast.25, ...), custom_call_target="tpu_custom_call", output_to_operand_aliasing={{0}: (6, {}), {1}: (7, {})} | custom-call | flops 200000000 | tf_op jit(solution)/shard_map/spatial_backward/pallas_call | solution.py:125
  75.2 1.9 %spatial_backward.7 = (bf16[256,1536]{1,0:T(8,128)(2,1)}, bf16[256,1536]{1,0:T(8,128)(2,1)}) custom-call(s32[3]{0:T(128)S(1)} %pad_add_fusion.scalars, bf16[256,1536]{1,0:T(8,128)(2,1)S(1)} %bitcast.16, bf16[256,1536]{1,0:T(8,128)(2,1)S(1)} %bitcast.21, bf16[256,1536]{1,0:T(8,128)(2,1)S(1)} %bitcast.26, ...), custom_call_target="tpu_custom_call", output_to_operand_aliasing={{0}: (6, {}), {1}: (7, {})} | custom-call | flops 200000000 | tf_op jit(solution)/shard_map/spatial_backward/pallas_call | solution.py:125
  (24 shorter events, 0.5 us)
Async XLA Ops:
  0.6 1.1 %copy-start.3 = (bf16[1,1,128,3072]{3,2,1,0:T(8,128)(2,1)S(1)}, bf16[1,1,128,3072]{3,2,1,0:T(8,128)(2,1)}, u32[]{:S(2)}) copy-start(bf16[1,1,128,3072]{3,2,1,0:T(8,128)(2,1)} %param.10) | copy-start | bytes 2359300
  1.8 21.2 %copy-start.4 = (f32[2,16,1536]{2,1,0:T(8,128)S(1)}, f32[2,16,1536]{2,1,0:T(8,128)}, u32[]{:S(2)}) copy-start(f32[2,16,1536]{2,1,0:T(8,128)} %refs_4_.1) | copy-start | bytes 589828
  2.7 37.4 %all-to-all-start = ((bf16[8,128,384]{2,1,0:T(8,128)(2,1)}), bf16[8,128,384]{2,1,0:T(8,128)(2,1)}, u32[]{:S(2)}, u32[]{:S(2)}) async-start(bf16[8,128,384]{2,1,0:T(8,128)(2,1)} %pack_cotangent.1), calls=%async_computation | async-start | bytes 1572864 | tf_op jit(solution)/shard_map/all_to_all | solution.py:384
  18.5 24.0 %collective-permute-start = (bf16[3,128,256]{2,1,0:T(8,128)(2,1)}, bf16[3,128,256]{2,1,0:T(8,128)(2,1)}, u32[]{:S(2)}, u32[]{:S(2)}) collective-permute-start(bf16[3,128,256]{2,1,0:T(8,128)(2,1)} %get-tuple-element.40), channel_id=1, source_target_pairs={{0,2},{2,0},{4,6},{6,4},{1,3},{3,1},{5,7},{7,5},{8,10},{10,8},{12,... | collective-permute-start | bytes 589832 | tf_op jit(solution)/shard_map/ppermute | solution.py:367
  20.5 23.8 %collective-permute-start.1 = (bf16[3,128,256]{2,1,0:T(8,128)(2,1)}, bf16[3,128,256]{2,1,0:T(8,128)(2,1)}, u32[]{:S(2)}, u32[]{:S(2)}) collective-permute-start(bf16[3,128,256]{2,1,0:T(8,128)(2,1)} %get-tuple-element.41), channel_id=1, source_target_pairs={{0,4},{2,6},{4,0},{6,2},{1,5},{3,7},{5,1},{7,3},{8,12},{10,14},{12... | collective-permute-start | bytes 589832 | tf_op jit(solution)/shard_map/ppermute | solution.py:367
  22.9 21.4 %collective-permute-start.2 = (bf16[3,128,256]{2,1,0:T(8,128)(2,1)}, bf16[3,128,256]{2,1,0:T(8,128)(2,1)}, u32[]{:S(2)}, u32[]{:S(2)}) collective-permute-start(bf16[3,128,256]{2,1,0:T(8,128)(2,1)} %get-tuple-element.42), channel_id=1, source_target_pairs={{0,6},{2,4},{4,2},{6,0},{1,7},{3,5},{5,3},{7,1},{8,14},{10,12},{12... | collective-permute-start | bytes 589832 | tf_op jit(solution)/shard_map/ppermute | solution.py:367
  40.1 15.3 %copy-start = (bf16[1,1,256,1536]{3,2,1,0:T(8,128)(2,1)S(1)}, bf16[1,1,256,1536]{3,2,1,0:T(8,128)(2,1)}, u32[]{:S(2)}) copy-start(bf16[1,1,256,1536]{3,2,1,0:T(8,128)(2,1)} %param.7) | copy-start | bytes 2359300
  40.1 15.3 %copy-start.1 = (bf16[1,1,256,1536]{3,2,1,0:T(8,128)(2,1)S(1)}, bf16[1,1,256,1536]{3,2,1,0:T(8,128)(2,1)}, u32[]{:S(2)}) copy-start(bf16[1,1,256,1536]{3,2,1,0:T(8,128)(2,1)} %param.8) | copy-start | bytes 2359300
  40.1 15.3 %copy-start.2 = (bf16[1,1,256,1536]{3,2,1,0:T(8,128)(2,1)S(1)}, bf16[1,1,256,1536]{3,2,1,0:T(8,128)(2,1)}, u32[]{:S(2)}) copy-start(bf16[1,1,256,1536]{3,2,1,0:T(8,128)(2,1)} %param.9) | copy-start | bytes 2359300
  48.8 5.0 %collective-permute-start.5 = (f32[8,128]{1,0:T(8,128)S(1)}, f32[8,128]{1,0:T(8,128)S(1)}, u32[]{:S(2)}, u32[]{:S(2)}) collective-permute-start(f32[8,128]{1,0:T(8,128)S(1)} %get-tuple-element.46), channel_id=1, source_target_pairs={{0,8},{8,0},{16,24},{24,16},{1,9},{9,1},{17,25},{25,17},{2,10},{10... | collective-permute-start | bytes 12296 | tf_op jit(solution)/shard_map/ppermute | solution.py:367
  48.9 26.4 %collective-permute-start.3 = (bf16[3,128,256]{2,1,0:T(8,128)(2,1)S(1)}, bf16[3,128,256]{2,1,0:T(8,128)(2,1)S(1)}, u32[]{:S(2)}, u32[]{:S(2)}) collective-permute-start(bf16[3,128,256]{2,1,0:T(8,128)(2,1)S(1)} %get-tuple-element.44), channel_id=1, source_target_pairs={{0,6},{2,4},{4,2},{6,0},{1,7},{3,5},{5,3},{7,1},{8,14},{10,12},{12... | collective-permute-start | bytes 589832 | tf_op jit(solution)/shard_map/ppermute | solution.py:367
  49.1 24.2 %collective-permute-start.4 = (bf16[3,128,256]{2,1,0:T(8,128)(2,1)S(1)}, bf16[3,128,256]{2,1,0:T(8,128)(2,1)S(1)}, u32[]{:S(2)}, u32[]{:S(2)}) collective-permute-start(bf16[3,128,256]{2,1,0:T(8,128)(2,1)S(1)} %get-tuple-element.45), channel_id=1, source_target_pairs={{0,4},{2,6},{4,0},{6,2},{1,5},{3,7},{5,1},{7,3},{8,12},{10,14},{12... | collective-permute-start | bytes 589832 | tf_op jit(solution)/shard_map/ppermute | solution.py:367
  53.8 9.1 %collective-permute-start.10 = (bf16[3,128,256]{2,1,0:T(8,128)(2,1)S(1)}, bf16[3,128,256]{2,1,0:T(8,128)(2,1)S(1)}, u32[]{:S(2)}, u32[]{:S(2)}) collective-permute-start(bf16[3,128,256]{2,1,0:T(8,128)(2,1)S(1)} %get-tuple-element.53), channel_id=1, source_target_pairs={{0,2},{2,0},{4,6},{6,4},{1,3},{3,1},{5,7},{7,5},{8,10},{10,8},{12,... | collective-permute-start | bytes 589832 | tf_op jit(solution)/shard_map/ppermute | solution.py:367
  53.8 3.7 %collective-permute-start.6 = (f32[16,128]{1,0:T(8,128)S(1)}, f32[16,128]{1,0:T(8,128)S(1)}, u32[]{:S(2)}, u32[]{:S(2)}) collective-permute-start(f32[16,128]{1,0:T(8,128)S(1)} %pad_maximum_fusion.1), channel_id=1, source_target_pairs={{0,16},{8,24},{16,0},{24,8},{1,17},{9,25},{17,1},{25,9},{2,18},{10... | collective-permute-start | bytes 24584 | tf_op jit(solution)/shard_map/ppermute | solution.py:367
  57.5 9.7 %collective-permute-start.9 = (f32[32,128]{1,0:T(8,128)S(1)}, f32[32,128]{1,0:T(8,128)S(1)}, u32[]{:S(2)}, u32[]{:S(2)}) collective-permute-start(f32[32,128]{1,0:T(8,128)S(1)} %pad_maximum_fusion.refs_0_), channel_id=1, source_target_pairs={{0,6},{2,4},{4,2},{6,0},{1,7},{3,5},{5,3},{7,1},{8,14},{10,12},{12... | collective-permute-start | bytes 49160 | tf_op jit(solution)/shard_map/ppermute | solution.py:367
  58.9 13.1 %collective-permute-start.8 = (f32[32,128]{1,0:T(8,128)S(1)}, f32[32,128]{1,0:T(8,128)S(1)}, u32[]{:S(2)}, u32[]{:S(2)}) collective-permute-start(f32[32,128]{1,0:T(8,128)S(1)} %pad_maximum_fusion.refs_0_), channel_id=1, source_target_pairs={{0,4},{2,6},{4,0},{6,2},{1,5},{3,7},{5,1},{7,3},{8,12},{10,14},{12... | collective-permute-start | bytes 49160 | tf_op jit(solution)/shard_map/ppermute | solution.py:367
  62.8 9.2 %collective-permute-start.7 = (f32[32,128]{1,0:T(8,128)S(1)}, f32[32,128]{1,0:T(8,128)S(1)}, u32[]{:S(2)}, u32[]{:S(2)}) collective-permute-start(f32[32,128]{1,0:T(8,128)S(1)} %pad_maximum_fusion.refs_0_), channel_id=1, source_target_pairs={{0,2},{2,0},{4,6},{6,4},{1,3},{3,1},{5,7},{7,5},{8,10},{10,8},{12,... | collective-permute-start | bytes 49160 | tf_op jit(solution)/shard_map/ppermute | solution.py:367

commit v6 on v5

--- a/solution.py
+++ b/solution.py
@@ -34,7 +34,7 @@
     return jnp.bitwise_xor(scalars[0], distance)
 
 
-def forward_kernel(scalars, query_ref, key_ref, value_ref, weights_ref, *refs):
+def forward_kernel(first, scalars, query_ref, key_ref, value_ref, weights_ref, *refs):
     (queries, key_rows, values, arrived), attended_refs = refs[-4:], refs[:-4]
     score_scale = HEAD_DIM ** (-0.5)
     groups, _, width = queries.shape
@@ -61,75 +61,94 @@
             weights = raised * (1.0 / jnp.sum(raised, axis=0, keepdims=True))
             weights_ref[group * own + head] = weights
             attended = dot(values[group, :, cols].T, weights.astype(jnp.bfloat16))
-            attended_refs[group][head] = attended.astype(jnp.bfloat16)
-
-
-def forward(scalars, queries, key_rows, values, groups):
+            chunk, place = (0, head) if head < first else (1, head - first)
+            attended_refs[chunk * groups + group][place] = attended.astype(jnp.bfloat16)
+
+
+def forward(scalars, queries, key_rows, values, groups, first):
     patches, feat = queries.shape
     heads = feat // HEAD_DIM
-    own = heads // groups
+    chunks = [first, heads // groups - first] if first < heads // groups else [first]
     fields = [
         pltpu.with_memory_space_constraint(field, pltpu.HBM) for field in (queries, key_rows, values)
     ]
     weights, *attended = pl.pallas_call(
-        forward_kernel,
+        functools.partial(forward_kernel, first),
         in_specs=[pl.BlockSpec(memory_space=pltpu.SMEM)]
         + [pl.BlockSpec(memory_space=pltpu.HBM)] * 3,
-        out_specs=[pl.BlockSpec(memory_space=pltpu.VMEM)] * (1 + groups),
+        out_specs=[pl.BlockSpec(memory_space=pltpu.VMEM)] * (1 + groups * len(chunks)),
         scratch_shapes=[pltpu.VMEM((groups, patches, feat // groups), jnp.bfloat16)] * 3
         + [pltpu.SemaphoreType.DMA((groups, 3))],
         out_shape=[jax.ShapeDtypeStruct((heads, patches, patches), jnp.float32)]
-        + [jax.ShapeDtypeStruct((own, HEAD_DIM, patches), jnp.bfloat16)] * groups,
+        + [
+            jax.ShapeDtypeStruct((size, HEAD_DIM, patches), jnp.bfloat16)
+            for size in chunks
+            for _ in range(groups)
+        ],
         compiler_params=params(patches),
         cost_estimate=cost(6),
         name="spatial_forward",
     )(scalars, *fields)
-    return weights, attended
-
-
-def backward_kernel(distance, scalars, query_ref, key_ref, value_ref, weights_ref, grad_ref, *refs):
+    return weights, [attended[start : start + groups] for start in range(0, len(attended), groups)]
+
+
+def backward_kernel(
+    runs_of, scalars, query_ref, key_ref, value_ref, weights_ref, grad_ref, *refs
+):
     gq_ref, gk_ref, gq, gk, sent = refs[-5:]
     score_scale = HEAD_DIM ** (-0.5)
-    own = grad_ref.shape[0]
-    start = partner(scalars, distance) * (own * HEAD_DIM)
-    columns = [
-        pl.ds(pl.multiple_of(start + head * HEAD_DIM, HEAD_DIM), HEAD_DIM) for head in range(own)
+    runs = runs_of(scalars)
+    each = grad_ref.shape[0] // len(runs)
+    heads = [
+        (pl.ds(pl.multiple_of((column + place) * HEAD_DIM, HEAD_DIM), HEAD_DIM), weight + place)
+        for column, weight in runs
+        for place in range(each)
     ]
-    spatial_grads = [dot(value_ref[:, columns[head]], grad_ref[head]) for head in range(own)]
+    spatial_grads = [
+        dot(value_ref[:, columns], grad_ref[head]) for head, (columns, _) in enumerate(heads)
+    ]
     all_scores = []
-    for head, spatial_grad in enumerate(spatial_grads):
-        weights = weights_ref[distance * own + head]
+    for spatial_grad, (_, weight) in zip(spatial_grads, heads):
+        weights = weights_ref[weight]
         row_sum = jnp.sum(spatial_grad * weights, axis=0, keepdims=True)
         scores = weights * (spatial_grad - row_sum) * score_scale
         all_scores.append(scores.astype(jnp.bfloat16))
-    there = pl.ds(pl.multiple_of(start, HEAD_DIM), own * HEAD_DIM)
-    copies = [
-        pltpu.make_async_copy(gk, gk_ref.at[:, there], sent.at[0]),
-        pltpu.make_async_copy(gq, gq_ref.at[:, there], sent.at[1]),
-    ]
+    copies = []
+
+    def send(side, source, target):
+        for run, (column, _) in enumerate(runs):
+            here = pl.ds(run * each * HEAD_DIM, each * HEAD_DIM)
+            there = pl.ds(pl.multiple_of(column * HEAD_DIM, HEAD_DIM), each * HEAD_DIM)
+            copy = pltpu.make_async_copy(
+                source.at[:, here], target.at[:, there], sent.at[side, run]
+            )
+            copy.start()
+            copies.append(copy)
+
     for head, scores in enumerate(all_scores):
         cols = pl.ds(head * HEAD_DIM, HEAD_DIM)
-        gk[:, cols] = dot(scores, query_ref[:, columns[head]]).astype(jnp.bfloat16)
-    copies[0].start()
+        gk[:, cols] = dot(scores, query_ref[:, heads[head][0]]).astype(jnp.bfloat16)
+    send(0, gk, gk_ref)
     for head, scores in enumerate(all_scores):
         cols = pl.ds(head * HEAD_DIM, HEAD_DIM)
-        gq[:, cols] = dot(key_ref[:, columns[head]].T, scores).astype(jnp.bfloat16).T
-    copies[1].start()
+        gq[:, cols] = dot(key_ref[:, heads[head][0]].T, scores).astype(jnp.bfloat16).T
+    send(1, gq, gq_ref)
     for copy in copies:
         copy.wait()
 
 
-def backward(scalars, fields, weights, grads, distance, earlier):
+def backward(scalars, fields, weights, grads, runs_of, earlier):
     patches, feat = fields[0].shape
-    own = grads.shape[0]
+    heads = grads.shape[0]
+    runs = len(runs_of([0]))
     return pl.pallas_call(
-        functools.partial(backward_kernel, distance),
+        functools.partial(backward_kernel, runs_of),
         in_specs=[pl.BlockSpec(memory_space=pltpu.SMEM)]
         + [pl.BlockSpec(memory_space=pltpu.VMEM)] * 5
         + [pl.BlockSpec(memory_space=pl.ANY)] * len(earlier),
         out_specs=[pl.BlockSpec(memory_space=pl.ANY)] * 2,
-        scratch_shapes=[pltpu.VMEM((patches, own * HEAD_DIM), jnp.bfloat16)] * 2
-        + [pltpu.SemaphoreType.DMA((2,))],
+        scratch_shapes=[pltpu.VMEM((patches, heads * HEAD_DIM), jnp.bfloat16)] * 2
+        + [pltpu.SemaphoreType.DMA((2, runs))],
         out_shape=[jax.ShapeDtypeStruct((patches, feat), jnp.bfloat16)] * 2,
         input_output_aliases={6 + index: index for index in range(len(earlier))},
         compiler_params=params(patches),
@@ -279,10 +298,9 @@
             ).astype(jnp.bfloat16)
 
 
-def temporal_kernel(frames, scalars, *refs):
-    attended_refs, (upstream_ref, gain_ref) = refs[:frames], refs[frames : frames + 2]
-    grad_refs, mixed_ref = refs[frames + 2 : 2 * frames + 2], refs[2 * frames + 2]
-    attended, grads, mixed_sum = refs[2 * frames + 3 :]
+def temporal_kernel(frames, first, scalars, *refs):
+    attended_refs, (upstream_ref, gain_ref, earlier_ref) = refs[:frames], refs[frames : frames + 3]
+    *grad_refs, mixed_ref, attended, grads, mixed_sum = refs[frames + 3 :]
     head = pl.program_id(0)
     for distance, ref in enumerate(attended_refs):
         attended[partner(scalars, distance)] = ref[0]
@@ -293,27 +311,31 @@
 
     @pl.when(head == 0)
     def _():
-        mixed_ref[...] = jnp.full(mixed_ref.shape, scalars[2].astype(jnp.float32))
-
-    mixed_ref[pl.ds(head, 1), :] = jnp.sum(mixed_sum[...].T, axis=0, keepdims=True) * 0.5
-
-
-def temporal(scalars, attended, upstream, gain):
-    spaces, frames, heads, feat, lanes = upstream.shape
-    patches = spaces * lanes
-    rows = -(-(heads + 1) // 8) * 8
+        mixed_ref[...] = earlier_ref[...]
+
+    summed = jnp.sum(mixed_sum[...].T, axis=0, keepdims=True) * 0.5
+    mixed_ref[pl.ds(first + head, 1), :] = summed
+
+
+def temporal(scalars, attended, upstream, gain, earlier, first):
+    spaces, frames, _, feat, lanes = upstream.shape
+    heads, _, patches = attended[0].shape
     plane = pl.BlockSpec((1, feat, patches), lambda i, sc: (i, 0, 0))
+    rows = pl.BlockSpec(earlier.shape, lambda i, sc: (0, 0))
     *grads, mixed = pl.pallas_call(
-        functools.partial(temporal_kernel, frames),
+        functools.partial(temporal_kernel, frames, first),
         grid_spec=pltpu.PrefetchScalarGridSpec(
             num_scalar_prefetch=1,
             grid=(heads,),
             in_specs=[plane] * frames
             + [
-                pl.BlockSpec((spaces, frames, 1, feat, lanes), lambda i, sc: (0, 0, i, 0, 0)),
-                pl.BlockSpec((1, feat, lanes), lambda i, sc: (i, 0, 0)),
+                pl.BlockSpec(
+                    (spaces, frames, 1, feat, lanes), lambda i, sc: (0, 0, first + i, 0, 0)
+                ),
+                pl.BlockSpec((1, feat, lanes), lambda i, sc: (first + i, 0, 0)),
+                rows,
             ],
-            out_specs=[plane] * frames + [pl.BlockSpec((rows, feat), lambda i, sc: (0, 0))],
+            out_specs=[plane] * frames + [rows],
             scratch_shapes=[
                 pltpu.VMEM((frames, feat, patches), jnp.bfloat16),
                 pltpu.VMEM((frames, feat, patches), jnp.bfloat16),
@@ -321,11 +343,11 @@
             ],
         ),
         out_shape=[jax.ShapeDtypeStruct((heads, feat, patches), jnp.bfloat16)] * frames
-        + [jax.ShapeDtypeStruct((rows, feat), jnp.float32)],
+        + [jax.ShapeDtypeStruct(earlier.shape, jnp.float32)],
         compiler_params=params(patches),
-        cost_estimate=cost(4),
+        cost_estimate=cost(2000),
         name="temporal",
-    )(scalars, *attended, upstream, gain)
+    )(scalars, *attended, upstream, gain, earlier)
     return grads, mixed
 
 
@@ -384,39 +406,72 @@
     incoming = lax.all_to_all(packed, ("tm", "space"), split_axis=0, concat_axis=0, tiled=True)
     queries, _ = lax.optimization_barrier((queries, packed))
     fields = (queries, key_rows, values)
-    weights, attended = forward(scalars, *fields, frames)
-    attended = [attended[0]] + [
-        swap(attended[distance], "tm", frames, distance) for distance in range(1, frames)
-    ]
+    first = max(1, own // 3)
+    weights, attended = forward(scalars, *fields, frames, first)
     incoming, _ = lax.optimization_barrier((incoming, weights))
+
+    def exchange(planes):
+        return [planes[0]] + [
+            swap(planes[distance], "tm", frames, distance) for distance in range(1, frames)
+        ]
+
+    early, later = attended
+    early, later, incoming = lax.optimization_barrier((exchange(early), later, incoming))
+    later = exchange(later)
     upstream = turn(incoming, frames, spaces)
     rows = lax.dynamic_index_in_dim(gains, task_ids[0], 1, keepdims=False)
     product = lax.dynamic_slice_in_dim(rows[0] * rows[1], frame * width, width, 0)
     gain = jnp.broadcast_to(
         product.reshape(own, HEAD_DIM, 1), (own, HEAD_DIM, patches // spaces)
     )
-    grads, mixed = temporal(scalars, attended, upstream, gain)
-    grads = [grads[0]] + [
-        swap(grads[distance], "tm", frames, distance) for distance in range(1, frames)
-    ]
-    here = grads[0]
+    marks = jnp.full((-(-(own + 1) // 8) * 8, HEAD_DIM), task_ids[0].astype(jnp.float32))
+    early_grads, mixed = temporal(scalars, early, upstream, gain, marks, 0)
+    early_grads = exchange(early_grads)
+    grads, mixed = temporal(scalars, later, upstream, gain, mixed, first)
+    grads = exchange(grads)
+
+    def first_heads(results):
+        return backward(
+            scalars,
+            fields,
+            weights,
+            jnp.concatenate(early_grads),
+            lambda scalars: [
+                (partner(scalars, group) * own, group * own) for group in range(frames)
+            ],
+            results,
+        )
+
+    def other_heads(distance, results):
+        return backward(
+            scalars,
+            fields,
+            weights,
+            grads[distance],
+            lambda scalars: [(partner(scalars, distance) * own + first, distance * own + first)],
+            results,
+        )
+
     for bit in range(clips.bit_length() - 1):
         other = swap(mixed, "dp", clips, 1 << bit)
         if bit == 0:
-            here, other = lax.optimization_barrier((here, other))
+            grads[0], early_grads, other = lax.optimization_barrier(
+                (grads[0], early_grads, other)
+            )
         mixed = jnp.concatenate([mixed, other], axis=0)
-    results = backward(scalars, fields, weights, here, 0, ())
+    results = other_heads(0, ())
     mixed, results = lax.optimization_barrier((mixed, results))
     mixed = [mixed] + [swap(mixed, "tm", frames, distance) for distance in range(1, frames)]
+    results = first_heads(results)
     distance = 1
     if frames > 2:
-        results = backward(scalars, fields, weights, grads[1], 1, results)
-        mixed, results = lax.optimization_barrier((mixed, results))
+        results = other_heads(1, results)
         distance = 2
+    mixed, results = lax.optimization_barrier((mixed, results))
     grad_gains = gain_gradients(scalars, mixed, gains, own, frames, clips)
     grad_gains, results = lax.optimization_barrier((grad_gains, results))
     for distance in range(distance, frames):
-        results = backward(scalars, fields, weights, grads[distance], distance, results)
+        results = other_heads(distance, results)
     grad_queries, grad_keys = results
     return (
         grad_queries.reshape(query_heads.shape),
@@ -469,8 +524,8 @@
     )
     scalars = jnp.zeros((1,), jnp.int32)
     fields = (queries, key_rows, values)
-    weights, attended = forward(scalars, *fields, 1)
-    attended_field = jnp.transpose(attended[0], (2, 0, 1)).reshape(1, 1, patches, feat)
+    weights, attended = forward(scalars, *fields, 1, heads)
+    attended_field = jnp.transpose(attended[0][0], (2, 0, 1)).reshape(1, 1, patches, feat)
     upstream = lax.all_to_all(
         lax.all_to_all(cotangent, "space", split_axis=3, concat_axis=2, tiled=True),
         "tm",
@@ -505,7 +560,9 @@
         tiled=True,
     )
     head_grads = jnp.transpose(returned.reshape(patches, heads, HEAD_DIM), (1, 2, 0))
-    grad_queries, grad_keys = backward(scalars, fields, weights, head_grads, 0, ())
+    grad_queries, grad_keys = backward(
+        scalars, fields, weights, head_grads, lambda scalars: [(0, 0)], ()
+    )
     return (
         grad_queries.reshape(query_heads.shape),
         grad_keys.reshape(query_heads.shape),
@@ -519,7 +576,7 @@
     def local(query_heads, *others):
         heads = query_heads.shape[3] // HEAD_DIM
         powers = all(size & (size - 1) == 0 for size in (clips, frames))
-        if powers and frames <= 4 and heads % frames == 0:
+        if powers and frames <= 4 and heads % frames == 0 and heads > frames:
             return split_by_heads(query_heads, *others, clips, frames, spaces)
         return split_by_patches(query_heads, *others)
 

time: 77.5 us -> 79 us (1.019)
  waiting for transfers between devices: 25.8 us -> 12.7 us
  starting transfers between devices: 24.3 us -> 32.1 us
  Pallas kernels: 23.6 us -> 27.3 us
  local copies, waits for them, and re-layouts: 1.25 us -> 3.21 us
  other arithmetic: 0.18 us -> 1.11 us
    ppermute x11 -> x17, starting transfers between devices: 17 us -> 24.8 us  [swap(): return lax.ppermute(field, axis, [(i, i ^ distance) for i in range(size)])]
    all_to_all x1, waiting for transfers between devices: 17 us -> 9.78 us  [split_by_heads(): lax.all_to_all(packed, ('tm', 'space'), split_axis=0, concat_axis=0, tile...]
    ppermute x11 -> x17, waiting for transfers between devices: 8.77 us -> 2.91 us  [swap(): return lax.ppermute(field, axis, [(i, i ^ distance) for i in range(size)])]
    pallas_call x6 -> x8, Pallas kernels: 19.1 us -> 22.9 us  [the longest x5 9.53 us: backward(): pl.pallas_call(functools.partial(backward_kernel, runs_of), in_specs=[pl....]
    unnamed x10 -> x16, local copies, waits for them, and re-layouts: 1.14 us -> 3.1 us
    concatenate x0 -> x1, other arithmetic: none -> 0.94 us  [first_heads(): jnp.concatenate(early_grads)]
  transfers between devices with their start and end apart: 12 -> 18, of which waited for: 5 -> 4; matrix products, arithmetic and copies ran while one was open for 0% -> 2% of each run, Pallas kernels for 21% -> 31%
where the time goes in v6:
time: 79 us; the launch traced here: 78.6 us
  starting transfers between devices  32.1 us (41%)
  Pallas kernels  27.3 us (35%)
  waiting for transfers between devices  12.7 us (16%)
  local copies, waits for them, and re-layouts  3.21 us (4%)
  between operations  2.17 us (3%)
  other arithmetic  1.11 us (1%)
    ppermute x17, starting transfers between devices, swap(): return lax.ppermute(field, axis, [(i, i ^ distance) for i in range(size)])  24.8 us
    all_to_all x1, waiting for transfers between devices, split_by_heads(): lax.all_to_all(packed, ('tm', 'space'), split_axis=0, concat_axis=0, tile...  9.78 us
    pallas_call x5, Pallas kernels, backward(): pl.pallas_call(functools.partial(backward_kernel, runs_of), in_specs=[pl....  9.53 us
    all_to_all x1, starting transfers between devices, split_by_heads(): lax.all_to_all(packed, ('tm', 'space'), split_axis=0, concat_axis=0, tile...  7.29 us
    pallas_call x1, Pallas kernels, forward(): pl.pallas_call(functools.partial(forward_kernel, first), in_specs=[pl.Blo...  6.86 us
    pallas_call x2, Pallas kernels, temporal(): pl.pallas_call(functools.partial(temporal_kernel, frames, first), grid_sp...  6.48 us
    unnamed x16, local copies, waits for them, and re-layouts  3.1 us
    ppermute x17, waiting for transfers between devices, swap(): return lax.ppermute(field, axis, [(i, i ^ distance) for i in range(size)])  2.91 us
  transfers between devices with their start and end apart: 18, of which 4 were waited for; matrix products, arithmetic and copies ran while one was open for 2% of the time, Pallas kernels for 31%

profile of v6, /device:TPU:0, one launch (start us, length us, event | category | flops | bytes accessed | tf_op | source)
XLA Modules:
  0.0 78.6 jit_solution(15889636814020562153)
XLA Ops:
  0.6 1.1 %copy-done.3 = bf16[1,1,128,3072]{3,2,1,0:T(8,128)(2,1)S(1)} copy-done((bf16[1,1,128,3072]{3,2,1,0:T(8,128)(2,1)S(1)}, bf16[1,1,128,3072]{3,2,1,0:T(8,128)(2,1)}, u32[]{:S(2)}) %copy-start.3) | copy-done | bytes 786456
  2.7 7.3 %all-to-all-start = ((bf16[8,128,384]{2,1,0:T(8,128)(2,1)}), bf16[8,128,384]{2,1,0:T(8,128)(2,1)}, u32[]{:S(2)}, u32[]{:S(2)}) async-start(bf16[8,128,384]{2,1,0:T(8,128)(2,1)} %pack_cotangent.1), calls=%async_computation | async-start | bytes 1572864 | tf_op jit(solution)/shard_map/all_to_all | solution.py:406
  11.4 6.9 %spatial_forward.1 = (f32[12,256,256]{2,1,0:T(8,128)S(1)}, bf16[1,128,256]{2,1,0:T(8,128)(2,1)S(1)}, bf16[1,128,256]{2,1,0:T(8,128)(2,1)}, bf16[1,128,256]{2,1,0...) custom-call(s32[3]{0:T(128)S(1)} %pad_add_fusion.scalars, ...), custom_call_target="tpu_custom_call" | custom-call | flops 600000000 | tf_op jit(solution)/shard_map/spatial_forward/pallas_call | solution.py:75
  20.2 2.0 %collective-permute-start = (bf16[1,128,256]{2,1,0:T(8,128)(2,1)}, bf16[1,128,256]{2,1,0:T(8,128)(2,1)}, u32[]{:S(2)}, u32[]{:S(2)}) collective-permute-start(bf16[1,128,256]{2,1,0:T(8,128)(2,1)} %get-tuple-element.64), channel_id=1, source_target_pairs={{0,2},{2,0},{4,6},{6,4},{1,3},{3,1},{5,7},{7,5},{8,10},{10,8},{12,... | collective-permute-start | bytes 196616 | tf_op jit(solution)/shard_map/ppermute | solution.py:389
  22.2 2.4 %collective-permute-start.1 = (bf16[1,128,256]{2,1,0:T(8,128)(2,1)}, bf16[1,128,256]{2,1,0:T(8,128)(2,1)}, u32[]{:S(2)}, u32[]{:S(2)}) collective-permute-start(bf16[1,128,256]{2,1,0:T(8,128)(2,1)} %get-tuple-element.65), channel_id=1, source_target_pairs={{0,4},{2,6},{4,0},{6,2},{1,5},{3,7},{5,1},{7,3},{8,12},{10,14},{12... | collective-permute-start | bytes 196616 | tf_op jit(solution)/shard_map/ppermute | solution.py:389
  24.7 9.8 %all-to-all-done.field_ref = bf16[8,128,384]{2,1,0:T(8,128)(2,1)} async-done(((bf16[8,128,384]{2,1,0:T(8,128)(2,1)}), bf16[8,128,384]{2,1,0:T(8,128)(2,1)}, u32[]{:S(2)}, u32[]{:S(2)}) %all-to-all-start) | async-done | bytes 786464 | tf_op jit(solution)/shard_map/all_to_all | solution.py:406
  35.2 1.3 %collective-permute-start.3 = (bf16[2,128,256]{2,1,0:T(8,128)(2,1)}, bf16[2,128,256]{2,1,0:T(8,128)(2,1)}, u32[]{:S(2)}, u32[]{:S(2)}) collective-permute-start(bf16[2,128,256]{2,1,0:T(8,128)(2,1)} %copy-done.7), channel_id=1, source_target_pairs={{0,2},{2,0},{4,6},{6,4},{1,3},{3,1},{5,7},{7,5},{8,10},{10,8},{12,... | collective-permute-start | bytes 393224 | tf_op jit(solution)/shard_map/ppermute | solution.py:389
  36.6 3.0 %collective-permute-start.5 = (bf16[2,128,256]{2,1,0:T(8,128)(2,1)}, bf16[2,128,256]{2,1,0:T(8,128)(2,1)}, u32[]{:S(2)}, u32[]{:S(2)}) collective-permute-start(bf16[2,128,256]{2,1,0:T(8,128)(2,1)} %copy-done.5), channel_id=1, source_target_pairs={{0,6},{2,4},{4,2},{6,0},{1,7},{3,5},{5,3},{7,1},{8,14},{10,12},{12... | collective-permute-start | bytes 393224 | tf_op jit(solution)/shard_map/ppermute | solution.py:389
  39.6 2.2 %turn_cotangent.1.refs_4_ = bf16[2,4,3,128,128]{4,3,2,1,0:T(8,128)(2,1)S(1)} custom-call(bf16[8,128,384]{2,1,0:T(8,128)(2,1)} %all-to-all-done.field_ref), custom_call_target="tpu_custom_call" | custom-call | flops 200000000 | tf_op jit(solution)/shard_map/turn_cotangent/pallas_call | solution.py:199
  41.9 3.0 %temporal.2 = (bf16[1,128,256]{2,1,0:T(8,128)(2,1)S(1)}, bf16[1,128,256]{2,1,0:T(8,128)(2,1)}, bf16[1,128,256]{2,1,0:T(8,128)(2,1)}, bf16[1,128,256]{2,1,0:T(8,128)(2,1)}, f32[8,128]{1,0:T(8,128)S(1)}) custom-call(s32[3]{0:T(128)S(1)} %pad_add_fusion.scalars, bf16[1,128,256]{2,1,0:T(8,128)(2,1)S(1)} %get-tuple-element.77.refs_0_, ...), custom_call_target="tpu_custom_call" | custom-call | flops 199999995904 | tf_op jit(solution)/shard_map/temporal/pallas_call | solution.py:325
  45.2 1.0 %collective-permute-start.9 = (bf16[1,128,256]{2,1,0:T(8,128)(2,1)}, bf16[1,128,256]{2,1,0:T(8,128)(2,1)}, u32[]{:S(2)}, u32[]{:S(2)}) collective-permute-start(bf16[1,128,256]{2,1,0:T(8,128)(2,1)} %get-tuple-element.88), channel_id=1, source_target_pairs={{0,4},{2,6},{4,0},{6,2},{1,5},{3,7},{5,1},{7,3},{8,12},{10,14},{12... | collective-permute-start | bytes 196616 | tf_op jit(solution)/shard_map/ppermute | solution.py:389
  46.3 3.0 %collective-permute-start.10 = (bf16[1,128,256]{2,1,0:T(8,128)(2,1)}, bf16[1,128,256]{2,1,0:T(8,128)(2,1)}, u32[]{:S(2)}, u32[]{:S(2)}) collective-permute-start(bf16[1,128,256]{2,1,0:T(8,128)(2,1)} %get-tuple-element.89), channel_id=1, source_target_pairs={{0,6},{2,4},{4,2},{6,0},{1,7},{3,5},{5,3},{7,1},{8,14},{10,12},{12... | collective-permute-start | bytes 196616 | tf_op jit(solution)/shard_map/ppermute | solution.py:389
  49.3 1.2 %collective-permute-done.4.refs_2_ = bf16[2,128,256]{2,1,0:T(8,128)(2,1)} collective-permute-done((bf16[2,128,256]{2,1,0:T(8,128)(2,1)}, bf16[2,128,256]{2,1,0:T(8,128)(2,1)}, u32[]{:S(2)}, u32[]{:S(2)}) %collective-permute-start.4) | collective-permute-done | bytes 131104 | tf_op jit(solution)/shard_map/ppermute | solution.py:389
  50.5 3.5 %temporal.3 = (bf16[2,128,256]{2,1,0:T(8,128)(2,1)S(1)}, bf16[2,128,256]{2,1,0:T(8,128)(2,1)S(1)}, bf16[2,128,256]{2,1,0:T(8,128)(2,1)S(1)}, bf16[2,128,256]{2,1,0:T(8,128)(2,1)S(1)}, f32[8,128]{1,0:T(8,128)S(1)}) custom-call(s32[3]{0:T(128)S(1)} %pad_add_fusion.scalars, bf16[2,128,256]{2,1,0:T(8,128)(2,1)S(1)} %get-tuple-element.72.refs_0_, ...), custom_call_target="tpu_custom_call" | custom-call | flops 199999995904 | tf_op jit(solution)/shard_map/temporal/pallas_call | solution.py:325
  54.2 5.5 %collective-permute-start.7 = (bf16[2,128,256]{2,1,0:T(8,128)(2,1)S(1)}, bf16[2,128,256]{2,1,0:T(8,128)(2,1)S(1)}, u32[]{:S(2)}, u32[]{:S(2)}) collective-permute-start(bf16[2,128,256]{2,1,0:T(8,128)(2,1)S(1)} %get-tuple-element.83), channel_id=1, source_target_pairs={{0,4},{2,6},{4,0},{6,2},{1,5},{3,7},{5,1},{7,3},{8,12},{10,14},{12... | collective-permute-start | bytes 393224 | tf_op jit(solution)/shard_map/ppermute | solution.py:389
  59.7 1.6 %collective-permute-start.12 = (f32[16,128]{1,0:T(8,128)S(1)}, f32[16,128]{1,0:T(8,128)S(1)}, u32[]{:S(2)}, u32[]{:S(2)}) collective-permute-start(f32[16,128]{1,0:T(8,128)S(1)} %pad_maximum_fusion.2), channel_id=1, source_target_pairs={{0,16},{8,24},{16,0},{24,8},{1,17},{9,25},{17,1},{25,9},{2,18},{10... | collective-permute-start | bytes 24584 | tf_op jit(solution)/shard_map/ppermute | solution.py:389
  62.2 1.8 %spatial_backward.5 = (bf16[256,1536]{1,0:T(8,128)(2,1)}, bf16[256,1536]{1,0:T(8,128)(2,1)}) custom-call(s32[3]{0:T(128)S(1)} %pad_add_fusion.scalars, bf16[256,1536]{1,0:T(8,128)(2,1)S(1)} %bitcast.14, bf16[256,1536]{1,0:T(8,128)(2,1)S(1)} %bitcast.20, bf16[256,1536]{1,0:T(8,128)(2,1)S(1)} %bitcast.26, f32[12,256,256]{2,1,0:T(8,128)S(1)} %get-tuple-element.62.weights_ref, ...), custom_call_target="tpu_custom_call" | custom-call | flops 200000000 | tf_op jit(solution)/shard_map/spatial_backward/pallas_call | solution.py:144
  64.1 1.6 %collective-permute-start.15 = (f32[32,128]{1,0:T(8,128)S(1)}, f32[32,128]{1,0:T(8,128)S(1)}, u32[]{:S(2)}, u32[]{:S(2)}) collective-permute-start(f32[32,128]{1,0:T(8,128)S(1)} %pad_maximum_fusion.1.refs_0_), channel_id=1, source_target_pairs={{0,6},{2,4},{4,2},{6,0},{1,7},{3,5},{5,3},{7,1},{8,14},{10,12},{12... | collective-permute-start | bytes 49160 | tf_op jit(solution)/shard_map/ppermute | solution.py:389
  65.7 2.0 %collective-permute-start.14 = (f32[32,128]{1,0:T(8,128)S(1)}, f32[32,128]{1,0:T(8,128)S(1)}, u32[]{:S(2)}, u32[]{:S(2)}) collective-permute-start(f32[32,128]{1,0:T(8,128)S(1)} %pad_maximum_fusion.1.refs_0_), channel_id=1, source_target_pairs={{0,4},{2,6},{4,0},{6,2},{1,5},{3,7},{5,1},{7,3},{8,12},{10,14},{12... | collective-permute-start | bytes 49160 | tf_op jit(solution)/shard_map/ppermute | solution.py:389
  67.6 2.2 %spatial_backward.6 = (bf16[256,1536]{1,0:T(8,128)(2,1)}, bf16[256,1536]{1,0:T(8,128)(2,1)}) custom-call(s32[3]{0:T(128)S(1)} %pad_add_fusion.scalars, bf16[256,1536]{1,0:T(8,128)(2,1)S(1)} %bitcast.15, bf16[256,1536]{1,0:T(8,128)(2,1)S(1)} %bitcast.21, bf16[256,1536]{1,0:T(8,128)(2,1)S(1)} %bitcast.27, ...), custom_call_target="tpu_custom_call", output_to_operand_aliasing={{0}: (6, {}), {1}: (7, {})} | custom-call | flops 200000000 | tf_op jit(solution)/shard_map/spatial_backward/pallas_call | solution.py:144
  70.8 1.8 %spatial_backward.7 = (bf16[256,1536]{1,0:T(8,128)(2,1)}, bf16[256,1536]{1,0:T(8,128)(2,1)}) custom-call(s32[3]{0:T(128)S(1)} %pad_add_fusion.scalars, bf16[256,1536]{1,0:T(8,128)(2,1)S(1)} %bitcast.16, bf16[256,1536]{1,0:T(8,128)(2,1)S(1)} %bitcast.22, bf16[256,1536]{1,0:T(8,128)(2,1)S(1)} %bitcast.28, ...), custom_call_target="tpu_custom_call", output_to_operand_aliasing={{0}: (6, {}), {1}: (7, {})} | custom-call | flops 200000000 | tf_op jit(solution)/shard_map/spatial_backward/pallas_call | solution.py:144
  73.6 1.3 %gain_gradients.1 = f32[2,16,1536]{2,1,0:T(8,128)} custom-call(s32[3]{0:T(128)S(1)} %pad_add_fusion.scalars, f32[32,128]{1,0:T(8,128)S(1)} %pad_maximum_fusion.1.refs_0_, f32[32,128]{1,0:T(8,128)S(1)} %collective-permute-done.13.refs_1_, f32[32,128]{1,0:T(8,128)S(1)} %collective-permute-done.14.refs_2_, f32[32,128]{1,0:T(8,128)S(1)} %collective-permute-done.15.refs_3_, ...), custom_call_target="tpu_custom_call" | custom-call | flops 100000000 | tf_op jit(solution)/shard_map/gain_gradients/pallas_call | solution.py:376
  74.9 1.8 %spatial_backward.8 = (bf16[256,1536]{1,0:T(8,128)(2,1)}, bf16[256,1536]{1,0:T(8,128)(2,1)}) custom-call(s32[3]{0:T(128)S(1)} %pad_add_fusion.scalars, bf16[256,1536]{1,0:T(8,128)(2,1)S(1)} %bitcast.17, bf16[256,1536]{1,0:T(8,128)(2,1)S(1)} %bitcast.23, bf16[256,1536]{1,0:T(8,128)(2,1)S(1)} %bitcast.29, ...), custom_call_target="tpu_custom_call", output_to_operand_aliasing={{0}: (6, {}), {1}: (7, {})} | custom-call | flops 200000000 | tf_op jit(solution)/shard_map/spatial_backward/pallas_call | solution.py:144
  76.7 1.8 %spatial_backward.9 = (bf16[256,1536]{1,0:T(8,128)(2,1)}, bf16[256,1536]{1,0:T(8,128)(2,1)}) custom-call(s32[3]{0:T(128)S(1)} %pad_add_fusion.scalars, bf16[256,1536]{1,0:T(8,128)(2,1)S(1)} %bitcast.18, bf16[256,1536]{1,0:T(8,128)(2,1)S(1)} %bitcast.24, bf16[256,1536]{1,0:T(8,128)(2,1)S(1)} %bitcast.30, ...), custom_call_target="tpu_custom_call", output_to_operand_aliasing={{0}: (6, {}), {1}: (7, {})} | custom-call | flops 200000000 | tf_op jit(solution)/shard_map/spatial_backward/pallas_call | solution.py:144
  (46 shorter events, 7.5 us)
Async XLA Ops:
  0.6 1.1 %copy-start.3 = (bf16[1,1,128,3072]{3,2,1,0:T(8,128)(2,1)S(1)}, bf16[1,1,128,3072]{3,2,1,0:T(8,128)(2,1)}, u32[]{:S(2)}) copy-start(bf16[1,1,128,3072]{3,2,1,0:T(8,128)(2,1)} %param.10) | copy-start | bytes 2359300
  1.8 22.8 %copy-start.4 = (f32[2,16,1536]{2,1,0:T(8,128)S(1)}, f32[2,16,1536]{2,1,0:T(8,128)}, u32[]{:S(2)}) copy-start(f32[2,16,1536]{2,1,0:T(8,128)} %refs_4_.1) | copy-start | bytes 589828
  2.7 31.8 %all-to-all-start = ((bf16[8,128,384]{2,1,0:T(8,128)(2,1)}), bf16[8,128,384]{2,1,0:T(8,128)(2,1)}, u32[]{:S(2)}, u32[]{:S(2)}) async-start(bf16[8,128,384]{2,1,0:T(8,128)(2,1)} %pack_cotangent.1), calls=%async_computation | async-start | bytes 1572864 | tf_op jit(solution)/shard_map/all_to_all | solution.py:406
  18.2 0.7 copy-start.5
  20.2 14.3 %collective-permute-start = (bf16[1,128,256]{2,1,0:T(8,128)(2,1)}, bf16[1,128,256]{2,1,0:T(8,128)(2,1)}, u32[]{:S(2)}, u32[]{:S(2)}) collective-permute-start(bf16[1,128,256]{2,1,0:T(8,128)(2,1)} %get-tuple-element.64), channel_id=1, source_target_pairs={{0,2},{2,0},{4,6},{6,4},{1,3},{3,1},{5,7},{7,5},{8,10},{10,8},{12,... | collective-permute-start | bytes 196616 | tf_op jit(solution)/shard_map/ppermute | solution.py:389
  22.2 13.0 %collective-permute-start.1 = (bf16[1,128,256]{2,1,0:T(8,128)(2,1)}, bf16[1,128,256]{2,1,0:T(8,128)(2,1)}, u32[]{:S(2)}, u32[]{:S(2)}) collective-permute-start(bf16[1,128,256]{2,1,0:T(8,128)(2,1)} %get-tuple-element.65), channel_id=1, source_target_pairs={{0,4},{2,6},{4,0},{6,2},{1,5},{3,7},{5,1},{7,3},{8,12},{10,14},{12... | collective-permute-start | bytes 196616 | tf_op jit(solution)/shard_map/ppermute | solution.py:389
  24.6 10.6 %collective-permute-start.2 = (bf16[1,128,256]{2,1,0:T(8,128)(2,1)}, bf16[1,128,256]{2,1,0:T(8,128)(2,1)}, u32[]{:S(2)}, u32[]{:S(2)}) collective-permute-start(bf16[1,128,256]{2,1,0:T(8,128)(2,1)} %get-tuple-element.66), channel_id=1, source_target_pairs={{0,6},{2,4},{4,2},{6,0},{1,7},{3,5},{5,3},{7,1},{8,14},{10,12},{12... | collective-permute-start | bytes 196616 | tf_op jit(solution)/shard_map/ppermute | solution.py:389
  35.2 11.1 %collective-permute-start.3 = (bf16[2,128,256]{2,1,0:T(8,128)(2,1)}, bf16[2,128,256]{2,1,0:T(8,128)(2,1)}, u32[]{:S(2)}, u32[]{:S(2)}) collective-permute-start(bf16[2,128,256]{2,1,0:T(8,128)(2,1)} %copy-done.7), channel_id=1, source_target_pairs={{0,2},{2,0},{4,6},{6,4},{1,3},{3,1},{5,7},{7,5},{8,10},{10,8},{12,... | collective-permute-start | bytes 393224 | tf_op jit(solution)/shard_map/ppermute | solution.py:389
  36.5 14.0 %collective-permute-start.4 = (bf16[2,128,256]{2,1,0:T(8,128)(2,1)}, bf16[2,128,256]{2,1,0:T(8,128)(2,1)}, u32[]{:S(2)}, u32[]{:S(2)}) collective-permute-start(bf16[2,128,256]{2,1,0:T(8,128)(2,1)} %copy-done.6), channel_id=1, source_target_pairs={{0,4},{2,6},{4,0},{6,2},{1,5},{3,7},{5,1},{7,3},{8,12},{10,14},{12... | collective-permute-start | bytes 393224 | tf_op jit(solution)/shard_map/ppermute | solution.py:389
  36.6 13.9 %collective-permute-start.5 = (bf16[2,128,256]{2,1,0:T(8,128)(2,1)}, bf16[2,128,256]{2,1,0:T(8,128)(2,1)}, u32[]{:S(2)}, u32[]{:S(2)}) collective-permute-start(bf16[2,128,256]{2,1,0:T(8,128)(2,1)} %copy-done.5), channel_id=1, source_target_pairs={{0,6},{2,4},{4,2},{6,0},{1,7},{3,5},{5,3},{7,1},{8,14},{10,12},{12... | collective-permute-start | bytes 393224 | tf_op jit(solution)/shard_map/ppermute | solution.py:389
  44.9 9.3 %collective-permute-start.8 = (bf16[1,128,256]{2,1,0:T(8,128)(2,1)}, bf16[1,128,256]{2,1,0:T(8,128)(2,1)}, u32[]{:S(2)}, u32[]{:S(2)}) collective-permute-start(bf16[1,128,256]{2,1,0:T(8,128)(2,1)} %get-tuple-element.87), channel_id=1, source_target_pairs={{0,2},{2,0},{4,6},{6,4},{1,3},{3,1},{5,7},{7,5},{8,10},{10,8},{12,... | collective-permute-start | bytes 196616 | tf_op jit(solution)/shard_map/ppermute | solution.py:389
  45.2 14.4 %collective-permute-start.9 = (bf16[1,128,256]{2,1,0:T(8,128)(2,1)}, bf16[1,128,256]{2,1,0:T(8,128)(2,1)}, u32[]{:S(2)}, u32[]{:S(2)}) collective-permute-start(bf16[1,128,256]{2,1,0:T(8,128)(2,1)} %get-tuple-element.88), channel_id=1, source_target_pairs={{0,4},{2,6},{4,0},{6,2},{1,5},{3,7},{5,1},{7,3},{8,12},{10,14},{12... | collective-permute-start | bytes 196616 | tf_op jit(solution)/shard_map/ppermute | solution.py:389
  46.3 13.4 %collective-permute-start.10 = (bf16[1,128,256]{2,1,0:T(8,128)(2,1)}, bf16[1,128,256]{2,1,0:T(8,128)(2,1)}, u32[]{:S(2)}, u32[]{:S(2)}) collective-permute-start(bf16[1,128,256]{2,1,0:T(8,128)(2,1)} %get-tuple-element.89), channel_id=1, source_target_pairs={{0,6},{2,4},{4,2},{6,0},{1,7},{3,5},{5,3},{7,1},{8,14},{10,12},{12... | collective-permute-start | bytes 196616 | tf_op jit(solution)/shard_map/ppermute | solution.py:389
  50.5 11.7 %copy-start = (bf16[1,1,256,1536]{3,2,1,0:T(8,128)(2,1)S(1)}, bf16[1,1,256,1536]{3,2,1,0:T(8,128)(2,1)}, u32[]{:S(2)}) copy-start(bf16[1,1,256,1536]{3,2,1,0:T(8,128)(2,1)} %param.7) | copy-start | bytes 2359300
  50.5 11.7 %copy-start.1 = (bf16[1,1,256,1536]{3,2,1,0:T(8,128)(2,1)S(1)}, bf16[1,1,256,1536]{3,2,1,0:T(8,128)(2,1)}, u32[]{:S(2)}) copy-start(bf16[1,1,256,1536]{3,2,1,0:T(8,128)(2,1)} %param.8) | copy-start | bytes 2359300
  50.5 11.7 %copy-start.2 = (bf16[1,1,256,1536]{3,2,1,0:T(8,128)(2,1)S(1)}, bf16[1,1,256,1536]{3,2,1,0:T(8,128)(2,1)}, u32[]{:S(2)}) copy-start(bf16[1,1,256,1536]{3,2,1,0:T(8,128)(2,1)} %param.9) | copy-start | bytes 2359300
  54.0 5.6 %collective-permute-start.11 = (f32[8,128]{1,0:T(8,128)S(1)}, f32[8,128]{1,0:T(8,128)S(1)}, u32[]{:S(2)}, u32[]{:S(2)}) collective-permute-start(f32[8,128]{1,0:T(8,128)S(1)} %get-tuple-element.84), channel_id=1, source_target_pairs={{0,8},{8,0},{16,24},{24,16},{1,9},{9,1},{17,25},{25,17},{2,10},{10... | collective-permute-start | bytes 12296 | tf_op jit(solution)/shard_map/ppermute | solution.py:389
  54.1 22.6 %collective-permute-start.6 = (bf16[2,128,256]{2,1,0:T(8,128)(2,1)S(1)}, bf16[2,128,256]{2,1,0:T(8,128)(2,1)S(1)}, u32[]{:S(2)}, u32[]{:S(2)}) collective-permute-start(bf16[2,128,256]{2,1,0:T(8,128)(2,1)S(1)} %get-tuple-element.82), channel_id=1, source_target_pairs={{0,6},{2,4},{4,2},{6,0},{1,7},{3,5},{5,3},{7,1},{8,14},{10,12},{12... | collective-permute-start | bytes 393224 | tf_op jit(solution)/shard_map/ppermute | solution.py:389
  54.2 20.7 %collective-permute-start.7 = (bf16[2,128,256]{2,1,0:T(8,128)(2,1)S(1)}, bf16[2,128,256]{2,1,0:T(8,128)(2,1)S(1)}, u32[]{:S(2)}, u32[]{:S(2)}) collective-permute-start(bf16[2,128,256]{2,1,0:T(8,128)(2,1)S(1)} %get-tuple-element.83), channel_id=1, source_target_pairs={{0,4},{2,6},{4,0},{6,2},{1,5},{3,7},{5,1},{7,3},{8,12},{10,14},{12... | collective-permute-start | bytes 393224 | tf_op jit(solution)/shard_map/ppermute | solution.py:389
  59.7 10.1 %collective-permute-start.16 = (bf16[2,128,256]{2,1,0:T(8,128)(2,1)S(1)}, bf16[2,128,256]{2,1,0:T(8,128)(2,1)S(1)}, u32[]{:S(2)}, u32[]{:S(2)}) collective-permute-start(bf16[2,128,256]{2,1,0:T(8,128)(2,1)S(1)} %get-tuple-element.95), channel_id=1, source_target_pairs={{0,2},{2,0},{4,6},{6,4},{1,3},{3,1},{5,7},{7,5},{8,10},{10,8},{12,... | collective-permute-start | bytes 393224 | tf_op jit(solution)/shard_map/ppermute | solution.py:389
  59.7 4.4 %collective-permute-start.12 = (f32[16,128]{1,0:T(8,128)S(1)}, f32[16,128]{1,0:T(8,128)S(1)}, u32[]{:S(2)}, u32[]{:S(2)}) collective-permute-start(f32[16,128]{1,0:T(8,128)S(1)} %pad_maximum_fusion.2), channel_id=1, source_target_pairs={{0,16},{8,24},{16,0},{24,8},{1,17},{9,25},{17,1},{25,9},{2,18},{10... | collective-permute-start | bytes 24584 | tf_op jit(solution)/shard_map/ppermute | solution.py:389
  64.1 8.5 %collective-permute-start.15 = (f32[32,128]{1,0:T(8,128)S(1)}, f32[32,128]{1,0:T(8,128)S(1)}, u32[]{:S(2)}, u32[]{:S(2)}) collective-permute-start(f32[32,128]{1,0:T(8,128)S(1)} %pad_maximum_fusion.1.refs_0_), channel_id=1, source_target_pairs={{0,6},{2,4},{4,2},{6,0},{1,7},{3,5},{5,3},{7,1},{8,14},{10,12},{12... | collective-permute-start | bytes 49160 | tf_op jit(solution)/shard_map/ppermute | solution.py:389
  65.7 7.0 %collective-permute-start.14 = (f32[32,128]{1,0:T(8,128)S(1)}, f32[32,128]{1,0:T(8,128)S(1)}, u32[]{:S(2)}, u32[]{:S(2)}) collective-permute-start(f32[32,128]{1,0:T(8,128)S(1)} %pad_maximum_fusion.1.refs_0_), channel_id=1, source_target_pairs={{0,4},{2,6},{4,0},{6,2},{1,5},{3,7},{5,1},{7,3},{8,12},{10,14},{12... | collective-permute-start | bytes 49160 | tf_op jit(solution)/shard_map/ppermute | solution.py:389
  69.8 3.8 %collective-permute-start.13 = (f32[32,128]{1,0:T(8,128)S(1)}, f32[32,128]{1,0:T(8,128)S(1)}, u32[]{:S(2)}, u32[]{:S(2)}) collective-permute-start(f32[32,128]{1,0:T(8,128)S(1)} %pad_maximum_fusion.1.refs_0_), channel_id=1, source_target_pairs={{0,2},{2,0},{4,6},{6,4},{1,3},{3,1},{5,7},{7,5},{8,10},{10,8},{12,... | collective-permute-start | bytes 49160 | tf_op jit(solution)/shard_map/ppermute | solution.py:389
  (2 other events, 1.3 us)

commit v7 on v5

--- a/solution.py
+++ b/solution.py
@@ -87,8 +87,8 @@
     return weights, attended
 
 
-def backward_kernel(distance, scalars, query_ref, key_ref, value_ref, weights_ref, grad_ref, *refs):
-    gq_ref, gk_ref, gq, gk, sent = refs[-5:]
+def backward_group(scalars, fields, weights_ref, grad_ref, distance, scratch, results, sent):
+    query_ref, key_ref, value_ref = fields
     score_scale = HEAD_DIM ** (-0.5)
     own = grad_ref.shape[0]
     start = partner(scalars, distance) * (own * HEAD_DIM)
@@ -102,40 +102,72 @@
         row_sum = jnp.sum(spatial_grad * weights, axis=0, keepdims=True)
         scores = weights * (spatial_grad - row_sum) * score_scale
         all_scores.append(scores.astype(jnp.bfloat16))
-    there = pl.ds(pl.multiple_of(start, HEAD_DIM), own * HEAD_DIM)
-    copies = [
-        pltpu.make_async_copy(gk, gk_ref.at[:, there], sent.at[0]),
-        pltpu.make_async_copy(gq, gq_ref.at[:, there], sent.at[1]),
-    ]
+    gq, gk = scratch
     for head, scores in enumerate(all_scores):
         cols = pl.ds(head * HEAD_DIM, HEAD_DIM)
         gk[:, cols] = dot(scores, query_ref[:, columns[head]]).astype(jnp.bfloat16)
-    copies[0].start()
-    for head, scores in enumerate(all_scores):
-        cols = pl.ds(head * HEAD_DIM, HEAD_DIM)
         gq[:, cols] = dot(key_ref[:, columns[head]].T, scores).astype(jnp.bfloat16).T
-    copies[1].start()
+    there = pl.ds(pl.multiple_of(start, HEAD_DIM), own * HEAD_DIM)
+    copies = [
+        pltpu.make_async_copy(source, target.at[:, there], sent.at[side])
+        for side, (source, target) in enumerate(zip(scratch, results))
+    ]
+    for copy in copies:
+        copy.start()
+    return copies
+
+
+def backward_kernel(distances, gains_of, scalars, *refs):
+    fields, weights_ref, refs = refs[:3], refs[3], refs[4:]
+    grad_refs, refs = refs[: len(distances)], refs[len(distances) :]
+    *refs, gq, gk, sent = refs
+    copies = []
+    if gains_of:
+        *mixed_refs, gains_ref, _, _, gq_ref, gk_ref, grad_gains_ref, grad_gains = refs
+        gain_gradients(*gains_of, scalars, mixed_refs, gains_ref, grad_gains)
+        copy = pltpu.make_async_copy(grad_gains, grad_gains_ref, sent.at[len(distances), 0])
+        copy.start()
+        copies.append(copy)
+    else:
+        gq_ref, gk_ref = refs
+    for place, (distance, grad_ref) in enumerate(zip(distances, grad_refs)):
+        copies += backward_group(
+            scalars,
+            fields,
+            weights_ref,
+            grad_ref,
+            distance,
+            (gq.at[place], gk.at[place]),
+            (gq_ref, gk_ref),
+            sent.at[place],
+        )
     for copy in copies:
         copy.wait()
 
 
-def backward(scalars, fields, weights, grads, distance, earlier):
+def backward(scalars, fields, weights, grads, distances, earlier=(), mixed=(), gains=None, gains_of=()):
     patches, feat = fields[0].shape
-    own = grads.shape[0]
+    own = grads[0].shape[0]
+    operands = [*fields, weights, *grads] + ([*mixed, gains] if gains_of else [])
+    block = pltpu.VMEM((len(distances), patches, own * HEAD_DIM), jnp.bfloat16)
+    out_shape = [jax.ShapeDtypeStruct((patches, feat), jnp.bfloat16)] * 2
+    scratch = [block, block, pltpu.SemaphoreType.DMA((len(distances) + 1, 2))]
+    if gains_of:
+        out_shape.append(jax.ShapeDtypeStruct(gains.shape, jnp.float32))
+        scratch.insert(0, pltpu.VMEM(gains.shape, jnp.float32))
     return pl.pallas_call(
-        functools.partial(backward_kernel, distance),
+        functools.partial(backward_kernel, distances, gains_of),
         in_specs=[pl.BlockSpec(memory_space=pltpu.SMEM)]
-        + [pl.BlockSpec(memory_space=pltpu.VMEM)] * 5
+        + [pl.BlockSpec(memory_space=pltpu.VMEM)] * len(operands)
         + [pl.BlockSpec(memory_space=pl.ANY)] * len(earlier),
-        out_specs=[pl.BlockSpec(memory_space=pl.ANY)] * 2,
-        scratch_shapes=[pltpu.VMEM((patches, own * HEAD_DIM), jnp.bfloat16)] * 2
-        + [pltpu.SemaphoreType.DMA((2,))],
-        out_shape=[jax.ShapeDtypeStruct((patches, feat), jnp.bfloat16)] * 2,
-        input_output_aliases={6 + index: index for index in range(len(earlier))},
+        out_specs=[pl.BlockSpec(memory_space=pl.ANY)] * len(out_shape),
+        scratch_shapes=scratch,
+        out_shape=out_shape,
+        input_output_aliases={len(operands) + 1 + index: index for index in range(len(earlier))},
         compiler_params=params(patches),
         cost_estimate=cost(2),
         name="spatial_backward",
-    )(scalars, *fields, weights, grads, *earlier)
+    )(scalars, *operands, *earlier)
 
 
 def pack_kernel(frames, spaces, field_ref, packed_ref, sent):
@@ -157,21 +189,23 @@
     devices = frames * spaces
     return pl.pallas_call(
         functools.partial(pack_kernel, frames, spaces),
-        in_specs=[pl.BlockSpec(memory_space=pl.ANY)],
-        out_specs=pl.BlockSpec(memory_space=pl.ANY),
+        in_specs=[pl.BlockSpec(memory_space=pltpu.HBM)],
+        out_specs=pl.BlockSpec(memory_space=pltpu.VMEM),
         out_shape=jax.ShapeDtypeStruct((devices, patches, feat // devices), field.dtype),
         scratch_shapes=[pltpu.SemaphoreType.DMA((devices,))],
-        compiler_params=params(0),
+        compiler_params=params(patches),
         cost_estimate=cost(1),
         name="pack_cotangent",
-    )(field)
+    )(pltpu.with_memory_space_constraint(field, pltpu.HBM))
 
 
 def turn_kernel(field_ref, turned_ref):
-    spaces, frames = turned_ref.shape[:2]
+    spaces, frames, heads = turned_ref.shape[:3]
     for space in range(spaces):
         for frame in range(frames):
-            turned_ref[space, frame, 0] = field_ref[frame * spaces + space].T
+            for head in range(heads):
+                cols = pl.ds(head * HEAD_DIM, HEAD_DIM)
+                turned_ref[space, frame, head] = field_ref[frame * spaces + space, :, cols].T
 
 
 def turn(field, frames, spaces):
@@ -179,9 +213,8 @@
     heads = feat // HEAD_DIM
     return pl.pallas_call(
         turn_kernel,
-        grid=(heads,),
-        in_specs=[pl.BlockSpec((devices, patches, HEAD_DIM), lambda i: (0, 0, i))],
-        out_specs=pl.BlockSpec((spaces, frames, 1, HEAD_DIM, patches), lambda i: (0, 0, i, 0, 0)),
+        in_specs=[pl.BlockSpec(memory_space=pltpu.VMEM)],
+        out_specs=pl.BlockSpec(memory_space=pltpu.VMEM),
         out_shape=jax.ShapeDtypeStruct((spaces, frames, heads, HEAD_DIM, patches), field.dtype),
         compiler_params=params(patches),
         cost_estimate=cost(2),
@@ -189,10 +222,8 @@
     )(field)
 
 
-def temporal_part(length, attended_ref, upstream_ref, gain_ref, grad_ref, mixed_sum, part):
-    frames, feat, _ = attended_ref.shape
-    lanes = upstream_ref.shape[-1]
-    here = pl.ds(part * lanes, lanes)
+def temporal_part(length, attended_ref, load_upstream, load_gain, grad_ref):
+    frames, feat, lanes = attended_ref.shape
     half = GROUP // 2
     score_scale = feat ** (-0.5)
     pairs = [(t, u) for t in range(frames) for u in range(t + 1)]
@@ -205,10 +236,10 @@
         return block[:half], block[half:]
 
     def load_fields(group):
-        return [split(attended_ref[t, pl.ds(group * GROUP, GROUP), here]) for t in every]
+        return [split(attended_ref[t, pl.ds(group * GROUP, GROUP), :]) for t in every]
 
     def load_ups(group):
-        return [split(upstream_ref[part, t, 0, pl.ds(group * GROUP, GROUP), :]) for t in every]
+        return [split(load_upstream(t, pl.ds(group * GROUP, GROUP))) for t in every]
 
     def total(piece):
         return jnp.broadcast_to(jnp.sum(piece, axis=0, keepdims=True), (half, lanes))
@@ -224,7 +255,7 @@
     for group in range(feat // GROUP):
         fields, ups = load_fields(group), load_ups(group)
         for side in range(2):
-            gain = gain_ref[0, pl.ds(group * GROUP + side * half, half), :]
+            gain = load_gain(pl.ds(group * GROUP + side * half, half))
             normed = [fields[t][side] * inverse[t] for t in every]
             gained = [normed[t] * gain for t in every]
             for t, u in pairs:
@@ -256,12 +287,13 @@
         for u in every
     ]
 
+    all_mixed = []
     for group in range(feat // GROUP):
         fields, ups = load_fields(group), load_ups(group)
         outs = [[] for _ in every]
         for side in range(2):
             rows = pl.ds(group * GROUP + side * half, half)
-            gain = gain_ref[0, rows, :]
+            gain = load_gain(rows)
             normed = [fields[t][side] * inverse[t] for t in every]
             mixed = jnp.zeros((half, lanes), jnp.float32)
             for u in every:
@@ -272,65 +304,61 @@
                     jnp.add, [value_part[t, u] * ups[t][side] for t in range(u, frames)]
                 )
                 outs[u].append(direct + from_norm)
-            mixed_sum[rows, :] = mixed if part == 0 else mixed_sum[rows, :] + mixed
+            all_mixed.append(mixed)
         for u in every:
-            grad_ref[u, pl.ds(group * GROUP, GROUP), here] = jnp.concatenate(
+            grad_ref[u, pl.ds(group * GROUP, GROUP), :] = jnp.concatenate(
                 outs[u], axis=0
             ).astype(jnp.bfloat16)
+    return jnp.sum(jnp.concatenate(all_mixed, axis=0).T, axis=0, keepdims=True) * 0.5
 
 
 def temporal_kernel(frames, scalars, *refs):
     attended_refs, (upstream_ref, gain_ref) = refs[:frames], refs[frames : frames + 2]
     grad_refs, mixed_ref = refs[frames + 2 : 2 * frames + 2], refs[2 * frames + 2]
-    attended, grads, mixed_sum = refs[2 * frames + 3 :]
-    head = pl.program_id(0)
-    for distance, ref in enumerate(attended_refs):
-        attended[partner(scalars, distance)] = ref[0]
-    for part in range(upstream_ref.shape[0]):
-        temporal_part(scalars[1], attended, upstream_ref, gain_ref, grads, mixed_sum, part)
-    for distance, ref in enumerate(grad_refs):
-        ref[0] = grads[partner(scalars, distance)]
-
-    @pl.when(head == 0)
-    def _():
-        mixed_ref[...] = jnp.full(mixed_ref.shape, scalars[2].astype(jnp.float32))
-
-    mixed_ref[pl.ds(head, 1), :] = jnp.sum(mixed_sum[...].T, axis=0, keepdims=True) * 0.5
+    attended, grads = refs[2 * frames + 3 :]
+    parts, _, heads, _, lanes = upstream_ref.shape
+    row_ids = lax.broadcasted_iota(jnp.int32, mixed_ref.shape, 0)
+    mixed_ref[...] = jnp.where(row_ids < heads, 0.0, scalars[2].astype(jnp.float32))
+
+    def step(index, carry):
+        head, part = index // parts, index % parts
+        here = pl.ds(pl.multiple_of(part * lanes, lanes), lanes)
+        for distance, ref in enumerate(reversed(attended_refs)):
+            attended[partner(scalars, distance)] = ref[head, :, here]
+        mixed_ref[pl.ds(head, 1), :] += temporal_part(
+            scalars[1],
+            attended,
+            lambda t, rows: upstream_ref[part, t, head, rows, :],
+            lambda rows: gain_ref[head, rows, :],
+            grads,
+        )
+        for distance, ref in enumerate(grad_refs):
+            ref[head, :, here] = grads[partner(scalars, distance)]
+        return carry
+
+    lax.fori_loop(0, heads * parts, step, 0)
 
 
 def temporal(scalars, attended, upstream, gain):
     spaces, frames, heads, feat, lanes = upstream.shape
     patches = spaces * lanes
     rows = -(-(heads + 1) // 8) * 8
-    plane = pl.BlockSpec((1, feat, patches), lambda i, sc: (i, 0, 0))
     *grads, mixed = pl.pallas_call(
         functools.partial(temporal_kernel, frames),
-        grid_spec=pltpu.PrefetchScalarGridSpec(
-            num_scalar_prefetch=1,
-            grid=(heads,),
-            in_specs=[plane] * frames
-            + [
-                pl.BlockSpec((spaces, frames, 1, feat, lanes), lambda i, sc: (0, 0, i, 0, 0)),
-                pl.BlockSpec((1, feat, lanes), lambda i, sc: (i, 0, 0)),
-            ],
-            out_specs=[plane] * frames + [pl.BlockSpec((rows, feat), lambda i, sc: (0, 0))],
-            scratch_shapes=[
-                pltpu.VMEM((frames, feat, patches), jnp.bfloat16),
-                pltpu.VMEM((frames, feat, patches), jnp.bfloat16),
-                pltpu.VMEM((feat, lanes), jnp.float32),
-            ],
-        ),
+        in_specs=[pl.BlockSpec(memory_space=pltpu.SMEM)]
+        + [pl.BlockSpec(memory_space=pltpu.VMEM)] * (frames + 2),
+        out_specs=[pl.BlockSpec(memory_space=pltpu.VMEM)] * (frames + 1),
+        scratch_shapes=[pltpu.VMEM((frames, feat, lanes), jnp.bfloat16)] * 2,
         out_shape=[jax.ShapeDtypeStruct((heads, feat, patches), jnp.bfloat16)] * frames
         + [jax.ShapeDtypeStruct((rows, feat), jnp.float32)],
         compiler_params=params(patches),
         cost_estimate=cost(4),
         name="temporal",
-    )(scalars, *attended, upstream, gain)
+    )(scalars, *reversed(attended), upstream, gain)
     return grads, mixed
 
 
-def gains_kernel(heads, frames, clips, scalars, *refs):
-    mixed_refs, gains_ref, grad_ref = refs[:-2], refs[-2], refs[-1]
+def gain_gradients(heads, frames, clips, scalars, mixed_refs, gains_ref, grad_ref):
     tasks = gains_ref.shape[1]
     rows = sum(ref.shape[0] for ref in mixed_refs) // (frames * clips)
     each = mixed_refs[0].shape[0] // rows
@@ -350,19 +378,6 @@
             grad_ref[1, :, cols] = gains_ref[0, :, cols] * mixed
 
 
-def gain_gradients(scalars, mixed, gains, heads, frames, clips):
-    return pl.pallas_call(
-        functools.partial(gains_kernel, heads, frames, clips),
-        in_specs=[pl.BlockSpec(memory_space=pltpu.SMEM)]
-        + [pl.BlockSpec(memory_space=pltpu.VMEM)] * (len(mixed) + 1),
-        out_specs=pl.BlockSpec(memory_space=pltpu.VMEM),
-        out_shape=jax.ShapeDtypeStruct(gains.shape, jnp.float32),
-        compiler_params=params(0),
-        cost_estimate=cost(1),
-        name="gain_gradients",
-    )(scalars, *mixed, gains)
-
-
 def swap(field, axis, size, distance):
     return lax.ppermute(field, axis, [(i, i ^ distance) for i in range(size)])
 
@@ -385,9 +400,8 @@
     queries, _ = lax.optimization_barrier((queries, packed))
     fields = (queries, key_rows, values)
     weights, attended = forward(scalars, *fields, frames)
-    attended = [attended[0]] + [
-        swap(attended[distance], "tm", frames, distance) for distance in range(1, frames)
-    ]
+    for distance in reversed(range(1, frames)):
+        attended[distance] = swap(attended[distance], "tm", frames, distance)
     incoming, _ = lax.optimization_barrier((incoming, weights))
     upstream = turn(incoming, frames, spaces)
     rows = lax.dynamic_index_in_dim(gains, task_ids[0], 1, keepdims=False)
@@ -396,28 +410,28 @@
         product.reshape(own, HEAD_DIM, 1), (own, HEAD_DIM, patches // spaces)
     )
     grads, mixed = temporal(scalars, attended, upstream, gain)
-    grads = [grads[0]] + [
-        swap(grads[distance], "tm", frames, distance) for distance in range(1, frames)
-    ]
+    for distance in reversed(range(1, frames)):
+        grads[distance] = swap(grads[distance], "tm", frames, distance)
     here = grads[0]
     for bit in range(clips.bit_length() - 1):
         other = swap(mixed, "dp", clips, 1 << bit)
         if bit == 0:
             here, other = lax.optimization_barrier((here, other))
         mixed = jnp.concatenate([mixed, other], axis=0)
-    results = backward(scalars, fields, weights, here, 0, ())
+    results = backward(scalars, fields, weights, [here], [0])
     mixed, results = lax.optimization_barrier((mixed, results))
     mixed = [mixed] + [swap(mixed, "tm", frames, distance) for distance in range(1, frames)]
-    distance = 1
-    if frames > 2:
-        results = backward(scalars, fields, weights, grads[1], 1, results)
-        mixed, results = lax.optimization_barrier((mixed, results))
-        distance = 2
-    grad_gains = gain_gradients(scalars, mixed, gains, own, frames, clips)
-    grad_gains, results = lax.optimization_barrier((grad_gains, results))
-    for distance in range(distance, frames):
-        results = backward(scalars, fields, weights, grads[distance], distance, results)
-    grad_queries, grad_keys = results
+    grad_queries, grad_keys, grad_gains = backward(
+        scalars,
+        fields,
+        weights,
+        grads[:0:-1],
+        list(range(frames - 1, 0, -1)),
+        results,
+        mixed,
+        gains,
+        (own, frames, clips),
+    )
     return (
         grad_queries.reshape(query_heads.shape),
         grad_keys.reshape(query_heads.shape),
@@ -505,7 +519,7 @@
         tiled=True,
     )
     head_grads = jnp.transpose(returned.reshape(patches, heads, HEAD_DIM), (1, 2, 0))
-    grad_queries, grad_keys = backward(scalars, fields, weights, head_grads, 0, ())
+    grad_queries, grad_keys = backward(scalars, fields, weights, [head_grads], [0])
     return (
         grad_queries.reshape(query_heads.shape),
         grad_keys.reshape(query_heads.shape),

time: 77.5 us -> 76.9 us (level)
  waiting for transfers between devices: 25.8 us -> 33.8 us
  Pallas kernels: 23.6 us -> 19.8 us
  starting transfers between devices: 24.3 us -> 20.7 us
  local copies, waits for them, and re-layouts: 1.25 us -> 0.12 us
    ppermute x11, waiting for transfers between devices: 8.77 us -> 16.7 us  [swap(): return lax.ppermute(field, axis, [(i, i ^ distance) for i in range(size)])]
    pallas_call x7 -> x4, Pallas kernels: 15.6 us -> 10.6 us  [the longest x2 4.94 us: backward(): pl.pallas_call(functools.partial(backward_kernel, distances, gains_of), i...]
    ppermute x11, starting transfers between devices: 17 us -> 13.4 us  [swap(): return lax.ppermute(field, axis, [(i, i ^ distance) for i in range(size)])]
    pallas_call x1, Pallas kernels: 0.93 us -> 2.2 us  [pack(): pl.pallas_call(functools.partial(pack_kernel, frames, spaces), in_specs=[...]
    unnamed x10 -> x8, local copies, waits for them, and re-layouts: 1.14 us -> 0.02 us
  transfers between devices with their start and end apart: 12 -> 12, of which waited for: 5 -> 5; matrix products, arithmetic and copies ran while one was open for 0% -> 0% of each run, Pallas kernels for 21% -> 14%
where the time goes in v7:
time: 76.9 us; the launch traced here: 76.6 us
  waiting for transfers between devices  33.8 us (44%)
  starting transfers between devices  20.7 us (27%)
  Pallas kernels  19.8 us (26%)
  between operations  2.01 us (3%)
    all_to_all x1, waiting for transfers between devices, split_by_heads(): lax.all_to_all(packed, ('tm', 'space'), split_axis=0, concat_axis=0, tile...  17.1 us
    ppermute x11, waiting for transfers between devices, swap(): return lax.ppermute(field, axis, [(i, i ^ distance) for i in range(size)])  16.7 us
    ppermute x11, starting transfers between devices, swap(): return lax.ppermute(field, axis, [(i, i ^ distance) for i in range(size)])  13.4 us
    all_to_all x1, starting transfers between devices, split_by_heads(): lax.all_to_all(packed, ('tm', 'space'), split_axis=0, concat_axis=0, tile...  7.29 us
    pallas_call x1, Pallas kernels, forward(): pl.pallas_call(forward_kernel, in_specs=[pl.BlockSpec(memory_space=pltpu....  7.07 us
    pallas_call x2, Pallas kernels, backward(): pl.pallas_call(functools.partial(backward_kernel, distances, gains_of), i...  4.94 us
    pallas_call x1, Pallas kernels, temporal(): pl.pallas_call(functools.partial(temporal_kernel, frames), in_specs=[pl.B...  4.1 us
    pallas_call x1, Pallas kernels, pack(): pl.pallas_call(functools.partial(pack_kernel, frames, spaces), in_specs=[...  2.2 us
  transfers between devices with their start and end apart: 12, of which 5 were waited for; matrix products, arithmetic and copies ran while one was open for 0% of the time, Pallas kernels for 14%

profile of v7, /device:TPU:0, one launch (start us, length us, event | category | flops | bytes accessed | tf_op | source)
XLA Modules:
  0.0 76.6 jit_solution(11534229058006371627)
XLA Ops:
  0.6 2.2 %pack_cotangent.1 = bf16[8,128,384]{2,1,0:T(8,128)(2,1)} custom-call(bf16[128,3072]{1,0:T(8,128)(2,1)} %bitcast.21), custom_call_target="tpu_custom_call" | custom-call | flops 100000000 | tf_op jit(solution)/shard_map/pack_cotangent/pallas_call | solution.py:190
  2.8 7.3 %all-to-all-start = ((bf16[8,128,384]{2,1,0:T(8,128)(2,1)}), bf16[8,128,384]{2,1,0:T(8,128)(2,1)}, u32[]{:S(2)}, u32[]{:S(2)}) async-start(bf16[8,128,384]{2,1,0:T(8,128)(2,1)} %pack_cotangent.1), calls=%async_computation | async-start | bytes 1572864 | tf_op jit(solution)/shard_map/all_to_all | solution.py:399
  11.4 0.1 pad_add_fusion.scalars
  11.5 7.1 %spatial_forward.1 = (f32[12,256,256]{2,1,0:T(8,128)S(1)}, bf16[3,128,256]{2,1,0:T(8,128)(2,1)S(1)}, bf16[3,128,256]{2,1,0:T(8,128)(2,1)}, bf16[3,128,256]{2,1,0:T(8,128)(2,1)}, bf16[3,128,256]{2,1,0:T(8,128)(2,1)}) custom-call(s32[3]{0:T(128)S(1)} %pad_add_fusion.scalars, bf16[256,1536]{1,0:T(8,128)(2,1)} %bitcast.12, bf16[256,1536]{1,0:T(8,128)(2,1)} %bitcast.15, ...), custom_call_target="tpu_custom_call" | custom-call | flops 600000000 | tf_op jit(solution)/shard_map/spatial_forward/pallas_call | solution.py:74
  18.6 3.9 %collective-permute-start = (bf16[3,128,256]{2,1,0:T(8,128)(2,1)}, bf16[3,128,256]{2,1,0:T(8,128)(2,1)}, u32[]{:S(2)}, u32[]{:S(2)}) collective-permute-start(bf16[3,128,256]{2,1,0:T(8,128)(2,1)} %get-tuple-element.27), channel_id=1, source_target_pairs={{0,6},{2,4},{4,2},{6,0},{1,7},{3,5},{5,3},{7,1},{8,14},{10,12},{12... | collective-permute-start | bytes 589832 | tf_op jit(solution)/shard_map/ppermute | solution.py:382
  22.5 0.6 collective-permute-start.2
  23.1 0.1 fusion
  23.2 17.1 %all-to-all-done.field_ref = bf16[8,128,384]{2,1,0:T(8,128)(2,1)} async-done(((bf16[8,128,384]{2,1,0:T(8,128)(2,1)}), bf16[8,128,384]{2,1,0:T(8,128)(2,1)}, u32[]{:S(2)}, u32[]{:S(2)}) %all-to-all-start) | async-done | bytes 786464 | tf_op jit(solution)/shard_map/all_to_all | solution.py:399
  40.3 1.5 %turn_cotangent.1.refs_4_ = bf16[2,4,3,128,128]{4,3,2,1,0:T(8,128)(2,1)S(1)} custom-call(bf16[8,128,384]{2,1,0:T(8,128)(2,1)} %all-to-all-done.field_ref), custom_call_target="tpu_custom_call" | custom-call | flops 200000000 | tf_op jit(solution)/shard_map/turn_cotangent/pallas_call | solution.py:214
  41.8 5.5 %collective-permute-done.1.refs_1_ = bf16[3,128,256]{2,1,0:T(8,128)(2,1)} collective-permute-done((bf16[3,128,256]{2,1,0:T(8,128)(2,1)}, bf16[3,128,256]{2,1,0:T(8,128)(2,1)}, u32[]{:S(2)}, u32[]{:S(2)}) %collective-permute-start.1) | collective-permute-done | bytes 196640 | tf_op jit(solution)/shard_map/ppermute | solution.py:382
  47.3 0.1 broadcast_in_dim.8.refs_5_
  47.4 4.1 %temporal.1 = (bf16[3,128,256]{2,1,0:T(8,128)(2,1)S(1)}, bf16[3,128,256]{2,1,0:T(8,128)(2,1)S(1)}, bf16[3,128,256]{2,1,0:T(8,128)(2,1)S(1)}, bf16[3,128,256]{2,1,0:T(8,128)(2,1)S(1)}, f32[8,128]{1,0:T(8,128)S(1)}) custom-call(s32[3]{0:T(128)S(1)} %pad_add_fusion.scalars, bf16[3,128,256]{2,1,0:T(8,128)(2,1)} %collective-permute-done.refs_0_, ...), custom_call_target="tpu_custom_call" | custom-call | flops 400000000 | tf_op jit(solution)/shard_map/temporal/pallas_call | solution.py:346
  51.5 0.1 collective-permute-start.6
  51.6 1.2 %collective-permute-start.3 = (bf16[3,128,256]{2,1,0:T(8,128)(2,1)S(1)}, bf16[3,128,256]{2,1,0:T(8,128)(2,1)S(1)}, u32[]{:S(2)}, u32[]{:S(2)}) collective-permute-start(bf16[3,128,256]{2,1,0:T(8,128)(2,1)S(1)} %get-tuple-element.32), channel_id=1, source_target_pairs={{0,6},{2,4},{4,2},{6,0},{1,7},{3,5},{5,3},{7,1},{8,14},{10,12},{12... | collective-permute-start | bytes 589832 | tf_op jit(solution)/shard_map/ppermute | solution.py:382
  52.8 3.3 %collective-permute-start.5 = (bf16[3,128,256]{2,1,0:T(8,128)(2,1)S(1)}, bf16[3,128,256]{2,1,0:T(8,128)(2,1)S(1)}, u32[]{:S(2)}, u32[]{:S(2)}) collective-permute-start(bf16[3,128,256]{2,1,0:T(8,128)(2,1)S(1)} %get-tuple-element.34), channel_id=1, source_target_pairs={{0,2},{2,0},{4,6},{6,4},{1,3},{3,1},{5,7},{7,5},{8,10},{10,8},{12,... | collective-permute-start | bytes 589832 | tf_op jit(solution)/shard_map/ppermute | solution.py:382
  56.1 1.5 %collective-permute-start.7 = (f32[16,128]{1,0:T(8,128)S(1)}, f32[16,128]{1,0:T(8,128)S(1)}, u32[]{:S(2)}, u32[]{:S(2)}) collective-permute-start(f32[16,128]{1,0:T(8,128)S(1)} %pad_maximum_fusion.1), channel_id=1, source_target_pairs={{0,16},{8,24},{16,0},{24,8},{1,17},{9,25},{17,1},{25,9},{2,18},{10... | collective-permute-start | bytes 24584 | tf_op jit(solution)/shard_map/ppermute | solution.py:382
  57.6 1.9 %spatial_backward.2 = (bf16[256,1536]{1,0:T(8,128)(2,1)}, bf16[256,1536]{1,0:T(8,128)(2,1)}) custom-call(s32[3]{0:T(128)S(1)} %pad_add_fusion.scalars, bf16[256,1536]{1,0:T(8,128)(2,1)S(1)} %bitcast.13, bf16[256,1536]{1,0:T(8,128)(2,1)S(1)} %bitcast.16, bf16[256,1536]{1,0:T(8,128)(2,1)S(1)} %bitcast.19, f32[12,256,256]{2,1,0:T(8,128)S(1)} %get-tuple-element.26.refs_3_, ...), custom_call_target="tpu_custom_call" | custom-call | flops 200000000 | tf_op jit(solution)/shard_map/spatial_backward/pallas_call | solution.py:158
  59.5 0.2 collective-permute-done.7
  59.7 1.1 %collective-permute-start.10 = (f32[32,128]{1,0:T(8,128)S(1)}, f32[32,128]{1,0:T(8,128)S(1)}, u32[]{:S(2)}, u32[]{:S(2)}) collective-permute-start(f32[32,128]{1,0:T(8,128)S(1)} %pad_maximum_fusion.refs_7_), channel_id=1, source_target_pairs={{0,6},{2,4},{4,2},{6,0},{1,7},{3,5},{5,3},{7,1},{8,14},{10,12},{12... | collective-permute-start | bytes 49160 | tf_op jit(solution)/shard_map/ppermute | solution.py:382
  60.8 0.4 collective-permute-start.9
  61.3 8.6 %collective-permute-done.10.refs_10_ = f32[32,128]{1,0:T(8,128)S(1)} collective-permute-done((f32[32,128]{1,0:T(8,128)S(1)}, f32[32,128]{1,0:T(8,128)S(1)}, u32[]{:S(2)}, u32[]{:S(2)}) %collective-permute-start.10) | collective-permute-done | bytes 16416 | tf_op jit(solution)/shard_map/ppermute | solution.py:382
  69.9 1.3 %collective-permute-start.8 = (f32[32,128]{1,0:T(8,128)S(1)}, f32[32,128]{1,0:T(8,128)S(1)}, u32[]{:S(2)}, u32[]{:S(2)}) collective-permute-start(f32[32,128]{1,0:T(8,128)S(1)} %pad_maximum_fusion.refs_7_), channel_id=1, source_target_pairs={{0,2},{2,0},{4,6},{6,4},{1,3},{3,1},{5,7},{7,5},{8,10},{10,8},{12,... | collective-permute-start | bytes 49160 | tf_op jit(solution)/shard_map/ppermute | solution.py:382
  71.2 2.4 %collective-permute-done.8.refs_8_ = f32[32,128]{1,0:T(8,128)S(1)} collective-permute-done((f32[32,128]{1,0:T(8,128)S(1)}, f32[32,128]{1,0:T(8,128)S(1)}, u32[]{:S(2)}, u32[]{:S(2)}) %collective-permute-start.8) | collective-permute-done | bytes 16416 | tf_op jit(solution)/shard_map/ppermute | solution.py:382
  73.6 3.0 %spatial_backward.3 = (bf16[256,1536]{1,0:T(8,128)(2,1)}, bf16[256,1536]{1,0:T(8,128)(2,1)}, f32[2,16,1536]{2,1,0:T(8,128)}) custom-call(s32[3]{0:T(128)S(1)} %pad_add_fusion.scalars, bf16[256,1536]{1,0:T(8,128)(2,1)S(1)} %bitcast.14, bf16[256,1536]{1,0:T(8,128)(2,1)S(1)} %bitcast.17, ...), custom_call_target="tpu_custom_call", output_to_operand_aliasing={{0}: (13, {}), {1}: (14, {})} | custom-call | flops 200000000 | tf_op jit(solution)/shard_map/spatial_backward/pallas_call | solution.py:158
  (19 shorter events, 0.0 us)
Async XLA Ops:
  0.6 22.5 %copy-start.3 = (f32[2,16,1536]{2,1,0:T(8,128)S(1)}, f32[2,16,1536]{2,1,0:T(8,128)}, u32[]{:S(2)}) copy-start(f32[2,16,1536]{2,1,0:T(8,128)} %refs_11_.1) | copy-start | bytes 589828
  2.8 37.4 %all-to-all-start = ((bf16[8,128,384]{2,1,0:T(8,128)(2,1)}), bf16[8,128,384]{2,1,0:T(8,128)(2,1)}, u32[]{:S(2)}, u32[]{:S(2)}) async-start(bf16[8,128,384]{2,1,0:T(8,128)(2,1)} %pack_cotangent.1), calls=%async_computation | async-start | bytes 1572864 | tf_op jit(solution)/shard_map/all_to_all | solution.py:399
  18.6 23.2 %collective-permute-start = (bf16[3,128,256]{2,1,0:T(8,128)(2,1)}, bf16[3,128,256]{2,1,0:T(8,128)(2,1)}, u32[]{:S(2)}, u32[]{:S(2)}) collective-permute-start(bf16[3,128,256]{2,1,0:T(8,128)(2,1)} %get-tuple-element.27), channel_id=1, source_target_pairs={{0,6},{2,4},{4,2},{6,0},{1,7},{3,5},{5,3},{7,1},{8,14},{10,12},{12... | collective-permute-start | bytes 589832 | tf_op jit(solution)/shard_map/ppermute | solution.py:382
  22.5 24.8 %collective-permute-start.1 = (bf16[3,128,256]{2,1,0:T(8,128)(2,1)}, bf16[3,128,256]{2,1,0:T(8,128)(2,1)}, u32[]{:S(2)}, u32[]{:S(2)}) collective-permute-start(bf16[3,128,256]{2,1,0:T(8,128)(2,1)} %get-tuple-element.28), channel_id=1, source_target_pairs={{0,4},{2,6},{4,0},{6,2},{1,5},{3,7},{5,1},{7,3},{8,12},{10,14},{12... | collective-permute-start | bytes 589832 | tf_op jit(solution)/shard_map/ppermute | solution.py:382
  22.5 24.8 %collective-permute-start.2 = (bf16[3,128,256]{2,1,0:T(8,128)(2,1)}, bf16[3,128,256]{2,1,0:T(8,128)(2,1)}, u32[]{:S(2)}, u32[]{:S(2)}) collective-permute-start(bf16[3,128,256]{2,1,0:T(8,128)(2,1)} %get-tuple-element.29), channel_id=1, source_target_pairs={{0,2},{2,0},{4,6},{6,4},{1,3},{3,1},{5,7},{7,5},{8,10},{10,8},{12,... | collective-permute-start | bytes 589832 | tf_op jit(solution)/shard_map/ppermute | solution.py:382
  40.3 17.3 %copy-start = (bf16[1,1,256,1536]{3,2,1,0:T(8,128)(2,1)S(1)}, bf16[1,1,256,1536]{3,2,1,0:T(8,128)(2,1)}, u32[]{:S(2)}) copy-start(bf16[1,1,256,1536]{3,2,1,0:T(8,128)(2,1)} %param.7) | copy-start | bytes 2359300
  40.3 17.3 %copy-start.1 = (bf16[1,1,256,1536]{3,2,1,0:T(8,128)(2,1)S(1)}, bf16[1,1,256,1536]{3,2,1,0:T(8,128)(2,1)}, u32[]{:S(2)}) copy-start(bf16[1,1,256,1536]{3,2,1,0:T(8,128)(2,1)} %param.8) | copy-start | bytes 2359300
  40.3 17.3 %copy-start.2 = (bf16[1,1,256,1536]{3,2,1,0:T(8,128)(2,1)S(1)}, bf16[1,1,256,1536]{3,2,1,0:T(8,128)(2,1)}, u32[]{:S(2)}) copy-start(bf16[1,1,256,1536]{3,2,1,0:T(8,128)(2,1)} %param.9) | copy-start | bytes 2359300
  51.5 4.5 %collective-permute-start.6 = (f32[8,128]{1,0:T(8,128)S(1)}, f32[8,128]{1,0:T(8,128)S(1)}, u32[]{:S(2)}, u32[]{:S(2)}) collective-permute-start(f32[8,128]{1,0:T(8,128)S(1)} %get-tuple-element.35), channel_id=1, source_target_pairs={{0,8},{8,0},{16,24},{24,16},{1,9},{9,1},{17,25},{25,17},{2,10},{10... | collective-permute-start | bytes 12296 | tf_op jit(solution)/shard_map/ppermute | solution.py:382
  51.6 22.0 %collective-permute-start.3 = (bf16[3,128,256]{2,1,0:T(8,128)(2,1)S(1)}, bf16[3,128,256]{2,1,0:T(8,128)(2,1)S(1)}, u32[]{:S(2)}, u32[]{:S(2)}) collective-permute-start(bf16[3,128,256]{2,1,0:T(8,128)(2,1)S(1)} %get-tuple-element.32), channel_id=1, source_target_pairs={{0,6},{2,4},{4,2},{6,0},{1,7},{3,5},{5,3},{7,1},{8,14},{10,12},{12... | collective-permute-start | bytes 589832 | tf_op jit(solution)/shard_map/ppermute | solution.py:382
  52.8 20.8 %collective-permute-start.4 = (bf16[3,128,256]{2,1,0:T(8,128)(2,1)S(1)}, bf16[3,128,256]{2,1,0:T(8,128)(2,1)S(1)}, u32[]{:S(2)}, u32[]{:S(2)}) collective-permute-start(bf16[3,128,256]{2,1,0:T(8,128)(2,1)S(1)} %get-tuple-element.33), channel_id=1, source_target_pairs={{0,4},{2,6},{4,0},{6,2},{1,5},{3,7},{5,1},{7,3},{8,12},{10,14},{12... | collective-permute-start | bytes 589832 | tf_op jit(solution)/shard_map/ppermute | solution.py:382
  52.8 20.8 %collective-permute-start.5 = (bf16[3,128,256]{2,1,0:T(8,128)(2,1)S(1)}, bf16[3,128,256]{2,1,0:T(8,128)(2,1)S(1)}, u32[]{:S(2)}, u32[]{:S(2)}) collective-permute-start(bf16[3,128,256]{2,1,0:T(8,128)(2,1)S(1)} %get-tuple-element.34), channel_id=1, source_target_pairs={{0,2},{2,0},{4,6},{6,4},{1,3},{3,1},{5,7},{7,5},{8,10},{10,8},{12,... | collective-permute-start | bytes 589832 | tf_op jit(solution)/shard_map/ppermute | solution.py:382
  56.1 3.7 %collective-permute-start.7 = (f32[16,128]{1,0:T(8,128)S(1)}, f32[16,128]{1,0:T(8,128)S(1)}, u32[]{:S(2)}, u32[]{:S(2)}) collective-permute-start(f32[16,128]{1,0:T(8,128)S(1)} %pad_maximum_fusion.1), channel_id=1, source_target_pairs={{0,16},{8,24},{16,0},{24,8},{1,17},{9,25},{17,1},{25,9},{2,18},{10... | collective-permute-start | bytes 24584 | tf_op jit(solution)/shard_map/ppermute | solution.py:382
  59.7 10.1 %collective-permute-start.10 = (f32[32,128]{1,0:T(8,128)S(1)}, f32[32,128]{1,0:T(8,128)S(1)}, u32[]{:S(2)}, u32[]{:S(2)}) collective-permute-start(f32[32,128]{1,0:T(8,128)S(1)} %pad_maximum_fusion.refs_7_), channel_id=1, source_target_pairs={{0,6},{2,4},{4,2},{6,0},{1,7},{3,5},{5,3},{7,1},{8,14},{10,12},{12... | collective-permute-start | bytes 49160 | tf_op jit(solution)/shard_map/ppermute | solution.py:382
  60.8 10.4 %collective-permute-start.9 = (f32[32,128]{1,0:T(8,128)S(1)}, f32[32,128]{1,0:T(8,128)S(1)}, u32[]{:S(2)}, u32[]{:S(2)}) collective-permute-start(f32[32,128]{1,0:T(8,128)S(1)} %pad_maximum_fusion.refs_7_), channel_id=1, source_target_pairs={{0,4},{2,6},{4,0},{6,2},{1,5},{3,7},{5,1},{7,3},{8,12},{10,14},{12... | collective-permute-start | bytes 49160 | tf_op jit(solution)/shard_map/ppermute | solution.py:382
  69.9 3.7 %collective-permute-start.8 = (f32[32,128]{1,0:T(8,128)S(1)}, f32[32,128]{1,0:T(8,128)S(1)}, u32[]{:S(2)}, u32[]{:S(2)}) collective-permute-start(f32[32,128]{1,0:T(8,128)S(1)} %pad_maximum_fusion.refs_7_), channel_id=1, source_target_pairs={{0,2},{2,0},{4,6},{6,4},{1,3},{3,1},{5,7},{7,5},{8,10},{10,8},{12,... | collective-permute-start | bytes 49160 | tf_op jit(solution)/shard_map/ppermute | solution.py:382

commit v8 on v7

--- a/solution.py
+++ b/solution.py
@@ -170,29 +170,40 @@
     )(scalars, *operands, *earlier)
 
 
-def pack_kernel(frames, spaces, field_ref, packed_ref, sent):
+def pack_kernel(frames, spaces, field_ref, packed_ref, rows, arrived):
+    chunks, size, _ = rows.shape
     width = packed_ref.shape[2]
-    copies = []
-    for frame in range(frames):
-        for space in range(spaces):
-            index = frame * spaces + space
-            cols = pl.ds((space * frames + frame) * width, width)
-            copy = pltpu.make_async_copy(field_ref.at[:, cols], packed_ref.at[index], sent.at[index])
-            copy.start()
-            copies.append(copy)
+    copies = [
+        pltpu.make_async_copy(
+            field_ref.at[pl.ds(chunk * size, size), :], rows.at[chunk], arrived.at[chunk]
+        )
+        for chunk in range(chunks)
+    ]
     for copy in copies:
+        copy.start()
+    for chunk, copy in enumerate(copies):
         copy.wait()
+        for frame in range(frames):
+            for space in range(spaces):
+                cols = pl.ds((space * frames + frame) * width, width)
+                packed_ref[frame * spaces + space, pl.ds(chunk * size, size), :] = rows[
+                    chunk, :, cols
+                ]
 
 
 def pack(field, frames, spaces):
     patches, feat = field.shape
     devices = frames * spaces
+    chunks = patches // GROUP
     return pl.pallas_call(
         functools.partial(pack_kernel, frames, spaces),
         in_specs=[pl.BlockSpec(memory_space=pltpu.HBM)],
         out_specs=pl.BlockSpec(memory_space=pltpu.VMEM),
         out_shape=jax.ShapeDtypeStruct((devices, patches, feat // devices), field.dtype),
-        scratch_shapes=[pltpu.SemaphoreType.DMA((devices,))],
+        scratch_shapes=[
+            pltpu.VMEM((chunks, patches // chunks, feat), field.dtype),
+            pltpu.SemaphoreType.DMA((chunks,)),
+        ],
         compiler_params=params(patches),
         cost_estimate=cost(1),
         name="pack_cotangent",
@@ -309,7 +320,7 @@
             grad_ref[u, pl.ds(group * GROUP, GROUP), :] = jnp.concatenate(
                 outs[u], axis=0
             ).astype(jnp.bfloat16)
-    return jnp.sum(jnp.concatenate(all_mixed, axis=0).T, axis=0, keepdims=True) * 0.5
+    return jnp.concatenate(all_mixed, axis=0)
 
 
 def temporal_kernel(frames, scalars, *refs):
@@ -317,26 +328,32 @@
     grad_refs, mixed_ref = refs[frames + 2 : 2 * frames + 2], refs[2 * frames + 2]
     attended, grads = refs[2 * frames + 3 :]
     parts, _, heads, _, lanes = upstream_ref.shape
-    row_ids = lax.broadcasted_iota(jnp.int32, mixed_ref.shape, 0)
-    mixed_ref[...] = jnp.where(row_ids < heads, 0.0, scalars[2].astype(jnp.float32))
-
-    def step(index, carry):
-        head, part = index // parts, index % parts
-        here = pl.ds(pl.multiple_of(part * lanes, lanes), lanes)
-        for distance, ref in enumerate(reversed(attended_refs)):
-            attended[partner(scalars, distance)] = ref[head, :, here]
-        mixed_ref[pl.ds(head, 1), :] += temporal_part(
-            scalars[1],
-            attended,
-            lambda t, rows: upstream_ref[part, t, head, rows, :],
-            lambda rows: gain_ref[head, rows, :],
-            grads,
-        )
+    mixed_ref[...] = jnp.full(mixed_ref.shape, scalars[2].astype(jnp.float32))
+
+    def step(head, carry):
+        for distance, ref in enumerate(attended_refs):
+            frame = partner(scalars, distance)
+            for part in range(parts):
+                attended[part, frame] = ref[head, :, pl.ds(part * lanes, lanes)]
+        mixed = [
+            temporal_part(
+                scalars[1],
+                attended.at[part],
+                lambda t, rows: upstream_ref[part, t, head, rows, :],
+                lambda rows: gain_ref[head, rows, :],
+                grads.at[part],
+            )
+            for part in range(parts)
+        ]
+        summed = functools.reduce(jnp.add, mixed)
+        mixed_ref[pl.ds(head, 1), :] = jnp.sum(summed.T, axis=0, keepdims=True) * 0.5
         for distance, ref in enumerate(grad_refs):
-            ref[head, :, here] = grads[partner(scalars, distance)]
+            frame = partner(scalars, distance)
+            for part in range(parts):
+                ref[head, :, pl.ds(part * lanes, lanes)] = grads[part, frame]
         return carry
 
-    lax.fori_loop(0, heads * parts, step, 0)
+    lax.fori_loop(0, heads, step, 0)
 
 
 def temporal(scalars, attended, upstream, gain):
@@ -348,13 +365,13 @@
         in_specs=[pl.BlockSpec(memory_space=pltpu.SMEM)]
         + [pl.BlockSpec(memory_space=pltpu.VMEM)] * (frames + 2),
         out_specs=[pl.BlockSpec(memory_space=pltpu.VMEM)] * (frames + 1),
-        scratch_shapes=[pltpu.VMEM((frames, feat, lanes), jnp.bfloat16)] * 2,
+        scratch_shapes=[pltpu.VMEM((spaces, frames, feat, lanes), jnp.bfloat16)] * 2,
         out_shape=[jax.ShapeDtypeStruct((heads, feat, patches), jnp.bfloat16)] * frames
         + [jax.ShapeDtypeStruct((rows, feat), jnp.float32)],
         compiler_params=params(patches),
         cost_estimate=cost(4),
         name="temporal",
-    )(scalars, *reversed(attended), upstream, gain)
+    )(scalars, *attended, upstream, gain)
     return grads, mixed
 
 
@@ -420,7 +437,10 @@
         mixed = jnp.concatenate([mixed, other], axis=0)
     results = backward(scalars, fields, weights, [here], [0])
     mixed, results = lax.optimization_barrier((mixed, results))
-    mixed = [mixed] + [swap(mixed, "tm", frames, distance) for distance in range(1, frames)]
+    near, grads[1] = lax.optimization_barrier((mixed, grads[1]))
+    mixed = [mixed, swap(near, "tm", frames, 1)] + [
+        swap(mixed, "tm", frames, distance) for distance in range(2, frames)
+    ]
     grad_queries, grad_keys, grad_gains = backward(
         scalars,
         fields,

time: 76.9 us -> 75 us (0.975)
  waiting for transfers between devices: 33.8 us -> 28.5 us
  starting transfers between devices: 20.7 us -> 24.3 us
    ppermute x11, waiting for transfers between devices: 16.7 us -> 11.5 us  [swap(): return lax.ppermute(field, axis, [(i, i ^ distance) for i in range(size)])]
    ppermute x11, starting transfers between devices: 13.4 us -> 17 us  [swap(): return lax.ppermute(field, axis, [(i, i ^ distance) for i in range(size)])]
  transfers between devices with their start and end apart: 12 -> 12, of which waited for: 5 -> 6; matrix products, arithmetic and copies ran while one was open for 0% -> 0% of each run, Pallas kernels for 14% -> 14%
where the time goes in v8:
time: 75 us; the launch traced here: 74.8 us
  waiting for transfers between devices  28.5 us (38%)
  starting transfers between devices  24.3 us (32%)
  Pallas kernels  19.7 us (26%)
  between operations  2.02 us (3%)
    all_to_all x1, waiting for transfers between devices, split_by_heads(): lax.all_to_all(packed, ('tm', 'space'), split_axis=0, concat_axis=0, tile...  17 us
    ppermute x11, starting transfers between devices, swap(): return lax.ppermute(field, axis, [(i, i ^ distance) for i in range(size)])  17 us
    ppermute x11, waiting for transfers between devices, swap(): return lax.ppermute(field, axis, [(i, i ^ distance) for i in range(size)])  11.5 us
    all_to_all x1, starting transfers between devices, split_by_heads(): lax.all_to_all(packed, ('tm', 'space'), split_axis=0, concat_axis=0, tile...  7.29 us
    pallas_call x1, Pallas kernels, forward(): pl.pallas_call(forward_kernel, in_specs=[pl.BlockSpec(memory_space=pltpu....  7.07 us
    pallas_call x2, Pallas kernels, backward(): pl.pallas_call(functools.partial(backward_kernel, distances, gains_of), i...  4.94 us
    pallas_call x1, Pallas kernels, temporal(): pl.pallas_call(functools.partial(temporal_kernel, frames), in_specs=[pl.B...  3.94 us
    pallas_call x1, Pallas kernels, pack(): pl.pallas_call(functools.partial(pack_kernel, frames, spaces), in_specs=[...  2.2 us
  transfers between devices with their start and end apart: 12, of which 6 were waited for; matrix products, arithmetic and copies ran while one was open for 0% of the time, Pallas kernels for 14%

profile of v8, /device:TPU:0, one launch (start us, length us, event | category | flops | bytes accessed | tf_op | source)
XLA Modules:
  0.0 74.8 jit_solution(4637029802013581040)
XLA Ops:
  0.6 2.2 %pack_cotangent.1 = bf16[8,128,384]{2,1,0:T(8,128)(2,1)} custom-call(bf16[128,3072]{1,0:T(8,128)(2,1)} %bitcast.21), custom_call_target="tpu_custom_call" | custom-call | flops 100000000 | tf_op jit(solution)/shard_map/pack_cotangent/pallas_call | solution.py:198
  2.8 7.3 %all-to-all-start = ((bf16[8,128,384]{2,1,0:T(8,128)(2,1)}), bf16[8,128,384]{2,1,0:T(8,128)(2,1)}, u32[]{:S(2)}, u32[]{:S(2)}) async-start(bf16[8,128,384]{2,1,0:T(8,128)(2,1)} %pack_cotangent.1), calls=%async_computation | async-start | bytes 1572864 | tf_op jit(solution)/shard_map/all_to_all | solution.py:416
  11.5 7.1 %spatial_forward.1 = (f32[12,256,256]{2,1,0:T(8,128)S(1)}, bf16[3,128,256]{2,1,0:T(8,128)(2,1)S(1)}, bf16[3,128,256]{2,1,0:T(8,128)(2,1)}, bf16[3,128,256]{2,1,0:T(8,128)(2,1)}, bf16[3,128,256]{2,1,0:T(8,128)(2,1)}) custom-call(s32[3]{0:T(128)S(1)} %pad_add_fusion.scalars, bf16[256,1536]{1,0:T(8,128)(2,1)} %bitcast.12, bf16[256,1536]{1,0:T(8,128)(2,1)} %bitcast.15, ...), custom_call_target="tpu_custom_call" | custom-call | flops 600000000 | tf_op jit(solution)/shard_map/spatial_forward/pallas_call | solution.py:74
  18.6 2.1 %collective-permute-start = (bf16[3,128,256]{2,1,0:T(8,128)(2,1)}, bf16[3,128,256]{2,1,0:T(8,128)(2,1)}, u32[]{:S(2)}, u32[]{:S(2)}) collective-permute-start(bf16[3,128,256]{2,1,0:T(8,128)(2,1)} %get-tuple-element.30), channel_id=1, source_target_pairs={{0,2},{2,0},{4,6},{6,4},{1,3},{3,1},{5,7},{7,5},{8,10},{10,8},{12,... | collective-permute-start | bytes 589832 | tf_op jit(solution)/shard_map/ppermute | solution.py:399
  20.7 2.4 %collective-permute-start.1 = (bf16[3,128,256]{2,1,0:T(8,128)(2,1)}, bf16[3,128,256]{2,1,0:T(8,128)(2,1)}, u32[]{:S(2)}, u32[]{:S(2)}) collective-permute-start(bf16[3,128,256]{2,1,0:T(8,128)(2,1)} %get-tuple-element.31), channel_id=1, source_target_pairs={{0,4},{2,6},{4,0},{6,2},{1,5},{3,7},{5,1},{7,3},{8,12},{10,14},{12... | collective-permute-start | bytes 589832 | tf_op jit(solution)/shard_map/ppermute | solution.py:399
  23.0 0.1 collective-permute-start.2
  23.1 0.1 fusion
  23.2 17.0 %all-to-all-done.field_ref = bf16[8,128,384]{2,1,0:T(8,128)(2,1)} async-done(((bf16[8,128,384]{2,1,0:T(8,128)(2,1)}), bf16[8,128,384]{2,1,0:T(8,128)(2,1)}, u32[]{:S(2)}, u32[]{:S(2)}) %all-to-all-start) | async-done | bytes 786464 | tf_op jit(solution)/shard_map/all_to_all | solution.py:416
  40.3 1.5 %turn_cotangent.1.refs_4_ = bf16[2,4,3,128,128]{4,3,2,1,0:T(8,128)(2,1)S(1)} custom-call(bf16[8,128,384]{2,1,0:T(8,128)(2,1)} %all-to-all-done.field_ref), custom_call_target="tpu_custom_call" | custom-call | flops 200000000 | tf_op jit(solution)/shard_map/turn_cotangent/pallas_call | solution.py:225
  41.8 2.7 %collective-permute-done.1.refs_2_ = bf16[3,128,256]{2,1,0:T(8,128)(2,1)} collective-permute-done((bf16[3,128,256]{2,1,0:T(8,128)(2,1)}, bf16[3,128,256]{2,1,0:T(8,128)(2,1)}, u32[]{:S(2)}, u32[]{:S(2)}) %collective-permute-start.1) | collective-permute-done | bytes 196640 | tf_op jit(solution)/shard_map/ppermute | solution.py:399
  44.5 0.1 broadcast_in_dim.8.refs_5_
  44.6 3.9 %temporal.1 = (bf16[3,128,256]{2,1,0:T(8,128)(2,1)S(1)}, bf16[3,128,256]{2,1,0:T(8,128)(2,1)S(1)}, bf16[3,128,256]{2,1,0:T(8,128)(2,1)S(1)}, bf16[3,128,256]{2,1,0:T(8,128)(2,1)S(1)}, f32[8,128]{1,0:T(8,128)S(1)}) custom-call(s32[3]{0:T(128)S(1)} %pad_add_fusion.scalars, bf16[3,128,256]{2,1,0:T(8,128)(2,1)S(1)} %get-tuple-element.29.refs_0_, ...), custom_call_target="tpu_custom_call" | custom-call | flops 400000000 | tf_op jit(solution)/shard_map/temporal/pallas_call | solution.py:363
  48.6 0.2 collective-permute-start.3
  48.8 4.7 %collective-permute-start.4 = (bf16[3,128,256]{2,1,0:T(8,128)(2,1)S(1)}, bf16[3,128,256]{2,1,0:T(8,128)(2,1)S(1)}, u32[]{:S(2)}, u32[]{:S(2)}) collective-permute-start(bf16[3,128,256]{2,1,0:T(8,128)(2,1)S(1)} %get-tuple-element.35), channel_id=1, source_target_pairs={{0,4},{2,6},{4,0},{6,2},{1,5},{3,7},{5,1},{7,3},{8,12},{10,14},{12... | collective-permute-start | bytes 589832 | tf_op jit(solution)/shard_map/ppermute | solution.py:399
  53.5 1.6 %collective-permute-start.6 = (f32[16,128]{1,0:T(8,128)S(1)}, f32[16,128]{1,0:T(8,128)S(1)}, u32[]{:S(2)}, u32[]{:S(2)}) collective-permute-start(f32[16,128]{1,0:T(8,128)S(1)} %pad_maximum_fusion.1), channel_id=1, source_target_pairs={{0,16},{8,24},{16,0},{24,8},{1,17},{9,25},{17,1},{25,9},{2,18},{10... | collective-permute-start | bytes 24584 | tf_op jit(solution)/shard_map/ppermute | solution.py:399
  55.1 1.9 %spatial_backward.2 = (bf16[256,1536]{1,0:T(8,128)(2,1)}, bf16[256,1536]{1,0:T(8,128)(2,1)}) custom-call(s32[3]{0:T(128)S(1)} %pad_add_fusion.scalars, bf16[256,1536]{1,0:T(8,128)(2,1)S(1)} %bitcast.13, bf16[256,1536]{1,0:T(8,128)(2,1)S(1)} %bitcast.16, bf16[256,1536]{1,0:T(8,128)(2,1)S(1)} %bitcast.19, f32[12,256,256]{2,1,0:T(8,128)S(1)} %get-tuple-element.28.refs_3_, ...), custom_call_target="tpu_custom_call" | custom-call | flops 200000000 | tf_op jit(solution)/shard_map/spatial_backward/pallas_call | solution.py:158
  57.0 0.2 collective-permute-done.6
  57.2 1.4 %collective-permute-start.10 = (f32[32,128]{1,0:T(8,128)S(1)}, f32[32,128]{1,0:T(8,128)S(1)}, u32[]{:S(2)}, u32[]{:S(2)}) collective-permute-start(f32[32,128]{1,0:T(8,128)S(1)} %pad_maximum_fusion.refs_7_), channel_id=1, source_target_pairs={{0,6},{2,4},{4,2},{6,0},{1,7},{3,5},{5,3},{7,1},{8,14},{10,12},{12... | collective-permute-start | bytes 49160 | tf_op jit(solution)/shard_map/ppermute | solution.py:399
  58.6 2.0 %collective-permute-start.9 = (f32[32,128]{1,0:T(8,128)S(1)}, f32[32,128]{1,0:T(8,128)S(1)}, u32[]{:S(2)}, u32[]{:S(2)}) collective-permute-start(f32[32,128]{1,0:T(8,128)S(1)} %pad_maximum_fusion.refs_7_), channel_id=1, source_target_pairs={{0,4},{2,6},{4,0},{6,2},{1,5},{3,7},{5,1},{7,3},{8,12},{10,14},{12... | collective-permute-start | bytes 49160 | tf_op jit(solution)/shard_map/ppermute | solution.py:399
  60.7 1.9 %collective-permute-done.7.refs_6_ = bf16[3,128,256]{2,1,0:T(8,128)(2,1)S(1)} collective-permute-done((bf16[3,128,256]{2,1,0:T(8,128)(2,1)S(1)}, bf16[3,128,256]{2,1,0:T(8,128)(2,1)S(1)}, u32[]{:S(2)}, u32[]{:S(2)}) %collective-permute-start.7) | collective-permute-done | bytes 196640 | tf_op jit(solution)/shard_map/ppermute | solution.py:399
  62.6 2.5 %collective-permute-start.8 = (f32[32,128]{1,0:T(8,128)S(1)}, f32[32,128]{1,0:T(8,128)S(1)}, u32[]{:S(2)}, u32[]{:S(2)}) collective-permute-start(f32[32,128]{1,0:T(8,128)S(1)} %pad_maximum_fusion.refs_7_), channel_id=1, source_target_pairs={{0,2},{2,0},{4,6},{6,4},{1,3},{3,1},{5,7},{7,5},{8,10},{10,8},{12,... | collective-permute-start | bytes 49160 | tf_op jit(solution)/shard_map/ppermute | solution.py:399
  65.0 1.8 %collective-permute-done.10.refs_10_ = f32[32,128]{1,0:T(8,128)S(1)} collective-permute-done((f32[32,128]{1,0:T(8,128)S(1)}, f32[32,128]{1,0:T(8,128)S(1)}, u32[]{:S(2)}, u32[]{:S(2)}) %collective-permute-start.10) | collective-permute-done | bytes 16416 | tf_op jit(solution)/shard_map/ppermute | solution.py:399
  66.8 4.9 %collective-permute-done.9.refs_9_ = f32[32,128]{1,0:T(8,128)S(1)} collective-permute-done((f32[32,128]{1,0:T(8,128)S(1)}, f32[32,128]{1,0:T(8,128)S(1)}, u32[]{:S(2)}, u32[]{:S(2)}) %collective-permute-start.9) | collective-permute-done | bytes 16416 | tf_op jit(solution)/shard_map/ppermute | solution.py:399
  71.8 3.0 %spatial_backward.3 = (bf16[256,1536]{1,0:T(8,128)(2,1)}, bf16[256,1536]{1,0:T(8,128)(2,1)}, f32[2,16,1536]{2,1,0:T(8,128)}) custom-call(s32[3]{0:T(128)S(1)} %pad_add_fusion.scalars, bf16[256,1536]{1,0:T(8,128)(2,1)S(1)} %bitcast.14, bf16[256,1536]{1,0:T(8,128)(2,1)S(1)} %bitcast.17, ...), custom_call_target="tpu_custom_call", output_to_operand_aliasing={{0}: (13, {}), {1}: (14, {})} | custom-call | flops 200000000 | tf_op jit(solution)/shard_map/spatial_backward/pallas_call | solution.py:158
  (19 shorter events, 0.2 us)
Async XLA Ops:
  0.6 22.5 %copy-start.3 = (f32[2,16,1536]{2,1,0:T(8,128)S(1)}, f32[2,16,1536]{2,1,0:T(8,128)}, u32[]{:S(2)}) copy-start(f32[2,16,1536]{2,1,0:T(8,128)} %refs_11_.1) | copy-start | bytes 589828
  2.8 37.4 %all-to-all-start = ((bf16[8,128,384]{2,1,0:T(8,128)(2,1)}), bf16[8,128,384]{2,1,0:T(8,128)(2,1)}, u32[]{:S(2)}, u32[]{:S(2)}) async-start(bf16[8,128,384]{2,1,0:T(8,128)(2,1)} %pack_cotangent.1), calls=%async_computation | async-start | bytes 1572864 | tf_op jit(solution)/shard_map/all_to_all | solution.py:416
  18.6 23.2 %collective-permute-start = (bf16[3,128,256]{2,1,0:T(8,128)(2,1)}, bf16[3,128,256]{2,1,0:T(8,128)(2,1)}, u32[]{:S(2)}, u32[]{:S(2)}) collective-permute-start(bf16[3,128,256]{2,1,0:T(8,128)(2,1)} %get-tuple-element.30), channel_id=1, source_target_pairs={{0,2},{2,0},{4,6},{6,4},{1,3},{3,1},{5,7},{7,5},{8,10},{10,8},{12,... | collective-permute-start | bytes 589832 | tf_op jit(solution)/shard_map/ppermute | solution.py:399
  20.7 23.8 %collective-permute-start.1 = (bf16[3,128,256]{2,1,0:T(8,128)(2,1)}, bf16[3,128,256]{2,1,0:T(8,128)(2,1)}, u32[]{:S(2)}, u32[]{:S(2)}) collective-permute-start(bf16[3,128,256]{2,1,0:T(8,128)(2,1)} %get-tuple-element.31), channel_id=1, source_target_pairs={{0,4},{2,6},{4,0},{6,2},{1,5},{3,7},{5,1},{7,3},{8,12},{10,14},{12... | collective-permute-start | bytes 589832 | tf_op jit(solution)/shard_map/ppermute | solution.py:399
  23.0 21.4 %collective-permute-start.2 = (bf16[3,128,256]{2,1,0:T(8,128)(2,1)}, bf16[3,128,256]{2,1,0:T(8,128)(2,1)}, u32[]{:S(2)}, u32[]{:S(2)}) collective-permute-start(bf16[3,128,256]{2,1,0:T(8,128)(2,1)} %get-tuple-element.32), channel_id=1, source_target_pairs={{0,6},{2,4},{4,2},{6,0},{1,7},{3,5},{5,3},{7,1},{8,14},{10,12},{12... | collective-permute-start | bytes 589832 | tf_op jit(solution)/shard_map/ppermute | solution.py:399
  40.2 14.8 %copy-start = (bf16[1,1,256,1536]{3,2,1,0:T(8,128)(2,1)S(1)}, bf16[1,1,256,1536]{3,2,1,0:T(8,128)(2,1)}, u32[]{:S(2)}) copy-start(bf16[1,1,256,1536]{3,2,1,0:T(8,128)(2,1)} %param.7) | copy-start | bytes 2359300
  40.2 14.8 %copy-start.1 = (bf16[1,1,256,1536]{3,2,1,0:T(8,128)(2,1)S(1)}, bf16[1,1,256,1536]{3,2,1,0:T(8,128)(2,1)}, u32[]{:S(2)}) copy-start(bf16[1,1,256,1536]{3,2,1,0:T(8,128)(2,1)} %param.8) | copy-start | bytes 2359300
  40.2 14.8 %copy-start.2 = (bf16[1,1,256,1536]{3,2,1,0:T(8,128)(2,1)S(1)}, bf16[1,1,256,1536]{3,2,1,0:T(8,128)(2,1)}, u32[]{:S(2)}) copy-start(bf16[1,1,256,1536]{3,2,1,0:T(8,128)(2,1)} %param.9) | copy-start | bytes 2359300
  48.5 5.0 %collective-permute-start.5 = (f32[8,128]{1,0:T(8,128)S(1)}, f32[8,128]{1,0:T(8,128)S(1)}, u32[]{:S(2)}, u32[]{:S(2)}) collective-permute-start(f32[8,128]{1,0:T(8,128)S(1)} %get-tuple-element.36), channel_id=1, source_target_pairs={{0,8},{8,0},{16,24},{24,16},{1,9},{9,1},{17,25},{25,17},{2,10},{10... | collective-permute-start | bytes 12296 | tf_op jit(solution)/shard_map/ppermute | solution.py:399
  48.6 23.2 %collective-permute-start.3 = (bf16[3,128,256]{2,1,0:T(8,128)(2,1)S(1)}, bf16[3,128,256]{2,1,0:T(8,128)(2,1)S(1)}, u32[]{:S(2)}, u32[]{:S(2)}) collective-permute-start(bf16[3,128,256]{2,1,0:T(8,128)(2,1)S(1)} %get-tuple-element.34), channel_id=1, source_target_pairs={{0,6},{2,4},{4,2},{6,0},{1,7},{3,5},{5,3},{7,1},{8,14},{10,12},{12... | collective-permute-start | bytes 589832 | tf_op jit(solution)/shard_map/ppermute | solution.py:399
  48.8 22.9 %collective-permute-start.4 = (bf16[3,128,256]{2,1,0:T(8,128)(2,1)S(1)}, bf16[3,128,256]{2,1,0:T(8,128)(2,1)S(1)}, u32[]{:S(2)}, u32[]{:S(2)}) collective-permute-start(bf16[3,128,256]{2,1,0:T(8,128)(2,1)S(1)} %get-tuple-element.35), channel_id=1, source_target_pairs={{0,4},{2,6},{4,0},{6,2},{1,5},{3,7},{5,1},{7,3},{8,12},{10,14},{12... | collective-permute-start | bytes 589832 | tf_op jit(solution)/shard_map/ppermute | solution.py:399
  53.5 9.1 %collective-permute-start.7 = (bf16[3,128,256]{2,1,0:T(8,128)(2,1)S(1)}, bf16[3,128,256]{2,1,0:T(8,128)(2,1)S(1)}, u32[]{:S(2)}, u32[]{:S(2)}) collective-permute-start(bf16[3,128,256]{2,1,0:T(8,128)(2,1)S(1)} %get-tuple-element.43), channel_id=1, source_target_pairs={{0,2},{2,0},{4,6},{6,4},{1,3},{3,1},{5,7},{7,5},{8,10},{10,8},{12,... | collective-permute-start | bytes 589832 | tf_op jit(solution)/shard_map/ppermute | solution.py:399
  53.5 3.7 %collective-permute-start.6 = (f32[16,128]{1,0:T(8,128)S(1)}, f32[16,128]{1,0:T(8,128)S(1)}, u32[]{:S(2)}, u32[]{:S(2)}) collective-permute-start(f32[16,128]{1,0:T(8,128)S(1)} %pad_maximum_fusion.1), channel_id=1, source_target_pairs={{0,16},{8,24},{16,0},{24,8},{1,17},{9,25},{17,1},{25,9},{2,18},{10... | collective-permute-start | bytes 24584 | tf_op jit(solution)/shard_map/ppermute | solution.py:399
  57.2 9.6 %collective-permute-start.10 = (f32[32,128]{1,0:T(8,128)S(1)}, f32[32,128]{1,0:T(8,128)S(1)}, u32[]{:S(2)}, u32[]{:S(2)}) collective-permute-start(f32[32,128]{1,0:T(8,128)S(1)} %pad_maximum_fusion.refs_7_), channel_id=1, source_target_pairs={{0,6},{2,4},{4,2},{6,0},{1,7},{3,5},{5,3},{7,1},{8,14},{10,12},{12... | collective-permute-start | bytes 49160 | tf_op jit(solution)/shard_map/ppermute | solution.py:399
  58.6 13.1 %collective-permute-start.9 = (f32[32,128]{1,0:T(8,128)S(1)}, f32[32,128]{1,0:T(8,128)S(1)}, u32[]{:S(2)}, u32[]{:S(2)}) collective-permute-start(f32[32,128]{1,0:T(8,128)S(1)} %pad_maximum_fusion.refs_7_), channel_id=1, source_target_pairs={{0,4},{2,6},{4,0},{6,2},{1,5},{3,7},{5,1},{7,3},{8,12},{10,14},{12... | collective-permute-start | bytes 49160 | tf_op jit(solution)/shard_map/ppermute | solution.py:399
  62.6 9.2 %collective-permute-start.8 = (f32[32,128]{1,0:T(8,128)S(1)}, f32[32,128]{1,0:T(8,128)S(1)}, u32[]{:S(2)}, u32[]{:S(2)}) collective-permute-start(f32[32,128]{1,0:T(8,128)S(1)} %pad_maximum_fusion.refs_7_), channel_id=1, source_target_pairs={{0,2},{2,0},{4,6},{6,4},{1,3},{3,1},{5,7},{7,5},{8,10},{10,8},{12,... | collective-permute-start | bytes 49160 | tf_op jit(solution)/shard_map/ppermute | solution.py:399

commit v9 on v8

--- a/solution.py
+++ b/solution.py
@@ -170,9 +170,10 @@
     )(scalars, *operands, *earlier)
 
 
-def pack_kernel(frames, spaces, field_ref, packed_ref, rows, arrived):
+def pack_kernel(scalars, field_ref, *refs):
+    *packed_refs, rows, arrived = refs
     chunks, size, _ = rows.shape
-    width = packed_ref.shape[2]
+    spaces, _, width = packed_refs[0].shape
     copies = [
         pltpu.make_async_copy(
             field_ref.at[pl.ds(chunk * size, size), :], rows.at[chunk], arrived.at[chunk]
@@ -183,23 +184,25 @@
         copy.start()
     for chunk, copy in enumerate(copies):
         copy.wait()
-        for frame in range(frames):
+        for distance, packed_ref in enumerate(packed_refs):
             for space in range(spaces):
-                cols = pl.ds((space * frames + frame) * width, width)
-                packed_ref[frame * spaces + space, pl.ds(chunk * size, size), :] = rows[
-                    chunk, :, cols
-                ]
-
-
-def pack(field, frames, spaces):
+                start = (space * len(packed_refs) + partner(scalars, distance)) * width
+                cols = pl.ds(pl.multiple_of(start, HEAD_DIM), width)
+                packed_ref[space, pl.ds(chunk * size, size), :] = rows[chunk, :, cols]
+
+
+def pack(scalars, field, frames, spaces):
     patches, feat = field.shape
-    devices = frames * spaces
     chunks = patches // GROUP
+    shape = (spaces, patches, feat // (frames * spaces))
     return pl.pallas_call(
-        functools.partial(pack_kernel, frames, spaces),
-        in_specs=[pl.BlockSpec(memory_space=pltpu.HBM)],
-        out_specs=pl.BlockSpec(memory_space=pltpu.VMEM),
-        out_shape=jax.ShapeDtypeStruct((devices, patches, feat // devices), field.dtype),
+        pack_kernel,
+        in_specs=[
+            pl.BlockSpec(memory_space=pltpu.SMEM),
+            pl.BlockSpec(memory_space=pltpu.HBM),
+        ],
+        out_specs=[pl.BlockSpec(memory_space=pltpu.VMEM)] * frames,
+        out_shape=[jax.ShapeDtypeStruct(shape, field.dtype)] * frames,
         scratch_shapes=[
             pltpu.VMEM((chunks, patches // chunks, feat), field.dtype),
             pltpu.SemaphoreType.DMA((chunks,)),
@@ -207,30 +210,43 @@
         compiler_params=params(patches),
         cost_estimate=cost(1),
         name="pack_cotangent",
-    )(pltpu.with_memory_space_constraint(field, pltpu.HBM))
-
-
-def turn_kernel(field_ref, turned_ref):
-    spaces, frames, heads = turned_ref.shape[:3]
+    )(scalars, pltpu.with_memory_space_constraint(field, pltpu.HBM))
+
+
+def turn_kernel(frames, scalars, *refs):
+    piece_refs, (own_ref, *other_refs), turned = refs[:frames], refs[frames:-1], refs[-1]
+    spaces = piece_refs[0].shape[0]
+    heads = own_ref.shape[1]
     for space in range(spaces):
-        for frame in range(frames):
+        target = turned if space else own_ref
+        source = jnp.bitwise_xor(scalars[1], space)
+        for distance, ref in enumerate(piece_refs):
+            frame = partner(scalars, distance)
             for head in range(heads):
                 cols = pl.ds(head * HEAD_DIM, HEAD_DIM)
-                turned_ref[space, frame, head] = field_ref[frame * spaces + space, :, cols].T
-
-
-def turn(field, frames, spaces):
-    devices, patches, feat = field.shape
-    heads = feat // HEAD_DIM
+                target[frame, head] = ref[source, :, cols].T
+        if space:
+            half = frames // 2
+            other_refs[2 * space - 2][...] = turned[:half]
+            other_refs[2 * space - 1][...] = turned[half:]
+
+
+def turn(scalars, pieces):
+    spaces, patches, feat = pieces[0].shape
+    frames, heads = len(pieces), feat // HEAD_DIM
+    turned = (heads, HEAD_DIM, patches)
+    sizes = [frames] + [frames // 2, frames - frames // 2] * (spaces - 1)
     return pl.pallas_call(
-        turn_kernel,
-        in_specs=[pl.BlockSpec(memory_space=pltpu.VMEM)],
-        out_specs=pl.BlockSpec(memory_space=pltpu.VMEM),
-        out_shape=jax.ShapeDtypeStruct((spaces, frames, heads, HEAD_DIM, patches), field.dtype),
+        functools.partial(turn_kernel, frames),
+        in_specs=[pl.BlockSpec(memory_space=pltpu.SMEM)]
+        + [pl.BlockSpec(memory_space=pltpu.VMEM)] * frames,
+        out_specs=[pl.BlockSpec(memory_space=pltpu.VMEM)] * len(sizes),
+        out_shape=[jax.ShapeDtypeStruct((size,) + turned, pieces[0].dtype) for size in sizes],
+        scratch_shapes=[pltpu.VMEM((frames,) + turned, pieces[0].dtype)],
         compiler_params=params(patches),
         cost_estimate=cost(2),
         name="turn_cotangent",
-    )(field)
+    )(scalars, *pieces)
 
 
 def temporal_part(length, attended_ref, load_upstream, load_gain, grad_ref):
@@ -323,47 +339,62 @@
     return jnp.concatenate(all_mixed, axis=0)
 
 
-def temporal_kernel(frames, scalars, *refs):
-    attended_refs, (upstream_ref, gain_ref) = refs[:frames], refs[frames : frames + 2]
-    grad_refs, mixed_ref = refs[frames + 2 : 2 * frames + 2], refs[2 * frames + 2]
-    attended, grads = refs[2 * frames + 3 :]
-    parts, _, heads, _, lanes = upstream_ref.shape
-    mixed_ref[...] = jnp.full(mixed_ref.shape, scalars[2].astype(jnp.float32))
+def temporal_kernel(frames, spaces, scalars, *refs):
+    attended_refs, (gain_ref, own_ref, *other_refs), refs = (
+        refs[:frames],
+        refs[frames : frames + 2 * spaces],
+        refs[frames + 2 * spaces :],
+    )
+    grad_refs, (mixed_ref, attended, grads) = refs[:frames], refs[frames:]
+    heads, lanes = own_ref.shape[1], own_ref.shape[3]
+    half = frames // 2
+    mixed_ref[...] = jnp.full(mixed_ref.shape, scalars[3].astype(jnp.float32))
+
+    def load_upstream(space, head, t, rows):
+        if space == 0:
+            return own_ref[t, head, rows, :]
+        return other_refs[2 * space - 2 + t // half][t % half, head, rows, :]
 
     def step(head, carry):
+        places = [
+            pl.ds(pl.multiple_of(jnp.bitwise_xor(scalars[1], space) * lanes, lanes), lanes)
+            for space in range(spaces)
+        ]
         for distance, ref in enumerate(attended_refs):
             frame = partner(scalars, distance)
-            for part in range(parts):
-                attended[part, frame] = ref[head, :, pl.ds(part * lanes, lanes)]
+            for space, here in enumerate(places):
+                attended[space, frame] = ref[head, :, here]
         mixed = [
             temporal_part(
-                scalars[1],
-                attended.at[part],
-                lambda t, rows: upstream_ref[part, t, head, rows, :],
+                scalars[2],
+                attended.at[space],
+                functools.partial(load_upstream, space, head),
                 lambda rows: gain_ref[head, rows, :],
-                grads.at[part],
+                grads.at[space],
             )
-            for part in range(parts)
+            for space in range(spaces)
         ]
         summed = functools.reduce(jnp.add, mixed)
         mixed_ref[pl.ds(head, 1), :] = jnp.sum(summed.T, axis=0, keepdims=True) * 0.5
         for distance, ref in enumerate(grad_refs):
             frame = partner(scalars, distance)
-            for part in range(parts):
-                ref[head, :, pl.ds(part * lanes, lanes)] = grads[part, frame]
+            for space, here in enumerate(places):
+                ref[head, :, here] = grads[space, frame]
         return carry
 
     lax.fori_loop(0, heads, step, 0)
 
 
 def temporal(scalars, attended, upstream, gain):
-    spaces, frames, heads, feat, lanes = upstream.shape
+    frames, heads, feat, lanes = upstream[0].shape
+    spaces = (len(upstream) + 1) // 2
     patches = spaces * lanes
     rows = -(-(heads + 1) // 8) * 8
+    operands = [*attended, gain, *upstream]
     *grads, mixed = pl.pallas_call(
-        functools.partial(temporal_kernel, frames),
+        functools.partial(temporal_kernel, frames, spaces),
         in_specs=[pl.BlockSpec(memory_space=pltpu.SMEM)]
-        + [pl.BlockSpec(memory_space=pltpu.VMEM)] * (frames + 2),
+        + [pl.BlockSpec(memory_space=pltpu.VMEM)] * len(operands),
         out_specs=[pl.BlockSpec(memory_space=pltpu.VMEM)] * (frames + 1),
         scratch_shapes=[pltpu.VMEM((spaces, frames, feat, lanes), jnp.bfloat16)] * 2,
         out_shape=[jax.ShapeDtypeStruct((heads, feat, patches), jnp.bfloat16)] * frames
@@ -371,7 +402,7 @@
         compiler_params=params(patches),
         cost_estimate=cost(4),
         name="temporal",
-    )(scalars, *attended, upstream, gain)
+    )(scalars, *operands)
     return grads, mixed
 
 
@@ -409,18 +440,21 @@
     queries, key_rows, values = (
         field.reshape(patches, feat) for field in (query_heads, key_heads, value_heads)
     )
-    frame = lax.axis_index("tm")
-    scalars = jnp.stack([frame, lengths[0], task_ids[0]]).astype(jnp.int32)
-
-    packed = pack(cotangent.reshape(cotangent.shape[2:]), frames, spaces)
-    incoming = lax.all_to_all(packed, ("tm", "space"), split_axis=0, concat_axis=0, tiled=True)
-    queries, _ = lax.optimization_barrier((queries, packed))
+    frame, space = lax.axis_index("tm"), lax.axis_index("space")
+    scalars = jnp.stack([frame, space, lengths[0], task_ids[0]]).astype(jnp.int32)
+
+    pieces = pack(scalars, cotangent.reshape(cotangent.shape[2:]), frames, spaces)
+    queries, pieces = lax.optimization_barrier((queries, list(pieces)))
+    for distance in range(1, frames):
+        pieces[distance] = swap(pieces[distance], "tm", frames, distance)
     fields = (queries, key_rows, values)
     weights, attended = forward(scalars, *fields, frames)
-    for distance in reversed(range(1, frames)):
+    for distance in range(1, frames):
         attended[distance] = swap(attended[distance], "tm", frames, distance)
-    incoming, _ = lax.optimization_barrier((incoming, weights))
-    upstream = turn(incoming, frames, spaces)
+    pieces, _ = lax.optimization_barrier((pieces, weights))
+    upstream = list(turn(scalars, pieces))
+    for index in range(1, len(upstream)):
+        upstream[index] = swap(upstream[index], "space", spaces, (index + 1) // 2)
     rows = lax.dynamic_index_in_dim(gains, task_ids[0], 1, keepdims=False)
     product = lax.dynamic_slice_in_dim(rows[0] * rows[1], frame * width, width, 0)
     gain = jnp.broadcast_to(
@@ -552,8 +586,8 @@
 
     def local(query_heads, *others):
         heads = query_heads.shape[3] // HEAD_DIM
-        powers = all(size & (size - 1) == 0 for size in (clips, frames))
-        if powers and frames <= 4 and heads % frames == 0:
+        powers = all(size & (size - 1) == 0 for size in (clips, frames, spaces))
+        if powers and 2 <= frames <= 4 and heads % frames == 0:
             return split_by_heads(query_heads, *others, clips, frames, spaces)
         return split_by_patches(query_heads, *others)
 

time: 75 us -> 72.9 us (0.972)
  waiting for transfers between devices: 28.5 us -> 20 us
  local copies, waits for them, and re-layouts: 0.12 us -> 4.44 us
  starting transfers between devices: 24.3 us -> 25.7 us
    all_to_all x1 -> x0, waiting for transfers between devices: 17 us -> none  [split_by_heads(): lax.all_to_all(packed, ('tm', 'space'), split_axis=0, concat_axis=0, tile...]
    ppermute x11 -> x16, starting transfers between devices: 17 us -> 25.7 us  [swap(): return lax.ppermute(field, axis, [(i, i ^ distance) for i in range(size)])]
    ppermute x11 -> x16, waiting for transfers between devices: 11.5 us -> 20 us  [swap(): return lax.ppermute(field, axis, [(i, i ^ distance) for i in range(size)])]
    all_to_all x1 -> x0, starting transfers between devices: 7.29 us -> none  [split_by_heads(): lax.all_to_all(packed, ('tm', 'space'), split_axis=0, concat_axis=0, tile...]
    unnamed x8 -> x12, local copies, waits for them, and re-layouts: 0.02 us -> 4.33 us
  transfers between devices with their start and end apart: 12 -> 16, of which waited for: 6 -> 4; matrix products, arithmetic and copies ran while one was open for 0% -> 1% of each run, Pallas kernels for 14% -> 15%
where the time goes in v9:
time: 72.9 us; the launch traced here: 72.5 us
  starting transfers between devices  25.7 us (35%)
  waiting for transfers between devices  20 us (27%)
  Pallas kernels  19.5 us (27%)
  local copies, waits for them, and re-layouts  4.44 us (6%)
  between operations  2.04 us (3%)
  other arithmetic  0.9 us (1%)
    ppermute x16, starting transfers between devices, swap(): return lax.ppermute(field, axis, [(i, i ^ distance) for i in range(size)])  25.7 us
    ppermute x16, waiting for transfers between devices, swap(): return lax.ppermute(field, axis, [(i, i ^ distance) for i in range(size)])  20 us
    pallas_call x1, Pallas kernels, forward(): pl.pallas_call(forward_kernel, in_specs=[pl.BlockSpec(memory_space=pltpu....  7.06 us
    pallas_call x2, Pallas kernels, backward(): pl.pallas_call(functools.partial(backward_kernel, distances, gains_of), i...  4.93 us
    unnamed x12, local copies, waits for them, and re-layouts  4.33 us
    pallas_call x1, Pallas kernels, temporal(): pl.pallas_call(functools.partial(temporal_kernel, frames, spaces), in_spe...  4.11 us
    pallas_call x1, Pallas kernels, pack(): pl.pallas_call(pack_kernel, in_specs=[pl.BlockSpec(memory_space=pltpu.SME...  1.83 us
    pallas_call x1, Pallas kernels, turn(): pl.pallas_call(functools.partial(turn_kernel, frames), in_specs=[pl.Block...  1.56 us
  transfers between devices with their start and end apart: 16, of which 4 were waited for; matrix products, arithmetic and copies ran while one was open for 1% of the time, Pallas kernels for 15%

profile of v9, /device:TPU:0, one launch (start us, length us, event | category | flops | bytes accessed | tf_op | source)
XLA Modules:
  0.0 72.5 jit_solution(4686947099461719254)
XLA Ops:
  2.0 1.8 %pack_cotangent.1 = (bf16[2,128,384]{2,1,0:T(8,128)(2,1)S(1)}, bf16[2,128,384]{2,1,0:T(8,128)(2,1)S(1)}, bf16[2,128,384]{2,1,0:T(8,128)(2,1)S(1)}, bf16[2,128,384]{2,1,0:T(8,128)(2,1)S(1)}) custom-call(s32[4]{0:T(128)S(1)} %pad_add_fusion.scalars, bf16[128,3072]{1,0:T(8,128)(2,1)} %bitcast.22), custom_call_target="tpu_custom_call" | custom-call | flops 100000000 | tf_op jit(solution)/shard_map/pack_cotangent/pallas_call | solution.py:198
  3.8 3.1 %collective-permute-start.3 = (bf16[2,128,384]{2,1,0:T(8,128)(2,1)S(1)}, bf16[2,128,384]{2,1,0:T(8,128)(2,1)S(1)}, u32[]{:S(2)}, u32[]{:S(2)}) collective-permute-start(bf16[2,128,384]{2,1,0:T(8,128)(2,1)S(1)} %get-tuple-element.52), channel_id=1, source_target_pairs={{0,2},{2,0},{4,6},{6,4},{1,3},{3,1},{5,7},{7,5},{8,10},{10,8},{12,... | collective-permute-start | bytes 589832 | tf_op jit(solution)/shard_map/ppermute | solution.py:430
  6.9 2.6 %collective-permute-start.4 = (bf16[2,128,384]{2,1,0:T(8,128)(2,1)S(1)}, bf16[2,128,384]{2,1,0:T(8,128)(2,1)S(1)}, u32[]{:S(2)}, u32[]{:S(2)}) collective-permute-start(bf16[2,128,384]{2,1,0:T(8,128)(2,1)S(1)} %get-tuple-element.53), channel_id=1, source_target_pairs={{0,4},{2,6},{4,0},{6,2},{1,5},{3,7},{5,1},{7,3},{8,12},{10,14},{12... | collective-permute-start | bytes 589832 | tf_op jit(solution)/shard_map/ppermute | solution.py:430
  9.5 7.1 %spatial_forward.1 = (f32[12,256,256]{2,1,0:T(8,128)S(1)}, bf16[3,128,256]{2,1,0:T(8,128)(2,1)S(1)}, bf16[3,128,256]{2,1,0:T(8,128)(2,1)}, bf16[3,128,256]{2,1,0:T(8,128)(2,1)}, bf16[3,128,256]{2,1,0:T(8,128)(2,1)}) custom-call(s32[4]{0:T(128)S(1)} %pad_add_fusion.scalars, bf16[256,1536]{1,0:T(8,128)(2,1)} %bitcast.13, bf16[256,1536]{1,0:T(8,128)(2,1)} %bitcast.16, ...), custom_call_target="tpu_custom_call" | custom-call | flops 600000000 | tf_op jit(solution)/shard_map/spatial_forward/pallas_call | solution.py:74
  16.6 1.0 %collective-permute-start = (bf16[3,128,256]{2,1,0:T(8,128)(2,1)}, bf16[3,128,256]{2,1,0:T(8,128)(2,1)}, u32[]{:S(2)}, u32[]{:S(2)}) collective-permute-start(bf16[3,128,256]{2,1,0:T(8,128)(2,1)} %get-tuple-element.48), channel_id=1, source_target_pairs={{0,2},{2,0},{4,6},{6,4},{1,3},{3,1},{5,7},{7,5},{8,10},{10,8},{12,... | collective-permute-start | bytes 589832 | tf_op jit(solution)/shard_map/ppermute | solution.py:430
  17.6 3.5 %collective-permute-start.1 = (bf16[3,128,256]{2,1,0:T(8,128)(2,1)}, bf16[3,128,256]{2,1,0:T(8,128)(2,1)}, u32[]{:S(2)}, u32[]{:S(2)}) collective-permute-start(bf16[3,128,256]{2,1,0:T(8,128)(2,1)} %get-tuple-element.49), channel_id=1, source_target_pairs={{0,4},{2,6},{4,0},{6,2},{1,5},{3,7},{5,1},{7,3},{8,12},{10,14},{12... | collective-permute-start | bytes 589832 | tf_op jit(solution)/shard_map/ppermute | solution.py:430
  21.1 3.1 %collective-permute-done.4.refs_2_ = bf16[2,128,384]{2,1,0:T(8,128)(2,1)S(1)} collective-permute-done((bf16[2,128,384]{2,1,0:T(8,128)(2,1)S(1)}, bf16[2,128,384]{2,1,0:T(8,128)(2,1)S(1)}, u32[]{:S(2)}, u32[]{:S(2)}) %collective-permute-start.4) | collective-permute-done | bytes 196640 | tf_op jit(solution)/shard_map/ppermute | solution.py:430
  24.1 1.6 %turn_cotangent.1 = (bf16[4,3,128,128]{3,2,1,0:T(8,128)(2,1)S(1)}, bf16[2,3,128,128]{3,2,1,0:T(8,128)(2,1)}, bf16[2,3,128,128]{3,2,1,0:T(8,128)(2,1)}) custom-call(s32[4]{0:T(128)S(1)} %pad_add_fusion.scalars, bf16[2,128,384]{2,1,0:T(8,128)(2,1)S(1)} %get-tuple-element.55.refs_0_, bf16[2,128,384]{2,1,0:T(8,128)(2,1)S(1)} %collective-permute-done.3.refs_1_, ...), custom_call_target="tpu_custom_call" | custom-call | flops 200000000 | tf_op jit(solution)/shard_map/turn_cotangent/pallas_call | solution.py:239
  25.7 1.5 %collective-permute-start.6 = (bf16[2,3,128,128]{3,2,1,0:T(8,128)(2,1)}, bf16[2,3,128,128]{3,2,1,0:T(8,128)(2,1)}, u32[]{:S(2)}, u32[]{:S(2)}) collective-permute-start(bf16[2,3,128,128]{3,2,1,0:T(8,128)(2,1)} %get-tuple-element.60), channel_id=1, source_target_pairs={{0,1},{1,0},{2,3},{3,2},{4,5},{5,4},{6,7},{7,6},{8,9},{9,8},{10,11... | collective-permute-start | bytes 589832 | tf_op jit(solution)/shard_map/ppermute | solution.py:430
  28.5 12.5 %collective-permute-done.1.refs_2_ = bf16[3,128,256]{2,1,0:T(8,128)(2,1)} collective-permute-done((bf16[3,128,256]{2,1,0:T(8,128)(2,1)}, bf16[3,128,256]{2,1,0:T(8,128)(2,1)}, u32[]{:S(2)}, u32[]{:S(2)}) %collective-permute-start.1) | collective-permute-done | bytes 196640 | tf_op jit(solution)/shard_map/ppermute | solution.py:430
  42.2 4.1 %temporal.1 = (bf16[3,128,256]{2,1,0:T(8,128)(2,1)S(1)}, bf16[3,128,256]{2,1,0:T(8,128)(2,1)S(1)}, bf16[3,128,256]{2,1,0:T(8,128)(2,1)S(1)}, bf16[3,128,256]{2,1,0:T(8,128)(2,1)S(1)}, f32[8,128]{1,0:T(8,128)S(1)}) custom-call(s32[4]{0:T(128)S(1)} %pad_add_fusion.scalars, bf16[3,128,256]{2,1,0:T(8,128)(2,1)S(1)} %copy-done.5, ...), custom_call_target="tpu_custom_call" | custom-call | flops 400000000 | tf_op jit(solution)/shard_map/temporal/pallas_call | solution.py:394
  46.3 2.5 %collective-permute-start.8 = (bf16[3,128,256]{2,1,0:T(8,128)(2,1)S(1)}, bf16[3,128,256]{2,1,0:T(8,128)(2,1)S(1)}, u32[]{:S(2)}, u32[]{:S(2)}) collective-permute-start(bf16[3,128,256]{2,1,0:T(8,128)(2,1)S(1)} %get-tuple-element.62), channel_id=1, source_target_pairs={{0,6},{2,4},{4,2},{6,0},{1,7},{3,5},{5,3},{7,1},{8,14},{10,12},{12... | collective-permute-start | bytes 589832 | tf_op jit(solution)/shard_map/ppermute | solution.py:430
  48.8 4.9 %collective-permute-start.9 = (bf16[3,128,256]{2,1,0:T(8,128)(2,1)S(1)}, bf16[3,128,256]{2,1,0:T(8,128)(2,1)S(1)}, u32[]{:S(2)}, u32[]{:S(2)}) collective-permute-start(bf16[3,128,256]{2,1,0:T(8,128)(2,1)S(1)} %get-tuple-element.63), channel_id=1, source_target_pairs={{0,4},{2,6},{4,0},{6,2},{1,5},{3,7},{5,1},{7,3},{8,12},{10,14},{12... | collective-permute-start | bytes 589832 | tf_op jit(solution)/shard_map/ppermute | solution.py:430
  53.8 1.5 %collective-permute-start.11 = (f32[16,128]{1,0:T(8,128)S(1)}, f32[16,128]{1,0:T(8,128)S(1)}, u32[]{:S(2)}, u32[]{:S(2)}) collective-permute-start(f32[16,128]{1,0:T(8,128)S(1)} %pad_maximum_fusion.1), channel_id=1, source_target_pairs={{0,16},{8,24},{16,0},{24,8},{1,17},{9,25},{17,1},{25,9},{2,18},{10... | collective-permute-start | bytes 24584 | tf_op jit(solution)/shard_map/ppermute | solution.py:430
  55.3 1.1 %copy-done = bf16[1,1,256,1536]{3,2,1,0:T(8,128)(2,1)S(1)} copy-done((bf16[1,1,256,1536]{3,2,1,0:T(8,128)(2,1)S(1)}, bf16[1,1,256,1536]{3,2,1,0:T(8,128)(2,1)}, u32[]{:S(2)}) %copy-start) | copy-done | bytes 786456
  56.5 1.1 %copy-done.1 = bf16[1,1,256,1536]{3,2,1,0:T(8,128)(2,1)S(1)} copy-done((bf16[1,1,256,1536]{3,2,1,0:T(8,128)(2,1)S(1)}, bf16[1,1,256,1536]{3,2,1,0:T(8,128)(2,1)}, u32[]{:S(2)}) %copy-start.1) | copy-done | bytes 786456
  57.6 1.1 %copy-done.2 = bf16[1,1,256,1536]{3,2,1,0:T(8,128)(2,1)S(1)} copy-done((bf16[1,1,256,1536]{3,2,1,0:T(8,128)(2,1)S(1)}, bf16[1,1,256,1536]{3,2,1,0:T(8,128)(2,1)}, u32[]{:S(2)}) %copy-start.2) | copy-done | bytes 786456
  58.7 1.9 %spatial_backward.2 = (bf16[256,1536]{1,0:T(8,128)(2,1)}, bf16[256,1536]{1,0:T(8,128)(2,1)}) custom-call(s32[4]{0:T(128)S(1)} %pad_add_fusion.scalars, bf16[256,1536]{1,0:T(8,128)(2,1)S(1)} %bitcast.14, bf16[256,1536]{1,0:T(8,128)(2,1)S(1)} %bitcast.17, bf16[256,1536]{1,0:T(8,128)(2,1)S(1)} %bitcast.20, f32[12,256,256]{2,1,0:T(8,128)S(1)} %get-tuple-element.46.refs_3_, ...), custom_call_target="tpu_custom_call" | custom-call | flops 200000000 | tf_op jit(solution)/shard_map/spatial_backward/pallas_call | solution.py:158
  60.7 2.5 %collective-permute-start.15 = (f32[32,128]{1,0:T(8,128)S(1)}, f32[32,128]{1,0:T(8,128)S(1)}, u32[]{:S(2)}, u32[]{:S(2)}) collective-permute-start(f32[32,128]{1,0:T(8,128)S(1)} %pad_maximum_fusion.refs_7_), channel_id=1, source_target_pairs={{0,6},{2,4},{4,2},{6,0},{1,7},{3,5},{5,3},{7,1},{8,14},{10,12},{12... | collective-permute-start | bytes 49160 | tf_op jit(solution)/shard_map/ppermute | solution.py:430
  63.2 1.0 %collective-permute-start.14 = (f32[32,128]{1,0:T(8,128)S(1)}, f32[32,128]{1,0:T(8,128)S(1)}, u32[]{:S(2)}, u32[]{:S(2)}) collective-permute-start(f32[32,128]{1,0:T(8,128)S(1)} %pad_maximum_fusion.refs_7_), channel_id=1, source_target_pairs={{0,4},{2,6},{4,0},{6,2},{1,5},{3,7},{5,1},{7,3},{8,12},{10,14},{12... | collective-permute-start | bytes 49160 | tf_op jit(solution)/shard_map/ppermute | solution.py:430
  64.2 1.0 %collective-permute-start.13 = (f32[32,128]{1,0:T(8,128)S(1)}, f32[32,128]{1,0:T(8,128)S(1)}, u32[]{:S(2)}, u32[]{:S(2)}) collective-permute-start(f32[32,128]{1,0:T(8,128)S(1)} %pad_maximum_fusion.refs_7_), channel_id=1, source_target_pairs={{0,2},{2,0},{4,6},{6,4},{1,3},{3,1},{5,7},{7,5},{8,10},{10,8},{12,... | collective-permute-start | bytes 49160 | tf_op jit(solution)/shard_map/ppermute | solution.py:430
  65.2 1.3 %collective-permute-done.15.refs_10_ = f32[32,128]{1,0:T(8,128)S(1)} collective-permute-done((f32[32,128]{1,0:T(8,128)S(1)}, f32[32,128]{1,0:T(8,128)S(1)}, u32[]{:S(2)}, u32[]{:S(2)}) %collective-permute-start.15) | collective-permute-done | bytes 16416 | tf_op jit(solution)/shard_map/ppermute | solution.py:430
  66.5 3.0 %collective-permute-done.14.refs_9_ = f32[32,128]{1,0:T(8,128)S(1)} collective-permute-done((f32[32,128]{1,0:T(8,128)S(1)}, f32[32,128]{1,0:T(8,128)S(1)}, u32[]{:S(2)}, u32[]{:S(2)}) %collective-permute-start.14) | collective-permute-done | bytes 16416 | tf_op jit(solution)/shard_map/ppermute | solution.py:430
  69.5 3.0 %spatial_backward.3 = (bf16[256,1536]{1,0:T(8,128)(2,1)}, bf16[256,1536]{1,0:T(8,128)(2,1)}, f32[2,16,1536]{2,1,0:T(8,128)}) custom-call(s32[4]{0:T(128)S(1)} %pad_add_fusion.scalars, bf16[256,1536]{1,0:T(8,128)(2,1)S(1)} %bitcast.15, bf16[256,1536]{1,0:T(8,128)(2,1)S(1)} %bitcast.18, ...), custom_call_target="tpu_custom_call", output_to_operand_aliasing={{0}: (13, {}), {1}: (14, {})} | custom-call | flops 200000000 | tf_op jit(solution)/shard_map/spatial_backward/pallas_call | solution.py:158
  (31 shorter events, 2.6 us)
Async XLA Ops:
  3.8 17.2 %collective-permute-start.3 = (bf16[2,128,384]{2,1,0:T(8,128)(2,1)S(1)}, bf16[2,128,384]{2,1,0:T(8,128)(2,1)S(1)}, u32[]{:S(2)}, u32[]{:S(2)}) collective-permute-start(bf16[2,128,384]{2,1,0:T(8,128)(2,1)S(1)} %get-tuple-element.52), channel_id=1, source_target_pairs={{0,2},{2,0},{4,6},{6,4},{1,3},{3,1},{5,7},{7,5},{8,10},{10,8},{12,... | collective-permute-start | bytes 589832 | tf_op jit(solution)/shard_map/ppermute | solution.py:430
  6.9 17.2 %collective-permute-start.4 = (bf16[2,128,384]{2,1,0:T(8,128)(2,1)S(1)}, bf16[2,128,384]{2,1,0:T(8,128)(2,1)S(1)}, u32[]{:S(2)}, u32[]{:S(2)}) collective-permute-start(bf16[2,128,384]{2,1,0:T(8,128)(2,1)S(1)} %get-tuple-element.53), channel_id=1, source_target_pairs={{0,4},{2,6},{4,0},{6,2},{1,5},{3,7},{5,1},{7,3},{8,12},{10,14},{12... | collective-permute-start | bytes 589832 | tf_op jit(solution)/shard_map/ppermute | solution.py:430
  9.5 14.6 %collective-permute-start.5 = (bf16[2,128,384]{2,1,0:T(8,128)(2,1)S(1)}, bf16[2,128,384]{2,1,0:T(8,128)(2,1)S(1)}, u32[]{:S(2)}, u32[]{:S(2)}) collective-permute-start(bf16[2,128,384]{2,1,0:T(8,128)(2,1)S(1)} %get-tuple-element.54), channel_id=1, source_target_pairs={{0,6},{2,4},{4,2},{6,0},{1,7},{3,5},{5,3},{7,1},{8,14},{10,12},{12... | collective-permute-start | bytes 589832 | tf_op jit(solution)/shard_map/ppermute | solution.py:430
  16.6 9.1 %copy-start.4 = (bf16[3,128,256]{2,1,0:T(8,128)(2,1)}, bf16[3,128,256]{2,1,0:T(8,128)(2,1)S(1)}, u32[]{:S(2)}) copy-start(bf16[3,128,256]{2,1,0:T(8,128)(2,1)S(1)} %get-tuple-element.47.refs_0_) | copy-start | bytes 589828
  16.6 11.9 %collective-permute-start = (bf16[3,128,256]{2,1,0:T(8,128)(2,1)}, bf16[3,128,256]{2,1,0:T(8,128)(2,1)}, u32[]{:S(2)}, u32[]{:S(2)}) collective-permute-start(bf16[3,128,256]{2,1,0:T(8,128)(2,1)} %get-tuple-element.48), channel_id=1, source_target_pairs={{0,2},{2,0},{4,6},{6,4},{1,3},{3,1},{5,7},{7,5},{8,10},{10,8},{12,... | collective-permute-start | bytes 589832 | tf_op jit(solution)/shard_map/ppermute | solution.py:430
  17.6 23.5 %collective-permute-start.1 = (bf16[3,128,256]{2,1,0:T(8,128)(2,1)}, bf16[3,128,256]{2,1,0:T(8,128)(2,1)}, u32[]{:S(2)}, u32[]{:S(2)}) collective-permute-start(bf16[3,128,256]{2,1,0:T(8,128)(2,1)} %get-tuple-element.49), channel_id=1, source_target_pairs={{0,4},{2,6},{4,0},{6,2},{1,5},{3,7},{5,1},{7,3},{8,12},{10,14},{12... | collective-permute-start | bytes 589832 | tf_op jit(solution)/shard_map/ppermute | solution.py:430
  21.1 20.0 %collective-permute-start.2 = (bf16[3,128,256]{2,1,0:T(8,128)(2,1)}, bf16[3,128,256]{2,1,0:T(8,128)(2,1)}, u32[]{:S(2)}, u32[]{:S(2)}) collective-permute-start(bf16[3,128,256]{2,1,0:T(8,128)(2,1)} %get-tuple-element.50), channel_id=1, source_target_pairs={{0,6},{2,4},{4,2},{6,0},{1,7},{3,5},{5,3},{7,1},{8,14},{10,12},{12... | collective-permute-start | bytes 589832 | tf_op jit(solution)/shard_map/ppermute | solution.py:430
  25.7 15.4 %collective-permute-start.6 = (bf16[2,3,128,128]{3,2,1,0:T(8,128)(2,1)}, bf16[2,3,128,128]{3,2,1,0:T(8,128)(2,1)}, u32[]{:S(2)}, u32[]{:S(2)}) collective-permute-start(bf16[2,3,128,128]{3,2,1,0:T(8,128)(2,1)} %get-tuple-element.60), channel_id=1, source_target_pairs={{0,1},{1,0},{2,3},{3,2},{4,5},{5,4},{6,7},{7,6},{8,9},{9,8},{10,11... | collective-permute-start | bytes 589832 | tf_op jit(solution)/shard_map/ppermute | solution.py:430
  27.2 13.9 %collective-permute-start.7 = (bf16[2,3,128,128]{3,2,1,0:T(8,128)(2,1)}, bf16[2,3,128,128]{3,2,1,0:T(8,128)(2,1)}, u32[]{:S(2)}, u32[]{:S(2)}) collective-permute-start(bf16[2,3,128,128]{3,2,1,0:T(8,128)(2,1)} %get-tuple-element.61), channel_id=1, source_target_pairs={{0,1},{1,0},{2,3},{3,2},{4,5},{5,4},{6,7},{7,6},{8,9},{9,8},{10,11... | collective-permute-start | bytes 589832 | tf_op jit(solution)/shard_map/ppermute | solution.py:430
  41.2 0.9 %copy-start.5 = (bf16[3,128,256]{2,1,0:T(8,128)(2,1)S(1)}, bf16[3,128,256]{2,1,0:T(8,128)(2,1)}, u32[]{:S(2)}) copy-start(bf16[3,128,256]{2,1,0:T(8,128)(2,1)} %copy-done.4) | copy-start | bytes 589828
  42.1 27.4 %copy-start.3 = (f32[2,16,1536]{2,1,0:T(8,128)S(1)}, f32[2,16,1536]{2,1,0:T(8,128)}, u32[]{:S(2)}) copy-start(f32[2,16,1536]{2,1,0:T(8,128)} %refs_11_.1) | copy-start | bytes 589828
  46.3 7.6 %collective-permute-start.10 = (f32[8,128]{1,0:T(8,128)S(1)}, f32[8,128]{1,0:T(8,128)S(1)}, u32[]{:S(2)}, u32[]{:S(2)}) collective-permute-start(f32[8,128]{1,0:T(8,128)S(1)} %get-tuple-element.64), channel_id=1, source_target_pairs={{0,8},{8,0},{16,24},{24,16},{1,9},{9,1},{17,25},{25,17},{2,10},{10... | collective-permute-start | bytes 12296 | tf_op jit(solution)/shard_map/ppermute | solution.py:430
  46.3 23.2 %collective-permute-start.8 = (bf16[3,128,256]{2,1,0:T(8,128)(2,1)S(1)}, bf16[3,128,256]{2,1,0:T(8,128)(2,1)S(1)}, u32[]{:S(2)}, u32[]{:S(2)}) collective-permute-start(bf16[3,128,256]{2,1,0:T(8,128)(2,1)S(1)} %get-tuple-element.62), channel_id=1, source_target_pairs={{0,6},{2,4},{4,2},{6,0},{1,7},{3,5},{5,3},{7,1},{8,14},{10,12},{12... | collective-permute-start | bytes 589832 | tf_op jit(solution)/shard_map/ppermute | solution.py:430
  48.8 20.7 %collective-permute-start.9 = (bf16[3,128,256]{2,1,0:T(8,128)(2,1)S(1)}, bf16[3,128,256]{2,1,0:T(8,128)(2,1)S(1)}, u32[]{:S(2)}, u32[]{:S(2)}) collective-permute-start(bf16[3,128,256]{2,1,0:T(8,128)(2,1)S(1)} %get-tuple-element.63), channel_id=1, source_target_pairs={{0,4},{2,6},{4,0},{6,2},{1,5},{3,7},{5,1},{7,3},{8,12},{10,14},{12... | collective-permute-start | bytes 589832 | tf_op jit(solution)/shard_map/ppermute | solution.py:430
  53.8 10.4 %collective-permute-start.12 = (bf16[3,128,256]{2,1,0:T(8,128)(2,1)S(1)}, bf16[3,128,256]{2,1,0:T(8,128)(2,1)S(1)}, u32[]{:S(2)}, u32[]{:S(2)}) collective-permute-start(bf16[3,128,256]{2,1,0:T(8,128)(2,1)S(1)} %get-tuple-element.71), channel_id=1, source_target_pairs={{0,2},{2,0},{4,6},{6,4},{1,3},{3,1},{5,7},{7,5},{8,10},{10,8},{12,... | collective-permute-start | bytes 589832 | tf_op jit(solution)/shard_map/ppermute | solution.py:430
  53.8 6.9 %collective-permute-start.11 = (f32[16,128]{1,0:T(8,128)S(1)}, f32[16,128]{1,0:T(8,128)S(1)}, u32[]{:S(2)}, u32[]{:S(2)}) collective-permute-start(f32[16,128]{1,0:T(8,128)S(1)} %pad_maximum_fusion.1), channel_id=1, source_target_pairs={{0,16},{8,24},{16,0},{24,8},{1,17},{9,25},{17,1},{25,9},{2,18},{10... | collective-permute-start | bytes 24584 | tf_op jit(solution)/shard_map/ppermute | solution.py:430
  55.3 1.1 %copy-start = (bf16[1,1,256,1536]{3,2,1,0:T(8,128)(2,1)S(1)}, bf16[1,1,256,1536]{3,2,1,0:T(8,128)(2,1)}, u32[]{:S(2)}) copy-start(bf16[1,1,256,1536]{3,2,1,0:T(8,128)(2,1)} %param.7) | copy-start | bytes 2359300
  56.5 1.1 %copy-start.1 = (bf16[1,1,256,1536]{3,2,1,0:T(8,128)(2,1)S(1)}, bf16[1,1,256,1536]{3,2,1,0:T(8,128)(2,1)}, u32[]{:S(2)}) copy-start(bf16[1,1,256,1536]{3,2,1,0:T(8,128)(2,1)} %param.8) | copy-start | bytes 2359300
  57.6 1.1 %copy-start.2 = (bf16[1,1,256,1536]{3,2,1,0:T(8,128)(2,1)S(1)}, bf16[1,1,256,1536]{3,2,1,0:T(8,128)(2,1)}, u32[]{:S(2)}) copy-start(bf16[1,1,256,1536]{3,2,1,0:T(8,128)(2,1)} %param.9) | copy-start | bytes 2359300
  60.7 5.8 %collective-permute-start.15 = (f32[32,128]{1,0:T(8,128)S(1)}, f32[32,128]{1,0:T(8,128)S(1)}, u32[]{:S(2)}, u32[]{:S(2)}) collective-permute-start(f32[32,128]{1,0:T(8,128)S(1)} %pad_maximum_fusion.refs_7_), channel_id=1, source_target_pairs={{0,6},{2,4},{4,2},{6,0},{1,7},{3,5},{5,3},{7,1},{8,14},{10,12},{12... | collective-permute-start | bytes 49160 | tf_op jit(solution)/shard_map/ppermute | solution.py:430
  63.2 6.3 %collective-permute-start.14 = (f32[32,128]{1,0:T(8,128)S(1)}, f32[32,128]{1,0:T(8,128)S(1)}, u32[]{:S(2)}, u32[]{:S(2)}) collective-permute-start(f32[32,128]{1,0:T(8,128)S(1)} %pad_maximum_fusion.refs_7_), channel_id=1, source_target_pairs={{0,4},{2,6},{4,0},{6,2},{1,5},{3,7},{5,1},{7,3},{8,12},{10,14},{12... | collective-permute-start | bytes 49160 | tf_op jit(solution)/shard_map/ppermute | solution.py:430
  64.2 5.3 %collective-permute-start.13 = (f32[32,128]{1,0:T(8,128)S(1)}, f32[32,128]{1,0:T(8,128)S(1)}, u32[]{:S(2)}, u32[]{:S(2)}) collective-permute-start(f32[32,128]{1,0:T(8,128)S(1)} %pad_maximum_fusion.refs_7_), channel_id=1, source_target_pairs={{0,2},{2,0},{4,6},{6,4},{1,3},{3,1},{5,7},{7,5},{8,10},{10,8},{12,... | collective-permute-start | bytes 49160 | tf_op jit(solution)/shard_map/ppermute | solution.py:430

commit v10 on v9

--- a/solution.py
+++ b/solution.py
@@ -20,6 +20,10 @@
     return pl.CostEstimate(flops=int(microseconds * 1e8), bytes_accessed=0, transcendentals=0)
 
 
+def in_hbm(field):
+    return pltpu.with_memory_space_constraint(field, pltpu.HBM)
+
+
 def columns_dot(left, right):
     return lax.dot_general(
         left, right, (((1,), (1,)), ((), ())), preferred_element_type=jnp.float32
@@ -30,18 +34,18 @@
     return jnp.dot(left, right, preferred_element_type=jnp.float32)
 
 
-def partner(scalars, distance):
-    return jnp.bitwise_xor(scalars[0], distance)
-
-
-def forward_kernel(scalars, query_ref, key_ref, value_ref, weights_ref, *refs):
+def partner(axis, distance):
+    return distance if axis is None else jnp.bitwise_xor(lax.axis_index(axis), distance)
+
+
+def forward_kernel(axis, query_ref, key_ref, value_ref, weights_ref, *refs):
     (queries, key_rows, values, arrived), attended_refs = refs[-4:], refs[:-4]
     score_scale = HEAD_DIM ** (-0.5)
     groups, _, width = queries.shape
     own = width // HEAD_DIM
     copies = []
     for group in range(groups):
-        cols = pl.ds(pl.multiple_of(partner(scalars, group) * width, HEAD_DIM), width)
+        cols = pl.ds(pl.multiple_of(partner(axis, group) * width, HEAD_DIM), width)
         for field, (source, target) in enumerate(
             ((query_ref, queries), (key_ref, key_rows), (value_ref, values))
         ):
@@ -64,17 +68,14 @@
             attended_refs[group][head] = attended.astype(jnp.bfloat16)
 
 
-def forward(scalars, queries, key_rows, values, groups):
+def forward(axis, queries, key_rows, values, groups):
     patches, feat = queries.shape
     heads = feat // HEAD_DIM
     own = heads // groups
-    fields = [
-        pltpu.with_memory_space_constraint(field, pltpu.HBM) for field in (queries, key_rows, values)
-    ]
+    fields = [in_hbm(field) for field in (queries, key_rows, values)]
     weights, *attended = pl.pallas_call(
-        forward_kernel,
-        in_specs=[pl.BlockSpec(memory_space=pltpu.SMEM)]
-        + [pl.BlockSpec(memory_space=pltpu.HBM)] * 3,
+        functools.partial(forward_kernel, axis),
+        in_specs=[pl.BlockSpec(memory_space=pltpu.HBM)] * 3,
         out_specs=[pl.BlockSpec(memory_space=pltpu.VMEM)] * (1 + groups),
         scratch_shapes=[pltpu.VMEM((groups, patches, feat // groups), jnp.bfloat16)] * 3
         + [pltpu.SemaphoreType.DMA((groups, 3))],
@@ -83,15 +84,15 @@
         compiler_params=params(patches),
         cost_estimate=cost(6),
         name="spatial_forward",
-    )(scalars, *fields)
+    )(*fields)
     return weights, attended
 
 
-def backward_group(scalars, fields, weights_ref, grad_ref, distance, scratch, results, sent):
+def backward_group(axis, fields, weights_ref, grad_ref, distance, scratch, results, sent):
     query_ref, key_ref, value_ref = fields
     score_scale = HEAD_DIM ** (-0.5)
     own = grad_ref.shape[0]
-    start = partner(scalars, distance) * (own * HEAD_DIM)
+    start = partner(axis, distance) * (own * HEAD_DIM)
     columns = [
         pl.ds(pl.multiple_of(start + head * HEAD_DIM, HEAD_DIM), HEAD_DIM) for head in range(own)
     ]
@@ -117,14 +118,14 @@
     return copies
 
 
-def backward_kernel(distances, gains_of, scalars, *refs):
+def backward_kernel(axis, distances, gains_of, *refs):
     fields, weights_ref, refs = refs[:3], refs[3], refs[4:]
     grad_refs, refs = refs[: len(distances)], refs[len(distances) :]
     *refs, gq, gk, sent = refs
     copies = []
     if gains_of:
         *mixed_refs, gains_ref, _, _, gq_ref, gk_ref, grad_gains_ref, grad_gains = refs
-        gain_gradients(*gains_of, scalars, mixed_refs, gains_ref, grad_gains)
+        gain_gradients(axis, *gains_of, mixed_refs, gains_ref, grad_gains)
         copy = pltpu.make_async_copy(grad_gains, grad_gains_ref, sent.at[len(distances), 0])
         copy.start()
         copies.append(copy)
@@ -132,7 +133,7 @@
         gq_ref, gk_ref = refs
     for place, (distance, grad_ref) in enumerate(zip(distances, grad_refs)):
         copies += backward_group(
-            scalars,
+            axis,
             fields,
             weights_ref,
             grad_ref,
@@ -145,7 +146,7 @@
         copy.wait()
 
 
-def backward(scalars, fields, weights, grads, distances, earlier=(), mixed=(), gains=None, gains_of=()):
+def backward(axis, fields, weights, grads, distances, earlier=(), mixed=(), gains=None, gains_of=()):
     patches, feat = fields[0].shape
     own = grads[0].shape[0]
     operands = [*fields, weights, *grads] + ([*mixed, gains] if gains_of else [])
@@ -156,21 +157,20 @@
         out_shape.append(jax.ShapeDtypeStruct(gains.shape, jnp.float32))
         scratch.insert(0, pltpu.VMEM(gains.shape, jnp.float32))
     return pl.pallas_call(
-        functools.partial(backward_kernel, distances, gains_of),
-        in_specs=[pl.BlockSpec(memory_space=pltpu.SMEM)]
-        + [pl.BlockSpec(memory_space=pltpu.VMEM)] * len(operands)
+        functools.partial(backward_kernel, axis, distances, gains_of),
+        in_specs=[pl.BlockSpec(memory_space=pltpu.VMEM)] * len(operands)
         + [pl.BlockSpec(memory_space=pl.ANY)] * len(earlier),
         out_specs=[pl.BlockSpec(memory_space=pl.ANY)] * len(out_shape),
         scratch_shapes=scratch,
         out_shape=out_shape,
-        input_output_aliases={len(operands) + 1 + index: index for index in range(len(earlier))},
+        input_output_aliases={len(operands) + index: index for index in range(len(earlier))},
         compiler_params=params(patches),
         cost_estimate=cost(2),
         name="spatial_backward",
-    )(scalars, *operands, *earlier)
-
-
-def pack_kernel(scalars, field_ref, *refs):
+    )(*operands, *earlier)
+
+
+def pack_kernel(field_ref, *refs):
     *packed_refs, rows, arrived = refs
     chunks, size, _ = rows.shape
     spaces, _, width = packed_refs[0].shape
@@ -186,21 +186,18 @@
         copy.wait()
         for distance, packed_ref in enumerate(packed_refs):
             for space in range(spaces):
-                start = (space * len(packed_refs) + partner(scalars, distance)) * width
+                start = (space * len(packed_refs) + partner("tm", distance)) * width
                 cols = pl.ds(pl.multiple_of(start, HEAD_DIM), width)
                 packed_ref[space, pl.ds(chunk * size, size), :] = rows[chunk, :, cols]
 
 
-def pack(scalars, field, frames, spaces):
+def pack(field, frames, spaces):
     patches, feat = field.shape
     chunks = patches // GROUP
     shape = (spaces, patches, feat // (frames * spaces))
     return pl.pallas_call(
         pack_kernel,
-        in_specs=[
-            pl.BlockSpec(memory_space=pltpu.SMEM),
-            pl.BlockSpec(memory_space=pltpu.HBM),
-        ],
+        in_specs=[pl.BlockSpec(memory_space=pltpu.HBM)],
         out_specs=[pl.BlockSpec(memory_space=pltpu.VMEM)] * frames,
         out_shape=[jax.ShapeDtypeStruct(shape, field.dtype)] * frames,
         scratch_shapes=[
@@ -210,18 +207,23 @@
         compiler_params=params(patches),
         cost_estimate=cost(1),
         name="pack_cotangent",
-    )(scalars, pltpu.with_memory_space_constraint(field, pltpu.HBM))
-
-
-def turn_kernel(frames, scalars, *refs):
-    piece_refs, (own_ref, *other_refs), turned = refs[:frames], refs[frames:-1], refs[-1]
+    )(in_hbm(field))
+
+
+def turn_kernel(frames, *refs):
+    piece_refs, (plane_ref, plane_out_ref, own_ref, *other_refs), turned = (
+        refs[:frames][::-1],
+        refs[frames:-1],
+        refs[-1],
+    )
+    plane_out_ref[...] = plane_ref[...]
     spaces = piece_refs[0].shape[0]
     heads = own_ref.shape[1]
     for space in range(spaces):
         target = turned if space else own_ref
-        source = jnp.bitwise_xor(scalars[1], space)
+        source = partner("space", space)
         for distance, ref in enumerate(piece_refs):
-            frame = partner(scalars, distance)
+            frame = partner("tm", distance)
             for head in range(heads):
                 cols = pl.ds(head * HEAD_DIM, HEAD_DIM)
                 target[frame, head] = ref[source, :, cols].T
@@ -231,22 +233,22 @@
             other_refs[2 * space - 1][...] = turned[half:]
 
 
-def turn(scalars, pieces):
+def turn(pieces, plane):
     spaces, patches, feat = pieces[0].shape
     frames, heads = len(pieces), feat // HEAD_DIM
     turned = (heads, HEAD_DIM, patches)
     sizes = [frames] + [frames // 2, frames - frames // 2] * (spaces - 1)
     return pl.pallas_call(
         functools.partial(turn_kernel, frames),
-        in_specs=[pl.BlockSpec(memory_space=pltpu.SMEM)]
-        + [pl.BlockSpec(memory_space=pltpu.VMEM)] * frames,
-        out_specs=[pl.BlockSpec(memory_space=pltpu.VMEM)] * len(sizes),
-        out_shape=[jax.ShapeDtypeStruct((size,) + turned, pieces[0].dtype) for size in sizes],
+        in_specs=[pl.BlockSpec(memory_space=pltpu.VMEM)] * (frames + 1),
+        out_specs=[pl.BlockSpec(memory_space=pltpu.VMEM)] * (len(sizes) + 1),
+        out_shape=[jax.ShapeDtypeStruct(plane.shape, plane.dtype)]
+        + [jax.ShapeDtypeStruct((size,) + turned, pieces[0].dtype) for size in sizes],
         scratch_shapes=[pltpu.VMEM((frames,) + turned, pieces[0].dtype)],
         compiler_params=params(patches),
         cost_estimate=cost(2),
         name="turn_cotangent",
-    )(scalars, *pieces)
+    )(*reversed(pieces), plane)
 
 
 def temporal_part(length, attended_ref, load_upstream, load_gain, grad_ref):
@@ -339,16 +341,26 @@
     return jnp.concatenate(all_mixed, axis=0)
 
 
-def temporal_kernel(frames, spaces, scalars, *refs):
+def temporal_kernel(frames, spaces, length_ref, task_ref, *refs):
     attended_refs, (gain_ref, own_ref, *other_refs), refs = (
-        refs[:frames],
+        (refs[frames - 1], *refs[: frames - 1]),
         refs[frames : frames + 2 * spaces],
         refs[frames + 2 * spaces :],
     )
-    grad_refs, (mixed_ref, attended, grads) = refs[:frames], refs[frames:]
+    field_refs, grad_refs, (mixed_ref, *kept_refs, attended, grads, arrived) = (
+        refs[:3],
+        refs[3 : frames + 3],
+        refs[frames + 3 :],
+    )
+    copies = [
+        pltpu.make_async_copy(source, target, arrived.at[index])
+        for index, (source, target) in enumerate(zip(field_refs, kept_refs))
+    ]
+    for copy in copies:
+        copy.start()
     heads, lanes = own_ref.shape[1], own_ref.shape[3]
     half = frames // 2
-    mixed_ref[...] = jnp.full(mixed_ref.shape, scalars[3].astype(jnp.float32))
+    mixed_ref[...] = jnp.full(mixed_ref.shape, task_ref[0].astype(jnp.float32))
 
     def load_upstream(space, head, t, rows):
         if space == 0:
@@ -357,16 +369,16 @@
 
     def step(head, carry):
         places = [
-            pl.ds(pl.multiple_of(jnp.bitwise_xor(scalars[1], space) * lanes, lanes), lanes)
+            pl.ds(pl.multiple_of(partner("space", space) * lanes, lanes), lanes)
             for space in range(spaces)
         ]
         for distance, ref in enumerate(attended_refs):
-            frame = partner(scalars, distance)
+            frame = partner("tm", distance)
             for space, here in enumerate(places):
                 attended[space, frame] = ref[head, :, here]
         mixed = [
             temporal_part(
-                scalars[2],
+                length_ref[0],
                 attended.at[space],
                 functools.partial(load_upstream, space, head),
                 lambda rows: gain_ref[head, rows, :],
@@ -377,36 +389,41 @@
         summed = functools.reduce(jnp.add, mixed)
         mixed_ref[pl.ds(head, 1), :] = jnp.sum(summed.T, axis=0, keepdims=True) * 0.5
         for distance, ref in enumerate(grad_refs):
-            frame = partner(scalars, distance)
+            frame = partner("tm", distance)
             for space, here in enumerate(places):
                 ref[head, :, here] = grads[space, frame]
         return carry
 
     lax.fori_loop(0, heads, step, 0)
-
-
-def temporal(scalars, attended, upstream, gain):
+    for copy in copies:
+        copy.wait()
+
+
+def temporal(lengths, task_ids, attended, upstream, gain, fields):
     frames, heads, feat, lanes = upstream[0].shape
     spaces = (len(upstream) + 1) // 2
     patches = spaces * lanes
     rows = -(-(heads + 1) // 8) * 8
-    operands = [*attended, gain, *upstream]
-    *grads, mixed = pl.pallas_call(
+    operands = [*attended[1:], attended[0], gain, *upstream]
+    results = pl.pallas_call(
         functools.partial(temporal_kernel, frames, spaces),
-        in_specs=[pl.BlockSpec(memory_space=pltpu.SMEM)]
-        + [pl.BlockSpec(memory_space=pltpu.VMEM)] * len(operands),
-        out_specs=[pl.BlockSpec(memory_space=pltpu.VMEM)] * (frames + 1),
-        scratch_shapes=[pltpu.VMEM((spaces, frames, feat, lanes), jnp.bfloat16)] * 2,
+        in_specs=[pl.BlockSpec(memory_space=pltpu.SMEM)] * 2
+        + [pl.BlockSpec(memory_space=pltpu.VMEM)] * len(operands)
+        + [pl.BlockSpec(memory_space=pltpu.HBM)] * len(fields),
+        out_specs=[pl.BlockSpec(memory_space=pltpu.VMEM)] * (frames + 1 + len(fields)),
+        scratch_shapes=[pltpu.VMEM((spaces, frames, feat, lanes), jnp.bfloat16)] * 2
+        + [pltpu.SemaphoreType.DMA((len(fields),))],
         out_shape=[jax.ShapeDtypeStruct((heads, feat, patches), jnp.bfloat16)] * frames
-        + [jax.ShapeDtypeStruct((rows, feat), jnp.float32)],
+        + [jax.ShapeDtypeStruct((rows, feat), jnp.float32)]
+        + [jax.ShapeDtypeStruct(field.shape, field.dtype) for field in fields],
         compiler_params=params(patches),
         cost_estimate=cost(4),
         name="temporal",
-    )(scalars, *operands)
-    return grads, mixed
-
-
-def gain_gradients(heads, frames, clips, scalars, mixed_refs, gains_ref, grad_ref):
+    )(lengths, task_ids, *operands, *[in_hbm(field) for field in fields])
+    return list(results[:frames]), results[frames], results[frames + 1 :]
+
+
+def gain_gradients(axis, heads, frames, clips, mixed_refs, gains_ref, grad_ref):
     tasks = gains_ref.shape[1]
     rows = sum(ref.shape[0] for ref in mixed_refs) // (frames * clips)
     each = mixed_refs[0].shape[0] // rows
@@ -420,7 +437,7 @@
                 task = ref[pl.ds(start + heads, 1), :]
                 row = ref[pl.ds(start + head, 1), :]
                 mixed = mixed + jnp.where(task_ids == task, row, 0.0)
-            start = (partner(scalars, distance) * heads + head) * HEAD_DIM
+            start = (partner(axis, distance) * heads + head) * HEAD_DIM
             cols = pl.ds(pl.multiple_of(start, HEAD_DIM), HEAD_DIM)
             grad_ref[0, :, cols] = gains_ref[1, :, cols] * mixed
             grad_ref[1, :, cols] = gains_ref[0, :, cols] * mixed
@@ -440,19 +457,18 @@
     queries, key_rows, values = (
         field.reshape(patches, feat) for field in (query_heads, key_heads, value_heads)
     )
-    frame, space = lax.axis_index("tm"), lax.axis_index("space")
-    scalars = jnp.stack([frame, space, lengths[0], task_ids[0]]).astype(jnp.int32)
-
-    pieces = pack(scalars, cotangent.reshape(cotangent.shape[2:]), frames, spaces)
-    queries, pieces = lax.optimization_barrier((queries, list(pieces)))
+    frame = lax.axis_index("tm")
+
+    pieces = list(pack(cotangent.reshape(cotangent.shape[2:]), frames, spaces))
+    queries, pieces = lax.optimization_barrier((queries, pieces))
     for distance in range(1, frames):
         pieces[distance] = swap(pieces[distance], "tm", frames, distance)
     fields = (queries, key_rows, values)
-    weights, attended = forward(scalars, *fields, frames)
+    weights, attended = forward("tm", *fields, frames)
     for distance in range(1, frames):
         attended[distance] = swap(attended[distance], "tm", frames, distance)
-    pieces, _ = lax.optimization_barrier((pieces, weights))
-    upstream = list(turn(scalars, pieces))
+    backwards, _ = lax.optimization_barrier((pieces[::-1], weights))
+    attended[0], *upstream = turn(backwards[::-1], attended[0])
     for index in range(1, len(upstream)):
         upstream[index] = swap(upstream[index], "space", spaces, (index + 1) // 2)
     rows = lax.dynamic_index_in_dim(gains, task_ids[0], 1, keepdims=False)
@@ -460,7 +476,7 @@
     gain = jnp.broadcast_to(
         product.reshape(own, HEAD_DIM, 1), (own, HEAD_DIM, patches // spaces)
     )
-    grads, mixed = temporal(scalars, attended, upstream, gain)
+    grads, mixed, kept = temporal(lengths, task_ids, attended, upstream, gain, fields)
     for distance in reversed(range(1, frames)):
         grads[distance] = swap(grads[distance], "tm", frames, distance)
     here = grads[0]
@@ -469,15 +485,15 @@
         if bit == 0:
             here, other = lax.optimization_barrier((here, other))
         mixed = jnp.concatenate([mixed, other], axis=0)
-    results = backward(scalars, fields, weights, [here], [0])
+    results = backward("tm", kept, weights, [here], [0])
     mixed, results = lax.optimization_barrier((mixed, results))
     near, grads[1] = lax.optimization_barrier((mixed, grads[1]))
     mixed = [mixed, swap(near, "tm", frames, 1)] + [
         swap(mixed, "tm", frames, distance) for distance in range(2, frames)
     ]
     grad_queries, grad_keys, grad_gains = backward(
-        scalars,
-        fields,
+        "tm",
+        kept,
         weights,
         grads[:0:-1],
         list(range(frames - 1, 0, -1)),
@@ -535,9 +551,8 @@
     queries, key_rows, values = (
         field.reshape(patches, feat) for field in (query_heads, key_heads, value_heads)
     )
-    scalars = jnp.zeros((1,), jnp.int32)
     fields = (queries, key_rows, values)
-    weights, attended = forward(scalars, *fields, 1)
+    weights, attended = forward(None, *fields, 1)
     attended_field = jnp.transpose(attended[0], (2, 0, 1)).reshape(1, 1, patches, feat)
     upstream = lax.all_to_all(
         lax.all_to_all(cotangent, "space", split_axis=3, concat_axis=2, tiled=True),
@@ -573,7 +588,7 @@
         tiled=True,
     )
     head_grads = jnp.transpose(returned.reshape(patches, heads, HEAD_DIM), (1, 2, 0))
-    grad_queries, grad_keys = backward(scalars, fields, weights, [head_grads], [0])
+    grad_queries, grad_keys = backward(None, fields, weights, [head_grads], [0])
     return (
         grad_queries.reshape(query_heads.shape),
         grad_keys.reshape(query_heads.shape),

time: 72.9 us -> 68.8 us (0.944)
  local copies, waits for them, and re-layouts: 4.44 us -> 1.7 us
  Pallas kernels: 19.5 us -> 16.8 us
  waiting for transfers between devices: 20 us -> 21.9 us
    unnamed x12 -> x6, local copies, waits for them, and re-layouts: 4.33 us -> 1.6 us
    pallas_call x4, Pallas kernels: 13.8 us -> 11.7 us  [the longest x1 6.52 us: forward(): pl.pallas_call(functools.partial(forward_kernel, axis), in_specs=[pl.Bloc...]
    ppermute x16, waiting for transfers between devices: 20 us -> 21.9 us  [swap(): return lax.ppermute(field, axis, [(i, i ^ distance) for i in range(size)])]
  transfers between devices with their start and end apart: 16 -> 16, of which waited for: 4 -> 5; matrix products, arithmetic and copies ran while one was open for 1% -> 1% of each run, Pallas kernels for 15% -> 13%
where the time goes in v10:
time: 68.8 us; the launch traced here: 68.4 us
  starting transfers between devices  25.1 us (36%)
  waiting for transfers between devices  21.9 us (32%)
  Pallas kernels  16.8 us (24%)
  between operations  2.04 us (3%)
  local copies, waits for them, and re-layouts  1.7 us (2%)
  other arithmetic  0.82 us (1%)
    ppermute x16, starting transfers between devices, swap(): return lax.ppermute(field, axis, [(i, i ^ distance) for i in range(size)])  25.1 us
    ppermute x16, waiting for transfers between devices, swap(): return lax.ppermute(field, axis, [(i, i ^ distance) for i in range(size)])  21.9 us
    pallas_call x1, Pallas kernels, forward(): pl.pallas_call(functools.partial(forward_kernel, axis), in_specs=[pl.Bloc...  6.52 us
    pallas_call x1, Pallas kernels, temporal(): pl.pallas_call(functools.partial(temporal_kernel, frames, spaces), in_spe...  4.11 us
    pallas_call x2, Pallas kernels, backward(): pl.pallas_call(functools.partial(backward_kernel, axis, distances, gains_...  3.87 us
    unnamed x6, local copies, waits for them, and re-layouts  1.6 us
  transfers between devices with their start and end apart: 16, of which 5 were waited for; matrix products, arithmetic and copies ran while one was open for 1% of the time, Pallas kernels for 13%

profile of v10, /device:TPU:0, one launch (start us, length us, event | category | flops | bytes accessed | tf_op | source)
XLA Modules:
  0.0 68.4 jit_solution(1033394442094192243)
XLA Ops:
  0.6 1.3 %pack_cotangent.1 = (bf16[2,128,384]{2,1,0:T(8,128)(2,1)S(1)}, bf16[2,128,384]{2,1,0:T(8,128)(2,1)S(1)}, bf16[2,128,384]{2,1,0:T(8,128)(2,1)S(1)}, bf16[2,128,384]{2,1,0:T(8,128)(2,1)S(1)}) custom-call(bf16[128,3072]{1,0:T(8,128)(2,1)} %bitcast.17), custom_call_target="tpu_custom_call" | custom-call | flops 100000000 | tf_op jit(solution)/shard_map/pack_cotangent/pallas_call | solution.py:198
  1.9 5.1 %collective-permute-start.3 = (bf16[2,128,384]{2,1,0:T(8,128)(2,1)S(1)}, bf16[2,128,384]{2,1,0:T(8,128)(2,1)S(1)}, u32[]{:S(2)}, u32[]{:S(2)}) collective-permute-start(bf16[2,128,384]{2,1,0:T(8,128)(2,1)S(1)} %get-tuple-element.53), channel_id=1, source_target_pairs={{0,6},{2,4},{4,2},{6,0},{1,7},{3,5},{5,3},{7,1},{8,14},{10,12},{12... | collective-permute-start | bytes 589832 | tf_op jit(solution)/shard_map/ppermute | solution.py:447
  7.7 6.5 %spatial_forward.1 = (f32[12,256,256]{2,1,0:T(8,128)S(1)}, bf16[3,128,256]{2,1,0:T(8,128)(2,1)S(1)}, bf16[3,128,256]{2,1,0:T(8,128)(2,1)}, bf16[3,128,256]{2,1,0:T(8,128)(2,1)}, bf16[3,128,256]{2,1,0:T(8,128)(2,1)}) custom-call(bf16[256,1536]{1,0:T(8,128)(2,1)} %bitcast.11, bf16[256,1536]{1,0:T(8,128)(2,1)} %bitcast.13, bf16[256,1536]{1,0:T(8,128)(2,1)} %bitcast.15), custom_call_target="tpu_custom_call" | custom-call | flops 600000000 | tf_op jit(solution)/shard_map/spatial_forward/pallas_call | solution.py:76
  14.2 1.4 %collective-permute-start = (bf16[3,128,256]{2,1,0:T(8,128)(2,1)}, bf16[3,128,256]{2,1,0:T(8,128)(2,1)}, u32[]{:S(2)}, u32[]{:S(2)}) collective-permute-start(bf16[3,128,256]{2,1,0:T(8,128)(2,1)} %get-tuple-element.50), channel_id=1, source_target_pairs={{0,2},{2,0},{4,6},{6,4},{1,3},{3,1},{5,7},{7,5},{8,10},{10,8},{12,... | collective-permute-start | bytes 589832 | tf_op jit(solution)/shard_map/ppermute | solution.py:447
  15.7 2.9 %collective-permute-start.1 = (bf16[3,128,256]{2,1,0:T(8,128)(2,1)}, bf16[3,128,256]{2,1,0:T(8,128)(2,1)}, u32[]{:S(2)}, u32[]{:S(2)}) collective-permute-start(bf16[3,128,256]{2,1,0:T(8,128)(2,1)} %get-tuple-element.51), channel_id=1, source_target_pairs={{0,4},{2,6},{4,0},{6,2},{1,5},{3,7},{5,1},{7,3},{8,12},{10,14},{12... | collective-permute-start | bytes 589832 | tf_op jit(solution)/shard_map/ppermute | solution.py:447
  18.7 6.9 %collective-permute-done.4.refs_1_ = bf16[2,128,384]{2,1,0:T(8,128)(2,1)S(1)} collective-permute-done((bf16[2,128,384]{2,1,0:T(8,128)(2,1)S(1)}, bf16[2,128,384]{2,1,0:T(8,128)(2,1)S(1)}, u32[]{:S(2)}, u32[]{:S(2)}) %collective-permute-start.4) | collective-permute-done | bytes 196640 | tf_op jit(solution)/shard_map/ppermute | solution.py:447
  25.6 1.1 %turn_cotangent.1 = (bf16[3,128,256]{2,1,0:T(8,128)(2,1)S(1)}, bf16[4,3,128,128]{3,2,1,0:T(8,128)(2,1)S(1)}, bf16[2,3,128,128]{3,2,1,0:T(8,128)(2,1)}, bf16[2,3,128,128]{3,2,1,0:T(8,128)(2,1)}) custom-call(bf16[2,128,384]{2,1,0:T(8,128)(2,1)S(1)} %collective-permute-done.3.refs_0_, bf16[2,128,384]{2,1,0:T(8,128)(2,1)S(1)} %collective-permute-done.4.refs_1_, ...), custom_call_target="tpu_custom_call" | custom-call | flops 200000000 | tf_op jit(solution)/shard_map/turn_cotangent/pallas_call | solution.py:241
  26.6 0.7 copy-done.1
  27.3 1.7 %collective-permute-start.6 = (bf16[2,3,128,128]{3,2,1,0:T(8,128)(2,1)}, bf16[2,3,128,128]{3,2,1,0:T(8,128)(2,1)}, u32[]{:S(2)}, u32[]{:S(2)}) collective-permute-start(bf16[2,3,128,128]{3,2,1,0:T(8,128)(2,1)} %get-tuple-element.65), channel_id=1, source_target_pairs={{0,1},{1,0},{2,3},{3,2},{4,5},{5,4},{6,7},{7,6},{8,9},{9,8},{10,11... | collective-permute-start | bytes 589832 | tf_op jit(solution)/shard_map/ppermute | solution.py:447
  30.6 0.8 %fusion = f32[384]{0:T(512)S(1)} fusion(f32[2,16,1536]{2,1,0:T(8,128)} %refs_11_.1, s32[]{:T(128)S(6)} %add.10, s32[]{:T(128)S(6)} %select_n.7, s32[]{:T(128)S(6)} %select_n.8), kind=kLoop, calls=%fused_computation.3 | loop fusion | flops 384 | bytes 4620 | tf_op jit(solution)/shard_map/dynamic_slice | solution.py:475
  31.5 6.0 %collective-permute-done.1.refs_1_ = bf16[3,128,256]{2,1,0:T(8,128)(2,1)} collective-permute-done((bf16[3,128,256]{2,1,0:T(8,128)(2,1)}, bf16[3,128,256]{2,1,0:T(8,128)(2,1)}, u32[]{:S(2)}, u32[]{:S(2)}) %collective-permute-start.1) | collective-permute-done | bytes 196640 | tf_op jit(solution)/shard_map/ppermute | solution.py:447
  37.6 0.9 %copy-done.2 = bf16[3,128,256]{2,1,0:T(8,128)(2,1)S(1)} copy-done((bf16[3,128,256]{2,1,0:T(8,128)(2,1)S(1)}, bf16[3,128,256]{2,1,0:T(8,128)(2,1)}, u32[]{:S(2)}) %copy-start.2) | copy-done | bytes 196632
  38.5 4.1 %temporal.1 = (bf16[3,128,256]{2,1,0:T(8,128)(2,1)S(1)}, bf16[3,128,256]{2,1,0:T(8,128)(2,1)S(1)}, bf16[3,128,256]{2,1,0:T(8,128)(2,1)S(1)}, bf16[3,128,256]{2,1...) custom-call(s32[1]{0:T(128)S(6)} %copy.15.length_ref, ...), custom_call_target="tpu_custom_call" | custom-call | flops 400000000 | tf_op jit(solution)/shard_map/temporal/pallas_call | solution.py:408
  42.8 2.7 %collective-permute-start.8 = (bf16[3,128,256]{2,1,0:T(8,128)(2,1)S(1)}, bf16[3,128,256]{2,1,0:T(8,128)(2,1)S(1)}, u32[]{:S(2)}, u32[]{:S(2)}) collective-permute-start(bf16[3,128,256]{2,1,0:T(8,128)(2,1)S(1)} %get-tuple-element.70), channel_id=1, source_target_pairs={{0,6},{2,4},{4,2},{6,0},{1,7},{3,5},{5,3},{7,1},{8,14},{10,12},{12... | collective-permute-start | bytes 589832 | tf_op jit(solution)/shard_map/ppermute | solution.py:447
  45.5 2.6 %collective-permute-start.9 = (bf16[3,128,256]{2,1,0:T(8,128)(2,1)S(1)}, bf16[3,128,256]{2,1,0:T(8,128)(2,1)S(1)}, u32[]{:S(2)}, u32[]{:S(2)}) collective-permute-start(bf16[3,128,256]{2,1,0:T(8,128)(2,1)S(1)} %get-tuple-element.71), channel_id=1, source_target_pairs={{0,4},{2,6},{4,0},{6,2},{1,5},{3,7},{5,1},{7,3},{8,12},{10,14},{12... | collective-permute-start | bytes 589832 | tf_op jit(solution)/shard_map/ppermute | solution.py:447
  48.2 1.5 %collective-permute-start.11 = (f32[16,128]{1,0:T(8,128)S(1)}, f32[16,128]{1,0:T(8,128)S(1)}, u32[]{:S(2)}, u32[]{:S(2)}) collective-permute-start(f32[16,128]{1,0:T(8,128)S(1)} %pad_maximum_fusion.1), channel_id=1, source_target_pairs={{0,16},{8,24},{16,0},{24,8},{1,17},{9,25},{17,1},{25,9},{2,18},{10... | collective-permute-start | bytes 24584 | tf_op jit(solution)/shard_map/ppermute | solution.py:447
  49.7 1.4 %spatial_backward.2 = (bf16[256,1536]{1,0:T(8,128)(2,1)}, bf16[256,1536]{1,0:T(8,128)(2,1)}) custom-call(bf16[256,1536]{1,0:T(8,128)(2,1)S(1)} %get-tuple-element.67.refs_0_, bf16[256,1536]{1,0:T(8,128)(2,1)S(1)} %get-tuple-element.68.refs_1_, bf16[256,1536]{1,0:T(8,128)(2,1)S(1)} %get-tuple-element.69.refs_2_, ...), custom_call_target="tpu_custom_call" | custom-call | flops 200000000 | tf_op jit(solution)/shard_map/spatial_backward/pallas_call | solution.py:159
  51.1 0.7 %collective-permute-done.11 = f32[16,128]{1,0:T(8,128)S(1)} collective-permute-done((f32[16,128]{1,0:T(8,128)S(1)}, f32[16,128]{1,0:T(8,128)S(1)}, u32[]{:S(2)}, u32[]{:S(2)}) %collective-permute-start.11) | collective-permute-done | bytes 8224 | tf_op jit(solution)/shard_map/ppermute | solution.py:447
  51.9 2.4 %collective-permute-start.15 = (f32[32,128]{1,0:T(8,128)S(1)}, f32[32,128]{1,0:T(8,128)S(1)}, u32[]{:S(2)}, u32[]{:S(2)}) collective-permute-start(f32[32,128]{1,0:T(8,128)S(1)} %pad_maximum_fusion.refs_7_), channel_id=1, source_target_pairs={{0,6},{2,4},{4,2},{6,0},{1,7},{3,5},{5,3},{7,1},{8,14},{10,12},{12... | collective-permute-start | bytes 49160 | tf_op jit(solution)/shard_map/ppermute | solution.py:447
  54.3 0.9 %collective-permute-start.14 = (f32[32,128]{1,0:T(8,128)S(1)}, f32[32,128]{1,0:T(8,128)S(1)}, u32[]{:S(2)}, u32[]{:S(2)}) collective-permute-start(f32[32,128]{1,0:T(8,128)S(1)} %pad_maximum_fusion.refs_7_), channel_id=1, source_target_pairs={{0,4},{2,6},{4,0},{6,2},{1,5},{3,7},{5,1},{7,3},{8,12},{10,14},{12... | collective-permute-start | bytes 49160 | tf_op jit(solution)/shard_map/ppermute | solution.py:447
  55.2 3.8 %collective-permute-done.12.refs_6_ = bf16[3,128,256]{2,1,0:T(8,128)(2,1)S(1)} collective-permute-done((bf16[3,128,256]{2,1,0:T(8,128)(2,1)S(1)}, bf16[3,128,256]{2,1,0:T(8,128)(2,1)S(1)}, u32[]{:S(2)}, u32[]{:S(2)}) %collective-permute-start.12) | collective-permute-done | bytes 196640 | tf_op jit(solution)/shard_map/ppermute | solution.py:447
  59.1 2.5 %collective-permute-start.13 = (f32[32,128]{1,0:T(8,128)S(1)}, f32[32,128]{1,0:T(8,128)S(1)}, u32[]{:S(2)}, u32[]{:S(2)}) collective-permute-start(f32[32,128]{1,0:T(8,128)S(1)} %pad_maximum_fusion.refs_7_), channel_id=1, source_target_pairs={{0,2},{2,0},{4,6},{6,4},{1,3},{3,1},{5,7},{7,5},{8,10},{10,8},{12,... | collective-permute-start | bytes 49160 | tf_op jit(solution)/shard_map/ppermute | solution.py:447
  61.6 4.4 %collective-permute-done.14.refs_9_ = f32[32,128]{1,0:T(8,128)S(1)} collective-permute-done((f32[32,128]{1,0:T(8,128)S(1)}, f32[32,128]{1,0:T(8,128)S(1)}, u32[]{:S(2)}, u32[]{:S(2)}) %collective-permute-start.14) | collective-permute-done | bytes 16416 | tf_op jit(solution)/shard_map/ppermute | solution.py:447
  66.0 2.5 %spatial_backward.3 = (bf16[256,1536]{1,0:T(8,128)(2,1)}, bf16[256,1536]{1,0:T(8,128)(2,1)}, f32[2,16,1536]{2,1,0:T(8,128)}) custom-call(bf16[256,1536]{1,0:T(8,128)(2,1)S(1)} %get-tuple-element.67.refs_0_, bf16[256,1536]{1,0:T(8,128)(2,1)S(1)} %get-tuple-element.68.refs_1_, ...), custom_call_target="tpu_custom_call", output_to_operand_aliasing={{0}: (12, {}), {1}: (13, {})} | custom-call | flops 200000000 | tf_op jit(solution)/shard_map/spatial_backward/pallas_call | solution.py:159
  (24 shorter events, 1.4 us)
Async XLA Ops:
  1.9 16.7 %collective-permute-start.3 = (bf16[2,128,384]{2,1,0:T(8,128)(2,1)S(1)}, bf16[2,128,384]{2,1,0:T(8,128)(2,1)S(1)}, u32[]{:S(2)}, u32[]{:S(2)}) collective-permute-start(bf16[2,128,384]{2,1,0:T(8,128)(2,1)S(1)} %get-tuple-element.53), channel_id=1, source_target_pairs={{0,6},{2,4},{4,2},{6,0},{1,7},{3,5},{5,3},{7,1},{8,14},{10,12},{12... | collective-permute-start | bytes 589832 | tf_op jit(solution)/shard_map/ppermute | solution.py:447
  7.0 18.5 %collective-permute-start.4 = (bf16[2,128,384]{2,1,0:T(8,128)(2,1)S(1)}, bf16[2,128,384]{2,1,0:T(8,128)(2,1)S(1)}, u32[]{:S(2)}, u32[]{:S(2)}) collective-permute-start(bf16[2,128,384]{2,1,0:T(8,128)(2,1)S(1)} %get-tuple-element.54), channel_id=1, source_target_pairs={{0,4},{2,6},{4,0},{6,2},{1,5},{3,7},{5,1},{7,3},{8,12},{10,14},{12... | collective-permute-start | bytes 589832 | tf_op jit(solution)/shard_map/ppermute | solution.py:447
  7.0 18.5 %collective-permute-start.5 = (bf16[2,128,384]{2,1,0:T(8,128)(2,1)S(1)}, bf16[2,128,384]{2,1,0:T(8,128)(2,1)S(1)}, u32[]{:S(2)}, u32[]{:S(2)}) collective-permute-start(bf16[2,128,384]{2,1,0:T(8,128)(2,1)S(1)} %get-tuple-element.55), channel_id=1, source_target_pairs={{0,2},{2,0},{4,6},{6,4},{1,3},{3,1},{5,7},{7,5},{8,10},{10,8},{12,... | collective-permute-start | bytes 589832 | tf_op jit(solution)/shard_map/ppermute | solution.py:447
  14.2 17.2 %collective-permute-start = (bf16[3,128,256]{2,1,0:T(8,128)(2,1)}, bf16[3,128,256]{2,1,0:T(8,128)(2,1)}, u32[]{:S(2)}, u32[]{:S(2)}) collective-permute-start(bf16[3,128,256]{2,1,0:T(8,128)(2,1)} %get-tuple-element.50), channel_id=1, source_target_pairs={{0,2},{2,0},{4,6},{6,4},{1,3},{3,1},{5,7},{7,5},{8,10},{10,8},{12,... | collective-permute-start | bytes 589832 | tf_op jit(solution)/shard_map/ppermute | solution.py:447
  15.7 21.8 %collective-permute-start.1 = (bf16[3,128,256]{2,1,0:T(8,128)(2,1)}, bf16[3,128,256]{2,1,0:T(8,128)(2,1)}, u32[]{:S(2)}, u32[]{:S(2)}) collective-permute-start(bf16[3,128,256]{2,1,0:T(8,128)(2,1)} %get-tuple-element.51), channel_id=1, source_target_pairs={{0,4},{2,6},{4,0},{6,2},{1,5},{3,7},{5,1},{7,3},{8,12},{10,14},{12... | collective-permute-start | bytes 589832 | tf_op jit(solution)/shard_map/ppermute | solution.py:447
  18.6 18.9 %collective-permute-start.2 = (bf16[3,128,256]{2,1,0:T(8,128)(2,1)}, bf16[3,128,256]{2,1,0:T(8,128)(2,1)}, u32[]{:S(2)}, u32[]{:S(2)}) collective-permute-start(bf16[3,128,256]{2,1,0:T(8,128)(2,1)} %get-tuple-element.52), channel_id=1, source_target_pairs={{0,6},{2,4},{4,2},{6,0},{1,7},{3,5},{5,3},{7,1},{8,14},{10,12},{12... | collective-permute-start | bytes 589832 | tf_op jit(solution)/shard_map/ppermute | solution.py:447
  26.6 0.7 copy-start.1
  27.3 10.2 %collective-permute-start.6 = (bf16[2,3,128,128]{3,2,1,0:T(8,128)(2,1)}, bf16[2,3,128,128]{3,2,1,0:T(8,128)(2,1)}, u32[]{:S(2)}, u32[]{:S(2)}) collective-permute-start(bf16[2,3,128,128]{3,2,1,0:T(8,128)(2,1)} %get-tuple-element.65), channel_id=1, source_target_pairs={{0,1},{1,0},{2,3},{3,2},{4,5},{5,4},{6,7},{7,6},{8,9},{9,8},{10,11... | collective-permute-start | bytes 589832 | tf_op jit(solution)/shard_map/ppermute | solution.py:447
  29.0 8.5 %collective-permute-start.7 = (bf16[2,3,128,128]{3,2,1,0:T(8,128)(2,1)}, bf16[2,3,128,128]{3,2,1,0:T(8,128)(2,1)}, u32[]{:S(2)}, u32[]{:S(2)}) collective-permute-start(bf16[2,3,128,128]{3,2,1,0:T(8,128)(2,1)} %get-tuple-element.66), channel_id=1, source_target_pairs={{0,1},{1,0},{2,3},{3,2},{4,5},{5,4},{6,7},{7,6},{8,9},{9,8},{10,11... | collective-permute-start | bytes 589832 | tf_op jit(solution)/shard_map/ppermute | solution.py:447
  37.6 0.9 %copy-start.2 = (bf16[3,128,256]{2,1,0:T(8,128)(2,1)S(1)}, bf16[3,128,256]{2,1,0:T(8,128)(2,1)}, u32[]{:S(2)}) copy-start(bf16[3,128,256]{2,1,0:T(8,128)(2,1)} %copy-done.1) | copy-start | bytes 589828
  42.7 23.3 %copy-start = (f32[2,16,1536]{2,1,0:T(8,128)S(1)}, f32[2,16,1536]{2,1,0:T(8,128)}, u32[]{:S(2)}) copy-start(f32[2,16,1536]{2,1,0:T(8,128)} %refs_11_.1) | copy-start | bytes 589828
  42.7 5.5 %collective-permute-start.10 = (f32[8,128]{1,0:T(8,128)S(1)}, f32[8,128]{1,0:T(8,128)S(1)}, u32[]{:S(2)}, u32[]{:S(2)}) collective-permute-start(f32[8,128]{1,0:T(8,128)S(1)} %get-tuple-element.72), channel_id=1, source_target_pairs={{0,8},{8,0},{16,24},{24,16},{1,9},{9,1},{17,25},{25,17},{2,10},{10... | collective-permute-start | bytes 12296 | tf_op jit(solution)/shard_map/ppermute | solution.py:447
  42.8 23.2 %collective-permute-start.8 = (bf16[3,128,256]{2,1,0:T(8,128)(2,1)S(1)}, bf16[3,128,256]{2,1,0:T(8,128)(2,1)S(1)}, u32[]{:S(2)}, u32[]{:S(2)}) collective-permute-start(bf16[3,128,256]{2,1,0:T(8,128)(2,1)S(1)} %get-tuple-element.70), channel_id=1, source_target_pairs={{0,6},{2,4},{4,2},{6,0},{1,7},{3,5},{5,3},{7,1},{8,14},{10,12},{12... | collective-permute-start | bytes 589832 | tf_op jit(solution)/shard_map/ppermute | solution.py:447
  45.5 20.5 %collective-permute-start.9 = (bf16[3,128,256]{2,1,0:T(8,128)(2,1)S(1)}, bf16[3,128,256]{2,1,0:T(8,128)(2,1)S(1)}, u32[]{:S(2)}, u32[]{:S(2)}) collective-permute-start(bf16[3,128,256]{2,1,0:T(8,128)(2,1)S(1)} %get-tuple-element.71), channel_id=1, source_target_pairs={{0,4},{2,6},{4,0},{6,2},{1,5},{3,7},{5,1},{7,3},{8,12},{10,14},{12... | collective-permute-start | bytes 589832 | tf_op jit(solution)/shard_map/ppermute | solution.py:447
  48.1 11.0 %collective-permute-start.12 = (bf16[3,128,256]{2,1,0:T(8,128)(2,1)S(1)}, bf16[3,128,256]{2,1,0:T(8,128)(2,1)S(1)}, u32[]{:S(2)}, u32[]{:S(2)}) collective-permute-start(bf16[3,128,256]{2,1,0:T(8,128)(2,1)S(1)} %get-tuple-element.79), channel_id=1, source_target_pairs={{0,2},{2,0},{4,6},{6,4},{1,3},{3,1},{5,7},{7,5},{8,10},{10,8},{12,... | collective-permute-start | bytes 589832 | tf_op jit(solution)/shard_map/ppermute | solution.py:447
  48.2 3.7 %collective-permute-start.11 = (f32[16,128]{1,0:T(8,128)S(1)}, f32[16,128]{1,0:T(8,128)S(1)}, u32[]{:S(2)}, u32[]{:S(2)}) collective-permute-start(f32[16,128]{1,0:T(8,128)S(1)} %pad_maximum_fusion.1), channel_id=1, source_target_pairs={{0,16},{8,24},{16,0},{24,8},{1,17},{9,25},{17,1},{25,9},{2,18},{10... | collective-permute-start | bytes 24584 | tf_op jit(solution)/shard_map/ppermute | solution.py:447
  51.9 9.7 %collective-permute-start.15 = (f32[32,128]{1,0:T(8,128)S(1)}, f32[32,128]{1,0:T(8,128)S(1)}, u32[]{:S(2)}, u32[]{:S(2)}) collective-permute-start(f32[32,128]{1,0:T(8,128)S(1)} %pad_maximum_fusion.refs_7_), channel_id=1, source_target_pairs={{0,6},{2,4},{4,2},{6,0},{1,7},{3,5},{5,3},{7,1},{8,14},{10,12},{12... | collective-permute-start | bytes 49160 | tf_op jit(solution)/shard_map/ppermute | solution.py:447
  54.3 11.7 %collective-permute-start.14 = (f32[32,128]{1,0:T(8,128)S(1)}, f32[32,128]{1,0:T(8,128)S(1)}, u32[]{:S(2)}, u32[]{:S(2)}) collective-permute-start(f32[32,128]{1,0:T(8,128)S(1)} %pad_maximum_fusion.refs_7_), channel_id=1, source_target_pairs={{0,4},{2,6},{4,0},{6,2},{1,5},{3,7},{5,1},{7,3},{8,12},{10,14},{12... | collective-permute-start | bytes 49160 | tf_op jit(solution)/shard_map/ppermute | solution.py:447
  59.1 6.9 %collective-permute-start.13 = (f32[32,128]{1,0:T(8,128)S(1)}, f32[32,128]{1,0:T(8,128)S(1)}, u32[]{:S(2)}, u32[]{:S(2)}) collective-permute-start(f32[32,128]{1,0:T(8,128)S(1)} %pad_maximum_fusion.refs_7_), channel_id=1, source_target_pairs={{0,2},{2,0},{4,6},{6,4},{1,3},{3,1},{5,7},{7,5},{8,10},{10,8},{12,... | collective-permute-start | bytes 49160 | tf_op jit(solution)/shard_map/ppermute | solution.py:447

commit v11 on v10

--- a/solution.py
+++ b/solution.py
@@ -211,13 +211,15 @@
 
 
 def turn_kernel(frames, *refs):
-    piece_refs, (plane_ref, plane_out_ref, own_ref, *other_refs), turned = (
+    piece_refs, (plane_ref, own_ref, *other_refs), turned = (
         refs[:frames][::-1],
         refs[frames:-1],
         refs[-1],
     )
-    plane_out_ref[...] = plane_ref[...]
-    spaces = piece_refs[0].shape[0]
+    spaces, lanes, _ = piece_refs[0].shape
+    for space in range(spaces):
+        place = pl.multiple_of(partner("space", space) * lanes, lanes)
+        own_ref[frames + space] = plane_ref[:, :, pl.ds(place, lanes)]
     heads = own_ref.shape[1]
     for space in range(spaces):
         target = turned if space else own_ref
@@ -237,13 +239,12 @@
     spaces, patches, feat = pieces[0].shape
     frames, heads = len(pieces), feat // HEAD_DIM
     turned = (heads, HEAD_DIM, patches)
-    sizes = [frames] + [frames // 2, frames - frames // 2] * (spaces - 1)
+    sizes = [frames + spaces] + [frames // 2, frames - frames // 2] * (spaces - 1)
     return pl.pallas_call(
         functools.partial(turn_kernel, frames),
         in_specs=[pl.BlockSpec(memory_space=pltpu.VMEM)] * (frames + 1),
-        out_specs=[pl.BlockSpec(memory_space=pltpu.VMEM)] * (len(sizes) + 1),
-        out_shape=[jax.ShapeDtypeStruct(plane.shape, plane.dtype)]
-        + [jax.ShapeDtypeStruct((size,) + turned, pieces[0].dtype) for size in sizes],
+        out_specs=[pl.BlockSpec(memory_space=pltpu.VMEM)] * len(sizes),
+        out_shape=[jax.ShapeDtypeStruct((size,) + turned, pieces[0].dtype) for size in sizes],
         scratch_shapes=[pltpu.VMEM((frames,) + turned, pieces[0].dtype)],
         compiler_params=params(patches),
         cost_estimate=cost(2),
@@ -251,8 +252,8 @@
     )(*reversed(pieces), plane)
 
 
-def temporal_part(length, attended_ref, load_upstream, load_gain, grad_ref):
-    frames, feat, lanes = attended_ref.shape
+def temporal_part(length, load_attended, load_upstream, load_gain, fields, ups, normed, grad_ref):
+    frames, feat, lanes = grad_ref.shape
     half = GROUP // 2
     score_scale = feat ** (-0.5)
     pairs = [(t, u) for t in range(frames) for u in range(t + 1)]
@@ -260,36 +261,34 @@
     valid = [jnp.where(t < length, 1.0, 0.0).astype(jnp.float32) for t in every]
     bias = [jnp.where(u < length, 0.0, -1e30).astype(jnp.float32) for u in every]
 
-    def split(block):
-        block = block.astype(jnp.float32)
-        return block[:half], block[half:]
-
-    def load_fields(group):
-        return [split(attended_ref[t, pl.ds(group * GROUP, GROUP), :]) for t in every]
-
-    def load_ups(group):
-        return [split(load_upstream(t, pl.ds(group * GROUP, GROUP))) for t in every]
-
     def total(piece):
         return jnp.broadcast_to(jnp.sum(piece, axis=0, keepdims=True), (half, lanes))
 
     squares = [jnp.zeros((half, lanes), jnp.float32) for _ in every]
     for group in range(feat // GROUP):
-        for t, (low, high) in enumerate(load_fields(group)):
+        rows = pl.ds(group * GROUP, GROUP)
+        for t in every:
+            field = load_attended(t, rows).astype(jnp.float32)
+            fields[t, rows, :] = field
+            ups[t, rows, :] = load_upstream(t, rows).astype(jnp.float32)
+            low, high = field[:half], field[half:]
             squares[t] = squares[t] + (low * low + high * high)
     inverse = [lax.rsqrt(total(squares[t]) * (1.0 / feat) + 1e-06) for t in every]
 
     raw = {pair: jnp.zeros((half, lanes), jnp.float32) for pair in pairs}
     grad = {pair: jnp.zeros((half, lanes), jnp.float32) for pair in pairs}
-    for group in range(feat // GROUP):
-        fields, ups = load_fields(group), load_ups(group)
-        for side in range(2):
-            gain = load_gain(pl.ds(group * GROUP + side * half, half))
-            normed = [fields[t][side] * inverse[t] for t in every]
-            gained = [normed[t] * gain for t in every]
-            for t, u in pairs:
-                raw[t, u] = raw[t, u] + gained[t] * normed[u]
-                grad[t, u] = grad[t, u] + ups[t][side] * fields[u][side]
+    for group in range(feat // half):
+        rows = pl.ds(group * half, half)
+        gain = load_gain(rows)
+        here = [fields[t, rows, :] for t in every]
+        above = [ups[t, rows, :] for t in every]
+        scaled = [here[t] * inverse[t] for t in every]
+        gained = [scaled[t] * gain for t in every]
+        for t in every:
+            normed[t, rows, :] = scaled[t]
+        for t, u in pairs:
+            raw[t, u] = raw[t, u] + gained[t] * scaled[u]
+            grad[t, u] = grad[t, u] + above[t] * here[u]
 
     value_part, score_part = {}, {}
     for t in every:
@@ -318,19 +317,19 @@
 
     all_mixed = []
     for group in range(feat // GROUP):
-        fields, ups = load_fields(group), load_ups(group)
         outs = [[] for _ in every]
         for side in range(2):
             rows = pl.ds(group * GROUP + side * half, half)
             gain = load_gain(rows)
-            normed = [fields[t][side] * inverse[t] for t in every]
+            scaled = [normed[t, rows, :] for t in every]
+            above = [ups[t, rows, :] for t in every]
             mixed = jnp.zeros((half, lanes), jnp.float32)
             for u in every:
-                crossed = functools.reduce(jnp.add, [both[u, v] * normed[v] for v in every])
-                mixed = mixed + crossed * normed[u]
-                from_norm = inverse[u] * (gain * crossed - normed[u] * mean_part[u])
+                crossed = functools.reduce(jnp.add, [both[u, v] * scaled[v] for v in every])
+                mixed = mixed + crossed * scaled[u]
+                from_norm = inverse[u] * (gain * crossed - scaled[u] * mean_part[u])
                 direct = functools.reduce(
-                    jnp.add, [value_part[t, u] * ups[t][side] for t in range(u, frames)]
+                    jnp.add, [value_part[t, u] * above[t] for t in range(u, frames)]
                 )
                 outs[u].append(direct + from_norm)
             all_mixed.append(mixed)
@@ -343,11 +342,11 @@
 
 def temporal_kernel(frames, spaces, length_ref, task_ref, *refs):
     attended_refs, (gain_ref, own_ref, *other_refs), refs = (
-        (refs[frames - 1], *refs[: frames - 1]),
-        refs[frames : frames + 2 * spaces],
-        refs[frames + 2 * spaces :],
-    )
-    field_refs, grad_refs, (mixed_ref, *kept_refs, attended, grads, arrived) = (
+        refs[: frames - 1],
+        refs[frames - 1 : frames - 1 + 2 * spaces],
+        refs[frames - 1 + 2 * spaces :],
+    )
+    field_refs, grad_refs, (mixed_ref, *kept_refs, attended, grads, wide, arrived) = (
         refs[:3],
         refs[3 : frames + 3],
         refs[frames + 3 :],
@@ -372,16 +371,19 @@
             pl.ds(pl.multiple_of(partner("space", space) * lanes, lanes), lanes)
             for space in range(spaces)
         ]
-        for distance, ref in enumerate(attended_refs):
-            frame = partner("tm", distance)
-            for space, here in enumerate(places):
-                attended[space, frame] = ref[head, :, here]
+        for space, here in enumerate(places):
+            attended[space, partner("tm", 0)] = own_ref[frames + space, head]
+            for distance, ref in enumerate(attended_refs):
+                attended[space, partner("tm", distance + 1)] = ref[head, :, here]
         mixed = [
             temporal_part(
                 length_ref[0],
-                attended.at[space],
+                lambda t, rows: attended[space, t, rows, :],
                 functools.partial(load_upstream, space, head),
                 lambda rows: gain_ref[head, rows, :],
+                wide.at[space, 0],
+                wide.at[space, 1],
+                wide.at[space, 2],
                 grads.at[space],
             )
             for space in range(spaces)
@@ -400,11 +402,11 @@
 
 
 def temporal(lengths, task_ids, attended, upstream, gain, fields):
-    frames, heads, feat, lanes = upstream[0].shape
-    spaces = (len(upstream) + 1) // 2
+    _, heads, feat, lanes = upstream[0].shape
+    frames, spaces = len(attended) + 1, (len(upstream) + 1) // 2
     patches = spaces * lanes
     rows = -(-(heads + 1) // 8) * 8
-    operands = [*attended[1:], attended[0], gain, *upstream]
+    operands = [*attended, gain, *upstream]
     results = pl.pallas_call(
         functools.partial(temporal_kernel, frames, spaces),
         in_specs=[pl.BlockSpec(memory_space=pltpu.SMEM)] * 2
@@ -412,6 +414,7 @@
         + [pl.BlockSpec(memory_space=pltpu.HBM)] * len(fields),
         out_specs=[pl.BlockSpec(memory_space=pltpu.VMEM)] * (frames + 1 + len(fields)),
         scratch_shapes=[pltpu.VMEM((spaces, frames, feat, lanes), jnp.bfloat16)] * 2
+        + [pltpu.VMEM((spaces, 3, frames, feat, lanes), jnp.float32)]
         + [pltpu.SemaphoreType.DMA((len(fields),))],
         out_shape=[jax.ShapeDtypeStruct((heads, feat, patches), jnp.bfloat16)] * frames
         + [jax.ShapeDtypeStruct((rows, feat), jnp.float32)]
@@ -468,7 +471,7 @@
     for distance in range(1, frames):
         attended[distance] = swap(attended[distance], "tm", frames, distance)
     backwards, _ = lax.optimization_barrier((pieces[::-1], weights))
-    attended[0], *upstream = turn(backwards[::-1], attended[0])
+    upstream = list(turn(backwards[::-1], attended[0]))
     for index in range(1, len(upstream)):
         upstream[index] = swap(upstream[index], "space", spaces, (index + 1) // 2)
     rows = lax.dynamic_index_in_dim(gains, task_ids[0], 1, keepdims=False)
@@ -476,7 +479,9 @@
     gain = jnp.broadcast_to(
         product.reshape(own, HEAD_DIM, 1), (own, HEAD_DIM, patches // spaces)
     )
-    grads, mixed, kept = temporal(lengths, task_ids, attended, upstream, gain, fields)
+    grads, mixed, kept = temporal(
+        lengths, task_ids, attended[1:], upstream, gain, fields
+    )
     for distance in reversed(range(1, frames)):
         grads[distance] = swap(grads[distance], "tm", frames, distance)
     here = grads[0]

time: 68.8 us -> 68.7 us (level)
  other arithmetic: 0.82 us -> 0.1 us
    dynamic_slice x1, other arithmetic: 0.82 us -> 0.1 us  [split_by_heads(): lax.dynamic_slice_in_dim(rows[0] * rows[1], frame * width, width, 0)]
  transfers between devices with their start and end apart: 16 -> 16, of which waited for: 5 -> 5; matrix products, arithmetic and copies ran while one was open for 1% -> 0% of each run, Pallas kernels for 13% -> 13%
where the time goes in v11:
time: 68.7 us; the launch traced here: 68.4 us
  starting transfers between devices  25.1 us (37%)
  waiting for transfers between devices  22.5 us (33%)
  Pallas kernels  16.7 us (24%)
  between operations  2.04 us (3%)
  local copies, waits for them, and re-layouts  1.99 us (3%)
    ppermute x16, starting transfers between devices, swap(): return lax.ppermute(field, axis, [(i, i ^ distance) for i in range(size)])  25.1 us
    ppermute x16, waiting for transfers between devices, swap(): return lax.ppermute(field, axis, [(i, i ^ distance) for i in range(size)])  22.5 us
    pallas_call x1, Pallas kernels, forward(): pl.pallas_call(functools.partial(forward_kernel, axis), in_specs=[pl.Bloc...  6.52 us
    pallas_call x1, Pallas kernels, temporal(): pl.pallas_call(functools.partial(temporal_kernel, frames, spaces), in_spe...  3.91 us
    pallas_call x2, Pallas kernels, backward(): pl.pallas_call(functools.partial(backward_kernel, axis, distances, gains_...  3.88 us
    unnamed x6, local copies, waits for them, and re-layouts  1.88 us
  transfers between devices with their start and end apart: 16, of which 5 were waited for; matrix products, arithmetic and copies ran while one was open for 0% of the time, Pallas kernels for 13%

profile of v11, /device:TPU:0, one launch (start us, length us, event | category | flops | bytes accessed | tf_op | source)
XLA Modules:
  0.0 68.4 jit_solution(13508887696096459462)
XLA Ops:
  0.6 1.3 %pack_cotangent.1 = (bf16[2,128,384]{2,1,0:T(8,128)(2,1)S(1)}, bf16[2,128,384]{2,1,0:T(8,128)(2,1)S(1)}, bf16[2,128,384]{2,1,0:T(8,128)(2,1)S(1)}, bf16[2,128,384]{2,1,0:T(8,128)(2,1)S(1)}) custom-call(bf16[128,3072]{1,0:T(8,128)(2,1)} %bitcast.17), custom_call_target="tpu_custom_call" | custom-call | flops 100000000 | tf_op jit(solution)/shard_map/pack_cotangent/pallas_call | solution.py:198
  2.0 5.1 %collective-permute-start.3 = (bf16[2,128,384]{2,1,0:T(8,128)(2,1)S(1)}, bf16[2,128,384]{2,1,0:T(8,128)(2,1)S(1)}, u32[]{:S(2)}, u32[]{:S(2)}) collective-permute-start(bf16[2,128,384]{2,1,0:T(8,128)(2,1)S(1)} %get-tuple-element.52), channel_id=1, source_target_pairs={{0,6},{2,4},{4,2},{6,0},{1,7},{3,5},{5,3},{7,1},{8,14},{10,12},{12... | collective-permute-start | bytes 589832 | tf_op jit(solution)/shard_map/ppermute | solution.py:450
  7.1 0.6 collective-permute-start.5
  7.7 6.5 %spatial_forward.1 = (f32[12,256,256]{2,1,0:T(8,128)S(1)}, bf16[3,128,256]{2,1,0:T(8,128)(2,1)S(1)}, bf16[3,128,256]{2,1,0:T(8,128)(2,1)}, bf16[3,128,256]{2,1,0:T(8,128)(2,1)}, bf16[3,128,256]{2,1,0:T(8,128)(2,1)}) custom-call(bf16[256,1536]{1,0:T(8,128)(2,1)} %bitcast.11, bf16[256,1536]{1,0:T(8,128)(2,1)} %bitcast.13, bf16[256,1536]{1,0:T(8,128)(2,1)} %bitcast.15), custom_call_target="tpu_custom_call" | custom-call | flops 600000000 | tf_op jit(solution)/shard_map/spatial_forward/pallas_call | solution.py:76
  14.3 1.4 %collective-permute-start = (bf16[3,128,256]{2,1,0:T(8,128)(2,1)}, bf16[3,128,256]{2,1,0:T(8,128)(2,1)S(1)}, u32[]{:S(2)}, u32[]{:S(2)}) collective-permute-start(bf16[3,128,256]{2,1,0:T(8,128)(2,1)} %get-tuple-element.49), channel_id=1, source_target_pairs={{0,2},{2,0},{4,6},{6,4},{1,3},{3,1},{5,7},{7,5},{8,10},{10,8},{12,... | collective-permute-start | bytes 589832 | tf_op jit(solution)/shard_map/ppermute | solution.py:450
  15.7 2.9 %collective-permute-start.1 = (bf16[3,128,256]{2,1,0:T(8,128)(2,1)}, bf16[3,128,256]{2,1,0:T(8,128)(2,1)}, u32[]{:S(2)}, u32[]{:S(2)}) collective-permute-start(bf16[3,128,256]{2,1,0:T(8,128)(2,1)} %get-tuple-element.50), channel_id=1, source_target_pairs={{0,4},{2,6},{4,0},{6,2},{1,5},{3,7},{5,1},{7,3},{8,12},{10,14},{12... | collective-permute-start | bytes 589832 | tf_op jit(solution)/shard_map/ppermute | solution.py:450
  18.7 6.9 %collective-permute-done.4.refs_1_ = bf16[2,128,384]{2,1,0:T(8,128)(2,1)S(1)} collective-permute-done((bf16[2,128,384]{2,1,0:T(8,128)(2,1)S(1)}, bf16[2,128,384]{2,1,0:T(8,128)(2,1)S(1)}, u32[]{:S(2)}, u32[]{:S(2)}) %collective-permute-start.4) | collective-permute-done | bytes 196640 | tf_op jit(solution)/shard_map/ppermute | solution.py:450
  25.6 1.1 %turn_cotangent.1 = (bf16[6,3,128,128]{3,2,1,0:T(8,128)(2,1)S(1)}, bf16[2,3,128,128]{3,2,1,0:T(8,128)(2,1)}, bf16[2,3,128,128]{3,2,1,0:T(8,128)(2,1)}) custom-call(bf16[2,128,384]{2,1,0:T(8,128)(2,1)S(1)} %collective-permute-done.3.refs_0_, bf16[2,128,384]{2,1,0:T(8,128)(2,1)S(1)} %collective-permute-done.4.refs_1_, ...), custom_call_target="tpu_custom_call" | custom-call | flops 200000000 | tf_op jit(solution)/shard_map/turn_cotangent/pallas_call | solution.py:243
  26.7 0.8 %copy-done = bf16[6,3,128,128]{3,2,1,0:T(8,128)(2,1)} copy-done((bf16[6,3,128,128]{3,2,1,0:T(8,128)(2,1)}, bf16[6,3,128,128]{3,2,1,0:T(8,128)(2,1)S(1)}, u32[]{:S(2)}) %copy-start) | copy-done | bytes 589848
  27.5 1.7 %collective-permute-start.6 = (bf16[2,3,128,128]{3,2,1,0:T(8,128)(2,1)}, bf16[2,3,128,128]{3,2,1,0:T(8,128)(2,1)}, u32[]{:S(2)}, u32[]{:S(2)}) collective-permute-start(bf16[2,3,128,128]{3,2,1,0:T(8,128)(2,1)} %get-tuple-element.63), channel_id=1, source_target_pairs={{0,1},{1,0},{2,3},{3,2},{4,5},{5,4},{6,7},{7,6},{8,9},{9,8},{10,11... | collective-permute-start | bytes 589832 | tf_op jit(solution)/shard_map/ppermute | solution.py:450
  31.0 6.6 %collective-permute-done.1.refs_1_ = bf16[3,128,256]{2,1,0:T(8,128)(2,1)} collective-permute-done((bf16[3,128,256]{2,1,0:T(8,128)(2,1)}, bf16[3,128,256]{2,1,0:T(8,128)(2,1)}, u32[]{:S(2)}, u32[]{:S(2)}) %collective-permute-start.1) | collective-permute-done | bytes 196640 | tf_op jit(solution)/shard_map/ppermute | solution.py:450
  37.7 1.1 %copy-done.1 = bf16[6,3,128,128]{3,2,1,0:T(8,128)(2,1)S(1)} copy-done((bf16[6,3,128,128]{3,2,1,0:T(8,128)(2,1)S(1)}, bf16[6,3,128,128]{3,2,1,0:T(8,128)(2,1)}, u32[]{:S(2)}) %copy-start.1) | copy-done | bytes 589848
  38.7 3.9 %temporal.1 = (bf16[3,128,256]{2,1,0:T(8,128)(2,1)S(1)}, bf16[3,128,256]{2,1,0:T(8,128)(2,1)S(1)}, bf16[3,128,256]{2,1,0:T(8,128)(2,1)S(1)}, bf16[3,128,256]{2,1...) custom-call(s32[1]{0:T(128)S(6)} %copy.15.length_ref, ...), custom_call_target="tpu_custom_call" | custom-call | flops 400000000 | tf_op jit(solution)/shard_map/temporal/pallas_call | solution.py:410
  42.7 2.7 %collective-permute-start.8 = (bf16[3,128,256]{2,1,0:T(8,128)(2,1)S(1)}, bf16[3,128,256]{2,1,0:T(8,128)(2,1)S(1)}, u32[]{:S(2)}, u32[]{:S(2)}) collective-permute-start(bf16[3,128,256]{2,1,0:T(8,128)(2,1)S(1)} %get-tuple-element.68), channel_id=1, source_target_pairs={{0,6},{2,4},{4,2},{6,0},{1,7},{3,5},{5,3},{7,1},{8,14},{10,12},{12... | collective-permute-start | bytes 589832 | tf_op jit(solution)/shard_map/ppermute | solution.py:450
  45.5 2.6 %collective-permute-start.9 = (bf16[3,128,256]{2,1,0:T(8,128)(2,1)S(1)}, bf16[3,128,256]{2,1,0:T(8,128)(2,1)S(1)}, u32[]{:S(2)}, u32[]{:S(2)}) collective-permute-start(bf16[3,128,256]{2,1,0:T(8,128)(2,1)S(1)} %get-tuple-element.69), channel_id=1, source_target_pairs={{0,4},{2,6},{4,0},{6,2},{1,5},{3,7},{5,1},{7,3},{8,12},{10,14},{12... | collective-permute-start | bytes 589832 | tf_op jit(solution)/shard_map/ppermute | solution.py:450
  48.2 1.5 %collective-permute-start.11 = (f32[16,128]{1,0:T(8,128)S(1)}, f32[16,128]{1,0:T(8,128)S(1)}, u32[]{:S(2)}, u32[]{:S(2)}) collective-permute-start(f32[16,128]{1,0:T(8,128)S(1)} %pad_maximum_fusion.1), channel_id=1, source_target_pairs={{0,16},{8,24},{16,0},{24,8},{1,17},{9,25},{17,1},{25,9},{2,18},{10... | collective-permute-start | bytes 24584 | tf_op jit(solution)/shard_map/ppermute | solution.py:450
  49.7 1.4 %spatial_backward.2 = (bf16[256,1536]{1,0:T(8,128)(2,1)}, bf16[256,1536]{1,0:T(8,128)(2,1)}) custom-call(bf16[256,1536]{1,0:T(8,128)(2,1)S(1)} %get-tuple-element.65.refs_0_, bf16[256,1536]{1,0:T(8,128)(2,1)S(1)} %get-tuple-element.66.refs_1_, bf16[256,1536]{1,0:T(8,128)(2,1)S(1)} %get-tuple-element.67.refs_2_, ...), custom_call_target="tpu_custom_call" | custom-call | flops 200000000 | tf_op jit(solution)/shard_map/spatial_backward/pallas_call | solution.py:159
  51.1 0.7 %collective-permute-done.11 = f32[16,128]{1,0:T(8,128)S(1)} collective-permute-done((f32[16,128]{1,0:T(8,128)S(1)}, f32[16,128]{1,0:T(8,128)S(1)}, u32[]{:S(2)}, u32[]{:S(2)}) %collective-permute-start.11) | collective-permute-done | bytes 8224 | tf_op jit(solution)/shard_map/ppermute | solution.py:450
  51.8 2.4 %collective-permute-start.15 = (f32[32,128]{1,0:T(8,128)S(1)}, f32[32,128]{1,0:T(8,128)S(1)}, u32[]{:S(2)}, u32[]{:S(2)}) collective-permute-start(f32[32,128]{1,0:T(8,128)S(1)} %pad_maximum_fusion.refs_7_), channel_id=1, source_target_pairs={{0,6},{2,4},{4,2},{6,0},{1,7},{3,5},{5,3},{7,1},{8,14},{10,12},{12... | collective-permute-start | bytes 49160 | tf_op jit(solution)/shard_map/ppermute | solution.py:450
  54.3 0.9 %collective-permute-start.14 = (f32[32,128]{1,0:T(8,128)S(1)}, f32[32,128]{1,0:T(8,128)S(1)}, u32[]{:S(2)}, u32[]{:S(2)}) collective-permute-start(f32[32,128]{1,0:T(8,128)S(1)} %pad_maximum_fusion.refs_7_), channel_id=1, source_target_pairs={{0,4},{2,6},{4,0},{6,2},{1,5},{3,7},{5,1},{7,3},{8,12},{10,14},{12... | collective-permute-start | bytes 49160 | tf_op jit(solution)/shard_map/ppermute | solution.py:450
  55.2 3.8 %collective-permute-done.12.refs_6_ = bf16[3,128,256]{2,1,0:T(8,128)(2,1)S(1)} collective-permute-done((bf16[3,128,256]{2,1,0:T(8,128)(2,1)S(1)}, bf16[3,128,256]{2,1,0:T(8,128)(2,1)S(1)}, u32[]{:S(2)}, u32[]{:S(2)}) %collective-permute-start.12) | collective-permute-done | bytes 196640 | tf_op jit(solution)/shard_map/ppermute | solution.py:450
  59.0 2.5 %collective-permute-start.13 = (f32[32,128]{1,0:T(8,128)S(1)}, f32[32,128]{1,0:T(8,128)S(1)}, u32[]{:S(2)}, u32[]{:S(2)}) collective-permute-start(f32[32,128]{1,0:T(8,128)S(1)} %pad_maximum_fusion.refs_7_), channel_id=1, source_target_pairs={{0,2},{2,0},{4,6},{6,4},{1,3},{3,1},{5,7},{7,5},{8,10},{10,8},{12,... | collective-permute-start | bytes 49160 | tf_op jit(solution)/shard_map/ppermute | solution.py:450
  61.5 4.4 %collective-permute-done.14.refs_9_ = f32[32,128]{1,0:T(8,128)S(1)} collective-permute-done((f32[32,128]{1,0:T(8,128)S(1)}, f32[32,128]{1,0:T(8,128)S(1)}, u32[]{:S(2)}, u32[]{:S(2)}) %collective-permute-start.14) | collective-permute-done | bytes 16416 | tf_op jit(solution)/shard_map/ppermute | solution.py:450
  65.9 2.5 %spatial_backward.3 = (bf16[256,1536]{1,0:T(8,128)(2,1)}, bf16[256,1536]{1,0:T(8,128)(2,1)}, f32[2,16,1536]{2,1,0:T(8,128)}) custom-call(bf16[256,1536]{1,0:T(8,128)(2,1)S(1)} %get-tuple-element.65.refs_0_, bf16[256,1536]{1,0:T(8,128)(2,1)S(1)} %get-tuple-element.66.refs_1_, ...), custom_call_target="tpu_custom_call", output_to_operand_aliasing={{0}: (12, {}), {1}: (13, {})} | custom-call | flops 200000000 | tf_op jit(solution)/shard_map/spatial_backward/pallas_call | solution.py:159
  (24 shorter events, 0.8 us)
Async XLA Ops:
  0.6 30.2 %copy-start.2 = (f32[2,16,1536]{2,1,0:T(8,128)S(1)}, f32[2,16,1536]{2,1,0:T(8,128)}, u32[]{:S(2)}) copy-start(f32[2,16,1536]{2,1,0:T(8,128)} %refs_11_.1) | copy-start | bytes 589828
  2.0 16.7 %collective-permute-start.3 = (bf16[2,128,384]{2,1,0:T(8,128)(2,1)S(1)}, bf16[2,128,384]{2,1,0:T(8,128)(2,1)S(1)}, u32[]{:S(2)}, u32[]{:S(2)}) collective-permute-start(bf16[2,128,384]{2,1,0:T(8,128)(2,1)S(1)} %get-tuple-element.52), channel_id=1, source_target_pairs={{0,6},{2,4},{4,2},{6,0},{1,7},{3,5},{5,3},{7,1},{8,14},{10,12},{12... | collective-permute-start | bytes 589832 | tf_op jit(solution)/shard_map/ppermute | solution.py:450
  7.1 18.5 %collective-permute-start.4 = (bf16[2,128,384]{2,1,0:T(8,128)(2,1)S(1)}, bf16[2,128,384]{2,1,0:T(8,128)(2,1)S(1)}, u32[]{:S(2)}, u32[]{:S(2)}) collective-permute-start(bf16[2,128,384]{2,1,0:T(8,128)(2,1)S(1)} %get-tuple-element.53), channel_id=1, source_target_pairs={{0,4},{2,6},{4,0},{6,2},{1,5},{3,7},{5,1},{7,3},{8,12},{10,14},{12... | collective-permute-start | bytes 589832 | tf_op jit(solution)/shard_map/ppermute | solution.py:450
  7.1 18.5 %collective-permute-start.5 = (bf16[2,128,384]{2,1,0:T(8,128)(2,1)S(1)}, bf16[2,128,384]{2,1,0:T(8,128)(2,1)S(1)}, u32[]{:S(2)}, u32[]{:S(2)}) collective-permute-start(bf16[2,128,384]{2,1,0:T(8,128)(2,1)S(1)} %get-tuple-element.54), channel_id=1, source_target_pairs={{0,2},{2,0},{4,6},{6,4},{1,3},{3,1},{5,7},{7,5},{8,10},{10,8},{12,... | collective-permute-start | bytes 589832 | tf_op jit(solution)/shard_map/ppermute | solution.py:450
  14.3 16.7 %collective-permute-start = (bf16[3,128,256]{2,1,0:T(8,128)(2,1)}, bf16[3,128,256]{2,1,0:T(8,128)(2,1)S(1)}, u32[]{:S(2)}, u32[]{:S(2)}) collective-permute-start(bf16[3,128,256]{2,1,0:T(8,128)(2,1)} %get-tuple-element.49), channel_id=1, source_target_pairs={{0,2},{2,0},{4,6},{6,4},{1,3},{3,1},{5,7},{7,5},{8,10},{10,8},{12,... | collective-permute-start | bytes 589832 | tf_op jit(solution)/shard_map/ppermute | solution.py:450
  15.7 21.8 %collective-permute-start.1 = (bf16[3,128,256]{2,1,0:T(8,128)(2,1)}, bf16[3,128,256]{2,1,0:T(8,128)(2,1)}, u32[]{:S(2)}, u32[]{:S(2)}) collective-permute-start(bf16[3,128,256]{2,1,0:T(8,128)(2,1)} %get-tuple-element.50), channel_id=1, source_target_pairs={{0,4},{2,6},{4,0},{6,2},{1,5},{3,7},{5,1},{7,3},{8,12},{10,14},{12... | collective-permute-start | bytes 589832 | tf_op jit(solution)/shard_map/ppermute | solution.py:450
  18.6 18.9 %collective-permute-start.2 = (bf16[3,128,256]{2,1,0:T(8,128)(2,1)}, bf16[3,128,256]{2,1,0:T(8,128)(2,1)}, u32[]{:S(2)}, u32[]{:S(2)}) collective-permute-start(bf16[3,128,256]{2,1,0:T(8,128)(2,1)} %get-tuple-element.51), channel_id=1, source_target_pairs={{0,6},{2,4},{4,2},{6,0},{1,7},{3,5},{5,3},{7,1},{8,14},{10,12},{12... | collective-permute-start | bytes 589832 | tf_op jit(solution)/shard_map/ppermute | solution.py:450
  26.7 0.8 %copy-start = (bf16[6,3,128,128]{3,2,1,0:T(8,128)(2,1)}, bf16[6,3,128,128]{3,2,1,0:T(8,128)(2,1)S(1)}, u32[]{:S(2)}) copy-start(bf16[6,3,128,128]{3,2,1,0:T(8,128)(2,1)S(1)} %get-tuple-element.62.refs_4_) | copy-start | bytes 1769476
  27.5 10.0 %collective-permute-start.6 = (bf16[2,3,128,128]{3,2,1,0:T(8,128)(2,1)}, bf16[2,3,128,128]{3,2,1,0:T(8,128)(2,1)}, u32[]{:S(2)}, u32[]{:S(2)}) collective-permute-start(bf16[2,3,128,128]{3,2,1,0:T(8,128)(2,1)} %get-tuple-element.63), channel_id=1, source_target_pairs={{0,1},{1,0},{2,3},{3,2},{4,5},{5,4},{6,7},{7,6},{8,9},{9,8},{10,11... | collective-permute-start | bytes 589832 | tf_op jit(solution)/shard_map/ppermute | solution.py:450
  29.2 8.3 %collective-permute-start.7 = (bf16[2,3,128,128]{3,2,1,0:T(8,128)(2,1)}, bf16[2,3,128,128]{3,2,1,0:T(8,128)(2,1)}, u32[]{:S(2)}, u32[]{:S(2)}) collective-permute-start(bf16[2,3,128,128]{3,2,1,0:T(8,128)(2,1)} %get-tuple-element.64), channel_id=1, source_target_pairs={{0,1},{1,0},{2,3},{3,2},{4,5},{5,4},{6,7},{7,6},{8,9},{9,8},{10,11... | collective-permute-start | bytes 589832 | tf_op jit(solution)/shard_map/ppermute | solution.py:450
  37.7 1.1 %copy-start.1 = (bf16[6,3,128,128]{3,2,1,0:T(8,128)(2,1)S(1)}, bf16[6,3,128,128]{3,2,1,0:T(8,128)(2,1)}, u32[]{:S(2)}) copy-start(bf16[6,3,128,128]{3,2,1,0:T(8,128)(2,1)} %copy-done) | copy-start | bytes 1769476
  42.6 5.5 %collective-permute-start.10 = (f32[8,128]{1,0:T(8,128)S(1)}, f32[8,128]{1,0:T(8,128)S(1)}, u32[]{:S(2)}, u32[]{:S(2)}) collective-permute-start(f32[8,128]{1,0:T(8,128)S(1)} %get-tuple-element.70), channel_id=1, source_target_pairs={{0,8},{8,0},{16,24},{24,16},{1,9},{9,1},{17,25},{25,17},{2,10},{10... | collective-permute-start | bytes 12296 | tf_op jit(solution)/shard_map/ppermute | solution.py:450
  42.7 23.2 %collective-permute-start.8 = (bf16[3,128,256]{2,1,0:T(8,128)(2,1)S(1)}, bf16[3,128,256]{2,1,0:T(8,128)(2,1)S(1)}, u32[]{:S(2)}, u32[]{:S(2)}) collective-permute-start(bf16[3,128,256]{2,1,0:T(8,128)(2,1)S(1)} %get-tuple-element.68), channel_id=1, source_target_pairs={{0,6},{2,4},{4,2},{6,0},{1,7},{3,5},{5,3},{7,1},{8,14},{10,12},{12... | collective-permute-start | bytes 589832 | tf_op jit(solution)/shard_map/ppermute | solution.py:450
  45.5 20.5 %collective-permute-start.9 = (bf16[3,128,256]{2,1,0:T(8,128)(2,1)S(1)}, bf16[3,128,256]{2,1,0:T(8,128)(2,1)S(1)}, u32[]{:S(2)}, u32[]{:S(2)}) collective-permute-start(bf16[3,128,256]{2,1,0:T(8,128)(2,1)S(1)} %get-tuple-element.69), channel_id=1, source_target_pairs={{0,4},{2,6},{4,0},{6,2},{1,5},{3,7},{5,1},{7,3},{8,12},{10,14},{12... | collective-permute-start | bytes 589832 | tf_op jit(solution)/shard_map/ppermute | solution.py:450
  48.1 11.0 %collective-permute-start.12 = (bf16[3,128,256]{2,1,0:T(8,128)(2,1)S(1)}, bf16[3,128,256]{2,1,0:T(8,128)(2,1)S(1)}, u32[]{:S(2)}, u32[]{:S(2)}) collective-permute-start(bf16[3,128,256]{2,1,0:T(8,128)(2,1)S(1)} %get-tuple-element.77), channel_id=1, source_target_pairs={{0,2},{2,0},{4,6},{6,4},{1,3},{3,1},{5,7},{7,5},{8,10},{10,8},{12,... | collective-permute-start | bytes 589832 | tf_op jit(solution)/shard_map/ppermute | solution.py:450
  48.2 3.7 %collective-permute-start.11 = (f32[16,128]{1,0:T(8,128)S(1)}, f32[16,128]{1,0:T(8,128)S(1)}, u32[]{:S(2)}, u32[]{:S(2)}) collective-permute-start(f32[16,128]{1,0:T(8,128)S(1)} %pad_maximum_fusion.1), channel_id=1, source_target_pairs={{0,16},{8,24},{16,0},{24,8},{1,17},{9,25},{17,1},{25,9},{2,18},{10... | collective-permute-start | bytes 24584 | tf_op jit(solution)/shard_map/ppermute | solution.py:450
  51.8 9.7 %collective-permute-start.15 = (f32[32,128]{1,0:T(8,128)S(1)}, f32[32,128]{1,0:T(8,128)S(1)}, u32[]{:S(2)}, u32[]{:S(2)}) collective-permute-start(f32[32,128]{1,0:T(8,128)S(1)} %pad_maximum_fusion.refs_7_), channel_id=1, source_target_pairs={{0,6},{2,4},{4,2},{6,0},{1,7},{3,5},{5,3},{7,1},{8,14},{10,12},{12... | collective-permute-start | bytes 49160 | tf_op jit(solution)/shard_map/ppermute | solution.py:450
  54.3 11.7 %collective-permute-start.14 = (f32[32,128]{1,0:T(8,128)S(1)}, f32[32,128]{1,0:T(8,128)S(1)}, u32[]{:S(2)}, u32[]{:S(2)}) collective-permute-start(f32[32,128]{1,0:T(8,128)S(1)} %pad_maximum_fusion.refs_7_), channel_id=1, source_target_pairs={{0,4},{2,6},{4,0},{6,2},{1,5},{3,7},{5,1},{7,3},{8,12},{10,14},{12... | collective-permute-start | bytes 49160 | tf_op jit(solution)/shard_map/ppermute | solution.py:450
  59.0 6.9 %collective-permute-start.13 = (f32[32,128]{1,0:T(8,128)S(1)}, f32[32,128]{1,0:T(8,128)S(1)}, u32[]{:S(2)}, u32[]{:S(2)}) collective-permute-start(f32[32,128]{1,0:T(8,128)S(1)} %pad_maximum_fusion.refs_7_), channel_id=1, source_target_pairs={{0,2},{2,0},{4,6},{6,4},{1,3},{3,1},{5,7},{7,5},{8,10},{10,8},{12,... | collective-permute-start | bytes 49160 | tf_op jit(solution)/shard_map/ppermute | solution.py:450

commit v12 on v11

--- a/solution.py
+++ b/solution.py
@@ -130,7 +130,7 @@
         copy.start()
         copies.append(copy)
     else:
-        gq_ref, gk_ref = refs
+        gq_ref, gk_ref = refs[-2:]
     for place, (distance, grad_ref) in enumerate(zip(distances, grad_refs)):
         copies += backward_group(
             axis,
@@ -211,10 +211,10 @@
 
 
 def turn_kernel(frames, *refs):
-    piece_refs, (plane_ref, own_ref, *other_refs), turned = (
+    piece_refs, (plane_ref, own_hbm, *other_refs), (turned, own_ref, sent) = (
         refs[:frames][::-1],
-        refs[frames:-1],
-        refs[-1],
+        refs[frames:-3],
+        refs[-3:],
     )
     spaces, lanes, _ = piece_refs[0].shape
     for space in range(spaces):
@@ -229,10 +229,14 @@
             for head in range(heads):
                 cols = pl.ds(head * HEAD_DIM, HEAD_DIM)
                 target[frame, head] = ref[source, :, cols].T
-        if space:
+        if space == 0:
+            copy = pltpu.make_async_copy(own_ref, own_hbm, sent)
+            copy.start()
+        else:
             half = frames // 2
             other_refs[2 * space - 2][...] = turned[:half]
             other_refs[2 * space - 1][...] = turned[half:]
+    copy.wait()
 
 
 def turn(pieces, plane):
@@ -243,9 +247,14 @@
     return pl.pallas_call(
         functools.partial(turn_kernel, frames),
         in_specs=[pl.BlockSpec(memory_space=pltpu.VMEM)] * (frames + 1),
-        out_specs=[pl.BlockSpec(memory_space=pltpu.VMEM)] * len(sizes),
+        out_specs=[pl.BlockSpec(memory_space=pltpu.HBM)]
+        + [pl.BlockSpec(memory_space=pltpu.VMEM)] * (len(sizes) - 1),
         out_shape=[jax.ShapeDtypeStruct((size,) + turned, pieces[0].dtype) for size in sizes],
-        scratch_shapes=[pltpu.VMEM((frames,) + turned, pieces[0].dtype)],
+        scratch_shapes=[
+            pltpu.VMEM((frames,) + turned, pieces[0].dtype),
+            pltpu.VMEM((frames + spaces,) + turned, pieces[0].dtype),
+            pltpu.SemaphoreType.DMA,
+        ],
         compiler_params=params(patches),
         cost_estimate=cost(2),
         name="turn_cotangent",
@@ -341,23 +350,23 @@
 
 
 def temporal_kernel(frames, spaces, length_ref, task_ref, *refs):
-    attended_refs, (gain_ref, own_ref, *other_refs), refs = (
+    attended_refs, (gain_ref, *other_refs), refs = (
         refs[: frames - 1],
-        refs[frames - 1 : frames - 1 + 2 * spaces],
-        refs[frames - 1 + 2 * spaces :],
-    )
-    field_refs, grad_refs, (mixed_ref, *kept_refs, attended, grads, wide, arrived) = (
-        refs[:3],
-        refs[3 : frames + 3],
-        refs[frames + 3 :],
-    )
+        refs[frames - 1 : frames - 2 + 2 * spaces],
+        refs[frames - 2 + 2 * spaces :],
+    )
+    (own_hbm, *field_refs), grad_refs, refs = refs[:4], refs[4 : frames + 4], refs[frames + 4 :]
+    mixed_ref, *kept_refs, attended, grads, wide, own_ref, arrived = refs
+    heads, lanes = own_ref.shape[1], own_ref.shape[3]
     copies = [
-        pltpu.make_async_copy(source, target, arrived.at[index])
+        pltpu.make_async_copy(own_hbm.at[:, head], own_ref.at[:, head], arrived.at[head])
+        for head in range(heads)
+    ] + [
+        pltpu.make_async_copy(source, target, arrived.at[heads + index])
         for index, (source, target) in enumerate(zip(field_refs, kept_refs))
     ]
     for copy in copies:
         copy.start()
-    heads, lanes = own_ref.shape[1], own_ref.shape[3]
     half = frames // 2
     mixed_ref[...] = jnp.full(mixed_ref.shape, task_ref[0].astype(jnp.float32))
 
@@ -366,25 +375,26 @@
             return own_ref[t, head, rows, :]
         return other_refs[2 * space - 2 + t // half][t % half, head, rows, :]
 
-    def step(head, carry):
-        places = [
-            pl.ds(pl.multiple_of(partner("space", space) * lanes, lanes), lanes)
-            for space in range(spaces)
-        ]
+    places = [
+        pl.ds(pl.multiple_of(partner("space", space) * lanes, lanes), lanes)
+        for space in range(spaces)
+    ]
+    for head in range(heads):
+        copies[head].wait()
         for space, here in enumerate(places):
-            attended[space, partner("tm", 0)] = own_ref[frames + space, head]
+            attended[head, space, partner("tm", 0)] = own_ref[frames + space, head]
             for distance, ref in enumerate(attended_refs):
-                attended[space, partner("tm", distance + 1)] = ref[head, :, here]
+                attended[head, space, partner("tm", distance + 1)] = ref[head, :, here]
         mixed = [
             temporal_part(
                 length_ref[0],
-                lambda t, rows: attended[space, t, rows, :],
+                lambda t, rows: attended[head, space, t, rows, :],
                 functools.partial(load_upstream, space, head),
                 lambda rows: gain_ref[head, rows, :],
-                wide.at[space, 0],
-                wide.at[space, 1],
-                wide.at[space, 2],
-                grads.at[space],
+                wide.at[head % 2, space, 0],
+                wide.at[head % 2, space, 1],
+                wide.at[head % 2, space, 2],
+                grads.at[head, space],
             )
             for space in range(spaces)
         ]
@@ -393,11 +403,8 @@
         for distance, ref in enumerate(grad_refs):
             frame = partner("tm", distance)
             for space, here in enumerate(places):
-                ref[head, :, here] = grads[space, frame]
-        return carry
-
-    lax.fori_loop(0, heads, step, 0)
-    for copy in copies:
+                ref[head, :, here] = grads[head, space, frame]
+    for copy in copies[heads:]:
         copy.wait()
 
 
@@ -406,23 +413,29 @@
     frames, spaces = len(attended) + 1, (len(upstream) + 1) // 2
     patches = spaces * lanes
     rows = -(-(heads + 1) // 8) * 8
-    operands = [*attended, gain, *upstream]
+    operands = [*attended, gain, *upstream[1:]]
+    in_place = [in_hbm(field) for field in (upstream[0], *fields)]
+    block = (heads, spaces, frames, feat, lanes)
     results = pl.pallas_call(
         functools.partial(temporal_kernel, frames, spaces),
         in_specs=[pl.BlockSpec(memory_space=pltpu.SMEM)] * 2
         + [pl.BlockSpec(memory_space=pltpu.VMEM)] * len(operands)
-        + [pl.BlockSpec(memory_space=pltpu.HBM)] * len(fields),
+        + [pl.BlockSpec(memory_space=pltpu.HBM)] * len(in_place),
         out_specs=[pl.BlockSpec(memory_space=pltpu.VMEM)] * (frames + 1 + len(fields)),
-        scratch_shapes=[pltpu.VMEM((spaces, frames, feat, lanes), jnp.bfloat16)] * 2
-        + [pltpu.VMEM((spaces, 3, frames, feat, lanes), jnp.float32)]
-        + [pltpu.SemaphoreType.DMA((len(fields),))],
+        scratch_shapes=[
+            pltpu.VMEM(block, jnp.bfloat16),
+            pltpu.VMEM(block, jnp.bfloat16),
+            pltpu.VMEM((2, spaces, 3, frames, feat, lanes), jnp.float32),
+            pltpu.VMEM(upstream[0].shape, upstream[0].dtype),
+            pltpu.SemaphoreType.DMA((heads + len(fields),)),
+        ],
         out_shape=[jax.ShapeDtypeStruct((heads, feat, patches), jnp.bfloat16)] * frames
         + [jax.ShapeDtypeStruct((rows, feat), jnp.float32)]
         + [jax.ShapeDtypeStruct(field.shape, field.dtype) for field in fields],
         compiler_params=params(patches),
         cost_estimate=cost(4),
         name="temporal",
-    )(lengths, task_ids, *operands, *[in_hbm(field) for field in fields])
+    )(lengths, task_ids, *operands, *in_place)
     return list(results[:frames]), results[frames], results[frames + 1 :]
 
 
@@ -496,12 +509,16 @@
     mixed = [mixed, swap(near, "tm", frames, 1)] + [
         swap(mixed, "tm", frames, distance) for distance in range(2, frames)
     ]
+    last = range(frames - 1, 0, -1)
+    if frames > 2:
+        results = backward("tm", kept, weights, [grads[1]], [1], results)
+        last = range(frames - 1, 1, -1)
     grad_queries, grad_keys, grad_gains = backward(
         "tm",
         kept,
         weights,
-        grads[:0:-1],
-        list(range(frames - 1, 0, -1)),
+        [grads[distance] for distance in last],
+        list(last),
         results,
         mixed,
         gains,

time: 68.7 us -> 68 us (0.990)
  Pallas kernels: 16.7 us -> 18.8 us
  waiting for transfers between devices: 22.5 us -> 20.8 us
  local copies, waits for them, and re-layouts: 1.99 us -> 0.92 us
    ppermute x16, waiting for transfers between devices: 22.5 us -> 20.8 us  [swap(): return lax.ppermute(field, axis, [(i, i ^ distance) for i in range(size)])]
    unnamed x6 -> x4, local copies, waits for them, and re-layouts: 1.88 us -> 0.81 us
    pallas_call x1, Pallas kernels: 3.91 us -> 4.85 us  [temporal(): pl.pallas_call(functools.partial(temporal_kernel, frames, spaces), in_spe...]
    pallas_call x2 -> x3, Pallas kernels: 3.88 us -> 4.81 us  [backward(): pl.pallas_call(functools.partial(backward_kernel, axis, distances, gains_...]
  transfers between devices with their start and end apart: 16 -> 16, of which waited for: 5 -> 5; matrix products, arithmetic and copies ran while one was open for 0% -> 0% of each run, Pallas kernels for 13% -> 16%
where the time goes in v12:
time: 68 us; the launch traced here: 67.8 us
  starting transfers between devices  25.1 us (37%)
  waiting for transfers between devices  20.8 us (31%)
  Pallas kernels  18.8 us (28%)
  between operations  2.06 us (3%)
  local copies, waits for them, and re-layouts  0.92 us (1%)
    ppermute x16, starting transfers between devices, swap(): return lax.ppermute(field, axis, [(i, i ^ distance) for i in range(size)])  25.1 us
    ppermute x16, waiting for transfers between devices, swap(): return lax.ppermute(field, axis, [(i, i ^ distance) for i in range(size)])  20.8 us
    pallas_call x1, Pallas kernels, forward(): pl.pallas_call(functools.partial(forward_kernel, axis), in_specs=[pl.Bloc...  6.52 us
    pallas_call x1, Pallas kernels, temporal(): pl.pallas_call(functools.partial(temporal_kernel, frames, spaces), in_spe...  4.85 us
    pallas_call x3, Pallas kernels, backward(): pl.pallas_call(functools.partial(backward_kernel, axis, distances, gains_...  4.81 us
  transfers between devices with their start and end apart: 16, of which 5 were waited for; matrix products, arithmetic and copies ran while one was open for 0% of the time, Pallas kernels for 16%

profile of v12, /device:TPU:0, one launch (start us, length us, event | category | flops | bytes accessed | tf_op | source)
XLA Modules:
  0.0 67.8 jit_solution(4456229414693206320)
XLA Ops:
  0.6 1.3 %pack_cotangent.1 = (bf16[2,128,384]{2,1,0:T(8,128)(2,1)S(1)}, bf16[2,128,384]{2,1,0:T(8,128)(2,1)S(1)}, bf16[2,128,384]{2,1,0:T(8,128)(2,1)S(1)}, bf16[2,128,384]{2,1,0:T(8,128)(2,1)S(1)}) custom-call(bf16[128,3072]{1,0:T(8,128)(2,1)} %bitcast.19), custom_call_target="tpu_custom_call" | custom-call | flops 100000000 | tf_op jit(solution)/shard_map/pack_cotangent/pallas_call | solution.py:198
  2.0 5.1 %collective-permute-start.3 = (bf16[2,128,384]{2,1,0:T(8,128)(2,1)S(1)}, bf16[2,128,384]{2,1,0:T(8,128)(2,1)S(1)}, u32[]{:S(2)}, u32[]{:S(2)}) collective-permute-start(bf16[2,128,384]{2,1,0:T(8,128)(2,1)S(1)} %get-tuple-element.54), channel_id=1, source_target_pairs={{0,6},{2,4},{4,2},{6,0},{1,7},{3,5},{5,3},{7,1},{8,14},{10,12},{12... | collective-permute-start | bytes 589832 | tf_op jit(solution)/shard_map/ppermute | solution.py:463
  7.1 0.6 collective-permute-start.5
  7.7 6.5 %spatial_forward.1 = (f32[12,256,256]{2,1,0:T(8,128)S(1)}, bf16[3,128,256]{2,1,0:T(8,128)(2,1)S(1)}, bf16[3,128,256]{2,1,0:T(8,128)(2,1)}, bf16[3,128,256]{2,1,0:T(8,128)(2,1)}, bf16[3,128,256]{2,1,0:T(8,128)(2,1)}) custom-call(bf16[256,1536]{1,0:T(8,128)(2,1)} %bitcast.13, bf16[256,1536]{1,0:T(8,128)(2,1)} %bitcast.15, bf16[256,1536]{1,0:T(8,128)(2,1)} %bitcast.17), custom_call_target="tpu_custom_call" | custom-call | flops 600000000 | tf_op jit(solution)/shard_map/spatial_forward/pallas_call | solution.py:76
  14.3 1.4 %collective-permute-start = (bf16[3,128,256]{2,1,0:T(8,128)(2,1)}, bf16[3,128,256]{2,1,0:T(8,128)(2,1)S(1)}, u32[]{:S(2)}, u32[]{:S(2)}) collective-permute-start(bf16[3,128,256]{2,1,0:T(8,128)(2,1)} %get-tuple-element.51), channel_id=1, source_target_pairs={{0,2},{2,0},{4,6},{6,4},{1,3},{3,1},{5,7},{7,5},{8,10},{10,8},{12,... | collective-permute-start | bytes 589832 | tf_op jit(solution)/shard_map/ppermute | solution.py:463
  15.7 2.9 %collective-permute-start.1 = (bf16[3,128,256]{2,1,0:T(8,128)(2,1)}, bf16[3,128,256]{2,1,0:T(8,128)(2,1)}, u32[]{:S(2)}, u32[]{:S(2)}) collective-permute-start(bf16[3,128,256]{2,1,0:T(8,128)(2,1)} %get-tuple-element.52), channel_id=1, source_target_pairs={{0,4},{2,6},{4,0},{6,2},{1,5},{3,7},{5,1},{7,3},{8,12},{10,14},{12... | collective-permute-start | bytes 589832 | tf_op jit(solution)/shard_map/ppermute | solution.py:463
  18.7 6.9 %collective-permute-done.4.refs_1_ = bf16[2,128,384]{2,1,0:T(8,128)(2,1)S(1)} collective-permute-done((bf16[2,128,384]{2,1,0:T(8,128)(2,1)S(1)}, bf16[2,128,384]{2,1,0:T(8,128)(2,1)S(1)}, u32[]{:S(2)}, u32[]{:S(2)}) %collective-permute-start.4) | collective-permute-done | bytes 196640 | tf_op jit(solution)/shard_map/ppermute | solution.py:463
  25.6 1.3 %turn_cotangent.1 = (bf16[6,3,128,128]{3,2,1,0:T(8,128)(2,1)S(1)}, bf16[2,3,128,128]{3,2,1,0:T(8,128)(2,1)}, bf16[2,3,128,128]{3,2,1,0:T(8,128)(2,1)}) custom-call(bf16[2,128,384]{2,1,0:T(8,128)(2,1)S(1)} %collective-permute-done.3.refs_0_, bf16[2,128,384]{2,1,0:T(8,128)(2,1)S(1)} %collective-permute-done.4.refs_1_, ...), custom_call_target="tpu_custom_call" | custom-call | flops 200000000 | tf_op jit(solution)/shard_map/turn_cotangent/pallas_call | solution.py:247
  26.9 0.8 %copy-done = bf16[6,3,128,128]{3,2,1,0:T(8,128)(2,1)} copy-done((bf16[6,3,128,128]{3,2,1,0:T(8,128)(2,1)}, bf16[6,3,128,128]{3,2,1,0:T(8,128)(2,1)S(1)}, u32[]{:S(2)}) %copy-start) | copy-done | bytes 589848
  27.7 1.7 %collective-permute-start.6 = (bf16[2,3,128,128]{3,2,1,0:T(8,128)(2,1)}, bf16[2,3,128,128]{3,2,1,0:T(8,128)(2,1)}, u32[]{:S(2)}, u32[]{:S(2)}) collective-permute-start(bf16[2,3,128,128]{3,2,1,0:T(8,128)(2,1)} %get-tuple-element.64), channel_id=1, source_target_pairs={{0,1},{1,0},{2,3},{3,2},{4,5},{5,4},{6,7},{7,6},{8,9},{9,8},{10,11... | collective-permute-start | bytes 589832 | tf_op jit(solution)/shard_map/ppermute | solution.py:463
  31.2 6.3 %collective-permute-done.1.refs_1_ = bf16[3,128,256]{2,1,0:T(8,128)(2,1)} collective-permute-done((bf16[3,128,256]{2,1,0:T(8,128)(2,1)}, bf16[3,128,256]{2,1,0:T(8,128)(2,1)}, u32[]{:S(2)}, u32[]{:S(2)}) %collective-permute-start.1) | collective-permute-done | bytes 196640 | tf_op jit(solution)/shard_map/ppermute | solution.py:463
  37.7 4.8 %temporal.1 = (bf16[3,128,256]{2,1,0:T(8,128)(2,1)S(1)}, bf16[3,128,256]{2,1,0:T(8,128)(2,1)S(1)}, bf16[3,128,256]{2,1,0:T(8,128)(2,1)S(1)}, bf16[3,128,256]{2,1...) custom-call(s32[1]{0:T(128)S(6)} %copy.19.length_ref, ...), custom_call_target="tpu_custom_call" | custom-call | flops 400000000 | tf_op jit(solution)/shard_map/temporal/pallas_call | solution.py:419
  42.6 2.7 %collective-permute-start.8 = (bf16[3,128,256]{2,1,0:T(8,128)(2,1)S(1)}, bf16[3,128,256]{2,1,0:T(8,128)(2,1)S(1)}, u32[]{:S(2)}, u32[]{:S(2)}) collective-permute-start(bf16[3,128,256]{2,1,0:T(8,128)(2,1)S(1)} %get-tuple-element.70), channel_id=1, source_target_pairs={{0,6},{2,4},{4,2},{6,0},{1,7},{3,5},{5,3},{7,1},{8,14},{10,12},{12... | collective-permute-start | bytes 589832 | tf_op jit(solution)/shard_map/ppermute | solution.py:463
  45.3 2.6 %collective-permute-start.9 = (bf16[3,128,256]{2,1,0:T(8,128)(2,1)S(1)}, bf16[3,128,256]{2,1,0:T(8,128)(2,1)S(1)}, u32[]{:S(2)}, u32[]{:S(2)}) collective-permute-start(bf16[3,128,256]{2,1,0:T(8,128)(2,1)S(1)} %get-tuple-element.71), channel_id=1, source_target_pairs={{0,4},{2,6},{4,0},{6,2},{1,5},{3,7},{5,1},{7,3},{8,12},{10,14},{12... | collective-permute-start | bytes 589832 | tf_op jit(solution)/shard_map/ppermute | solution.py:463
  48.1 1.5 %collective-permute-start.11 = (f32[16,128]{1,0:T(8,128)S(1)}, f32[16,128]{1,0:T(8,128)S(1)}, u32[]{:S(2)}, u32[]{:S(2)}) collective-permute-start(f32[16,128]{1,0:T(8,128)S(1)} %pad_maximum_fusion.1), channel_id=1, source_target_pairs={{0,16},{8,24},{16,0},{24,8},{1,17},{9,25},{17,1},{25,9},{2,18},{10... | collective-permute-start | bytes 24584 | tf_op jit(solution)/shard_map/ppermute | solution.py:463
  49.5 1.4 %spatial_backward.3 = (bf16[256,1536]{1,0:T(8,128)(2,1)}, bf16[256,1536]{1,0:T(8,128)(2,1)}) custom-call(bf16[256,1536]{1,0:T(8,128)(2,1)S(1)} %get-tuple-element.67.refs_0_, bf16[256,1536]{1,0:T(8,128)(2,1)S(1)} %get-tuple-element.68.refs_1_, bf16[256,1536]{1,0:T(8,128)(2,1)S(1)} %get-tuple-element.69.refs_2_, ...), custom_call_target="tpu_custom_call" | custom-call | flops 200000000 | tf_op jit(solution)/shard_map/spatial_backward/pallas_call | solution.py:159
  51.0 0.7 %collective-permute-done.11 = f32[16,128]{1,0:T(8,128)S(1)} collective-permute-done((f32[16,128]{1,0:T(8,128)S(1)}, f32[16,128]{1,0:T(8,128)S(1)}, u32[]{:S(2)}, u32[]{:S(2)}) %collective-permute-start.11) | collective-permute-done | bytes 8224 | tf_op jit(solution)/shard_map/ppermute | solution.py:463
  51.7 2.4 %collective-permute-start.15 = (f32[32,128]{1,0:T(8,128)S(1)}, f32[32,128]{1,0:T(8,128)S(1)}, u32[]{:S(2)}, u32[]{:S(2)}) collective-permute-start(f32[32,128]{1,0:T(8,128)S(1)} %pad_maximum_fusion.refs_6_), channel_id=1, source_target_pairs={{0,6},{2,4},{4,2},{6,0},{1,7},{3,5},{5,3},{7,1},{8,14},{10,12},{12... | collective-permute-start | bytes 49160 | tf_op jit(solution)/shard_map/ppermute | solution.py:463
  54.1 0.9 %collective-permute-start.14 = (f32[32,128]{1,0:T(8,128)S(1)}, f32[32,128]{1,0:T(8,128)S(1)}, u32[]{:S(2)}, u32[]{:S(2)}) collective-permute-start(f32[32,128]{1,0:T(8,128)S(1)} %pad_maximum_fusion.refs_6_), channel_id=1, source_target_pairs={{0,4},{2,6},{4,0},{6,2},{1,5},{3,7},{5,1},{7,3},{8,12},{10,14},{12... | collective-permute-start | bytes 49160 | tf_op jit(solution)/shard_map/ppermute | solution.py:463
  55.1 3.8 %collective-permute-done.12.refs_4_ = bf16[3,128,256]{2,1,0:T(8,128)(2,1)S(1)} collective-permute-done((bf16[3,128,256]{2,1,0:T(8,128)(2,1)S(1)}, bf16[3,128,256]{2,1,0:T(8,128)(2,1)S(1)}, u32[]{:S(2)}, u32[]{:S(2)}) %collective-permute-start.12) | collective-permute-done | bytes 196640 | tf_op jit(solution)/shard_map/ppermute | solution.py:463
  58.9 2.5 %collective-permute-start.13 = (f32[32,128]{1,0:T(8,128)S(1)}, f32[32,128]{1,0:T(8,128)S(1)}, u32[]{:S(2)}, u32[]{:S(2)}) collective-permute-start(f32[32,128]{1,0:T(8,128)S(1)} %pad_maximum_fusion.refs_6_), channel_id=1, source_target_pairs={{0,2},{2,0},{4,6},{6,4},{1,3},{3,1},{5,7},{7,5},{8,10},{10,8},{12,... | collective-permute-start | bytes 49160 | tf_op jit(solution)/shard_map/ppermute | solution.py:463
  61.4 1.4 %spatial_backward.4 = (bf16[256,1536]{1,0:T(8,128)(2,1)}, bf16[256,1536]{1,0:T(8,128)(2,1)}) custom-call(bf16[256,1536]{1,0:T(8,128)(2,1)S(1)} %get-tuple-element.67.refs_0_, bf16[256,1536]{1,0:T(8,128)(2,1)S(1)} %get-tuple-element.68.refs_1_, bf16[256,1536]{1,0:T(8,128)(2,1)S(1)} %get-tuple-element.69.refs_2_, ...), custom_call_target="tpu_custom_call", output_to_operand_aliasing={{0}: (5, {}), {1}: (6, {})} | custom-call | flops 200000000 | tf_op jit(solution)/shard_map/spatial_backward/pallas_call | solution.py:159
  62.8 3.0 %collective-permute-done.14.refs_8_ = f32[32,128]{1,0:T(8,128)S(1)} collective-permute-done((f32[32,128]{1,0:T(8,128)S(1)}, f32[32,128]{1,0:T(8,128)S(1)}, u32[]{:S(2)}, u32[]{:S(2)}) %collective-permute-start.14) | collective-permute-done | bytes 16416 | tf_op jit(solution)/shard_map/ppermute | solution.py:463
  65.8 2.0 %spatial_backward.5 = (bf16[256,1536]{1,0:T(8,128)(2,1)}, bf16[256,1536]{1,0:T(8,128)(2,1)}, f32[2,16,1536]{2,1,0:T(8,128)}) custom-call(bf16[256,1536]{1,0:T(8,128)(2,1)S(1)} %get-tuple-element.67.refs_0_, bf16[256,1536]{1,0:T(8,128)(2,1)S(1)} %get-tuple-element.68.refs_1_, ...), custom_call_target="tpu_custom_call", output_to_operand_aliasing={{0}: (11, {}), {1}: (12, {})} | custom-call | flops 200000000 | tf_op jit(solution)/shard_map/spatial_backward/pallas_call | solution.py:159
  (23 shorter events, 0.8 us)
Async XLA Ops:
  0.6 30.4 %copy-start.1 = (f32[2,16,1536]{2,1,0:T(8,128)S(1)}, f32[2,16,1536]{2,1,0:T(8,128)}, u32[]{:S(2)}) copy-start(f32[2,16,1536]{2,1,0:T(8,128)} %refs_10_.1) | copy-start | bytes 589828
  2.0 16.7 %collective-permute-start.3 = (bf16[2,128,384]{2,1,0:T(8,128)(2,1)S(1)}, bf16[2,128,384]{2,1,0:T(8,128)(2,1)S(1)}, u32[]{:S(2)}, u32[]{:S(2)}) collective-permute-start(bf16[2,128,384]{2,1,0:T(8,128)(2,1)S(1)} %get-tuple-element.54), channel_id=1, source_target_pairs={{0,6},{2,4},{4,2},{6,0},{1,7},{3,5},{5,3},{7,1},{8,14},{10,12},{12... | collective-permute-start | bytes 589832 | tf_op jit(solution)/shard_map/ppermute | solution.py:463
  7.1 18.5 %collective-permute-start.4 = (bf16[2,128,384]{2,1,0:T(8,128)(2,1)S(1)}, bf16[2,128,384]{2,1,0:T(8,128)(2,1)S(1)}, u32[]{:S(2)}, u32[]{:S(2)}) collective-permute-start(bf16[2,128,384]{2,1,0:T(8,128)(2,1)S(1)} %get-tuple-element.55), channel_id=1, source_target_pairs={{0,4},{2,6},{4,0},{6,2},{1,5},{3,7},{5,1},{7,3},{8,12},{10,14},{12... | collective-permute-start | bytes 589832 | tf_op jit(solution)/shard_map/ppermute | solution.py:463
  7.1 18.5 %collective-permute-start.5 = (bf16[2,128,384]{2,1,0:T(8,128)(2,1)S(1)}, bf16[2,128,384]{2,1,0:T(8,128)(2,1)S(1)}, u32[]{:S(2)}, u32[]{:S(2)}) collective-permute-start(bf16[2,128,384]{2,1,0:T(8,128)(2,1)S(1)} %get-tuple-element.56), channel_id=1, source_target_pairs={{0,2},{2,0},{4,6},{6,4},{1,3},{3,1},{5,7},{7,5},{8,10},{10,8},{12,... | collective-permute-start | bytes 589832 | tf_op jit(solution)/shard_map/ppermute | solution.py:463
  14.3 16.9 %collective-permute-start = (bf16[3,128,256]{2,1,0:T(8,128)(2,1)}, bf16[3,128,256]{2,1,0:T(8,128)(2,1)S(1)}, u32[]{:S(2)}, u32[]{:S(2)}) collective-permute-start(bf16[3,128,256]{2,1,0:T(8,128)(2,1)} %get-tuple-element.51), channel_id=1, source_target_pairs={{0,2},{2,0},{4,6},{6,4},{1,3},{3,1},{5,7},{7,5},{8,10},{10,8},{12,... | collective-permute-start | bytes 589832 | tf_op jit(solution)/shard_map/ppermute | solution.py:463
  15.7 21.8 %collective-permute-start.1 = (bf16[3,128,256]{2,1,0:T(8,128)(2,1)}, bf16[3,128,256]{2,1,0:T(8,128)(2,1)}, u32[]{:S(2)}, u32[]{:S(2)}) collective-permute-start(bf16[3,128,256]{2,1,0:T(8,128)(2,1)} %get-tuple-element.52), channel_id=1, source_target_pairs={{0,4},{2,6},{4,0},{6,2},{1,5},{3,7},{5,1},{7,3},{8,12},{10,14},{12... | collective-permute-start | bytes 589832 | tf_op jit(solution)/shard_map/ppermute | solution.py:463
  18.6 18.9 %collective-permute-start.2 = (bf16[3,128,256]{2,1,0:T(8,128)(2,1)}, bf16[3,128,256]{2,1,0:T(8,128)(2,1)}, u32[]{:S(2)}, u32[]{:S(2)}) collective-permute-start(bf16[3,128,256]{2,1,0:T(8,128)(2,1)} %get-tuple-element.53), channel_id=1, source_target_pairs={{0,6},{2,4},{4,2},{6,0},{1,7},{3,5},{5,3},{7,1},{8,14},{10,12},{12... | collective-permute-start | bytes 589832 | tf_op jit(solution)/shard_map/ppermute | solution.py:463
  26.9 0.8 %copy-start = (bf16[6,3,128,128]{3,2,1,0:T(8,128)(2,1)}, bf16[6,3,128,128]{3,2,1,0:T(8,128)(2,1)S(1)}, u32[]{:S(2)}) copy-start(bf16[6,3,128,128]{3,2,1,0:T(8,128)(2,1)S(1)} %get-tuple-element.66.refs_6_) | copy-start | bytes 1769476
  27.7 9.8 %collective-permute-start.6 = (bf16[2,3,128,128]{3,2,1,0:T(8,128)(2,1)}, bf16[2,3,128,128]{3,2,1,0:T(8,128)(2,1)}, u32[]{:S(2)}, u32[]{:S(2)}) collective-permute-start(bf16[2,3,128,128]{3,2,1,0:T(8,128)(2,1)} %get-tuple-element.64), channel_id=1, source_target_pairs={{0,1},{1,0},{2,3},{3,2},{4,5},{5,4},{6,7},{7,6},{8,9},{9,8},{10,11... | collective-permute-start | bytes 589832 | tf_op jit(solution)/shard_map/ppermute | solution.py:463
  29.5 8.1 %collective-permute-start.7 = (bf16[2,3,128,128]{3,2,1,0:T(8,128)(2,1)}, bf16[2,3,128,128]{3,2,1,0:T(8,128)(2,1)}, u32[]{:S(2)}, u32[]{:S(2)}) collective-permute-start(bf16[2,3,128,128]{3,2,1,0:T(8,128)(2,1)} %get-tuple-element.65), channel_id=1, source_target_pairs={{0,1},{1,0},{2,3},{3,2},{4,5},{5,4},{6,7},{7,6},{8,9},{9,8},{10,11... | collective-permute-start | bytes 589832 | tf_op jit(solution)/shard_map/ppermute | solution.py:463
  42.5 5.5 %collective-permute-start.10 = (f32[8,128]{1,0:T(8,128)S(1)}, f32[8,128]{1,0:T(8,128)S(1)}, u32[]{:S(2)}, u32[]{:S(2)}) collective-permute-start(f32[8,128]{1,0:T(8,128)S(1)} %get-tuple-element.72), channel_id=1, source_target_pairs={{0,8},{8,0},{16,24},{24,16},{1,9},{9,1},{17,25},{25,17},{2,10},{10... | collective-permute-start | bytes 12296 | tf_op jit(solution)/shard_map/ppermute | solution.py:463
  42.6 23.2 %collective-permute-start.8 = (bf16[3,128,256]{2,1,0:T(8,128)(2,1)S(1)}, bf16[3,128,256]{2,1,0:T(8,128)(2,1)S(1)}, u32[]{:S(2)}, u32[]{:S(2)}) collective-permute-start(bf16[3,128,256]{2,1,0:T(8,128)(2,1)S(1)} %get-tuple-element.70), channel_id=1, source_target_pairs={{0,6},{2,4},{4,2},{6,0},{1,7},{3,5},{5,3},{7,1},{8,14},{10,12},{12... | collective-permute-start | bytes 589832 | tf_op jit(solution)/shard_map/ppermute | solution.py:463
  45.3 20.5 %collective-permute-start.9 = (bf16[3,128,256]{2,1,0:T(8,128)(2,1)S(1)}, bf16[3,128,256]{2,1,0:T(8,128)(2,1)S(1)}, u32[]{:S(2)}, u32[]{:S(2)}) collective-permute-start(bf16[3,128,256]{2,1,0:T(8,128)(2,1)S(1)} %get-tuple-element.71), channel_id=1, source_target_pairs={{0,4},{2,6},{4,0},{6,2},{1,5},{3,7},{5,1},{7,3},{8,12},{10,14},{12... | collective-permute-start | bytes 589832 | tf_op jit(solution)/shard_map/ppermute | solution.py:463
  47.9 11.0 %collective-permute-start.12 = (bf16[3,128,256]{2,1,0:T(8,128)(2,1)S(1)}, bf16[3,128,256]{2,1,0:T(8,128)(2,1)S(1)}, u32[]{:S(2)}, u32[]{:S(2)}) collective-permute-start(bf16[3,128,256]{2,1,0:T(8,128)(2,1)S(1)} %get-tuple-element.79), channel_id=1, source_target_pairs={{0,2},{2,0},{4,6},{6,4},{1,3},{3,1},{5,7},{7,5},{8,10},{10,8},{12,... | collective-permute-start | bytes 589832 | tf_op jit(solution)/shard_map/ppermute | solution.py:463
  48.1 3.7 %collective-permute-start.11 = (f32[16,128]{1,0:T(8,128)S(1)}, f32[16,128]{1,0:T(8,128)S(1)}, u32[]{:S(2)}, u32[]{:S(2)}) collective-permute-start(f32[16,128]{1,0:T(8,128)S(1)} %pad_maximum_fusion.1), channel_id=1, source_target_pairs={{0,16},{8,24},{16,0},{24,8},{1,17},{9,25},{17,1},{25,9},{2,18},{10... | collective-permute-start | bytes 24584 | tf_op jit(solution)/shard_map/ppermute | solution.py:463
  51.7 11.1 %collective-permute-start.15 = (f32[32,128]{1,0:T(8,128)S(1)}, f32[32,128]{1,0:T(8,128)S(1)}, u32[]{:S(2)}, u32[]{:S(2)}) collective-permute-start(f32[32,128]{1,0:T(8,128)S(1)} %pad_maximum_fusion.refs_6_), channel_id=1, source_target_pairs={{0,6},{2,4},{4,2},{6,0},{1,7},{3,5},{5,3},{7,1},{8,14},{10,12},{12... | collective-permute-start | bytes 49160 | tf_op jit(solution)/shard_map/ppermute | solution.py:463
  54.1 11.7 %collective-permute-start.14 = (f32[32,128]{1,0:T(8,128)S(1)}, f32[32,128]{1,0:T(8,128)S(1)}, u32[]{:S(2)}, u32[]{:S(2)}) collective-permute-start(f32[32,128]{1,0:T(8,128)S(1)} %pad_maximum_fusion.refs_6_), channel_id=1, source_target_pairs={{0,4},{2,6},{4,0},{6,2},{1,5},{3,7},{5,1},{7,3},{8,12},{10,14},{12... | collective-permute-start | bytes 49160 | tf_op jit(solution)/shard_map/ppermute | solution.py:463
  58.9 6.9 %collective-permute-start.13 = (f32[32,128]{1,0:T(8,128)S(1)}, f32[32,128]{1,0:T(8,128)S(1)}, u32[]{:S(2)}, u32[]{:S(2)}) collective-permute-start(f32[32,128]{1,0:T(8,128)S(1)} %pad_maximum_fusion.refs_6_), channel_id=1, source_target_pairs={{0,2},{2,0},{4,6},{6,4},{1,3},{3,1},{5,7},{7,5},{8,10},{10,8},{12,... | collective-permute-start | bytes 49160 | tf_op jit(solution)/shard_map/ppermute | solution.py:463

commit v13 on v12

--- a/solution.py
+++ b/solution.py
@@ -38,7 +38,7 @@
     return distance if axis is None else jnp.bitwise_xor(lax.axis_index(axis), distance)
 
 
-def forward_kernel(axis, query_ref, key_ref, value_ref, weights_ref, *refs):
+def forward_kernel(axis, chunks, query_ref, key_ref, value_ref, weights_ref, *refs):
     (queries, key_rows, values, arrived), attended_refs = refs[-4:], refs[:-4]
     score_scale = HEAD_DIM ** (-0.5)
     groups, _, width = queries.shape
@@ -65,41 +65,50 @@
             weights = raised * (1.0 / jnp.sum(raised, axis=0, keepdims=True))
             weights_ref[group * own + head] = weights
             attended = dot(values[group, :, cols].T, weights.astype(jnp.bfloat16))
-            attended_refs[group][head] = attended.astype(jnp.bfloat16)
-
-
-def forward(axis, queries, key_rows, values, groups):
+            part, place = (0, head) if head < chunks[group][0] else (1, head - chunks[group][0])
+            ref = attended_refs[sum(len(sizes) for sizes in chunks[:group]) + part]
+            ref[place] = attended.astype(jnp.bfloat16)
+
+
+def forward(axis, queries, key_rows, values, chunks):
     patches, feat = queries.shape
-    heads = feat // HEAD_DIM
-    own = heads // groups
+    heads, groups = feat // HEAD_DIM, len(chunks)
     fields = [in_hbm(field) for field in (queries, key_rows, values)]
     weights, *attended = pl.pallas_call(
-        functools.partial(forward_kernel, axis),
+        functools.partial(forward_kernel, axis, chunks),
         in_specs=[pl.BlockSpec(memory_space=pltpu.HBM)] * 3,
-        out_specs=[pl.BlockSpec(memory_space=pltpu.VMEM)] * (1 + groups),
+        out_specs=[pl.BlockSpec(memory_space=pltpu.VMEM)] * (1 + sum(map(len, chunks))),
         scratch_shapes=[pltpu.VMEM((groups, patches, feat // groups), jnp.bfloat16)] * 3
         + [pltpu.SemaphoreType.DMA((groups, 3))],
         out_shape=[jax.ShapeDtypeStruct((heads, patches, patches), jnp.float32)]
-        + [jax.ShapeDtypeStruct((own, HEAD_DIM, patches), jnp.bfloat16)] * groups,
+        + [
+            jax.ShapeDtypeStruct((size, HEAD_DIM, patches), jnp.bfloat16)
+            for sizes in chunks
+            for size in sizes
+        ],
         compiler_params=params(patches),
         cost_estimate=cost(6),
         name="spatial_forward",
     )(*fields)
-    return weights, attended
-
-
-def backward_group(axis, fields, weights_ref, grad_ref, distance, scratch, results, sent):
+    attended = iter(attended)
+    return weights, [[next(attended) for _ in sizes] for sizes in chunks]
+
+
+def backward_group(axis, whole, first, fields, weights_ref, grad_refs, distance, scratch, results, sent):
     query_ref, key_ref, value_ref = fields
     score_scale = HEAD_DIM ** (-0.5)
-    own = grad_ref.shape[0]
-    start = partner(axis, distance) * (own * HEAD_DIM)
+    grads = [(ref, place) for ref in grad_refs for place in range(ref.shape[0])]
+    own = len(grads)
+    start = (partner(axis, distance) * whole + first) * HEAD_DIM
     columns = [
         pl.ds(pl.multiple_of(start + head * HEAD_DIM, HEAD_DIM), HEAD_DIM) for head in range(own)
     ]
-    spatial_grads = [dot(value_ref[:, columns[head]], grad_ref[head]) for head in range(own)]
+    spatial_grads = [
+        dot(value_ref[:, columns[head]], ref[place]) for head, (ref, place) in enumerate(grads)
+    ]
     all_scores = []
     for head, spatial_grad in enumerate(spatial_grads):
-        weights = weights_ref[distance * own + head]
+        weights = weights_ref[distance * whole + first + head]
         row_sum = jnp.sum(spatial_grad * weights, axis=0, keepdims=True)
         scores = weights * (spatial_grad - row_sum) * score_scale
         all_scores.append(scores.astype(jnp.bfloat16))
@@ -118,9 +127,11 @@
     return copies
 
 
-def backward_kernel(axis, distances, gains_of, *refs):
+def backward_kernel(axis, distances, arrays, whole, first, gains_of, *refs):
     fields, weights_ref, refs = refs[:3], refs[3], refs[4:]
-    grad_refs, refs = refs[: len(distances)], refs[len(distances) :]
+    ends = [sum(arrays[: place + 1]) for place in range(len(arrays))]
+    grad_refs = [refs[end - size : end] for end, size in zip(ends, arrays)]
+    refs = refs[ends[-1] :]
     *refs, gq, gk, sent = refs
     copies = []
     if gains_of:
@@ -131,12 +142,14 @@
         copies.append(copy)
     else:
         gq_ref, gk_ref = refs[-2:]
-    for place, (distance, grad_ref) in enumerate(zip(distances, grad_refs)):
+    for place, distance in enumerate(distances):
         copies += backward_group(
             axis,
+            whole,
+            first,
             fields,
             weights_ref,
-            grad_ref,
+            grad_refs[place],
             distance,
             (gq.at[place], gk.at[place]),
             (gq_ref, gk_ref),
@@ -146,10 +159,13 @@
         copy.wait()
 
 
-def backward(axis, fields, weights, grads, distances, earlier=(), mixed=(), gains=None, gains_of=()):
+def backward(
+    axis, fields, weights, grads, distances, whole, first=0, earlier=(), mixed=(), gains=None, gains_of=()
+):
     patches, feat = fields[0].shape
-    own = grads[0].shape[0]
-    operands = [*fields, weights, *grads] + ([*mixed, gains] if gains_of else [])
+    own = sum(part.shape[0] for part in grads[0])
+    arrays = [len(parts) for parts in grads]
+    operands = [*fields, weights, *sum(grads, [])] + ([*mixed, gains] if gains_of else [])
     block = pltpu.VMEM((len(distances), patches, own * HEAD_DIM), jnp.bfloat16)
     out_shape = [jax.ShapeDtypeStruct((patches, feat), jnp.bfloat16)] * 2
     scratch = [block, block, pltpu.SemaphoreType.DMA((len(distances) + 1, 2))]
@@ -157,7 +173,7 @@
         out_shape.append(jax.ShapeDtypeStruct(gains.shape, jnp.float32))
         scratch.insert(0, pltpu.VMEM(gains.shape, jnp.float32))
     return pl.pallas_call(
-        functools.partial(backward_kernel, axis, distances, gains_of),
+        functools.partial(backward_kernel, axis, distances, arrays, whole, first, gains_of),
         in_specs=[pl.BlockSpec(memory_space=pltpu.VMEM)] * len(operands)
         + [pl.BlockSpec(memory_space=pl.ANY)] * len(earlier),
         out_specs=[pl.BlockSpec(memory_space=pl.ANY)] * len(out_shape),
@@ -233,9 +249,8 @@
             copy = pltpu.make_async_copy(own_ref, own_hbm, sent)
             copy.start()
         else:
-            half = frames // 2
-            other_refs[2 * space - 2][...] = turned[:half]
-            other_refs[2 * space - 1][...] = turned[half:]
+            for head in range(heads):
+                other_refs[(space - 1) * heads + head][:, 0] = turned[:, head]
     copy.wait()
 
 
@@ -243,13 +258,15 @@
     spaces, patches, feat = pieces[0].shape
     frames, heads = len(pieces), feat // HEAD_DIM
     turned = (heads, HEAD_DIM, patches)
-    sizes = [frames + spaces] + [frames // 2, frames - frames // 2] * (spaces - 1)
+    others = heads * (spaces - 1)
+    other = jax.ShapeDtypeStruct((frames, 1, HEAD_DIM, patches), pieces[0].dtype)
     return pl.pallas_call(
         functools.partial(turn_kernel, frames),
         in_specs=[pl.BlockSpec(memory_space=pltpu.VMEM)] * (frames + 1),
         out_specs=[pl.BlockSpec(memory_space=pltpu.HBM)]
-        + [pl.BlockSpec(memory_space=pltpu.VMEM)] * (len(sizes) - 1),
-        out_shape=[jax.ShapeDtypeStruct((size,) + turned, pieces[0].dtype) for size in sizes],
+        + [pl.BlockSpec(memory_space=pltpu.VMEM)] * others,
+        out_shape=[jax.ShapeDtypeStruct((frames + spaces,) + turned, pieces[0].dtype)]
+        + [other] * others,
         scratch_shapes=[
             pltpu.VMEM((frames,) + turned, pieces[0].dtype),
             pltpu.VMEM((frames + spaces,) + turned, pieces[0].dtype),
@@ -349,75 +366,99 @@
     return jnp.concatenate(all_mixed, axis=0)
 
 
-def temporal_kernel(frames, spaces, length_ref, task_ref, *refs):
-    attended_refs, (gain_ref, *other_refs), refs = (
-        refs[: frames - 1],
-        refs[frames - 1 : frames - 2 + 2 * spaces],
-        refs[frames - 2 + 2 * spaces :],
-    )
-    (own_hbm, *field_refs), grad_refs, refs = refs[:4], refs[4 : frames + 4], refs[frames + 4 :]
-    mixed_ref, *kept_refs, attended, grads, wide, own_ref, arrived = refs
-    heads, lanes = own_ref.shape[1], own_ref.shape[3]
+def temporal_kernel(frames, spaces, heads, length_ref, task_ref, *refs):
+    first, count, whole = heads
+    refs = list(refs)
+
+    def take(number):
+        taken, refs[:] = refs[:number], refs[number:]
+        return taken
+
+    attended_refs, (gain_ref,), other_refs = take(frames - 1), take(1), take((spaces - 1) * count)
+    earlier_refs = take(3 if first else 0)
+    (own_hbm,), field_refs = take(1), take(0 if first else 3)
+    grad_refs, (mixed_ref,), kept_refs = take(frames), take(1), take(len(field_refs))
+    attended, grads, wide, own_ref, arrived = refs
+    lanes = own_ref.shape[3]
+    own_copies = [
+        pltpu.make_async_copy(
+            own_hbm.at[:, first + place], own_ref.at[:, place], arrived.at[place]
+        )
+        for place in range(count)
+    ]
     copies = [
-        pltpu.make_async_copy(own_hbm.at[:, head], own_ref.at[:, head], arrived.at[head])
-        for head in range(heads)
-    ] + [
-        pltpu.make_async_copy(source, target, arrived.at[heads + index])
+        pltpu.make_async_copy(source, target, arrived.at[count + index])
         for index, (source, target) in enumerate(zip(field_refs, kept_refs))
     ]
-    for copy in copies:
+    for copy in own_copies + copies:
         copy.start()
-    half = frames // 2
-    mixed_ref[...] = jnp.full(mixed_ref.shape, task_ref[0].astype(jnp.float32))
-
-    def load_upstream(space, head, t, rows):
+    if first:
+        *plane_refs, rows_ref = earlier_refs
+        mixed_ref[...] = rows_ref[...]
+        for ref, earlier_ref in zip(grad_refs, plane_refs):
+            ref[:first] = earlier_ref[...]
+    else:
+        mixed_ref[...] = jnp.full(mixed_ref.shape, task_ref[0].astype(jnp.float32))
+
+    def load_upstream(space, place, t, rows):
         if space == 0:
-            return own_ref[t, head, rows, :]
-        return other_refs[2 * space - 2 + t // half][t % half, head, rows, :]
+            return own_ref[t, place, rows, :]
+        return other_refs[(space - 1) * count + place][t, 0, rows, :]
 
     places = [
         pl.ds(pl.multiple_of(partner("space", space) * lanes, lanes), lanes)
         for space in range(spaces)
     ]
-    for head in range(heads):
-        copies[head].wait()
+    for place in range(count):
+        own_copies[place].wait()
         for space, here in enumerate(places):
-            attended[head, space, partner("tm", 0)] = own_ref[frames + space, head]
+            attended[place, space, partner("tm", 0)] = own_ref[frames + space, place]
             for distance, ref in enumerate(attended_refs):
-                attended[head, space, partner("tm", distance + 1)] = ref[head, :, here]
+                source = place + (first if ref.shape[0] == whole else 0)
+                attended[place, space, partner("tm", distance + 1)] = ref[source, :, here]
         mixed = [
             temporal_part(
                 length_ref[0],
-                lambda t, rows: attended[head, space, t, rows, :],
-                functools.partial(load_upstream, space, head),
-                lambda rows: gain_ref[head, rows, :],
-                wide.at[head % 2, space, 0],
-                wide.at[head % 2, space, 1],
-                wide.at[head % 2, space, 2],
-                grads.at[head, space],
+                lambda t, rows: attended[place, space, t, rows, :],
+                functools.partial(load_upstream, space, place),
+                lambda rows: gain_ref[first + place, rows, :],
+                wide.at[place % 2, space, 0],
+                wide.at[place % 2, space, 1],
+                wide.at[place % 2, space, 2],
+                grads.at[place, space],
             )
             for space in range(spaces)
         ]
         summed = functools.reduce(jnp.add, mixed)
-        mixed_ref[pl.ds(head, 1), :] = jnp.sum(summed.T, axis=0, keepdims=True) * 0.5
+        mixed_ref[pl.ds(first + place, 1), :] = jnp.sum(summed.T, axis=0, keepdims=True) * 0.5
         for distance, ref in enumerate(grad_refs):
             frame = partner("tm", distance)
+            target = place + (first if ref.shape[0] == whole else 0)
             for space, here in enumerate(places):
-                ref[head, :, here] = grads[head, space, frame]
-    for copy in copies[heads:]:
+                ref[target, :, here] = grads[place, space, frame]
+    for copy in copies:
         copy.wait()
 
 
-def temporal(lengths, task_ids, attended, upstream, gain, fields):
-    _, heads, feat, lanes = upstream[0].shape
-    frames, spaces = len(attended) + 1, (len(upstream) + 1) // 2
+def temporal(lengths, task_ids, attended, upstream, gain, fields, heads, earlier):
+    feat, lanes = upstream[0].shape[2:]
+    first, count, whole = heads
+    frames, spaces = len(attended) + 1, 1 + (len(upstream) - 1) // whole
     patches = spaces * lanes
-    rows = -(-(heads + 1) // 8) * 8
-    operands = [*attended, gain, *upstream[1:]]
+    others = [
+        upstream[1 + (space - 1) * whole + first + place]
+        for space in range(1, spaces)
+        for place in range(count)
+    ]
+    rows = -(-(whole + 1) // 8) * 8
+    sizes = [whole if first else count] * 2 + [count] * (frames - 2)
+    operands = [*attended, gain, *others, *earlier]
+    fields = [] if first else fields
     in_place = [in_hbm(field) for field in (upstream[0], *fields)]
-    block = (heads, spaces, frames, feat, lanes)
+    block = (count, spaces, frames, feat, lanes)
+    own = (upstream[0].shape[0], count, feat, lanes)
     results = pl.pallas_call(
-        functools.partial(temporal_kernel, frames, spaces),
+        functools.partial(temporal_kernel, frames, spaces, heads),
         in_specs=[pl.BlockSpec(memory_space=pltpu.SMEM)] * 2
         + [pl.BlockSpec(memory_space=pltpu.VMEM)] * len(operands)
         + [pl.BlockSpec(memory_space=pltpu.HBM)] * len(in_place),
@@ -426,14 +467,14 @@
             pltpu.VMEM(block, jnp.bfloat16),
             pltpu.VMEM(block, jnp.bfloat16),
             pltpu.VMEM((2, spaces, 3, frames, feat, lanes), jnp.float32),
-            pltpu.VMEM(upstream[0].shape, upstream[0].dtype),
-            pltpu.SemaphoreType.DMA((heads + len(fields),)),
+            pltpu.VMEM(own, upstream[0].dtype),
+            pltpu.SemaphoreType.DMA((count + len(fields),)),
         ],
-        out_shape=[jax.ShapeDtypeStruct((heads, feat, patches), jnp.bfloat16)] * frames
+        out_shape=[jax.ShapeDtypeStruct((size, feat, patches), jnp.bfloat16) for size in sizes]
         + [jax.ShapeDtypeStruct((rows, feat), jnp.float32)]
         + [jax.ShapeDtypeStruct(field.shape, field.dtype) for field in fields],
         compiler_params=params(patches),
-        cost_estimate=cost(4),
+        cost_estimate=cost(2000),
         name="temporal",
     )(lengths, task_ids, *operands, *in_place)
     return list(results[:frames]), results[frames], results[frames + 1 :]
@@ -480,45 +521,71 @@
     for distance in range(1, frames):
         pieces[distance] = swap(pieces[distance], "tm", frames, distance)
     fields = (queries, key_rows, values)
-    weights, attended = forward("tm", *fields, frames)
-    for distance in range(1, frames):
-        attended[distance] = swap(attended[distance], "tm", frames, distance)
+    early = max(1, own - 1)
+    late = own - early
+    weights, attended = forward(
+        "tm", *fields, [(own,), (own,)] + [(early, late)] * (frames - 2)
+    )
+    plane, near, *far = [parts[0] for parts in attended]
+    late_far = [parts[1] for parts in attended[2:]]
+    near = swap(near, "tm", frames, 1)
+    far = [swap(part, "tm", frames, distance) for distance, part in enumerate(far, 2)]
     backwards, _ = lax.optimization_barrier((pieces[::-1], weights))
-    upstream = list(turn(backwards[::-1], attended[0]))
+    upstream = list(turn(backwards[::-1], plane))
+    late_far, upstream[0] = lax.optimization_barrier((late_far, upstream[0]))
     for index in range(1, len(upstream)):
-        upstream[index] = swap(upstream[index], "space", spaces, (index + 1) // 2)
+        upstream[index] = swap(upstream[index], "space", spaces, 1 + (index - 1) // own)
+    late_far = [swap(part, "tm", frames, distance) for distance, part in enumerate(late_far, 2)]
     rows = lax.dynamic_index_in_dim(gains, task_ids[0], 1, keepdims=False)
     product = lax.dynamic_slice_in_dim(rows[0] * rows[1], frame * width, width, 0)
     gain = jnp.broadcast_to(
         product.reshape(own, HEAD_DIM, 1), (own, HEAD_DIM, patches // spaces)
     )
-    grads, mixed, kept = temporal(
-        lengths, task_ids, attended[1:], upstream, gain, fields
-    )
-    for distance in reversed(range(1, frames)):
-        grads[distance] = swap(grads[distance], "tm", frames, distance)
+    (own_part, near_part, *far_grads), mixed, kept = temporal(
+        lengths, task_ids, [near, *far], upstream, gain, fields, (0, early, own), ()
+    )
+    far_grads = [swap(part, "tm", frames, distance) for distance, part in enumerate(far_grads, 2)]
+    (here, near_grads, *late_grads), mixed, _ = temporal(
+        lengths,
+        task_ids,
+        [near, *late_far],
+        upstream,
+        gain,
+        fields,
+        (early, late, own),
+        (own_part, near_part, mixed),
+    )
+    late_grads = [
+        swap(part, "tm", frames, distance) for distance, part in enumerate(late_grads, 2)
+    ]
+    near_grads = swap(near_grads, "tm", frames, 1)
+    grads = [[here], [near_grads]] + [list(parts) for parts in zip(far_grads, late_grads)]
     here = grads[0]
     for bit in range(clips.bit_length() - 1):
         other = swap(mixed, "dp", clips, 1 << bit)
         if bit == 0:
-            here, other = lax.optimization_barrier((here, other))
+            here, far_grads, other = lax.optimization_barrier((here, far_grads, other))
         mixed = jnp.concatenate([mixed, other], axis=0)
-    results = backward("tm", kept, weights, [here], [0])
+    results = backward("tm", kept, weights, [here], [0], own)
     mixed, results = lax.optimization_barrier((mixed, results))
-    near, grads[1] = lax.optimization_barrier((mixed, grads[1]))
-    mixed = [mixed, swap(near, "tm", frames, 1)] + [
+    close, grads[1] = lax.optimization_barrier((mixed, grads[1]))
+    mixed = [mixed, swap(close, "tm", frames, 1)] + [
         swap(mixed, "tm", frames, distance) for distance in range(2, frames)
     ]
-    last = range(frames - 1, 0, -1)
     if frames > 2:
-        results = backward("tm", kept, weights, [grads[1]], [1], results)
-        last = range(frames - 1, 1, -1)
+        results = backward(
+            "tm", kept, weights, [[part] for part in far_grads], list(range(2, frames)), own, 0, results
+        )
+        results = backward("tm", kept, weights, [grads[1]], [1], own, 0, results)
+    last = list(range(frames - 1, 1, -1)) or [1]
     grad_queries, grad_keys, grad_gains = backward(
         "tm",
         kept,
         weights,
-        [grads[distance] for distance in last],
-        list(last),
+        [grads[distance][-1:] for distance in last],
+        last,
+        own,
+        early if frames > 2 else 0,
         results,
         mixed,
         gains,
@@ -574,8 +641,8 @@
         field.reshape(patches, feat) for field in (query_heads, key_heads, value_heads)
     )
     fields = (queries, key_rows, values)
-    weights, attended = forward(None, *fields, 1)
-    attended_field = jnp.transpose(attended[0], (2, 0, 1)).reshape(1, 1, patches, feat)
+    weights, attended = forward(None, *fields, [(heads,)])
+    attended_field = jnp.transpose(attended[0][0], (2, 0, 1)).reshape(1, 1, patches, feat)
     upstream = lax.all_to_all(
         lax.all_to_all(cotangent, "space", split_axis=3, concat_axis=2, tiled=True),
         "tm",
@@ -610,7 +677,7 @@
         tiled=True,
     )
     head_grads = jnp.transpose(returned.reshape(patches, heads, HEAD_DIM), (1, 2, 0))
-    grad_queries, grad_keys = backward(None, fields, weights, [head_grads], [0])
+    grad_queries, grad_keys = backward(None, fields, weights, [[head_grads]], [0], heads)
     return (
         grad_queries.reshape(query_heads.shape),
         grad_keys.reshape(query_heads.shape),
@@ -624,7 +691,7 @@
     def local(query_heads, *others):
         heads = query_heads.shape[3] // HEAD_DIM
         powers = all(size & (size - 1) == 0 for size in (clips, frames, spaces))
-        if powers and 2 <= frames <= 4 and heads % frames == 0:
+        if powers and 2 <= frames <= 4 and heads % frames == 0 and heads > frames:
             return split_by_heads(query_heads, *others, clips, frames, spaces)
         return split_by_patches(query_heads, *others)
 

time: 68 us -> 70.6 us (1.038)
  waiting for transfers between devices: 20.8 us -> 9.36 us
  starting transfers between devices: 25.1 us -> 32.7 us
  Pallas kernels: 18.8 us -> 23.2 us
  local copies, waits for them, and re-layouts: 0.92 us -> 2.8 us
    ppermute x16 -> x21, waiting for transfers between devices: 20.8 us -> 9.36 us  [swap(): return lax.ppermute(field, axis, [(i, i ^ distance) for i in range(size)])]
    ppermute x16 -> x21, starting transfers between devices: 25.1 us -> 32.7 us  [swap(): return lax.ppermute(field, axis, [(i, i ^ distance) for i in range(size)])]
    pallas_call x5 -> x7, Pallas kernels: 16.2 us -> 20.6 us  [the longest x2 7.34 us: temporal(): pl.pallas_call(functools.partial(temporal_kernel, frames, spaces, heads),...]
    unnamed x4 -> x10, local copies, waits for them, and re-layouts: 0.81 us -> 2.7 us
  transfers between devices with their start and end apart: 16 -> 21, of which waited for: 5 -> 5; matrix products, arithmetic and copies ran while one was open for 0% -> 0% of each run, Pallas kernels for 16% -> 29%
where the time goes in v13:
time: 70.6 us; the launch traced here: 70.3 us
  starting transfers between devices  32.7 us (46%)
  Pallas kernels  23.2 us (33%)
  waiting for transfers between devices  9.36 us (13%)
  local copies, waits for them, and re-layouts  2.8 us (4%)
  between operations  2.11 us (3%)
    ppermute x21, starting transfers between devices, swap(): return lax.ppermute(field, axis, [(i, i ^ distance) for i in range(size)])  32.7 us
    ppermute x21, waiting for transfers between devices, swap(): return lax.ppermute(field, axis, [(i, i ^ distance) for i in range(size)])  9.36 us
    pallas_call x2, Pallas kernels, temporal(): pl.pallas_call(functools.partial(temporal_kernel, frames, spaces, heads),...  7.34 us
    pallas_call x4, Pallas kernels, backward(): pl.pallas_call(functools.partial(backward_kernel, axis, distances, arrays...  6.92 us
    pallas_call x1, Pallas kernels, forward(): pl.pallas_call(functools.partial(forward_kernel, axis, chunks), in_specs=...  6.36 us
    unnamed x10, local copies, waits for them, and re-layouts  2.7 us
  transfers between devices with their start and end apart: 21, of which 5 were waited for; matrix products, arithmetic and copies ran while one was open for 0% of the time, Pallas kernels for 29%

profile of v13, /device:TPU:0, one launch (start us, length us, event | category | flops | bytes accessed | tf_op | source)
XLA Modules:
  0.0 70.3 jit_solution(8172090775685474554)
XLA Ops:
  0.6 1.3 %pack_cotangent.1 = (bf16[2,128,384]{2,1,0:T(8,128)(2,1)S(1)}, bf16[2,128,384]{2,1,0:T(8,128)(2,1)S(1)}, bf16[2,128,384]{2,1,0:T(8,128)(2,1)S(1)}, bf16[2,128,384]{2,1,0:T(8,128)(2,1)S(1)}) custom-call(bf16[128,3072]{1,0:T(8,128)(2,1)} %bitcast.13), custom_call_target="tpu_custom_call" | custom-call | flops 100000000 | tf_op jit(solution)/shard_map/pack_cotangent/pallas_call | solution.py:214
  2.0 5.1 %collective-permute-start.3 = (bf16[2,128,384]{2,1,0:T(8,128)(2,1)S(1)}, bf16[2,128,384]{2,1,0:T(8,128)(2,1)S(1)}, u32[]{:S(2)}, u32[]{:S(2)}) collective-permute-start(bf16[2,128,384]{2,1,0:T(8,128)(2,1)S(1)} %get-tuple-element.69), channel_id=1, source_target_pairs={{0,6},{2,4},{4,2},{6,0},{1,7},{3,5},{5,3},{7,1},{8,14},{10,12},{12... | collective-permute-start | bytes 589832 | tf_op jit(solution)/shard_map/ppermute | solution.py:504
  7.7 6.4 %spatial_forward.1 = (f32[12,256,256]{2,1,0:T(8,128)S(1)}, bf16[3,128,256]{2,1,0:T(8,128)(2,1)S(1)}, bf16[3,128,256]{2,1,0:T(8,128)(2,1)}, bf16[2,128,256]{2,1,0...) custom-call(bf16[256,1536]{1,0:T(8,128)(2,1)} %bitcast.14, ...), custom_call_target="tpu_custom_call" | custom-call | flops 600000000 | tf_op jit(solution)/shard_map/spatial_forward/pallas_call | solution.py:77
  15.3 1.4 %collective-permute-start = (bf16[3,128,256]{2,1,0:T(8,128)(2,1)}, bf16[3,128,256]{2,1,0:T(8,128)(2,1)S(1)}, u32[]{:S(2)}, u32[]{:S(2)}) collective-permute-start(bf16[3,128,256]{2,1,0:T(8,128)(2,1)} %get-tuple-element.66), channel_id=1, source_target_pairs={{0,2},{2,0},{4,6},{6,4},{1,3},{3,1},{5,7},{7,5},{8,10},{10,8},{12,... | collective-permute-start | bytes 589832 | tf_op jit(solution)/shard_map/ppermute | solution.py:504
  16.7 2.9 %collective-permute-start.1 = (bf16[2,128,256]{2,1,0:T(8,128)(2,1)}, bf16[2,128,256]{2,1,0:T(8,128)(2,1)}, u32[]{:S(2)}, u32[]{:S(2)}) collective-permute-start(bf16[2,128,256]{2,1,0:T(8,128)(2,1)} %get-tuple-element.67), channel_id=1, source_target_pairs={{0,4},{2,6},{4,0},{6,2},{1,5},{3,7},{5,1},{7,3},{8,12},{10,14},{12... | collective-permute-start | bytes 393224 | tf_op jit(solution)/shard_map/ppermute | solution.py:504
  19.7 5.9 %collective-permute-done.4.refs_1_ = bf16[2,128,384]{2,1,0:T(8,128)(2,1)S(1)} collective-permute-done((bf16[2,128,384]{2,1,0:T(8,128)(2,1)S(1)}, bf16[2,128,384]{2,1,0:T(8,128)(2,1)S(1)}, u32[]{:S(2)}, u32[]{:S(2)}) %collective-permute-start.4) | collective-permute-done | bytes 196640 | tf_op jit(solution)/shard_map/ppermute | solution.py:504
  25.6 1.2 %turn_cotangent.1 = (bf16[6,3,128,128]{3,2,1,0:T(8,128)(2,1)S(1)}, bf16[4,1,128,128]{3,2,1,0:T(8,128)(2,1)}, bf16[4,1,128,128]{3,2,1,0:T(8,128)(2,1)}, bf16[4,1,128,128]{3,2,1,0:T(8,128)(2,1)S(1)}) custom-call(bf16[2,128,384]{2,1,0:T(8,128)(2,1)S(1)} %collective-permute-done.3.refs_0_, bf16[2,128,384]{2,1,0:T(8,128)(2,1)S(1)} %collective-permute-done.4.refs_1_, ...), custom_call_target="tpu_custom_call" | custom-call | flops 200000000 | tf_op jit(solution)/shard_map/turn_cotangent/pallas_call | solution.py:263
  28.3 1.7 %collective-permute-start.6 = (bf16[4,1,128,128]{3,2,1,0:T(8,128)(2,1)}, bf16[4,1,128,128]{3,2,1,0:T(8,128)(2,1)}, u32[]{:S(2)}, u32[]{:S(2)}) collective-permute-start(bf16[4,1,128,128]{3,2,1,0:T(8,128)(2,1)} %get-tuple-element.79), channel_id=1, source_target_pairs={{0,1},{1,0},{2,3},{3,2},{4,5},{5,4},{6,7},{7,6},{8,9},{9,8},{10,11... | collective-permute-start | bytes 393224 | tf_op jit(solution)/shard_map/ppermute | solution.py:504
  31.8 2.2 %collective-permute-done.1.refs_1_ = bf16[2,128,256]{2,1,0:T(8,128)(2,1)} collective-permute-done((bf16[2,128,256]{2,1,0:T(8,128)(2,1)}, bf16[2,128,256]{2,1,0:T(8,128)(2,1)}, u32[]{:S(2)}, u32[]{:S(2)}) %collective-permute-start.1) | collective-permute-done | bytes 131104 | tf_op jit(solution)/shard_map/ppermute | solution.py:504
  34.0 2.0 %collective-permute-start.9 = (bf16[1,128,256]{2,1,0:T(8,128)(2,1)}, bf16[1,128,256]{2,1,0:T(8,128)(2,1)}, u32[]{:S(2)}, u32[]{:S(2)}) collective-permute-start(bf16[1,128,256]{2,1,0:T(8,128)(2,1)} %copy-done.3), channel_id=1, source_target_pairs={{0,6},{2,4},{4,2},{6,0},{1,7},{3,5},{5,3},{7,1},{8,14},{10,12},{12... | collective-permute-start | bytes 196616 | tf_op jit(solution)/shard_map/ppermute | solution.py:504
  36.0 1.5 %collective-permute-start.10 = (bf16[4,1,128,128]{3,2,1,0:T(8,128)(2,1)}, bf16[4,1,128,128]{3,2,1,0:T(8,128)(2,1)}, u32[]{:S(2)}, u32[]{:S(2)}) collective-permute-start(bf16[4,1,128,128]{3,2,1,0:T(8,128)(2,1)} %copy-done.2), channel_id=1, source_target_pairs={{0,1},{1,0},{2,3},{3,2},{4,5},{5,4},{6,7},{7,6},{8,9},{9,8},{10,11... | collective-permute-start | bytes 393224 | tf_op jit(solution)/shard_map/ppermute | solution.py:504
  37.6 4.5 %temporal.2 = (bf16[2,128,256]{2,1,0:T(8,128)(2,1)S(1)}, bf16[2,128,256]{2,1,0:T(8,128)(2,1)S(1)}, bf16[2,128,256]{2,1,0:T(8,128)(2,1)}, bf16[2,128,256]{2,1,0:T...) custom-call(s32[1]{0:T(128)S(6)} %copy.23.length_ref, ...), custom_call_target="tpu_custom_call" | custom-call | flops 199999995904 | tf_op jit(solution)/shard_map/temporal/pallas_call | solution.py:460
  42.2 3.8 %collective-permute-start.13 = (bf16[2,128,256]{2,1,0:T(8,128)(2,1)}, bf16[2,128,256]{2,1,0:T(8,128)(2,1)}, u32[]{:S(2)}, u32[]{:S(2)}) collective-permute-start(bf16[2,128,256]{2,1,0:T(8,128)(2,1)} %get-tuple-element.98), channel_id=1, source_target_pairs={{0,4},{2,6},{4,0},{6,2},{1,5},{3,7},{5,1},{7,3},{8,12},{10,14},{12... | collective-permute-start | bytes 393224 | tf_op jit(solution)/shard_map/ppermute | solution.py:504
  46.0 2.9 %collective-permute-start.14 = (bf16[2,128,256]{2,1,0:T(8,128)(2,1)}, bf16[2,128,256]{2,1,0:T(8,128)(2,1)}, u32[]{:S(2)}, u32[]{:S(2)}) collective-permute-start(bf16[2,128,256]{2,1,0:T(8,128)(2,1)} %get-tuple-element.99), channel_id=1, source_target_pairs={{0,6},{2,4},{4,2},{6,0},{1,7},{3,5},{5,3},{7,1},{8,14},{10,12},{12... | collective-permute-start | bytes 393224 | tf_op jit(solution)/shard_map/ppermute | solution.py:504
  48.9 2.8 %temporal.3 = (bf16[3,128,256]{2,1,0:T(8,128)(2,1)S(1)}, bf16[3,128,256]{2,1,0:T(8,128)(2,1)S(1)}, bf16[1,128,256]{2,1,0:T(8,128)(2,1)S(1)}, bf16[1,128,256]{2,1,0:T(8,128)(2,1)S(1)}, f32[8,128]{1,0:T(8,128)S(1)}) custom-call(s32[1]{0:T(128)S(6)} %copy.23.length_ref, s32[1]{0:T(128)} %copy.22.task_ref, ...), custom_call_target="tpu_custom_call" | custom-call | flops 199999995904 | tf_op jit(solution)/shard_map/temporal/pallas_call | solution.py:460
  51.8 1.0 %collective-permute-start.11 = (bf16[1,128,256]{2,1,0:T(8,128)(2,1)S(1)}, bf16[1,128,256]{2,1,0:T(8,128)(2,1)S(1)}, u32[]{:S(2)}, u32[]{:S(2)}) collective-permute-start(bf16[1,128,256]{2,1,0:T(8,128)(2,1)S(1)} %get-tuple-element.94), channel_id=1, source_target_pairs={{0,6},{2,4},{4,2},{6,0},{1,7},{3,5},{5,3},{7,1},{8,14},{10,12},{12... | collective-permute-start | bytes 196616 | tf_op jit(solution)/shard_map/ppermute | solution.py:504
  52.9 3.3 %collective-permute-start.17 = (bf16[3,128,256]{2,1,0:T(8,128)(2,1)S(1)}, bf16[3,128,256]{2,1,0:T(8,128)(2,1)S(1)}, u32[]{:S(2)}, u32[]{:S(2)}) collective-permute-start(bf16[3,128,256]{2,1,0:T(8,128)(2,1)S(1)} %get-tuple-element.105), channel_id=1, source_target_pairs={{0,2},{2,0},{4,6},{6,4},{1,3},{3,1},{5,7},{7,5},{8,10},{10,8},{12,... | collective-permute-start | bytes 589832 | tf_op jit(solution)/shard_map/ppermute | solution.py:504
  56.3 1.6 %collective-permute-start.16 = (f32[16,128]{1,0:T(8,128)S(1)}, f32[16,128]{1,0:T(8,128)S(1)}, u32[]{:S(2)}, u32[]{:S(2)}) collective-permute-start(f32[16,128]{1,0:T(8,128)S(1)} %pad_maximum_fusion.1), channel_id=1, source_target_pairs={{0,16},{8,24},{16,0},{24,8},{1,17},{9,25},{17,1},{25,9},{2,18},{10... | collective-permute-start | bytes 24584 | tf_op jit(solution)/shard_map/ppermute | solution.py:504
  57.8 1.4 %spatial_backward.4 = (bf16[256,1536]{1,0:T(8,128)(2,1)}, bf16[256,1536]{1,0:T(8,128)(2,1)}) custom-call(bf16[256,1536]{1,0:T(8,128)(2,1)S(1)} %get-tuple-element.85.refs_0_, bf16[256,1536]{1,0:T(8,128)(2,1)S(1)} %get-tuple-element.86.refs_1_, bf16[256,1536]{1,0:T(8,128)(2,1)S(1)} %get-tuple-element.87.refs_2_, ...), custom_call_target="tpu_custom_call" | custom-call | flops 200000000 | tf_op jit(solution)/shard_map/spatial_backward/pallas_call | solution.py:175
  60.0 0.9 %collective-permute-start.20 = (f32[32,128]{1,0:T(8,128)S(1)}, f32[32,128]{1,0:T(8,128)S(1)}, u32[]{:S(2)}, u32[]{:S(2)}) collective-permute-start(f32[32,128]{1,0:T(8,128)S(1)} %pad_maximum_fusion.refs_6_), channel_id=1, source_target_pairs={{0,6},{2,4},{4,2},{6,0},{1,7},{3,5},{5,3},{7,1},{8,14},{10,12},{12... | collective-permute-start | bytes 49160 | tf_op jit(solution)/shard_map/ppermute | solution.py:504
  61.5 2.6 %spatial_backward.5 = (bf16[256,1536]{1,0:T(8,128)(2,1)}, bf16[256,1536]{1,0:T(8,128)(2,1)}) custom-call(bf16[256,1536]{1,0:T(8,128)(2,1)S(1)} %get-tuple-element.85.refs_0_, bf16[256,1536]{1,0:T(8,128)(2,1)S(1)} %get-tuple-element.86.refs_1_, bf16[256,1536]{1,0:T(8,128)(2,1)S(1)} %get-tuple-element.87.refs_2_, ...), custom_call_target="tpu_custom_call", output_to_operand_aliasing={{0}: (6, {}), {1}: (7, {})} | custom-call | flops 200000000 | tf_op jit(solution)/shard_map/spatial_backward/pallas_call | solution.py:175
  64.2 2.9 %collective-permute-start.18 = (f32[32,128]{1,0:T(8,128)S(1)}, f32[32,128]{1,0:T(8,128)S(1)}, u32[]{:S(2)}, u32[]{:S(2)}) collective-permute-start(f32[32,128]{1,0:T(8,128)S(1)} %pad_maximum_fusion.refs_6_), channel_id=1, source_target_pairs={{0,2},{2,0},{4,6},{6,4},{1,3},{3,1},{5,7},{7,5},{8,10},{10,8},{12,... | collective-permute-start | bytes 49160 | tf_op jit(solution)/shard_map/ppermute | solution.py:504
  67.1 1.4 %spatial_backward.6 = (bf16[256,1536]{1,0:T(8,128)(2,1)}, bf16[256,1536]{1,0:T(8,128)(2,1)}) custom-call(bf16[256,1536]{1,0:T(8,128)(2,1)S(1)} %get-tuple-element.85.refs_0_, bf16[256,1536]{1,0:T(8,128)(2,1)S(1)} %get-tuple-element.86.refs_1_, bf16[256,1536]{1,0:T(8,128)(2,1)S(1)} %get-tuple-element.87.refs_2_, ...), custom_call_target="tpu_custom_call", output_to_operand_aliasing={{0}: (5, {}), {1}: (6, {})} | custom-call | flops 200000000 | tf_op jit(solution)/shard_map/spatial_backward/pallas_call | solution.py:175
  68.8 1.5 %spatial_backward.7 = (bf16[256,1536]{1,0:T(8,128)(2,1)}, bf16[256,1536]{1,0:T(8,128)(2,1)}, f32[2,16,1536]{2,1,0:T(8,128)}) custom-call(bf16[256,1536]{1,0:T(8,128)(2,1)S(1)} %get-tuple-element.85.refs_0_, bf16[256,1536]{1,0:T(8,128)(2,1)S(1)} %get-tuple-element.86.refs_1_, ...), custom_call_target="tpu_custom_call", output_to_operand_aliasing={{0}: (11, {}), {1}: (12, {})} | custom-call | flops 200000000 | tf_op jit(solution)/shard_map/spatial_backward/pallas_call | solution.py:175
  (41 shorter events, 5.9 us)
Async XLA Ops:
  0.6 31.1 %copy-start = (f32[2,16,1536]{2,1,0:T(8,128)S(1)}, f32[2,16,1536]{2,1,0:T(8,128)}, u32[]{:S(2)}) copy-start(f32[2,16,1536]{2,1,0:T(8,128)} %refs_10_.1) | copy-start | bytes 589828
  2.0 17.7 %collective-permute-start.3 = (bf16[2,128,384]{2,1,0:T(8,128)(2,1)S(1)}, bf16[2,128,384]{2,1,0:T(8,128)(2,1)S(1)}, u32[]{:S(2)}, u32[]{:S(2)}) collective-permute-start(bf16[2,128,384]{2,1,0:T(8,128)(2,1)S(1)} %get-tuple-element.69), channel_id=1, source_target_pairs={{0,6},{2,4},{4,2},{6,0},{1,7},{3,5},{5,3},{7,1},{8,14},{10,12},{12... | collective-permute-start | bytes 589832 | tf_op jit(solution)/shard_map/ppermute | solution.py:504
  7.1 18.5 %collective-permute-start.4 = (bf16[2,128,384]{2,1,0:T(8,128)(2,1)S(1)}, bf16[2,128,384]{2,1,0:T(8,128)(2,1)S(1)}, u32[]{:S(2)}, u32[]{:S(2)}) collective-permute-start(bf16[2,128,384]{2,1,0:T(8,128)(2,1)S(1)} %get-tuple-element.70), channel_id=1, source_target_pairs={{0,4},{2,6},{4,0},{6,2},{1,5},{3,7},{5,1},{7,3},{8,12},{10,14},{12... | collective-permute-start | bytes 589832 | tf_op jit(solution)/shard_map/ppermute | solution.py:504
  7.1 18.5 %collective-permute-start.5 = (bf16[2,128,384]{2,1,0:T(8,128)(2,1)S(1)}, bf16[2,128,384]{2,1,0:T(8,128)(2,1)S(1)}, u32[]{:S(2)}, u32[]{:S(2)}) collective-permute-start(bf16[2,128,384]{2,1,0:T(8,128)(2,1)S(1)} %get-tuple-element.71), channel_id=1, source_target_pairs={{0,2},{2,0},{4,6},{6,4},{1,3},{3,1},{5,7},{7,5},{8,10},{10,8},{12,... | collective-permute-start | bytes 589832 | tf_op jit(solution)/shard_map/ppermute | solution.py:504
  15.3 20.6 %collective-permute-start = (bf16[3,128,256]{2,1,0:T(8,128)(2,1)}, bf16[3,128,256]{2,1,0:T(8,128)(2,1)S(1)}, u32[]{:S(2)}, u32[]{:S(2)}) collective-permute-start(bf16[3,128,256]{2,1,0:T(8,128)(2,1)} %get-tuple-element.66), channel_id=1, source_target_pairs={{0,2},{2,0},{4,6},{6,4},{1,3},{3,1},{5,7},{7,5},{8,10},{10,8},{12,... | collective-permute-start | bytes 589832 | tf_op jit(solution)/shard_map/ppermute | solution.py:504
  16.7 17.3 %collective-permute-start.1 = (bf16[2,128,256]{2,1,0:T(8,128)(2,1)}, bf16[2,128,256]{2,1,0:T(8,128)(2,1)}, u32[]{:S(2)}, u32[]{:S(2)}) collective-permute-start(bf16[2,128,256]{2,1,0:T(8,128)(2,1)} %get-tuple-element.67), channel_id=1, source_target_pairs={{0,4},{2,6},{4,0},{6,2},{1,5},{3,7},{5,1},{7,3},{8,12},{10,14},{12... | collective-permute-start | bytes 393224 | tf_op jit(solution)/shard_map/ppermute | solution.py:504
  19.6 14.4 %collective-permute-start.2 = (bf16[2,128,256]{2,1,0:T(8,128)(2,1)}, bf16[2,128,256]{2,1,0:T(8,128)(2,1)}, u32[]{:S(2)}, u32[]{:S(2)}) collective-permute-start(bf16[2,128,256]{2,1,0:T(8,128)(2,1)} %get-tuple-element.68), channel_id=1, source_target_pairs={{0,6},{2,4},{4,2},{6,0},{1,7},{3,5},{5,3},{7,1},{8,14},{10,12},{12... | collective-permute-start | bytes 393224 | tf_op jit(solution)/shard_map/ppermute | solution.py:504
  26.9 0.8 %copy-start.1 = (bf16[6,3,128,128]{3,2,1,0:T(8,128)(2,1)}, bf16[6,3,128,128]{3,2,1,0:T(8,128)(2,1)S(1)}, u32[]{:S(2)}) copy-start(bf16[6,3,128,128]{3,2,1,0:T(8,128)(2,1)S(1)} %get-tuple-element.84.refs_6_.refs_8_) | copy-start | bytes 1769476
  27.7 0.7 copy-start.2
  28.3 9.2 %collective-permute-start.6 = (bf16[4,1,128,128]{3,2,1,0:T(8,128)(2,1)}, bf16[4,1,128,128]{3,2,1,0:T(8,128)(2,1)}, u32[]{:S(2)}, u32[]{:S(2)}) collective-permute-start(bf16[4,1,128,128]{3,2,1,0:T(8,128)(2,1)} %get-tuple-element.79), channel_id=1, source_target_pairs={{0,1},{1,0},{2,3},{3,2},{4,5},{5,4},{6,7},{7,6},{8,9},{9,8},{10,11... | collective-permute-start | bytes 393224 | tf_op jit(solution)/shard_map/ppermute | solution.py:504
  30.1 7.4 %collective-permute-start.7 = (bf16[4,1,128,128]{3,2,1,0:T(8,128)(2,1)}, bf16[4,1,128,128]{3,2,1,0:T(8,128)(2,1)}, u32[]{:S(2)}, u32[]{:S(2)}) collective-permute-start(bf16[4,1,128,128]{3,2,1,0:T(8,128)(2,1)} %get-tuple-element.80), channel_id=1, source_target_pairs={{0,1},{1,0},{2,3},{3,2},{4,5},{5,4},{6,7},{7,6},{8,9},{9,8},{10,11... | collective-permute-start | bytes 393224 | tf_op jit(solution)/shard_map/ppermute | solution.py:504
  34.0 14.9 %collective-permute-start.8 = (bf16[1,128,256]{2,1,0:T(8,128)(2,1)}, bf16[1,128,256]{2,1,0:T(8,128)(2,1)}, u32[]{:S(2)}, u32[]{:S(2)}) collective-permute-start(bf16[1,128,256]{2,1,0:T(8,128)(2,1)} %copy-done.4), channel_id=1, source_target_pairs={{0,4},{2,6},{4,0},{6,2},{1,5},{3,7},{5,1},{7,3},{8,12},{10,14},{12... | collective-permute-start | bytes 196616 | tf_op jit(solution)/shard_map/ppermute | solution.py:504
  34.0 14.9 %collective-permute-start.9 = (bf16[1,128,256]{2,1,0:T(8,128)(2,1)}, bf16[1,128,256]{2,1,0:T(8,128)(2,1)}, u32[]{:S(2)}, u32[]{:S(2)}) collective-permute-start(bf16[1,128,256]{2,1,0:T(8,128)(2,1)} %copy-done.3), channel_id=1, source_target_pairs={{0,6},{2,4},{4,2},{6,0},{1,7},{3,5},{5,3},{7,1},{8,14},{10,12},{12... | collective-permute-start | bytes 196616 | tf_op jit(solution)/shard_map/ppermute | solution.py:504
  36.0 12.9 %collective-permute-start.10 = (bf16[4,1,128,128]{3,2,1,0:T(8,128)(2,1)}, bf16[4,1,128,128]{3,2,1,0:T(8,128)(2,1)}, u32[]{:S(2)}, u32[]{:S(2)}) collective-permute-start(bf16[4,1,128,128]{3,2,1,0:T(8,128)(2,1)} %copy-done.2), channel_id=1, source_target_pairs={{0,1},{1,0},{2,3},{3,2},{4,5},{5,4},{6,7},{7,6},{8,9},{9,8},{10,11... | collective-permute-start | bytes 393224 | tf_op jit(solution)/shard_map/ppermute | solution.py:504
  42.2 14.1 %collective-permute-start.13 = (bf16[2,128,256]{2,1,0:T(8,128)(2,1)}, bf16[2,128,256]{2,1,0:T(8,128)(2,1)}, u32[]{:S(2)}, u32[]{:S(2)}) collective-permute-start(bf16[2,128,256]{2,1,0:T(8,128)(2,1)} %get-tuple-element.98), channel_id=1, source_target_pairs={{0,4},{2,6},{4,0},{6,2},{1,5},{3,7},{5,1},{7,3},{8,12},{10,14},{12... | collective-permute-start | bytes 393224 | tf_op jit(solution)/shard_map/ppermute | solution.py:504
  46.0 10.3 %collective-permute-start.14 = (bf16[2,128,256]{2,1,0:T(8,128)(2,1)}, bf16[2,128,256]{2,1,0:T(8,128)(2,1)}, u32[]{:S(2)}, u32[]{:S(2)}) collective-permute-start(bf16[2,128,256]{2,1,0:T(8,128)(2,1)} %get-tuple-element.99), channel_id=1, source_target_pairs={{0,6},{2,4},{4,2},{6,0},{1,7},{3,5},{5,3},{7,1},{8,14},{10,12},{12... | collective-permute-start | bytes 393224 | tf_op jit(solution)/shard_map/ppermute | solution.py:504
  51.7 1.2 %collective-permute-start.15 = (f32[8,128]{1,0:T(8,128)S(1)}, f32[8,128]{1,0:T(8,128)S(1)}, u32[]{:S(2)}, u32[]{:S(2)}) collective-permute-start(f32[8,128]{1,0:T(8,128)S(1)} %get-tuple-element.96), channel_id=1, source_target_pairs={{0,8},{8,0},{16,24},{24,16},{1,9},{9,1},{17,25},{25,17},{2,10},{10... | collective-permute-start | bytes 12296 | tf_op jit(solution)/shard_map/ppermute | solution.py:504
  51.8 16.7 %collective-permute-start.11 = (bf16[1,128,256]{2,1,0:T(8,128)(2,1)S(1)}, bf16[1,128,256]{2,1,0:T(8,128)(2,1)S(1)}, u32[]{:S(2)}, u32[]{:S(2)}) collective-permute-start(bf16[1,128,256]{2,1,0:T(8,128)(2,1)S(1)} %get-tuple-element.94), channel_id=1, source_target_pairs={{0,6},{2,4},{4,2},{6,0},{1,7},{3,5},{5,3},{7,1},{8,14},{10,12},{12... | collective-permute-start | bytes 196616 | tf_op jit(solution)/shard_map/ppermute | solution.py:504
  52.8 15.7 %collective-permute-start.12 = (bf16[1,128,256]{2,1,0:T(8,128)(2,1)S(1)}, bf16[1,128,256]{2,1,0:T(8,128)(2,1)S(1)}, u32[]{:S(2)}, u32[]{:S(2)}) collective-permute-start(bf16[1,128,256]{2,1,0:T(8,128)(2,1)S(1)} %get-tuple-element.95), channel_id=1, source_target_pairs={{0,4},{2,6},{4,0},{6,2},{1,5},{3,7},{5,1},{7,3},{8,12},{10,14},{12... | collective-permute-start | bytes 196616 | tf_op jit(solution)/shard_map/ppermute | solution.py:504
  52.9 11.2 %collective-permute-start.17 = (bf16[3,128,256]{2,1,0:T(8,128)(2,1)S(1)}, bf16[3,128,256]{2,1,0:T(8,128)(2,1)S(1)}, u32[]{:S(2)}, u32[]{:S(2)}) collective-permute-start(bf16[3,128,256]{2,1,0:T(8,128)(2,1)S(1)} %get-tuple-element.105), channel_id=1, source_target_pairs={{0,2},{2,0},{4,6},{6,4},{1,3},{3,1},{5,7},{7,5},{8,10},{10,8},{12,... | collective-permute-start | bytes 589832 | tf_op jit(solution)/shard_map/ppermute | solution.py:504
  56.3 3.7 %collective-permute-start.16 = (f32[16,128]{1,0:T(8,128)S(1)}, f32[16,128]{1,0:T(8,128)S(1)}, u32[]{:S(2)}, u32[]{:S(2)}) collective-permute-start(f32[16,128]{1,0:T(8,128)S(1)} %pad_maximum_fusion.1), channel_id=1, source_target_pairs={{0,16},{8,24},{16,0},{24,8},{1,17},{9,25},{17,1},{25,9},{2,18},{10... | collective-permute-start | bytes 24584 | tf_op jit(solution)/shard_map/ppermute | solution.py:504
  60.0 8.5 %collective-permute-start.20 = (f32[32,128]{1,0:T(8,128)S(1)}, f32[32,128]{1,0:T(8,128)S(1)}, u32[]{:S(2)}, u32[]{:S(2)}) collective-permute-start(f32[32,128]{1,0:T(8,128)S(1)} %pad_maximum_fusion.refs_6_), channel_id=1, source_target_pairs={{0,6},{2,4},{4,2},{6,0},{1,7},{3,5},{5,3},{7,1},{8,14},{10,12},{12... | collective-permute-start | bytes 49160 | tf_op jit(solution)/shard_map/ppermute | solution.py:504
  60.9 7.6 %collective-permute-start.19 = (f32[32,128]{1,0:T(8,128)S(1)}, f32[32,128]{1,0:T(8,128)S(1)}, u32[]{:S(2)}, u32[]{:S(2)}) collective-permute-start(f32[32,128]{1,0:T(8,128)S(1)} %pad_maximum_fusion.refs_6_), channel_id=1, source_target_pairs={{0,4},{2,6},{4,0},{6,2},{1,5},{3,7},{5,1},{7,3},{8,12},{10,14},{12... | collective-permute-start | bytes 49160 | tf_op jit(solution)/shard_map/ppermute | solution.py:504
  64.2 4.6 %collective-permute-start.18 = (f32[32,128]{1,0:T(8,128)S(1)}, f32[32,128]{1,0:T(8,128)S(1)}, u32[]{:S(2)}, u32[]{:S(2)}) collective-permute-start(f32[32,128]{1,0:T(8,128)S(1)} %pad_maximum_fusion.refs_6_), channel_id=1, source_target_pairs={{0,2},{2,0},{4,6},{6,4},{1,3},{3,1},{5,7},{7,5},{8,10},{10,8},{12,... | collective-permute-start | bytes 49160 | tf_op jit(solution)/shard_map/ppermute | solution.py:504
  (2 other events, 1.2 us)

commit v14 on v12

--- a/solution.py
+++ b/solution.py
@@ -349,20 +349,41 @@
     return jnp.concatenate(all_mixed, axis=0)
 
 
+def fetch_kernel(source_ref, target_ref, arrived):
+    copies = [
+        pltpu.make_async_copy(source_ref.at[index], target_ref.at[index], arrived.at[index])
+        for index in range(source_ref.shape[0])
+    ]
+    for copy in copies:
+        copy.start()
+    for copy in copies:
+        copy.wait()
+
+
+def fetch(field):
+    return pl.pallas_call(
+        fetch_kernel,
+        in_specs=[pl.BlockSpec(memory_space=pltpu.HBM)],
+        out_specs=pl.BlockSpec(memory_space=pltpu.VMEM),
+        out_shape=jax.ShapeDtypeStruct(field.shape, field.dtype),
+        scratch_shapes=[pltpu.SemaphoreType.DMA((field.shape[0],))],
+        compiler_params=params(0),
+        cost_estimate=cost(1),
+        name="fetch_own",
+    )(in_hbm(field))
+
+
 def temporal_kernel(frames, spaces, length_ref, task_ref, *refs):
-    attended_refs, (gain_ref, *other_refs), refs = (
+    attended_refs, (gain_ref, own_ref, *other_refs), refs = (
         refs[: frames - 1],
-        refs[frames - 1 : frames - 2 + 2 * spaces],
-        refs[frames - 2 + 2 * spaces :],
-    )
-    (own_hbm, *field_refs), grad_refs, refs = refs[:4], refs[4 : frames + 4], refs[frames + 4 :]
-    mixed_ref, *kept_refs, attended, grads, wide, own_ref, arrived = refs
+        refs[frames - 1 : frames - 1 + 2 * spaces],
+        refs[frames - 1 + 2 * spaces :],
+    )
+    field_refs, grad_refs, refs = refs[:3], refs[3 : frames + 3], refs[frames + 3 :]
+    mixed_ref, *kept_refs, attended, grads, wide, arrived = refs
     heads, lanes = own_ref.shape[1], own_ref.shape[3]
     copies = [
-        pltpu.make_async_copy(own_hbm.at[:, head], own_ref.at[:, head], arrived.at[head])
-        for head in range(heads)
-    ] + [
-        pltpu.make_async_copy(source, target, arrived.at[heads + index])
+        pltpu.make_async_copy(source, target, arrived.at[index])
         for index, (source, target) in enumerate(zip(field_refs, kept_refs))
     ]
     for copy in copies:
@@ -380,7 +401,6 @@
         for space in range(spaces)
     ]
     for head in range(heads):
-        copies[head].wait()
         for space, here in enumerate(places):
             attended[head, space, partner("tm", 0)] = own_ref[frames + space, head]
             for distance, ref in enumerate(attended_refs):
@@ -404,7 +424,7 @@
             frame = partner("tm", distance)
             for space, here in enumerate(places):
                 ref[head, :, here] = grads[head, space, frame]
-    for copy in copies[heads:]:
+    for copy in copies:
         copy.wait()
 
 
@@ -413,8 +433,8 @@
     frames, spaces = len(attended) + 1, (len(upstream) + 1) // 2
     patches = spaces * lanes
     rows = -(-(heads + 1) // 8) * 8
-    operands = [*attended, gain, *upstream[1:]]
-    in_place = [in_hbm(field) for field in (upstream[0], *fields)]
+    operands = [*attended, gain, *upstream]
+    in_place = [in_hbm(field) for field in fields]
     block = (heads, spaces, frames, feat, lanes)
     results = pl.pallas_call(
         functools.partial(temporal_kernel, frames, spaces),
@@ -426,8 +446,7 @@
             pltpu.VMEM(block, jnp.bfloat16),
             pltpu.VMEM(block, jnp.bfloat16),
             pltpu.VMEM((2, spaces, 3, frames, feat, lanes), jnp.float32),
-            pltpu.VMEM(upstream[0].shape, upstream[0].dtype),
-            pltpu.SemaphoreType.DMA((heads + len(fields),)),
+            pltpu.SemaphoreType.DMA((len(fields),)),
         ],
         out_shape=[jax.ShapeDtypeStruct((heads, feat, patches), jnp.bfloat16)] * frames
         + [jax.ShapeDtypeStruct((rows, feat), jnp.float32)]
@@ -492,6 +511,8 @@
     gain = jnp.broadcast_to(
         product.reshape(own, HEAD_DIM, 1), (own, HEAD_DIM, patches // spaces)
     )
+    attended[1], upstream[0] = lax.optimization_barrier((attended[1], upstream[0]))
+    upstream[0] = fetch(upstream[0])
     grads, mixed, kept = temporal(
         lengths, task_ids, attended[1:], upstream, gain, fields
     )

time: 68 us -> 66.9 us (0.984)
  waiting for transfers between devices: 20.8 us -> 19.6 us
    pallas_call x1, Pallas kernels: 4.85 us -> 3.66 us  [temporal(): pl.pallas_call(functools.partial(temporal_kernel, frames, spaces), in_spe...]
    ppermute x16, waiting for transfers between devices: 20.8 us -> 19.6 us  [swap(): return lax.ppermute(field, axis, [(i, i ^ distance) for i in range(size)])]
    pallas_call x0 -> x1, Pallas kernels: none -> 1.18 us  [fetch(): pl.pallas_call(fetch_kernel, in_specs=[pl.BlockSpec(memory_space=pltpu.HB...]
  transfers between devices with their start and end apart: 16 -> 16, of which waited for: 5 -> 5; matrix products, arithmetic and copies ran while one was open for 0% -> 0% of each run, Pallas kernels for 16% -> 18%
where the time goes in v14:
time: 66.9 us; the launch traced here: 66.6 us
  starting transfers between devices  25.1 us (38%)
  waiting for transfers between devices  19.6 us (29%)
  Pallas kernels  18.8 us (28%)
  between operations  2.07 us (3%)
  local copies, waits for them, and re-layouts  0.92 us (1%)
    ppermute x16, starting transfers between devices, swap(): return lax.ppermute(field, axis, [(i, i ^ distance) for i in range(size)])  25.1 us
    ppermute x16, waiting for transfers between devices, swap(): return lax.ppermute(field, axis, [(i, i ^ distance) for i in range(size)])  19.6 us
    pallas_call x1, Pallas kernels, forward(): pl.pallas_call(functools.partial(forward_kernel, axis), in_specs=[pl.Bloc...  6.52 us
    pallas_call x3, Pallas kernels, backward(): pl.pallas_call(functools.partial(backward_kernel, axis, distances, gains_...  4.82 us
    pallas_call x1, Pallas kernels, temporal(): pl.pallas_call(functools.partial(temporal_kernel, frames, spaces), in_spe...  3.66 us
  transfers between devices with their start and end apart: 16, of which 5 were waited for; matrix products, arithmetic and copies ran while one was open for 0% of the time, Pallas kernels for 18%

profile of v14, /device:TPU:0, one launch (start us, length us, event | category | flops | bytes accessed | tf_op | source)
XLA Modules:
  0.0 66.6 jit_solution(18441593963689056151)
XLA Ops:
  0.6 1.3 %pack_cotangent.1 = (bf16[2,128,384]{2,1,0:T(8,128)(2,1)S(1)}, bf16[2,128,384]{2,1,0:T(8,128)(2,1)S(1)}, bf16[2,128,384]{2,1,0:T(8,128)(2,1)S(1)}, bf16[2,128,384]{2,1,0:T(8,128)(2,1)S(1)}) custom-call(bf16[128,3072]{1,0:T(8,128)(2,1)} %bitcast.19), custom_call_target="tpu_custom_call" | custom-call | flops 100000000 | tf_op jit(solution)/shard_map/pack_cotangent/pallas_call | solution.py:198
  2.0 5.1 %collective-permute-start.1 = (bf16[2,128,384]{2,1,0:T(8,128)(2,1)S(1)}, bf16[2,128,384]{2,1,0:T(8,128)(2,1)S(1)}, u32[]{:S(2)}, u32[]{:S(2)}) collective-permute-start(bf16[2,128,384]{2,1,0:T(8,128)(2,1)S(1)} %get-tuple-element.54), channel_id=1, source_target_pairs={{0,6},{2,4},{4,2},{6,0},{1,7},{3,5},{5,3},{7,1},{8,14},{10,12},{12... | collective-permute-start | bytes 589832 | tf_op jit(solution)/shard_map/ppermute | solution.py:482
  7.7 6.5 %spatial_forward.1 = (f32[12,256,256]{2,1,0:T(8,128)S(1)}, bf16[3,128,256]{2,1,0:T(8,128)(2,1)S(1)}, bf16[3,128,256]{2,1,0:T(8,128)(2,1)}, bf16[3,128,256]{2,1,0:T(8,128)(2,1)}, bf16[3,128,256]{2,1,0:T(8,128)(2,1)}) custom-call(bf16[256,1536]{1,0:T(8,128)(2,1)} %bitcast.13, bf16[256,1536]{1,0:T(8,128)(2,1)} %bitcast.15, bf16[256,1536]{1,0:T(8,128)(2,1)} %bitcast.17), custom_call_target="tpu_custom_call" | custom-call | flops 600000000 | tf_op jit(solution)/shard_map/spatial_forward/pallas_call | solution.py:76
  14.3 1.4 %collective-permute-start = (bf16[3,128,256]{2,1,0:T(8,128)(2,1)}, bf16[3,128,256]{2,1,0:T(8,128)(2,1)S(1)}, u32[]{:S(2)}, u32[]{:S(2)}) collective-permute-start(bf16[3,128,256]{2,1,0:T(8,128)(2,1)} %get-tuple-element.53), channel_id=1, source_target_pairs={{0,2},{2,0},{4,6},{6,4},{1,3},{3,1},{5,7},{7,5},{8,10},{10,8},{12,... | collective-permute-start | bytes 589832 | tf_op jit(solution)/shard_map/ppermute | solution.py:482
  15.7 2.9 %collective-permute-start.4 = (bf16[3,128,256]{2,1,0:T(8,128)(2,1)}, bf16[3,128,256]{2,1,0:T(8,128)(2,1)}, u32[]{:S(2)}, u32[]{:S(2)}) collective-permute-start(bf16[3,128,256]{2,1,0:T(8,128)(2,1)} %get-tuple-element.66), channel_id=1, source_target_pairs={{0,4},{2,6},{4,0},{6,2},{1,5},{3,7},{5,1},{7,3},{8,12},{10,14},{12... | collective-permute-start | bytes 589832 | tf_op jit(solution)/shard_map/ppermute | solution.py:482
  18.7 6.9 %collective-permute-done.2.refs_1_ = bf16[2,128,384]{2,1,0:T(8,128)(2,1)S(1)} collective-permute-done((bf16[2,128,384]{2,1,0:T(8,128)(2,1)S(1)}, bf16[2,128,384]{2,1,0:T(8,128)(2,1)S(1)}, u32[]{:S(2)}, u32[]{:S(2)}) %collective-permute-start.2) | collective-permute-done | bytes 196640 | tf_op jit(solution)/shard_map/ppermute | solution.py:482
  25.6 1.3 %turn_cotangent.1 = (bf16[6,3,128,128]{3,2,1,0:T(8,128)(2,1)S(1)}, bf16[2,3,128,128]{3,2,1,0:T(8,128)(2,1)}, bf16[2,3,128,128]{3,2,1,0:T(8,128)(2,1)}) custom-call(bf16[2,128,384]{2,1,0:T(8,128)(2,1)S(1)} %collective-permute-done.1.refs_0_, bf16[2,128,384]{2,1,0:T(8,128)(2,1)S(1)} %collective-permute-done.2.refs_1_, ...), custom_call_target="tpu_custom_call" | custom-call | flops 200000000 | tf_op jit(solution)/shard_map/turn_cotangent/pallas_call | solution.py:247
  26.9 0.8 %copy-done = bf16[6,3,128,128]{3,2,1,0:T(8,128)(2,1)} copy-done((bf16[6,3,128,128]{3,2,1,0:T(8,128)(2,1)}, bf16[6,3,128,128]{3,2,1,0:T(8,128)(2,1)S(1)}, u32[]{:S(2)}) %copy-start) | copy-done | bytes 589848
  27.7 1.7 %collective-permute-start.6 = (bf16[2,3,128,128]{3,2,1,0:T(8,128)(2,1)}, bf16[2,3,128,128]{3,2,1,0:T(8,128)(2,1)}, u32[]{:S(2)}, u32[]{:S(2)}) collective-permute-start(bf16[2,3,128,128]{3,2,1,0:T(8,128)(2,1)} %get-tuple-element.69), channel_id=1, source_target_pairs={{0,1},{1,0},{2,3},{3,2},{4,5},{5,4},{6,7},{7,6},{8,9},{9,8},{10,11... | collective-permute-start | bytes 589832 | tf_op jit(solution)/shard_map/ppermute | solution.py:482
  31.2 1.2 %fetch_own.1.refs_4_ = bf16[6,3,128,128]{3,2,1,0:T(8,128)(2,1)S(1)} custom-call(bf16[6,3,128,128]{3,2,1,0:T(8,128)(2,1)} %copy-done), custom_call_target="tpu_custom_call" | custom-call | flops 100000000 | tf_op jit(solution)/shard_map/fetch_own/pallas_call | solution.py:364
  32.4 5.1 %collective-permute-done.4.refs_1_ = bf16[3,128,256]{2,1,0:T(8,128)(2,1)} collective-permute-done((bf16[3,128,256]{2,1,0:T(8,128)(2,1)}, bf16[3,128,256]{2,1,0:T(8,128)(2,1)}, u32[]{:S(2)}, u32[]{:S(2)}) %collective-permute-start.4) | collective-permute-done | bytes 196640 | tf_op jit(solution)/shard_map/ppermute | solution.py:482
  37.7 3.7 %temporal.1 = (bf16[3,128,256]{2,1,0:T(8,128)(2,1)S(1)}, bf16[3,128,256]{2,1,0:T(8,128)(2,1)S(1)}, bf16[3,128,256]{2,1,0:T(8,128)(2,1)S(1)}, bf16[3,128,256]{2,1...) custom-call(s32[1]{0:T(128)S(6)} %copy.19.length_ref, ...), custom_call_target="tpu_custom_call" | custom-call | flops 400000000 | tf_op jit(solution)/shard_map/temporal/pallas_call | solution.py:439
  41.4 2.8 %collective-permute-start.8 = (bf16[3,128,256]{2,1,0:T(8,128)(2,1)S(1)}, bf16[3,128,256]{2,1,0:T(8,128)(2,1)S(1)}, u32[]{:S(2)}, u32[]{:S(2)}) collective-permute-start(bf16[3,128,256]{2,1,0:T(8,128)(2,1)S(1)} %get-tuple-element.74), channel_id=1, source_target_pairs={{0,6},{2,4},{4,2},{6,0},{1,7},{3,5},{5,3},{7,1},{8,14},{10,12},{12... | collective-permute-start | bytes 589832 | tf_op jit(solution)/shard_map/ppermute | solution.py:482
  44.2 2.6 %collective-permute-start.9 = (bf16[3,128,256]{2,1,0:T(8,128)(2,1)S(1)}, bf16[3,128,256]{2,1,0:T(8,128)(2,1)S(1)}, u32[]{:S(2)}, u32[]{:S(2)}) collective-permute-start(bf16[3,128,256]{2,1,0:T(8,128)(2,1)S(1)} %get-tuple-element.75), channel_id=1, source_target_pairs={{0,4},{2,6},{4,0},{6,2},{1,5},{3,7},{5,1},{7,3},{8,12},{10,14},{12... | collective-permute-start | bytes 589832 | tf_op jit(solution)/shard_map/ppermute | solution.py:482
  46.9 1.5 %collective-permute-start.11 = (f32[16,128]{1,0:T(8,128)S(1)}, f32[16,128]{1,0:T(8,128)S(1)}, u32[]{:S(2)}, u32[]{:S(2)}) collective-permute-start(f32[16,128]{1,0:T(8,128)S(1)} %pad_maximum_fusion.1), channel_id=1, source_target_pairs={{0,16},{8,24},{16,0},{24,8},{1,17},{9,25},{17,1},{25,9},{2,18},{10... | collective-permute-start | bytes 24584 | tf_op jit(solution)/shard_map/ppermute | solution.py:482
  48.4 1.4 %spatial_backward.3 = (bf16[256,1536]{1,0:T(8,128)(2,1)}, bf16[256,1536]{1,0:T(8,128)(2,1)}) custom-call(bf16[256,1536]{1,0:T(8,128)(2,1)S(1)} %get-tuple-element.71.refs_0_, bf16[256,1536]{1,0:T(8,128)(2,1)S(1)} %get-tuple-element.72.refs_1_, bf16[256,1536]{1,0:T(8,128)(2,1)S(1)} %get-tuple-element.73.refs_2_, ...), custom_call_target="tpu_custom_call" | custom-call | flops 200000000 | tf_op jit(solution)/shard_map/spatial_backward/pallas_call | solution.py:159
  49.8 0.7 %collective-permute-done.11 = f32[16,128]{1,0:T(8,128)S(1)} collective-permute-done((f32[16,128]{1,0:T(8,128)S(1)}, f32[16,128]{1,0:T(8,128)S(1)}, u32[]{:S(2)}, u32[]{:S(2)}) %collective-permute-start.11) | collective-permute-done | bytes 8224 | tf_op jit(solution)/shard_map/ppermute | solution.py:482
  50.5 2.4 %collective-permute-start.15 = (f32[32,128]{1,0:T(8,128)S(1)}, f32[32,128]{1,0:T(8,128)S(1)}, u32[]{:S(2)}, u32[]{:S(2)}) collective-permute-start(f32[32,128]{1,0:T(8,128)S(1)} %pad_maximum_fusion.refs_6_), channel_id=1, source_target_pairs={{0,6},{2,4},{4,2},{6,0},{1,7},{3,5},{5,3},{7,1},{8,14},{10,12},{12... | collective-permute-start | bytes 49160 | tf_op jit(solution)/shard_map/ppermute | solution.py:482
  53.0 0.9 %collective-permute-start.14 = (f32[32,128]{1,0:T(8,128)S(1)}, f32[32,128]{1,0:T(8,128)S(1)}, u32[]{:S(2)}, u32[]{:S(2)}) collective-permute-start(f32[32,128]{1,0:T(8,128)S(1)} %pad_maximum_fusion.refs_6_), channel_id=1, source_target_pairs={{0,4},{2,6},{4,0},{6,2},{1,5},{3,7},{5,1},{7,3},{8,12},{10,14},{12... | collective-permute-start | bytes 49160 | tf_op jit(solution)/shard_map/ppermute | solution.py:482
  53.9 3.9 %collective-permute-done.12.refs_4_ = bf16[3,128,256]{2,1,0:T(8,128)(2,1)S(1)} collective-permute-done((bf16[3,128,256]{2,1,0:T(8,128)(2,1)S(1)}, bf16[3,128,256]{2,1,0:T(8,128)(2,1)S(1)}, u32[]{:S(2)}, u32[]{:S(2)}) %collective-permute-start.12) | collective-permute-done | bytes 196640 | tf_op jit(solution)/shard_map/ppermute | solution.py:482
  57.7 2.5 %collective-permute-start.13 = (f32[32,128]{1,0:T(8,128)S(1)}, f32[32,128]{1,0:T(8,128)S(1)}, u32[]{:S(2)}, u32[]{:S(2)}) collective-permute-start(f32[32,128]{1,0:T(8,128)S(1)} %pad_maximum_fusion.refs_6_), channel_id=1, source_target_pairs={{0,2},{2,0},{4,6},{6,4},{1,3},{3,1},{5,7},{7,5},{8,10},{10,8},{12,... | collective-permute-start | bytes 49160 | tf_op jit(solution)/shard_map/ppermute | solution.py:482
  60.2 1.4 %spatial_backward.4 = (bf16[256,1536]{1,0:T(8,128)(2,1)}, bf16[256,1536]{1,0:T(8,128)(2,1)}) custom-call(bf16[256,1536]{1,0:T(8,128)(2,1)S(1)} %get-tuple-element.71.refs_0_, bf16[256,1536]{1,0:T(8,128)(2,1)S(1)} %get-tuple-element.72.refs_1_, bf16[256,1536]{1,0:T(8,128)(2,1)S(1)} %get-tuple-element.73.refs_2_, ...), custom_call_target="tpu_custom_call", output_to_operand_aliasing={{0}: (5, {}), {1}: (6, {})} | custom-call | flops 200000000 | tf_op jit(solution)/shard_map/spatial_backward/pallas_call | solution.py:159
  61.6 3.0 %collective-permute-done.14.refs_8_ = f32[32,128]{1,0:T(8,128)S(1)} collective-permute-done((f32[32,128]{1,0:T(8,128)S(1)}, f32[32,128]{1,0:T(8,128)S(1)}, u32[]{:S(2)}, u32[]{:S(2)}) %collective-permute-start.14) | collective-permute-done | bytes 16416 | tf_op jit(solution)/shard_map/ppermute | solution.py:482
  64.6 2.0 %spatial_backward.5 = (bf16[256,1536]{1,0:T(8,128)(2,1)}, bf16[256,1536]{1,0:T(8,128)(2,1)}, f32[2,16,1536]{2,1,0:T(8,128)}) custom-call(bf16[256,1536]{1,0:T(8,128)(2,1)S(1)} %get-tuple-element.71.refs_0_, bf16[256,1536]{1,0:T(8,128)(2,1)S(1)} %get-tuple-element.72.refs_1_, ...), custom_call_target="tpu_custom_call", output_to_operand_aliasing={{0}: (11, {}), {1}: (12, {})} | custom-call | flops 200000000 | tf_op jit(solution)/shard_map/spatial_backward/pallas_call | solution.py:159
  (24 shorter events, 1.5 us)
Async XLA Ops:
  0.6 30.4 %copy-start.1 = (f32[2,16,1536]{2,1,0:T(8,128)S(1)}, f32[2,16,1536]{2,1,0:T(8,128)}, u32[]{:S(2)}) copy-start(f32[2,16,1536]{2,1,0:T(8,128)} %refs_10_.1) | copy-start | bytes 589828
  2.0 16.7 %collective-permute-start.1 = (bf16[2,128,384]{2,1,0:T(8,128)(2,1)S(1)}, bf16[2,128,384]{2,1,0:T(8,128)(2,1)S(1)}, u32[]{:S(2)}, u32[]{:S(2)}) collective-permute-start(bf16[2,128,384]{2,1,0:T(8,128)(2,1)S(1)} %get-tuple-element.54), channel_id=1, source_target_pairs={{0,6},{2,4},{4,2},{6,0},{1,7},{3,5},{5,3},{7,1},{8,14},{10,12},{12... | collective-permute-start | bytes 589832 | tf_op jit(solution)/shard_map/ppermute | solution.py:482
  7.1 18.5 %collective-permute-start.2 = (bf16[2,128,384]{2,1,0:T(8,128)(2,1)S(1)}, bf16[2,128,384]{2,1,0:T(8,128)(2,1)S(1)}, u32[]{:S(2)}, u32[]{:S(2)}) collective-permute-start(bf16[2,128,384]{2,1,0:T(8,128)(2,1)S(1)} %get-tuple-element.55), channel_id=1, source_target_pairs={{0,4},{2,6},{4,0},{6,2},{1,5},{3,7},{5,1},{7,3},{8,12},{10,14},{12... | collective-permute-start | bytes 589832 | tf_op jit(solution)/shard_map/ppermute | solution.py:482
  7.1 18.5 %collective-permute-start.3 = (bf16[2,128,384]{2,1,0:T(8,128)(2,1)S(1)}, bf16[2,128,384]{2,1,0:T(8,128)(2,1)S(1)}, u32[]{:S(2)}, u32[]{:S(2)}) collective-permute-start(bf16[2,128,384]{2,1,0:T(8,128)(2,1)S(1)} %get-tuple-element.56), channel_id=1, source_target_pairs={{0,2},{2,0},{4,6},{6,4},{1,3},{3,1},{5,7},{7,5},{8,10},{10,8},{12,... | collective-permute-start | bytes 589832 | tf_op jit(solution)/shard_map/ppermute | solution.py:482
  14.3 16.9 %collective-permute-start = (bf16[3,128,256]{2,1,0:T(8,128)(2,1)}, bf16[3,128,256]{2,1,0:T(8,128)(2,1)S(1)}, u32[]{:S(2)}, u32[]{:S(2)}) collective-permute-start(bf16[3,128,256]{2,1,0:T(8,128)(2,1)} %get-tuple-element.53), channel_id=1, source_target_pairs={{0,2},{2,0},{4,6},{6,4},{1,3},{3,1},{5,7},{7,5},{8,10},{10,8},{12,... | collective-permute-start | bytes 589832 | tf_op jit(solution)/shard_map/ppermute | solution.py:482
  15.7 21.8 %collective-permute-start.4 = (bf16[3,128,256]{2,1,0:T(8,128)(2,1)}, bf16[3,128,256]{2,1,0:T(8,128)(2,1)}, u32[]{:S(2)}, u32[]{:S(2)}) collective-permute-start(bf16[3,128,256]{2,1,0:T(8,128)(2,1)} %get-tuple-element.66), channel_id=1, source_target_pairs={{0,4},{2,6},{4,0},{6,2},{1,5},{3,7},{5,1},{7,3},{8,12},{10,14},{12... | collective-permute-start | bytes 589832 | tf_op jit(solution)/shard_map/ppermute | solution.py:482
  18.6 18.9 %collective-permute-start.5 = (bf16[3,128,256]{2,1,0:T(8,128)(2,1)}, bf16[3,128,256]{2,1,0:T(8,128)(2,1)}, u32[]{:S(2)}, u32[]{:S(2)}) collective-permute-start(bf16[3,128,256]{2,1,0:T(8,128)(2,1)} %get-tuple-element.67), channel_id=1, source_target_pairs={{0,6},{2,4},{4,2},{6,0},{1,7},{3,5},{5,3},{7,1},{8,14},{10,12},{12... | collective-permute-start | bytes 589832 | tf_op jit(solution)/shard_map/ppermute | solution.py:482
  26.9 0.8 %copy-start = (bf16[6,3,128,128]{3,2,1,0:T(8,128)(2,1)}, bf16[6,3,128,128]{3,2,1,0:T(8,128)(2,1)S(1)}, u32[]{:S(2)}) copy-start(bf16[6,3,128,128]{3,2,1,0:T(8,128)(2,1)S(1)} %get-tuple-element.68.source_ref) | copy-start | bytes 1769476
  27.7 9.8 %collective-permute-start.6 = (bf16[2,3,128,128]{3,2,1,0:T(8,128)(2,1)}, bf16[2,3,128,128]{3,2,1,0:T(8,128)(2,1)}, u32[]{:S(2)}, u32[]{:S(2)}) collective-permute-start(bf16[2,3,128,128]{3,2,1,0:T(8,128)(2,1)} %get-tuple-element.69), channel_id=1, source_target_pairs={{0,1},{1,0},{2,3},{3,2},{4,5},{5,4},{6,7},{7,6},{8,9},{9,8},{10,11... | collective-permute-start | bytes 589832 | tf_op jit(solution)/shard_map/ppermute | solution.py:482
  29.5 8.1 %collective-permute-start.7 = (bf16[2,3,128,128]{3,2,1,0:T(8,128)(2,1)}, bf16[2,3,128,128]{3,2,1,0:T(8,128)(2,1)}, u32[]{:S(2)}, u32[]{:S(2)}) collective-permute-start(bf16[2,3,128,128]{3,2,1,0:T(8,128)(2,1)} %get-tuple-element.70), channel_id=1, source_target_pairs={{0,1},{1,0},{2,3},{3,2},{4,5},{5,4},{6,7},{7,6},{8,9},{9,8},{10,11... | collective-permute-start | bytes 589832 | tf_op jit(solution)/shard_map/ppermute | solution.py:482
  41.3 5.6 %collective-permute-start.10 = (f32[8,128]{1,0:T(8,128)S(1)}, f32[8,128]{1,0:T(8,128)S(1)}, u32[]{:S(2)}, u32[]{:S(2)}) collective-permute-start(f32[8,128]{1,0:T(8,128)S(1)} %get-tuple-element.76), channel_id=1, source_target_pairs={{0,8},{8,0},{16,24},{24,16},{1,9},{9,1},{17,25},{25,17},{2,10},{10... | collective-permute-start | bytes 12296 | tf_op jit(solution)/shard_map/ppermute | solution.py:482
  41.4 23.2 %collective-permute-start.8 = (bf16[3,128,256]{2,1,0:T(8,128)(2,1)S(1)}, bf16[3,128,256]{2,1,0:T(8,128)(2,1)S(1)}, u32[]{:S(2)}, u32[]{:S(2)}) collective-permute-start(bf16[3,128,256]{2,1,0:T(8,128)(2,1)S(1)} %get-tuple-element.74), channel_id=1, source_target_pairs={{0,6},{2,4},{4,2},{6,0},{1,7},{3,5},{5,3},{7,1},{8,14},{10,12},{12... | collective-permute-start | bytes 589832 | tf_op jit(solution)/shard_map/ppermute | solution.py:482
  44.2 20.5 %collective-permute-start.9 = (bf16[3,128,256]{2,1,0:T(8,128)(2,1)S(1)}, bf16[3,128,256]{2,1,0:T(8,128)(2,1)S(1)}, u32[]{:S(2)}, u32[]{:S(2)}) collective-permute-start(bf16[3,128,256]{2,1,0:T(8,128)(2,1)S(1)} %get-tuple-element.75), channel_id=1, source_target_pairs={{0,4},{2,6},{4,0},{6,2},{1,5},{3,7},{5,1},{7,3},{8,12},{10,14},{12... | collective-permute-start | bytes 589832 | tf_op jit(solution)/shard_map/ppermute | solution.py:482
  46.7 11.0 %collective-permute-start.12 = (bf16[3,128,256]{2,1,0:T(8,128)(2,1)S(1)}, bf16[3,128,256]{2,1,0:T(8,128)(2,1)S(1)}, u32[]{:S(2)}, u32[]{:S(2)}) collective-permute-start(bf16[3,128,256]{2,1,0:T(8,128)(2,1)S(1)} %get-tuple-element.83), channel_id=1, source_target_pairs={{0,2},{2,0},{4,6},{6,4},{1,3},{3,1},{5,7},{7,5},{8,10},{10,8},{12,... | collective-permute-start | bytes 589832 | tf_op jit(solution)/shard_map/ppermute | solution.py:482
  46.9 3.7 %collective-permute-start.11 = (f32[16,128]{1,0:T(8,128)S(1)}, f32[16,128]{1,0:T(8,128)S(1)}, u32[]{:S(2)}, u32[]{:S(2)}) collective-permute-start(f32[16,128]{1,0:T(8,128)S(1)} %pad_maximum_fusion.1), channel_id=1, source_target_pairs={{0,16},{8,24},{16,0},{24,8},{1,17},{9,25},{17,1},{25,9},{2,18},{10... | collective-permute-start | bytes 24584 | tf_op jit(solution)/shard_map/ppermute | solution.py:482
  50.5 11.1 %collective-permute-start.15 = (f32[32,128]{1,0:T(8,128)S(1)}, f32[32,128]{1,0:T(8,128)S(1)}, u32[]{:S(2)}, u32[]{:S(2)}) collective-permute-start(f32[32,128]{1,0:T(8,128)S(1)} %pad_maximum_fusion.refs_6_), channel_id=1, source_target_pairs={{0,6},{2,4},{4,2},{6,0},{1,7},{3,5},{5,3},{7,1},{8,14},{10,12},{12... | collective-permute-start | bytes 49160 | tf_op jit(solution)/shard_map/ppermute | solution.py:482
  53.0 11.6 %collective-permute-start.14 = (f32[32,128]{1,0:T(8,128)S(1)}, f32[32,128]{1,0:T(8,128)S(1)}, u32[]{:S(2)}, u32[]{:S(2)}) collective-permute-start(f32[32,128]{1,0:T(8,128)S(1)} %pad_maximum_fusion.refs_6_), channel_id=1, source_target_pairs={{0,4},{2,6},{4,0},{6,2},{1,5},{3,7},{5,1},{7,3},{8,12},{10,14},{12... | collective-permute-start | bytes 49160 | tf_op jit(solution)/shard_map/ppermute | solution.py:482
  57.7 6.9 %collective-permute-start.13 = (f32[32,128]{1,0:T(8,128)S(1)}, f32[32,128]{1,0:T(8,128)S(1)}, u32[]{:S(2)}, u32[]{:S(2)}) collective-permute-start(f32[32,128]{1,0:T(8,128)S(1)} %pad_maximum_fusion.refs_6_), channel_id=1, source_target_pairs={{0,2},{2,0},{4,6},{6,4},{1,3},{3,1},{5,7},{7,5},{8,10},{10,8},{12,... | collective-permute-start | bytes 49160 | tf_op jit(solution)/shard_map/ppermute | solution.py:482

commit v15 on v14

--- a/solution.py
+++ b/solution.py
@@ -349,10 +349,12 @@
     return jnp.concatenate(all_mixed, axis=0)
 
 
-def fetch_kernel(source_ref, target_ref, arrived):
+def fetch_kernel(*refs):
+    *refs, arrived = refs
+    number = len(refs) // 2
     copies = [
-        pltpu.make_async_copy(source_ref.at[index], target_ref.at[index], arrived.at[index])
-        for index in range(source_ref.shape[0])
+        pltpu.make_async_copy(source, target, arrived.at[index])
+        for index, (source, target) in enumerate(zip(refs[:number], refs[number:]))
     ]
     for copy in copies:
         copy.start()
@@ -360,17 +362,17 @@
         copy.wait()
 
 
-def fetch(field):
+def fetch(*fields):
     return pl.pallas_call(
         fetch_kernel,
-        in_specs=[pl.BlockSpec(memory_space=pltpu.HBM)],
-        out_specs=pl.BlockSpec(memory_space=pltpu.VMEM),
-        out_shape=jax.ShapeDtypeStruct(field.shape, field.dtype),
-        scratch_shapes=[pltpu.SemaphoreType.DMA((field.shape[0],))],
+        in_specs=[pl.BlockSpec(memory_space=pltpu.HBM)] * len(fields),
+        out_specs=[pl.BlockSpec(memory_space=pltpu.VMEM)] * len(fields),
+        out_shape=[jax.ShapeDtypeStruct(field.shape, field.dtype) for field in fields],
+        scratch_shapes=[pltpu.SemaphoreType.DMA((len(fields),))],
         compiler_params=params(0),
         cost_estimate=cost(1),
-        name="fetch_own",
-    )(in_hbm(field))
+        name="fetch",
+    )(*[in_hbm(field) for field in fields])
 
 
 def temporal_kernel(frames, spaces, length_ref, task_ref, *refs):
@@ -379,15 +381,8 @@
         refs[frames - 1 : frames - 1 + 2 * spaces],
         refs[frames - 1 + 2 * spaces :],
     )
-    field_refs, grad_refs, refs = refs[:3], refs[3 : frames + 3], refs[frames + 3 :]
-    mixed_ref, *kept_refs, attended, grads, wide, arrived = refs
+    grad_refs, (mixed_ref, attended, grads, wide) = refs[:frames], refs[frames:]
     heads, lanes = own_ref.shape[1], own_ref.shape[3]
-    copies = [
-        pltpu.make_async_copy(source, target, arrived.at[index])
-        for index, (source, target) in enumerate(zip(field_refs, kept_refs))
-    ]
-    for copy in copies:
-        copy.start()
     half = frames // 2
     mixed_ref[...] = jnp.full(mixed_ref.shape, task_ref[0].astype(jnp.float32))
 
@@ -424,38 +419,32 @@
             frame = partner("tm", distance)
             for space, here in enumerate(places):
                 ref[head, :, here] = grads[head, space, frame]
-    for copy in copies:
-        copy.wait()
-
-
-def temporal(lengths, task_ids, attended, upstream, gain, fields):
+
+
+def temporal(lengths, task_ids, attended, upstream, gain):
     _, heads, feat, lanes = upstream[0].shape
     frames, spaces = len(attended) + 1, (len(upstream) + 1) // 2
     patches = spaces * lanes
     rows = -(-(heads + 1) // 8) * 8
     operands = [*attended, gain, *upstream]
-    in_place = [in_hbm(field) for field in fields]
     block = (heads, spaces, frames, feat, lanes)
     results = pl.pallas_call(
         functools.partial(temporal_kernel, frames, spaces),
         in_specs=[pl.BlockSpec(memory_space=pltpu.SMEM)] * 2
-        + [pl.BlockSpec(memory_space=pltpu.VMEM)] * len(operands)
-        + [pl.BlockSpec(memory_space=pltpu.HBM)] * len(in_place),
-        out_specs=[pl.BlockSpec(memory_space=pltpu.VMEM)] * (frames + 1 + len(fields)),
+        + [pl.BlockSpec(memory_space=pltpu.VMEM)] * len(operands),
+        out_specs=[pl.BlockSpec(memory_space=pltpu.VMEM)] * (frames + 1),
         scratch_shapes=[
             pltpu.VMEM(block, jnp.bfloat16),
             pltpu.VMEM(block, jnp.bfloat16),
             pltpu.VMEM((2, spaces, 3, frames, feat, lanes), jnp.float32),
-            pltpu.SemaphoreType.DMA((len(fields),)),
         ],
         out_shape=[jax.ShapeDtypeStruct((heads, feat, patches), jnp.bfloat16)] * frames
-        + [jax.ShapeDtypeStruct((rows, feat), jnp.float32)]
-        + [jax.ShapeDtypeStruct(field.shape, field.dtype) for field in fields],
+        + [jax.ShapeDtypeStruct((rows, feat), jnp.float32)],
         compiler_params=params(patches),
         cost_estimate=cost(4),
         name="temporal",
-    )(lengths, task_ids, *operands, *in_place)
-    return list(results[:frames]), results[frames], results[frames + 1 :]
+    )(lengths, task_ids, *operands)
+    return list(results[:frames]), results[frames]
 
 
 def gain_gradients(axis, heads, frames, clips, mixed_refs, gains_ref, grad_ref):
@@ -511,11 +500,9 @@
     gain = jnp.broadcast_to(
         product.reshape(own, HEAD_DIM, 1), (own, HEAD_DIM, patches // spaces)
     )
-    attended[1], upstream[0] = lax.optimization_barrier((attended[1], upstream[0]))
-    upstream[0] = fetch(upstream[0])
-    grads, mixed, kept = temporal(
-        lengths, task_ids, attended[1:], upstream, gain, fields
-    )
+    attended[1], gain, upstream[0] = lax.optimization_barrier((attended[1], gain, upstream[0]))
+    upstream[0], *kept = fetch(upstream[0], *fields)
+    grads, mixed = temporal(lengths, task_ids, attended[1:], upstream, gain)
     for distance in reversed(range(1, frames)):
         grads[distance] = swap(grads[distance], "tm", frames, distance)
     here = grads[0]

time: 66.9 us -> 66.7 us (level)
  waiting for transfers between devices: 19.6 us -> 18.9 us
    ppermute x16, waiting for transfers between devices: 19.6 us -> 18.9 us  [swap(): return lax.ppermute(field, axis, [(i, i ^ distance) for i in range(size)])]
  transfers between devices with their start and end apart: 16 -> 16, of which waited for: 5 -> 5; matrix products, arithmetic and copies ran while one was open for 0% -> 0% of each run, Pallas kernels for 18% -> 19%
where the time goes in v15:
time: 66.7 us; the launch traced here: 66.5 us
  starting transfers between devices  25.1 us (38%)
  Pallas kernels  19.4 us (29%)
  waiting for transfers between devices  18.9 us (28%)
  between operations  2.07 us (3%)
  local copies, waits for them, and re-layouts  0.92 us (1%)
    ppermute x16, starting transfers between devices, swap(): return lax.ppermute(field, axis, [(i, i ^ distance) for i in range(size)])  25.1 us
    ppermute x16, waiting for transfers between devices, swap(): return lax.ppermute(field, axis, [(i, i ^ distance) for i in range(size)])  18.9 us
    pallas_call x1, Pallas kernels, forward(): pl.pallas_call(functools.partial(forward_kernel, axis), in_specs=[pl.Bloc...  6.52 us
    pallas_call x3, Pallas kernels, backward(): pl.pallas_call(functools.partial(backward_kernel, axis, distances, gains_...  4.81 us
    pallas_call x1, Pallas kernels, temporal(): pl.pallas_call(functools.partial(temporal_kernel, frames, spaces), in_spe...  3.62 us
    pallas_call x1, Pallas kernels, fetch(): pl.pallas_call(fetch_kernel, in_specs=[pl.BlockSpec(memory_space=pltpu.HB...  1.83 us
  transfers between devices with their start and end apart: 16, of which 5 were waited for; matrix products, arithmetic and copies ran while one was open for 0% of the time, Pallas kernels for 19%

profile of v15, /device:TPU:0, one launch (start us, length us, event | category | flops | bytes accessed | tf_op | source)
XLA Modules:
  0.0 66.5 jit_solution(17068322494769243017)
XLA Ops:
  0.6 1.3 %pack_cotangent.1 = (bf16[2,128,384]{2,1,0:T(8,128)(2,1)S(1)}, bf16[2,128,384]{2,1,0:T(8,128)(2,1)S(1)}, bf16[2,128,384]{2,1,0:T(8,128)(2,1)S(1)}, bf16[2,128,384]{2,1,0:T(8,128)(2,1)S(1)}) custom-call(bf16[128,3072]{1,0:T(8,128)(2,1)} %bitcast.19), custom_call_target="tpu_custom_call" | custom-call | flops 100000000 | tf_op jit(solution)/shard_map/pack_cotangent/pallas_call | solution.py:198
  2.0 5.1 %collective-permute-start.1 = (bf16[2,128,384]{2,1,0:T(8,128)(2,1)S(1)}, bf16[2,128,384]{2,1,0:T(8,128)(2,1)S(1)}, u32[]{:S(2)}, u32[]{:S(2)}) collective-permute-start(bf16[2,128,384]{2,1,0:T(8,128)(2,1)S(1)} %get-tuple-element.56), channel_id=1, source_target_pairs={{0,6},{2,4},{4,2},{6,0},{1,7},{3,5},{5,3},{7,1},{8,14},{10,12},{12... | collective-permute-start | bytes 589832 | tf_op jit(solution)/shard_map/ppermute | solution.py:471
  7.7 6.5 %spatial_forward.1 = (f32[12,256,256]{2,1,0:T(8,128)S(1)}, bf16[3,128,256]{2,1,0:T(8,128)(2,1)S(1)}, bf16[3,128,256]{2,1,0:T(8,128)(2,1)}, bf16[3,128,256]{2,1,0:T(8,128)(2,1)}, bf16[3,128,256]{2,1,0:T(8,128)(2,1)}) custom-call(bf16[256,1536]{1,0:T(8,128)(2,1)} %bitcast.13, bf16[256,1536]{1,0:T(8,128)(2,1)} %bitcast.15, bf16[256,1536]{1,0:T(8,128)(2,1)} %bitcast.17), custom_call_target="tpu_custom_call" | custom-call | flops 600000000 | tf_op jit(solution)/shard_map/spatial_forward/pallas_call | solution.py:76
  14.3 1.4 %collective-permute-start = (bf16[3,128,256]{2,1,0:T(8,128)(2,1)}, bf16[3,128,256]{2,1,0:T(8,128)(2,1)S(1)}, u32[]{:S(2)}, u32[]{:S(2)}) collective-permute-start(bf16[3,128,256]{2,1,0:T(8,128)(2,1)} %get-tuple-element.55), channel_id=1, source_target_pairs={{0,2},{2,0},{4,6},{6,4},{1,3},{3,1},{5,7},{7,5},{8,10},{10,8},{12,... | collective-permute-start | bytes 589832 | tf_op jit(solution)/shard_map/ppermute | solution.py:471
  15.7 2.9 %collective-permute-start.4 = (bf16[3,128,256]{2,1,0:T(8,128)(2,1)}, bf16[3,128,256]{2,1,0:T(8,128)(2,1)}, u32[]{:S(2)}, u32[]{:S(2)}) collective-permute-start(bf16[3,128,256]{2,1,0:T(8,128)(2,1)} %get-tuple-element.72), channel_id=1, source_target_pairs={{0,4},{2,6},{4,0},{6,2},{1,5},{3,7},{5,1},{7,3},{8,12},{10,14},{12... | collective-permute-start | bytes 589832 | tf_op jit(solution)/shard_map/ppermute | solution.py:471
  18.7 6.9 %collective-permute-done.2.refs_1_ = bf16[2,128,384]{2,1,0:T(8,128)(2,1)S(1)} collective-permute-done((bf16[2,128,384]{2,1,0:T(8,128)(2,1)S(1)}, bf16[2,128,384]{2,1,0:T(8,128)(2,1)S(1)}, u32[]{:S(2)}, u32[]{:S(2)}) %collective-permute-start.2) | collective-permute-done | bytes 196640 | tf_op jit(solution)/shard_map/ppermute | solution.py:471
  25.6 1.3 %turn_cotangent.1 = (bf16[6,3,128,128]{3,2,1,0:T(8,128)(2,1)S(1)}, bf16[2,3,128,128]{3,2,1,0:T(8,128)(2,1)}, bf16[2,3,128,128]{3,2,1,0:T(8,128)(2,1)}) custom-call(bf16[2,128,384]{2,1,0:T(8,128)(2,1)S(1)} %collective-permute-done.1.refs_0_, bf16[2,128,384]{2,1,0:T(8,128)(2,1)S(1)} %collective-permute-done.2.refs_1_, ...), custom_call_target="tpu_custom_call" | custom-call | flops 200000000 | tf_op jit(solution)/shard_map/turn_cotangent/pallas_call | solution.py:247
  26.9 0.8 %copy-done = bf16[6,3,128,128]{3,2,1,0:T(8,128)(2,1)} copy-done((bf16[6,3,128,128]{3,2,1,0:T(8,128)(2,1)}, bf16[6,3,128,128]{3,2,1,0:T(8,128)(2,1)S(1)}, u32[]{:S(2)}) %copy-start) | copy-done | bytes 589848
  27.7 1.7 %collective-permute-start.6 = (bf16[2,3,128,128]{3,2,1,0:T(8,128)(2,1)}, bf16[2,3,128,128]{3,2,1,0:T(8,128)(2,1)}, u32[]{:S(2)}, u32[]{:S(2)}) collective-permute-start(bf16[2,3,128,128]{3,2,1,0:T(8,128)(2,1)} %get-tuple-element.76), channel_id=1, source_target_pairs={{0,1},{1,0},{2,3},{3,2},{4,5},{5,4},{6,7},{7,6},{8,9},{9,8},{10,11... | collective-permute-start | bytes 589832 | tf_op jit(solution)/shard_map/ppermute | solution.py:471
  31.3 1.8 %fetch.1 = (bf16[6,3,128,128]{3,2,1,0:T(8,128)(2,1)S(1)}, bf16[256,1536]{1,0:T(8,128)(2,1)S(1)}, bf16[256,1536]{1,0:T(8,128)(2,1)S(1)}, bf16[256,1536]{1,0:T(8,128)(2,1)S(1)}) custom-call(bf16[6,3,128,128]{3,2,1,0:T(8,128)(2,1)} %copy-done, bf16[256,1536]{1,0:T(8,128)(2,1)} %bitcast.14, bf16[256,1536]{1,0:T(8,128)(2,1)} %bitcast.16, bf16[256,1536]{1,0:T(8,128)(2,1)} %bitcast.18), custom_call_target="tpu_custom_call" | custom-call | flops 100000000 | tf_op jit(solution)/shard_map/fetch/pallas_call | solution.py:366
  33.1 4.4 %collective-permute-done.4.refs_1_ = bf16[3,128,256]{2,1,0:T(8,128)(2,1)} collective-permute-done((bf16[3,128,256]{2,1,0:T(8,128)(2,1)}, bf16[3,128,256]{2,1,0:T(8,128)(2,1)}, u32[]{:S(2)}, u32[]{:S(2)}) %collective-permute-start.4) | collective-permute-done | bytes 196640 | tf_op jit(solution)/shard_map/ppermute | solution.py:471
  37.5 3.6 %temporal.1 = (bf16[3,128,256]{2,1,0:T(8,128)(2,1)S(1)}, bf16[3,128,256]{2,1,0:T(8,128)(2,1)S(1)}, bf16[3,128,256]{2,1,0:T(8,128)(2,1)S(1)}, bf16[3,128,256]{2,1,0:T(8,128)(2,1)S(1)}, f32[8,128]{1,0:T(8,128)S(1)}) custom-call(s32[1]{0:T(128)S(6)} %copy.19.length_ref, s32[1]{0:T(128)} %copy.18.task_ref, ...), custom_call_target="tpu_custom_call" | custom-call | flops 400000000 | tf_op jit(solution)/shard_map/temporal/pallas_call | solution.py:431
  41.2 2.7 %collective-permute-start.8 = (bf16[3,128,256]{2,1,0:T(8,128)(2,1)S(1)}, bf16[3,128,256]{2,1,0:T(8,128)(2,1)S(1)}, u32[]{:S(2)}, u32[]{:S(2)}) collective-permute-start(bf16[3,128,256]{2,1,0:T(8,128)(2,1)S(1)} %get-tuple-element.78), channel_id=1, source_target_pairs={{0,6},{2,4},{4,2},{6,0},{1,7},{3,5},{5,3},{7,1},{8,14},{10,12},{12... | collective-permute-start | bytes 589832 | tf_op jit(solution)/shard_map/ppermute | solution.py:471
  44.0 2.6 %collective-permute-start.9 = (bf16[3,128,256]{2,1,0:T(8,128)(2,1)S(1)}, bf16[3,128,256]{2,1,0:T(8,128)(2,1)S(1)}, u32[]{:S(2)}, u32[]{:S(2)}) collective-permute-start(bf16[3,128,256]{2,1,0:T(8,128)(2,1)S(1)} %get-tuple-element.79), channel_id=1, source_target_pairs={{0,4},{2,6},{4,0},{6,2},{1,5},{3,7},{5,1},{7,3},{8,12},{10,14},{12... | collective-permute-start | bytes 589832 | tf_op jit(solution)/shard_map/ppermute | solution.py:471
  46.7 1.5 %collective-permute-start.11 = (f32[16,128]{1,0:T(8,128)S(1)}, f32[16,128]{1,0:T(8,128)S(1)}, u32[]{:S(2)}, u32[]{:S(2)}) collective-permute-start(f32[16,128]{1,0:T(8,128)S(1)} %pad_maximum_fusion.1), channel_id=1, source_target_pairs={{0,16},{8,24},{16,0},{24,8},{1,17},{9,25},{17,1},{25,9},{2,18},{10... | collective-permute-start | bytes 24584 | tf_op jit(solution)/shard_map/ppermute | solution.py:471
  48.2 1.4 %spatial_backward.3 = (bf16[256,1536]{1,0:T(8,128)(2,1)}, bf16[256,1536]{1,0:T(8,128)(2,1)}) custom-call(bf16[256,1536]{1,0:T(8,128)(2,1)S(1)} %get-tuple-element.68.refs_0_, bf16[256,1536]{1,0:T(8,128)(2,1)S(1)} %get-tuple-element.69.refs_1_, bf16[256,1536]{1,0:T(8,128)(2,1)S(1)} %get-tuple-element.70.refs_2_, ...), custom_call_target="tpu_custom_call" | custom-call | flops 200000000 | tf_op jit(solution)/shard_map/spatial_backward/pallas_call | solution.py:159
  49.6 0.7 %collective-permute-done.11 = f32[16,128]{1,0:T(8,128)S(1)} collective-permute-done((f32[16,128]{1,0:T(8,128)S(1)}, f32[16,128]{1,0:T(8,128)S(1)}, u32[]{:S(2)}, u32[]{:S(2)}) %collective-permute-start.11) | collective-permute-done | bytes 8224 | tf_op jit(solution)/shard_map/ppermute | solution.py:471
  50.4 2.4 %collective-permute-start.15 = (f32[32,128]{1,0:T(8,128)S(1)}, f32[32,128]{1,0:T(8,128)S(1)}, u32[]{:S(2)}, u32[]{:S(2)}) collective-permute-start(f32[32,128]{1,0:T(8,128)S(1)} %pad_maximum_fusion.refs_6_), channel_id=1, source_target_pairs={{0,6},{2,4},{4,2},{6,0},{1,7},{3,5},{5,3},{7,1},{8,14},{10,12},{12... | collective-permute-start | bytes 49160 | tf_op jit(solution)/shard_map/ppermute | solution.py:471
  52.8 0.9 %collective-permute-start.14 = (f32[32,128]{1,0:T(8,128)S(1)}, f32[32,128]{1,0:T(8,128)S(1)}, u32[]{:S(2)}, u32[]{:S(2)}) collective-permute-start(f32[32,128]{1,0:T(8,128)S(1)} %pad_maximum_fusion.refs_6_), channel_id=1, source_target_pairs={{0,4},{2,6},{4,0},{6,2},{1,5},{3,7},{5,1},{7,3},{8,12},{10,14},{12... | collective-permute-start | bytes 49160 | tf_op jit(solution)/shard_map/ppermute | solution.py:471
  53.7 3.9 %collective-permute-done.12.refs_4_ = bf16[3,128,256]{2,1,0:T(8,128)(2,1)S(1)} collective-permute-done((bf16[3,128,256]{2,1,0:T(8,128)(2,1)S(1)}, bf16[3,128,256]{2,1,0:T(8,128)(2,1)S(1)}, u32[]{:S(2)}, u32[]{:S(2)}) %collective-permute-start.12) | collective-permute-done | bytes 196640 | tf_op jit(solution)/shard_map/ppermute | solution.py:471
  57.6 2.5 %collective-permute-start.13 = (f32[32,128]{1,0:T(8,128)S(1)}, f32[32,128]{1,0:T(8,128)S(1)}, u32[]{:S(2)}, u32[]{:S(2)}) collective-permute-start(f32[32,128]{1,0:T(8,128)S(1)} %pad_maximum_fusion.refs_6_), channel_id=1, source_target_pairs={{0,2},{2,0},{4,6},{6,4},{1,3},{3,1},{5,7},{7,5},{8,10},{10,8},{12,... | collective-permute-start | bytes 49160 | tf_op jit(solution)/shard_map/ppermute | solution.py:471
  60.1 1.4 %spatial_backward.4 = (bf16[256,1536]{1,0:T(8,128)(2,1)}, bf16[256,1536]{1,0:T(8,128)(2,1)}) custom-call(bf16[256,1536]{1,0:T(8,128)(2,1)S(1)} %get-tuple-element.68.refs_0_, bf16[256,1536]{1,0:T(8,128)(2,1)S(1)} %get-tuple-element.69.refs_1_, bf16[256,1536]{1,0:T(8,128)(2,1)S(1)} %get-tuple-element.70.refs_2_, ...), custom_call_target="tpu_custom_call", output_to_operand_aliasing={{0}: (5, {}), {1}: (6, {})} | custom-call | flops 200000000 | tf_op jit(solution)/shard_map/spatial_backward/pallas_call | solution.py:159
  61.5 3.0 %collective-permute-done.14.refs_8_ = f32[32,128]{1,0:T(8,128)S(1)} collective-permute-done((f32[32,128]{1,0:T(8,128)S(1)}, f32[32,128]{1,0:T(8,128)S(1)}, u32[]{:S(2)}, u32[]{:S(2)}) %collective-permute-start.14) | collective-permute-done | bytes 16416 | tf_op jit(solution)/shard_map/ppermute | solution.py:471
  64.5 2.0 %spatial_backward.5 = (bf16[256,1536]{1,0:T(8,128)(2,1)}, bf16[256,1536]{1,0:T(8,128)(2,1)}, f32[2,16,1536]{2,1,0:T(8,128)}) custom-call(bf16[256,1536]{1,0:T(8,128)(2,1)S(1)} %get-tuple-element.68.refs_0_, bf16[256,1536]{1,0:T(8,128)(2,1)S(1)} %get-tuple-element.69.refs_1_, ...), custom_call_target="tpu_custom_call", output_to_operand_aliasing={{0}: (11, {}), {1}: (12, {})} | custom-call | flops 200000000 | tf_op jit(solution)/shard_map/spatial_backward/pallas_call | solution.py:159
  (24 shorter events, 1.5 us)
Async XLA Ops:
  0.6 30.4 %copy-start.1 = (f32[2,16,1536]{2,1,0:T(8,128)S(1)}, f32[2,16,1536]{2,1,0:T(8,128)}, u32[]{:S(2)}) copy-start(f32[2,16,1536]{2,1,0:T(8,128)} %refs_10_.1) | copy-start | bytes 589828
  2.0 16.7 %collective-permute-start.1 = (bf16[2,128,384]{2,1,0:T(8,128)(2,1)S(1)}, bf16[2,128,384]{2,1,0:T(8,128)(2,1)S(1)}, u32[]{:S(2)}, u32[]{:S(2)}) collective-permute-start(bf16[2,128,384]{2,1,0:T(8,128)(2,1)S(1)} %get-tuple-element.56), channel_id=1, source_target_pairs={{0,6},{2,4},{4,2},{6,0},{1,7},{3,5},{5,3},{7,1},{8,14},{10,12},{12... | collective-permute-start | bytes 589832 | tf_op jit(solution)/shard_map/ppermute | solution.py:471
  7.1 18.5 %collective-permute-start.2 = (bf16[2,128,384]{2,1,0:T(8,128)(2,1)S(1)}, bf16[2,128,384]{2,1,0:T(8,128)(2,1)S(1)}, u32[]{:S(2)}, u32[]{:S(2)}) collective-permute-start(bf16[2,128,384]{2,1,0:T(8,128)(2,1)S(1)} %get-tuple-element.57), channel_id=1, source_target_pairs={{0,4},{2,6},{4,0},{6,2},{1,5},{3,7},{5,1},{7,3},{8,12},{10,14},{12... | collective-permute-start | bytes 589832 | tf_op jit(solution)/shard_map/ppermute | solution.py:471
  7.1 18.5 %collective-permute-start.3 = (bf16[2,128,384]{2,1,0:T(8,128)(2,1)S(1)}, bf16[2,128,384]{2,1,0:T(8,128)(2,1)S(1)}, u32[]{:S(2)}, u32[]{:S(2)}) collective-permute-start(bf16[2,128,384]{2,1,0:T(8,128)(2,1)S(1)} %get-tuple-element.58), channel_id=1, source_target_pairs={{0,2},{2,0},{4,6},{6,4},{1,3},{3,1},{5,7},{7,5},{8,10},{10,8},{12,... | collective-permute-start | bytes 589832 | tf_op jit(solution)/shard_map/ppermute | solution.py:471
  14.3 16.9 %collective-permute-start = (bf16[3,128,256]{2,1,0:T(8,128)(2,1)}, bf16[3,128,256]{2,1,0:T(8,128)(2,1)S(1)}, u32[]{:S(2)}, u32[]{:S(2)}) collective-permute-start(bf16[3,128,256]{2,1,0:T(8,128)(2,1)} %get-tuple-element.55), channel_id=1, source_target_pairs={{0,2},{2,0},{4,6},{6,4},{1,3},{3,1},{5,7},{7,5},{8,10},{10,8},{12,... | collective-permute-start | bytes 589832 | tf_op jit(solution)/shard_map/ppermute | solution.py:471
  15.7 21.8 %collective-permute-start.4 = (bf16[3,128,256]{2,1,0:T(8,128)(2,1)}, bf16[3,128,256]{2,1,0:T(8,128)(2,1)}, u32[]{:S(2)}, u32[]{:S(2)}) collective-permute-start(bf16[3,128,256]{2,1,0:T(8,128)(2,1)} %get-tuple-element.72), channel_id=1, source_target_pairs={{0,4},{2,6},{4,0},{6,2},{1,5},{3,7},{5,1},{7,3},{8,12},{10,14},{12... | collective-permute-start | bytes 589832 | tf_op jit(solution)/shard_map/ppermute | solution.py:471
  18.6 18.9 %collective-permute-start.5 = (bf16[3,128,256]{2,1,0:T(8,128)(2,1)}, bf16[3,128,256]{2,1,0:T(8,128)(2,1)}, u32[]{:S(2)}, u32[]{:S(2)}) collective-permute-start(bf16[3,128,256]{2,1,0:T(8,128)(2,1)} %get-tuple-element.73), channel_id=1, source_target_pairs={{0,6},{2,4},{4,2},{6,0},{1,7},{3,5},{5,3},{7,1},{8,14},{10,12},{12... | collective-permute-start | bytes 589832 | tf_op jit(solution)/shard_map/ppermute | solution.py:471
  26.9 0.8 %copy-start = (bf16[6,3,128,128]{3,2,1,0:T(8,128)(2,1)}, bf16[6,3,128,128]{3,2,1,0:T(8,128)(2,1)S(1)}, u32[]{:S(2)}) copy-start(bf16[6,3,128,128]{3,2,1,0:T(8,128)(2,1)S(1)} %get-tuple-element.67.refs_0_) | copy-start | bytes 1769476
  27.7 9.8 %collective-permute-start.6 = (bf16[2,3,128,128]{3,2,1,0:T(8,128)(2,1)}, bf16[2,3,128,128]{3,2,1,0:T(8,128)(2,1)}, u32[]{:S(2)}, u32[]{:S(2)}) collective-permute-start(bf16[2,3,128,128]{3,2,1,0:T(8,128)(2,1)} %get-tuple-element.76), channel_id=1, source_target_pairs={{0,1},{1,0},{2,3},{3,2},{4,5},{5,4},{6,7},{7,6},{8,9},{9,8},{10,11... | collective-permute-start | bytes 589832 | tf_op jit(solution)/shard_map/ppermute | solution.py:471
  29.5 8.1 %collective-permute-start.7 = (bf16[2,3,128,128]{3,2,1,0:T(8,128)(2,1)}, bf16[2,3,128,128]{3,2,1,0:T(8,128)(2,1)}, u32[]{:S(2)}, u32[]{:S(2)}) collective-permute-start(bf16[2,3,128,128]{3,2,1,0:T(8,128)(2,1)} %get-tuple-element.77), channel_id=1, source_target_pairs={{0,1},{1,0},{2,3},{3,2},{4,5},{5,4},{6,7},{7,6},{8,9},{9,8},{10,11... | collective-permute-start | bytes 589832 | tf_op jit(solution)/shard_map/ppermute | solution.py:471
  41.2 5.5 %collective-permute-start.10 = (f32[8,128]{1,0:T(8,128)S(1)}, f32[8,128]{1,0:T(8,128)S(1)}, u32[]{:S(2)}, u32[]{:S(2)}) collective-permute-start(f32[8,128]{1,0:T(8,128)S(1)} %get-tuple-element.80), channel_id=1, source_target_pairs={{0,8},{8,0},{16,24},{24,16},{1,9},{9,1},{17,25},{25,17},{2,10},{10... | collective-permute-start | bytes 12296 | tf_op jit(solution)/shard_map/ppermute | solution.py:471
  41.2 23.2 %collective-permute-start.8 = (bf16[3,128,256]{2,1,0:T(8,128)(2,1)S(1)}, bf16[3,128,256]{2,1,0:T(8,128)(2,1)S(1)}, u32[]{:S(2)}, u32[]{:S(2)}) collective-permute-start(bf16[3,128,256]{2,1,0:T(8,128)(2,1)S(1)} %get-tuple-element.78), channel_id=1, source_target_pairs={{0,6},{2,4},{4,2},{6,0},{1,7},{3,5},{5,3},{7,1},{8,14},{10,12},{12... | collective-permute-start | bytes 589832 | tf_op jit(solution)/shard_map/ppermute | solution.py:471
  44.0 20.5 %collective-permute-start.9 = (bf16[3,128,256]{2,1,0:T(8,128)(2,1)S(1)}, bf16[3,128,256]{2,1,0:T(8,128)(2,1)S(1)}, u32[]{:S(2)}, u32[]{:S(2)}) collective-permute-start(bf16[3,128,256]{2,1,0:T(8,128)(2,1)S(1)} %get-tuple-element.79), channel_id=1, source_target_pairs={{0,4},{2,6},{4,0},{6,2},{1,5},{3,7},{5,1},{7,3},{8,12},{10,14},{12... | collective-permute-start | bytes 589832 | tf_op jit(solution)/shard_map/ppermute | solution.py:471
  46.6 11.0 %collective-permute-start.12 = (bf16[3,128,256]{2,1,0:T(8,128)(2,1)S(1)}, bf16[3,128,256]{2,1,0:T(8,128)(2,1)S(1)}, u32[]{:S(2)}, u32[]{:S(2)}) collective-permute-start(bf16[3,128,256]{2,1,0:T(8,128)(2,1)S(1)} %get-tuple-element.87), channel_id=1, source_target_pairs={{0,2},{2,0},{4,6},{6,4},{1,3},{3,1},{5,7},{7,5},{8,10},{10,8},{12,... | collective-permute-start | bytes 589832 | tf_op jit(solution)/shard_map/ppermute | solution.py:471
  46.7 3.7 %collective-permute-start.11 = (f32[16,128]{1,0:T(8,128)S(1)}, f32[16,128]{1,0:T(8,128)S(1)}, u32[]{:S(2)}, u32[]{:S(2)}) collective-permute-start(f32[16,128]{1,0:T(8,128)S(1)} %pad_maximum_fusion.1), channel_id=1, source_target_pairs={{0,16},{8,24},{16,0},{24,8},{1,17},{9,25},{17,1},{25,9},{2,18},{10... | collective-permute-start | bytes 24584 | tf_op jit(solution)/shard_map/ppermute | solution.py:471
  50.4 11.1 %collective-permute-start.15 = (f32[32,128]{1,0:T(8,128)S(1)}, f32[32,128]{1,0:T(8,128)S(1)}, u32[]{:S(2)}, u32[]{:S(2)}) collective-permute-start(f32[32,128]{1,0:T(8,128)S(1)} %pad_maximum_fusion.refs_6_), channel_id=1, source_target_pairs={{0,6},{2,4},{4,2},{6,0},{1,7},{3,5},{5,3},{7,1},{8,14},{10,12},{12... | collective-permute-start | bytes 49160 | tf_op jit(solution)/shard_map/ppermute | solution.py:471
  52.8 11.6 %collective-permute-start.14 = (f32[32,128]{1,0:T(8,128)S(1)}, f32[32,128]{1,0:T(8,128)S(1)}, u32[]{:S(2)}, u32[]{:S(2)}) collective-permute-start(f32[32,128]{1,0:T(8,128)S(1)} %pad_maximum_fusion.refs_6_), channel_id=1, source_target_pairs={{0,4},{2,6},{4,0},{6,2},{1,5},{3,7},{5,1},{7,3},{8,12},{10,14},{12... | collective-permute-start | bytes 49160 | tf_op jit(solution)/shard_map/ppermute | solution.py:471
  57.6 6.9 %collective-permute-start.13 = (f32[32,128]{1,0:T(8,128)S(1)}, f32[32,128]{1,0:T(8,128)S(1)}, u32[]{:S(2)}, u32[]{:S(2)}) collective-permute-start(f32[32,128]{1,0:T(8,128)S(1)} %pad_maximum_fusion.refs_6_), channel_id=1, source_target_pairs={{0,2},{2,0},{4,6},{6,4},{1,3},{3,1},{5,7},{7,5},{8,10},{10,8},{12,... | collective-permute-start | bytes 49160 | tf_op jit(solution)/shard_map/ppermute | solution.py:471

commit v16 on v15

--- a/solution.py
+++ b/solution.py
@@ -261,92 +261,108 @@
     )(*reversed(pieces), plane)
 
 
-def temporal_part(length, load_attended, load_upstream, load_gain, fields, ups, normed, grad_ref):
-    frames, feat, lanes = grad_ref.shape
-    half = GROUP // 2
-    score_scale = feat ** (-0.5)
-    pairs = [(t, u) for t in range(frames) for u in range(t + 1)]
-    every = range(frames)
-    valid = [jnp.where(t < length, 1.0, 0.0).astype(jnp.float32) for t in every]
-    bias = [jnp.where(u < length, 0.0, -1e30).astype(jnp.float32) for u in every]
-
-    def total(piece):
-        return jnp.broadcast_to(jnp.sum(piece, axis=0, keepdims=True), (half, lanes))
-
-    squares = [jnp.zeros((half, lanes), jnp.float32) for _ in every]
-    for group in range(feat // GROUP):
-        rows = pl.ds(group * GROUP, GROUP)
-        for t in every:
-            field = load_attended(t, rows).astype(jnp.float32)
-            fields[t, rows, :] = field
-            ups[t, rows, :] = load_upstream(t, rows).astype(jnp.float32)
-            low, high = field[:half], field[half:]
-            squares[t] = squares[t] + (low * low + high * high)
-    inverse = [lax.rsqrt(total(squares[t]) * (1.0 / feat) + 1e-06) for t in every]
-
-    raw = {pair: jnp.zeros((half, lanes), jnp.float32) for pair in pairs}
-    grad = {pair: jnp.zeros((half, lanes), jnp.float32) for pair in pairs}
-    for group in range(feat // half):
-        rows = pl.ds(group * half, half)
-        gain = load_gain(rows)
-        here = [fields[t, rows, :] for t in every]
-        above = [ups[t, rows, :] for t in every]
-        scaled = [here[t] * inverse[t] for t in every]
-        gained = [scaled[t] * gain for t in every]
-        for t in every:
-            normed[t, rows, :] = scaled[t]
-        for t, u in pairs:
-            raw[t, u] = raw[t, u] + gained[t] * scaled[u]
-            grad[t, u] = grad[t, u] + above[t] * here[u]
-
-    value_part, score_part = {}, {}
-    for t in every:
-        seen = range(t + 1)
-        for u in seen:
-            raw[t, u] = total(raw[t, u])
-            grad[t, u] = total(grad[t, u]) * valid[t]
-        scores = [raw[t, u] * score_scale + bias[u] for u in seen]
-        largest = functools.reduce(jnp.maximum, scores)
-        raised = [jnp.exp(score - largest) for score in scores]
-        over = 1.0 / functools.reduce(jnp.add, raised)
-        weights = [piece * over for piece in raised]
-        mean_grad = functools.reduce(jnp.add, [weights[u] * grad[t, u] for u in seen])
-        for u in seen:
-            rounded = weights[u].astype(jnp.bfloat16).astype(jnp.float32)
-            value_part[t, u] = (rounded + (1.0 if u == t else 0.0)) * valid[t]
-            score_part[t, u] = weights[u] * (grad[t, u] - mean_grad) * score_scale
-
-    both = {(t, u): score_part[t, u] * (2.0 if t == u else 1.0) for t, u in pairs}
-    both.update({(u, t): both[t, u] for t, u in pairs})
-    raw.update({(u, t): raw[t, u] for t, u in pairs})
-    mean_part = [
-        functools.reduce(jnp.add, [both[u, v] * raw[u, v] for v in every]) * (1.0 / feat)
-        for u in every
-    ]
-
-    all_mixed = []
-    for group in range(feat // GROUP):
-        outs = [[] for _ in every]
-        for side in range(2):
-            rows = pl.ds(group * GROUP + side * half, half)
-            gain = load_gain(rows)
-            scaled = [normed[t, rows, :] for t in every]
-            above = [ups[t, rows, :] for t in every]
-            mixed = jnp.zeros((half, lanes), jnp.float32)
-            for u in every:
-                crossed = functools.reduce(jnp.add, [both[u, v] * scaled[v] for v in every])
-                mixed = mixed + crossed * scaled[u]
-                from_norm = inverse[u] * (gain * crossed - scaled[u] * mean_part[u])
-                direct = functools.reduce(
-                    jnp.add, [value_part[t, u] * above[t] for t in range(u, frames)]
-                )
-                outs[u].append(direct + from_norm)
-            all_mixed.append(mixed)
-        for u in every:
-            grad_ref[u, pl.ds(group * GROUP, GROUP), :] = jnp.concatenate(
-                outs[u], axis=0
-            ).astype(jnp.bfloat16)
-    return jnp.concatenate(all_mixed, axis=0)
+class Block:
+    def __init__(self, length, load_attended, load_upstream, load_gain, scratch, grad_ref):
+        self.load_attended, self.load_upstream = load_attended, load_upstream
+        self.load_gain, self.grad_ref = load_gain, grad_ref
+        self.fields, self.ups, self.normed = (scratch.at[index] for index in range(3))
+        self.frames, self.feat, self.lanes = grad_ref.shape
+        self.half = GROUP // 2
+        self.every = range(self.frames)
+        self.pairs = [(t, u) for t in self.every for u in range(t + 1)]
+        self.valid = [jnp.where(t < length, 1.0, 0.0).astype(jnp.float32) for t in self.every]
+        self.bias = [jnp.where(u < length, 0.0, -1e30).astype(jnp.float32) for u in self.every]
+
+    def total(self, piece):
+        return jnp.broadcast_to(jnp.sum(piece, axis=0, keepdims=True), (self.half, self.lanes))
+
+    def zeros(self):
+        return jnp.zeros((self.half, self.lanes), jnp.float32)
+
+    def widen(self):
+        squares = [self.zeros() for _ in self.every]
+        for group in range(self.feat // GROUP):
+            rows = pl.ds(group * GROUP, GROUP)
+            for t in self.every:
+                field = self.load_attended(t, rows).astype(jnp.float32)
+                self.fields[t, rows, :] = field
+                self.ups[t, rows, :] = self.load_upstream(t, rows).astype(jnp.float32)
+                low, high = field[: self.half], field[self.half :]
+                squares[t] = squares[t] + (low * low + high * high)
+        self.inverse = [
+            lax.rsqrt(self.total(square) * (1.0 / self.feat) + 1e-06) for square in squares
+        ]
+
+    def sums(self):
+        raw = {pair: self.zeros() for pair in self.pairs}
+        grad = {pair: self.zeros() for pair in self.pairs}
+        for group in range(self.feat // self.half):
+            rows = pl.ds(group * self.half, self.half)
+            gain = self.load_gain(rows)
+            here = [self.fields[t, rows, :] for t in self.every]
+            above = [self.ups[t, rows, :] for t in self.every]
+            scaled = [here[t] * self.inverse[t] for t in self.every]
+            gained = [scaled[t] * gain for t in self.every]
+            for t in self.every:
+                self.normed[t, rows, :] = scaled[t]
+            for t, u in self.pairs:
+                raw[t, u] = raw[t, u] + gained[t] * scaled[u]
+                grad[t, u] = grad[t, u] + above[t] * here[u]
+        self.raw = {pair: self.total(raw[pair]) for pair in self.pairs}
+        self.grad = {pair: self.total(grad[pair]) * self.valid[pair[0]] for pair in self.pairs}
+
+    def weigh(self):
+        score_scale = self.feat ** (-0.5)
+        raw, grad = self.raw, self.grad
+        self.value_part, score_part = {}, {}
+        for t in self.every:
+            seen = range(t + 1)
+            scores = [raw[t, u] * score_scale + self.bias[u] for u in seen]
+            largest = functools.reduce(jnp.maximum, scores)
+            raised = [jnp.exp(score - largest) for score in scores]
+            over = 1.0 / functools.reduce(jnp.add, raised)
+            weights = [piece * over for piece in raised]
+            mean_grad = functools.reduce(jnp.add, [weights[u] * grad[t, u] for u in seen])
+            for u in seen:
+                rounded = weights[u].astype(jnp.bfloat16).astype(jnp.float32)
+                self.value_part[t, u] = (rounded + (1.0 if u == t else 0.0)) * self.valid[t]
+                score_part[t, u] = weights[u] * (grad[t, u] - mean_grad) * score_scale
+        both = {(t, u): score_part[t, u] * (2.0 if t == u else 1.0) for t, u in self.pairs}
+        both.update({(u, t): both[t, u] for t, u in self.pairs})
+        raw.update({(u, t): raw[t, u] for t, u in self.pairs})
+        self.both = both
+        self.mean_part = [
+            functools.reduce(jnp.add, [both[u, v] * raw[u, v] for v in self.every])
+            * (1.0 / self.feat)
+            for u in self.every
+        ]
+
+    def gradients(self):
+        all_mixed = []
+        for group in range(self.feat // GROUP):
+            outs = [[] for _ in self.every]
+            for side in range(2):
+                rows = pl.ds(group * GROUP + side * self.half, self.half)
+                gain = self.load_gain(rows)
+                scaled = [self.normed[t, rows, :] for t in self.every]
+                above = [self.ups[t, rows, :] for t in self.every]
+                mixed = self.zeros()
+                for u in self.every:
+                    crossed = functools.reduce(
+                        jnp.add, [self.both[u, v] * scaled[v] for v in self.every]
+                    )
+                    mixed = mixed + crossed * scaled[u]
+                    from_norm = self.inverse[u] * (gain * crossed - scaled[u] * self.mean_part[u])
+                    direct = functools.reduce(
+                        jnp.add, [self.value_part[t, u] * above[t] for t in range(u, self.frames)]
+                    )
+                    outs[u].append(direct + from_norm)
+                all_mixed.append(mixed)
+            for u in self.every:
+                self.grad_ref[u, pl.ds(group * GROUP, GROUP), :] = jnp.concatenate(
+                    outs[u], axis=0
+                ).astype(jnp.bfloat16)
+        return jnp.concatenate(all_mixed, axis=0)
 
 
 def fetch_kernel(*refs):
@@ -400,23 +416,33 @@
             attended[head, space, partner("tm", 0)] = own_ref[frames + space, head]
             for distance, ref in enumerate(attended_refs):
                 attended[head, space, partner("tm", distance + 1)] = ref[head, :, here]
-        mixed = [
-            temporal_part(
-                length_ref[0],
-                lambda t, rows: attended[head, space, t, rows, :],
-                functools.partial(load_upstream, space, head),
-                lambda rows: gain_ref[head, rows, :],
-                wide.at[head % 2, space, 0],
-                wide.at[head % 2, space, 1],
-                wide.at[head % 2, space, 2],
-                grads.at[head, space],
-            )
-            for space in range(spaces)
-        ]
-        summed = functools.reduce(jnp.add, mixed)
+    blocks = [
+        Block(
+            length_ref[0],
+            functools.partial(lambda head, space, t, rows: attended[head, space, t, rows, :], head, space),
+            functools.partial(load_upstream, space, head),
+            functools.partial(lambda head, rows: gain_ref[head, rows, :], head),
+            wide.at[head, space],
+            grads.at[head, space],
+        )
+        for head in range(heads)
+        for space in range(spaces)
+    ]
+    for block in blocks:
+        block.widen()
+    blocks[0].sums()
+    mixed = []
+    for block, later in zip(blocks, blocks[1:] + [None]):
+        block.weigh()
+        if later:
+            later.sums()
+        mixed.append(block.gradients())
+    for head in range(heads):
+        summed = functools.reduce(jnp.add, mixed[head * spaces : (head + 1) * spaces])
         mixed_ref[pl.ds(head, 1), :] = jnp.sum(summed.T, axis=0, keepdims=True) * 0.5
-        for distance, ref in enumerate(grad_refs):
-            frame = partner("tm", distance)
+    for distance, ref in enumerate(grad_refs):
+        frame = partner("tm", distance)
+        for head in range(heads):
             for space, here in enumerate(places):
                 ref[head, :, here] = grads[head, space, frame]
 
@@ -436,7 +462,7 @@
         scratch_shapes=[
             pltpu.VMEM(block, jnp.bfloat16),
             pltpu.VMEM(block, jnp.bfloat16),
-            pltpu.VMEM((2, spaces, 3, frames, feat, lanes), jnp.float32),
+            pltpu.VMEM((heads, spaces, 3, frames, feat, lanes), jnp.float32),
         ],
         out_shape=[jax.ShapeDtypeStruct((heads, feat, patches), jnp.bfloat16)] * frames
         + [jax.ShapeDtypeStruct((rows, feat), jnp.float32)],

time: 66.7 us -> 66.8 us (level)
  no operation moved by 1% of the time
where the time goes in v16:
time: 66.8 us; the launch traced here: 66.5 us
  starting transfers between devices  25.1 us (38%)
  Pallas kernels  19.4 us (29%)
  waiting for transfers between devices  18.9 us (28%)
  between operations  2.07 us (3%)
  local copies, waits for them, and re-layouts  0.92 us (1%)
    ppermute x16, starting transfers between devices, swap(): return lax.ppermute(field, axis, [(i, i ^ distance) for i in range(size)])  25.1 us
    ppermute x16, waiting for transfers between devices, swap(): return lax.ppermute(field, axis, [(i, i ^ distance) for i in range(size)])  18.9 us
    pallas_call x1, Pallas kernels, forward(): pl.pallas_call(functools.partial(forward_kernel, axis), in_specs=[pl.Bloc...  6.52 us
    pallas_call x3, Pallas kernels, backward(): pl.pallas_call(functools.partial(backward_kernel, axis, distances, gains_...  4.82 us
    pallas_call x1, Pallas kernels, temporal(): pl.pallas_call(functools.partial(temporal_kernel, frames, spaces), in_spe...  3.66 us
    pallas_call x1, Pallas kernels, fetch(): pl.pallas_call(fetch_kernel, in_specs=[pl.BlockSpec(memory_space=pltpu.HB...  1.83 us
  transfers between devices with their start and end apart: 16, of which 5 were waited for; matrix products, arithmetic and copies ran while one was open for 0% of the time, Pallas kernels for 19%

profile of v16, /device:TPU:0, one launch (start us, length us, event | category | flops | bytes accessed | tf_op | source)
XLA Modules:
  0.0 66.5 jit_solution(7314453296502459286)
XLA Ops:
  0.6 1.3 %pack_cotangent.1 = (bf16[2,128,384]{2,1,0:T(8,128)(2,1)S(1)}, bf16[2,128,384]{2,1,0:T(8,128)(2,1)S(1)}, bf16[2,128,384]{2,1,0:T(8,128)(2,1)S(1)}, bf16[2,128,384]{2,1,0:T(8,128)(2,1)S(1)}) custom-call(bf16[128,3072]{1,0:T(8,128)(2,1)} %bitcast.19), custom_call_target="tpu_custom_call" | custom-call | flops 100000000 | tf_op jit(solution)/shard_map/pack_cotangent/pallas_call | solution.py:198
  2.0 5.1 %collective-permute-start.1 = (bf16[2,128,384]{2,1,0:T(8,128)(2,1)S(1)}, bf16[2,128,384]{2,1,0:T(8,128)(2,1)S(1)}, u32[]{:S(2)}, u32[]{:S(2)}) collective-permute-start(bf16[2,128,384]{2,1,0:T(8,128)(2,1)S(1)} %get-tuple-element.56), channel_id=1, source_target_pairs={{0,6},{2,4},{4,2},{6,0},{1,7},{3,5},{5,3},{7,1},{8,14},{10,12},{12... | collective-permute-start | bytes 589832 | tf_op jit(solution)/shard_map/ppermute | solution.py:497
  7.7 6.5 %spatial_forward.1 = (f32[12,256,256]{2,1,0:T(8,128)S(1)}, bf16[3,128,256]{2,1,0:T(8,128)(2,1)S(1)}, bf16[3,128,256]{2,1,0:T(8,128)(2,1)}, bf16[3,128,256]{2,1,0:T(8,128)(2,1)}, bf16[3,128,256]{2,1,0:T(8,128)(2,1)}) custom-call(bf16[256,1536]{1,0:T(8,128)(2,1)} %bitcast.13, bf16[256,1536]{1,0:T(8,128)(2,1)} %bitcast.15, bf16[256,1536]{1,0:T(8,128)(2,1)} %bitcast.17), custom_call_target="tpu_custom_call" | custom-call | flops 600000000 | tf_op jit(solution)/shard_map/spatial_forward/pallas_call | solution.py:76
  14.3 1.4 %collective-permute-start = (bf16[3,128,256]{2,1,0:T(8,128)(2,1)}, bf16[3,128,256]{2,1,0:T(8,128)(2,1)S(1)}, u32[]{:S(2)}, u32[]{:S(2)}) collective-permute-start(bf16[3,128,256]{2,1,0:T(8,128)(2,1)} %get-tuple-element.55), channel_id=1, source_target_pairs={{0,2},{2,0},{4,6},{6,4},{1,3},{3,1},{5,7},{7,5},{8,10},{10,8},{12,... | collective-permute-start | bytes 589832 | tf_op jit(solution)/shard_map/ppermute | solution.py:497
  15.7 2.9 %collective-permute-start.4 = (bf16[3,128,256]{2,1,0:T(8,128)(2,1)}, bf16[3,128,256]{2,1,0:T(8,128)(2,1)}, u32[]{:S(2)}, u32[]{:S(2)}) collective-permute-start(bf16[3,128,256]{2,1,0:T(8,128)(2,1)} %get-tuple-element.72), channel_id=1, source_target_pairs={{0,4},{2,6},{4,0},{6,2},{1,5},{3,7},{5,1},{7,3},{8,12},{10,14},{12... | collective-permute-start | bytes 589832 | tf_op jit(solution)/shard_map/ppermute | solution.py:497
  18.7 6.9 %collective-permute-done.2.refs_1_ = bf16[2,128,384]{2,1,0:T(8,128)(2,1)S(1)} collective-permute-done((bf16[2,128,384]{2,1,0:T(8,128)(2,1)S(1)}, bf16[2,128,384]{2,1,0:T(8,128)(2,1)S(1)}, u32[]{:S(2)}, u32[]{:S(2)}) %collective-permute-start.2) | collective-permute-done | bytes 196640 | tf_op jit(solution)/shard_map/ppermute | solution.py:497
  25.6 1.3 %turn_cotangent.1 = (bf16[6,3,128,128]{3,2,1,0:T(8,128)(2,1)S(1)}, bf16[2,3,128,128]{3,2,1,0:T(8,128)(2,1)}, bf16[2,3,128,128]{3,2,1,0:T(8,128)(2,1)}) custom-call(bf16[2,128,384]{2,1,0:T(8,128)(2,1)S(1)} %collective-permute-done.1.refs_0_, bf16[2,128,384]{2,1,0:T(8,128)(2,1)S(1)} %collective-permute-done.2.refs_1_, ...), custom_call_target="tpu_custom_call" | custom-call | flops 200000000 | tf_op jit(solution)/shard_map/turn_cotangent/pallas_call | solution.py:247
  26.9 0.8 %copy-done = bf16[6,3,128,128]{3,2,1,0:T(8,128)(2,1)} copy-done((bf16[6,3,128,128]{3,2,1,0:T(8,128)(2,1)}, bf16[6,3,128,128]{3,2,1,0:T(8,128)(2,1)S(1)}, u32[]{:S(2)}) %copy-start) | copy-done | bytes 589848
  27.7 1.7 %collective-permute-start.6 = (bf16[2,3,128,128]{3,2,1,0:T(8,128)(2,1)}, bf16[2,3,128,128]{3,2,1,0:T(8,128)(2,1)}, u32[]{:S(2)}, u32[]{:S(2)}) collective-permute-start(bf16[2,3,128,128]{3,2,1,0:T(8,128)(2,1)} %get-tuple-element.76), channel_id=1, source_target_pairs={{0,1},{1,0},{2,3},{3,2},{4,5},{5,4},{6,7},{7,6},{8,9},{9,8},{10,11... | collective-permute-start | bytes 589832 | tf_op jit(solution)/shard_map/ppermute | solution.py:497
  31.3 1.8 %fetch.1 = (bf16[6,3,128,128]{3,2,1,0:T(8,128)(2,1)S(1)}, bf16[256,1536]{1,0:T(8,128)(2,1)S(1)}, bf16[256,1536]{1,0:T(8,128)(2,1)S(1)}, bf16[256,1536]{1,0:T(8,128)(2,1)S(1)}) custom-call(bf16[6,3,128,128]{3,2,1,0:T(8,128)(2,1)} %copy-done, bf16[256,1536]{1,0:T(8,128)(2,1)} %bitcast.14, bf16[256,1536]{1,0:T(8,128)(2,1)} %bitcast.16, bf16[256,1536]{1,0:T(8,128)(2,1)} %bitcast.18), custom_call_target="tpu_custom_call" | custom-call | flops 100000000 | tf_op jit(solution)/shard_map/fetch/pallas_call | solution.py:382
  33.1 4.4 %collective-permute-done.4.refs_1_ = bf16[3,128,256]{2,1,0:T(8,128)(2,1)} collective-permute-done((bf16[3,128,256]{2,1,0:T(8,128)(2,1)}, bf16[3,128,256]{2,1,0:T(8,128)(2,1)}, u32[]{:S(2)}, u32[]{:S(2)}) %collective-permute-start.4) | collective-permute-done | bytes 196640 | tf_op jit(solution)/shard_map/ppermute | solution.py:497
  37.5 3.7 %temporal.1 = (bf16[3,128,256]{2,1,0:T(8,128)(2,1)S(1)}, bf16[3,128,256]{2,1,0:T(8,128)(2,1)S(1)}, bf16[3,128,256]{2,1,0:T(8,128)(2,1)S(1)}, bf16[3,128,256]{2,1,0:T(8,128)(2,1)S(1)}, f32[8,128]{1,0:T(8,128)S(1)}) custom-call(s32[1]{0:T(128)S(6)} %copy.19.length_ref, s32[1]{0:T(128)} %copy.18.task_ref, ...), custom_call_target="tpu_custom_call" | custom-call | flops 400000000 | tf_op jit(solution)/shard_map/temporal/pallas_call | solution.py:457
  41.3 2.7 %collective-permute-start.8 = (bf16[3,128,256]{2,1,0:T(8,128)(2,1)S(1)}, bf16[3,128,256]{2,1,0:T(8,128)(2,1)S(1)}, u32[]{:S(2)}, u32[]{:S(2)}) collective-permute-start(bf16[3,128,256]{2,1,0:T(8,128)(2,1)S(1)} %get-tuple-element.78), channel_id=1, source_target_pairs={{0,6},{2,4},{4,2},{6,0},{1,7},{3,5},{5,3},{7,1},{8,14},{10,12},{12... | collective-permute-start | bytes 589832 | tf_op jit(solution)/shard_map/ppermute | solution.py:497
  44.0 2.6 %collective-permute-start.9 = (bf16[3,128,256]{2,1,0:T(8,128)(2,1)S(1)}, bf16[3,128,256]{2,1,0:T(8,128)(2,1)S(1)}, u32[]{:S(2)}, u32[]{:S(2)}) collective-permute-start(bf16[3,128,256]{2,1,0:T(8,128)(2,1)S(1)} %get-tuple-element.79), channel_id=1, source_target_pairs={{0,4},{2,6},{4,0},{6,2},{1,5},{3,7},{5,1},{7,3},{8,12},{10,14},{12... | collective-permute-start | bytes 589832 | tf_op jit(solution)/shard_map/ppermute | solution.py:497
  46.7 1.5 %collective-permute-start.11 = (f32[16,128]{1,0:T(8,128)S(1)}, f32[16,128]{1,0:T(8,128)S(1)}, u32[]{:S(2)}, u32[]{:S(2)}) collective-permute-start(f32[16,128]{1,0:T(8,128)S(1)} %pad_maximum_fusion.1), channel_id=1, source_target_pairs={{0,16},{8,24},{16,0},{24,8},{1,17},{9,25},{17,1},{25,9},{2,18},{10... | collective-permute-start | bytes 24584 | tf_op jit(solution)/shard_map/ppermute | solution.py:497
  48.2 1.4 %spatial_backward.3 = (bf16[256,1536]{1,0:T(8,128)(2,1)}, bf16[256,1536]{1,0:T(8,128)(2,1)}) custom-call(bf16[256,1536]{1,0:T(8,128)(2,1)S(1)} %get-tuple-element.68.refs_0_, bf16[256,1536]{1,0:T(8,128)(2,1)S(1)} %get-tuple-element.69.refs_1_, bf16[256,1536]{1,0:T(8,128)(2,1)S(1)} %get-tuple-element.70.refs_2_, ...), custom_call_target="tpu_custom_call" | custom-call | flops 200000000 | tf_op jit(solution)/shard_map/spatial_backward/pallas_call | solution.py:159
  49.7 0.7 %collective-permute-done.11 = f32[16,128]{1,0:T(8,128)S(1)} collective-permute-done((f32[16,128]{1,0:T(8,128)S(1)}, f32[16,128]{1,0:T(8,128)S(1)}, u32[]{:S(2)}, u32[]{:S(2)}) %collective-permute-start.11) | collective-permute-done | bytes 8224 | tf_op jit(solution)/shard_map/ppermute | solution.py:497
  50.4 2.4 %collective-permute-start.15 = (f32[32,128]{1,0:T(8,128)S(1)}, f32[32,128]{1,0:T(8,128)S(1)}, u32[]{:S(2)}, u32[]{:S(2)}) collective-permute-start(f32[32,128]{1,0:T(8,128)S(1)} %pad_maximum_fusion.refs_6_), channel_id=1, source_target_pairs={{0,6},{2,4},{4,2},{6,0},{1,7},{3,5},{5,3},{7,1},{8,14},{10,12},{12... | collective-permute-start | bytes 49160 | tf_op jit(solution)/shard_map/ppermute | solution.py:497
  52.8 0.9 %collective-permute-start.14 = (f32[32,128]{1,0:T(8,128)S(1)}, f32[32,128]{1,0:T(8,128)S(1)}, u32[]{:S(2)}, u32[]{:S(2)}) collective-permute-start(f32[32,128]{1,0:T(8,128)S(1)} %pad_maximum_fusion.refs_6_), channel_id=1, source_target_pairs={{0,4},{2,6},{4,0},{6,2},{1,5},{3,7},{5,1},{7,3},{8,12},{10,14},{12... | collective-permute-start | bytes 49160 | tf_op jit(solution)/shard_map/ppermute | solution.py:497
  53.8 3.8 %collective-permute-done.12.refs_4_ = bf16[3,128,256]{2,1,0:T(8,128)(2,1)S(1)} collective-permute-done((bf16[3,128,256]{2,1,0:T(8,128)(2,1)S(1)}, bf16[3,128,256]{2,1,0:T(8,128)(2,1)S(1)}, u32[]{:S(2)}, u32[]{:S(2)}) %collective-permute-start.12) | collective-permute-done | bytes 196640 | tf_op jit(solution)/shard_map/ppermute | solution.py:497
  57.6 2.5 %collective-permute-start.13 = (f32[32,128]{1,0:T(8,128)S(1)}, f32[32,128]{1,0:T(8,128)S(1)}, u32[]{:S(2)}, u32[]{:S(2)}) collective-permute-start(f32[32,128]{1,0:T(8,128)S(1)} %pad_maximum_fusion.refs_6_), channel_id=1, source_target_pairs={{0,2},{2,0},{4,6},{6,4},{1,3},{3,1},{5,7},{7,5},{8,10},{10,8},{12,... | collective-permute-start | bytes 49160 | tf_op jit(solution)/shard_map/ppermute | solution.py:497
  60.1 1.4 %spatial_backward.4 = (bf16[256,1536]{1,0:T(8,128)(2,1)}, bf16[256,1536]{1,0:T(8,128)(2,1)}) custom-call(bf16[256,1536]{1,0:T(8,128)(2,1)S(1)} %get-tuple-element.68.refs_0_, bf16[256,1536]{1,0:T(8,128)(2,1)S(1)} %get-tuple-element.69.refs_1_, bf16[256,1536]{1,0:T(8,128)(2,1)S(1)} %get-tuple-element.70.refs_2_, ...), custom_call_target="tpu_custom_call", output_to_operand_aliasing={{0}: (5, {}), {1}: (6, {})} | custom-call | flops 200000000 | tf_op jit(solution)/shard_map/spatial_backward/pallas_call | solution.py:159
  61.5 3.0 %collective-permute-done.14.refs_8_ = f32[32,128]{1,0:T(8,128)S(1)} collective-permute-done((f32[32,128]{1,0:T(8,128)S(1)}, f32[32,128]{1,0:T(8,128)S(1)}, u32[]{:S(2)}, u32[]{:S(2)}) %collective-permute-start.14) | collective-permute-done | bytes 16416 | tf_op jit(solution)/shard_map/ppermute | solution.py:497
  64.5 2.0 %spatial_backward.5 = (bf16[256,1536]{1,0:T(8,128)(2,1)}, bf16[256,1536]{1,0:T(8,128)(2,1)}, f32[2,16,1536]{2,1,0:T(8,128)}) custom-call(bf16[256,1536]{1,0:T(8,128)(2,1)S(1)} %get-tuple-element.68.refs_0_, bf16[256,1536]{1,0:T(8,128)(2,1)S(1)} %get-tuple-element.69.refs_1_, ...), custom_call_target="tpu_custom_call", output_to_operand_aliasing={{0}: (11, {}), {1}: (12, {})} | custom-call | flops 200000000 | tf_op jit(solution)/shard_map/spatial_backward/pallas_call | solution.py:159
  (24 shorter events, 1.5 us)
Async XLA Ops:
  0.6 30.4 %copy-start.1 = (f32[2,16,1536]{2,1,0:T(8,128)S(1)}, f32[2,16,1536]{2,1,0:T(8,128)}, u32[]{:S(2)}) copy-start(f32[2,16,1536]{2,1,0:T(8,128)} %refs_10_.1) | copy-start | bytes 589828
  2.0 16.7 %collective-permute-start.1 = (bf16[2,128,384]{2,1,0:T(8,128)(2,1)S(1)}, bf16[2,128,384]{2,1,0:T(8,128)(2,1)S(1)}, u32[]{:S(2)}, u32[]{:S(2)}) collective-permute-start(bf16[2,128,384]{2,1,0:T(8,128)(2,1)S(1)} %get-tuple-element.56), channel_id=1, source_target_pairs={{0,6},{2,4},{4,2},{6,0},{1,7},{3,5},{5,3},{7,1},{8,14},{10,12},{12... | collective-permute-start | bytes 589832 | tf_op jit(solution)/shard_map/ppermute | solution.py:497
  7.1 18.5 %collective-permute-start.2 = (bf16[2,128,384]{2,1,0:T(8,128)(2,1)S(1)}, bf16[2,128,384]{2,1,0:T(8,128)(2,1)S(1)}, u32[]{:S(2)}, u32[]{:S(2)}) collective-permute-start(bf16[2,128,384]{2,1,0:T(8,128)(2,1)S(1)} %get-tuple-element.57), channel_id=1, source_target_pairs={{0,4},{2,6},{4,0},{6,2},{1,5},{3,7},{5,1},{7,3},{8,12},{10,14},{12... | collective-permute-start | bytes 589832 | tf_op jit(solution)/shard_map/ppermute | solution.py:497
  7.1 18.5 %collective-permute-start.3 = (bf16[2,128,384]{2,1,0:T(8,128)(2,1)S(1)}, bf16[2,128,384]{2,1,0:T(8,128)(2,1)S(1)}, u32[]{:S(2)}, u32[]{:S(2)}) collective-permute-start(bf16[2,128,384]{2,1,0:T(8,128)(2,1)S(1)} %get-tuple-element.58), channel_id=1, source_target_pairs={{0,2},{2,0},{4,6},{6,4},{1,3},{3,1},{5,7},{7,5},{8,10},{10,8},{12,... | collective-permute-start | bytes 589832 | tf_op jit(solution)/shard_map/ppermute | solution.py:497
  14.3 16.9 %collective-permute-start = (bf16[3,128,256]{2,1,0:T(8,128)(2,1)}, bf16[3,128,256]{2,1,0:T(8,128)(2,1)S(1)}, u32[]{:S(2)}, u32[]{:S(2)}) collective-permute-start(bf16[3,128,256]{2,1,0:T(8,128)(2,1)} %get-tuple-element.55), channel_id=1, source_target_pairs={{0,2},{2,0},{4,6},{6,4},{1,3},{3,1},{5,7},{7,5},{8,10},{10,8},{12,... | collective-permute-start | bytes 589832 | tf_op jit(solution)/shard_map/ppermute | solution.py:497
  15.7 21.8 %collective-permute-start.4 = (bf16[3,128,256]{2,1,0:T(8,128)(2,1)}, bf16[3,128,256]{2,1,0:T(8,128)(2,1)}, u32[]{:S(2)}, u32[]{:S(2)}) collective-permute-start(bf16[3,128,256]{2,1,0:T(8,128)(2,1)} %get-tuple-element.72), channel_id=1, source_target_pairs={{0,4},{2,6},{4,0},{6,2},{1,5},{3,7},{5,1},{7,3},{8,12},{10,14},{12... | collective-permute-start | bytes 589832 | tf_op jit(solution)/shard_map/ppermute | solution.py:497
  18.6 18.9 %collective-permute-start.5 = (bf16[3,128,256]{2,1,0:T(8,128)(2,1)}, bf16[3,128,256]{2,1,0:T(8,128)(2,1)}, u32[]{:S(2)}, u32[]{:S(2)}) collective-permute-start(bf16[3,128,256]{2,1,0:T(8,128)(2,1)} %get-tuple-element.73), channel_id=1, source_target_pairs={{0,6},{2,4},{4,2},{6,0},{1,7},{3,5},{5,3},{7,1},{8,14},{10,12},{12... | collective-permute-start | bytes 589832 | tf_op jit(solution)/shard_map/ppermute | solution.py:497
  26.9 0.8 %copy-start = (bf16[6,3,128,128]{3,2,1,0:T(8,128)(2,1)}, bf16[6,3,128,128]{3,2,1,0:T(8,128)(2,1)S(1)}, u32[]{:S(2)}) copy-start(bf16[6,3,128,128]{3,2,1,0:T(8,128)(2,1)S(1)} %get-tuple-element.67.refs_0_) | copy-start | bytes 1769476
  27.7 9.8 %collective-permute-start.6 = (bf16[2,3,128,128]{3,2,1,0:T(8,128)(2,1)}, bf16[2,3,128,128]{3,2,1,0:T(8,128)(2,1)}, u32[]{:S(2)}, u32[]{:S(2)}) collective-permute-start(bf16[2,3,128,128]{3,2,1,0:T(8,128)(2,1)} %get-tuple-element.76), channel_id=1, source_target_pairs={{0,1},{1,0},{2,3},{3,2},{4,5},{5,4},{6,7},{7,6},{8,9},{9,8},{10,11... | collective-permute-start | bytes 589832 | tf_op jit(solution)/shard_map/ppermute | solution.py:497
  29.5 8.1 %collective-permute-start.7 = (bf16[2,3,128,128]{3,2,1,0:T(8,128)(2,1)}, bf16[2,3,128,128]{3,2,1,0:T(8,128)(2,1)}, u32[]{:S(2)}, u32[]{:S(2)}) collective-permute-start(bf16[2,3,128,128]{3,2,1,0:T(8,128)(2,1)} %get-tuple-element.77), channel_id=1, source_target_pairs={{0,1},{1,0},{2,3},{3,2},{4,5},{5,4},{6,7},{7,6},{8,9},{9,8},{10,11... | collective-permute-start | bytes 589832 | tf_op jit(solution)/shard_map/ppermute | solution.py:497
  41.2 5.5 %collective-permute-start.10 = (f32[8,128]{1,0:T(8,128)S(1)}, f32[8,128]{1,0:T(8,128)S(1)}, u32[]{:S(2)}, u32[]{:S(2)}) collective-permute-start(f32[8,128]{1,0:T(8,128)S(1)} %get-tuple-element.80), channel_id=1, source_target_pairs={{0,8},{8,0},{16,24},{24,16},{1,9},{9,1},{17,25},{25,17},{2,10},{10... | collective-permute-start | bytes 12296 | tf_op jit(solution)/shard_map/ppermute | solution.py:497
  41.3 23.2 %collective-permute-start.8 = (bf16[3,128,256]{2,1,0:T(8,128)(2,1)S(1)}, bf16[3,128,256]{2,1,0:T(8,128)(2,1)S(1)}, u32[]{:S(2)}, u32[]{:S(2)}) collective-permute-start(bf16[3,128,256]{2,1,0:T(8,128)(2,1)S(1)} %get-tuple-element.78), channel_id=1, source_target_pairs={{0,6},{2,4},{4,2},{6,0},{1,7},{3,5},{5,3},{7,1},{8,14},{10,12},{12... | collective-permute-start | bytes 589832 | tf_op jit(solution)/shard_map/ppermute | solution.py:497
  44.0 20.5 %collective-permute-start.9 = (bf16[3,128,256]{2,1,0:T(8,128)(2,1)S(1)}, bf16[3,128,256]{2,1,0:T(8,128)(2,1)S(1)}, u32[]{:S(2)}, u32[]{:S(2)}) collective-permute-start(bf16[3,128,256]{2,1,0:T(8,128)(2,1)S(1)} %get-tuple-element.79), channel_id=1, source_target_pairs={{0,4},{2,6},{4,0},{6,2},{1,5},{3,7},{5,1},{7,3},{8,12},{10,14},{12... | collective-permute-start | bytes 589832 | tf_op jit(solution)/shard_map/ppermute | solution.py:497
  46.6 11.0 %collective-permute-start.12 = (bf16[3,128,256]{2,1,0:T(8,128)(2,1)S(1)}, bf16[3,128,256]{2,1,0:T(8,128)(2,1)S(1)}, u32[]{:S(2)}, u32[]{:S(2)}) collective-permute-start(bf16[3,128,256]{2,1,0:T(8,128)(2,1)S(1)} %get-tuple-element.87), channel_id=1, source_target_pairs={{0,2},{2,0},{4,6},{6,4},{1,3},{3,1},{5,7},{7,5},{8,10},{10,8},{12,... | collective-permute-start | bytes 589832 | tf_op jit(solution)/shard_map/ppermute | solution.py:497
  46.7 3.7 %collective-permute-start.11 = (f32[16,128]{1,0:T(8,128)S(1)}, f32[16,128]{1,0:T(8,128)S(1)}, u32[]{:S(2)}, u32[]{:S(2)}) collective-permute-start(f32[16,128]{1,0:T(8,128)S(1)} %pad_maximum_fusion.1), channel_id=1, source_target_pairs={{0,16},{8,24},{16,0},{24,8},{1,17},{9,25},{17,1},{25,9},{2,18},{10... | collective-permute-start | bytes 24584 | tf_op jit(solution)/shard_map/ppermute | solution.py:497
  50.4 11.1 %collective-permute-start.15 = (f32[32,128]{1,0:T(8,128)S(1)}, f32[32,128]{1,0:T(8,128)S(1)}, u32[]{:S(2)}, u32[]{:S(2)}) collective-permute-start(f32[32,128]{1,0:T(8,128)S(1)} %pad_maximum_fusion.refs_6_), channel_id=1, source_target_pairs={{0,6},{2,4},{4,2},{6,0},{1,7},{3,5},{5,3},{7,1},{8,14},{10,12},{12... | collective-permute-start | bytes 49160 | tf_op jit(solution)/shard_map/ppermute | solution.py:497
  52.8 11.7 %collective-permute-start.14 = (f32[32,128]{1,0:T(8,128)S(1)}, f32[32,128]{1,0:T(8,128)S(1)}, u32[]{:S(2)}, u32[]{:S(2)}) collective-permute-start(f32[32,128]{1,0:T(8,128)S(1)} %pad_maximum_fusion.refs_6_), channel_id=1, source_target_pairs={{0,4},{2,6},{4,0},{6,2},{1,5},{3,7},{5,1},{7,3},{8,12},{10,14},{12... | collective-permute-start | bytes 49160 | tf_op jit(solution)/shard_map/ppermute | solution.py:497
  57.6 6.9 %collective-permute-start.13 = (f32[32,128]{1,0:T(8,128)S(1)}, f32[32,128]{1,0:T(8,128)S(1)}, u32[]{:S(2)}, u32[]{:S(2)}) collective-permute-start(f32[32,128]{1,0:T(8,128)S(1)} %pad_maximum_fusion.refs_6_), channel_id=1, source_target_pairs={{0,2},{2,0},{4,6},{6,4},{1,3},{3,1},{5,7},{7,5},{8,10},{10,8},{12,... | collective-permute-start | bytes 49160 | tf_op jit(solution)/shard_map/ppermute | solution.py:497

commit v17 on v15

--- a/solution.py
+++ b/solution.py
@@ -377,7 +377,7 @@
 
 def temporal_kernel(frames, spaces, length_ref, task_ref, *refs):
     attended_refs, (gain_ref, own_ref, *other_refs), refs = (
-        refs[: frames - 1],
+        (refs[frames - 2], *refs[: frames - 2]),
         refs[frames - 1 : frames - 1 + 2 * spaces],
         refs[frames - 1 + 2 * spaces :],
     )
@@ -426,7 +426,7 @@
     frames, spaces = len(attended) + 1, (len(upstream) + 1) // 2
     patches = spaces * lanes
     rows = -(-(heads + 1) // 8) * 8
-    operands = [*attended, gain, *upstream]
+    operands = [*attended[1:], attended[0], gain, *upstream]
     block = (heads, spaces, frames, feat, lanes)
     results = pl.pallas_call(
         functools.partial(temporal_kernel, frames, spaces),
@@ -500,7 +500,7 @@
     gain = jnp.broadcast_to(
         product.reshape(own, HEAD_DIM, 1), (own, HEAD_DIM, patches // spaces)
     )
-    attended[1], gain, upstream[0] = lax.optimization_barrier((attended[1], gain, upstream[0]))
+    attended[-2], gain, upstream[0] = lax.optimization_barrier((attended[-2], gain, upstream[0]))
     upstream[0], *kept = fetch(upstream[0], *fields)
     grads, mixed = temporal(lengths, task_ids, attended[1:], upstream, gain)
     for distance in reversed(range(1, frames)):

time: 66.7 us -> 71 us (1.064)
  waiting for transfers between devices: 18.9 us -> 22 us
  starting transfers between devices: 25.1 us -> 26.2 us
    ppermute x16, waiting for transfers between devices: 18.9 us -> 22 us  [swap(): return lax.ppermute(field, axis, [(i, i ^ distance) for i in range(size)])]
    ppermute x16, starting transfers between devices: 25.1 us -> 26.2 us  [swap(): return lax.ppermute(field, axis, [(i, i ^ distance) for i in range(size)])]
  transfers between devices with their start and end apart: 16 -> 16, of which waited for: 5 -> 6; matrix products, arithmetic and copies ran while one was open for 0% -> 0% of each run, Pallas kernels for 19% -> 18%
where the time goes in v17:
time: 71 us; the launch traced here: 70.7 us
  starting transfers between devices  26.2 us (37%)
  waiting for transfers between devices  22 us (31%)
  Pallas kernels  19.4 us (27%)
  between operations  2.1 us (3%)
  local copies, waits for them, and re-layouts  0.92 us (1%)
    ppermute x16, starting transfers between devices, swap(): return lax.ppermute(field, axis, [(i, i ^ distance) for i in range(size)])  26.2 us
    ppermute x16, waiting for transfers between devices, swap(): return lax.ppermute(field, axis, [(i, i ^ distance) for i in range(size)])  22 us
    pallas_call x1, Pallas kernels, forward(): pl.pallas_call(functools.partial(forward_kernel, axis), in_specs=[pl.Bloc...  6.52 us
    pallas_call x3, Pallas kernels, backward(): pl.pallas_call(functools.partial(backward_kernel, axis, distances, gains_...  4.81 us
    pallas_call x1, Pallas kernels, temporal(): pl.pallas_call(functools.partial(temporal_kernel, frames, spaces), in_spe...  3.61 us
    pallas_call x1, Pallas kernels, fetch(): pl.pallas_call(fetch_kernel, in_specs=[pl.BlockSpec(memory_space=pltpu.HB...  1.83 us
  transfers between devices with their start and end apart: 16, of which 6 were waited for; matrix products, arithmetic and copies ran while one was open for 0% of the time, Pallas kernels for 18%

profile of v17, /device:TPU:0, one launch (start us, length us, event | category | flops | bytes accessed | tf_op | source)
XLA Modules:
  0.0 70.7 jit_solution(1081596538517136040)
XLA Ops:
  0.6 1.3 %pack_cotangent.1 = (bf16[2,128,384]{2,1,0:T(8,128)(2,1)S(1)}, bf16[2,128,384]{2,1,0:T(8,128)(2,1)S(1)}, bf16[2,128,384]{2,1,0:T(8,128)(2,1)S(1)}, bf16[2,128,384]{2,1,0:T(8,128)(2,1)S(1)}) custom-call(bf16[128,3072]{1,0:T(8,128)(2,1)} %bitcast.19), custom_call_target="tpu_custom_call" | custom-call | flops 100000000 | tf_op jit(solution)/shard_map/pack_cotangent/pallas_call | solution.py:198
  2.0 5.1 %collective-permute-start.1 = (bf16[2,128,384]{2,1,0:T(8,128)(2,1)S(1)}, bf16[2,128,384]{2,1,0:T(8,128)(2,1)S(1)}, u32[]{:S(2)}, u32[]{:S(2)}) collective-permute-start(bf16[2,128,384]{2,1,0:T(8,128)(2,1)S(1)} %get-tuple-element.56), channel_id=1, source_target_pairs={{0,6},{2,4},{4,2},{6,0},{1,7},{3,5},{5,3},{7,1},{8,14},{10,12},{12... | collective-permute-start | bytes 589832 | tf_op jit(solution)/shard_map/ppermute | solution.py:471
  7.7 6.5 %spatial_forward.1 = (f32[12,256,256]{2,1,0:T(8,128)S(1)}, bf16[3,128,256]{2,1,0:T(8,128)(2,1)S(1)}, bf16[3,128,256]{2,1,0:T(8,128)(2,1)}, bf16[3,128,256]{2,1,0:T(8,128)(2,1)}, bf16[3,128,256]{2,1,0:T(8,128)(2,1)}) custom-call(bf16[256,1536]{1,0:T(8,128)(2,1)} %bitcast.13, bf16[256,1536]{1,0:T(8,128)(2,1)} %bitcast.15, bf16[256,1536]{1,0:T(8,128)(2,1)} %bitcast.17), custom_call_target="tpu_custom_call" | custom-call | flops 600000000 | tf_op jit(solution)/shard_map/spatial_forward/pallas_call | solution.py:76
  14.3 2.3 %collective-permute-start = (bf16[3,128,256]{2,1,0:T(8,128)(2,1)}, bf16[3,128,256]{2,1,0:T(8,128)(2,1)S(1)}, u32[]{:S(2)}, u32[]{:S(2)}) collective-permute-start(bf16[3,128,256]{2,1,0:T(8,128)(2,1)} %get-tuple-element.55), channel_id=1, source_target_pairs={{0,4},{2,6},{4,0},{6,2},{1,5},{3,7},{5,1},{7,3},{8,12},{10,14},{12... | collective-permute-start | bytes 589832 | tf_op jit(solution)/shard_map/ppermute | solution.py:471
  16.6 1.5 %collective-permute-start.4 = (bf16[3,128,256]{2,1,0:T(8,128)(2,1)}, bf16[3,128,256]{2,1,0:T(8,128)(2,1)}, u32[]{:S(2)}, u32[]{:S(2)}) collective-permute-start(bf16[3,128,256]{2,1,0:T(8,128)(2,1)} %get-tuple-element.72), channel_id=1, source_target_pairs={{0,6},{2,4},{4,2},{6,0},{1,7},{3,5},{5,3},{7,1},{8,14},{10,12},{12... | collective-permute-start | bytes 589832 | tf_op jit(solution)/shard_map/ppermute | solution.py:471
  18.1 3.8 %collective-permute-start.5 = (bf16[3,128,256]{2,1,0:T(8,128)(2,1)}, bf16[3,128,256]{2,1,0:T(8,128)(2,1)}, u32[]{:S(2)}, u32[]{:S(2)}) collective-permute-start(bf16[3,128,256]{2,1,0:T(8,128)(2,1)} %get-tuple-element.73), channel_id=1, source_target_pairs={{0,2},{2,0},{4,6},{6,4},{1,3},{3,1},{5,7},{7,5},{8,10},{10,8},{12,... | collective-permute-start | bytes 589832 | tf_op jit(solution)/shard_map/ppermute | solution.py:471
  21.9 11.3 %collective-permute-done.2.refs_1_ = bf16[2,128,384]{2,1,0:T(8,128)(2,1)S(1)} collective-permute-done((bf16[2,128,384]{2,1,0:T(8,128)(2,1)S(1)}, bf16[2,128,384]{2,1,0:T(8,128)(2,1)S(1)}, u32[]{:S(2)}, u32[]{:S(2)}) %collective-permute-start.2) | collective-permute-done | bytes 196640 | tf_op jit(solution)/shard_map/ppermute | solution.py:471
  33.3 1.3 %turn_cotangent.1 = (bf16[6,3,128,128]{3,2,1,0:T(8,128)(2,1)S(1)}, bf16[2,3,128,128]{3,2,1,0:T(8,128)(2,1)}, bf16[2,3,128,128]{3,2,1,0:T(8,128)(2,1)}) custom-call(bf16[2,128,384]{2,1,0:T(8,128)(2,1)S(1)} %collective-permute-done.1.refs_0_, bf16[2,128,384]{2,1,0:T(8,128)(2,1)S(1)} %collective-permute-done.2.refs_1_, ...), custom_call_target="tpu_custom_call" | custom-call | flops 200000000 | tf_op jit(solution)/shard_map/turn_cotangent/pallas_call | solution.py:247
  34.6 0.8 %copy-done = bf16[6,3,128,128]{3,2,1,0:T(8,128)(2,1)} copy-done((bf16[6,3,128,128]{3,2,1,0:T(8,128)(2,1)}, bf16[6,3,128,128]{3,2,1,0:T(8,128)(2,1)S(1)}, u32[]{:S(2)}) %copy-start) | copy-done | bytes 589848
  35.4 1.5 %collective-permute-start.6 = (bf16[2,3,128,128]{3,2,1,0:T(8,128)(2,1)}, bf16[2,3,128,128]{3,2,1,0:T(8,128)(2,1)}, u32[]{:S(2)}, u32[]{:S(2)}) collective-permute-start(bf16[2,3,128,128]{3,2,1,0:T(8,128)(2,1)} %get-tuple-element.76), channel_id=1, source_target_pairs={{0,1},{1,0},{2,3},{3,2},{4,5},{5,4},{6,7},{7,6},{8,9},{9,8},{10,11... | collective-permute-start | bytes 589832 | tf_op jit(solution)/shard_map/ppermute | solution.py:471
  38.9 1.8 %fetch.1 = (bf16[6,3,128,128]{3,2,1,0:T(8,128)(2,1)S(1)}, bf16[256,1536]{1,0:T(8,128)(2,1)S(1)}, bf16[256,1536]{1,0:T(8,128)(2,1)S(1)}, bf16[256,1536]{1,0:T(8,128)(2,1)S(1)}) custom-call(bf16[6,3,128,128]{3,2,1,0:T(8,128)(2,1)} %copy-done, bf16[256,1536]{1,0:T(8,128)(2,1)} %bitcast.14, bf16[256,1536]{1,0:T(8,128)(2,1)} %bitcast.16, bf16[256,1536]{1,0:T(8,128)(2,1)} %bitcast.18), custom_call_target="tpu_custom_call" | custom-call | flops 100000000 | tf_op jit(solution)/shard_map/fetch/pallas_call | solution.py:366
  40.8 1.9 %collective-permute-done.6.refs_5_ = bf16[2,3,128,128]{3,2,1,0:T(8,128)(2,1)} collective-permute-done((bf16[2,3,128,128]{3,2,1,0:T(8,128)(2,1)}, bf16[2,3,128,128]{3,2,1,0:T(8,128)(2,1)}, u32[]{:S(2)}, u32[]{:S(2)}) %collective-permute-start.6) | collective-permute-done | bytes 196640 | tf_op jit(solution)/shard_map/ppermute | solution.py:471
  42.7 2.1 %collective-permute-done.7.refs_6_ = bf16[2,3,128,128]{3,2,1,0:T(8,128)(2,1)} collective-permute-done((bf16[2,3,128,128]{3,2,1,0:T(8,128)(2,1)}, bf16[2,3,128,128]{3,2,1,0:T(8,128)(2,1)}, u32[]{:S(2)}, u32[]{:S(2)}) %collective-permute-start.7) | collective-permute-done | bytes 196640 | tf_op jit(solution)/shard_map/ppermute | solution.py:471
  44.8 3.6 %temporal.1 = (bf16[3,128,256]{2,1,0:T(8,128)(2,1)S(1)}, bf16[3,128,256]{2,1,0:T(8,128)(2,1)S(1)}, bf16[3,128,256]{2,1,0:T(8,128)(2,1)S(1)}, bf16[3,128,256]{2,1,0:T(8,128)(2,1)S(1)}, f32[8,128]{1,0:T(8,128)S(1)}) custom-call(s32[1]{0:T(128)S(6)} %copy.19.length_ref, s32[1]{0:T(128)} %copy.18.task_ref, ...), custom_call_target="tpu_custom_call" | custom-call | flops 400000000 | tf_op jit(solution)/shard_map/temporal/pallas_call | solution.py:431
  48.5 2.3 %collective-permute-start.8 = (bf16[3,128,256]{2,1,0:T(8,128)(2,1)S(1)}, bf16[3,128,256]{2,1,0:T(8,128)(2,1)S(1)}, u32[]{:S(2)}, u32[]{:S(2)}) collective-permute-start(bf16[3,128,256]{2,1,0:T(8,128)(2,1)S(1)} %get-tuple-element.78), channel_id=1, source_target_pairs={{0,6},{2,4},{4,2},{6,0},{1,7},{3,5},{5,3},{7,1},{8,14},{10,12},{12... | collective-permute-start | bytes 589832 | tf_op jit(solution)/shard_map/ppermute | solution.py:471
  50.9 2.1 %collective-permute-start.12 = (bf16[3,128,256]{2,1,0:T(8,128)(2,1)S(1)}, bf16[3,128,256]{2,1,0:T(8,128)(2,1)S(1)}, u32[]{:S(2)}, u32[]{:S(2)}) collective-permute-start(bf16[3,128,256]{2,1,0:T(8,128)(2,1)S(1)} %get-tuple-element.87), channel_id=1, source_target_pairs={{0,2},{2,0},{4,6},{6,4},{1,3},{3,1},{5,7},{7,5},{8,10},{10,8},{12,... | collective-permute-start | bytes 589832 | tf_op jit(solution)/shard_map/ppermute | solution.py:471
  53.0 1.5 %collective-permute-start.11 = (f32[16,128]{1,0:T(8,128)S(1)}, f32[16,128]{1,0:T(8,128)S(1)}, u32[]{:S(2)}, u32[]{:S(2)}) collective-permute-start(f32[16,128]{1,0:T(8,128)S(1)} %pad_maximum_fusion.1), channel_id=1, source_target_pairs={{0,16},{8,24},{16,0},{24,8},{1,17},{9,25},{17,1},{25,9},{2,18},{10... | collective-permute-start | bytes 24584 | tf_op jit(solution)/shard_map/ppermute | solution.py:471
  54.5 1.4 %spatial_backward.3 = (bf16[256,1536]{1,0:T(8,128)(2,1)}, bf16[256,1536]{1,0:T(8,128)(2,1)}) custom-call(bf16[256,1536]{1,0:T(8,128)(2,1)S(1)} %get-tuple-element.68.refs_0_, bf16[256,1536]{1,0:T(8,128)(2,1)S(1)} %get-tuple-element.69.refs_1_, bf16[256,1536]{1,0:T(8,128)(2,1)S(1)} %get-tuple-element.70.refs_2_, ...), custom_call_target="tpu_custom_call" | custom-call | flops 200000000 | tf_op jit(solution)/shard_map/spatial_backward/pallas_call | solution.py:159
  55.9 0.7 %collective-permute-done.11 = f32[16,128]{1,0:T(8,128)S(1)} collective-permute-done((f32[16,128]{1,0:T(8,128)S(1)}, f32[16,128]{1,0:T(8,128)S(1)}, u32[]{:S(2)}, u32[]{:S(2)}) %collective-permute-start.11) | collective-permute-done | bytes 8224 | tf_op jit(solution)/shard_map/ppermute | solution.py:471
  56.6 2.3 %collective-permute-start.15 = (f32[32,128]{1,0:T(8,128)S(1)}, f32[32,128]{1,0:T(8,128)S(1)}, u32[]{:S(2)}, u32[]{:S(2)}) collective-permute-start(f32[32,128]{1,0:T(8,128)S(1)} %pad_maximum_fusion.refs_6_), channel_id=1, source_target_pairs={{0,6},{2,4},{4,2},{6,0},{1,7},{3,5},{5,3},{7,1},{8,14},{10,12},{12... | collective-permute-start | bytes 49160 | tf_op jit(solution)/shard_map/ppermute | solution.py:471
  58.9 5.6 %collective-permute-done.12.refs_4_ = bf16[3,128,256]{2,1,0:T(8,128)(2,1)S(1)} collective-permute-done((bf16[3,128,256]{2,1,0:T(8,128)(2,1)S(1)}, bf16[3,128,256]{2,1,0:T(8,128)(2,1)S(1)}, u32[]{:S(2)}, u32[]{:S(2)}) %collective-permute-start.12) | collective-permute-done | bytes 196640 | tf_op jit(solution)/shard_map/ppermute | solution.py:471
  64.5 2.5 %collective-permute-start.13 = (f32[32,128]{1,0:T(8,128)S(1)}, f32[32,128]{1,0:T(8,128)S(1)}, u32[]{:S(2)}, u32[]{:S(2)}) collective-permute-start(f32[32,128]{1,0:T(8,128)S(1)} %pad_maximum_fusion.refs_6_), channel_id=1, source_target_pairs={{0,2},{2,0},{4,6},{6,4},{1,3},{3,1},{5,7},{7,5},{8,10},{10,8},{12,... | collective-permute-start | bytes 49160 | tf_op jit(solution)/shard_map/ppermute | solution.py:471
  67.0 1.4 %spatial_backward.4 = (bf16[256,1536]{1,0:T(8,128)(2,1)}, bf16[256,1536]{1,0:T(8,128)(2,1)}) custom-call(bf16[256,1536]{1,0:T(8,128)(2,1)S(1)} %get-tuple-element.68.refs_0_, bf16[256,1536]{1,0:T(8,128)(2,1)S(1)} %get-tuple-element.69.refs_1_, bf16[256,1536]{1,0:T(8,128)(2,1)S(1)} %get-tuple-element.70.refs_2_, ...), custom_call_target="tpu_custom_call", output_to_operand_aliasing={{0}: (5, {}), {1}: (6, {})} | custom-call | flops 200000000 | tf_op jit(solution)/shard_map/spatial_backward/pallas_call | solution.py:159
  68.7 2.0 %spatial_backward.5 = (bf16[256,1536]{1,0:T(8,128)(2,1)}, bf16[256,1536]{1,0:T(8,128)(2,1)}, f32[2,16,1536]{2,1,0:T(8,128)}) custom-call(bf16[256,1536]{1,0:T(8,128)(2,1)S(1)} %get-tuple-element.68.refs_0_, bf16[256,1536]{1,0:T(8,128)(2,1)S(1)} %get-tuple-element.69.refs_1_, ...), custom_call_target="tpu_custom_call", output_to_operand_aliasing={{0}: (11, {}), {1}: (12, {})} | custom-call | flops 200000000 | tf_op jit(solution)/shard_map/spatial_backward/pallas_call | solution.py:159
  (24 shorter events, 1.7 us)
Async XLA Ops:
  0.6 38.1 %copy-start.1 = (f32[2,16,1536]{2,1,0:T(8,128)S(1)}, f32[2,16,1536]{2,1,0:T(8,128)}, u32[]{:S(2)}) copy-start(f32[2,16,1536]{2,1,0:T(8,128)} %refs_10_.1) | copy-start | bytes 589828
  2.0 16.2 %collective-permute-start.1 = (bf16[2,128,384]{2,1,0:T(8,128)(2,1)S(1)}, bf16[2,128,384]{2,1,0:T(8,128)(2,1)S(1)}, u32[]{:S(2)}, u32[]{:S(2)}) collective-permute-start(bf16[2,128,384]{2,1,0:T(8,128)(2,1)S(1)} %get-tuple-element.56), channel_id=1, source_target_pairs={{0,6},{2,4},{4,2},{6,0},{1,7},{3,5},{5,3},{7,1},{8,14},{10,12},{12... | collective-permute-start | bytes 589832 | tf_op jit(solution)/shard_map/ppermute | solution.py:471
  7.1 26.2 %collective-permute-start.2 = (bf16[2,128,384]{2,1,0:T(8,128)(2,1)S(1)}, bf16[2,128,384]{2,1,0:T(8,128)(2,1)S(1)}, u32[]{:S(2)}, u32[]{:S(2)}) collective-permute-start(bf16[2,128,384]{2,1,0:T(8,128)(2,1)S(1)} %get-tuple-element.57), channel_id=1, source_target_pairs={{0,4},{2,6},{4,0},{6,2},{1,5},{3,7},{5,1},{7,3},{8,12},{10,14},{12... | collective-permute-start | bytes 589832 | tf_op jit(solution)/shard_map/ppermute | solution.py:471
  7.1 26.2 %collective-permute-start.3 = (bf16[2,128,384]{2,1,0:T(8,128)(2,1)S(1)}, bf16[2,128,384]{2,1,0:T(8,128)(2,1)S(1)}, u32[]{:S(2)}, u32[]{:S(2)}) collective-permute-start(bf16[2,128,384]{2,1,0:T(8,128)(2,1)S(1)} %get-tuple-element.58), channel_id=1, source_target_pairs={{0,2},{2,0},{4,6},{6,4},{1,3},{3,1},{5,7},{7,5},{8,10},{10,8},{12,... | collective-permute-start | bytes 589832 | tf_op jit(solution)/shard_map/ppermute | solution.py:471
  14.3 24.6 %collective-permute-start = (bf16[3,128,256]{2,1,0:T(8,128)(2,1)}, bf16[3,128,256]{2,1,0:T(8,128)(2,1)S(1)}, u32[]{:S(2)}, u32[]{:S(2)}) collective-permute-start(bf16[3,128,256]{2,1,0:T(8,128)(2,1)} %get-tuple-element.55), channel_id=1, source_target_pairs={{0,4},{2,6},{4,0},{6,2},{1,5},{3,7},{5,1},{7,3},{8,12},{10,14},{12... | collective-permute-start | bytes 589832 | tf_op jit(solution)/shard_map/ppermute | solution.py:471
  16.6 24.2 %collective-permute-start.4 = (bf16[3,128,256]{2,1,0:T(8,128)(2,1)}, bf16[3,128,256]{2,1,0:T(8,128)(2,1)}, u32[]{:S(2)}, u32[]{:S(2)}) collective-permute-start(bf16[3,128,256]{2,1,0:T(8,128)(2,1)} %get-tuple-element.72), channel_id=1, source_target_pairs={{0,6},{2,4},{4,2},{6,0},{1,7},{3,5},{5,3},{7,1},{8,14},{10,12},{12... | collective-permute-start | bytes 589832 | tf_op jit(solution)/shard_map/ppermute | solution.py:471
  18.1 22.6 %collective-permute-start.5 = (bf16[3,128,256]{2,1,0:T(8,128)(2,1)}, bf16[3,128,256]{2,1,0:T(8,128)(2,1)}, u32[]{:S(2)}, u32[]{:S(2)}) collective-permute-start(bf16[3,128,256]{2,1,0:T(8,128)(2,1)} %get-tuple-element.73), channel_id=1, source_target_pairs={{0,2},{2,0},{4,6},{6,4},{1,3},{3,1},{5,7},{7,5},{8,10},{10,8},{12,... | collective-permute-start | bytes 589832 | tf_op jit(solution)/shard_map/ppermute | solution.py:471
  34.6 0.8 %copy-start = (bf16[6,3,128,128]{3,2,1,0:T(8,128)(2,1)}, bf16[6,3,128,128]{3,2,1,0:T(8,128)(2,1)S(1)}, u32[]{:S(2)}) copy-start(bf16[6,3,128,128]{3,2,1,0:T(8,128)(2,1)S(1)} %get-tuple-element.67.refs_0_) | copy-start | bytes 1769476
  35.4 7.4 %collective-permute-start.6 = (bf16[2,3,128,128]{3,2,1,0:T(8,128)(2,1)}, bf16[2,3,128,128]{3,2,1,0:T(8,128)(2,1)}, u32[]{:S(2)}, u32[]{:S(2)}) collective-permute-start(bf16[2,3,128,128]{3,2,1,0:T(8,128)(2,1)} %get-tuple-element.76), channel_id=1, source_target_pairs={{0,1},{1,0},{2,3},{3,2},{4,5},{5,4},{6,7},{7,6},{8,9},{9,8},{10,11... | collective-permute-start | bytes 589832 | tf_op jit(solution)/shard_map/ppermute | solution.py:471
  36.9 8.0 %collective-permute-start.7 = (bf16[2,3,128,128]{3,2,1,0:T(8,128)(2,1)}, bf16[2,3,128,128]{3,2,1,0:T(8,128)(2,1)}, u32[]{:S(2)}, u32[]{:S(2)}) collective-permute-start(bf16[2,3,128,128]{3,2,1,0:T(8,128)(2,1)} %get-tuple-element.77), channel_id=1, source_target_pairs={{0,1},{1,0},{2,3},{3,2},{4,5},{5,4},{6,7},{7,6},{8,9},{9,8},{10,11... | collective-permute-start | bytes 589832 | tf_op jit(solution)/shard_map/ppermute | solution.py:471
  48.5 4.5 %collective-permute-start.10 = (f32[8,128]{1,0:T(8,128)S(1)}, f32[8,128]{1,0:T(8,128)S(1)}, u32[]{:S(2)}, u32[]{:S(2)}) collective-permute-start(f32[8,128]{1,0:T(8,128)S(1)} %get-tuple-element.80), channel_id=1, source_target_pairs={{0,8},{8,0},{16,24},{24,16},{1,9},{9,1},{17,25},{25,17},{2,10},{10... | collective-permute-start | bytes 12296 | tf_op jit(solution)/shard_map/ppermute | solution.py:471
  48.5 19.9 %collective-permute-start.8 = (bf16[3,128,256]{2,1,0:T(8,128)(2,1)S(1)}, bf16[3,128,256]{2,1,0:T(8,128)(2,1)S(1)}, u32[]{:S(2)}, u32[]{:S(2)}) collective-permute-start(bf16[3,128,256]{2,1,0:T(8,128)(2,1)S(1)} %get-tuple-element.78), channel_id=1, source_target_pairs={{0,6},{2,4},{4,2},{6,0},{1,7},{3,5},{5,3},{7,1},{8,14},{10,12},{12... | collective-permute-start | bytes 589832 | tf_op jit(solution)/shard_map/ppermute | solution.py:471
  50.9 17.6 %collective-permute-start.9 = (bf16[3,128,256]{2,1,0:T(8,128)(2,1)S(1)}, bf16[3,128,256]{2,1,0:T(8,128)(2,1)S(1)}, u32[]{:S(2)}, u32[]{:S(2)}) collective-permute-start(bf16[3,128,256]{2,1,0:T(8,128)(2,1)S(1)} %get-tuple-element.79), channel_id=1, source_target_pairs={{0,4},{2,6},{4,0},{6,2},{1,5},{3,7},{5,1},{7,3},{8,12},{10,14},{12... | collective-permute-start | bytes 589832 | tf_op jit(solution)/shard_map/ppermute | solution.py:471
  50.9 13.6 %collective-permute-start.12 = (bf16[3,128,256]{2,1,0:T(8,128)(2,1)S(1)}, bf16[3,128,256]{2,1,0:T(8,128)(2,1)S(1)}, u32[]{:S(2)}, u32[]{:S(2)}) collective-permute-start(bf16[3,128,256]{2,1,0:T(8,128)(2,1)S(1)} %get-tuple-element.87), channel_id=1, source_target_pairs={{0,2},{2,0},{4,6},{6,4},{1,3},{3,1},{5,7},{7,5},{8,10},{10,8},{12,... | collective-permute-start | bytes 589832 | tf_op jit(solution)/shard_map/ppermute | solution.py:471
  53.0 3.7 %collective-permute-start.11 = (f32[16,128]{1,0:T(8,128)S(1)}, f32[16,128]{1,0:T(8,128)S(1)}, u32[]{:S(2)}, u32[]{:S(2)}) collective-permute-start(f32[16,128]{1,0:T(8,128)S(1)} %pad_maximum_fusion.1), channel_id=1, source_target_pairs={{0,16},{8,24},{16,0},{24,8},{1,17},{9,25},{17,1},{25,9},{2,18},{10... | collective-permute-start | bytes 24584 | tf_op jit(solution)/shard_map/ppermute | solution.py:471
  56.6 11.8 %collective-permute-start.15 = (f32[32,128]{1,0:T(8,128)S(1)}, f32[32,128]{1,0:T(8,128)S(1)}, u32[]{:S(2)}, u32[]{:S(2)}) collective-permute-start(f32[32,128]{1,0:T(8,128)S(1)} %pad_maximum_fusion.refs_6_), channel_id=1, source_target_pairs={{0,6},{2,4},{4,2},{6,0},{1,7},{3,5},{5,3},{7,1},{8,14},{10,12},{12... | collective-permute-start | bytes 49160 | tf_op jit(solution)/shard_map/ppermute | solution.py:471
  58.9 9.5 %collective-permute-start.14 = (f32[32,128]{1,0:T(8,128)S(1)}, f32[32,128]{1,0:T(8,128)S(1)}, u32[]{:S(2)}, u32[]{:S(2)}) collective-permute-start(f32[32,128]{1,0:T(8,128)S(1)} %pad_maximum_fusion.refs_6_), channel_id=1, source_target_pairs={{0,4},{2,6},{4,0},{6,2},{1,5},{3,7},{5,1},{7,3},{8,12},{10,14},{12... | collective-permute-start | bytes 49160 | tf_op jit(solution)/shard_map/ppermute | solution.py:471
  64.5 4.2 %collective-permute-start.13 = (f32[32,128]{1,0:T(8,128)S(1)}, f32[32,128]{1,0:T(8,128)S(1)}, u32[]{:S(2)}, u32[]{:S(2)}) collective-permute-start(f32[32,128]{1,0:T(8,128)S(1)} %pad_maximum_fusion.refs_6_), channel_id=1, source_target_pairs={{0,2},{2,0},{4,6},{6,4},{1,3},{3,1},{5,7},{7,5},{8,10},{10,8},{12,... | collective-permute-start | bytes 49160 | tf_op jit(solution)/shard_map/ppermute | solution.py:471

commit v18 on v15

--- a/solution.py
+++ b/solution.py
@@ -261,91 +261,83 @@
     )(*reversed(pieces), plane)
 
 
-def temporal_part(length, load_attended, load_upstream, load_gain, fields, ups, normed, grad_ref):
-    frames, feat, lanes = grad_ref.shape
-    half = GROUP // 2
+HALF = GROUP // 2
+
+
+def total(piece):
+    return jnp.broadcast_to(jnp.sum(piece, axis=0, keepdims=True), piece.shape)
+
+
+def groups(feat):
+    return [pl.ds(start, HALF) for start in range(0, feat, HALF)]
+
+
+def normalize(field_ref, normed_ref):
+    feat = field_ref.shape[0]
+    squares = functools.reduce(
+        jnp.add, [field_ref[rows, :] * field_ref[rows, :] for rows in groups(feat)]
+    )
+    inverse = lax.rsqrt(total(squares) * (1.0 / feat) + 1e-06)
+    for rows in groups(feat):
+        normed_ref[rows, :] = field_ref[rows, :] * inverse
+    return inverse
+
+
+def weigh(length, raw, grad, frames, feat):
     score_scale = feat ** (-0.5)
-    pairs = [(t, u) for t in range(frames) for u in range(t + 1)]
     every = range(frames)
+    pairs = [(t, u) for t in every for u in range(t + 1)]
     valid = [jnp.where(t < length, 1.0, 0.0).astype(jnp.float32) for t in every]
     bias = [jnp.where(u < length, 0.0, -1e30).astype(jnp.float32) for u in every]
-
-    def total(piece):
-        return jnp.broadcast_to(jnp.sum(piece, axis=0, keepdims=True), (half, lanes))
-
-    squares = [jnp.zeros((half, lanes), jnp.float32) for _ in every]
-    for group in range(feat // GROUP):
-        rows = pl.ds(group * GROUP, GROUP)
-        for t in every:
-            field = load_attended(t, rows).astype(jnp.float32)
-            fields[t, rows, :] = field
-            ups[t, rows, :] = load_upstream(t, rows).astype(jnp.float32)
-            low, high = field[:half], field[half:]
-            squares[t] = squares[t] + (low * low + high * high)
-    inverse = [lax.rsqrt(total(squares[t]) * (1.0 / feat) + 1e-06) for t in every]
-
-    raw = {pair: jnp.zeros((half, lanes), jnp.float32) for pair in pairs}
-    grad = {pair: jnp.zeros((half, lanes), jnp.float32) for pair in pairs}
-    for group in range(feat // half):
-        rows = pl.ds(group * half, half)
-        gain = load_gain(rows)
-        here = [fields[t, rows, :] for t in every]
-        above = [ups[t, rows, :] for t in every]
-        scaled = [here[t] * inverse[t] for t in every]
-        gained = [scaled[t] * gain for t in every]
-        for t in every:
-            normed[t, rows, :] = scaled[t]
-        for t, u in pairs:
-            raw[t, u] = raw[t, u] + gained[t] * scaled[u]
-            grad[t, u] = grad[t, u] + above[t] * here[u]
-
     value_part, score_part = {}, {}
     for t in every:
         seen = range(t + 1)
-        for u in seen:
-            raw[t, u] = total(raw[t, u])
-            grad[t, u] = total(grad[t, u]) * valid[t]
+        masked = [grad[t, u] * valid[t] for u in seen]
         scores = [raw[t, u] * score_scale + bias[u] for u in seen]
         largest = functools.reduce(jnp.maximum, scores)
         raised = [jnp.exp(score - largest) for score in scores]
         over = 1.0 / functools.reduce(jnp.add, raised)
         weights = [piece * over for piece in raised]
-        mean_grad = functools.reduce(jnp.add, [weights[u] * grad[t, u] for u in seen])
+        mean_grad = functools.reduce(jnp.add, [weights[u] * masked[u] for u in seen])
         for u in seen:
             rounded = weights[u].astype(jnp.bfloat16).astype(jnp.float32)
             value_part[t, u] = (rounded + (1.0 if u == t else 0.0)) * valid[t]
-            score_part[t, u] = weights[u] * (grad[t, u] - mean_grad) * score_scale
-
+            score_part[t, u] = weights[u] * (masked[u] - mean_grad) * score_scale
     both = {(t, u): score_part[t, u] * (2.0 if t == u else 1.0) for t, u in pairs}
     both.update({(u, t): both[t, u] for t, u in pairs})
-    raw.update({(u, t): raw[t, u] for t, u in pairs})
+    raw = {**raw, **{(u, t): raw[t, u] for t, u in pairs}}
     mean_part = [
         functools.reduce(jnp.add, [both[u, v] * raw[u, v] for v in every]) * (1.0 / feat)
         for u in every
     ]
-
+    return value_part, both, mean_part
+
+
+def gradients(parts, inverse, normed_ref, ups_ref, load_gain, grad_ref):
+    value_part, both, mean_part = parts
+    frames, feat, _ = grad_ref.shape
+    every = range(frames)
     all_mixed = []
-    for group in range(feat // GROUP):
+    for start in range(0, feat, GROUP):
         outs = [[] for _ in every]
-        for side in range(2):
-            rows = pl.ds(group * GROUP + side * half, half)
+        for rows in (pl.ds(start, HALF), pl.ds(start + HALF, HALF)):
             gain = load_gain(rows)
-            scaled = [normed[t, rows, :] for t in every]
-            above = [ups[t, rows, :] for t in every]
-            mixed = jnp.zeros((half, lanes), jnp.float32)
+            scaled = [normed_ref[t, rows, :] for t in every]
+            above = [ups_ref[t, rows, :] for t in every]
+            mixed = []
             for u in every:
                 crossed = functools.reduce(jnp.add, [both[u, v] * scaled[v] for v in every])
-                mixed = mixed + crossed * scaled[u]
+                mixed.append(crossed * scaled[u])
                 from_norm = inverse[u] * (gain * crossed - scaled[u] * mean_part[u])
                 direct = functools.reduce(
                     jnp.add, [value_part[t, u] * above[t] for t in range(u, frames)]
                 )
                 outs[u].append(direct + from_norm)
-            all_mixed.append(mixed)
+            all_mixed.append(functools.reduce(jnp.add, mixed))
         for u in every:
-            grad_ref[u, pl.ds(group * GROUP, GROUP), :] = jnp.concatenate(
-                outs[u], axis=0
-            ).astype(jnp.bfloat16)
+            grad_ref[u, pl.ds(start, GROUP), :] = jnp.concatenate(outs[u], axis=0).astype(
+                jnp.bfloat16
+            )
     return jnp.concatenate(all_mixed, axis=0)
 
 
@@ -370,79 +362,193 @@
         out_shape=[jax.ShapeDtypeStruct(field.shape, field.dtype) for field in fields],
         scratch_shapes=[pltpu.SemaphoreType.DMA((len(fields),))],
         compiler_params=params(0),
-        cost_estimate=cost(1),
+        cost_estimate=cost(0),
         name="fetch",
     )(*[in_hbm(field) for field in fields])
 
 
-def temporal_kernel(frames, spaces, length_ref, task_ref, *refs):
-    attended_refs, (gain_ref, own_ref, *other_refs), refs = (
-        refs[: frames - 1],
-        refs[frames - 1 : frames - 1 + 2 * spaces],
-        refs[frames - 1 + 2 * spaces :],
-    )
-    grad_refs, (mixed_ref, attended, grads, wide) = refs[:frames], refs[frames:]
-    heads, lanes = own_ref.shape[1], own_ref.shape[3]
+def order(frame, other):
+    return jnp.maximum(frame, other), jnp.minimum(frame, other)
+
+
+def early_kernel(frames, spaces, *refs):
+    last = frames - 1
+    attended_refs, (gain_ref, own_ref), outs = refs[: last - 1], refs[last - 1 : -5], refs[-5:]
+    ups, fields, normed, sums, inverse = outs
+    heads, feat, lanes = own_ref.shape[1:]
+    mine = [partner("tm", distance) for distance in range(last)]
+    for head in range(heads):
+        for space in range(spaces):
+            block = head * spaces + space
+            here = pl.ds(pl.multiple_of(partner("space", space) * lanes, lanes), lanes)
+            if space == 0:
+                ups[head] = own_ref[:frames, head].astype(jnp.float32)
+            for distance in range(last):
+                if distance == 0:
+                    field = own_ref[frames + space, head]
+                else:
+                    field = attended_refs[distance - 1][head, :, here]
+                fields[block, distance] = field.astype(jnp.float32)
+                inverse[block, mine[distance]] = normalize(
+                    fields.at[block, distance], normed.at[block, distance]
+                )
+            pairs = [(x, y) for x in range(last) for y in range(x + 1)]
+            raw = {pair: jnp.zeros((HALF, lanes), jnp.float32) for pair in pairs}
+            grad = dict(raw)
+            for rows in groups(feat):
+                gain = gain_ref[head, rows, :]
+                scaled = [normed[block, distance, rows, :] for distance in range(last)]
+                gained = [piece * gain for piece in scaled]
+                for x, y in pairs:
+                    raw[x, y] = raw[x, y] + gained[x] * scaled[y]
+                    if space == 0:
+                        later, _ = order(mine[x], mine[y])
+                        lower = jnp.where(mine[x] < mine[y], x, y)
+                        product = ups[head, later, rows, :] * fields[block, lower, rows, :]
+                        grad[x, y] = grad[x, y] + product
+            for x, y in pairs:
+                later, earlier = order(mine[x], mine[y])
+                sums[block, 0, later * frames + earlier] = total(raw[x, y])
+                if space == 0:
+                    sums[block, 1, later * frames + earlier] = total(grad[x, y])
+
+
+def late_kernel(frames, spaces, length_ref, task_ref, *refs):
+    last = frames - 1
+    (attended_ref, gain_ref, own_ups, fields, normed, sums, inverse), refs = refs[:7], refs[7:]
+    other_refs, refs = refs[: 2 * spaces - 2], refs[2 * spaces - 2 :]
+    grad_refs, (mixed_ref, own_field, own_normed, whole, table, inverses, grads, other_ups) = (
+        refs[:frames],
+        refs[frames:],
+    )
+    heads, feat, _ = attended_ref.shape
+    lanes = own_ups.shape[-1]
     half = frames // 2
+    mine = [partner("tm", distance) for distance in range(frames)]
     mixed_ref[...] = jnp.full(mixed_ref.shape, task_ref[0].astype(jnp.float32))
-
-    def load_upstream(space, head, t, rows):
-        if space == 0:
-            return own_ref[t, head, rows, :]
-        return other_refs[2 * space - 2 + t // half][t % half, head, rows, :]
-
-    places = [
-        pl.ds(pl.multiple_of(partner("space", space) * lanes, lanes), lanes)
-        for space in range(spaces)
-    ]
     for head in range(heads):
-        for space, here in enumerate(places):
-            attended[head, space, partner("tm", 0)] = own_ref[frames + space, head]
-            for distance, ref in enumerate(attended_refs):
-                attended[head, space, partner("tm", distance + 1)] = ref[head, :, here]
-        mixed = [
-            temporal_part(
+        mixed = []
+        for space in range(spaces):
+            block = head * spaces + space
+            here = pl.ds(pl.multiple_of(partner("space", space) * lanes, lanes), lanes)
+            field_ref, normed_ref = own_field.at[block], own_normed.at[block]
+            field_ref[...] = attended_ref[head, :, here].astype(jnp.float32)
+            table[block] = sums[block]
+            inverses[block] = inverse[block]
+            inverses[block, mine[last]] = normalize(field_ref, normed_ref)
+            for distance in range(last):
+                whole[block, mine[distance]] = normed[block, distance]
+            whole[block, mine[last]] = normed_ref[...]
+            if space == 0:
+                ups = own_ups.at[head]
+            else:
+                ups = other_ups.at[block]
+                for t in range(frames):
+                    upstream = other_refs[2 * space - 2 + t // half][t % half, head]
+                    ups[t] = upstream.astype(jnp.float32)
+            near = [(x, y) for x in range(last) for y in range(x + 1)] if space else []
+            nearer = {pair: jnp.zeros((HALF, lanes), jnp.float32) for pair in near}
+            raw = [jnp.zeros((HALF, lanes), jnp.float32) for _ in range(frames)]
+            grad = list(raw)
+            for rows in groups(feat):
+                for x, y in near:
+                    later, _ = order(mine[x], mine[y])
+                    lower = jnp.where(mine[x] < mine[y], x, y)
+                    nearer[x, y] = nearer[x, y] + ups[later, rows, :] * fields[block, lower, rows, :]
+                field, scaled = field_ref[rows, :], normed_ref[rows, :]
+                gained = scaled * gain_ref[head, rows, :]
+                for distance in range(frames):
+                    later, _ = order(mine[last], mine[distance])
+                    if distance < last:
+                        other = normed[block, distance, rows, :]
+                        lower = jnp.where(
+                            mine[last] < mine[distance], field, fields[block, distance, rows, :]
+                        )
+                    else:
+                        other, lower = scaled, field
+                    raw[distance] = raw[distance] + gained * other
+                    grad[distance] = grad[distance] + ups[later, rows, :] * lower
+            for distance in range(frames):
+                later, earlier = order(mine[last], mine[distance])
+                table[block, 0, later * frames + earlier] = total(raw[distance])
+                table[block, 1, later * frames + earlier] = total(grad[distance])
+            for x, y in near:
+                later, earlier = order(mine[x], mine[y])
+                table[block, 1, later * frames + earlier] = total(nearer[x, y])
+            pairs = [(t, u) for t in range(frames) for u in range(t + 1)]
+            parts = weigh(
                 length_ref[0],
-                lambda t, rows: attended[head, space, t, rows, :],
-                functools.partial(load_upstream, space, head),
-                lambda rows: gain_ref[head, rows, :],
-                wide.at[head % 2, space, 0],
-                wide.at[head % 2, space, 1],
-                wide.at[head % 2, space, 2],
-                grads.at[head, space],
+                {(t, u): table[block, 0, t * frames + u] for t, u in pairs},
+                {(t, u): table[block, 1, t * frames + u] for t, u in pairs},
+                frames,
+                feat,
             )
-            for space in range(spaces)
-        ]
+            mixed.append(
+                gradients(
+                    parts,
+                    [inverses[block, t] for t in range(frames)],
+                    whole.at[block],
+                    ups,
+                    lambda rows: gain_ref[head, rows, :],
+                    grads.at[block],
+                )
+            )
+            for distance, ref in enumerate(grad_refs):
+                ref[head, :, here] = grads[block, mine[distance]]
         summed = functools.reduce(jnp.add, mixed)
         mixed_ref[pl.ds(head, 1), :] = jnp.sum(summed.T, axis=0, keepdims=True) * 0.5
-        for distance, ref in enumerate(grad_refs):
-            frame = partner("tm", distance)
-            for space, here in enumerate(places):
-                ref[head, :, here] = grads[head, space, frame]
-
-
-def temporal(lengths, task_ids, attended, upstream, gain):
-    _, heads, feat, lanes = upstream[0].shape
-    frames, spaces = len(attended) + 1, (len(upstream) + 1) // 2
-    patches = spaces * lanes
+
+
+def temporal_early(attended, upstream, gain):
+    planes, heads, feat, lanes = upstream.shape
+    frames = len(attended) + 2
+    spaces = planes - frames
+    blocks = heads * spaces
+    operands = [*attended, gain, upstream]
+    shapes = [
+        (heads, frames, feat, lanes),
+        (blocks, frames - 1, feat, lanes),
+        (blocks, frames - 1, feat, lanes),
+        (blocks, 2, frames * frames, HALF, lanes),
+        (blocks, frames, HALF, lanes),
+    ]
+    return pl.pallas_call(
+        functools.partial(early_kernel, frames, spaces),
+        in_specs=[pl.BlockSpec(memory_space=pltpu.VMEM)] * len(operands),
+        out_specs=[pl.BlockSpec(memory_space=pltpu.VMEM)] * len(shapes),
+        out_shape=[jax.ShapeDtypeStruct(shape, jnp.float32) for shape in shapes],
+        compiler_params=params(spaces * lanes),
+        cost_estimate=cost(0),
+        name="temporal_early",
+    )(*operands)
+
+
+def temporal_late(lengths, task_ids, attended, upstream, gain, early):
+    heads, frames, feat, lanes = early[0].shape
+    blocks, patches = early[1].shape[0], attended.shape[2]
+    spaces = blocks // heads
     rows = -(-(heads + 1) // 8) * 8
-    operands = [*attended, gain, *upstream]
-    block = (heads, spaces, frames, feat, lanes)
+    operands = [attended, gain, *early, *upstream]
+    block = (blocks, feat, lanes)
     results = pl.pallas_call(
-        functools.partial(temporal_kernel, frames, spaces),
+        functools.partial(late_kernel, frames, spaces),
         in_specs=[pl.BlockSpec(memory_space=pltpu.SMEM)] * 2
         + [pl.BlockSpec(memory_space=pltpu.VMEM)] * len(operands),
         out_specs=[pl.BlockSpec(memory_space=pltpu.VMEM)] * (frames + 1),
         scratch_shapes=[
-            pltpu.VMEM(block, jnp.bfloat16),
-            pltpu.VMEM(block, jnp.bfloat16),
-            pltpu.VMEM((2, spaces, 3, frames, feat, lanes), jnp.float32),
+            pltpu.VMEM(block, jnp.float32),
+            pltpu.VMEM(block, jnp.float32),
+            pltpu.VMEM((blocks, frames, feat, lanes), jnp.float32),
+            pltpu.VMEM(early[3].shape, jnp.float32),
+            pltpu.VMEM(early[4].shape, jnp.float32),
+            pltpu.VMEM((blocks, frames, feat, lanes), jnp.bfloat16),
+            pltpu.VMEM((blocks, frames, feat, lanes), jnp.float32),
         ],
         out_shape=[jax.ShapeDtypeStruct((heads, feat, patches), jnp.bfloat16)] * frames
         + [jax.ShapeDtypeStruct((rows, feat), jnp.float32)],
         compiler_params=params(patches),
         cost_estimate=cost(4),
-        name="temporal",
+        name="temporal_late",
     )(lengths, task_ids, *operands)
     return list(results[:frames]), results[frames]
 
@@ -502,15 +608,17 @@
     )
     attended[1], gain, upstream[0] = lax.optimization_barrier((attended[1], gain, upstream[0]))
     upstream[0], *kept = fetch(upstream[0], *fields)
-    grads, mixed = temporal(lengths, task_ids, attended[1:], upstream, gain)
-    for distance in reversed(range(1, frames)):
+    early = temporal_early(attended[1:-1], upstream[0], gain)
+    grads, mixed = temporal_late(lengths, task_ids, attended[-1], upstream[1:], gain, early)
+    for distance in reversed(range(2, frames)):
         grads[distance] = swap(grads[distance], "tm", frames, distance)
     here = grads[0]
     for bit in range(clips.bit_length() - 1):
         other = swap(mixed, "dp", clips, 1 << bit)
         if bit == 0:
-            here, other = lax.optimization_barrier((here, other))
+            here, grads[1], other = lax.optimization_barrier((here, grads[1], other))
         mixed = jnp.concatenate([mixed, other], axis=0)
+    grads[1] = swap(grads[1], "tm", frames, 1)
     results = backward("tm", kept, weights, [here], [0])
     mixed, results = lax.optimization_barrier((mixed, results))
     near, grads[1] = lax.optimization_barrier((mixed, grads[1]))
@@ -632,7 +740,7 @@
     def local(query_heads, *others):
         heads = query_heads.shape[3] // HEAD_DIM
         powers = all(size & (size - 1) == 0 for size in (clips, frames, spaces))
-        if powers and 2 <= frames <= 4 and heads % frames == 0:
+        if powers and frames == 4 and heads % frames == 0:
             return split_by_heads(query_heads, *others, clips, frames, spaces)
         return split_by_patches(query_heads, *others)
 

time: 66.7 us -> 67.7 us (1.015)
  Pallas kernels: 19.4 us -> 20.5 us
  starting transfers between devices: 25.1 us -> 24.4 us
    pallas_call x1 -> x2, Pallas kernels: 3.62 us -> 4.75 us  [the longest x1 3.21 us: temporal_late(): pl.pallas_call(functools.partial(late_kernel, frames, spaces), in_specs=[...]
  transfers between devices with their start and end apart: 16 -> 16, of which waited for: 5 -> 6; matrix products, arithmetic and copies ran while one was open for 0% -> 0% of each run, Pallas kernels for 19% -> 21%
where the time goes in v18:
time: 67.7 us; the launch traced here: 67.4 us
  starting transfers between devices  24.4 us (36%)
  Pallas kernels  20.5 us (30%)
  waiting for transfers between devices  19.4 us (29%)
  between operations  2.07 us (3%)
  local copies, waits for them, and re-layouts  0.92 us (1%)
    ppermute x16, starting transfers between devices, swap(): return lax.ppermute(field, axis, [(i, i ^ distance) for i in range(size)])  24.4 us
    ppermute x16, waiting for transfers between devices, swap(): return lax.ppermute(field, axis, [(i, i ^ distance) for i in range(size)])  19.4 us
    pallas_call x1, Pallas kernels, forward(): pl.pallas_call(functools.partial(forward_kernel, axis), in_specs=[pl.Bloc...  6.56 us
    pallas_call x3, Pallas kernels, backward(): pl.pallas_call(functools.partial(backward_kernel, axis, distances, gains_...  4.81 us
    pallas_call x1, Pallas kernels, temporal_late(): pl.pallas_call(functools.partial(late_kernel, frames, spaces), in_specs=[...  3.21 us
    pallas_call x1, Pallas kernels, fetch(): pl.pallas_call(fetch_kernel, in_specs=[pl.BlockSpec(memory_space=pltpu.HB...  1.83 us
    pallas_call x1, Pallas kernels, temporal_early(): pl.pallas_call(functools.partial(early_kernel, frames, spaces), in_specs=...  1.53 us
  transfers between devices with their start and end apart: 16, of which 6 were waited for; matrix products, arithmetic and copies ran while one was open for 0% of the time, Pallas kernels for 21%

profile of v18, /device:TPU:0, one launch (start us, length us, event | category | flops | bytes accessed | tf_op | source)
XLA Modules:
  0.0 67.4 jit_solution(11374271387767150428)
XLA Ops:
  0.6 1.3 %pack_cotangent.1 = (bf16[2,128,384]{2,1,0:T(8,128)(2,1)S(1)}, bf16[2,128,384]{2,1,0:T(8,128)(2,1)S(1)}, bf16[2,128,384]{2,1,0:T(8,128)(2,1)S(1)}, bf16[2,128,384]{2,1,0:T(8,128)(2,1)S(1)}) custom-call(bf16[128,3072]{1,0:T(8,128)(2,1)} %bitcast.19), custom_call_target="tpu_custom_call" | custom-call | flops 100000000 | tf_op jit(solution)/shard_map/pack_cotangent/pallas_call | solution.py:198
  1.9 5.1 %collective-permute-start.1 = (bf16[2,128,384]{2,1,0:T(8,128)(2,1)S(1)}, bf16[2,128,384]{2,1,0:T(8,128)(2,1)S(1)}, u32[]{:S(2)}, u32[]{:S(2)}) collective-permute-start(bf16[2,128,384]{2,1,0:T(8,128)(2,1)S(1)} %get-tuple-element.62), channel_id=1, source_target_pairs={{0,6},{2,4},{4,2},{6,0},{1,7},{3,5},{5,3},{7,1},{8,14},{10,12},{12... | collective-permute-start | bytes 589832 | tf_op jit(solution)/shard_map/ppermute | solution.py:577
  7.7 6.6 %spatial_forward.1 = (f32[12,256,256]{2,1,0:T(8,128)S(1)}, bf16[3,128,256]{2,1,0:T(8,128)(2,1)S(1)}, bf16[3,128,256]{2,1,0:T(8,128)(2,1)}, bf16[3,128,256]{2,1,0:T(8,128)(2,1)}, bf16[3,128,256]{2,1,0:T(8,128)(2,1)}) custom-call(bf16[256,1536]{1,0:T(8,128)(2,1)} %bitcast.13, bf16[256,1536]{1,0:T(8,128)(2,1)} %bitcast.15, bf16[256,1536]{1,0:T(8,128)(2,1)} %bitcast.17), custom_call_target="tpu_custom_call" | custom-call | flops 600000000 | tf_op jit(solution)/shard_map/spatial_forward/pallas_call | solution.py:76
  14.3 1.4 %collective-permute-start = (bf16[3,128,256]{2,1,0:T(8,128)(2,1)}, bf16[3,128,256]{2,1,0:T(8,128)(2,1)S(1)}, u32[]{:S(2)}, u32[]{:S(2)}) collective-permute-start(bf16[3,128,256]{2,1,0:T(8,128)(2,1)} %get-tuple-element.61), channel_id=1, source_target_pairs={{0,2},{2,0},{4,6},{6,4},{1,3},{3,1},{5,7},{7,5},{8,10},{10,8},{12,... | collective-permute-start | bytes 589832 | tf_op jit(solution)/shard_map/ppermute | solution.py:577
  15.7 2.9 %collective-permute-start.5 = (bf16[3,128,256]{2,1,0:T(8,128)(2,1)}, bf16[3,128,256]{2,1,0:T(8,128)(2,1)}, u32[]{:S(2)}, u32[]{:S(2)}) collective-permute-start(bf16[3,128,256]{2,1,0:T(8,128)(2,1)} %get-tuple-element.80), channel_id=1, source_target_pairs={{0,4},{2,6},{4,0},{6,2},{1,5},{3,7},{5,1},{7,3},{8,12},{10,14},{12... | collective-permute-start | bytes 589832 | tf_op jit(solution)/shard_map/ppermute | solution.py:577
  18.7 6.9 %collective-permute-done.2.refs_1_ = bf16[2,128,384]{2,1,0:T(8,128)(2,1)S(1)} collective-permute-done((bf16[2,128,384]{2,1,0:T(8,128)(2,1)S(1)}, bf16[2,128,384]{2,1,0:T(8,128)(2,1)S(1)}, u32[]{:S(2)}, u32[]{:S(2)}) %collective-permute-start.2) | collective-permute-done | bytes 196640 | tf_op jit(solution)/shard_map/ppermute | solution.py:577
  25.6 1.3 %turn_cotangent.1 = (bf16[6,3,128,128]{3,2,1,0:T(8,128)(2,1)S(1)}, bf16[2,3,128,128]{3,2,1,0:T(8,128)(2,1)}, bf16[2,3,128,128]{3,2,1,0:T(8,128)(2,1)}) custom-call(bf16[2,128,384]{2,1,0:T(8,128)(2,1)S(1)} %collective-permute-done.1.refs_0_, bf16[2,128,384]{2,1,0:T(8,128)(2,1)S(1)} %collective-permute-done.2.refs_1_, ...), custom_call_target="tpu_custom_call" | custom-call | flops 200000000 | tf_op jit(solution)/shard_map/turn_cotangent/pallas_call | solution.py:247
  26.9 0.8 %copy-done = bf16[6,3,128,128]{3,2,1,0:T(8,128)(2,1)} copy-done((bf16[6,3,128,128]{3,2,1,0:T(8,128)(2,1)}, bf16[6,3,128,128]{3,2,1,0:T(8,128)(2,1)S(1)}, u32[]{:S(2)}) %copy-start) | copy-done | bytes 589848
  27.7 1.7 %collective-permute-start.6 = (bf16[2,3,128,128]{3,2,1,0:T(8,128)(2,1)}, bf16[2,3,128,128]{3,2,1,0:T(8,128)(2,1)}, u32[]{:S(2)}, u32[]{:S(2)}) collective-permute-start(bf16[2,3,128,128]{3,2,1,0:T(8,128)(2,1)} %get-tuple-element.87), channel_id=1, source_target_pairs={{0,1},{1,0},{2,3},{3,2},{4,5},{5,4},{6,7},{7,6},{8,9},{9,8},{10,11... | collective-permute-start | bytes 589832 | tf_op jit(solution)/shard_map/ppermute | solution.py:577
  31.3 1.8 %fetch.1 = (bf16[6,3,128,128]{3,2,1,0:T(8,128)(2,1)S(1)}, bf16[256,1536]{1,0:T(8,128)(2,1)S(1)}, bf16[256,1536]{1,0:T(8,128)(2,1)S(1)}, bf16[256,1536]{1,0:T(8,128)(2,1)S(1)}) custom-call(bf16[6,3,128,128]{3,2,1,0:T(8,128)(2,1)} %copy-done, bf16[256,1536]{1,0:T(8,128)(2,1)} %bitcast.14, bf16[256,1536]{1,0:T(8,128)(2,1)} %bitcast.16, bf16[256,1536]{1,0:T(8,128)(2,1)} %bitcast.18), custom_call_target="tpu_custom_call" | custom-call | tf_op jit(solution)/shard_map/fetch/pallas_call | solution.py:358
  33.1 4.4 %collective-permute-done.5.refs_1_ = bf16[3,128,256]{2,1,0:T(8,128)(2,1)} collective-permute-done((bf16[3,128,256]{2,1,0:T(8,128)(2,1)}, bf16[3,128,256]{2,1,0:T(8,128)(2,1)}, u32[]{:S(2)}, u32[]{:S(2)}) %collective-permute-start.5) | collective-permute-done | bytes 196640 | tf_op jit(solution)/shard_map/ppermute | solution.py:577
  37.5 1.5 %temporal_early.1 = (f32[3,4,128,128]{3,2,1,0:T(8,128)S(1)}, f32[6,3,128,128]{3,2,1,0:T(8,128)S(1)}, f32[6,3,128,128]{3,2,1,0:T(8,128)S(1)}, f32[6,2,16,8,128]{4,3,2,1,0:T(8,128)S(1)}, f32[6,4,8,128]{3,2,1,0:T(8,128)S(1)}) custom-call(bf16[3,128,256]{2,1,0:T(8,128)(2,1)S(1)} %collective-permute-done.refs_0_, ...), custom_call_target="tpu_custom_call" | custom-call | tf_op jit(solution)/shard_map/temporal_early/pallas_call | solution.py:515
  39.1 3.2 %temporal_late.1 = (bf16[3,128,256]{2,1,0:T(8,128)(2,1)S(1)}, bf16[3,128,256]{2,1,0:T(8,128)(2,1)S(1)}, bf16[3,128,256]{2,1,0:T(8,128)(2,1)S(1)}, bf16[3,128,256]{2,1,0:T(8,128)(2,1)S(1)}, f32[8,128]{1,0:T(8,128)S(1)}) custom-call(s32[1]{0:T(128)S(6)} %copy.19.length_ref, s32[1]{0:T(128)} %copy.18.task_ref, ...), custom_call_target="tpu_custom_call" | custom-call | flops 400000000 | tf_op jit(solution)/shard_map/temporal_late/pallas_call | solution.py:533
  42.4 2.8 %collective-permute-start.8 = (bf16[3,128,256]{2,1,0:T(8,128)(2,1)S(1)}, bf16[3,128,256]{2,1,0:T(8,128)(2,1)S(1)}, u32[]{:S(2)}, u32[]{:S(2)}) collective-permute-start(bf16[3,128,256]{2,1,0:T(8,128)(2,1)S(1)} %get-tuple-element.89), channel_id=1, source_target_pairs={{0,6},{2,4},{4,2},{6,0},{1,7},{3,5},{5,3},{7,1},{8,14},{10,12},{12... | collective-permute-start | bytes 589832 | tf_op jit(solution)/shard_map/ppermute | solution.py:577
  45.2 1.0 %collective-permute-start.9 = (bf16[3,128,256]{2,1,0:T(8,128)(2,1)S(1)}, bf16[3,128,256]{2,1,0:T(8,128)(2,1)S(1)}, u32[]{:S(2)}, u32[]{:S(2)}) collective-permute-start(bf16[3,128,256]{2,1,0:T(8,128)(2,1)S(1)} %get-tuple-element.90), channel_id=1, source_target_pairs={{0,4},{2,6},{4,0},{6,2},{1,5},{3,7},{5,1},{7,3},{8,12},{10,14},{12... | collective-permute-start | bytes 589832 | tf_op jit(solution)/shard_map/ppermute | solution.py:577
  46.8 1.5 %collective-permute-start.11 = (f32[16,128]{1,0:T(8,128)S(1)}, f32[16,128]{1,0:T(8,128)S(1)}, u32[]{:S(2)}, u32[]{:S(2)}) collective-permute-start(f32[16,128]{1,0:T(8,128)S(1)} %pad_maximum_fusion.1), channel_id=1, source_target_pairs={{0,16},{8,24},{16,0},{24,8},{1,17},{9,25},{17,1},{25,9},{2,18},{10... | collective-permute-start | bytes 24584 | tf_op jit(solution)/shard_map/ppermute | solution.py:577
  48.3 1.4 %spatial_backward.3 = (bf16[256,1536]{1,0:T(8,128)(2,1)}, bf16[256,1536]{1,0:T(8,128)(2,1)}) custom-call(bf16[256,1536]{1,0:T(8,128)(2,1)S(1)} %get-tuple-element.74.refs_0_, bf16[256,1536]{1,0:T(8,128)(2,1)S(1)} %get-tuple-element.75.refs_1_, bf16[256,1536]{1,0:T(8,128)(2,1)S(1)} %get-tuple-element.76.refs_2_, ...), custom_call_target="tpu_custom_call" | custom-call | flops 200000000 | tf_op jit(solution)/shard_map/spatial_backward/pallas_call | solution.py:159
  50.5 2.4 %collective-permute-start.14 = (f32[32,128]{1,0:T(8,128)S(1)}, f32[32,128]{1,0:T(8,128)S(1)}, u32[]{:S(2)}, u32[]{:S(2)}) collective-permute-start(f32[32,128]{1,0:T(8,128)S(1)} %pad_maximum_fusion.refs_6_), channel_id=1, source_target_pairs={{0,4},{2,6},{4,0},{6,2},{1,5},{3,7},{5,1},{7,3},{8,12},{10,14},{12... | collective-permute-start | bytes 49160 | tf_op jit(solution)/shard_map/ppermute | solution.py:577
  52.8 1.3 %collective-permute-start.15 = (f32[32,128]{1,0:T(8,128)S(1)}, f32[32,128]{1,0:T(8,128)S(1)}, u32[]{:S(2)}, u32[]{:S(2)}) collective-permute-start(f32[32,128]{1,0:T(8,128)S(1)} %pad_maximum_fusion.refs_6_), channel_id=1, source_target_pairs={{0,6},{2,4},{4,2},{6,0},{1,7},{3,5},{5,3},{7,1},{8,14},{10,12},{12... | collective-permute-start | bytes 49160 | tf_op jit(solution)/shard_map/ppermute | solution.py:577
  54.2 4.6 %collective-permute-done.12.refs_4_ = bf16[3,128,256]{2,1,0:T(8,128)(2,1)S(1)} collective-permute-done((bf16[3,128,256]{2,1,0:T(8,128)(2,1)S(1)}, bf16[3,128,256]{2,1,0:T(8,128)(2,1)S(1)}, u32[]{:S(2)}, u32[]{:S(2)}) %collective-permute-start.12) | collective-permute-done | bytes 196640 | tf_op jit(solution)/shard_map/ppermute | solution.py:577
  58.8 2.5 %collective-permute-start.13 = (f32[32,128]{1,0:T(8,128)S(1)}, f32[32,128]{1,0:T(8,128)S(1)}, u32[]{:S(2)}, u32[]{:S(2)}) collective-permute-start(f32[32,128]{1,0:T(8,128)S(1)} %pad_maximum_fusion.refs_6_), channel_id=1, source_target_pairs={{0,2},{2,0},{4,6},{6,4},{1,3},{3,1},{5,7},{7,5},{8,10},{10,8},{12,... | collective-permute-start | bytes 49160 | tf_op jit(solution)/shard_map/ppermute | solution.py:577
  61.3 1.4 %spatial_backward.4 = (bf16[256,1536]{1,0:T(8,128)(2,1)}, bf16[256,1536]{1,0:T(8,128)(2,1)}) custom-call(bf16[256,1536]{1,0:T(8,128)(2,1)S(1)} %get-tuple-element.74.refs_0_, bf16[256,1536]{1,0:T(8,128)(2,1)S(1)} %get-tuple-element.75.refs_1_, bf16[256,1536]{1,0:T(8,128)(2,1)S(1)} %get-tuple-element.76.refs_2_, ...), custom_call_target="tpu_custom_call", output_to_operand_aliasing={{0}: (5, {}), {1}: (6, {})} | custom-call | flops 200000000 | tf_op jit(solution)/shard_map/spatial_backward/pallas_call | solution.py:159
  62.7 2.6 %collective-permute-done.14.refs_8_ = f32[32,128]{1,0:T(8,128)S(1)} collective-permute-done((f32[32,128]{1,0:T(8,128)S(1)}, f32[32,128]{1,0:T(8,128)S(1)}, u32[]{:S(2)}, u32[]{:S(2)}) %collective-permute-start.14) | collective-permute-done | bytes 16416 | tf_op jit(solution)/shard_map/ppermute | solution.py:577
  65.4 2.0 %spatial_backward.5 = (bf16[256,1536]{1,0:T(8,128)(2,1)}, bf16[256,1536]{1,0:T(8,128)(2,1)}, f32[2,16,1536]{2,1,0:T(8,128)}) custom-call(bf16[256,1536]{1,0:T(8,128)(2,1)S(1)} %get-tuple-element.74.refs_0_, bf16[256,1536]{1,0:T(8,128)(2,1)S(1)} %get-tuple-element.75.refs_1_, ...), custom_call_target="tpu_custom_call", output_to_operand_aliasing={{0}: (11, {}), {1}: (12, {})} | custom-call | flops 200000000 | tf_op jit(solution)/shard_map/spatial_backward/pallas_call | solution.py:159
  (25 shorter events, 2.9 us)
Async XLA Ops:
  1.9 16.7 %collective-permute-start.1 = (bf16[2,128,384]{2,1,0:T(8,128)(2,1)S(1)}, bf16[2,128,384]{2,1,0:T(8,128)(2,1)S(1)}, u32[]{:S(2)}, u32[]{:S(2)}) collective-permute-start(bf16[2,128,384]{2,1,0:T(8,128)(2,1)S(1)} %get-tuple-element.62), channel_id=1, source_target_pairs={{0,6},{2,4},{4,2},{6,0},{1,7},{3,5},{5,3},{7,1},{8,14},{10,12},{12... | collective-permute-start | bytes 589832 | tf_op jit(solution)/shard_map/ppermute | solution.py:577
  7.0 18.5 %collective-permute-start.2 = (bf16[2,128,384]{2,1,0:T(8,128)(2,1)S(1)}, bf16[2,128,384]{2,1,0:T(8,128)(2,1)S(1)}, u32[]{:S(2)}, u32[]{:S(2)}) collective-permute-start(bf16[2,128,384]{2,1,0:T(8,128)(2,1)S(1)} %get-tuple-element.63), channel_id=1, source_target_pairs={{0,4},{2,6},{4,0},{6,2},{1,5},{3,7},{5,1},{7,3},{8,12},{10,14},{12... | collective-permute-start | bytes 589832 | tf_op jit(solution)/shard_map/ppermute | solution.py:577
  7.0 18.5 %collective-permute-start.3 = (bf16[2,128,384]{2,1,0:T(8,128)(2,1)S(1)}, bf16[2,128,384]{2,1,0:T(8,128)(2,1)S(1)}, u32[]{:S(2)}, u32[]{:S(2)}) collective-permute-start(bf16[2,128,384]{2,1,0:T(8,128)(2,1)S(1)} %get-tuple-element.64), channel_id=1, source_target_pairs={{0,2},{2,0},{4,6},{6,4},{1,3},{3,1},{5,7},{7,5},{8,10},{10,8},{12,... | collective-permute-start | bytes 589832 | tf_op jit(solution)/shard_map/ppermute | solution.py:577
  7.7 23.3 %copy-start.1 = (f32[2,16,1536]{2,1,0:T(8,128)S(1)}, f32[2,16,1536]{2,1,0:T(8,128)}, u32[]{:S(2)}) copy-start(f32[2,16,1536]{2,1,0:T(8,128)} %refs_10_.1) | copy-start | bytes 589828
  14.3 16.9 %collective-permute-start = (bf16[3,128,256]{2,1,0:T(8,128)(2,1)}, bf16[3,128,256]{2,1,0:T(8,128)(2,1)S(1)}, u32[]{:S(2)}, u32[]{:S(2)}) collective-permute-start(bf16[3,128,256]{2,1,0:T(8,128)(2,1)} %get-tuple-element.61), channel_id=1, source_target_pairs={{0,2},{2,0},{4,6},{6,4},{1,3},{3,1},{5,7},{7,5},{8,10},{10,8},{12,... | collective-permute-start | bytes 589832 | tf_op jit(solution)/shard_map/ppermute | solution.py:577
  15.7 21.8 %collective-permute-start.5 = (bf16[3,128,256]{2,1,0:T(8,128)(2,1)}, bf16[3,128,256]{2,1,0:T(8,128)(2,1)}, u32[]{:S(2)}, u32[]{:S(2)}) collective-permute-start(bf16[3,128,256]{2,1,0:T(8,128)(2,1)} %get-tuple-element.80), channel_id=1, source_target_pairs={{0,4},{2,6},{4,0},{6,2},{1,5},{3,7},{5,1},{7,3},{8,12},{10,14},{12... | collective-permute-start | bytes 589832 | tf_op jit(solution)/shard_map/ppermute | solution.py:577
  18.6 20.4 %collective-permute-start.4 = (bf16[3,128,256]{2,1,0:T(8,128)(2,1)}, bf16[3,128,256]{2,1,0:T(8,128)(2,1)}, u32[]{:S(2)}, u32[]{:S(2)}) collective-permute-start(bf16[3,128,256]{2,1,0:T(8,128)(2,1)} %get-tuple-element.77), channel_id=1, source_target_pairs={{0,6},{2,4},{4,2},{6,0},{1,7},{3,5},{5,3},{7,1},{8,14},{10,12},{12... | collective-permute-start | bytes 589832 | tf_op jit(solution)/shard_map/ppermute | solution.py:577
  26.9 0.8 %copy-start = (bf16[6,3,128,128]{3,2,1,0:T(8,128)(2,1)}, bf16[6,3,128,128]{3,2,1,0:T(8,128)(2,1)S(1)}, u32[]{:S(2)}) copy-start(bf16[6,3,128,128]{3,2,1,0:T(8,128)(2,1)S(1)} %get-tuple-element.73.refs_0_) | copy-start | bytes 1769476
  27.7 11.3 %collective-permute-start.6 = (bf16[2,3,128,128]{3,2,1,0:T(8,128)(2,1)}, bf16[2,3,128,128]{3,2,1,0:T(8,128)(2,1)}, u32[]{:S(2)}, u32[]{:S(2)}) collective-permute-start(bf16[2,3,128,128]{3,2,1,0:T(8,128)(2,1)} %get-tuple-element.87), channel_id=1, source_target_pairs={{0,1},{1,0},{2,3},{3,2},{4,5},{5,4},{6,7},{7,6},{8,9},{9,8},{10,11... | collective-permute-start | bytes 589832 | tf_op jit(solution)/shard_map/ppermute | solution.py:577
  29.4 9.6 %collective-permute-start.7 = (bf16[2,3,128,128]{3,2,1,0:T(8,128)(2,1)}, bf16[2,3,128,128]{3,2,1,0:T(8,128)(2,1)}, u32[]{:S(2)}, u32[]{:S(2)}) collective-permute-start(bf16[2,3,128,128]{3,2,1,0:T(8,128)(2,1)} %get-tuple-element.88), channel_id=1, source_target_pairs={{0,1},{1,0},{2,3},{3,2},{4,5},{5,4},{6,7},{7,6},{8,9},{9,8},{10,11... | collective-permute-start | bytes 589832 | tf_op jit(solution)/shard_map/ppermute | solution.py:577
  42.3 3.9 %collective-permute-start.10 = (f32[8,128]{1,0:T(8,128)S(1)}, f32[8,128]{1,0:T(8,128)S(1)}, u32[]{:S(2)}, u32[]{:S(2)}) collective-permute-start(f32[8,128]{1,0:T(8,128)S(1)} %get-tuple-element.91), channel_id=1, source_target_pairs={{0,8},{8,0},{16,24},{24,16},{1,9},{9,1},{17,25},{25,17},{2,10},{10... | collective-permute-start | bytes 12296 | tf_op jit(solution)/shard_map/ppermute | solution.py:577
  42.4 22.9 %collective-permute-start.8 = (bf16[3,128,256]{2,1,0:T(8,128)(2,1)S(1)}, bf16[3,128,256]{2,1,0:T(8,128)(2,1)S(1)}, u32[]{:S(2)}, u32[]{:S(2)}) collective-permute-start(bf16[3,128,256]{2,1,0:T(8,128)(2,1)S(1)} %get-tuple-element.89), channel_id=1, source_target_pairs={{0,6},{2,4},{4,2},{6,0},{1,7},{3,5},{5,3},{7,1},{8,14},{10,12},{12... | collective-permute-start | bytes 589832 | tf_op jit(solution)/shard_map/ppermute | solution.py:577
  45.2 20.1 %collective-permute-start.9 = (bf16[3,128,256]{2,1,0:T(8,128)(2,1)S(1)}, bf16[3,128,256]{2,1,0:T(8,128)(2,1)S(1)}, u32[]{:S(2)}, u32[]{:S(2)}) collective-permute-start(bf16[3,128,256]{2,1,0:T(8,128)(2,1)S(1)} %get-tuple-element.90), channel_id=1, source_target_pairs={{0,4},{2,6},{4,0},{6,2},{1,5},{3,7},{5,1},{7,3},{8,12},{10,14},{12... | collective-permute-start | bytes 589832 | tf_op jit(solution)/shard_map/ppermute | solution.py:577
  46.1 12.7 %collective-permute-start.12 = (bf16[3,128,256]{2,1,0:T(8,128)(2,1)S(1)}, bf16[3,128,256]{2,1,0:T(8,128)(2,1)S(1)}, u32[]{:S(2)}, u32[]{:S(2)}) collective-permute-start(bf16[3,128,256]{2,1,0:T(8,128)(2,1)S(1)} %get-tuple-element.99), channel_id=1, source_target_pairs={{0,2},{2,0},{4,6},{6,4},{1,3},{3,1},{5,7},{7,5},{8,10},{10,8},{12,... | collective-permute-start | bytes 589832 | tf_op jit(solution)/shard_map/ppermute | solution.py:577
  46.8 3.7 %collective-permute-start.11 = (f32[16,128]{1,0:T(8,128)S(1)}, f32[16,128]{1,0:T(8,128)S(1)}, u32[]{:S(2)}, u32[]{:S(2)}) collective-permute-start(f32[16,128]{1,0:T(8,128)S(1)} %pad_maximum_fusion.1), channel_id=1, source_target_pairs={{0,16},{8,24},{16,0},{24,8},{1,17},{9,25},{17,1},{25,9},{2,18},{10... | collective-permute-start | bytes 24584 | tf_op jit(solution)/shard_map/ppermute | solution.py:577
  50.5 14.8 %collective-permute-start.14 = (f32[32,128]{1,0:T(8,128)S(1)}, f32[32,128]{1,0:T(8,128)S(1)}, u32[]{:S(2)}, u32[]{:S(2)}) collective-permute-start(f32[32,128]{1,0:T(8,128)S(1)} %pad_maximum_fusion.refs_6_), channel_id=1, source_target_pairs={{0,4},{2,6},{4,0},{6,2},{1,5},{3,7},{5,1},{7,3},{8,12},{10,14},{12... | collective-permute-start | bytes 49160 | tf_op jit(solution)/shard_map/ppermute | solution.py:577
  52.8 12.4 %collective-permute-start.15 = (f32[32,128]{1,0:T(8,128)S(1)}, f32[32,128]{1,0:T(8,128)S(1)}, u32[]{:S(2)}, u32[]{:S(2)}) collective-permute-start(f32[32,128]{1,0:T(8,128)S(1)} %pad_maximum_fusion.refs_6_), channel_id=1, source_target_pairs={{0,6},{2,4},{4,2},{6,0},{1,7},{3,5},{5,3},{7,1},{8,14},{10,12},{12... | collective-permute-start | bytes 49160 | tf_op jit(solution)/shard_map/ppermute | solution.py:577
  58.8 6.6 %collective-permute-start.13 = (f32[32,128]{1,0:T(8,128)S(1)}, f32[32,128]{1,0:T(8,128)S(1)}, u32[]{:S(2)}, u32[]{:S(2)}) collective-permute-start(f32[32,128]{1,0:T(8,128)S(1)} %pad_maximum_fusion.refs_6_), channel_id=1, source_target_pairs={{0,2},{2,0},{4,6},{6,4},{1,3},{3,1},{5,7},{7,5},{8,10},{10,8},{12,... | collective-permute-start | bytes 49160 | tf_op jit(solution)/shard_map/ppermute | solution.py:577

commit v19 on v15

--- a/solution.py
+++ b/solution.py
@@ -503,14 +503,15 @@
     attended[1], gain, upstream[0] = lax.optimization_barrier((attended[1], gain, upstream[0]))
     upstream[0], *kept = fetch(upstream[0], *fields)
     grads, mixed = temporal(lengths, task_ids, attended[1:], upstream, gain)
-    for distance in reversed(range(1, frames)):
+    for distance in reversed(range(2, frames)):
         grads[distance] = swap(grads[distance], "tm", frames, distance)
     here = grads[0]
     for bit in range(clips.bit_length() - 1):
         other = swap(mixed, "dp", clips, 1 << bit)
         if bit == 0:
-            here, other = lax.optimization_barrier((here, other))
+            here, grads[1], other = lax.optimization_barrier((here, grads[1], other))
         mixed = jnp.concatenate([mixed, other], axis=0)
+    grads[1] = swap(grads[1], "tm", frames, 1)
     results = backward("tm", kept, weights, [here], [0])
     mixed, results = lax.optimization_barrier((mixed, results))
     near, grads[1] = lax.optimization_barrier((mixed, grads[1]))
@@ -519,8 +520,9 @@
     ]
     last = range(frames - 1, 0, -1)
     if frames > 2:
-        results = backward("tm", kept, weights, [grads[1]], [1], results)
-        last = range(frames - 1, 1, -1)
+        for distance in [1, *range(3, frames)]:
+            results = backward("tm", kept, weights, [grads[distance]], [distance], results)
+        last = [2]
     grad_queries, grad_keys, grad_gains = backward(
         "tm",
         kept,

time: 66.7 us -> 67.4 us (1.010)
  starting transfers between devices: 25.1 us -> 24.2 us
  Pallas kernels: 19.4 us -> 20.2 us
  waiting for transfers between devices: 18.9 us -> 19.7 us
    ppermute x16, starting transfers between devices: 25.1 us -> 24.2 us  [swap(): return lax.ppermute(field, axis, [(i, i ^ distance) for i in range(size)])]
    pallas_call x3 -> x4, Pallas kernels: 4.81 us -> 5.68 us  [backward(): pl.pallas_call(functools.partial(backward_kernel, axis, distances, gains_...]
    ppermute x16, waiting for transfers between devices: 18.9 us -> 19.7 us  [swap(): return lax.ppermute(field, axis, [(i, i ^ distance) for i in range(size)])]
  transfers between devices with their start and end apart: 16 -> 16, of which waited for: 5 -> 5; matrix products, arithmetic and copies ran while one was open for 0% -> 0% of each run, Pallas kernels for 19% -> 21%
where the time goes in v19:
time: 67.4 us; the launch traced here: 67.2 us
  starting transfers between devices  24.2 us (36%)
  Pallas kernels  20.2 us (30%)
  waiting for transfers between devices  19.7 us (29%)
  between operations  2.08 us (3%)
  local copies, waits for them, and re-layouts  0.92 us (1%)
    ppermute x16, starting transfers between devices, swap(): return lax.ppermute(field, axis, [(i, i ^ distance) for i in range(size)])  24.2 us
    ppermute x16, waiting for transfers between devices, swap(): return lax.ppermute(field, axis, [(i, i ^ distance) for i in range(size)])  19.7 us
    pallas_call x1, Pallas kernels, forward(): pl.pallas_call(functools.partial(forward_kernel, axis), in_specs=[pl.Bloc...  6.51 us
    pallas_call x4, Pallas kernels, backward(): pl.pallas_call(functools.partial(backward_kernel, axis, distances, gains_...  5.68 us
    pallas_call x1, Pallas kernels, temporal(): pl.pallas_call(functools.partial(temporal_kernel, frames, spaces), in_spe...  3.62 us
    pallas_call x1, Pallas kernels, fetch(): pl.pallas_call(fetch_kernel, in_specs=[pl.BlockSpec(memory_space=pltpu.HB...  1.83 us
  transfers between devices with their start and end apart: 16, of which 5 were waited for; matrix products, arithmetic and copies ran while one was open for 0% of the time, Pallas kernels for 21%

profile of v19, /device:TPU:0, one launch (start us, length us, event | category | flops | bytes accessed | tf_op | source)
XLA Modules:
  0.0 67.2 jit_solution(18031543109405008791)
XLA Ops:
  0.6 1.3 %pack_cotangent.1 = (bf16[2,128,384]{2,1,0:T(8,128)(2,1)S(1)}, bf16[2,128,384]{2,1,0:T(8,128)(2,1)S(1)}, bf16[2,128,384]{2,1,0:T(8,128)(2,1)S(1)}, bf16[2,128,384]{2,1,0:T(8,128)(2,1)S(1)}) custom-call(bf16[128,3072]{1,0:T(8,128)(2,1)} %bitcast.19), custom_call_target="tpu_custom_call" | custom-call | flops 100000000 | tf_op jit(solution)/shard_map/pack_cotangent/pallas_call | solution.py:198
  2.0 5.1 %collective-permute-start.1 = (bf16[2,128,384]{2,1,0:T(8,128)(2,1)S(1)}, bf16[2,128,384]{2,1,0:T(8,128)(2,1)S(1)}, u32[]{:S(2)}, u32[]{:S(2)}) collective-permute-start(bf16[2,128,384]{2,1,0:T(8,128)(2,1)S(1)} %get-tuple-element.59), channel_id=1, source_target_pairs={{0,6},{2,4},{4,2},{6,0},{1,7},{3,5},{5,3},{7,1},{8,14},{10,12},{12... | collective-permute-start | bytes 589832 | tf_op jit(solution)/shard_map/ppermute | solution.py:471
  7.7 6.5 %spatial_forward.1 = (f32[12,256,256]{2,1,0:T(8,128)S(1)}, bf16[3,128,256]{2,1,0:T(8,128)(2,1)S(1)}, bf16[3,128,256]{2,1,0:T(8,128)(2,1)}, bf16[3,128,256]{2,1,0:T(8,128)(2,1)}, bf16[3,128,256]{2,1,0:T(8,128)(2,1)}) custom-call(bf16[256,1536]{1,0:T(8,128)(2,1)} %bitcast.13, bf16[256,1536]{1,0:T(8,128)(2,1)} %bitcast.15, bf16[256,1536]{1,0:T(8,128)(2,1)} %bitcast.17), custom_call_target="tpu_custom_call" | custom-call | flops 600000000 | tf_op jit(solution)/shard_map/spatial_forward/pallas_call | solution.py:76
  14.2 1.4 %collective-permute-start = (bf16[3,128,256]{2,1,0:T(8,128)(2,1)}, bf16[3,128,256]{2,1,0:T(8,128)(2,1)S(1)}, u32[]{:S(2)}, u32[]{:S(2)}) collective-permute-start(bf16[3,128,256]{2,1,0:T(8,128)(2,1)} %get-tuple-element.58), channel_id=1, source_target_pairs={{0,2},{2,0},{4,6},{6,4},{1,3},{3,1},{5,7},{7,5},{8,10},{10,8},{12,... | collective-permute-start | bytes 589832 | tf_op jit(solution)/shard_map/ppermute | solution.py:471
  15.7 2.9 %collective-permute-start.4 = (bf16[3,128,256]{2,1,0:T(8,128)(2,1)}, bf16[3,128,256]{2,1,0:T(8,128)(2,1)}, u32[]{:S(2)}, u32[]{:S(2)}) collective-permute-start(bf16[3,128,256]{2,1,0:T(8,128)(2,1)} %get-tuple-element.75), channel_id=1, source_target_pairs={{0,4},{2,6},{4,0},{6,2},{1,5},{3,7},{5,1},{7,3},{8,12},{10,14},{12... | collective-permute-start | bytes 589832 | tf_op jit(solution)/shard_map/ppermute | solution.py:471
  18.7 6.9 %collective-permute-done.2.refs_1_ = bf16[2,128,384]{2,1,0:T(8,128)(2,1)S(1)} collective-permute-done((bf16[2,128,384]{2,1,0:T(8,128)(2,1)S(1)}, bf16[2,128,384]{2,1,0:T(8,128)(2,1)S(1)}, u32[]{:S(2)}, u32[]{:S(2)}) %collective-permute-start.2) | collective-permute-done | bytes 196640 | tf_op jit(solution)/shard_map/ppermute | solution.py:471
  25.6 1.3 %turn_cotangent.1 = (bf16[6,3,128,128]{3,2,1,0:T(8,128)(2,1)S(1)}, bf16[2,3,128,128]{3,2,1,0:T(8,128)(2,1)}, bf16[2,3,128,128]{3,2,1,0:T(8,128)(2,1)}) custom-call(bf16[2,128,384]{2,1,0:T(8,128)(2,1)S(1)} %collective-permute-done.1.refs_0_, bf16[2,128,384]{2,1,0:T(8,128)(2,1)S(1)} %collective-permute-done.2.refs_1_, ...), custom_call_target="tpu_custom_call" | custom-call | flops 200000000 | tf_op jit(solution)/shard_map/turn_cotangent/pallas_call | solution.py:247
  26.9 0.8 %copy-done = bf16[6,3,128,128]{3,2,1,0:T(8,128)(2,1)} copy-done((bf16[6,3,128,128]{3,2,1,0:T(8,128)(2,1)}, bf16[6,3,128,128]{3,2,1,0:T(8,128)(2,1)S(1)}, u32[]{:S(2)}) %copy-start) | copy-done | bytes 589848
  27.7 1.7 %collective-permute-start.6 = (bf16[2,3,128,128]{3,2,1,0:T(8,128)(2,1)}, bf16[2,3,128,128]{3,2,1,0:T(8,128)(2,1)}, u32[]{:S(2)}, u32[]{:S(2)}) collective-permute-start(bf16[2,3,128,128]{3,2,1,0:T(8,128)(2,1)} %get-tuple-element.79), channel_id=1, source_target_pairs={{0,1},{1,0},{2,3},{3,2},{4,5},{5,4},{6,7},{7,6},{8,9},{9,8},{10,11... | collective-permute-start | bytes 589832 | tf_op jit(solution)/shard_map/ppermute | solution.py:471
  31.3 1.8 %fetch.1 = (bf16[6,3,128,128]{3,2,1,0:T(8,128)(2,1)S(1)}, bf16[256,1536]{1,0:T(8,128)(2,1)S(1)}, bf16[256,1536]{1,0:T(8,128)(2,1)S(1)}, bf16[256,1536]{1,0:T(8,128)(2,1)S(1)}) custom-call(bf16[6,3,128,128]{3,2,1,0:T(8,128)(2,1)} %copy-done, bf16[256,1536]{1,0:T(8,128)(2,1)} %bitcast.14, bf16[256,1536]{1,0:T(8,128)(2,1)} %bitcast.16, bf16[256,1536]{1,0:T(8,128)(2,1)} %bitcast.18), custom_call_target="tpu_custom_call" | custom-call | flops 100000000 | tf_op jit(solution)/shard_map/fetch/pallas_call | solution.py:366
  33.1 4.4 %collective-permute-done.4.refs_1_ = bf16[3,128,256]{2,1,0:T(8,128)(2,1)} collective-permute-done((bf16[3,128,256]{2,1,0:T(8,128)(2,1)}, bf16[3,128,256]{2,1,0:T(8,128)(2,1)}, u32[]{:S(2)}, u32[]{:S(2)}) %collective-permute-start.4) | collective-permute-done | bytes 196640 | tf_op jit(solution)/shard_map/ppermute | solution.py:471
  37.5 3.6 %temporal.1 = (bf16[3,128,256]{2,1,0:T(8,128)(2,1)S(1)}, bf16[3,128,256]{2,1,0:T(8,128)(2,1)S(1)}, bf16[3,128,256]{2,1,0:T(8,128)(2,1)S(1)}, bf16[3,128,256]{2,1,0:T(8,128)(2,1)S(1)}, f32[8,128]{1,0:T(8,128)S(1)}) custom-call(s32[1]{0:T(128)S(6)} %copy.23.length_ref, s32[1]{0:T(128)} %copy.22.task_ref, ...), custom_call_target="tpu_custom_call" | custom-call | flops 400000000 | tf_op jit(solution)/shard_map/temporal/pallas_call | solution.py:431
  41.2 4.9 %collective-permute-start.8 = (bf16[3,128,256]{2,1,0:T(8,128)(2,1)S(1)}, bf16[3,128,256]{2,1,0:T(8,128)(2,1)S(1)}, u32[]{:S(2)}, u32[]{:S(2)}) collective-permute-start(bf16[3,128,256]{2,1,0:T(8,128)(2,1)S(1)} %get-tuple-element.81), channel_id=1, source_target_pairs={{0,4},{2,6},{4,0},{6,2},{1,5},{3,7},{5,1},{7,3},{8,12},{10,14},{12... | collective-permute-start | bytes 589832 | tf_op jit(solution)/shard_map/ppermute | solution.py:471
  46.1 1.3 %collective-permute-start.15 = (bf16[3,128,256]{2,1,0:T(8,128)(2,1)S(1)}, bf16[3,128,256]{2,1,0:T(8,128)(2,1)S(1)}, u32[]{:S(2)}, u32[]{:S(2)}) collective-permute-start(bf16[3,128,256]{2,1,0:T(8,128)(2,1)S(1)} %get-tuple-element.92), channel_id=1, source_target_pairs={{0,6},{2,4},{4,2},{6,0},{1,7},{3,5},{5,3},{7,1},{8,14},{10,12},{12... | collective-permute-start | bytes 589832 | tf_op jit(solution)/shard_map/ppermute | solution.py:471
  47.5 1.6 %collective-permute-start.10 = (f32[16,128]{1,0:T(8,128)S(1)}, f32[16,128]{1,0:T(8,128)S(1)}, u32[]{:S(2)}, u32[]{:S(2)}) collective-permute-start(f32[16,128]{1,0:T(8,128)S(1)} %pad_maximum_fusion.1), channel_id=1, source_target_pairs={{0,16},{8,24},{16,0},{24,8},{1,17},{9,25},{17,1},{25,9},{2,18},{10... | collective-permute-start | bytes 24584 | tf_op jit(solution)/shard_map/ppermute | solution.py:471
  49.0 1.4 %spatial_backward.4 = (bf16[256,1536]{1,0:T(8,128)(2,1)}, bf16[256,1536]{1,0:T(8,128)(2,1)}) custom-call(bf16[256,1536]{1,0:T(8,128)(2,1)S(1)} %get-tuple-element.71.refs_0_, bf16[256,1536]{1,0:T(8,128)(2,1)S(1)} %get-tuple-element.72.refs_1_, bf16[256,1536]{1,0:T(8,128)(2,1)S(1)} %get-tuple-element.73.refs_2_, ...), custom_call_target="tpu_custom_call" | custom-call | flops 200000000 | tf_op jit(solution)/shard_map/spatial_backward/pallas_call | solution.py:159
  50.5 0.7 %collective-permute-done.10 = f32[16,128]{1,0:T(8,128)S(1)} collective-permute-done((f32[16,128]{1,0:T(8,128)S(1)}, f32[16,128]{1,0:T(8,128)S(1)}, u32[]{:S(2)}, u32[]{:S(2)}) %collective-permute-start.10) | collective-permute-done | bytes 8224 | tf_op jit(solution)/shard_map/ppermute | solution.py:471
  51.2 2.5 %collective-permute-start.14 = (f32[32,128]{1,0:T(8,128)S(1)}, f32[32,128]{1,0:T(8,128)S(1)}, u32[]{:S(2)}, u32[]{:S(2)}) collective-permute-start(f32[32,128]{1,0:T(8,128)S(1)} %pad_maximum_fusion.refs_5_), channel_id=1, source_target_pairs={{0,6},{2,4},{4,2},{6,0},{1,7},{3,5},{5,3},{7,1},{8,14},{10,12},{12... | collective-permute-start | bytes 49160 | tf_op jit(solution)/shard_map/ppermute | solution.py:471
  53.7 0.9 %collective-permute-start.13 = (f32[32,128]{1,0:T(8,128)S(1)}, f32[32,128]{1,0:T(8,128)S(1)}, u32[]{:S(2)}, u32[]{:S(2)}) collective-permute-start(f32[32,128]{1,0:T(8,128)S(1)} %pad_maximum_fusion.refs_5_), channel_id=1, source_target_pairs={{0,4},{2,6},{4,0},{6,2},{1,5},{3,7},{5,1},{7,3},{8,12},{10,14},{12... | collective-permute-start | bytes 49160 | tf_op jit(solution)/shard_map/ppermute | solution.py:471
  54.6 7.0 %collective-permute-done.11.refs_4_ = bf16[3,128,256]{2,1,0:T(8,128)(2,1)S(1)} collective-permute-done((bf16[3,128,256]{2,1,0:T(8,128)(2,1)S(1)}, bf16[3,128,256]{2,1,0:T(8,128)(2,1)S(1)}, u32[]{:S(2)}, u32[]{:S(2)}) %collective-permute-start.11) | collective-permute-done | bytes 196640 | tf_op jit(solution)/shard_map/ppermute | solution.py:471
  61.6 0.6 collective-permute-start.12
  62.3 1.4 %spatial_backward.5 = (bf16[256,1536]{1,0:T(8,128)(2,1)}, bf16[256,1536]{1,0:T(8,128)(2,1)}) custom-call(bf16[256,1536]{1,0:T(8,128)(2,1)S(1)} %get-tuple-element.71.refs_0_, bf16[256,1536]{1,0:T(8,128)(2,1)S(1)} %get-tuple-element.72.refs_1_, bf16[256,1536]{1,0:T(8,128)(2,1)S(1)} %get-tuple-element.73.refs_2_, ...), custom_call_target="tpu_custom_call", output_to_operand_aliasing={{0}: (5, {}), {1}: (6, {})} | custom-call | flops 200000000 | tf_op jit(solution)/shard_map/spatial_backward/pallas_call | solution.py:159
  63.7 1.4 %spatial_backward.6 = (bf16[256,1536]{1,0:T(8,128)(2,1)}, bf16[256,1536]{1,0:T(8,128)(2,1)}) custom-call(bf16[256,1536]{1,0:T(8,128)(2,1)S(1)} %get-tuple-element.71.refs_0_, bf16[256,1536]{1,0:T(8,128)(2,1)S(1)} %get-tuple-element.72.refs_1_, bf16[256,1536]{1,0:T(8,128)(2,1)S(1)} %get-tuple-element.73.refs_2_, ...), custom_call_target="tpu_custom_call", output_to_operand_aliasing={{0}: (5, {}), {1}: (6, {})} | custom-call | flops 200000000 | tf_op jit(solution)/shard_map/spatial_backward/pallas_call | solution.py:159
  65.7 1.4 %spatial_backward.7 = (bf16[256,1536]{1,0:T(8,128)(2,1)}, bf16[256,1536]{1,0:T(8,128)(2,1)}, f32[2,16,1536]{2,1,0:T(8,128)}) custom-call(bf16[256,1536]{1,0:T(8,128)(2,1)S(1)} %get-tuple-element.71.refs_0_, bf16[256,1536]{1,0:T(8,128)(2,1)S(1)} %get-tuple-element.72.refs_1_, ...), custom_call_target="tpu_custom_call", output_to_operand_aliasing={{0}: (10, {}), {1}: (11, {})} | custom-call | flops 200000000 | tf_op jit(solution)/shard_map/spatial_backward/pallas_call | solution.py:159
  (25 shorter events, 2.0 us)
Async XLA Ops:
  0.6 30.4 %copy-start.1 = (f32[2,16,1536]{2,1,0:T(8,128)S(1)}, f32[2,16,1536]{2,1,0:T(8,128)}, u32[]{:S(2)}) copy-start(f32[2,16,1536]{2,1,0:T(8,128)} %refs_9_.1) | copy-start | bytes 589828
  2.0 16.7 %collective-permute-start.1 = (bf16[2,128,384]{2,1,0:T(8,128)(2,1)S(1)}, bf16[2,128,384]{2,1,0:T(8,128)(2,1)S(1)}, u32[]{:S(2)}, u32[]{:S(2)}) collective-permute-start(bf16[2,128,384]{2,1,0:T(8,128)(2,1)S(1)} %get-tuple-element.59), channel_id=1, source_target_pairs={{0,6},{2,4},{4,2},{6,0},{1,7},{3,5},{5,3},{7,1},{8,14},{10,12},{12... | collective-permute-start | bytes 589832 | tf_op jit(solution)/shard_map/ppermute | solution.py:471
  7.1 18.5 %collective-permute-start.2 = (bf16[2,128,384]{2,1,0:T(8,128)(2,1)S(1)}, bf16[2,128,384]{2,1,0:T(8,128)(2,1)S(1)}, u32[]{:S(2)}, u32[]{:S(2)}) collective-permute-start(bf16[2,128,384]{2,1,0:T(8,128)(2,1)S(1)} %get-tuple-element.60), channel_id=1, source_target_pairs={{0,4},{2,6},{4,0},{6,2},{1,5},{3,7},{5,1},{7,3},{8,12},{10,14},{12... | collective-permute-start | bytes 589832 | tf_op jit(solution)/shard_map/ppermute | solution.py:471
  7.1 18.5 %collective-permute-start.3 = (bf16[2,128,384]{2,1,0:T(8,128)(2,1)S(1)}, bf16[2,128,384]{2,1,0:T(8,128)(2,1)S(1)}, u32[]{:S(2)}, u32[]{:S(2)}) collective-permute-start(bf16[2,128,384]{2,1,0:T(8,128)(2,1)S(1)} %get-tuple-element.61), channel_id=1, source_target_pairs={{0,2},{2,0},{4,6},{6,4},{1,3},{3,1},{5,7},{7,5},{8,10},{10,8},{12,... | collective-permute-start | bytes 589832 | tf_op jit(solution)/shard_map/ppermute | solution.py:471
  14.2 16.9 %collective-permute-start = (bf16[3,128,256]{2,1,0:T(8,128)(2,1)}, bf16[3,128,256]{2,1,0:T(8,128)(2,1)S(1)}, u32[]{:S(2)}, u32[]{:S(2)}) collective-permute-start(bf16[3,128,256]{2,1,0:T(8,128)(2,1)} %get-tuple-element.58), channel_id=1, source_target_pairs={{0,2},{2,0},{4,6},{6,4},{1,3},{3,1},{5,7},{7,5},{8,10},{10,8},{12,... | collective-permute-start | bytes 589832 | tf_op jit(solution)/shard_map/ppermute | solution.py:471
  15.7 21.8 %collective-permute-start.4 = (bf16[3,128,256]{2,1,0:T(8,128)(2,1)}, bf16[3,128,256]{2,1,0:T(8,128)(2,1)}, u32[]{:S(2)}, u32[]{:S(2)}) collective-permute-start(bf16[3,128,256]{2,1,0:T(8,128)(2,1)} %get-tuple-element.75), channel_id=1, source_target_pairs={{0,4},{2,6},{4,0},{6,2},{1,5},{3,7},{5,1},{7,3},{8,12},{10,14},{12... | collective-permute-start | bytes 589832 | tf_op jit(solution)/shard_map/ppermute | solution.py:471
  18.6 18.9 %collective-permute-start.5 = (bf16[3,128,256]{2,1,0:T(8,128)(2,1)}, bf16[3,128,256]{2,1,0:T(8,128)(2,1)}, u32[]{:S(2)}, u32[]{:S(2)}) collective-permute-start(bf16[3,128,256]{2,1,0:T(8,128)(2,1)} %get-tuple-element.76), channel_id=1, source_target_pairs={{0,6},{2,4},{4,2},{6,0},{1,7},{3,5},{5,3},{7,1},{8,14},{10,12},{12... | collective-permute-start | bytes 589832 | tf_op jit(solution)/shard_map/ppermute | solution.py:471
  26.9 0.8 %copy-start = (bf16[6,3,128,128]{3,2,1,0:T(8,128)(2,1)}, bf16[6,3,128,128]{3,2,1,0:T(8,128)(2,1)S(1)}, u32[]{:S(2)}) copy-start(bf16[6,3,128,128]{3,2,1,0:T(8,128)(2,1)S(1)} %get-tuple-element.70.refs_0_) | copy-start | bytes 1769476
  27.7 9.8 %collective-permute-start.6 = (bf16[2,3,128,128]{3,2,1,0:T(8,128)(2,1)}, bf16[2,3,128,128]{3,2,1,0:T(8,128)(2,1)}, u32[]{:S(2)}, u32[]{:S(2)}) collective-permute-start(bf16[2,3,128,128]{3,2,1,0:T(8,128)(2,1)} %get-tuple-element.79), channel_id=1, source_target_pairs={{0,1},{1,0},{2,3},{3,2},{4,5},{5,4},{6,7},{7,6},{8,9},{9,8},{10,11... | collective-permute-start | bytes 589832 | tf_op jit(solution)/shard_map/ppermute | solution.py:471
  29.5 8.1 %collective-permute-start.7 = (bf16[2,3,128,128]{3,2,1,0:T(8,128)(2,1)}, bf16[2,3,128,128]{3,2,1,0:T(8,128)(2,1)}, u32[]{:S(2)}, u32[]{:S(2)}) collective-permute-start(bf16[2,3,128,128]{3,2,1,0:T(8,128)(2,1)} %get-tuple-element.80), channel_id=1, source_target_pairs={{0,1},{1,0},{2,3},{3,2},{4,5},{5,4},{6,7},{7,6},{8,9},{9,8},{10,11... | collective-permute-start | bytes 589832 | tf_op jit(solution)/shard_map/ppermute | solution.py:471
  41.2 6.3 %collective-permute-start.9 = (f32[8,128]{1,0:T(8,128)S(1)}, f32[8,128]{1,0:T(8,128)S(1)}, u32[]{:S(2)}, u32[]{:S(2)}) collective-permute-start(f32[8,128]{1,0:T(8,128)S(1)} %get-tuple-element.82), channel_id=1, source_target_pairs={{0,8},{8,0},{16,24},{24,16},{1,9},{9,1},{17,25},{25,17},{2,10},{10... | collective-permute-start | bytes 12296 | tf_op jit(solution)/shard_map/ppermute | solution.py:471
  41.2 24.5 %collective-permute-start.8 = (bf16[3,128,256]{2,1,0:T(8,128)(2,1)S(1)}, bf16[3,128,256]{2,1,0:T(8,128)(2,1)S(1)}, u32[]{:S(2)}, u32[]{:S(2)}) collective-permute-start(bf16[3,128,256]{2,1,0:T(8,128)(2,1)S(1)} %get-tuple-element.81), channel_id=1, source_target_pairs={{0,4},{2,6},{4,0},{6,2},{1,5},{3,7},{5,1},{7,3},{8,12},{10,14},{12... | collective-permute-start | bytes 589832 | tf_op jit(solution)/shard_map/ppermute | solution.py:471
  46.1 17.5 %collective-permute-start.15 = (bf16[3,128,256]{2,1,0:T(8,128)(2,1)S(1)}, bf16[3,128,256]{2,1,0:T(8,128)(2,1)S(1)}, u32[]{:S(2)}, u32[]{:S(2)}) collective-permute-start(bf16[3,128,256]{2,1,0:T(8,128)(2,1)S(1)} %get-tuple-element.92), channel_id=1, source_target_pairs={{0,6},{2,4},{4,2},{6,0},{1,7},{3,5},{5,3},{7,1},{8,14},{10,12},{12... | collective-permute-start | bytes 589832 | tf_op jit(solution)/shard_map/ppermute | solution.py:471
  47.5 14.1 %collective-permute-start.11 = (bf16[3,128,256]{2,1,0:T(8,128)(2,1)S(1)}, bf16[3,128,256]{2,1,0:T(8,128)(2,1)S(1)}, u32[]{:S(2)}, u32[]{:S(2)}) collective-permute-start(bf16[3,128,256]{2,1,0:T(8,128)(2,1)S(1)} %get-tuple-element.90), channel_id=1, source_target_pairs={{0,2},{2,0},{4,6},{6,4},{1,3},{3,1},{5,7},{7,5},{8,10},{10,8},{12,... | collective-permute-start | bytes 589832 | tf_op jit(solution)/shard_map/ppermute | solution.py:471
  47.5 3.7 %collective-permute-start.10 = (f32[16,128]{1,0:T(8,128)S(1)}, f32[16,128]{1,0:T(8,128)S(1)}, u32[]{:S(2)}, u32[]{:S(2)}) collective-permute-start(f32[16,128]{1,0:T(8,128)S(1)} %pad_maximum_fusion.1), channel_id=1, source_target_pairs={{0,16},{8,24},{16,0},{24,8},{1,17},{9,25},{17,1},{25,9},{2,18},{10... | collective-permute-start | bytes 24584 | tf_op jit(solution)/shard_map/ppermute | solution.py:471
  51.2 13.9 %collective-permute-start.14 = (f32[32,128]{1,0:T(8,128)S(1)}, f32[32,128]{1,0:T(8,128)S(1)}, u32[]{:S(2)}, u32[]{:S(2)}) collective-permute-start(f32[32,128]{1,0:T(8,128)S(1)} %pad_maximum_fusion.refs_5_), channel_id=1, source_target_pairs={{0,6},{2,4},{4,2},{6,0},{1,7},{3,5},{5,3},{7,1},{8,14},{10,12},{12... | collective-permute-start | bytes 49160 | tf_op jit(solution)/shard_map/ppermute | solution.py:471
  53.7 12.0 %collective-permute-start.13 = (f32[32,128]{1,0:T(8,128)S(1)}, f32[32,128]{1,0:T(8,128)S(1)}, u32[]{:S(2)}, u32[]{:S(2)}) collective-permute-start(f32[32,128]{1,0:T(8,128)S(1)} %pad_maximum_fusion.refs_5_), channel_id=1, source_target_pairs={{0,4},{2,6},{4,0},{6,2},{1,5},{3,7},{5,1},{7,3},{8,12},{10,14},{12... | collective-permute-start | bytes 49160 | tf_op jit(solution)/shard_map/ppermute | solution.py:471
  61.6 4.1 %collective-permute-start.12 = (f32[32,128]{1,0:T(8,128)S(1)}, f32[32,128]{1,0:T(8,128)S(1)}, u32[]{:S(2)}, u32[]{:S(2)}) collective-permute-start(f32[32,128]{1,0:T(8,128)S(1)} %pad_maximum_fusion.refs_5_), channel_id=1, source_target_pairs={{0,2},{2,0},{4,6},{6,4},{1,3},{3,1},{5,7},{7,5},{8,10},{10,8},{12,... | collective-permute-start | bytes 49160 | tf_op jit(solution)/shard_map/ppermute | solution.py:471

commit v20 on v15

--- a/solution.py
+++ b/solution.py
@@ -88,60 +88,52 @@
     return weights, attended
 
 
-def backward_group(axis, fields, weights_ref, grad_ref, distance, scratch, results, sent):
-    query_ref, key_ref, value_ref = fields
+def backward_kernel(axis, distances, gains_of, *refs):
+    (query_ref, key_ref, value_ref), weights_ref, refs = refs[:3], refs[3], refs[4:]
+    grad_refs, refs = refs[: len(distances)], refs[len(distances) :]
+    *refs, gq, gk, sent = refs
     score_scale = HEAD_DIM ** (-0.5)
-    own = grad_ref.shape[0]
-    start = partner(axis, distance) * (own * HEAD_DIM)
+    own = grad_refs[0].shape[0]
+    copies = []
+
+    def send(source, target, semaphore):
+        copy = pltpu.make_async_copy(source, target, semaphore)
+        copy.start()
+        copies.append(copy)
+
+    if gains_of:
+        *mixed_refs, gains_ref, _, _, gq_ref, gk_ref, grad_gains_ref, grad_gains = refs
+        gain_gradients(axis, *gains_of, mixed_refs, gains_ref, grad_gains)
+        send(grad_gains, grad_gains_ref, sent.at[len(distances), 0])
+    else:
+        gq_ref, gk_ref = refs[-2:]
+    starts = [partner(axis, distance) * (own * HEAD_DIM) for distance in distances]
+    heads = [(group, head) for group in range(len(distances)) for head in range(own)]
     columns = [
-        pl.ds(pl.multiple_of(start + head * HEAD_DIM, HEAD_DIM), HEAD_DIM) for head in range(own)
+        pl.ds(pl.multiple_of(starts[group] + head * HEAD_DIM, HEAD_DIM), HEAD_DIM)
+        for group, head in heads
     ]
-    spatial_grads = [dot(value_ref[:, columns[head]], grad_ref[head]) for head in range(own)]
+    spatial_grads = [
+        dot(value_ref[:, cols], grad_refs[group][head])
+        for cols, (group, head) in zip(columns, heads)
+    ]
     all_scores = []
-    for head, spatial_grad in enumerate(spatial_grads):
-        weights = weights_ref[distance * own + head]
+    for spatial_grad, (group, head) in zip(spatial_grads, heads):
+        weights = weights_ref[distances[group] * own + head]
         row_sum = jnp.sum(spatial_grad * weights, axis=0, keepdims=True)
         scores = weights * (spatial_grad - row_sum) * score_scale
         all_scores.append(scores.astype(jnp.bfloat16))
-    gq, gk = scratch
-    for head, scores in enumerate(all_scores):
-        cols = pl.ds(head * HEAD_DIM, HEAD_DIM)
-        gk[:, cols] = dot(scores, query_ref[:, columns[head]]).astype(jnp.bfloat16)
-        gq[:, cols] = dot(key_ref[:, columns[head]].T, scores).astype(jnp.bfloat16).T
-    there = pl.ds(pl.multiple_of(start, HEAD_DIM), own * HEAD_DIM)
-    copies = [
-        pltpu.make_async_copy(source, target.at[:, there], sent.at[side])
-        for side, (source, target) in enumerate(zip(scratch, results))
-    ]
-    for copy in copies:
-        copy.start()
-    return copies
-
-
-def backward_kernel(axis, distances, gains_of, *refs):
-    fields, weights_ref, refs = refs[:3], refs[3], refs[4:]
-    grad_refs, refs = refs[: len(distances)], refs[len(distances) :]
-    *refs, gq, gk, sent = refs
-    copies = []
-    if gains_of:
-        *mixed_refs, gains_ref, _, _, gq_ref, gk_ref, grad_gains_ref, grad_gains = refs
-        gain_gradients(axis, *gains_of, mixed_refs, gains_ref, grad_gains)
-        copy = pltpu.make_async_copy(grad_gains, grad_gains_ref, sent.at[len(distances), 0])
-        copy.start()
-        copies.append(copy)
-    else:
-        gq_ref, gk_ref = refs[-2:]
-    for place, (distance, grad_ref) in enumerate(zip(distances, grad_refs)):
-        copies += backward_group(
-            axis,
-            fields,
-            weights_ref,
-            grad_ref,
-            distance,
-            (gq.at[place], gk.at[place]),
-            (gq_ref, gk_ref),
-            sent.at[place],
-        )
+    there = [pl.ds(pl.multiple_of(start, HEAD_DIM), own * HEAD_DIM) for start in starts]
+    for scores, cols, (group, head) in zip(all_scores, columns, heads):
+        here = pl.ds(head * HEAD_DIM, HEAD_DIM)
+        gk[group, :, here] = dot(scores, query_ref[:, cols]).astype(jnp.bfloat16)
+    for group, cols in enumerate(there):
+        send(gk.at[group], gk_ref.at[:, cols], sent.at[group, 1])
+    for scores, cols, (group, head) in zip(all_scores, columns, heads):
+        here = pl.ds(head * HEAD_DIM, HEAD_DIM)
+        gq[group, :, here] = dot(key_ref[:, cols].T, scores).astype(jnp.bfloat16).T
+    for group, cols in enumerate(there):
+        send(gq.at[group], gq_ref.at[:, cols], sent.at[group, 0])
     for copy in copies:
         copy.wait()
 

time: 66.7 us -> 66.5 us (level)
  no operation moved by 1% of the time
where the time goes in v20:
time: 66.5 us; the launch traced here: 66.3 us
  starting transfers between devices  25.1 us (38%)
  Pallas kernels  19.2 us (29%)
  waiting for transfers between devices  18.9 us (28%)
  between operations  2.07 us (3%)
  local copies, waits for them, and re-layouts  0.92 us (1%)
    ppermute x16, starting transfers between devices, swap(): return lax.ppermute(field, axis, [(i, i ^ distance) for i in range(size)])  25.1 us
    ppermute x16, waiting for transfers between devices, swap(): return lax.ppermute(field, axis, [(i, i ^ distance) for i in range(size)])  18.9 us
    pallas_call x1, Pallas kernels, forward(): pl.pallas_call(functools.partial(forward_kernel, axis), in_specs=[pl.Bloc...  6.52 us
    pallas_call x3, Pallas kernels, backward(): pl.pallas_call(functools.partial(backward_kernel, axis, distances, gains_...  4.63 us
    pallas_call x1, Pallas kernels, temporal(): pl.pallas_call(functools.partial(temporal_kernel, frames, spaces), in_spe...  3.62 us
    pallas_call x1, Pallas kernels, fetch(): pl.pallas_call(fetch_kernel, in_specs=[pl.BlockSpec(memory_space=pltpu.HB...  1.83 us
  transfers between devices with their start and end apart: 16, of which 5 were waited for; matrix products, arithmetic and copies ran while one was open for 0% of the time, Pallas kernels for 19%

profile of v20, /device:TPU:0, one launch (start us, length us, event | category | flops | bytes accessed | tf_op | source)
XLA Modules:
  0.0 66.3 jit_solution(7432126909260559878)
XLA Ops:
  0.6 1.3 %pack_cotangent.1 = (bf16[2,128,384]{2,1,0:T(8,128)(2,1)S(1)}, bf16[2,128,384]{2,1,0:T(8,128)(2,1)S(1)}, bf16[2,128,384]{2,1,0:T(8,128)(2,1)S(1)}, bf16[2,128,384]{2,1,0:T(8,128)(2,1)S(1)}) custom-call(bf16[128,3072]{1,0:T(8,128)(2,1)} %bitcast.19), custom_call_target="tpu_custom_call" | custom-call | flops 100000000 | tf_op jit(solution)/shard_map/pack_cotangent/pallas_call | solution.py:190
  2.0 5.1 %collective-permute-start.1 = (bf16[2,128,384]{2,1,0:T(8,128)(2,1)S(1)}, bf16[2,128,384]{2,1,0:T(8,128)(2,1)S(1)}, u32[]{:S(2)}, u32[]{:S(2)}) collective-permute-start(bf16[2,128,384]{2,1,0:T(8,128)(2,1)S(1)} %get-tuple-element.56), channel_id=1, source_target_pairs={{0,6},{2,4},{4,2},{6,0},{1,7},{3,5},{5,3},{7,1},{8,14},{10,12},{12... | collective-permute-start | bytes 589832 | tf_op jit(solution)/shard_map/ppermute | solution.py:463
  7.7 6.5 %spatial_forward.1 = (f32[12,256,256]{2,1,0:T(8,128)S(1)}, bf16[3,128,256]{2,1,0:T(8,128)(2,1)S(1)}, bf16[3,128,256]{2,1,0:T(8,128)(2,1)}, bf16[3,128,256]{2,1,0:T(8,128)(2,1)}, bf16[3,128,256]{2,1,0:T(8,128)(2,1)}) custom-call(bf16[256,1536]{1,0:T(8,128)(2,1)} %bitcast.13, bf16[256,1536]{1,0:T(8,128)(2,1)} %bitcast.15, bf16[256,1536]{1,0:T(8,128)(2,1)} %bitcast.17), custom_call_target="tpu_custom_call" | custom-call | flops 600000000 | tf_op jit(solution)/shard_map/spatial_forward/pallas_call | solution.py:76
  14.3 1.4 %collective-permute-start = (bf16[3,128,256]{2,1,0:T(8,128)(2,1)}, bf16[3,128,256]{2,1,0:T(8,128)(2,1)S(1)}, u32[]{:S(2)}, u32[]{:S(2)}) collective-permute-start(bf16[3,128,256]{2,1,0:T(8,128)(2,1)} %get-tuple-element.55), channel_id=1, source_target_pairs={{0,2},{2,0},{4,6},{6,4},{1,3},{3,1},{5,7},{7,5},{8,10},{10,8},{12,... | collective-permute-start | bytes 589832 | tf_op jit(solution)/shard_map/ppermute | solution.py:463
  15.7 2.9 %collective-permute-start.4 = (bf16[3,128,256]{2,1,0:T(8,128)(2,1)}, bf16[3,128,256]{2,1,0:T(8,128)(2,1)}, u32[]{:S(2)}, u32[]{:S(2)}) collective-permute-start(bf16[3,128,256]{2,1,0:T(8,128)(2,1)} %get-tuple-element.72), channel_id=1, source_target_pairs={{0,4},{2,6},{4,0},{6,2},{1,5},{3,7},{5,1},{7,3},{8,12},{10,14},{12... | collective-permute-start | bytes 589832 | tf_op jit(solution)/shard_map/ppermute | solution.py:463
  18.7 6.9 %collective-permute-done.2.refs_1_ = bf16[2,128,384]{2,1,0:T(8,128)(2,1)S(1)} collective-permute-done((bf16[2,128,384]{2,1,0:T(8,128)(2,1)S(1)}, bf16[2,128,384]{2,1,0:T(8,128)(2,1)S(1)}, u32[]{:S(2)}, u32[]{:S(2)}) %collective-permute-start.2) | collective-permute-done | bytes 196640 | tf_op jit(solution)/shard_map/ppermute | solution.py:463
  25.6 1.3 %turn_cotangent.1 = (bf16[6,3,128,128]{3,2,1,0:T(8,128)(2,1)S(1)}, bf16[2,3,128,128]{3,2,1,0:T(8,128)(2,1)}, bf16[2,3,128,128]{3,2,1,0:T(8,128)(2,1)}) custom-call(bf16[2,128,384]{2,1,0:T(8,128)(2,1)S(1)} %collective-permute-done.1.refs_0_, bf16[2,128,384]{2,1,0:T(8,128)(2,1)S(1)} %collective-permute-done.2.refs_1_, ...), custom_call_target="tpu_custom_call" | custom-call | flops 200000000 | tf_op jit(solution)/shard_map/turn_cotangent/pallas_call | solution.py:239
  26.9 0.8 %copy-done = bf16[6,3,128,128]{3,2,1,0:T(8,128)(2,1)} copy-done((bf16[6,3,128,128]{3,2,1,0:T(8,128)(2,1)}, bf16[6,3,128,128]{3,2,1,0:T(8,128)(2,1)S(1)}, u32[]{:S(2)}) %copy-start) | copy-done | bytes 589848
  27.7 1.7 %collective-permute-start.6 = (bf16[2,3,128,128]{3,2,1,0:T(8,128)(2,1)}, bf16[2,3,128,128]{3,2,1,0:T(8,128)(2,1)}, u32[]{:S(2)}, u32[]{:S(2)}) collective-permute-start(bf16[2,3,128,128]{3,2,1,0:T(8,128)(2,1)} %get-tuple-element.76), channel_id=1, source_target_pairs={{0,1},{1,0},{2,3},{3,2},{4,5},{5,4},{6,7},{7,6},{8,9},{9,8},{10,11... | collective-permute-start | bytes 589832 | tf_op jit(solution)/shard_map/ppermute | solution.py:463
  31.3 1.8 %fetch.1 = (bf16[6,3,128,128]{3,2,1,0:T(8,128)(2,1)S(1)}, bf16[256,1536]{1,0:T(8,128)(2,1)S(1)}, bf16[256,1536]{1,0:T(8,128)(2,1)S(1)}, bf16[256,1536]{1,0:T(8,128)(2,1)S(1)}) custom-call(bf16[6,3,128,128]{3,2,1,0:T(8,128)(2,1)} %copy-done, bf16[256,1536]{1,0:T(8,128)(2,1)} %bitcast.14, bf16[256,1536]{1,0:T(8,128)(2,1)} %bitcast.16, bf16[256,1536]{1,0:T(8,128)(2,1)} %bitcast.18), custom_call_target="tpu_custom_call" | custom-call | flops 100000000 | tf_op jit(solution)/shard_map/fetch/pallas_call | solution.py:358
  33.1 4.4 %collective-permute-done.4.refs_1_ = bf16[3,128,256]{2,1,0:T(8,128)(2,1)} collective-permute-done((bf16[3,128,256]{2,1,0:T(8,128)(2,1)}, bf16[3,128,256]{2,1,0:T(8,128)(2,1)}, u32[]{:S(2)}, u32[]{:S(2)}) %collective-permute-start.4) | collective-permute-done | bytes 196640 | tf_op jit(solution)/shard_map/ppermute | solution.py:463
  37.5 3.6 %temporal.1 = (bf16[3,128,256]{2,1,0:T(8,128)(2,1)S(1)}, bf16[3,128,256]{2,1,0:T(8,128)(2,1)S(1)}, bf16[3,128,256]{2,1,0:T(8,128)(2,1)S(1)}, bf16[3,128,256]{2,1,0:T(8,128)(2,1)S(1)}, f32[8,128]{1,0:T(8,128)S(1)}) custom-call(s32[1]{0:T(128)S(6)} %copy.19.length_ref, s32[1]{0:T(128)} %copy.18.task_ref, ...), custom_call_target="tpu_custom_call" | custom-call | flops 400000000 | tf_op jit(solution)/shard_map/temporal/pallas_call | solution.py:423
  41.2 2.7 %collective-permute-start.8 = (bf16[3,128,256]{2,1,0:T(8,128)(2,1)S(1)}, bf16[3,128,256]{2,1,0:T(8,128)(2,1)S(1)}, u32[]{:S(2)}, u32[]{:S(2)}) collective-permute-start(bf16[3,128,256]{2,1,0:T(8,128)(2,1)S(1)} %get-tuple-element.78), channel_id=1, source_target_pairs={{0,6},{2,4},{4,2},{6,0},{1,7},{3,5},{5,3},{7,1},{8,14},{10,12},{12... | collective-permute-start | bytes 589832 | tf_op jit(solution)/shard_map/ppermute | solution.py:463
  44.0 2.6 %collective-permute-start.9 = (bf16[3,128,256]{2,1,0:T(8,128)(2,1)S(1)}, bf16[3,128,256]{2,1,0:T(8,128)(2,1)S(1)}, u32[]{:S(2)}, u32[]{:S(2)}) collective-permute-start(bf16[3,128,256]{2,1,0:T(8,128)(2,1)S(1)} %get-tuple-element.79), channel_id=1, source_target_pairs={{0,4},{2,6},{4,0},{6,2},{1,5},{3,7},{5,1},{7,3},{8,12},{10,14},{12... | collective-permute-start | bytes 589832 | tf_op jit(solution)/shard_map/ppermute | solution.py:463
  46.7 1.5 %collective-permute-start.11 = (f32[16,128]{1,0:T(8,128)S(1)}, f32[16,128]{1,0:T(8,128)S(1)}, u32[]{:S(2)}, u32[]{:S(2)}) collective-permute-start(f32[16,128]{1,0:T(8,128)S(1)} %pad_maximum_fusion.1), channel_id=1, source_target_pairs={{0,16},{8,24},{16,0},{24,8},{1,17},{9,25},{17,1},{25,9},{2,18},{10... | collective-permute-start | bytes 24584 | tf_op jit(solution)/shard_map/ppermute | solution.py:463
  48.2 1.4 %spatial_backward.3 = (bf16[256,1536]{1,0:T(8,128)(2,1)}, bf16[256,1536]{1,0:T(8,128)(2,1)}) custom-call(bf16[256,1536]{1,0:T(8,128)(2,1)S(1)} %get-tuple-element.68.refs_0_, bf16[256,1536]{1,0:T(8,128)(2,1)S(1)} %get-tuple-element.69.refs_1_, bf16[256,1536]{1,0:T(8,128)(2,1)S(1)} %get-tuple-element.70.refs_2_, ...), custom_call_target="tpu_custom_call" | custom-call | flops 200000000 | tf_op jit(solution)/shard_map/spatial_backward/pallas_call | solution.py:151
  49.6 0.8 %collective-permute-done.11 = f32[16,128]{1,0:T(8,128)S(1)} collective-permute-done((f32[16,128]{1,0:T(8,128)S(1)}, f32[16,128]{1,0:T(8,128)S(1)}, u32[]{:S(2)}, u32[]{:S(2)}) %collective-permute-start.11) | collective-permute-done | bytes 8224 | tf_op jit(solution)/shard_map/ppermute | solution.py:463
  50.4 2.4 %collective-permute-start.15 = (f32[32,128]{1,0:T(8,128)S(1)}, f32[32,128]{1,0:T(8,128)S(1)}, u32[]{:S(2)}, u32[]{:S(2)}) collective-permute-start(f32[32,128]{1,0:T(8,128)S(1)} %pad_maximum_fusion.refs_6_), channel_id=1, source_target_pairs={{0,6},{2,4},{4,2},{6,0},{1,7},{3,5},{5,3},{7,1},{8,14},{10,12},{12... | collective-permute-start | bytes 49160 | tf_op jit(solution)/shard_map/ppermute | solution.py:463
  52.8 0.9 %collective-permute-start.14 = (f32[32,128]{1,0:T(8,128)S(1)}, f32[32,128]{1,0:T(8,128)S(1)}, u32[]{:S(2)}, u32[]{:S(2)}) collective-permute-start(f32[32,128]{1,0:T(8,128)S(1)} %pad_maximum_fusion.refs_6_), channel_id=1, source_target_pairs={{0,4},{2,6},{4,0},{6,2},{1,5},{3,7},{5,1},{7,3},{8,12},{10,14},{12... | collective-permute-start | bytes 49160 | tf_op jit(solution)/shard_map/ppermute | solution.py:463
  53.7 3.9 %collective-permute-done.12.refs_4_ = bf16[3,128,256]{2,1,0:T(8,128)(2,1)S(1)} collective-permute-done((bf16[3,128,256]{2,1,0:T(8,128)(2,1)S(1)}, bf16[3,128,256]{2,1,0:T(8,128)(2,1)S(1)}, u32[]{:S(2)}, u32[]{:S(2)}) %collective-permute-start.12) | collective-permute-done | bytes 196640 | tf_op jit(solution)/shard_map/ppermute | solution.py:463
  57.6 2.5 %collective-permute-start.13 = (f32[32,128]{1,0:T(8,128)S(1)}, f32[32,128]{1,0:T(8,128)S(1)}, u32[]{:S(2)}, u32[]{:S(2)}) collective-permute-start(f32[32,128]{1,0:T(8,128)S(1)} %pad_maximum_fusion.refs_6_), channel_id=1, source_target_pairs={{0,2},{2,0},{4,6},{6,4},{1,3},{3,1},{5,7},{7,5},{8,10},{10,8},{12,... | collective-permute-start | bytes 49160 | tf_op jit(solution)/shard_map/ppermute | solution.py:463
  60.1 1.4 %spatial_backward.4 = (bf16[256,1536]{1,0:T(8,128)(2,1)}, bf16[256,1536]{1,0:T(8,128)(2,1)}) custom-call(bf16[256,1536]{1,0:T(8,128)(2,1)S(1)} %get-tuple-element.68.refs_0_, bf16[256,1536]{1,0:T(8,128)(2,1)S(1)} %get-tuple-element.69.refs_1_, bf16[256,1536]{1,0:T(8,128)(2,1)S(1)} %get-tuple-element.70.refs_2_, ...), custom_call_target="tpu_custom_call", output_to_operand_aliasing={{0}: (5, {}), {1}: (6, {})} | custom-call | flops 200000000 | tf_op jit(solution)/shard_map/spatial_backward/pallas_call | solution.py:151
  61.5 3.0 %collective-permute-done.14.refs_8_ = f32[32,128]{1,0:T(8,128)S(1)} collective-permute-done((f32[32,128]{1,0:T(8,128)S(1)}, f32[32,128]{1,0:T(8,128)S(1)}, u32[]{:S(2)}, u32[]{:S(2)}) %collective-permute-start.14) | collective-permute-done | bytes 16416 | tf_op jit(solution)/shard_map/ppermute | solution.py:463
  64.5 1.8 %spatial_backward.5 = (bf16[256,1536]{1,0:T(8,128)(2,1)}, bf16[256,1536]{1,0:T(8,128)(2,1)}, f32[2,16,1536]{2,1,0:T(8,128)}) custom-call(bf16[256,1536]{1,0:T(8,128)(2,1)S(1)} %get-tuple-element.68.refs_0_, bf16[256,1536]{1,0:T(8,128)(2,1)S(1)} %get-tuple-element.69.refs_1_, ...), custom_call_target="tpu_custom_call", output_to_operand_aliasing={{0}: (11, {}), {1}: (12, {})} | custom-call | flops 200000000 | tf_op jit(solution)/shard_map/spatial_backward/pallas_call | solution.py:151
  (24 shorter events, 1.5 us)
Async XLA Ops:
  0.6 30.4 %copy-start.1 = (f32[2,16,1536]{2,1,0:T(8,128)S(1)}, f32[2,16,1536]{2,1,0:T(8,128)}, u32[]{:S(2)}) copy-start(f32[2,16,1536]{2,1,0:T(8,128)} %refs_10_.1) | copy-start | bytes 589828
  2.0 16.7 %collective-permute-start.1 = (bf16[2,128,384]{2,1,0:T(8,128)(2,1)S(1)}, bf16[2,128,384]{2,1,0:T(8,128)(2,1)S(1)}, u32[]{:S(2)}, u32[]{:S(2)}) collective-permute-start(bf16[2,128,384]{2,1,0:T(8,128)(2,1)S(1)} %get-tuple-element.56), channel_id=1, source_target_pairs={{0,6},{2,4},{4,2},{6,0},{1,7},{3,5},{5,3},{7,1},{8,14},{10,12},{12... | collective-permute-start | bytes 589832 | tf_op jit(solution)/shard_map/ppermute | solution.py:463
  7.1 18.5 %collective-permute-start.2 = (bf16[2,128,384]{2,1,0:T(8,128)(2,1)S(1)}, bf16[2,128,384]{2,1,0:T(8,128)(2,1)S(1)}, u32[]{:S(2)}, u32[]{:S(2)}) collective-permute-start(bf16[2,128,384]{2,1,0:T(8,128)(2,1)S(1)} %get-tuple-element.57), channel_id=1, source_target_pairs={{0,4},{2,6},{4,0},{6,2},{1,5},{3,7},{5,1},{7,3},{8,12},{10,14},{12... | collective-permute-start | bytes 589832 | tf_op jit(solution)/shard_map/ppermute | solution.py:463
  7.1 18.5 %collective-permute-start.3 = (bf16[2,128,384]{2,1,0:T(8,128)(2,1)S(1)}, bf16[2,128,384]{2,1,0:T(8,128)(2,1)S(1)}, u32[]{:S(2)}, u32[]{:S(2)}) collective-permute-start(bf16[2,128,384]{2,1,0:T(8,128)(2,1)S(1)} %get-tuple-element.58), channel_id=1, source_target_pairs={{0,2},{2,0},{4,6},{6,4},{1,3},{3,1},{5,7},{7,5},{8,10},{10,8},{12,... | collective-permute-start | bytes 589832 | tf_op jit(solution)/shard_map/ppermute | solution.py:463
  14.3 16.9 %collective-permute-start = (bf16[3,128,256]{2,1,0:T(8,128)(2,1)}, bf16[3,128,256]{2,1,0:T(8,128)(2,1)S(1)}, u32[]{:S(2)}, u32[]{:S(2)}) collective-permute-start(bf16[3,128,256]{2,1,0:T(8,128)(2,1)} %get-tuple-element.55), channel_id=1, source_target_pairs={{0,2},{2,0},{4,6},{6,4},{1,3},{3,1},{5,7},{7,5},{8,10},{10,8},{12,... | collective-permute-start | bytes 589832 | tf_op jit(solution)/shard_map/ppermute | solution.py:463
  15.7 21.8 %collective-permute-start.4 = (bf16[3,128,256]{2,1,0:T(8,128)(2,1)}, bf16[3,128,256]{2,1,0:T(8,128)(2,1)}, u32[]{:S(2)}, u32[]{:S(2)}) collective-permute-start(bf16[3,128,256]{2,1,0:T(8,128)(2,1)} %get-tuple-element.72), channel_id=1, source_target_pairs={{0,4},{2,6},{4,0},{6,2},{1,5},{3,7},{5,1},{7,3},{8,12},{10,14},{12... | collective-permute-start | bytes 589832 | tf_op jit(solution)/shard_map/ppermute | solution.py:463
  18.6 18.9 %collective-permute-start.5 = (bf16[3,128,256]{2,1,0:T(8,128)(2,1)}, bf16[3,128,256]{2,1,0:T(8,128)(2,1)}, u32[]{:S(2)}, u32[]{:S(2)}) collective-permute-start(bf16[3,128,256]{2,1,0:T(8,128)(2,1)} %get-tuple-element.73), channel_id=1, source_target_pairs={{0,6},{2,4},{4,2},{6,0},{1,7},{3,5},{5,3},{7,1},{8,14},{10,12},{12... | collective-permute-start | bytes 589832 | tf_op jit(solution)/shard_map/ppermute | solution.py:463
  26.9 0.8 %copy-start = (bf16[6,3,128,128]{3,2,1,0:T(8,128)(2,1)}, bf16[6,3,128,128]{3,2,1,0:T(8,128)(2,1)S(1)}, u32[]{:S(2)}) copy-start(bf16[6,3,128,128]{3,2,1,0:T(8,128)(2,1)S(1)} %get-tuple-element.67.refs_0_) | copy-start | bytes 1769476
  27.7 9.8 %collective-permute-start.6 = (bf16[2,3,128,128]{3,2,1,0:T(8,128)(2,1)}, bf16[2,3,128,128]{3,2,1,0:T(8,128)(2,1)}, u32[]{:S(2)}, u32[]{:S(2)}) collective-permute-start(bf16[2,3,128,128]{3,2,1,0:T(8,128)(2,1)} %get-tuple-element.76), channel_id=1, source_target_pairs={{0,1},{1,0},{2,3},{3,2},{4,5},{5,4},{6,7},{7,6},{8,9},{9,8},{10,11... | collective-permute-start | bytes 589832 | tf_op jit(solution)/shard_map/ppermute | solution.py:463
  29.5 8.1 %collective-permute-start.7 = (bf16[2,3,128,128]{3,2,1,0:T(8,128)(2,1)}, bf16[2,3,128,128]{3,2,1,0:T(8,128)(2,1)}, u32[]{:S(2)}, u32[]{:S(2)}) collective-permute-start(bf16[2,3,128,128]{3,2,1,0:T(8,128)(2,1)} %get-tuple-element.77), channel_id=1, source_target_pairs={{0,1},{1,0},{2,3},{3,2},{4,5},{5,4},{6,7},{7,6},{8,9},{9,8},{10,11... | collective-permute-start | bytes 589832 | tf_op jit(solution)/shard_map/ppermute | solution.py:463
  41.2 5.5 %collective-permute-start.10 = (f32[8,128]{1,0:T(8,128)S(1)}, f32[8,128]{1,0:T(8,128)S(1)}, u32[]{:S(2)}, u32[]{:S(2)}) collective-permute-start(f32[8,128]{1,0:T(8,128)S(1)} %get-tuple-element.80), channel_id=1, source_target_pairs={{0,8},{8,0},{16,24},{24,16},{1,9},{9,1},{17,25},{25,17},{2,10},{10... | collective-permute-start | bytes 12296 | tf_op jit(solution)/shard_map/ppermute | solution.py:463
  41.2 23.2 %collective-permute-start.8 = (bf16[3,128,256]{2,1,0:T(8,128)(2,1)S(1)}, bf16[3,128,256]{2,1,0:T(8,128)(2,1)S(1)}, u32[]{:S(2)}, u32[]{:S(2)}) collective-permute-start(bf16[3,128,256]{2,1,0:T(8,128)(2,1)S(1)} %get-tuple-element.78), channel_id=1, source_target_pairs={{0,6},{2,4},{4,2},{6,0},{1,7},{3,5},{5,3},{7,1},{8,14},{10,12},{12... | collective-permute-start | bytes 589832 | tf_op jit(solution)/shard_map/ppermute | solution.py:463
  44.0 20.5 %collective-permute-start.9 = (bf16[3,128,256]{2,1,0:T(8,128)(2,1)S(1)}, bf16[3,128,256]{2,1,0:T(8,128)(2,1)S(1)}, u32[]{:S(2)}, u32[]{:S(2)}) collective-permute-start(bf16[3,128,256]{2,1,0:T(8,128)(2,1)S(1)} %get-tuple-element.79), channel_id=1, source_target_pairs={{0,4},{2,6},{4,0},{6,2},{1,5},{3,7},{5,1},{7,3},{8,12},{10,14},{12... | collective-permute-start | bytes 589832 | tf_op jit(solution)/shard_map/ppermute | solution.py:463
  46.6 11.0 %collective-permute-start.12 = (bf16[3,128,256]{2,1,0:T(8,128)(2,1)S(1)}, bf16[3,128,256]{2,1,0:T(8,128)(2,1)S(1)}, u32[]{:S(2)}, u32[]{:S(2)}) collective-permute-start(bf16[3,128,256]{2,1,0:T(8,128)(2,1)S(1)} %get-tuple-element.87), channel_id=1, source_target_pairs={{0,2},{2,0},{4,6},{6,4},{1,3},{3,1},{5,7},{7,5},{8,10},{10,8},{12,... | collective-permute-start | bytes 589832 | tf_op jit(solution)/shard_map/ppermute | solution.py:463
  46.7 3.7 %collective-permute-start.11 = (f32[16,128]{1,0:T(8,128)S(1)}, f32[16,128]{1,0:T(8,128)S(1)}, u32[]{:S(2)}, u32[]{:S(2)}) collective-permute-start(f32[16,128]{1,0:T(8,128)S(1)} %pad_maximum_fusion.1), channel_id=1, source_target_pairs={{0,16},{8,24},{16,0},{24,8},{1,17},{9,25},{17,1},{25,9},{2,18},{10... | collective-permute-start | bytes 24584 | tf_op jit(solution)/shard_map/ppermute | solution.py:463
  50.4 11.1 %collective-permute-start.15 = (f32[32,128]{1,0:T(8,128)S(1)}, f32[32,128]{1,0:T(8,128)S(1)}, u32[]{:S(2)}, u32[]{:S(2)}) collective-permute-start(f32[32,128]{1,0:T(8,128)S(1)} %pad_maximum_fusion.refs_6_), channel_id=1, source_target_pairs={{0,6},{2,4},{4,2},{6,0},{1,7},{3,5},{5,3},{7,1},{8,14},{10,12},{12... | collective-permute-start | bytes 49160 | tf_op jit(solution)/shard_map/ppermute | solution.py:463
  52.8 11.6 %collective-permute-start.14 = (f32[32,128]{1,0:T(8,128)S(1)}, f32[32,128]{1,0:T(8,128)S(1)}, u32[]{:S(2)}, u32[]{:S(2)}) collective-permute-start(f32[32,128]{1,0:T(8,128)S(1)} %pad_maximum_fusion.refs_6_), channel_id=1, source_target_pairs={{0,4},{2,6},{4,0},{6,2},{1,5},{3,7},{5,1},{7,3},{8,12},{10,14},{12... | collective-permute-start | bytes 49160 | tf_op jit(solution)/shard_map/ppermute | solution.py:463
  57.6 6.9 %collective-permute-start.13 = (f32[32,128]{1,0:T(8,128)S(1)}, f32[32,128]{1,0:T(8,128)S(1)}, u32[]{:S(2)}, u32[]{:S(2)}) collective-permute-start(f32[32,128]{1,0:T(8,128)S(1)} %pad_maximum_fusion.refs_6_), channel_id=1, source_target_pairs={{0,2},{2,0},{4,6},{6,4},{1,3},{3,1},{5,7},{7,5},{8,10},{10,8},{12,... | collective-permute-start | bytes 49160 | tf_op jit(solution)/shard_map/ppermute | solution.py:463

commit v21 on v20

--- a/solution.py
+++ b/solution.py
@@ -253,7 +253,7 @@
     )(*reversed(pieces), plane)
 
 
-def temporal_part(length, load_attended, load_upstream, load_gain, fields, ups, normed, grad_ref):
+def temporal_part(length, load_upstream, load_gain, fields, ups, normed, grad_ref):
     frames, feat, lanes = grad_ref.shape
     half = GROUP // 2
     score_scale = feat ** (-0.5)
@@ -269,8 +269,7 @@
     for group in range(feat // GROUP):
         rows = pl.ds(group * GROUP, GROUP)
         for t in every:
-            field = load_attended(t, rows).astype(jnp.float32)
-            fields[t, rows, :] = field
+            field = fields[t, rows, :]
             ups[t, rows, :] = load_upstream(t, rows).astype(jnp.float32)
             low, high = field[:half], field[half:]
             squares[t] = squares[t] + (low * low + high * high)
@@ -312,9 +311,12 @@
     both.update({(u, t): both[t, u] for t, u in pairs})
     raw.update({(u, t): raw[t, u] for t, u in pairs})
     mean_part = [
-        functools.reduce(jnp.add, [both[u, v] * raw[u, v] for v in every]) * (1.0 / feat)
+        functools.reduce(jnp.add, [both[u, v] * raw[u, v] for v in every])
+        * (1.0 / feat)
+        * inverse[u]
         for u in every
     ]
+    both = {(u, v): both[u, v] * inverse[u] for u in every for v in every}
 
     all_mixed = []
     for group in range(feat // GROUP):
@@ -322,13 +324,14 @@
         for side in range(2):
             rows = pl.ds(group * GROUP + side * half, half)
             gain = load_gain(rows)
+            here = [fields[t, rows, :] for t in every]
             scaled = [normed[t, rows, :] for t in every]
             above = [ups[t, rows, :] for t in every]
             mixed = jnp.zeros((half, lanes), jnp.float32)
             for u in every:
                 crossed = functools.reduce(jnp.add, [both[u, v] * scaled[v] for v in every])
-                mixed = mixed + crossed * scaled[u]
-                from_norm = inverse[u] * (gain * crossed - scaled[u] * mean_part[u])
+                mixed = mixed + crossed * here[u]
+                from_norm = gain * crossed - scaled[u] * mean_part[u]
                 direct = functools.reduce(
                     jnp.add, [value_part[t, u] * above[t] for t in range(u, frames)]
                 )
@@ -373,7 +376,7 @@
         refs[frames - 1 : frames - 1 + 2 * spaces],
         refs[frames - 1 + 2 * spaces :],
     )
-    grad_refs, (mixed_ref, attended, grads, wide) = refs[:frames], refs[frames:]
+    grad_refs, (mixed_ref, grads, wide) = refs[:frames], refs[frames:]
     heads, lanes = own_ref.shape[1], own_ref.shape[3]
     half = frames // 2
     mixed_ref[...] = jnp.full(mixed_ref.shape, task_ref[0].astype(jnp.float32))
@@ -389,18 +392,19 @@
     ]
     for head in range(heads):
         for space, here in enumerate(places):
-            attended[head, space, partner("tm", 0)] = own_ref[frames + space, head]
+            fields = wide.at[head, space, 0]
+            fields[partner("tm", 0)] = own_ref[frames + space, head].astype(jnp.float32)
             for distance, ref in enumerate(attended_refs):
-                attended[head, space, partner("tm", distance + 1)] = ref[head, :, here]
+                plane = ref[head, :, here].astype(jnp.float32)
+                fields[partner("tm", distance + 1)] = plane
         mixed = [
             temporal_part(
                 length_ref[0],
-                lambda t, rows: attended[head, space, t, rows, :],
                 functools.partial(load_upstream, space, head),
                 lambda rows: gain_ref[head, rows, :],
-                wide.at[head % 2, space, 0],
-                wide.at[head % 2, space, 1],
-                wide.at[head % 2, space, 2],
+                wide.at[head, space, 0],
+                wide.at[head, space, 1],
+                wide.at[head, space, 2],
                 grads.at[head, space],
             )
             for space in range(spaces)
@@ -427,8 +431,7 @@
         out_specs=[pl.BlockSpec(memory_space=pltpu.VMEM)] * (frames + 1),
         scratch_shapes=[
             pltpu.VMEM(block, jnp.bfloat16),
-            pltpu.VMEM(block, jnp.bfloat16),
-            pltpu.VMEM((2, spaces, 3, frames, feat, lanes), jnp.float32),
+            pltpu.VMEM((heads, spaces, 3, frames, feat, lanes), jnp.float32),
         ],
         out_shape=[jax.ShapeDtypeStruct((heads, feat, patches), jnp.bfloat16)] * frames
         + [jax.ShapeDtypeStruct((rows, feat), jnp.float32)],

time: 66.5 us -> 66.5 us (level)
  no operation moved by 1% of the time
where the time goes in v21:
time: 66.5 us; the launch traced here: 66.2 us
  starting transfers between devices  25.1 us (38%)
  Pallas kernels  19.1 us (29%)
  waiting for transfers between devices  18.9 us (28%)
  between operations  2.07 us (3%)
  local copies, waits for them, and re-layouts  0.92 us (1%)
    ppermute x16, starting transfers between devices, swap(): return lax.ppermute(field, axis, [(i, i ^ distance) for i in range(size)])  25.1 us
    ppermute x16, waiting for transfers between devices, swap(): return lax.ppermute(field, axis, [(i, i ^ distance) for i in range(size)])  18.9 us
    pallas_call x1, Pallas kernels, forward(): pl.pallas_call(functools.partial(forward_kernel, axis), in_specs=[pl.Bloc...  6.52 us
    pallas_call x3, Pallas kernels, backward(): pl.pallas_call(functools.partial(backward_kernel, axis, distances, gains_...  4.63 us
    pallas_call x1, Pallas kernels, temporal(): pl.pallas_call(functools.partial(temporal_kernel, frames, spaces), in_spe...  3.53 us
    pallas_call x1, Pallas kernels, fetch(): pl.pallas_call(fetch_kernel, in_specs=[pl.BlockSpec(memory_space=pltpu.HB...  1.83 us
  transfers between devices with their start and end apart: 16, of which 5 were waited for; matrix products, arithmetic and copies ran while one was open for 0% of the time, Pallas kernels for 19%

profile of v21, /device:TPU:0, one launch (start us, length us, event | category | flops | bytes accessed | tf_op | source)
XLA Modules:
  0.0 66.2 jit_solution(16177568416204226768)
XLA Ops:
  0.6 1.3 %pack_cotangent.1 = (bf16[2,128,384]{2,1,0:T(8,128)(2,1)S(1)}, bf16[2,128,384]{2,1,0:T(8,128)(2,1)S(1)}, bf16[2,128,384]{2,1,0:T(8,128)(2,1)S(1)}, bf16[2,128,384]{2,1,0:T(8,128)(2,1)S(1)}) custom-call(bf16[128,3072]{1,0:T(8,128)(2,1)} %bitcast.19), custom_call_target="tpu_custom_call" | custom-call | flops 100000000 | tf_op jit(solution)/shard_map/pack_cotangent/pallas_call | solution.py:190
  2.0 5.1 %collective-permute-start.1 = (bf16[2,128,384]{2,1,0:T(8,128)(2,1)S(1)}, bf16[2,128,384]{2,1,0:T(8,128)(2,1)S(1)}, u32[]{:S(2)}, u32[]{:S(2)}) collective-permute-start(bf16[2,128,384]{2,1,0:T(8,128)(2,1)S(1)} %get-tuple-element.56), channel_id=1, source_target_pairs={{0,6},{2,4},{4,2},{6,0},{1,7},{3,5},{5,3},{7,1},{8,14},{10,12},{12... | collective-permute-start | bytes 589832 | tf_op jit(solution)/shard_map/ppermute | solution.py:466
  7.7 6.5 %spatial_forward.1 = (f32[12,256,256]{2,1,0:T(8,128)S(1)}, bf16[3,128,256]{2,1,0:T(8,128)(2,1)S(1)}, bf16[3,128,256]{2,1,0:T(8,128)(2,1)}, bf16[3,128,256]{2,1,0:T(8,128)(2,1)}, bf16[3,128,256]{2,1,0:T(8,128)(2,1)}) custom-call(bf16[256,1536]{1,0:T(8,128)(2,1)} %bitcast.13, bf16[256,1536]{1,0:T(8,128)(2,1)} %bitcast.15, bf16[256,1536]{1,0:T(8,128)(2,1)} %bitcast.17), custom_call_target="tpu_custom_call" | custom-call | flops 600000000 | tf_op jit(solution)/shard_map/spatial_forward/pallas_call | solution.py:76
  14.3 1.4 %collective-permute-start = (bf16[3,128,256]{2,1,0:T(8,128)(2,1)}, bf16[3,128,256]{2,1,0:T(8,128)(2,1)S(1)}, u32[]{:S(2)}, u32[]{:S(2)}) collective-permute-start(bf16[3,128,256]{2,1,0:T(8,128)(2,1)} %get-tuple-element.55), channel_id=1, source_target_pairs={{0,2},{2,0},{4,6},{6,4},{1,3},{3,1},{5,7},{7,5},{8,10},{10,8},{12,... | collective-permute-start | bytes 589832 | tf_op jit(solution)/shard_map/ppermute | solution.py:466
  15.7 2.9 %collective-permute-start.4 = (bf16[3,128,256]{2,1,0:T(8,128)(2,1)}, bf16[3,128,256]{2,1,0:T(8,128)(2,1)}, u32[]{:S(2)}, u32[]{:S(2)}) collective-permute-start(bf16[3,128,256]{2,1,0:T(8,128)(2,1)} %get-tuple-element.72), channel_id=1, source_target_pairs={{0,4},{2,6},{4,0},{6,2},{1,5},{3,7},{5,1},{7,3},{8,12},{10,14},{12... | collective-permute-start | bytes 589832 | tf_op jit(solution)/shard_map/ppermute | solution.py:466
  18.7 6.9 %collective-permute-done.2.refs_1_ = bf16[2,128,384]{2,1,0:T(8,128)(2,1)S(1)} collective-permute-done((bf16[2,128,384]{2,1,0:T(8,128)(2,1)S(1)}, bf16[2,128,384]{2,1,0:T(8,128)(2,1)S(1)}, u32[]{:S(2)}, u32[]{:S(2)}) %collective-permute-start.2) | collective-permute-done | bytes 196640 | tf_op jit(solution)/shard_map/ppermute | solution.py:466
  25.6 1.3 %turn_cotangent.1 = (bf16[6,3,128,128]{3,2,1,0:T(8,128)(2,1)S(1)}, bf16[2,3,128,128]{3,2,1,0:T(8,128)(2,1)}, bf16[2,3,128,128]{3,2,1,0:T(8,128)(2,1)}) custom-call(bf16[2,128,384]{2,1,0:T(8,128)(2,1)S(1)} %collective-permute-done.1.refs_0_, bf16[2,128,384]{2,1,0:T(8,128)(2,1)S(1)} %collective-permute-done.2.refs_1_, ...), custom_call_target="tpu_custom_call" | custom-call | flops 200000000 | tf_op jit(solution)/shard_map/turn_cotangent/pallas_call | solution.py:239
  26.9 0.8 %copy-done = bf16[6,3,128,128]{3,2,1,0:T(8,128)(2,1)} copy-done((bf16[6,3,128,128]{3,2,1,0:T(8,128)(2,1)}, bf16[6,3,128,128]{3,2,1,0:T(8,128)(2,1)S(1)}, u32[]{:S(2)}) %copy-start) | copy-done | bytes 589848
  27.7 1.7 %collective-permute-start.6 = (bf16[2,3,128,128]{3,2,1,0:T(8,128)(2,1)}, bf16[2,3,128,128]{3,2,1,0:T(8,128)(2,1)}, u32[]{:S(2)}, u32[]{:S(2)}) collective-permute-start(bf16[2,3,128,128]{3,2,1,0:T(8,128)(2,1)} %get-tuple-element.76), channel_id=1, source_target_pairs={{0,1},{1,0},{2,3},{3,2},{4,5},{5,4},{6,7},{7,6},{8,9},{9,8},{10,11... | collective-permute-start | bytes 589832 | tf_op jit(solution)/shard_map/ppermute | solution.py:466
  31.3 1.8 %fetch.1 = (bf16[6,3,128,128]{3,2,1,0:T(8,128)(2,1)S(1)}, bf16[256,1536]{1,0:T(8,128)(2,1)S(1)}, bf16[256,1536]{1,0:T(8,128)(2,1)S(1)}, bf16[256,1536]{1,0:T(8,128)(2,1)S(1)}) custom-call(bf16[6,3,128,128]{3,2,1,0:T(8,128)(2,1)} %copy-done, bf16[256,1536]{1,0:T(8,128)(2,1)} %bitcast.14, bf16[256,1536]{1,0:T(8,128)(2,1)} %bitcast.16, bf16[256,1536]{1,0:T(8,128)(2,1)} %bitcast.18), custom_call_target="tpu_custom_call" | custom-call | flops 100000000 | tf_op jit(solution)/shard_map/fetch/pallas_call | solution.py:361
  33.1 4.4 %collective-permute-done.4.refs_1_ = bf16[3,128,256]{2,1,0:T(8,128)(2,1)} collective-permute-done((bf16[3,128,256]{2,1,0:T(8,128)(2,1)}, bf16[3,128,256]{2,1,0:T(8,128)(2,1)}, u32[]{:S(2)}, u32[]{:S(2)}) %collective-permute-start.4) | collective-permute-done | bytes 196640 | tf_op jit(solution)/shard_map/ppermute | solution.py:466
  37.5 3.5 %temporal.1 = (bf16[3,128,256]{2,1,0:T(8,128)(2,1)S(1)}, bf16[3,128,256]{2,1,0:T(8,128)(2,1)S(1)}, bf16[3,128,256]{2,1,0:T(8,128)(2,1)S(1)}, bf16[3,128,256]{2,1,0:T(8,128)(2,1)S(1)}, f32[8,128]{1,0:T(8,128)S(1)}) custom-call(s32[1]{0:T(128)S(6)} %copy.19.length_ref, s32[1]{0:T(128)} %copy.18.task_ref, ...), custom_call_target="tpu_custom_call" | custom-call | flops 400000000 | tf_op jit(solution)/shard_map/temporal/pallas_call | solution.py:427
  41.2 2.8 %collective-permute-start.8 = (bf16[3,128,256]{2,1,0:T(8,128)(2,1)S(1)}, bf16[3,128,256]{2,1,0:T(8,128)(2,1)S(1)}, u32[]{:S(2)}, u32[]{:S(2)}) collective-permute-start(bf16[3,128,256]{2,1,0:T(8,128)(2,1)S(1)} %get-tuple-element.78), channel_id=1, source_target_pairs={{0,6},{2,4},{4,2},{6,0},{1,7},{3,5},{5,3},{7,1},{8,14},{10,12},{12... | collective-permute-start | bytes 589832 | tf_op jit(solution)/shard_map/ppermute | solution.py:466
  43.9 2.6 %collective-permute-start.9 = (bf16[3,128,256]{2,1,0:T(8,128)(2,1)S(1)}, bf16[3,128,256]{2,1,0:T(8,128)(2,1)S(1)}, u32[]{:S(2)}, u32[]{:S(2)}) collective-permute-start(bf16[3,128,256]{2,1,0:T(8,128)(2,1)S(1)} %get-tuple-element.79), channel_id=1, source_target_pairs={{0,4},{2,6},{4,0},{6,2},{1,5},{3,7},{5,1},{7,3},{8,12},{10,14},{12... | collective-permute-start | bytes 589832 | tf_op jit(solution)/shard_map/ppermute | solution.py:466
  46.6 1.5 %collective-permute-start.11 = (f32[16,128]{1,0:T(8,128)S(1)}, f32[16,128]{1,0:T(8,128)S(1)}, u32[]{:S(2)}, u32[]{:S(2)}) collective-permute-start(f32[16,128]{1,0:T(8,128)S(1)} %pad_maximum_fusion.1), channel_id=1, source_target_pairs={{0,16},{8,24},{16,0},{24,8},{1,17},{9,25},{17,1},{25,9},{2,18},{10... | collective-permute-start | bytes 24584 | tf_op jit(solution)/shard_map/ppermute | solution.py:466
  48.1 1.4 %spatial_backward.3 = (bf16[256,1536]{1,0:T(8,128)(2,1)}, bf16[256,1536]{1,0:T(8,128)(2,1)}) custom-call(bf16[256,1536]{1,0:T(8,128)(2,1)S(1)} %get-tuple-element.68.refs_0_, bf16[256,1536]{1,0:T(8,128)(2,1)S(1)} %get-tuple-element.69.refs_1_, bf16[256,1536]{1,0:T(8,128)(2,1)S(1)} %get-tuple-element.70.refs_2_, ...), custom_call_target="tpu_custom_call" | custom-call | flops 200000000 | tf_op jit(solution)/shard_map/spatial_backward/pallas_call | solution.py:151
  49.5 0.8 %collective-permute-done.11 = f32[16,128]{1,0:T(8,128)S(1)} collective-permute-done((f32[16,128]{1,0:T(8,128)S(1)}, f32[16,128]{1,0:T(8,128)S(1)}, u32[]{:S(2)}, u32[]{:S(2)}) %collective-permute-start.11) | collective-permute-done | bytes 8224 | tf_op jit(solution)/shard_map/ppermute | solution.py:466
  50.3 2.4 %collective-permute-start.15 = (f32[32,128]{1,0:T(8,128)S(1)}, f32[32,128]{1,0:T(8,128)S(1)}, u32[]{:S(2)}, u32[]{:S(2)}) collective-permute-start(f32[32,128]{1,0:T(8,128)S(1)} %pad_maximum_fusion.refs_6_), channel_id=1, source_target_pairs={{0,6},{2,4},{4,2},{6,0},{1,7},{3,5},{5,3},{7,1},{8,14},{10,12},{12... | collective-permute-start | bytes 49160 | tf_op jit(solution)/shard_map/ppermute | solution.py:466
  52.7 0.9 %collective-permute-start.14 = (f32[32,128]{1,0:T(8,128)S(1)}, f32[32,128]{1,0:T(8,128)S(1)}, u32[]{:S(2)}, u32[]{:S(2)}) collective-permute-start(f32[32,128]{1,0:T(8,128)S(1)} %pad_maximum_fusion.refs_6_), channel_id=1, source_target_pairs={{0,4},{2,6},{4,0},{6,2},{1,5},{3,7},{5,1},{7,3},{8,12},{10,14},{12... | collective-permute-start | bytes 49160 | tf_op jit(solution)/shard_map/ppermute | solution.py:466
  53.6 3.8 %collective-permute-done.12.refs_4_ = bf16[3,128,256]{2,1,0:T(8,128)(2,1)S(1)} collective-permute-done((bf16[3,128,256]{2,1,0:T(8,128)(2,1)S(1)}, bf16[3,128,256]{2,1,0:T(8,128)(2,1)S(1)}, u32[]{:S(2)}, u32[]{:S(2)}) %collective-permute-start.12) | collective-permute-done | bytes 196640 | tf_op jit(solution)/shard_map/ppermute | solution.py:466
  57.5 2.5 %collective-permute-start.13 = (f32[32,128]{1,0:T(8,128)S(1)}, f32[32,128]{1,0:T(8,128)S(1)}, u32[]{:S(2)}, u32[]{:S(2)}) collective-permute-start(f32[32,128]{1,0:T(8,128)S(1)} %pad_maximum_fusion.refs_6_), channel_id=1, source_target_pairs={{0,2},{2,0},{4,6},{6,4},{1,3},{3,1},{5,7},{7,5},{8,10},{10,8},{12,... | collective-permute-start | bytes 49160 | tf_op jit(solution)/shard_map/ppermute | solution.py:466
  60.0 1.4 %spatial_backward.4 = (bf16[256,1536]{1,0:T(8,128)(2,1)}, bf16[256,1536]{1,0:T(8,128)(2,1)}) custom-call(bf16[256,1536]{1,0:T(8,128)(2,1)S(1)} %get-tuple-element.68.refs_0_, bf16[256,1536]{1,0:T(8,128)(2,1)S(1)} %get-tuple-element.69.refs_1_, bf16[256,1536]{1,0:T(8,128)(2,1)S(1)} %get-tuple-element.70.refs_2_, ...), custom_call_target="tpu_custom_call", output_to_operand_aliasing={{0}: (5, {}), {1}: (6, {})} | custom-call | flops 200000000 | tf_op jit(solution)/shard_map/spatial_backward/pallas_call | solution.py:151
  61.4 3.0 %collective-permute-done.14.refs_8_ = f32[32,128]{1,0:T(8,128)S(1)} collective-permute-done((f32[32,128]{1,0:T(8,128)S(1)}, f32[32,128]{1,0:T(8,128)S(1)}, u32[]{:S(2)}, u32[]{:S(2)}) %collective-permute-start.14) | collective-permute-done | bytes 16416 | tf_op jit(solution)/shard_map/ppermute | solution.py:466
  64.4 1.8 %spatial_backward.5 = (bf16[256,1536]{1,0:T(8,128)(2,1)}, bf16[256,1536]{1,0:T(8,128)(2,1)}, f32[2,16,1536]{2,1,0:T(8,128)}) custom-call(bf16[256,1536]{1,0:T(8,128)(2,1)S(1)} %get-tuple-element.68.refs_0_, bf16[256,1536]{1,0:T(8,128)(2,1)S(1)} %get-tuple-element.69.refs_1_, ...), custom_call_target="tpu_custom_call", output_to_operand_aliasing={{0}: (11, {}), {1}: (12, {})} | custom-call | flops 200000000 | tf_op jit(solution)/shard_map/spatial_backward/pallas_call | solution.py:151
  (24 shorter events, 1.5 us)
Async XLA Ops:
  0.6 30.4 %copy-start.1 = (f32[2,16,1536]{2,1,0:T(8,128)S(1)}, f32[2,16,1536]{2,1,0:T(8,128)}, u32[]{:S(2)}) copy-start(f32[2,16,1536]{2,1,0:T(8,128)} %refs_10_.1) | copy-start | bytes 589828
  2.0 16.7 %collective-permute-start.1 = (bf16[2,128,384]{2,1,0:T(8,128)(2,1)S(1)}, bf16[2,128,384]{2,1,0:T(8,128)(2,1)S(1)}, u32[]{:S(2)}, u32[]{:S(2)}) collective-permute-start(bf16[2,128,384]{2,1,0:T(8,128)(2,1)S(1)} %get-tuple-element.56), channel_id=1, source_target_pairs={{0,6},{2,4},{4,2},{6,0},{1,7},{3,5},{5,3},{7,1},{8,14},{10,12},{12... | collective-permute-start | bytes 589832 | tf_op jit(solution)/shard_map/ppermute | solution.py:466
  7.1 18.5 %collective-permute-start.2 = (bf16[2,128,384]{2,1,0:T(8,128)(2,1)S(1)}, bf16[2,128,384]{2,1,0:T(8,128)(2,1)S(1)}, u32[]{:S(2)}, u32[]{:S(2)}) collective-permute-start(bf16[2,128,384]{2,1,0:T(8,128)(2,1)S(1)} %get-tuple-element.57), channel_id=1, source_target_pairs={{0,4},{2,6},{4,0},{6,2},{1,5},{3,7},{5,1},{7,3},{8,12},{10,14},{12... | collective-permute-start | bytes 589832 | tf_op jit(solution)/shard_map/ppermute | solution.py:466
  7.1 18.5 %collective-permute-start.3 = (bf16[2,128,384]{2,1,0:T(8,128)(2,1)S(1)}, bf16[2,128,384]{2,1,0:T(8,128)(2,1)S(1)}, u32[]{:S(2)}, u32[]{:S(2)}) collective-permute-start(bf16[2,128,384]{2,1,0:T(8,128)(2,1)S(1)} %get-tuple-element.58), channel_id=1, source_target_pairs={{0,2},{2,0},{4,6},{6,4},{1,3},{3,1},{5,7},{7,5},{8,10},{10,8},{12,... | collective-permute-start | bytes 589832 | tf_op jit(solution)/shard_map/ppermute | solution.py:466
  14.3 16.9 %collective-permute-start = (bf16[3,128,256]{2,1,0:T(8,128)(2,1)}, bf16[3,128,256]{2,1,0:T(8,128)(2,1)S(1)}, u32[]{:S(2)}, u32[]{:S(2)}) collective-permute-start(bf16[3,128,256]{2,1,0:T(8,128)(2,1)} %get-tuple-element.55), channel_id=1, source_target_pairs={{0,2},{2,0},{4,6},{6,4},{1,3},{3,1},{5,7},{7,5},{8,10},{10,8},{12,... | collective-permute-start | bytes 589832 | tf_op jit(solution)/shard_map/ppermute | solution.py:466
  15.7 21.8 %collective-permute-start.4 = (bf16[3,128,256]{2,1,0:T(8,128)(2,1)}, bf16[3,128,256]{2,1,0:T(8,128)(2,1)}, u32[]{:S(2)}, u32[]{:S(2)}) collective-permute-start(bf16[3,128,256]{2,1,0:T(8,128)(2,1)} %get-tuple-element.72), channel_id=1, source_target_pairs={{0,4},{2,6},{4,0},{6,2},{1,5},{3,7},{5,1},{7,3},{8,12},{10,14},{12... | collective-permute-start | bytes 589832 | tf_op jit(solution)/shard_map/ppermute | solution.py:466
  18.6 18.9 %collective-permute-start.5 = (bf16[3,128,256]{2,1,0:T(8,128)(2,1)}, bf16[3,128,256]{2,1,0:T(8,128)(2,1)}, u32[]{:S(2)}, u32[]{:S(2)}) collective-permute-start(bf16[3,128,256]{2,1,0:T(8,128)(2,1)} %get-tuple-element.73), channel_id=1, source_target_pairs={{0,6},{2,4},{4,2},{6,0},{1,7},{3,5},{5,3},{7,1},{8,14},{10,12},{12... | collective-permute-start | bytes 589832 | tf_op jit(solution)/shard_map/ppermute | solution.py:466
  26.9 0.8 %copy-start = (bf16[6,3,128,128]{3,2,1,0:T(8,128)(2,1)}, bf16[6,3,128,128]{3,2,1,0:T(8,128)(2,1)S(1)}, u32[]{:S(2)}) copy-start(bf16[6,3,128,128]{3,2,1,0:T(8,128)(2,1)S(1)} %get-tuple-element.67.refs_0_) | copy-start | bytes 1769476
  27.7 9.8 %collective-permute-start.6 = (bf16[2,3,128,128]{3,2,1,0:T(8,128)(2,1)}, bf16[2,3,128,128]{3,2,1,0:T(8,128)(2,1)}, u32[]{:S(2)}, u32[]{:S(2)}) collective-permute-start(bf16[2,3,128,128]{3,2,1,0:T(8,128)(2,1)} %get-tuple-element.76), channel_id=1, source_target_pairs={{0,1},{1,0},{2,3},{3,2},{4,5},{5,4},{6,7},{7,6},{8,9},{9,8},{10,11... | collective-permute-start | bytes 589832 | tf_op jit(solution)/shard_map/ppermute | solution.py:466
  29.5 8.1 %collective-permute-start.7 = (bf16[2,3,128,128]{3,2,1,0:T(8,128)(2,1)}, bf16[2,3,128,128]{3,2,1,0:T(8,128)(2,1)}, u32[]{:S(2)}, u32[]{:S(2)}) collective-permute-start(bf16[2,3,128,128]{3,2,1,0:T(8,128)(2,1)} %get-tuple-element.77), channel_id=1, source_target_pairs={{0,1},{1,0},{2,3},{3,2},{4,5},{5,4},{6,7},{7,6},{8,9},{9,8},{10,11... | collective-permute-start | bytes 589832 | tf_op jit(solution)/shard_map/ppermute | solution.py:466
  41.1 5.5 %collective-permute-start.10 = (f32[8,128]{1,0:T(8,128)S(1)}, f32[8,128]{1,0:T(8,128)S(1)}, u32[]{:S(2)}, u32[]{:S(2)}) collective-permute-start(f32[8,128]{1,0:T(8,128)S(1)} %get-tuple-element.80), channel_id=1, source_target_pairs={{0,8},{8,0},{16,24},{24,16},{1,9},{9,1},{17,25},{25,17},{2,10},{10... | collective-permute-start | bytes 12296 | tf_op jit(solution)/shard_map/ppermute | solution.py:466
  41.2 23.2 %collective-permute-start.8 = (bf16[3,128,256]{2,1,0:T(8,128)(2,1)S(1)}, bf16[3,128,256]{2,1,0:T(8,128)(2,1)S(1)}, u32[]{:S(2)}, u32[]{:S(2)}) collective-permute-start(bf16[3,128,256]{2,1,0:T(8,128)(2,1)S(1)} %get-tuple-element.78), channel_id=1, source_target_pairs={{0,6},{2,4},{4,2},{6,0},{1,7},{3,5},{5,3},{7,1},{8,14},{10,12},{12... | collective-permute-start | bytes 589832 | tf_op jit(solution)/shard_map/ppermute | solution.py:466
  43.9 20.5 %collective-permute-start.9 = (bf16[3,128,256]{2,1,0:T(8,128)(2,1)S(1)}, bf16[3,128,256]{2,1,0:T(8,128)(2,1)S(1)}, u32[]{:S(2)}, u32[]{:S(2)}) collective-permute-start(bf16[3,128,256]{2,1,0:T(8,128)(2,1)S(1)} %get-tuple-element.79), channel_id=1, source_target_pairs={{0,4},{2,6},{4,0},{6,2},{1,5},{3,7},{5,1},{7,3},{8,12},{10,14},{12... | collective-permute-start | bytes 589832 | tf_op jit(solution)/shard_map/ppermute | solution.py:466
  46.5 11.0 %collective-permute-start.12 = (bf16[3,128,256]{2,1,0:T(8,128)(2,1)S(1)}, bf16[3,128,256]{2,1,0:T(8,128)(2,1)S(1)}, u32[]{:S(2)}, u32[]{:S(2)}) collective-permute-start(bf16[3,128,256]{2,1,0:T(8,128)(2,1)S(1)} %get-tuple-element.87), channel_id=1, source_target_pairs={{0,2},{2,0},{4,6},{6,4},{1,3},{3,1},{5,7},{7,5},{8,10},{10,8},{12,... | collective-permute-start | bytes 589832 | tf_op jit(solution)/shard_map/ppermute | solution.py:466
  46.6 3.7 %collective-permute-start.11 = (f32[16,128]{1,0:T(8,128)S(1)}, f32[16,128]{1,0:T(8,128)S(1)}, u32[]{:S(2)}, u32[]{:S(2)}) collective-permute-start(f32[16,128]{1,0:T(8,128)S(1)} %pad_maximum_fusion.1), channel_id=1, source_target_pairs={{0,16},{8,24},{16,0},{24,8},{1,17},{9,25},{17,1},{25,9},{2,18},{10... | collective-permute-start | bytes 24584 | tf_op jit(solution)/shard_map/ppermute | solution.py:466
  50.3 11.1 %collective-permute-start.15 = (f32[32,128]{1,0:T(8,128)S(1)}, f32[32,128]{1,0:T(8,128)S(1)}, u32[]{:S(2)}, u32[]{:S(2)}) collective-permute-start(f32[32,128]{1,0:T(8,128)S(1)} %pad_maximum_fusion.refs_6_), channel_id=1, source_target_pairs={{0,6},{2,4},{4,2},{6,0},{1,7},{3,5},{5,3},{7,1},{8,14},{10,12},{12... | collective-permute-start | bytes 49160 | tf_op jit(solution)/shard_map/ppermute | solution.py:466
  52.7 11.7 %collective-permute-start.14 = (f32[32,128]{1,0:T(8,128)S(1)}, f32[32,128]{1,0:T(8,128)S(1)}, u32[]{:S(2)}, u32[]{:S(2)}) collective-permute-start(f32[32,128]{1,0:T(8,128)S(1)} %pad_maximum_fusion.refs_6_), channel_id=1, source_target_pairs={{0,4},{2,6},{4,0},{6,2},{1,5},{3,7},{5,1},{7,3},{8,12},{10,14},{12... | collective-permute-start | bytes 49160 | tf_op jit(solution)/shard_map/ppermute | solution.py:466
  57.5 6.9 %collective-permute-start.13 = (f32[32,128]{1,0:T(8,128)S(1)}, f32[32,128]{1,0:T(8,128)S(1)}, u32[]{:S(2)}, u32[]{:S(2)}) collective-permute-start(f32[32,128]{1,0:T(8,128)S(1)} %pad_maximum_fusion.refs_6_), channel_id=1, source_target_pairs={{0,2},{2,0},{4,6},{6,4},{1,3},{3,1},{5,7},{7,5},{8,10},{10,8},{12,... | collective-permute-start | bytes 49160 | tf_op jit(solution)/shard_map/ppermute | solution.py:466
